TPU v7x, 32 devices: a whole 2x2x4 slice. The times are simulated.
32 devices in a mesh: groups: 2 (over x), dp: 16 (over z, y, core).
Axes of the slice: x: 2, y: 2, z: 4, core: 2. Of those that a mesh axis runs over, the one named last changes fastest.
Arguments:
- tokens: bfloat16 [4096, 8192], P(('groups', 'dp')), parts along dimension 0, may hold values from -6 to 6
- output_gradient: bfloat16 [4096, 1024], P(('groups', 'dp')), parts along dimension 0, may hold values from -6 to 6
- value_weight: bfloat16 [1024, 8192], P(None, 'dp'), may hold values from -0.1875 to 0.1875
- down_maps: bfloat16 [64, 128, 8192], P(None, None, 'dp'), may hold values from -0.1875 to 0.1875
- up_maps: bfloat16 [64, 1024, 128], P(None, 'dp'), may hold values from -0.1875 to 0.1875
- adapter_per_block: int32 [32], P('groups'), parts along dimension 0, may hold values from 0 to 63
- ranks: int32 [64], replicated, may hold values from 16 to 128
Outputs:
- input_grad: bfloat16 [4096, 8192], P(('groups', 'dp')), parts along dimension 0
- down_gradient: bfloat16 [128, 128, 8192], P('groups', None, 'dp'), parts along dimension 0
- up_gradient: bfloat16 [128, 1024, 128], P('groups', 'dp'), parts along dimension 0
There are 2 independent parts, one for each index of `groups`. A program takes and returns all parts, laid end to end along the dimension named above; an argument that names none is the same for every part. Nothing has to cross between parts.
All inputs are finite; a program needn't handle non-finite values.
Results may differ from a plain program's by a relative error of at most 0.0049.
Values may be sent and summed in bfloat16 or wider, within the bound.
No kernel may reach another device: no remote copies, remote signals or barrier semaphores. Data moves between devices by JAX's collectives and lax.ppermute only.
A program may use at most 128 MiB of HBM per device.

v0:
```python
import jax
import jax.numpy as jnp
from jax import lax
from jax.sharding import PartitionSpec as P

adapter_alpha = 32.0


def rank_parts(down_maps, up_maps, adapter_per_block, token_piece, gradient_piece):
    num_blocks = adapter_per_block.shape[0]
    width_local = token_piece.shape[1]
    block_rows = token_piece.shape[0] // num_blocks
    token_block_rows = token_piece.reshape(num_blocks, block_rows, width_local)
    grad_blocks = gradient_piece.reshape(num_blocks, block_rows, gradient_piece.shape[1])
    selected_down = down_maps[adapter_per_block]
    selected_up = up_maps[adapter_per_block]
    hidden_part = jnp.einsum(
        "out,oyt->ouy", token_block_rows, selected_down, preferred_element_type=jnp.float32
    )
    back_part = jnp.einsum(
        "bkv,bvr->bkr", grad_blocks, selected_up, preferred_element_type=jnp.float32
    )
    return (token_block_rows, grad_blocks, selected_down, hidden_part, back_part)


def finish_layout(
    adapter_per_block,
    ranks,
    rank_extent,
    token_block_rows,
    grad_blocks,
    selected_down,
    hidden_full,
    back_full,
):
    num_blocks = adapter_per_block.shape[0]
    num_adapters = ranks.shape[0]
    block_rows = token_block_rows.shape[1]
    width_local = token_block_rows.shape[2]
    alive_mask = (jnp.arange(rank_extent, dtype=jnp.int32)[None, :] < ranks[:, None]).astype(
        jnp.float32
    )
    adapter_scale = adapter_alpha / ranks.astype(jnp.float32)
    block_mask = alive_mask[adapter_per_block][:, None, :]
    block_factor = adapter_scale[adapter_per_block][:, None, None]
    hidden_low = (hidden_full * block_mask).astype(jnp.bfloat16)
    rank_backward = (block_factor * back_full * block_mask).astype(jnp.bfloat16)
    member_table = (
        adapter_per_block[None, :] == jnp.arange(num_adapters, dtype=jnp.int32)[:, None]
    ).astype(jnp.float32)
    down_piece = jnp.einsum(
        "qoi,qoe->qie", rank_backward, token_block_rows, preferred_element_type=jnp.float32
    )
    part_b = block_factor * jnp.einsum(
        "bkv,bkr->bvr", grad_blocks, hidden_low, preferred_element_type=jnp.float32
    )
    down_gradient = jnp.einsum(
        "ab,brd->ard", member_table, down_piece, precision=lax.Precision.HIGHEST
    ).astype(jnp.bfloat16)
    up_gradient = jnp.einsum(
        "ab,bvr->avr", member_table, part_b, precision=lax.Precision.HIGHEST
    ).astype(jnp.bfloat16)
    adapter_slice = jnp.einsum(
        "wyt,wtv->wyv", rank_backward, selected_down, preferred_element_type=jnp.float32
    ).reshape(num_blocks * block_rows, width_local)
    return (down_gradient, up_gradient, adapter_slice)


def local(tokens, output_gradient, value_weight, down_maps, up_maps, adapter_per_block, ranks):
    rank_extent = down_maps.shape[1]
    grad_whole = lax.all_gather(output_gradient, "dp", axis=0, tiled=True)
    value_shard = up_maps.shape[1]
    gradient_piece = lax.dynamic_slice_in_dim(
        grad_whole, lax.axis_index("dp") * value_shard, value_shard, 1
    )
    token_piece = lax.all_to_all(tokens, "dp", split_axis=1, concat_axis=0, tiled=True)
    token_block_rows, grad_blocks, selected_down, hidden_part, back_part = rank_parts(
        down_maps, up_maps, adapter_per_block, token_piece, gradient_piece
    )
    hidden_full, back_full = lax.psum((hidden_part, back_part), "dp")
    down_gradient, up_gradient, adapter_slice = finish_layout(
        adapter_per_block,
        ranks,
        rank_extent,
        token_block_rows,
        grad_blocks,
        selected_down,
        hidden_full,
        back_full,
    )
    frozen_slice = jnp.dot(grad_whole, value_weight, preferred_element_type=jnp.float32)
    input_grad = lax.all_to_all(
        (frozen_slice + adapter_slice).astype(jnp.bfloat16),
        "dp",
        split_axis=0,
        concat_axis=1,
        tiled=True,
    )
    return (input_grad, down_gradient, up_gradient)


def solution(mesh):
    in_specs = (
        P(("groups", "dp"), None),
        P(("groups", "dp"), None),
        P(None, "dp"),
        P(None, None, "dp"),
        P(None, "dp", None),
        P("groups"),
        P(),
    )
    out_specs = (P(("groups", "dp"), None), P("groups", None, "dp"), P("groups", "dp", None))
    return jax.shard_map(local, mesh=mesh, in_specs=in_specs, out_specs=out_specs, check_vma=False)
```

profile of v0, /device:TPU:13, one launch (start us, length us, event | category | flops | bytes accessed | tf_op | source)
XLA Modules:
  0.0 266.2 jit_solution(1109935050562392585)
XLA Ops:
  7.2 0.0 copy-start
  7.2 0.0 all-gather.2.cloned.1.call-start
  7.2 0.7 all-gather.2.cloned.1.call-update
  7.9 3.2 %copy.31 = bf16[128,8192]{0,1:T(8,128)(2,1)S(1)} copy(bf16[128,8192]{1,0:T(8,128)(2,1)} %param.7) | data formatting | bytes 4194304 | tf_op args[0]
  11.1 2.6 copy.32
  13.7 0.0 copy-start.4
  13.7 6.7 %all-to-all-start.1 = ((bf16[128,16,512]{2,0,1:T(8,128)(2,1)}), bf16[128,16,512]{2,0,1:T(8,128)(2,1)S(1)}, u32[]{:S(2)}, u32[]{:S(2)}) async-start(bf16[128,16,512]{2,0,1:T(8,128)(2,1)} %copy.32), calls=%async_computation.1 | async-start | bytes 4194304 | tf_op jit(solution)/shard_map/all_to_all | solution.py:76
  20.4 0.0 all-reduce.3.cloned.1.call-start
  20.5 0.0 copy-done.4
  20.5 1.8 gather_fusion.1
  22.3 5.4 %gather_fusion.3 = bf16[16,128,512]{2,1,0:T(8,128)(2,1)} fusion(bf16[64,128,512]{2,1,0:T(8,128)(2,1)} %param.10, s32[1024]{0:T(1024)S(1)} %pad_clamp_fusion), kind=kCustom, calls=%fused_computation.3 | custom fusion | bytes 4194368 | tf_op jit(solution)/shard_map/gather | solution.py:15
  27.8 64.9 %all-to-all-done.1 = bf16[128,16,512]{2,0,1:T(8,128)(2,1)S(1)} async-done(((bf16[128,16,512]{2,0,1:T(8,128)(2,1)}), bf16[128,16,512]{2,0,1:T(8,128)(2,1)S(1)}, u32[]{:S(2)}, u32[]{:S(2)}) %all-to-all-start.1) | async-done | bytes 2097184 | tf_op jit(solution)/shard_map/all_to_all | solution.py:76
  92.6 3.3 %fusion.6 = f32[16,128,128]{2,1,0:T(8,128)} fusion(bf16[16,128,512]{2,1,0:T(8,128)(2,1)} %gather_fusion.3, bf16[128,16,512]{2,0,1:T(8,128)(2,1)S(1)} %all-to-all-done.1), kind=kOutput, calls=%fused_computation.13 | convolution fusion | flops 268435456 | bytes 5242880 | tf_op jit(solution)/shard_map/out,oyt->ouy/dot_general | solution.py:17
  95.9 0.0 all-gather.2.cloned.1.call-done
  95.9 1.2 constant_dynamic-slice_fusion
  97.2 0.0 copy-start.1
  97.2 0.0 copy-start.5
  97.2 0.8 copy-done.1
  98.0 1.2 fusion.18
  99.2 0.0 all-reduce.3.cloned.1.call-update
  99.2 0.0 copy-done.5
  99.3 0.7 gather_fusion
  99.9 0.1 fusion.11
  100.0 0.6 gather_fusion.2
  100.6 94.2 %all-reduce.3.cloned.1.call-done = (f32[16,128,128]{2,1,0:T(8,128)}, f32[16,128,128]{2,1,0:T(8,128)}) async-done(((f32[16,128,128]{2,1,0:T(8,128)}, f32[16,128,128]{2,1,0:T(8,128)}), (f32[16,128,128]{2,1,0:T(8,128)}, f32[16,128,128]{2,1,0:T(8,128)})) %all-reduce.3.cloned.1.call-update) | async-done | bytes 2097168 | tf_op jit(solution)/shard_map/psum | solution.py:80
  194.8 0.0 copy-start.3
  194.8 2.8 %fusion.17 = f32[16,128,512]{2,1,0:T(8,128)S(1)} fusion(bf16[16,128,512]{2,1,0:T(8,128)(2,1)} %gather_fusion.3, f32[16,128,128]{2,1,0:T(8,128)} %get-tuple-element.15, f32[16,128]{1,0:T(8,128)S(1)} %gather_fusion.2, f32[16]{0:T(128)S(1)} %gather_fusion), kind=kOutput, calls=%fused_computation.29 | convolution fusion | flops 269221888 | bytes 7348288 | tf_op jit(solution)/shard_map/wyt,wtv->wyv/dot_general | solution.py:63
  197.6 0.0 copy-done
  197.6 0.3 copy-done.3
  197.9 3.7 %fusion = bf16[2048,512]{1,0:T(8,128)(2,1)} fusion(f32[16,128,512]{2,1,0:T(8,128)S(1)} %fusion.17, bf16[2048,1024]{1,0:T(8,128)(2,1)S(1)} %copy-done.3, bf16[1024,512]{1,0:T(8,128)(2,1)S(1)} %copy-done), kind=kOutput, calls=%fused_computation.6 | convolution fusion | flops 2149580800 | bytes 11534336 | tf_op jit(solution)/shard_map/dot_general | solution.py:91
  201.6 7.1 %all-to-all-start = ((bf16[16,128,512]{2,1,0:T(8,128)(2,1)}), bf16[16,128,512]{2,1,0:T(8,128)(2,1)}, u32[]{:S(2)}, u32[]{:S(2)}) async-start(bf16[16,128,512]{2,1,0:T(8,128)(2,1)} %bitcast.33), calls=%async_computation | async-start | bytes 4194304 | tf_op jit(solution)/shard_map/all_to_all | solution.py:92
  208.7 1.7 convolution_multiply_fusion
  210.4 0.0 copy-start.2
  210.4 1.2 convolution_convert_fusion.1
  211.6 1.6 copy.39
  213.2 0.0 copy-done.2
  213.2 0.9 fusion.4
  214.1 9.3 %convolution_convert_fusion = bf16[64,128,512]{2,0,1:T(8,128)(2,1)} fusion(f32[16,128,512]{2,1,0:T(8,128)S(1)} %fusion.4, s32[16]{0:T(128)S(1)} %copy-done.4), kind=kOutput, calls=%fused_computation.4 | convolution fusion | flops 809501696 | bytes 12582976 | tf_op jit(solution)/shard_map/ab,brd->ard/dot_general | solution.py:57
  223.5 11.5 %copy.38 = bf16[64,128,512]{2,1,0:T(8,128)(2,1)} copy(bf16[64,128,512]{2,0,1:T(8,128)(2,1)} %convolution_convert_fusion) | data formatting | bytes 16777216
  235.0 21.2 %all-to-all-done = bf16[16,128,512]{2,1,0:T(8,128)(2,1)} async-done(((bf16[16,128,512]{2,1,0:T(8,128)(2,1)}), bf16[16,128,512]{2,1,0:T(8,128)(2,1)}, u32[]{:S(2)}, u32[]{:S(2)}) %all-to-all-start) | async-done | bytes 2097184 | tf_op jit(solution)/shard_map/all_to_all | solution.py:92
  256.2 3.1 %copy.45 = bf16[16,16,8,512]{3,2,0,1:T(8,128)(2,1)} copy(bf16[16,16,8,512]{3,2,1,0:T(8,128)(2,1)} %bitcast.8) | data formatting | bytes 4194304 | tf_op jit(solution)/shard_map/all_to_all | solution.py:92
  (3 shorter events, 0.0 us)
Async XLA Ops:
  7.2 190.4 %copy-start = (bf16[1024,512]{1,0:T(8,128)(2,1)S(1)}, bf16[1024,512]{1,0:T(8,128)(2,1)}, u32[]{:S(2)}) copy-start(bf16[1024,512]{1,0:T(8,128)(2,1)} %param.9) | copy-start | bytes 3145732
  7.2 88.7 %all-gather.2.cloned.1.call-start = ((), (), s32[]{:S(2)}) async-start(), calls=%async_computation.2 | async-start | bytes 4456448 | tf_op jit(solution)/shard_map/all_gather | solution.py:71
  13.7 6.7 %copy-start.4 = (s32[16]{0:T(128)S(1)}, s32[16]{0:T(128)}, u32[]{:S(2)}) copy-start(s32[16]{0:T(128)} %param.12) | copy-start | bytes 196
  13.7 78.9 %all-to-all-start.1 = ((bf16[128,16,512]{2,0,1:T(8,128)(2,1)}), bf16[128,16,512]{2,0,1:T(8,128)(2,1)S(1)}, u32[]{:S(2)}, u32[]{:S(2)}) async-start(bf16[128,16,512]{2,0,1:T(8,128)(2,1)} %copy.32), calls=%async_computation.1 | async-start | bytes 4194304 | tf_op jit(solution)/shard_map/all_to_all | solution.py:76
  20.4 174.3 %all-reduce.3.cloned.1.call-start = ((), (), s32[]{:S(2)}) async-start(), calls=%async_computation.3 | async-start | bytes 4194304 | tf_op jit(solution)/shard_map/psum | solution.py:80
  97.2 0.8 copy-start.1
  97.2 2.1 copy-start.5
  194.8 3.1 %copy-start.3 = (bf16[2048,1024]{1,0:T(8,128)(2,1)S(1)}, bf16[2048,1024]{1,0:T(8,128)(2,1)}, u32[]{:S(2)}) copy-start(bf16[2048,1024]{1,0:T(8,128)(2,1)} %all-gather.2.cloned.1.call-done) | copy-start | bytes 12582916
  201.6 54.7 %all-to-all-start = ((bf16[16,128,512]{2,1,0:T(8,128)(2,1)}), bf16[16,128,512]{2,1,0:T(8,128)(2,1)}, u32[]{:S(2)}, u32[]{:S(2)}) async-start(bf16[16,128,512]{2,1,0:T(8,128)(2,1)} %bitcast.33), calls=%async_computation | async-start | bytes 4194304 | tf_op jit(solution)/shard_map/all_to_all | solution.py:92
  210.4 2.8 %copy-start.2 = (f32[16,128,128]{2,1,0:T(8,128)S(1)}, f32[16,128,128]{2,1,0:T(8,128)}, u32[]{:S(2)}) copy-start(f32[16,128,128]{2,1,0:T(8,128)} %get-tuple-element.15) | copy-start | bytes 3145732
Sparse Core Ops, SparseCore 0:
  10.2 75.7 all-gather.1
  99.4 95.3 all-reduce.2
where the time goes:
time: 267 us; the launch traced here: 266 us
  waiting for transfers between devices  181 us (68%)
  local copies, waits for them, and re-layouts  33 us (12%)
  matrix products  24.1 us (9%)
  between operations  14.2 us (5%)
  starting transfers between devices  13.9 us (5%)
    psum x1, waiting for transfers between devices, local(): hidden_full, back_full = lax.psum((hidden_part, back_part), 'dp')  94.2 us
    all_to_all x1, waiting for transfers between devices, local(): lax.all_to_all(tokens, 'dp', split_axis=1, concat_axis=0, tiled=True)  64.9 us
    all_to_all x1, waiting for transfers between devices, local(): lax.all_to_all((frozen_slice + adapter_slice).astype(jnp.bfloat16), 'dp',...  21.2 us
    unnamed x15, local copies, waits for them, and re-layouts  17.5 us
    dot_general x1, matrix products, finish_layout(): jnp.einsum('ab,brd->ard', member_table, down_piece, precision=lax.Precisi...  9.35 us
    all_to_all x1, starting transfers between devices, local(): lax.all_to_all((frozen_slice + adapter_slice).astype(jnp.bfloat16), 'dp',...  7.14 us
    all_to_all x1, starting transfers between devices, local(): lax.all_to_all(tokens, 'dp', split_axis=1, concat_axis=0, tiled=True)  6.69 us
    gather x1, local copies, waits for them, and re-layouts, rank_parts(): selected_down = down_maps[adapter_per_block]  5.41 us
  transfers between devices with their start and end apart: 4, of which 3 were waited for; matrix products, arithmetic and copies ran while one was open for 16% of the time, Pallas kernels for 0%

commit v1 on v0

v1 whole, which is shorter than its diff:
```python
import functools

import jax
import jax.numpy as jnp
from jax import lax
from jax.experimental import pallas as pl
from jax.experimental.pallas import tpu as pltpu
from jax.sharding import PartitionSpec as P

adapter_alpha = 32.0
vmem_limit = 48 * 1024 * 1024


def group_of(count):
    return 4 if count % 4 == 0 else 1


def gather_up_kernel(adapters, up_maps, out, sems):
    count = out.shape[0]
    copies = [
        pltpu.make_async_copy(up_maps.at[adapters[block]], out.at[block], sems.at[block])
        for block in range(count)
    ]
    for copy in copies:
        copy.start()
    for copy in copies:
        copy.wait()


def gather_up(adapters, up_maps):
    count = adapters.shape[0]
    return pl.pallas_call(
        gather_up_kernel,
        out_shape=jax.ShapeDtypeStruct((count,) + up_maps.shape[1:], up_maps.dtype),
        grid_spec=pltpu.PrefetchScalarGridSpec(
            num_scalar_prefetch=1,
            grid=(),
            in_specs=[pl.BlockSpec(memory_space=pl.ANY)],
            out_specs=pl.BlockSpec(memory_space=pl.ANY),
            scratch_shapes=[pltpu.SemaphoreType.DMA((count,))],
        ),
        name="gather_up",
    )(adapters, up_maps)


def split_kernel(source, out):
    width = out.shape[2]
    for piece in range(out.shape[0]):
        out[piece] = source[:, piece * width : (piece + 1) * width]


def split_columns(source, pieces):
    rows, columns = source.shape
    width = columns // pieces
    step = group_of(pieces)
    return pl.pallas_call(
        split_kernel,
        out_shape=jax.ShapeDtypeStruct((pieces, rows, width), source.dtype),
        grid=(pieces // step,),
        in_specs=[pl.BlockSpec((rows, step * width), lambda i: (0, i))],
        out_specs=pl.BlockSpec((step, rows, width), lambda i: (i, 0, 0)),
        name="split_columns",
    )(source)


def join_kernel(source, out):
    width = source.shape[2]
    for piece in range(source.shape[0]):
        out[:, piece * width : (piece + 1) * width] = source[piece]


def join_columns(source):
    pieces, rows, width = source.shape
    step = group_of(pieces)
    return pl.pallas_call(
        join_kernel,
        out_shape=jax.ShapeDtypeStruct((rows, pieces * width), source.dtype),
        grid=(pieces // step,),
        in_specs=[pl.BlockSpec((step, rows, width), lambda i: (i, 0, 0))],
        out_specs=pl.BlockSpec((rows, step * width), lambda i: (0, i)),
        name="join_columns",
    )(source)


def rank_row(ranks, adapter, extent):
    rank = jnp.full((1, extent), ranks[adapter], jnp.int32)
    alive = (lax.broadcasted_iota(jnp.int32, (1, extent), 1) < rank).astype(jnp.float32)
    return alive, adapter_alpha / rank.astype(jnp.float32)


def back_kernel(adapters, ranks, place, gradient, up, out):
    alive, factor = rank_row(ranks, adapters[place[0]], up.shape[1])
    back = jnp.dot(gradient[...], up[...], preferred_element_type=jnp.float32)
    width = gradient.shape[1]
    out[:, :width] = gradient[...]
    out[:, width:] = (factor * back * alive).astype(out.dtype)


def back_beside_gradient(adapters, ranks, place, gradient, up):
    rows, width = gradient.shape
    return pl.pallas_call(
        back_kernel,
        out_shape=jax.ShapeDtypeStruct((rows, width + up.shape[1]), gradient.dtype),
        grid_spec=pltpu.PrefetchScalarGridSpec(
            num_scalar_prefetch=3,
            grid=(1,),
            in_specs=[
                pl.BlockSpec(gradient.shape, lambda i, *_: (0, 0)),
                pl.BlockSpec(up.shape, lambda i, *_: (0, 0)),
            ],
            out_specs=pl.BlockSpec((rows, width + up.shape[1]), lambda i, *_: (0, 0)),
        ),
        compiler_params=pltpu.CompilerParams(vmem_limit_bytes=vmem_limit),
        name="back_low",
    )(adapters, ranks, place, gradient, up)


def down_specs(step, down_maps):
    def spec(offset):
        return pl.BlockSpec(
            (1,) + down_maps.shape[1:],
            lambda i, adapters: (adapters[i * step + offset], 0, 0),
        )

    return [spec(offset) for offset in range(step)]


def hidden_kernel(adapters, tokens, *refs):
    out = refs[-1]
    for offset in range(tokens.shape[0]):
        out[offset] = lax.dot_general(
            tokens[offset],
            refs[offset][0],
            (((1,), (1,)), ((), ())),
            preferred_element_type=jnp.float32,
        ).astype(out.dtype)


def hidden_parts(adapters, tokens, down_maps):
    count, rows, width = tokens.shape
    step = group_of(count)
    extent = down_maps.shape[1]
    return pl.pallas_call(
        hidden_kernel,
        out_shape=jax.ShapeDtypeStruct((count, rows, extent), jnp.bfloat16),
        grid_spec=pltpu.PrefetchScalarGridSpec(
            num_scalar_prefetch=1,
            grid=(count // step,),
            in_specs=[pl.BlockSpec((step, rows, width), lambda i, _: (i, 0, 0))]
            + down_specs(step, down_maps),
            out_specs=pl.BlockSpec((step, rows, extent), lambda i, _: (i, 0, 0)),
        ),
        compiler_params=pltpu.CompilerParams(vmem_limit_bytes=vmem_limit),
        name="hidden_parts",
    )(adapters, tokens, *([down_maps] * step))


def input_kernel(adapters, gathered, weight, *refs):
    out = refs[-1]
    step, rows, _ = out.shape
    depth = weight.shape[0]
    frozen = jnp.dot(gathered[:, :depth], weight[...], preferred_element_type=jnp.float32)
    for offset in range(step):
        low = gathered[offset * rows : (offset + 1) * rows, depth:]
        adapter = jnp.dot(low, refs[offset][0], preferred_element_type=jnp.float32)
        out[offset] = (frozen[offset * rows : (offset + 1) * rows] + adapter).astype(out.dtype)


def input_slices(adapters, gathered, weight, down_maps):
    count = adapters.shape[0]
    step = group_of(count)
    rows = gathered.shape[0] // count
    width = weight.shape[1]
    return pl.pallas_call(
        input_kernel,
        out_shape=jax.ShapeDtypeStruct((count, rows, width), jnp.bfloat16),
        grid_spec=pltpu.PrefetchScalarGridSpec(
            num_scalar_prefetch=1,
            grid=(count // step,),
            in_specs=[
                pl.BlockSpec((step * rows, gathered.shape[1]), lambda i, _: (i, 0)),
                pl.BlockSpec(weight.shape, lambda i, _: (0, 0)),
            ]
            + down_specs(step, down_maps),
            out_specs=pl.BlockSpec((step, rows, width), lambda i, _: (i, 0, 0)),
        ),
        compiler_params=pltpu.CompilerParams(vmem_limit_bytes=vmem_limit),
        name="input_slices",
    )(adapters, gathered, weight, *([down_maps] * step))


def up_piece_kernel(adapters, ranks, place, parts, gradient, out):
    extent = parts.shape[2]
    alive, factor = rank_row(ranks, adapters[place[0]], extent)
    hidden = parts[0].astype(jnp.float32)
    for part in range(1, parts.shape[0]):
        hidden += parts[part].astype(jnp.float32)
    hidden_low = (hidden * alive).astype(jnp.bfloat16)
    piece = lax.dot_general(
        gradient[...], hidden_low, (((0,), (0,)), ((), ())), preferred_element_type=jnp.float32
    )
    out[...] = (factor * piece).astype(out.dtype)


def up_piece(adapters, ranks, place, parts, gradient):
    width = gradient.shape[1]
    extent = parts.shape[2]
    return pl.pallas_call(
        up_piece_kernel,
        out_shape=jax.ShapeDtypeStruct((width, extent), jnp.bfloat16),
        grid_spec=pltpu.PrefetchScalarGridSpec(
            num_scalar_prefetch=3,
            grid=(1,),
            in_specs=[
                pl.BlockSpec(parts.shape, lambda i, *_: (0, 0, 0)),
                pl.BlockSpec(gradient.shape, lambda i, *_: (0, 0)),
            ],
            out_specs=pl.BlockSpec((width, extent), lambda i, *_: (0, 0)),
        ),
        compiler_params=pltpu.CompilerParams(vmem_limit_bytes=vmem_limit),
        name="up_piece",
    )(adapters, ranks, place, parts, gradient)


def list_members(adapters, head, following):
    def clear(adapter, carry):
        head[adapter] = -1
        return carry

    lax.fori_loop(0, head.shape[0], clear, 0)

    def link(step, carry):
        block = following.shape[0] - 1 - step
        adapter = adapters[block]
        following[block] = head[adapter]
        head[adapter] = block
        return carry

    lax.fori_loop(0, following.shape[0], link, 0)


def sum_members(head, following, total, out, term):
    chunk = out.shape[0]

    def per_adapter(slot, carry):
        first = head[pl.program_id(0) * chunk + slot]

        @pl.when(first < 0)
        def _():
            out[slot] = jnp.zeros(out.shape[1:], out.dtype)

        @pl.when(first >= 0)
        def _():
            total[...] = term(first)

            def more(block):
                total[...] += term(block)
                return following[block]

            lax.while_loop(lambda block: block >= 0, more, following[first])
            out[slot] = total[...].astype(out.dtype)

        return carry

    lax.fori_loop(0, chunk, per_adapter, 0)


def down_gradient_kernel(adapters, gathered, tokens, out, head, following, total):
    rows = tokens.shape[1]

    @pl.when(pl.program_id(0) == 0)
    def _():
        list_members(adapters, head, following)

    def term(block):
        low = gathered[pl.ds(pl.multiple_of(block * rows, rows), rows), :]
        return lax.dot_general(
            low, tokens[block], (((0,), (0,)), ((), ())), preferred_element_type=jnp.float32
        )

    sum_members(head, following, total, out, term)


def down_gradients(adapters, gathered, tokens, num_adapters, extent):
    count, rows, width = tokens.shape
    chunk = 8 if num_adapters % 8 == 0 else 1
    low_at = gathered.shape[1] // extent - 1
    return pl.pallas_call(
        down_gradient_kernel,
        out_shape=jax.ShapeDtypeStruct((num_adapters, extent, width), jnp.bfloat16),
        grid_spec=pltpu.PrefetchScalarGridSpec(
            num_scalar_prefetch=1,
            grid=(num_adapters // chunk,),
            in_specs=[
                pl.BlockSpec((count * rows, extent), lambda i, _: (0, low_at)),
                pl.BlockSpec(tokens.shape, lambda i, _: (0, 0, 0)),
            ],
            out_specs=pl.BlockSpec((chunk, extent, width), lambda i, _: (i, 0, 0)),
            scratch_shapes=[
                pltpu.SMEM((num_adapters,), jnp.int32),
                pltpu.SMEM((count,), jnp.int32),
                pltpu.VMEM((extent, width), jnp.float32),
            ],
        ),
        compiler_params=pltpu.CompilerParams(vmem_limit_bytes=vmem_limit),
        name="down_gradients",
    )(adapters, gathered, tokens)


def up_gradient_kernel(adapters, pieces, out, head, following, total):
    @pl.when(pl.program_id(0) == 0)
    def _():
        list_members(adapters, head, following)

    sum_members(
        head, following, total, out, lambda block: pieces[block].astype(jnp.float32)
    )


def up_gradients(adapters, pieces, num_adapters):
    count, width, extent = pieces.shape
    chunk = 32 if num_adapters % 32 == 0 else 1
    return pl.pallas_call(
        up_gradient_kernel,
        out_shape=jax.ShapeDtypeStruct((num_adapters, width, extent), jnp.bfloat16),
        grid_spec=pltpu.PrefetchScalarGridSpec(
            num_scalar_prefetch=1,
            grid=(num_adapters // chunk,),
            in_specs=[pl.BlockSpec(pieces.shape, lambda i, _: (0, 0, 0))],
            out_specs=pl.BlockSpec((chunk, width, extent), lambda i, _: (i, 0, 0)),
            scratch_shapes=[
                pltpu.SMEM((num_adapters,), jnp.int32),
                pltpu.SMEM((count,), jnp.int32),
                pltpu.VMEM((width, extent), jnp.float32),
            ],
        ),
        compiler_params=pltpu.CompilerParams(vmem_limit_bytes=vmem_limit),
        name="up_gradients",
    )(adapters, pieces)


def exchange(pieces):
    return lax.all_to_all(pieces, "dp", split_axis=0, concat_axis=0, tiled=True)


def local(tokens, output_gradient, value_weight, down_maps, up_maps, adapter_per_block, ranks):
    devices = lax.axis_size("dp")
    num_adapters, extent, _ = down_maps.shape
    width = output_gradient.shape[1]
    place = lax.axis_index("dp").astype(jnp.int32).reshape(1)

    own_up = exchange(gather_up(adapter_per_block, up_maps)).reshape(width, extent)
    token_pieces = split_columns(tokens, devices)
    token_pieces, own_up = lax.optimization_barrier((token_pieces, own_up))
    token_blocks = exchange(token_pieces)

    beside = back_beside_gradient(adapter_per_block, ranks, place, output_gradient, own_up)
    gathered = lax.all_gather(beside, "dp", axis=0, tiled=True)
    slices = input_slices(adapter_per_block, gathered, value_weight, down_maps)

    parts = exchange(hidden_parts(adapter_per_block, token_blocks, down_maps))
    slices, parts = lax.optimization_barrier((slices, parts))
    input_grad = join_columns(exchange(slices))

    piece = up_piece(adapter_per_block, ranks, place, parts, output_gradient)
    pieces = exchange(piece.reshape(devices, width // devices, extent))
    down_gradient = down_gradients(
        adapter_per_block, gathered, token_blocks, num_adapters, extent
    )
    up_gradient = up_gradients(adapter_per_block, pieces, num_adapters)
    return (input_grad, down_gradient, up_gradient)


def solution(mesh):
    in_specs = (
        P(("groups", "dp"), None),
        P(("groups", "dp"), None),
        P(None, "dp"),
        P(None, None, "dp"),
        P(None, "dp", None),
        P("groups"),
        P(),
    )
    out_specs = (P(("groups", "dp"), None), P("groups", None, "dp"), P("groups", "dp", None))
    return jax.shard_map(local, mesh=mesh, in_specs=in_specs, out_specs=out_specs, check_vma=False)
```

time: 267 us -> 217 us (0.81)
  waiting for transfers between devices: 181 us -> 44.2 us
  blocking collectives: 0 us -> 94.2 us
  Pallas kernels: 0 us -> 42.9 us
  local copies, waits for them, and re-layouts: 33 us -> 2.55 us
  matrix products: 24.1 us -> 0 us
  starting transfers between devices: 13.9 us -> 18 us
    all_to_all x0 -> x2, blocking collectives: none -> 94.2 us  [exchange(): return lax.all_to_all(pieces, 'dp', split_axis=0, concat_axis=0, tiled=True)]
    psum x1 -> x0, waiting for transfers between devices: 94.2 us -> none  [local(): hidden_full, back_full = lax.psum((hidden_part, back_part), 'dp')]
    pallas_call x0 -> x9, Pallas kernels: none -> 42.9 us  [the longest x1 9.86 us: gather_up(): pl.pallas_call(gather_up_kernel, out_shape=jax.ShapeDtypeStruct((count,)...]
    all_to_all x2 -> x3, waiting for transfers between devices: 86.1 us -> 44.1 us  [exchange(): return lax.all_to_all(pieces, 'dp', split_axis=0, concat_axis=0, tiled=True)]
    dot_general x8 -> x0, matrix products: 24.1 us -> none  [the longest x1 9.35 us: finish_layout(): jnp.einsum('ab,brd->ard', member_table, down_piece, precision=lax.Precisi...]
    unnamed x15 -> x10, local copies, waits for them, and re-layouts: 17.5 us -> 2.55 us
    gather x4 -> x0, local copies, waits for them, and re-layouts: 8.46 us -> none  [the longest x1 5.41 us: rank_parts(): selected_down = down_maps[adapter_per_block]]
    all_to_all x2 -> x0, local copies, waits for them, and re-layouts: 5.74 us -> none  [the longest x1 3.14 us: local(): lax.all_to_all((frozen_slice + adapter_slice).astype(jnp.bfloat16), 'dp',...]
  transfers between devices with their start and end apart: 4 -> 4, of which waited for: 3 -> 3; matrix products, arithmetic and copies ran while one was open for 16% -> 0% of each run, Pallas kernels for 0% -> 12%
where the time goes in v1:
time: 217 us; the launch traced here: 216 us
  blocking collectives  94.2 us (43%)
  waiting for transfers between devices  44.2 us (20%)
  Pallas kernels  42.9 us (20%)
  starting transfers between devices  18 us (8%)
  between operations  14.1 us (6%)
  local copies, waits for them, and re-layouts  2.55 us (1%)
    all_to_all x2, blocking collectives, exchange(): return lax.all_to_all(pieces, 'dp', split_axis=0, concat_axis=0, tiled=True)  94.2 us
    all_to_all x3, waiting for transfers between devices, exchange(): return lax.all_to_all(pieces, 'dp', split_axis=0, concat_axis=0, tiled=True)  44.1 us
    all_to_all x3, starting transfers between devices, exchange(): return lax.all_to_all(pieces, 'dp', split_axis=0, concat_axis=0, tiled=True)  17.9 us
    pallas_call x1, Pallas kernels, gather_up(): pl.pallas_call(gather_up_kernel, out_shape=jax.ShapeDtypeStruct((count,)...  9.86 us
    pallas_call x1, Pallas kernels, down_gradients(): pl.pallas_call(down_gradient_kernel, out_shape=jax.ShapeDtypeStruct((num_...  9.01 us
    pallas_call x1, Pallas kernels, input_slices(): pl.pallas_call(input_kernel, out_shape=jax.ShapeDtypeStruct((count, rows,...  6.16 us
    pallas_call x1, Pallas kernels, hidden_parts(): pl.pallas_call(hidden_kernel, out_shape=jax.ShapeDtypeStruct((count, rows...  4.65 us
  transfers between devices with their start and end apart: 4, of which 3 were waited for; matrix products, arithmetic and copies ran while one was open for 0% of the time, Pallas kernels for 12%

profile of v1, /device:TPU:13, one launch (start us, length us, event | category | flops | bytes accessed | tf_op | source)
XLA Modules:
  0.0 215.9 jit_solution(8988090700822613617)
XLA Ops:
  7.2 9.9 %gather_up.1 = bf16[16,64,128]{2,1,0:T(8,128)(2,1)} custom-call(s32[16]{0:T(128)} %adapters.13, bf16[64,64,128]{2,1,0:T(8,128)(2,1)} %up_maps.1), custom_call_target="tpu_custom_call" | custom-call | tf_op jit(solution)/shard_map/gather_up/pallas_call | solution.py:32
  17.0 6.6 %all-to-all-start = ((bf16[16,64,128]{2,1,0:T(8,128)(2,1)}), bf16[16,64,128]{2,1,0:T(8,128)(2,1)S(1)}, u32[]{:S(2)}, u32[]{:S(2)}) async-start(bf16[16,64,128]{2,1,0:T(8,128)(2,1)} %gather_up.1), calls=%async_computation | async-start | bytes 524288 | tf_op jit(solution)/shard_map/all_to_all | solution.py:343
  23.6 0.0 all-gather.2.cloned.1.call-start
  23.6 0.0 copy-start.2
  23.7 0.0 copy-start.3
  23.7 0.0 copy-start.4
  23.7 3.8 %split_columns.1 = bf16[16,128,512]{2,1,0:T(8,128)(2,1)} custom-call(bf16[128,8192]{1,0:T(8,128)(2,1)} %source.1), custom_call_target="tpu_custom_call" | custom-call | tf_op jit(solution)/shard_map/split_columns/pallas_call | solution.py:56
  27.5 4.0 %all-to-all-done = bf16[16,64,128]{2,1,0:T(8,128)(2,1)S(1)} async-done(((bf16[16,64,128]{2,1,0:T(8,128)(2,1)}), bf16[16,64,128]{2,1,0:T(8,128)(2,1)S(1)}, u32[]{:S(2)}, u32[]{:S(2)}) %all-to-all-start) | async-done | bytes 262176 | tf_op jit(solution)/shard_map/all_to_all | solution.py:343
  31.5 0.0 copy-done.2
  31.6 0.0 copy-done.3
  31.6 0.0 copy-done.4
  31.6 1.5 back_low.1
  33.0 0.0 all-gather.2.cloned.1.call-update
  33.1 81.5 %all_to_all.25.tokens = bf16[16,128,512]{2,1,0:T(8,128)(2,1)S(1)} all-to-all(bf16[16,128,512]{2,1,0:T(8,128)(2,1)} %split_columns.1), channel_id=1, replica_groups=mesh['groups'=2,'dp'=16] {'dp'}, dimensions={0} | all-to-all | bytes 4194304 | tf_op jit(solution)/shard_map/all_to_all | solution.py:343
  114.6 4.7 %hidden_parts.1 = bf16[16,128,128]{2,1,0:T(8,128)(2,1)} custom-call(s32[16]{0:T(128)S(1)} %copy-done.3, bf16[16,128,512]{2,1,0:T(8,128)(2,1)S(1)} %all_to_all.25.tokens, bf16[64,128,512]{2,1,0:T(8,128)(2,1)} %refs_3_.3, bf16[64,128,512]{2,1,0:T(8,128)(2,1)} %refs_3_.3, bf16[64,128,512]{2,1,0:T(8,128)(2,1)} %refs_3_.3, bf16[64,128,512]{2,1,0:T(8,128)(2,1)} %refs_3_.3), custom_call_target="tpu_custom_call" | custom-call | tf_op jit(solution)/shard_map/hidden_parts/pallas_call | solution.py:143
  119.2 5.0 %all-to-all-start.2 = ((bf16[16,128,128]{2,1,0:T(8,128)(2,1)}), bf16[16,128,128]{2,1,0:T(8,128)(2,1)S(1)}, u32[]{:S(2)}, u32[]{:S(2)}) async-start(bf16[16,128,128]{2,1,0:T(8,128)(2,1)} %hidden_parts.1), calls=%async_computation.2 | async-start | bytes 1048576 | tf_op jit(solution)/shard_map/all_to_all | solution.py:343
  124.2 0.0 all-gather.2.cloned.1.call-done.gathered
  124.2 0.0 copy-start.1
  124.2 1.2 copy-done.1
  125.4 6.2 %input_slices.1 = bf16[16,128,512]{2,1,0:T(8,128)(2,1)S(1)} custom-call(s32[16]{0:T(128)S(1)} %copy-done.3, bf16[2048,1152]{1,0:T(8,128)(2,1)} %all-gather.2.cloned.1.call-done.gathered, bf16[1024,512]{1,0:T(8,128)(2,1)S(1)} %copy-done.1, bf16[64,128,512]{2,1,0:T(8,128)(2,1)} %refs_3_.3, bf16[64,128,512]{2,1,0:T(8,128)(2,1)} %refs_3_.3, ...), custom_call_target="tpu_custom_call" | custom-call | tf_op jit(solution)/shard_map/input_slices/pallas_call | solution.py:174
  131.6 0.0 copy-start
  131.6 1.3 copy-done
  132.9 4.9 %all-to-all-done.2.parts = bf16[16,128,128]{2,1,0:T(8,128)(2,1)S(1)} async-done(((bf16[16,128,128]{2,1,0:T(8,128)(2,1)}), bf16[16,128,128]{2,1,0:T(8,128)(2,1)S(1)}, u32[]{:S(2)}, u32[]{:S(2)}) %all-to-all-start.2) | async-done | bytes 524320 | tf_op jit(solution)/shard_map/all_to_all | solution.py:343
  137.8 0.8 up_piece.1
  138.6 12.7 %all_to_all.26.pieces = bf16[16,64,128]{2,1,0:T(8,128)(2,1)S(1)} all-to-all(bf16[16,64,128]{2,1,0:T(8,128)(2,1)S(1)} %bitcast.3), channel_id=1, replica_groups=mesh['groups'=2,'dp'=16] {'dp'}, dimensions={0} | all-to-all | bytes 524288 | tf_op jit(solution)/shard_map/all_to_all | solution.py:343
  151.3 6.4 %all-to-all-start.3 = ((bf16[16,128,512]{2,1,0:T(8,128)(2,1)}), bf16[16,128,512]{2,1,0:T(8,128)(2,1)}, u32[]{:S(2)}, u32[]{:S(2)}) async-start(bf16[16,128,512]{2,1,0:T(8,128)(2,1)} %copy-done), calls=%async_computation.3 | async-start | bytes 4194304 | tf_op jit(solution)/shard_map/all_to_all | solution.py:343
  157.7 9.0 %down_gradients.1 = bf16[64,128,512]{2,1,0:T(8,128)(2,1)} custom-call(s32[16]{0:T(128)S(1)} %copy-done.3, bf16[2048,1152]{1,0:T(8,128)(2,1)} %all-gather.2.cloned.1.call-done.gathered, bf16[16,128,512]{2,1,0:T(8,128)(2,1)S(1)} %all_to_all.25.tokens), custom_call_target="tpu_custom_call" | custom-call | tf_op jit(solution)/shard_map/down_gradients/pallas_call | solution.py:288
  166.7 3.3 %up_gradients.1 = bf16[64,64,128]{2,1,0:T(8,128)(2,1)} custom-call(s32[16]{0:T(128)S(1)} %copy-done.3, bf16[16,64,128]{2,1,0:T(8,128)(2,1)S(1)} %all_to_all.26.pieces), custom_call_target="tpu_custom_call" | custom-call | tf_op jit(solution)/shard_map/up_gradients/pallas_call | solution.py:323
  170.0 35.2 %all-to-all-done.3.source = bf16[16,128,512]{2,1,0:T(8,128)(2,1)} async-done(((bf16[16,128,512]{2,1,0:T(8,128)(2,1)}), bf16[16,128,512]{2,1,0:T(8,128)(2,1)}, u32[]{:S(2)}, u32[]{:S(2)}) %all-to-all-start.3) | async-done | bytes 2097184 | tf_op jit(solution)/shard_map/all_to_all | solution.py:343
  205.3 3.8 %join_columns.1 = bf16[128,8192]{1,0:T(8,128)(2,1)} custom-call(bf16[16,128,512]{2,1,0:T(8,128)(2,1)} %all-to-all-done.3.source), custom_call_target="tpu_custom_call" | custom-call | tf_op jit(solution)/shard_map/join_columns/pallas_call | solution.py:75
Async XLA Ops:
  17.0 14.5 %all-to-all-start = ((bf16[16,64,128]{2,1,0:T(8,128)(2,1)}), bf16[16,64,128]{2,1,0:T(8,128)(2,1)S(1)}, u32[]{:S(2)}, u32[]{:S(2)}) async-start(bf16[16,64,128]{2,1,0:T(8,128)(2,1)} %gather_up.1), calls=%async_computation | async-start | bytes 524288 | tf_op jit(solution)/shard_map/all_to_all | solution.py:343
  23.6 100.6 %all-gather.2.cloned.1.call-start = ((), (), s32[]{:S(2)}) async-start(), calls=%async_computation.5 | async-start | bytes 5013504 | tf_op jit(solution)/shard_map/all_gather | solution.py:358
  23.6 7.9 %copy-start.2 = (bf16[128,1024]{1,0:T(8,128)(2,1)S(1)}, bf16[128,1024]{1,0:T(8,128)(2,1)}, u32[]{:S(2)}) copy-start(bf16[128,1024]{1,0:T(8,128)(2,1)} %gradient.3) | copy-start | bytes 786436
  23.7 7.9 %copy-start.3 = (s32[16]{0:T(128)S(1)}, s32[16]{0:T(128)}, u32[]{:S(2)}) copy-start(s32[16]{0:T(128)} %adapters.13) | copy-start | bytes 196
  23.7 7.9 %copy-start.4 = (s32[64]{0:T(128)S(1)}, s32[64]{0:T(128)}, u32[]{:S(2)}) copy-start(s32[64]{0:T(128)} %ranks.3) | copy-start | bytes 772
  119.2 18.5 %all-to-all-start.2 = ((bf16[16,128,128]{2,1,0:T(8,128)(2,1)}), bf16[16,128,128]{2,1,0:T(8,128)(2,1)S(1)}, u32[]{:S(2)}, u32[]{:S(2)}) async-start(bf16[16,128,128]{2,1,0:T(8,128)(2,1)} %hidden_parts.1), calls=%async_computation.2 | async-start | bytes 1048576 | tf_op jit(solution)/shard_map/all_to_all | solution.py:343
  124.2 1.2 copy-start.1
  131.6 1.3 copy-start
  151.3 53.9 %all-to-all-start.3 = ((bf16[16,128,512]{2,1,0:T(8,128)(2,1)}), bf16[16,128,512]{2,1,0:T(8,128)(2,1)}, u32[]{:S(2)}, u32[]{:S(2)}) async-start(bf16[16,128,512]{2,1,0:T(8,128)(2,1)} %copy-done), calls=%async_computation.3 | async-start | bytes 4194304 | tf_op jit(solution)/shard_map/all_to_all | solution.py:343
Sparse Core Ops, SparseCore 0:
  33.2 75.6 all-gather.1

commit v2 on v1

v2 whole, which is shorter than its diff:
```python
import functools

import jax
import jax.numpy as jnp
from jax import lax
from jax.experimental import pallas as pl
from jax.experimental.pallas import tpu as pltpu
from jax.sharding import PartitionSpec as P

adapter_alpha = 32.0
vmem_limit = 48 * 1024 * 1024


def group_of(count):
    return 4 if count % 4 == 0 else 1


def order_of(slot, place, count):
    block = place
    bits = count.bit_length() - 1
    for bit in range(bits):
        block = block ^ (((slot >> bit) & 1) << (bits - 1 - bit))
    return block


def gather_up_kernel(adapters, *refs):
    out = refs[-1]
    for offset in range(out.shape[0]):
        out[offset] = refs[offset][0]


def gather_up(adapters, up_maps):
    count = adapters.shape[0]
    step = 16 if count % 16 == 0 else 1

    def spec(offset):
        return pl.BlockSpec(
            (1,) + up_maps.shape[1:], lambda i, adapters: (adapters[i * step + offset], 0, 0)
        )

    return pl.pallas_call(
        gather_up_kernel,
        out_shape=jax.ShapeDtypeStruct((count,) + up_maps.shape[1:], up_maps.dtype),
        grid_spec=pltpu.PrefetchScalarGridSpec(
            num_scalar_prefetch=1,
            grid=(count // step,),
            in_specs=[spec(offset) for offset in range(step)],
            out_specs=pl.BlockSpec((step,) + up_maps.shape[1:], lambda i, _: (i, 0, 0)),
        ),
        name="gather_up",
    )(adapters, *([up_maps] * step))


def split_kernel(source, out):
    width = out.shape[2]
    for piece in range(out.shape[0]):
        out[piece] = source[:, piece * width : (piece + 1) * width]


def split_columns(source, pieces):
    rows, columns = source.shape
    width = columns // pieces
    step = group_of(pieces)
    return pl.pallas_call(
        split_kernel,
        out_shape=jax.ShapeDtypeStruct((pieces, rows, width), source.dtype),
        grid=(pieces // step,),
        in_specs=[pl.BlockSpec((rows, step * width), lambda i: (0, i))],
        out_specs=pl.BlockSpec((step, rows, width), lambda i: (i, 0, 0)),
        name="split_columns",
    )(source)


def join_kernel(source, out):
    width = source.shape[2]
    for piece in range(source.shape[0]):
        out[:, piece * width : (piece + 1) * width] = source[piece]


def join_columns(source):
    pieces, rows, width = source.shape
    step = group_of(pieces)
    return pl.pallas_call(
        join_kernel,
        out_shape=jax.ShapeDtypeStruct((rows, pieces * width), source.dtype),
        grid=(pieces // step,),
        in_specs=[pl.BlockSpec((step, rows, width), lambda i: (i, 0, 0))],
        out_specs=pl.BlockSpec((rows, step * width), lambda i: (0, i)),
        name="join_columns",
    )(source)


def rank_row(ranks, adapter, extent):
    rank = jnp.full((1, extent), ranks[adapter], jnp.int32)
    alive = (lax.broadcasted_iota(jnp.int32, (1, extent), 1) < rank).astype(jnp.float32)
    return alive, adapter_alpha / rank.astype(jnp.float32)


def back_kernel(adapters, ranks, place, gradient, up, out):
    alive, factor = rank_row(ranks, adapters[place[0]], up.shape[1])
    back = jnp.dot(gradient[...], up[...], preferred_element_type=jnp.float32)
    out[0] = (factor * back * alive).astype(out.dtype)


def back_rows(adapters, ranks, place, gradient, up):
    rows = gradient.shape[0]
    extent = up.shape[1]
    return pl.pallas_call(
        back_kernel,
        out_shape=jax.ShapeDtypeStruct((1, rows, extent), jnp.bfloat16),
        grid_spec=pltpu.PrefetchScalarGridSpec(
            num_scalar_prefetch=3,
            grid=(1,),
            in_specs=[
                pl.BlockSpec(gradient.shape, lambda i, *_: (0, 0)),
                pl.BlockSpec(up.shape, lambda i, *_: (0, 0)),
            ],
            out_specs=pl.BlockSpec((1, rows, extent), lambda i, *_: (0, 0, 0)),
        ),
        compiler_params=pltpu.CompilerParams(vmem_limit_bytes=vmem_limit),
        name="back_low",
    )(adapters, ranks, place, gradient, up)


def down_specs(step, count, down_maps):
    def spec(offset):
        return pl.BlockSpec(
            (1,) + down_maps.shape[1:],
            lambda i, adapters, place: (
                adapters[order_of(i * step + offset, place[0], count)],
                0,
                0,
            ),
        )

    return [spec(offset) for offset in range(step)]


def hidden_kernel(adapters, place, tokens, *refs):
    out = refs[-1]
    step = out.shape[0]
    count = tokens.shape[0]
    for offset in range(step):
        block = order_of(pl.program_id(0) * step + offset, place[0], count)
        out[offset] = lax.dot_general(
            tokens[block],
            refs[offset][0],
            (((1,), (1,)), ((), ())),
            preferred_element_type=jnp.float32,
        )


def hidden_parts(adapters, place, tokens, down_maps):
    count, rows, width = tokens.shape
    step = group_of(count)
    extent = down_maps.shape[1]
    return pl.pallas_call(
        hidden_kernel,
        out_shape=jax.ShapeDtypeStruct((count, rows, extent), jnp.float32),
        grid_spec=pltpu.PrefetchScalarGridSpec(
            num_scalar_prefetch=2,
            grid=(count // step,),
            in_specs=[pl.BlockSpec((count, rows, width), lambda i, *_: (0, 0, 0))]
            + down_specs(step, count, down_maps),
            out_specs=pl.BlockSpec((step, rows, extent), lambda i, *_: (i, 0, 0)),
        ),
        compiler_params=pltpu.CompilerParams(vmem_limit_bytes=vmem_limit),
        name="hidden_parts",
    )(adapters, place, tokens, *([down_maps] * step))


def input_kernel(adapters, place, gradients, backs, weight, *refs):
    out = refs[-1]
    count = out.shape[0]
    step, rows, depth = gradients.shape
    frozen = jnp.dot(
        gradients[...].reshape(step * rows, depth),
        weight[...],
        preferred_element_type=jnp.float32,
    )
    for offset in range(step):
        block = order_of(pl.program_id(0) * step + offset, place[0], count)
        adapter = jnp.dot(backs[offset], refs[offset][0], preferred_element_type=jnp.float32)
        out[block] = (frozen[offset * rows : (offset + 1) * rows] + adapter).astype(out.dtype)


def input_slices(adapters, place, gradients, backs, weight, down_maps):
    count, rows, depth = gradients.shape
    step = group_of(count)
    extent = backs.shape[2]
    width = weight.shape[1]
    return pl.pallas_call(
        input_kernel,
        out_shape=jax.ShapeDtypeStruct((count, rows, width), jnp.bfloat16),
        grid_spec=pltpu.PrefetchScalarGridSpec(
            num_scalar_prefetch=2,
            grid=(count // step,),
            in_specs=[
                pl.BlockSpec((step, rows, depth), lambda i, *_: (i, 0, 0)),
                pl.BlockSpec((step, rows, extent), lambda i, *_: (i, 0, 0)),
                pl.BlockSpec(weight.shape, lambda i, *_: (0, 0)),
            ]
            + down_specs(step, count, down_maps),
            out_specs=pl.BlockSpec((count, rows, width), lambda i, *_: (0, 0, 0)),
        ),
        compiler_params=pltpu.CompilerParams(vmem_limit_bytes=vmem_limit),
        name="input_slices",
    )(adapters, place, gradients, backs, weight, *([down_maps] * step))


def hidden_low_kernel(adapters, ranks, place, kept, received, out):
    alive, _ = rank_row(ranks, adapters[place[0]], out.shape[2])
    out[0] = ((kept[0] + received[0]) * alive).astype(out.dtype)


def hidden_rows(adapters, ranks, place, kept, received):
    whole = pl.BlockSpec(kept.shape, lambda i, *_: (0, 0, 0))
    return pl.pallas_call(
        hidden_low_kernel,
        out_shape=jax.ShapeDtypeStruct(kept.shape, jnp.bfloat16),
        grid_spec=pltpu.PrefetchScalarGridSpec(
            num_scalar_prefetch=3, grid=(1,), in_specs=[whole, whole], out_specs=whole
        ),
        name="hidden_low",
    )(adapters, ranks, place, kept, received)


def list_members(adapters, place, head, following):
    count = following.shape[0]

    def clear(adapter, carry):
        head[adapter] = -1
        return carry

    lax.fori_loop(0, head.shape[0], clear, 0)

    def link(step, carry):
        slot = count - 1 - step
        adapter = adapters[order_of(slot, place[0], count)]
        following[slot] = head[adapter]
        head[adapter] = slot
        return carry

    lax.fori_loop(0, count, link, 0)


def sum_members(head, following, total, out, term, finish):
    chunk = out.shape[0]

    def per_adapter(entry, carry):
        adapter = pl.program_id(0) * chunk + entry
        first = head[adapter]

        @pl.when(first < 0)
        def _():
            out[entry] = jnp.zeros(out.shape[1:], out.dtype)

        @pl.when(first >= 0)
        def _():
            total[...] = term(first)

            def more(slot):
                total[...] += term(slot)
                return following[slot]

            lax.while_loop(lambda slot: slot >= 0, more, following[first])
            out[entry] = finish(adapter).astype(out.dtype)

        return carry

    lax.fori_loop(0, chunk, per_adapter, 0)


def down_gradient_kernel(adapters, place, backs, tokens, out, head, following, total):
    count = tokens.shape[0]

    @pl.when(pl.program_id(0) == 0)
    def _():
        list_members(adapters, place, head, following)

    def term(slot):
        return lax.dot_general(
            backs[slot],
            tokens[order_of(slot, place[0], count)],
            (((0,), (0,)), ((), ())),
            preferred_element_type=jnp.float32,
        )

    sum_members(head, following, total, out, term, lambda adapter: total[...])


def down_gradients(adapters, place, backs, tokens, num_adapters):
    count, rows, width = tokens.shape
    extent = backs.shape[2]
    chunk = 8 if num_adapters % 8 == 0 else 1
    return pl.pallas_call(
        down_gradient_kernel,
        out_shape=jax.ShapeDtypeStruct((num_adapters, extent, width), jnp.bfloat16),
        grid_spec=pltpu.PrefetchScalarGridSpec(
            num_scalar_prefetch=2,
            grid=(num_adapters // chunk,),
            in_specs=[
                pl.BlockSpec(backs.shape, lambda i, *_: (0, 0, 0)),
                pl.BlockSpec(tokens.shape, lambda i, *_: (0, 0, 0)),
            ],
            out_specs=pl.BlockSpec((chunk, extent, width), lambda i, *_: (i, 0, 0)),
            scratch_shapes=[
                pltpu.SMEM((num_adapters,), jnp.int32),
                pltpu.SMEM((count,), jnp.int32),
                pltpu.VMEM((extent, width), jnp.float32),
            ],
        ),
        compiler_params=pltpu.CompilerParams(vmem_limit_bytes=vmem_limit),
        name="down_gradients",
    )(adapters, place, backs, tokens)


def up_gradient_kernel(
    adapters, place, ranks, gradients, hiddens, out, head, following, total
):
    width = out.shape[1]
    lanes = gradients.shape[2]
    extent = out.shape[2]

    @pl.when(pl.program_id(0) == 0)
    def _():
        list_members(adapters, place, head, following)

    def term(slot):
        return lax.dot_general(
            gradients[slot],
            hiddens[slot],
            (((0,), (0,)), ((), ())),
            preferred_element_type=jnp.float32,
        )

    def finish(adapter):
        _, factor = rank_row(ranks, adapter, extent)
        inside = lax.rem(place[0], lanes // width) * width
        return factor * total[pl.ds(pl.multiple_of(inside, width), width), :]

    sum_members(head, following, total, out, term, finish)


def up_gradients(adapters, place, ranks, gradients, hiddens, width):
    count, rows, _ = gradients.shape
    extent = hiddens.shape[2]
    num_adapters = ranks.shape[0]
    lanes = 128 if width < 128 else width
    chunk = 32 if num_adapters % 32 == 0 else 1
    return pl.pallas_call(
        up_gradient_kernel,
        out_shape=jax.ShapeDtypeStruct((num_adapters, width, extent), jnp.bfloat16),
        grid_spec=pltpu.PrefetchScalarGridSpec(
            num_scalar_prefetch=3,
            grid=(num_adapters // chunk,),
            in_specs=[
                pl.BlockSpec(
                    (count, rows, lanes),
                    lambda i, adapters, place, ranks: (0, 0, place[0] * width // lanes),
                ),
                pl.BlockSpec(hiddens.shape, lambda i, *_: (0, 0, 0)),
            ],
            out_specs=pl.BlockSpec((chunk, width, extent), lambda i, *_: (i, 0, 0)),
            scratch_shapes=[
                pltpu.SMEM((num_adapters,), jnp.int32),
                pltpu.SMEM((count,), jnp.int32),
                pltpu.VMEM((lanes, extent), jnp.float32),
            ],
        ),
        compiler_params=pltpu.CompilerParams(vmem_limit_bytes=vmem_limit),
        name="up_gradients",
    )(adapters, place, ranks, gradients, hiddens)


def exchange(pieces):
    return lax.all_to_all(pieces, "dp", split_axis=0, concat_axis=0, tiled=True)


def swap(array, distance):
    devices = lax.axis_size("dp")
    return lax.ppermute(array, "dp", [(i, i ^ distance) for i in range(devices)])


def gather_blocks(own):
    distance = lax.axis_size("dp") // 2
    while distance:
        own = jnp.concatenate([own, swap(own, distance)], axis=0)
        distance //= 2
    return own


def reduce_blocks(parts):
    devices = lax.axis_size("dp")
    distance = 1
    while True:
        half = parts.shape[0] // 2
        kept, received = parts[:half], swap(parts[half:], distance)
        distance *= 2
        if distance == devices:
            return kept, received
        parts = kept + received


def local(tokens, output_gradient, value_weight, down_maps, up_maps, adapter_per_block, ranks):
    devices = lax.axis_size("dp")
    num_adapters, extent, _ = down_maps.shape
    rows, width = output_gradient.shape
    place = lax.axis_index("dp").astype(jnp.int32).reshape(1)

    own_up = exchange(gather_up(adapter_per_block, up_maps)).reshape(width, extent)
    gradients = gather_blocks(output_gradient.reshape(1, rows, width))
    token_pieces = split_columns(tokens, devices)
    token_pieces, own_up = lax.optimization_barrier((token_pieces, own_up))
    token_blocks = exchange(token_pieces)

    backs = gather_blocks(back_rows(adapter_per_block, ranks, place, output_gradient, own_up))
    slices = input_slices(adapter_per_block, place, gradients, backs, value_weight, down_maps)
    slices, token_blocks = lax.optimization_barrier((slices, token_blocks))
    input_grad = join_columns(exchange(slices))

    parts = hidden_parts(adapter_per_block, place, token_blocks, down_maps)
    kept, received = reduce_blocks(parts)
    hiddens = gather_blocks(hidden_rows(adapter_per_block, ranks, place, kept, received))
    down_gradient = down_gradients(
        adapter_per_block, place, backs, token_blocks, num_adapters
    )
    up_gradient = up_gradients(
        adapter_per_block, place, ranks, gradients, hiddens, width // devices
    )
    return (input_grad, down_gradient, up_gradient)


def solution(mesh):
    in_specs = (
        P(("groups", "dp"), None),
        P(("groups", "dp"), None),
        P(None, "dp"),
        P(None, None, "dp"),
        P(None, "dp", None),
        P("groups"),
        P(),
    )
    out_specs = (P(("groups", "dp"), None), P("groups", None, "dp"), P("groups", "dp", None))
    return jax.shard_map(local, mesh=mesh, in_specs=in_specs, out_specs=out_specs, check_vma=False)
```

time: 217 us -> 203 us (0.935)
  the two profiles are of different devices: /device:TPU:13 before, /device:TPU:0 now
where the time goes in v2:
time: 203 us; the launch traced here: 202 us
  waiting for transfers between devices  120 us (59%)
  Pallas kernels  38.3 us (19%)
  starting transfers between devices  31.5 us (16%)
  local copies, waits for them, and re-layouts  7.69 us (4%)
  other arithmetic  4.19 us (2%)
    ppermute x16, waiting for transfers between devices, swap(): lax.ppermute(array, 'dp', [(i, i ^ distance) for i in range(devices)])  120 us
    ppermute x16, starting transfers between devices, swap(): lax.ppermute(array, 'dp', [(i, i ^ distance) for i in range(devices)])  17.3 us
    all_to_all x3, starting transfers between devices, exchange(): return lax.all_to_all(pieces, 'dp', split_axis=0, concat_axis=0, tiled=True)  14.2 us
    pallas_call x1, Pallas kernels, down_gradients(): pl.pallas_call(down_gradient_kernel, out_shape=jax.ShapeDtypeStruct((num_...  9.17 us
    pallas_call x1, Pallas kernels, up_gradients(): pl.pallas_call(up_gradient_kernel, out_shape=jax.ShapeDtypeStruct((num_ad...  6.4 us
    pallas_call x1, Pallas kernels, input_slices(): pl.pallas_call(input_kernel, out_shape=jax.ShapeDtypeStruct((count, rows,...  6.15 us
    unnamed x38, local copies, waits for them, and re-layouts  5.16 us
    concatenate x9, other arithmetic, gather_blocks(): own = jnp.concatenate([own, swap(own, distance)], axis=0)  4.08 us
  transfers between devices with their start and end apart: 19, of which 14 were waited for; matrix products, arithmetic and copies ran while one was open for 3% of the time, Pallas kernels for 17%

profile of v2, /device:TPU:0, one launch (start us, length us, event | category | flops | bytes accessed | tf_op | source)
XLA Modules:
  0.0 202.3 jit_solution(2088662260386838558)
XLA Ops:
  0.6 4.1 %collective-permute-start = (bf16[1,128,1024]{2,1,0:T(8,128)(2,1)}, bf16[1,128,1024]{2,1,0:T(8,128)(2,1)S(1)}, u32[]{:S(2)}, u32[]{:S(2)}) collective-permute-start(bf16[1,128,1024]{2,1,0:T(8,128)(2,1)} %bitcast.4), channel_id=1, source_target_pairs={{0,8},{1,9},{2,10},{3,11},{4,12},{5,13},{6,14},{7,15},{8,0},{9,1},... | collective-permute-start | bytes 786440 | tf_op jit(solution)/shard_map/ppermute | solution.py:382
  4.7 2.3 %gather_up.1 = bf16[16,64,128]{2,1,0:T(8,128)(2,1)} custom-call(s32[16]{0:T(128)} %adapters.13, bf16[64,64,128]{2,1,0:T(8,128)(2,1)} %refs_15_.1, bf16[64,64,128]{2,1,0:T(8,128)(2,1)} %refs_15_.1, bf16[64,64,128]{2,1,0:T(8,128)(2,1)} %refs_15_.1, bf16[64,64,128]{2,1,0:T(8,128)(2,1)} %refs_15_.1, bf16[64,64,128]{2,1,0:T(8,128)(2,1)} %refs_15_.1, ...), custom_call_target="tpu_custom_call" | custom-call | tf_op jit(solution)/shard_map/gather_up/pallas_call | solution.py:41
  7.0 3.9 %all-to-all-start = ((bf16[16,64,128]{2,1,0:T(8,128)(2,1)}), bf16[16,64,128]{2,1,0:T(8,128)(2,1)S(1)}, u32[]{:S(2)}, u32[]{:S(2)}) async-start(bf16[16,64,128]{2,1,0:T(8,128)(2,1)} %gather_up.1), calls=%async_computation | async-start | bytes 524288 | tf_op jit(solution)/shard_map/all_to_all | solution.py:377
  10.9 9.6 %collective-permute-done = bf16[1,128,1024]{2,1,0:T(8,128)(2,1)S(1)} collective-permute-done((bf16[1,128,1024]{2,1,0:T(8,128)(2,1)}, bf16[1,128,1024]{2,1,0:T(8,128)(2,1)S(1)}, u32[]{:S(2)}, u32[]{:S(2)}) %collective-permute-start) | collective-permute-done | bytes 262176 | tf_op jit(solution)/shard_map/ppermute | solution.py:382
  20.6 0.8 pad_maximum_fusion.2
  21.4 3.8 %split_columns.1 = bf16[16,128,512]{2,1,0:T(8,128)(2,1)} custom-call(bf16[128,8192]{1,0:T(8,128)(2,1)} %source.1), custom_call_target="tpu_custom_call" | custom-call | tf_op jit(solution)/shard_map/split_columns/pallas_call | solution.py:64
  25.2 5.6 %all-to-all-start.1 = ((bf16[16,128,512]{2,1,0:T(8,128)(2,1)}), bf16[16,128,512]{2,1,0:T(8,128)(2,1)S(1)}, u32[]{:S(2)}, u32[]{:S(2)}) async-start(bf16[16,128,512]{2,1,0:T(8,128)(2,1)} %split_columns.1), calls=%async_computation.1 | async-start | bytes 4194304 | tf_op jit(solution)/shard_map/all_to_all | solution.py:377
  30.9 3.2 %collective-permute-done.1 = bf16[2,128,1024]{2,1,0:T(8,128)(2,1)S(1)} collective-permute-done((bf16[2,128,1024]{2,1,0:T(8,128)(2,1)}, bf16[2,128,1024]{2,1,0:T(8,128)(2,1)S(1)}, u32[]{:S(2)}, u32[]{:S(2)}) %collective-permute-start.1) | collective-permute-done | bytes 524320 | tf_op jit(solution)/shard_map/ppermute | solution.py:382
  34.1 0.1 pad_maximum_fusion.1
  34.2 1.4 collective-permute-start.2
  35.6 43.3 %collective-permute-done.2 = bf16[4,128,1024]{2,1,0:T(8,128)(2,1)S(1)} collective-permute-done((bf16[4,128,1024]{2,1,0:T(8,128)(2,1)S(1)}, bf16[4,128,1024]{2,1,0:T(8,128)(2,1)S(1)}, u32[]{:S(2)}, u32[]{:S(2)}) %collective-permute-start.2) | collective-permute-done | bytes 1048608 | tf_op jit(solution)/shard_map/ppermute | solution.py:382
  78.9 1.0 copy-done.9
  79.9 1.5 pad_maximum_fusion
  81.4 0.8 back_low.1
  82.2 0.5 collective-permute-start.4
  82.7 4.3 %collective-permute-done.4 = bf16[1,128,128]{2,1,0:T(8,128)(2,1)S(1)} collective-permute-done((bf16[1,128,128]{2,1,0:T(8,128)(2,1)S(1)}, bf16[1,128,128]{2,1,0:T(8,128)(2,1)S(1)}, u32[]{:S(2)}, u32[]{:S(2)}) %collective-permute-start.4) | collective-permute-done | bytes 32800 | tf_op jit(solution)/shard_map/ppermute | solution.py:382
  87.1 1.5 collective-permute-start.5
  88.6 2.8 %collective-permute-done.5 = bf16[2,128,128]{2,1,0:T(8,128)(2,1)S(1)} collective-permute-done((bf16[2,128,128]{2,1,0:T(8,128)(2,1)S(1)}, bf16[2,128,128]{2,1,0:T(8,128)(2,1)S(1)}, u32[]{:S(2)}, u32[]{:S(2)}) %collective-permute-start.5) | collective-permute-done | bytes 65568 | tf_op jit(solution)/shard_map/ppermute | solution.py:382
  91.4 1.0 collective-permute-start.6
  92.5 4.0 %collective-permute-done.6 = bf16[4,128,128]{2,1,0:T(8,128)(2,1)S(1)} collective-permute-done((bf16[4,128,128]{2,1,0:T(8,128)(2,1)S(1)}, bf16[4,128,128]{2,1,0:T(8,128)(2,1)S(1)}, u32[]{:S(2)}, u32[]{:S(2)}) %collective-permute-start.6) | collective-permute-done | bytes 131104 | tf_op jit(solution)/shard_map/ppermute | solution.py:382
  96.5 0.1 collective-permute-start.7
  96.7 1.4 collective-permute-done.7
  98.3 1.8 constant_dynamic-update-slice_fusion.gradients
  100.0 2.0 copy-done
  102.0 6.2 %input_slices.1 = bf16[16,128,512]{2,1,0:T(8,128)(2,1)S(1)} custom-call(s32[16]{0:T(128)S(1)} %copy-done.5, s32[1]{0:T(128)} %bitcast.place, bf16[16,128,1024]{2,1,0:T(8,128)(2,1)} %copy-done, bf16[16,128,128]{2,1,0:T(8,128)(2,1)S(1)} %constant_dynamic-update-slice_fusion.5.backs, bf16[1024,512]{1,0:T(8,128)(2,1)S(1)} %copy-done.4, ...), custom_call_target="tpu_custom_call" | custom-call | tf_op jit(solution)/shard_map/input_slices/pallas_call | solution.py:192
  108.2 1.3 copy-done.2
  109.5 4.7 %all-to-all-start.2 = ((bf16[16,128,512]{2,1,0:T(8,128)(2,1)}), bf16[16,128,512]{2,1,0:T(8,128)(2,1)}, u32[]{:S(2)}, u32[]{:S(2)}) async-start(bf16[16,128,512]{2,1,0:T(8,128)(2,1)} %copy-done.2), calls=%async_computation.2 | async-start | bytes 4194304 | tf_op jit(solution)/shard_map/all_to_all | solution.py:377
  114.2 3.9 %hidden_parts.1 = f32[16,128,128]{2,1,0:T(8,128)S(1)} custom-call(s32[16]{0:T(128)S(1)} %copy-done.5, s32[1]{0:T(128)} %bitcast.place, bf16[16,128,512]{2,1,0:T(8,128)(2,1)S(1)} %all-to-all-done.1.tokens, bf16[64,128,512]{2,1,0:T(8,128)(2,1)} %refs_3_.5, bf16[64,128,512]{2,1,0:T(8,128)(2,1)} %refs_3_.5, bf16[64,128,512]{2,1,0:T(8,128)(2,1)} %refs_3_.5, ...), custom_call_target="tpu_custom_call" | custom-call | tf_op jit(solution)/shard_map/hidden_parts/pallas_call | solution.py:157
  118.1 0.4 collective-permute-start.8
  118.5 1.6 collective-permute-done.8
  120.2 1.9 collective-permute-start.9
  122.1 16.8 %collective-permute-done.9 = f32[4,128,128]{2,1,0:T(8,128)S(1)} collective-permute-done((f32[4,128,128]{2,1,0:T(8,128)S(1)}, f32[4,128,128]{2,1,0:T(8,128)S(1)}, u32[]{:S(2)}, u32[]{:S(2)}) %collective-permute-start.9) | collective-permute-done | bytes 262176 | tf_op jit(solution)/shard_map/ppermute | solution.py:382
  139.0 0.1 collective-permute-start.10
  139.1 12.8 %collective-permute-done.10 = f32[2,128,128]{2,1,0:T(8,128)S(1)} collective-permute-done((f32[2,128,128]{2,1,0:T(8,128)S(1)}, f32[2,128,128]{2,1,0:T(8,128)S(1)}, u32[]{:S(2)}, u32[]{:S(2)}) %collective-permute-start.10) | collective-permute-done | bytes 131104 | tf_op jit(solution)/shard_map/ppermute | solution.py:382
  151.9 0.6 fusion
  152.5 4.5 %collective-permute-start.11 = (f32[1,128,128]{2,1,0:T(8,128)S(1)}, f32[1,128,128]{2,1,0:T(8,128)S(1)}, u32[]{:S(2)}, u32[]{:S(2)}) collective-permute-start(f32[1,128,128]{2,1,0:T(8,128)S(1)} %get-tuple-element.11), channel_id=1, source_target_pairs={{0,8},{1,9},{2,10},{3,11},{4,12},{5,13},{6,14},{7,15},{8,0},{9,1},... | collective-permute-start | bytes 196616 | tf_op jit(solution)/shard_map/ppermute | solution.py:382
  157.0 9.0 %collective-permute-done.11.received = f32[1,128,128]{2,1,0:T(8,128)S(1)} collective-permute-done((f32[1,128,128]{2,1,0:T(8,128)S(1)}, f32[1,128,128]{2,1,0:T(8,128)S(1)}, u32[]{:S(2)}, u32[]{:S(2)}) %collective-permute-start.11) | collective-permute-done | bytes 65568 | tf_op jit(solution)/shard_map/ppermute | solution.py:382
  166.0 0.6 copy-done.12
  166.6 2.2 %hidden_low.1 = bf16[1,128,128]{2,1,0:T(8,128)(2,1)} custom-call(s32[16]{0:T(128)} %adapters.13, s32[64]{0:T(128)} %ranks.5, s32[1]{0:T(128)} %bitcast.place, f32[1,128,128]{2,1,0:T(8,128)} %get-tuple-element.12.kept, f32[1,128,128]{2,1,0:T(8,128)} %copy-done.12), custom_call_target="tpu_custom_call" | custom-call | tf_op jit(solution)/shard_map/hidden_low/pallas_call | solution.py:218
  168.8 5.0 %collective-permute-done.12 = bf16[1,128,128]{2,1,0:T(8,128)(2,1)S(1)} collective-permute-done((bf16[1,128,128]{2,1,0:T(8,128)(2,1)}, bf16[1,128,128]{2,1,0:T(8,128)(2,1)S(1)}, u32[]{:S(2)}, u32[]{:S(2)}) %collective-permute-start.12) | collective-permute-done | bytes 32800 | tf_op jit(solution)/shard_map/ppermute | solution.py:382
  173.8 0.8 pad_maximum_fusion.8
  174.6 4.3 %collective-permute-done.13 = bf16[2,128,128]{2,1,0:T(8,128)(2,1)S(1)} collective-permute-done((bf16[2,128,128]{2,1,0:T(8,128)(2,1)S(1)}, bf16[2,128,128]{2,1,0:T(8,128)(2,1)S(1)}, u32[]{:S(2)}, u32[]{:S(2)}) %collective-permute-start.13) | collective-permute-done | bytes 65568 | tf_op jit(solution)/shard_map/ppermute | solution.py:382
  178.8 0.8 pad_maximum_fusion.6
  179.6 1.6 collective-permute-start.14
  181.3 9.2 %down_gradients.1 = bf16[64,128,512]{2,1,0:T(8,128)(2,1)} custom-call(s32[16]{0:T(128)S(1)} %copy-done.6, s32[1]{0:T(128)} %bitcast.place, bf16[16,128,128]{2,1,0:T(8,128)(2,1)S(1)} %constant_dynamic-update-slice_fusion.5.backs, bf16[16,128,512]{2,1,0:T(8,128)(2,1)S(1)} %all-to-all-done.1.tokens), custom_call_target="tpu_custom_call" | custom-call | tf_op jit(solution)/shard_map/down_gradients/pallas_call | solution.py:296
  190.6 1.5 collective-permute-done.15
  192.2 6.4 %up_gradients.1 = bf16[64,64,128]{2,1,0:T(8,128)(2,1)} custom-call(s32[16]{0:T(128)S(1)} %copy-done.6, s32[1]{0:T(128)} %bitcast.place, s32[64]{0:T(128)S(1)} %copy-done.8, bf16[16,128,1024]{2,1,0:T(8,128)(2,1)S(1)} %copy-done.1, bf16[16,128,128]{2,1,0:T(8,128)(2,1)S(1)} %constant_dynamic-update-slice_fusion.10.hiddens), custom_call_target="tpu_custom_call" | custom-call | tf_op jit(solution)/shard_map/up_gradients/pallas_call | solution.py:351
  198.6 3.8 %join_columns.1 = bf16[128,8192]{1,0:T(8,128)(2,1)} custom-call(bf16[16,128,512]{2,1,0:T(8,128)(2,1)} %all-to-all-done.2.source), custom_call_target="tpu_custom_call" | custom-call | tf_op jit(solution)/shard_map/join_columns/pallas_call | solution.py:83
  (56 shorter events, 0.8 us)
Async XLA Ops:
  0.6 19.9 %copy-start.3 = (bf16[128,1024]{1,0:T(8,128)(2,1)S(1)}, bf16[128,1024]{1,0:T(8,128)(2,1)}, u32[]{:S(2)}) copy-start(bf16[128,1024]{1,0:T(8,128)(2,1)} %gradient.1) | copy-start | bytes 786436
  0.6 19.9 %collective-permute-start = (bf16[1,128,1024]{2,1,0:T(8,128)(2,1)}, bf16[1,128,1024]{2,1,0:T(8,128)(2,1)S(1)}, u32[]{:S(2)}, u32[]{:S(2)}) collective-permute-start(bf16[1,128,1024]{2,1,0:T(8,128)(2,1)} %bitcast.4), channel_id=1, source_target_pairs={{0,8},{1,9},{2,10},{3,11},{4,12},{5,13},{6,14},{7,15},{8,0},{9,1},... | collective-permute-start | bytes 786440 | tf_op jit(solution)/shard_map/ppermute | solution.py:382
  7.0 18.2 %all-to-all-start = ((bf16[16,64,128]{2,1,0:T(8,128)(2,1)}), bf16[16,64,128]{2,1,0:T(8,128)(2,1)S(1)}, u32[]{:S(2)}, u32[]{:S(2)}) async-start(bf16[16,64,128]{2,1,0:T(8,128)(2,1)} %gather_up.1), calls=%async_computation | async-start | bytes 524288 | tf_op jit(solution)/shard_map/all_to_all | solution.py:377
  21.4 12.7 %collective-permute-start.1 = (bf16[2,128,1024]{2,1,0:T(8,128)(2,1)}, bf16[2,128,1024]{2,1,0:T(8,128)(2,1)S(1)}, u32[]{:S(2)}, u32[]{:S(2)}) collective-permute-start(bf16[2,128,1024]{2,1,0:T(8,128)(2,1)} %pad_maximum_fusion.2), channel_id=1, source_target_pairs={{0,4},{1,5},{2,6},{3,7},{4,0},{5,1},{6,2},{7,3},{8,12},{9,13},{10,... | collective-permute-start | bytes 1572872 | tf_op jit(solution)/shard_map/ppermute | solution.py:382
  25.2 84.2 %all-to-all-start.1 = ((bf16[16,128,512]{2,1,0:T(8,128)(2,1)}), bf16[16,128,512]{2,1,0:T(8,128)(2,1)S(1)}, u32[]{:S(2)}, u32[]{:S(2)}) async-start(bf16[16,128,512]{2,1,0:T(8,128)(2,1)} %split_columns.1), calls=%async_computation.1 | async-start | bytes 4194304 | tf_op jit(solution)/shard_map/all_to_all | solution.py:377
  30.8 50.6 %copy-start.5 = (s32[16]{0:T(128)S(1)}, s32[16]{0:T(128)}, u32[]{:S(2)}) copy-start(s32[16]{0:T(128)} %adapters.13) | copy-start | bytes 196
  30.9 50.6 %copy-start.7 = (s32[64]{0:T(128)S(1)}, s32[64]{0:T(128)}, u32[]{:S(2)}) copy-start(s32[64]{0:T(128)} %ranks.5) | copy-start | bytes 772
  34.2 44.7 %collective-permute-start.2 = (bf16[4,128,1024]{2,1,0:T(8,128)(2,1)S(1)}, bf16[4,128,1024]{2,1,0:T(8,128)(2,1)S(1)}, u32[]{:S(2)}, u32[]{:S(2)}) collective-permute-start(bf16[4,128,1024]{2,1,0:T(8,128)(2,1)S(1)} %pad_maximum_fusion.1), channel_id=1, source_target_pairs={{0,2},{1,3},{2,0},{3,1},{4,6},{5,7},{6,4},{7,5},{8,10},{9,11},{10,... | collective-permute-start | bytes 3145736 | tf_op jit(solution)/shard_map/ppermute | solution.py:382
  78.9 1.0 copy-start.9
  81.4 16.8 %collective-permute-start.3 = (bf16[8,128,1024]{2,1,0:T(8,128)(2,1)}, bf16[8,128,1024]{2,1,0:T(8,128)(2,1)}, u32[]{:S(2)}, u32[]{:S(2)}) collective-permute-start(bf16[8,128,1024]{2,1,0:T(8,128)(2,1)} %pad_maximum_fusion), channel_id=1, source_target_pairs={{0,1},{1,0},{2,3},{3,2},{4,5},{5,4},{6,7},{7,6},{8,9},{9,8},{10,11... | collective-permute-start | bytes 6291464 | tf_op jit(solution)/shard_map/ppermute | solution.py:382
  81.4 16.7 %copy-start.10 = (bf16[4,128,1024]{2,1,0:T(8,128)(2,1)S(1)}, bf16[4,128,1024]{2,1,0:T(8,128)(2,1)}, u32[]{:S(2)}) copy-start(bf16[4,128,1024]{2,1,0:T(8,128)(2,1)} %copy-done.9) | copy-start | bytes 3145732
  82.2 4.9 %collective-permute-start.4 = (bf16[1,128,128]{2,1,0:T(8,128)(2,1)S(1)}, bf16[1,128,128]{2,1,0:T(8,128)(2,1)S(1)}, u32[]{:S(2)}, u32[]{:S(2)}) collective-permute-start(bf16[1,128,128]{2,1,0:T(8,128)(2,1)S(1)} %back_low.1), channel_id=1, source_target_pairs={{0,8},{1,9},{2,10},{3,11},{4,12},{5,13},{6,14},{7,15},{8,0},{9,1},... | collective-permute-start | bytes 98312 | tf_op jit(solution)/shard_map/ppermute | solution.py:382
  87.1 4.3 %collective-permute-start.5 = (bf16[2,128,128]{2,1,0:T(8,128)(2,1)S(1)}, bf16[2,128,128]{2,1,0:T(8,128)(2,1)S(1)}, u32[]{:S(2)}, u32[]{:S(2)}) collective-permute-start(bf16[2,128,128]{2,1,0:T(8,128)(2,1)S(1)} %pad_maximum_fusion.7), channel_id=1, source_target_pairs={{0,4},{1,5},{2,6},{3,7},{4,0},{5,1},{6,2},{7,3},{8,12},{9,13},{10,... | collective-permute-start | bytes 196616 | tf_op jit(solution)/shard_map/ppermute | solution.py:382
  91.4 5.0 %collective-permute-start.6 = (bf16[4,128,128]{2,1,0:T(8,128)(2,1)S(1)}, bf16[4,128,128]{2,1,0:T(8,128)(2,1)S(1)}, u32[]{:S(2)}, u32[]{:S(2)}) collective-permute-start(bf16[4,128,128]{2,1,0:T(8,128)(2,1)S(1)} %pad_maximum_fusion.5), channel_id=1, source_target_pairs={{0,2},{1,3},{2,0},{3,1},{4,6},{5,7},{6,4},{7,5},{8,10},{9,11},{10,... | collective-permute-start | bytes 393224 | tf_op jit(solution)/shard_map/ppermute | solution.py:382
  96.5 5.5 %copy-start.4 = (bf16[1024,512]{1,0:T(8,128)(2,1)S(1)}, bf16[1024,512]{1,0:T(8,128)(2,1)}, u32[]{:S(2)}) copy-start(bf16[1024,512]{1,0:T(8,128)(2,1)} %weight.1) | copy-start | bytes 3145732
  96.5 1.6 collective-permute-start.7
  100.0 2.0 copy-start
  108.2 1.3 copy-start.2
  109.5 89.1 %all-to-all-start.2 = ((bf16[16,128,512]{2,1,0:T(8,128)(2,1)}), bf16[16,128,512]{2,1,0:T(8,128)(2,1)}, u32[]{:S(2)}, u32[]{:S(2)}) async-start(bf16[16,128,512]{2,1,0:T(8,128)(2,1)} %copy-done.2), calls=%async_computation.2 | async-start | bytes 4194304 | tf_op jit(solution)/shard_map/all_to_all | solution.py:377
  118.0 63.2 %copy-start.6 = (s32[16]{0:T(128)S(1)}, s32[16]{0:T(128)}, u32[]{:S(2)}) copy-start(s32[16]{0:T(128)} %adapters.13) | copy-start | bytes 196
  118.1 2.0 collective-permute-start.8
  120.2 18.8 %collective-permute-start.9 = (f32[4,128,128]{2,1,0:T(8,128)S(1)}, f32[4,128,128]{2,1,0:T(8,128)S(1)}, u32[]{:S(2)}, u32[]{:S(2)}) collective-permute-start(f32[4,128,128]{2,1,0:T(8,128)S(1)} %slice.35), channel_id=1, source_target_pairs={{0,2},{1,3},{2,0},{3,1},{4,6},{5,7},{6,4},{7,5},{8,10},{9,11},{10,... | collective-permute-start | bytes 786440 | tf_op jit(solution)/shard_map/ppermute | solution.py:382
  139.0 12.9 %collective-permute-start.10 = (f32[2,128,128]{2,1,0:T(8,128)S(1)}, f32[2,128,128]{2,1,0:T(8,128)S(1)}, u32[]{:S(2)}, u32[]{:S(2)}) collective-permute-start(f32[2,128,128]{2,1,0:T(8,128)S(1)} %slice.37), channel_id=1, source_target_pairs={{0,4},{1,5},{2,6},{3,7},{4,0},{5,1},{6,2},{7,3},{8,12},{9,13},{10,... | collective-permute-start | bytes 393224 | tf_op jit(solution)/shard_map/ppermute | solution.py:382
  152.5 13.5 %collective-permute-start.11 = (f32[1,128,128]{2,1,0:T(8,128)S(1)}, f32[1,128,128]{2,1,0:T(8,128)S(1)}, u32[]{:S(2)}, u32[]{:S(2)}) collective-permute-start(f32[1,128,128]{2,1,0:T(8,128)S(1)} %get-tuple-element.11), channel_id=1, source_target_pairs={{0,8},{1,9},{2,10},{3,11},{4,12},{5,13},{6,14},{7,15},{8,0},{9,1},... | collective-permute-start | bytes 196616 | tf_op jit(solution)/shard_map/ppermute | solution.py:382
  166.0 0.6 copy-start.12
  168.8 5.0 %collective-permute-start.12 = (bf16[1,128,128]{2,1,0:T(8,128)(2,1)}, bf16[1,128,128]{2,1,0:T(8,128)(2,1)S(1)}, u32[]{:S(2)}, u32[]{:S(2)}) collective-permute-start(bf16[1,128,128]{2,1,0:T(8,128)(2,1)} %hidden_low.1), channel_id=1, source_target_pairs={{0,8},{1,9},{2,10},{3,11},{4,12},{5,13},{6,14},{7,15},{8,0},{9,1},... | collective-permute-start | bytes 98312 | tf_op jit(solution)/shard_map/ppermute | solution.py:382
  174.6 4.3 %collective-permute-start.13 = (bf16[2,128,128]{2,1,0:T(8,128)(2,1)S(1)}, bf16[2,128,128]{2,1,0:T(8,128)(2,1)S(1)}, u32[]{:S(2)}, u32[]{:S(2)}) collective-permute-start(bf16[2,128,128]{2,1,0:T(8,128)(2,1)S(1)} %pad_maximum_fusion.8), channel_id=1, source_target_pairs={{0,4},{1,5},{2,6},{3,7},{4,0},{5,1},{6,2},{7,3},{8,12},{9,13},{10,... | collective-permute-start | bytes 196616 | tf_op jit(solution)/shard_map/ppermute | solution.py:382
  179.6 10.8 %copy-start.11 = (bf16[1,128,128]{2,1,0:T(8,128)(2,1)S(1)}, bf16[1,128,128]{2,1,0:T(8,128)(2,1)}, u32[]{:S(2)}) copy-start(bf16[1,128,128]{2,1,0:T(8,128)(2,1)} %hidden_low.1) | copy-start | bytes 98308
  179.6 12.5 %copy-start.1 = (bf16[16,128,1024]{2,1,0:T(8,128)(2,1)S(1)}, bf16[16,128,1024]{2,1,0:T(8,128)(2,1)}, u32[]{:S(2)}) copy-start(bf16[16,128,1024]{2,1,0:T(8,128)(2,1)} %copy-done) | copy-start | bytes 12582916
  179.6 12.5 %copy-start.8 = (s32[64]{0:T(128)S(1)}, s32[64]{0:T(128)}, u32[]{:S(2)}) copy-start(s32[64]{0:T(128)} %ranks.5) | copy-start | bytes 772
  179.6 10.8 %collective-permute-start.14 = (bf16[4,128,128]{2,1,0:T(8,128)(2,1)S(1)}, bf16[4,128,128]{2,1,0:T(8,128)(2,1)S(1)}, u32[]{:S(2)}, u32[]{:S(2)}) collective-permute-start(bf16[4,128,128]{2,1,0:T(8,128)(2,1)S(1)} %pad_maximum_fusion.6), channel_id=1, source_target_pairs={{0,2},{1,3},{2,0},{3,1},{4,6},{5,7},{6,4},{7,5},{8,10},{9,11},{10,... | collective-permute-start | bytes 393224 | tf_op jit(solution)/shard_map/ppermute | solution.py:382
  190.5 1.6 collective-permute-start.15

commit v3 on v0

v3 whole, which is shorter than its diff:
```python
import jax
import jax.numpy as jnp
from jax import lax
from jax.experimental import pallas as pl
from jax.experimental.pallas import tpu as pltpu
from jax.sharding import PartitionSpec as P

adapter_alpha = 32.0
vmem_limit = 48 * 1024 * 1024
pair_bit = 2


def line_offset(slot, members):
    bits = members.bit_length() - 1
    line = 0
    for bit in range(bits):
        line |= ((slot >> bit) & 1) << (bits - 1 - bit)
    return ((line // pair_bit) * 2 * pair_bit) | (line % pair_bit)


def params():
    return pltpu.CompilerParams(vmem_limit_bytes=vmem_limit)


def whole(shape):
    return pl.BlockSpec(shape, lambda *_: (0,) * len(shape))


def picked(maps, flip):
    return pl.BlockSpec(
        (1,) + maps.shape[1:], lambda i, adapters, place, *_: (adapters[place[0] ^ flip], 0, 0)
    )


def call(kernel, name, prefetch, operands, in_specs, out_shapes, scratch=(), grid=(1,), out_specs=None):
    if out_specs is None:
        out_specs = [whole(shape.shape) for shape in out_shapes]
    return pl.pallas_call(
        kernel,
        out_shape=out_shapes,
        grid_spec=pltpu.PrefetchScalarGridSpec(
            num_scalar_prefetch=len(prefetch),
            grid=grid,
            in_specs=in_specs,
            out_specs=out_specs,
            scratch_shapes=list(scratch),
        ),
        compiler_params=params(),
        name=name,
    )(*prefetch, *operands)


def collect_kernel(adapters, place, *refs):
    out = refs[-1]
    for entry in range(out.shape[0]):
        out[entry] = refs[entry][0]


def collect(adapters, place, maps, flips, name):
    shape = jax.ShapeDtypeStruct((len(flips),) + maps.shape[1:], maps.dtype)
    return call(
        collect_kernel,
        name,
        (adapters, place),
        [maps] * len(flips),
        [picked(maps, flip) for flip in flips],
        [shape],
    )[0]


def gather_up_kernel(adapters, place, *refs):
    out = refs[-1]
    for entry in range(out.shape[0]):
        out[entry] = refs[entry][0]


def gather_up(adapters, place, up_maps):
    count = adapters.shape[0]

    def spec(block):
        return pl.BlockSpec(
            (1,) + up_maps.shape[1:], lambda i, adapters, place: (adapters[block], 0, 0)
        )

    shape = jax.ShapeDtypeStruct((count,) + up_maps.shape[1:], up_maps.dtype)
    return call(
        gather_up_kernel,
        "gather_up",
        (adapters, place),
        [up_maps] * count,
        [spec(block) for block in range(count)],
        [shape],
    )[0]


def pack_kernel(place, *refs):
    count = len(refs) // 3
    for slot in range(count):
        out = refs[2 * count + slot]
        out[0] = refs[2 * slot][...]
        out[1] = refs[2 * slot + 1][...]


def pack_tokens(place, tokens, members, width):
    rows = tokens.shape[0]

    def spec(flip):
        return pl.BlockSpec((rows, width), lambda i, place: (0, place[0] ^ flip))

    specs = []
    for slot in range(members):
        offset = line_offset(slot, members)
        specs += [spec(offset), spec(offset ^ pair_bit)]
    shape = jax.ShapeDtypeStruct((2, rows, width), tokens.dtype)
    return call(
        pack_kernel, "pack_tokens", (place,), [tokens] * len(specs), specs, [shape] * members
    )


def rank_row(ranks, adapter, extent):
    rank = jnp.full((1, extent), ranks[adapter], jnp.int32)
    alive = (lax.broadcasted_iota(jnp.int32, (1, extent), 1) < rank).astype(jnp.float32)
    return alive, adapter_alpha / rank.astype(jnp.float32)


def back_kernel(adapters, place, ranks, gradient, up, out):
    alive, factor = rank_row(ranks, adapters[place[0]], up.shape[1])
    back = jnp.dot(gradient[...], up[...], preferred_element_type=jnp.float32)
    out[0] = (factor * back * alive).astype(out.dtype)


def back_rows(adapters, place, ranks, gradient, up):
    shape = jax.ShapeDtypeStruct((1, gradient.shape[0], up.shape[1]), jnp.bfloat16)
    return call(
        back_kernel,
        "back_low",
        (adapters, place, ranks),
        (gradient, up),
        [whole(gradient.shape), whole(up.shape)],
        [shape],
    )[0]


def input_kernel(adapters, place, gradients, backs, weight, weight_pair, down_pair, *refs):
    members, rows, depth = gradients.shape
    downs, outs = refs[:members], refs[members:]
    for first in range(0, members, 4):
        some = min(4, members - first)
        lines = gradients[first : first + some].reshape(some * rows, depth)
        for half in range(2):
            frozen = jnp.dot(
                lines, (weight, weight_pair)[half][...], preferred_element_type=jnp.float32
            )
            for slot in range(first, first + some):
                down = downs[slot][0] if half == 0 else down_pair[slot]
                low = jnp.dot(backs[slot], down, preferred_element_type=jnp.float32)
                at = (slot - first) * rows
                outs[slot][half] = (frozen[at : at + rows] + low).astype(jnp.bfloat16)


def input_slices(adapters, place, gradients, backs, weight, weight_pair, down_maps, down_pair):
    members, rows, _ = gradients.shape
    operands = (gradients, backs, weight, weight_pair, down_pair)
    shape = jax.ShapeDtypeStruct((2, rows, weight.shape[1]), jnp.bfloat16)
    return call(
        input_kernel,
        "input_slices",
        (adapters, place),
        operands + (down_maps,) * members,
        [whole(operand.shape) for operand in operands]
        + [picked(down_maps, line_offset(slot, members)) for slot in range(members)],
        [shape] * members,
    )


def hidden_kernel(adapters, place, down_pair, *refs):
    members = down_pair.shape[0]
    downs, tokens = refs[:members], refs[members : 2 * members]
    parts, own, pair = refs[2 * members :]
    across = (((1,), (1,)), ((), ()))
    for slot in range(members):
        own[slot] = tokens[slot][0]
        pair[slot] = tokens[slot][1]
        parts[slot] = lax.dot_general(
            tokens[slot][0], downs[slot][0], across, preferred_element_type=jnp.float32
        ) + lax.dot_general(
            tokens[slot][1], down_pair[slot], across, preferred_element_type=jnp.float32
        )


def hidden_parts(adapters, place, down_maps, down_pair, tokens):
    members = len(tokens)
    _, rows, width = tokens[0].shape
    extent = down_maps.shape[1]
    tokens_shape = jax.ShapeDtypeStruct((members, rows, width), tokens[0].dtype)
    return call(
        hidden_kernel,
        "hidden_parts",
        (adapters, place),
        [down_pair] + [down_maps] * members + list(tokens),
        [whole(down_pair.shape)]
        + [picked(down_maps, line_offset(slot, members)) for slot in range(members)]
        + [whole(tokens[0].shape)] * members,
        [
            jax.ShapeDtypeStruct((members, rows, extent), jnp.float32),
            tokens_shape,
            tokens_shape,
        ],
    )


def hidden_low_kernel(adapters, place, ranks, kept, received, out):
    alive, _ = rank_row(ranks, adapters[place[0]], out.shape[2])
    out[0] = ((kept[0] + received[0]) * alive).astype(out.dtype)


def hidden_rows(adapters, place, ranks, kept, received):
    return call(
        hidden_low_kernel,
        "hidden_low",
        (adapters, place, ranks),
        (kept, received),
        [whole(kept.shape)] * 2,
        [jax.ShapeDtypeStruct(kept.shape, jnp.bfloat16)],
    )[0]


def join_kernel(place, *refs):
    out = refs[-1]
    members = len(refs) - 1
    width = refs[0].shape[2]
    for slot in range(members):
        for half in range(2):
            source = place[0] ^ line_offset(slot, members) ^ (half * pair_bit)
            columns = pl.ds(pl.multiple_of(source * width, width), width)
            out[:, columns] = refs[slot][half]


def join_columns(place, pieces):
    members = len(pieces)
    _, rows, width = pieces[0].shape
    return call(
        join_kernel,
        "join_columns",
        (place,),
        pieces,
        [whole(pieces[0].shape)] * members,
        [jax.ShapeDtypeStruct((rows, 2 * members * width), pieces[0].dtype)],
    )[0]


def list_members(adapters, place, members, head, following):
    num_adapters = head.shape[1]

    def clear(adapter, carry):
        head[0, adapter] = -1
        head[1, adapter] = -1
        return carry

    lax.fori_loop(0, num_adapters, clear, 0)
    for side in range(2):
        for slot in reversed(range(members)):
            adapter = adapters[place[0] ^ line_offset(slot, members) ^ (side * pair_bit)]
            following[side, slot] = head[side, adapter]
            head[side, adapter] = slot


def sum_members(head, following, total, out, terms, finish):
    chunk = out.shape[0]

    def per_adapter(entry, carry):
        adapter = pl.program_id(0) * chunk + entry
        firsts = [head[0, adapter], head[1, adapter]]
        used = jnp.logical_or(firsts[0] >= 0, firsts[1] >= 0)

        @pl.when(jnp.logical_not(used))
        def _():
            out[entry] = jnp.zeros(out.shape[1:], out.dtype)

        @pl.when(used)
        def _():
            total[...] = jnp.zeros_like(total)
            for side in range(2):

                def more(slot, side=side):
                    total[...] += terms[side](slot)
                    return following[side, slot]

                lax.while_loop(lambda slot: slot >= 0, more, firsts[side])
            out[entry] = finish(adapter).astype(out.dtype)

        return carry

    lax.fori_loop(0, chunk, per_adapter, 0)


def by_rows(left, right):
    return lax.dot_general(
        left, right, (((0,), (0,)), ((), ())), preferred_element_type=jnp.float32
    )


def down_gradient_kernel(
    adapters, place, backs, backs_pair, own, other, out, head, following, total
):
    @pl.when(pl.program_id(0) == 0)
    def _():
        list_members(adapters, place, own.shape[0], head, following)

    terms = (
        lambda slot: by_rows(backs[slot], own[slot]),
        lambda slot: by_rows(backs_pair[slot], other[slot]),
    )
    sum_members(head, following, total, out, terms, lambda adapter: total[...])


def down_gradients(adapters, place, backs, backs_pair, own, other, num_adapters):
    members, _, width = own.shape
    extent = backs.shape[2]
    chunk = 8 if num_adapters % 8 == 0 else 1
    operands = (backs, backs_pair, own, other)
    return call(
        down_gradient_kernel,
        "down_gradients",
        (adapters, place),
        operands,
        [whole(operand.shape) for operand in operands],
        [jax.ShapeDtypeStruct((num_adapters, extent, width), jnp.bfloat16)],
        scratch=[
            pltpu.SMEM((2, num_adapters), jnp.int32),
            pltpu.SMEM((2, members), jnp.int32),
            pltpu.VMEM((extent, width), jnp.float32),
        ],
        grid=(num_adapters // chunk,),
        out_specs=[pl.BlockSpec((chunk, extent, width), lambda i, *_: (i, 0, 0))],
    )[0]


def up_gradient_kernel(
    adapters, place, ranks, gradients, gradients_pair, hiddens, hiddens_pair, out, head, following, total
):
    width, extent = out.shape[1:]
    lanes = gradients.shape[2]

    @pl.when(pl.program_id(0) == 0)
    def _():
        list_members(adapters, place, gradients.shape[0], head, following)

    def finish(adapter):
        _, factor = rank_row(ranks, adapter, extent)
        inside = lax.rem(place[0], lanes // width) * width
        return factor * total[pl.ds(pl.multiple_of(inside, width), width), :]

    terms = (
        lambda slot: by_rows(gradients[slot], hiddens[slot]),
        lambda slot: by_rows(gradients_pair[slot], hiddens_pair[slot]),
    )
    sum_members(head, following, total, out, terms, finish)


def up_gradients(adapters, place, ranks, gradients, gradients_pair, hiddens, hiddens_pair, width):
    members, rows, lanes = gradients_pair.shape
    extent = hiddens.shape[2]
    num_adapters = ranks.shape[0]
    chunk = 32 if num_adapters % 32 == 0 else 1
    return call(
        up_gradient_kernel,
        "up_gradients",
        (adapters, place, ranks),
        (gradients, gradients_pair, hiddens, hiddens_pair),
        [
            pl.BlockSpec(
                (members, rows, lanes),
                lambda i, adapters, place, ranks: (0, 0, place[0] * width // lanes),
            ),
            whole(gradients_pair.shape),
            whole(hiddens.shape),
            whole(hiddens.shape),
        ],
        [jax.ShapeDtypeStruct((num_adapters, width, extent), jnp.bfloat16)],
        scratch=[
            pltpu.SMEM((2, num_adapters), jnp.int32),
            pltpu.SMEM((2, members), jnp.int32),
            pltpu.VMEM((lanes, extent), jnp.float32),
        ],
        grid=(num_adapters // chunk,),
        out_specs=[pl.BlockSpec((chunk, width, extent), lambda i, *_: (i, 0, 0))],
    )[0]


def exchange(pieces):
    return lax.all_to_all(pieces, "dp", split_axis=0, concat_axis=0, tiled=True)


def swap(array, flip):
    devices = lax.axis_size("dp")
    return lax.ppermute(array, "dp", [(i, i ^ flip) for i in range(devices)])


def tie(first, second):
    return lax.optimization_barrier((first, second))


def gather_step(held, members):
    return jnp.concatenate([held, swap(held, line_offset(held.shape[0], members))], axis=0)


def gather_line(held, members):
    while held.shape[0] < members:
        held = gather_step(held, members)
    return held


def reduce_line(parts, members):
    while True:
        half = parts.shape[0] // 2
        kept, received = parts[:half], swap(parts[half:], line_offset(half, members))
        if half == 1:
            return kept, received
        parts = kept + received


def local(tokens, output_gradient, value_weight, down_maps, up_maps, adapter_per_block, ranks):
    devices = lax.axis_size("dp")
    members = devices // 2
    num_adapters, extent, width = down_maps.shape
    rows, depth = output_gradient.shape
    value_width = depth // devices
    place = lax.axis_index("dp").astype(jnp.int32).reshape(1)
    adapters = adapter_per_block
    offsets = [line_offset(slot, members) for slot in range(members)]
    far = [slot for slot in range(members) if slot % 2]
    near = [slot for slot in range(1, members) if slot % 2 == 0]

    gradients = gather_step(output_gradient.reshape(1, rows, depth), members)
    own_up = exchange(gather_up(adapters, place, up_maps)).reshape(depth, extent)
    down_pair = swap(
        collect(adapters, place, down_maps, [o ^ pair_bit for o in offsets], "collect_down"),
        pair_bit,
    )
    weight_pair = swap(value_weight, pair_bit)

    packs = list(pack_tokens(place, tokens, members, width))
    arrived = [packs[0]] + [None] * (members - 1)
    early = far[: len(far) // 2]
    for slot in early:
        arrived[slot] = swap(packs[slot], offsets[slot])
    gradients = gather_step(gradients, members)
    gradients, packs = tie(gradients, packs)
    for slot in near + far[len(far) // 2 :]:
        arrived[slot] = swap(packs[slot], offsets[slot])
    gradients = gather_line(gradients, members)

    backs = gather_line(back_rows(adapters, place, ranks, output_gradient, own_up), members)
    slices = list(
        input_slices(
            adapters, place, gradients, backs, value_weight, weight_pair, down_maps, down_pair
        )
    )
    results = [slices[0]] + [None] * (members - 1)
    for slot in early:
        results[slot] = swap(slices[slot], offsets[slot])

    slices, arrived = tie(slices, arrived)
    parts, tokens_own, tokens_pair = hidden_parts(
        adapters, place, down_maps, down_pair, arrived
    )
    kept, received = reduce_line(parts, members)
    received, slices = tie(received, slices)
    for slot in near + far[len(far) // 2 :]:
        results[slot] = swap(slices[slot], offsets[slot])
    input_grad = join_columns(place, results)

    tokens_other = swap(tokens_pair, pair_bit)
    backs_pair = swap(backs, pair_bit)
    down_gradient = down_gradients(
        adapters, place, backs, backs_pair, tokens_own, tokens_other, num_adapters
    )

    lanes = max(128, value_width)
    column = (place[0] ^ pair_bit) * value_width // lanes * lanes
    gradients_pair = swap(
        lax.dynamic_slice(gradients, (0, 0, column), (members, rows, lanes)), pair_bit
    )
    hiddens = gather_line(hidden_rows(adapters, place, ranks, kept, received), members)
    hiddens_pair = swap(hiddens, pair_bit)
    up_gradient = up_gradients(
        adapters, place, ranks, gradients, gradients_pair, hiddens, hiddens_pair, value_width
    )
    return (input_grad, down_gradient, up_gradient)


def solution(mesh):
    in_specs = (
        P(("groups", "dp"), None),
        P(("groups", "dp"), None),
        P(None, "dp"),
        P(None, None, "dp"),
        P(None, "dp", None),
        P("groups"),
        P(),
    )
    out_specs = (P(("groups", "dp"), None), P("groups", None, "dp"), P("groups", "dp", None))
    return jax.shard_map(local, mesh=mesh, in_specs=in_specs, out_specs=out_specs, check_vma=False)
```

time: 267 us -> 189 us (0.71)
  the two profiles are of different devices: /device:TPU:13 before, /device:TPU:0 now
where the time goes in v3:
time: 189 us; the launch traced here: 188 us
  waiting for transfers between devices  85.9 us (45%)
  starting transfers between devices  51.6 us (27%)
  Pallas kernels  35.5 us (19%)
  local copies, waits for them, and re-layouts  9.27 us (5%)
  other arithmetic  5.14 us (3%)
    ppermute x32, waiting for transfers between devices, swap(): return lax.ppermute(array, 'dp', [(i, i ^ flip) for i in range(devices)])  83 us
    ppermute x32, starting transfers between devices, swap(): return lax.ppermute(array, 'dp', [(i, i ^ flip) for i in range(devices)])  46 us
    pallas_call x10, Pallas kernels, call(): pl.pallas_call(kernel, out_shape=out_shapes, grid_spec=pltpu.PrefetchScal...  35.5 us
    unnamed x41, local copies, waits for them, and re-layouts  7.86 us
    all_to_all x1, starting transfers between devices, exchange(): return lax.all_to_all(pieces, 'dp', split_axis=0, concat_axis=0, tiled=True)  5.61 us
    concatenate x8, other arithmetic, gather_step(): jnp.concatenate([held, swap(held, line_offset(held.shape[0], members))],...  5.09 us
  transfers between devices with their start and end apart: 33, of which 15 were waited for; matrix products, arithmetic and copies ran while one was open for 3% of the time, Pallas kernels for 12%

profile of v3, /device:TPU:0, one launch (start us, length us, event | category | flops | bytes accessed | tf_op | source)
XLA Modules:
  0.0 188.3 jit_solution(9264388800086641658)
XLA Ops:
  0.6 4.1 %collective-permute-start = (bf16[1,128,1024]{2,1,0:T(8,128)(2,1)}, bf16[1,128,1024]{2,1,0:T(8,128)(2,1)S(1)}, u32[]{:S(2)}, u32[]{:S(2)}) collective-permute-start(bf16[1,128,1024]{2,1,0:T(8,128)(2,1)} %bitcast.3), channel_id=1, source_target_pairs={{0,8},{1,9},{2,10},{3,11},{4,12},{5,13},{6,14},{7,15},{8,0},{9,1},... | collective-permute-start | bytes 786440 | tf_op jit(solution)/shard_map/ppermute | solution.py:397
  4.7 12.1 %collective-permute-done = bf16[1,128,1024]{2,1,0:T(8,128)(2,1)S(1)} collective-permute-done((bf16[1,128,1024]{2,1,0:T(8,128)(2,1)}, bf16[1,128,1024]{2,1,0:T(8,128)(2,1)S(1)}, u32[]{:S(2)}, u32[]{:S(2)}) %collective-permute-start) | collective-permute-done | bytes 262176 | tf_op jit(solution)/shard_map/ppermute | solution.py:397
  16.9 1.9 %pad_maximum_fusion.1 = bf16[2,128,1024]{2,1,0:T(8,128)(2,1)} fusion(bf16[1,128,1024]{2,1,0:T(8,128)(2,1)S(1)} %collective-permute-done, bf16[1,128,1024]{2,1,0:T(8,128)(2,1)} %bitcast.4), kind=kLoop, calls=%fused_computation.1 | loop fusion | flops 262144 | bytes 1048576 | tf_op jit(solution)/shard_map/concatenate | solution.py:405
  19.6 1.2 copy-done.1
  21.5 1.3 gather_up.1
  22.8 5.6 %all-to-all-start = ((bf16[16,64,128]{2,1,0:T(8,128)(2,1)}), bf16[16,64,128]{2,1,0:T(8,128)(2,1)S(1)}, u32[]{:S(2)}, u32[]{:S(2)}) async-start(bf16[16,64,128]{2,1,0:T(8,128)(2,1)} %gather_up.1), calls=%async_computation | async-start | bytes 524288 | tf_op jit(solution)/shard_map/all_to_all | solution.py:392
  28.4 3.2 %collect_down.1 = bf16[8,128,512]{2,1,0:T(8,128)(2,1)} custom-call(s32[16]{0:T(128)S(1)} %copy-done.16, s32[1]{0:T(128)} %bitcast.place, bf16[64,128,512]{2,1,0:T(8,128)(2,1)} %refs_7_.9, bf16[64,128,512]{2,1,0:T(8,128)(2,1)} %refs_7_.9, bf16[64,128,512]{2,1,0:T(8,128)(2,1)} %refs_7_.9, bf16[64,128,512]{2,1,0:T(8,128)(2,1)} %refs_7_.9, ...), custom_call_target="tpu_custom_call" | custom-call | tf_op jit(solution)/shard_map/collect_down/pallas_call | solution.py:38
  31.6 1.9 %collective-permute-start.7 = (bf16[8,128,512]{2,1,0:T(8,128)(2,1)}, bf16[8,128,512]{2,1,0:T(8,128)(2,1)S(1)}, u32[]{:S(2)}, u32[]{:S(2)}) collective-permute-start(bf16[8,128,512]{2,1,0:T(8,128)(2,1)} %collect_down.1), channel_id=1, source_target_pairs={{0,2},{1,3},{2,0},{3,1},{4,6},{5,7},{6,4},{7,5},{8,10},{9,11},{10,... | collective-permute-start | bytes 3145736 | tf_op jit(solution)/shard_map/ppermute | solution.py:397
  33.6 1.2 pack_tokens.1
  34.8 2.2 %pad_maximum_fusion = bf16[4,128,1024]{2,1,0:T(8,128)(2,1)} fusion(bf16[2,128,1024]{2,1,0:T(8,128)(2,1)} %collective-permute-done.1, bf16[1,128,1024]{2,1,0:T(8,128)(2,1)S(1)} %copy-done.19, bf16[1,128,1024]{2,1,0:T(8,128)(2,1)S(1)} %bitcast.5), kind=kLoop, calls=%fused_computation | loop fusion | flops 1048576 | bytes 2097152 | tf_op jit(solution)/shard_map/concatenate | solution.py:405
  37.0 2.9 %all-to-all-done = bf16[16,64,128]{2,1,0:T(8,128)(2,1)S(1)} async-done(((bf16[16,64,128]{2,1,0:T(8,128)(2,1)}), bf16[16,64,128]{2,1,0:T(8,128)(2,1)S(1)}, u32[]{:S(2)}, u32[]{:S(2)}) %all-to-all-start) | async-done | bytes 262176 | tf_op jit(solution)/shard_map/all_to_all | solution.py:392
  40.7 4.8 %collective-permute-done.3 = bf16[1,128,128]{2,1,0:T(8,128)(2,1)S(1)} collective-permute-done((bf16[1,128,128]{2,1,0:T(8,128)(2,1)S(1)}, bf16[1,128,128]{2,1,0:T(8,128)(2,1)S(1)}, u32[]{:S(2)}, u32[]{:S(2)}) %collective-permute-start.3) | collective-permute-done | bytes 32800 | tf_op jit(solution)/shard_map/ppermute | solution.py:397
  45.6 4.2 %collective-permute-done.4 = bf16[2,128,128]{2,1,0:T(8,128)(2,1)S(1)} collective-permute-done((bf16[2,128,128]{2,1,0:T(8,128)(2,1)S(1)}, bf16[2,128,128]{2,1,0:T(8,128)(2,1)S(1)}, u32[]{:S(2)}, u32[]{:S(2)}) %collective-permute-start.4) | collective-permute-done | bytes 65568 | tf_op jit(solution)/shard_map/ppermute | solution.py:397
  51.3 2.2 %collective-permute-start.11 = (bf16[2,128,512]{2,1,0:T(8,128)(2,1)S(1)}, bf16[2,128,512]{2,1,0:T(8,128)(2,1)S(1)}, u32[]{:S(2)}, u32[]{:S(2)}) collective-permute-start(bf16[2,128,512]{2,1,0:T(8,128)(2,1)S(1)} %get-tuple-element.50), channel_id=1, source_target_pairs={{0,12},{1,13},{2,14},{3,15},{4,8},{5,9},{6,10},{7,11},{8,4},{9,5},... | collective-permute-start | bytes 786440 | tf_op jit(solution)/shard_map/ppermute | solution.py:397
  53.6 16.9 %collective-permute-done.9.refs_9_ = bf16[2,128,512]{2,1,0:T(8,128)(2,1)S(1)} collective-permute-done((bf16[2,128,512]{2,1,0:T(8,128)(2,1)S(1)}, bf16[2,128,512]{2,1,0:T(8,128)(2,1)S(1)}, u32[]{:S(2)}, u32[]{:S(2)}) %collective-permute-start.9) | collective-permute-done | bytes 262176 | tf_op jit(solution)/shard_map/ppermute | solution.py:397
  70.5 6.9 %collective-permute-start.13 = (bf16[2,128,512]{2,1,0:T(8,128)(2,1)}, bf16[2,128,512]{2,1,0:T(8,128)(2,1)S(1)}, u32[]{:S(2)}, u32[]{:S(2)}) collective-permute-start(bf16[2,128,512]{2,1,0:T(8,128)(2,1)} %get-tuple-element.66), channel_id=1, source_target_pairs={{0,9},{1,8},{2,11},{3,10},{4,13},{5,12},{6,15},{7,14},{8,1},{9,0},... | collective-permute-start | bytes 786440 | tf_op jit(solution)/shard_map/ppermute | solution.py:397
  77.3 3.6 %collective-permute-done.6.weight_pair = bf16[1024,512]{1,0:T(8,128)(2,1)} collective-permute-done((bf16[1024,512]{1,0:T(8,128)(2,1)S(1)}, bf16[1024,512]{1,0:T(8,128)(2,1)}, u32[]{:S(2)}, u32[]{:S(2)}) %collective-permute-start.6) | collective-permute-done | bytes 1048608 | tf_op jit(solution)/shard_map/ppermute | solution.py:397
  80.9 0.9 collective-permute-start.14
  81.8 2.7 %collective-permute-start.15 = (bf16[2,128,512]{2,1,0:T(8,128)(2,1)}, bf16[2,128,512]{2,1,0:T(8,128)(2,1)S(1)}, u32[]{:S(2)}, u32[]{:S(2)}) collective-permute-start(bf16[2,128,512]{2,1,0:T(8,128)(2,1)} %get-tuple-element.68), channel_id=1, source_target_pairs={{0,13},{1,12},{2,15},{3,14},{4,9},{5,8},{6,11},{7,10},{8,5},{9,4},... | collective-permute-start | bytes 786440 | tf_op jit(solution)/shard_map/ppermute | solution.py:397
  84.5 1.3 constant_dynamic-update-slice_fusion.1
  85.8 1.3 constant_dynamic-update-slice_fusion.gradients
  87.1 1.3 copy-done.2
  88.4 6.2 %input_slices.1 = (bf16[2,128,512]{2,1,0:T(8,128)(2,1)S(1)}, bf16[2,128,512]{2,1,0:T(8,128)(2,1)S(1)}, bf16[2,128,512]{2,1,0:T(8,128)(2,1)}, bf16[2,128,512]{2,1...) custom-call(s32[16]{0:T(128)S(1)} %copy-done.16, ...), custom_call_target="tpu_custom_call" | custom-call | tf_op jit(solution)/shard_map/input_slices/pallas_call | solution.py:38
  95.4 3.7 %collective-permute-done.14.refs_14_ = bf16[2,128,512]{2,1,0:T(8,128)(2,1)S(1)} collective-permute-done((bf16[2,128,512]{2,1,0:T(8,128)(2,1)}, bf16[2,128,512]{2,1,0:T(8,128)(2,1)S(1)}, u32[]{:S(2)}, u32[]{:S(2)}) %collective-permute-start.14) | collective-permute-done | bytes 262176 | tf_op jit(solution)/shard_map/ppermute | solution.py:397
  99.1 3.5 %hidden_parts.1 = (f32[8,128,128]{2,1,0:T(8,128)S(1)}, bf16[8,128,512]{2,1,0:T(8,128)(2,1)S(1)}, bf16[8,128,512]{2,1,0:T(8,128)(2,1)}) custom-call(s32[16]{0:T(128)S(1)} %copy-done.16, s32[1]{0:T(128)} %bitcast.place, bf16[8,128,512]{2,1,0:T(8,128)(2,1)S(1)} %collective-permute-done.7.down_pair, bf16[64,128,512]{2,1,0:T(8,128)(2,1)} %refs_7_.9, ...), custom_call_target="tpu_custom_call" | custom-call | tf_op jit(solution)/shard_map/hidden_parts/pallas_call | solution.py:38
  102.6 1.0 copy-done.7
  103.8 1.4 collective-permute-done.16
  105.3 2.6 %collective-permute-start.17 = (f32[2,128,128]{2,1,0:T(8,128)S(1)}, f32[2,128,128]{2,1,0:T(8,128)S(1)}, u32[]{:S(2)}, u32[]{:S(2)}) collective-permute-start(f32[2,128,128]{2,1,0:T(8,128)S(1)} %slice.25), channel_id=1, source_target_pairs={{0,4},{1,5},{2,6},{3,7},{4,0},{5,1},{6,2},{7,3},{8,12},{9,13},{10,... | collective-permute-start | bytes 393224 | tf_op jit(solution)/shard_map/ppermute | solution.py:397
  107.9 3.8 %collective-permute-done.17 = f32[2,128,128]{2,1,0:T(8,128)S(1)} collective-permute-done((f32[2,128,128]{2,1,0:T(8,128)S(1)}, f32[2,128,128]{2,1,0:T(8,128)S(1)}, u32[]{:S(2)}, u32[]{:S(2)}) %collective-permute-start.17) | collective-permute-done | bytes 131104 | tf_op jit(solution)/shard_map/ppermute | solution.py:397
  111.7 2.1 %collective-permute-start.18 = (f32[1,128,128]{2,1,0:T(8,128)S(1)}, f32[1,128,128]{2,1,0:T(8,128)S(1)}, u32[]{:S(2)}, u32[]{:S(2)}) collective-permute-start(f32[1,128,128]{2,1,0:T(8,128)S(1)} %get-tuple-element.92), channel_id=1, source_target_pairs={{0,8},{1,9},{2,10},{3,11},{4,12},{5,13},{6,14},{7,15},{8,0},{9,1},... | collective-permute-start | bytes 196616 | tf_op jit(solution)/shard_map/ppermute | solution.py:397
  114.3 2.8 %collective-permute-done.18.received = f32[1,128,128]{2,1,0:T(8,128)S(1)} collective-permute-done((f32[1,128,128]{2,1,0:T(8,128)S(1)}, f32[1,128,128]{2,1,0:T(8,128)S(1)}, u32[]{:S(2)}, u32[]{:S(2)}) %collective-permute-start.18) | collective-permute-done | bytes 65568 | tf_op jit(solution)/shard_map/ppermute | solution.py:397
  117.7 2.0 %collective-permute-start.28 = (bf16[1,128,128]{2,1,0:T(8,128)(2,1)S(1)}, bf16[1,128,128]{2,1,0:T(8,128)(2,1)S(1)}, u32[]{:S(2)}, u32[]{:S(2)}) collective-permute-start(bf16[1,128,128]{2,1,0:T(8,128)(2,1)S(1)} %hidden_low.1), channel_id=1, source_target_pairs={{0,8},{1,9},{2,10},{3,11},{4,12},{5,13},{6,14},{7,15},{8,0},{9,1},... | collective-permute-start | bytes 98312 | tf_op jit(solution)/shard_map/ppermute | solution.py:397
  119.7 2.9 %collective-permute-done.28 = bf16[1,128,128]{2,1,0:T(8,128)(2,1)S(1)} collective-permute-done((bf16[1,128,128]{2,1,0:T(8,128)(2,1)S(1)}, bf16[1,128,128]{2,1,0:T(8,128)(2,1)S(1)}, u32[]{:S(2)}, u32[]{:S(2)}) %collective-permute-start.28) | collective-permute-done | bytes 32800 | tf_op jit(solution)/shard_map/ppermute | solution.py:397
  122.6 1.6 collective-permute-start.29
  124.2 2.3 %collective-permute-start.8 = (bf16[2,128,512]{2,1,0:T(8,128)(2,1)S(1)}, bf16[2,128,512]{2,1,0:T(8,128)(2,1)S(1)}, u32[]{:S(2)}, u32[]{:S(2)}) collective-permute-start(bf16[2,128,512]{2,1,0:T(8,128)(2,1)S(1)} %get-tuple-element.57), channel_id=1, source_target_pairs={{0,8},{1,9},{2,10},{3,11},{4,12},{5,13},{6,14},{7,15},{8,0},{9,1},... | collective-permute-start | bytes 786440 | tf_op jit(solution)/shard_map/ppermute | solution.py:397
  127.2 2.2 %collective-permute-start.19 = (bf16[2,128,512]{2,1,0:T(8,128)(2,1)}, bf16[2,128,512]{2,1,0:T(8,128)(2,1)}, u32[]{:S(2)}, u32[]{:S(2)}) collective-permute-start(bf16[2,128,512]{2,1,0:T(8,128)(2,1)} %get-tuple-element.83), channel_id=1, source_target_pairs={{0,4},{1,5},{2,6},{3,7},{4,0},{5,1},{6,2},{7,3},{8,12},{9,13},{10,... | collective-permute-start | bytes 786440 | tf_op jit(solution)/shard_map/ppermute | solution.py:397
  129.4 12.6 %collective-permute-done.8.refs_1_ = bf16[2,128,512]{2,1,0:T(8,128)(2,1)S(1)} collective-permute-done((bf16[2,128,512]{2,1,0:T(8,128)(2,1)S(1)}, bf16[2,128,512]{2,1,0:T(8,128)(2,1)S(1)}, u32[]{:S(2)}, u32[]{:S(2)}) %collective-permute-start.8) | collective-permute-done | bytes 262176 | tf_op jit(solution)/shard_map/ppermute | solution.py:397
  142.7 4.2 %collective-permute-start.22 = (bf16[2,128,512]{2,1,0:T(8,128)(2,1)}, bf16[2,128,512]{2,1,0:T(8,128)(2,1)}, u32[]{:S(2)}, u32[]{:S(2)}) collective-permute-start(bf16[2,128,512]{2,1,0:T(8,128)(2,1)} %get-tuple-element.85), channel_id=1, source_target_pairs={{0,9},{1,8},{2,11},{3,10},{4,13},{5,12},{6,15},{7,14},{8,1},{9,0},... | collective-permute-start | bytes 786440 | tf_op jit(solution)/shard_map/ppermute | solution.py:397
  147.4 0.9 pad_maximum_fusion.3.hiddens
  148.3 3.1 %collective-permute-start.24 = (bf16[2,128,512]{2,1,0:T(8,128)(2,1)S(1)}, bf16[2,128,512]{2,1,0:T(8,128)(2,1)S(1)}, u32[]{:S(2)}, u32[]{:S(2)}) collective-permute-start(bf16[2,128,512]{2,1,0:T(8,128)(2,1)S(1)} %get-tuple-element.87), channel_id=1, source_target_pairs={{0,13},{1,12},{2,15},{3,14},{4,9},{5,8},{6,11},{7,10},{8,5},{9,4},... | collective-permute-start | bytes 786440 | tf_op jit(solution)/shard_map/ppermute | solution.py:397
  151.4 1.3 collective-permute-start.27
  152.7 4.5 %collective-permute-done.22.refs_5_ = bf16[2,128,512]{2,1,0:T(8,128)(2,1)} collective-permute-done((bf16[2,128,512]{2,1,0:T(8,128)(2,1)}, bf16[2,128,512]{2,1,0:T(8,128)(2,1)}, u32[]{:S(2)}, u32[]{:S(2)}) %collective-permute-start.22) | collective-permute-done | bytes 262176 | tf_op jit(solution)/shard_map/ppermute | solution.py:397
  157.2 1.3 collective-permute-start.31
  159.3 9.1 %collective-permute-done.24.refs_7_ = bf16[2,128,512]{2,1,0:T(8,128)(2,1)S(1)} collective-permute-done((bf16[2,128,512]{2,1,0:T(8,128)(2,1)S(1)}, bf16[2,128,512]{2,1,0:T(8,128)(2,1)S(1)}, u32[]{:S(2)}, u32[]{:S(2)}) %collective-permute-start.24) | collective-permute-done | bytes 262176 | tf_op jit(solution)/shard_map/ppermute | solution.py:397
  168.4 0.9 copy-done.14
  169.4 2.7 %join_columns.1 = bf16[128,8192]{1,0:T(8,128)(2,1)} custom-call(s32[1]{0:T(128)} %bitcast.place, bf16[2,128,512]{2,1,0:T(8,128)(2,1)S(1)} %copy-done.12, bf16[2,128,512]{2,1,0:T(8,128)(2,1)S(1)} %collective-permute-done.8.refs_1_, bf16[2,128,512]{2,1,0:T(8,128)(2,1)} %collective-permute-done.19.refs_2_, bf16[2,128,512]{2,1,0:T(8,128)(2,1)S(1)} %copy-done.14, ...), custom_call_target="tpu_custom_call" | custom-call | tf_op jit(solution)/shard_map/join_columns/pallas_call | solution.py:38
  172.0 6.6 %up_gradients.1 = bf16[64,64,128]{2,1,0:T(8,128)(2,1)} custom-call(s32[16]{0:T(128)S(1)} %copy-done.16, s32[1]{0:T(128)} %bitcast.place, s32[64]{0:T(128)S(1)} %copy-done.17, bf16[8,128,1024]{2,1,0:T(8,128)(2,1)S(1)} %copy-done.3, bf16[8,128,128]{2,1,0:T(8,128)(2,1)S(1)} %collective-permute-done.27.gradients_pair, ...), custom_call_target="tpu_custom_call" | custom-call | tf_op jit(solution)/shard_map/up_gradients/pallas_call | solution.py:38
  178.6 9.6 %down_gradients.1 = bf16[64,128,512]{2,1,0:T(8,128)(2,1)} custom-call(s32[16]{0:T(128)S(1)} %copy-done.16, s32[1]{0:T(128)} %bitcast.place, bf16[8,128,128]{2,1,0:T(8,128)(2,1)S(1)} %pad_maximum_fusion.2.backs, bf16[8,128,128]{2,1,0:T(8,128)(2,1)S(1)} %collective-permute-done.25.backs_pair, bf16[8,128,512]{2,1,0:T(8,128)(2,1)S(1)} %copy-done.8, ...), custom_call_target="tpu_custom_call" | custom-call | tf_op jit(solution)/shard_map/down_gradients/pallas_call | solution.py:38
  (84 shorter events, 9.0 us)
Async XLA Ops:
  0.6 16.2 %collective-permute-start = (bf16[1,128,1024]{2,1,0:T(8,128)(2,1)}, bf16[1,128,1024]{2,1,0:T(8,128)(2,1)S(1)}, u32[]{:S(2)}, u32[]{:S(2)}) collective-permute-start(bf16[1,128,1024]{2,1,0:T(8,128)(2,1)} %bitcast.3), channel_id=1, source_target_pairs={{0,8},{1,9},{2,10},{3,11},{4,12},{5,13},{6,14},{7,15},{8,0},{9,1},... | collective-permute-start | bytes 786440 | tf_op jit(solution)/shard_map/ppermute | solution.py:397
  16.9 2.7 %copy-start.18 = (bf16[1,128,1024]{2,1,0:T(8,128)(2,1)}, bf16[1,128,1024]{2,1,0:T(8,128)(2,1)S(1)}, u32[]{:S(2)}) copy-start(bf16[1,128,1024]{2,1,0:T(8,128)(2,1)S(1)} %collective-permute-done) | copy-start | bytes 786436
  18.8 16.0 %collective-permute-start.1 = (bf16[2,128,1024]{2,1,0:T(8,128)(2,1)}, bf16[2,128,1024]{2,1,0:T(8,128)(2,1)}, u32[]{:S(2)}, u32[]{:S(2)}) collective-permute-start(bf16[2,128,1024]{2,1,0:T(8,128)(2,1)} %pad_maximum_fusion.1), channel_id=1, source_target_pairs={{0,4},{1,5},{2,6},{3,7},{4,0},{5,1},{6,2},{7,3},{8,12},{9,13},{10,... | collective-permute-start | bytes 1572872 | tf_op jit(solution)/shard_map/ppermute | solution.py:397
  19.6 1.2 copy-start.1
  21.5 6.9 %copy-start.16 = (s32[16]{0:T(128)S(1)}, s32[16]{0:T(128)}, u32[]{:S(2)}) copy-start(s32[16]{0:T(128)} %adapters.15) | copy-start | bytes 196
  22.8 17.1 %all-to-all-start = ((bf16[16,64,128]{2,1,0:T(8,128)(2,1)}), bf16[16,64,128]{2,1,0:T(8,128)(2,1)S(1)}, u32[]{:S(2)}, u32[]{:S(2)}) async-start(bf16[16,64,128]{2,1,0:T(8,128)(2,1)} %gather_up.1), calls=%async_computation | async-start | bytes 524288 | tf_op jit(solution)/shard_map/all_to_all | solution.py:392
  28.4 5.1 %copy-start.5 = (bf16[1024,512]{1,0:T(8,128)(2,1)S(1)}, bf16[1024,512]{1,0:T(8,128)(2,1)}, u32[]{:S(2)}) copy-start(bf16[1024,512]{1,0:T(8,128)(2,1)} %weight.1) | copy-start | bytes 3145732
  28.4 5.2 %copy-start = (bf16[128,8192]{1,0:T(8,128)(2,1)S(1)}, bf16[128,8192]{1,0:T(8,128)(2,1)}, u32[]{:S(2)}) copy-start(bf16[128,8192]{1,0:T(8,128)(2,1)} %refs_15_.2) | copy-start | bytes 6291460
  31.6 3.2 %copy-start.4 = (bf16[128,1024]{1,0:T(8,128)(2,1)S(1)}, bf16[128,1024]{1,0:T(8,128)(2,1)}, u32[]{:S(2)}) copy-start(bf16[128,1024]{1,0:T(8,128)(2,1)} %gradient.1) | copy-start | bytes 786436
  31.6 3.2 %copy-start.19 = (bf16[1,128,1024]{2,1,0:T(8,128)(2,1)S(1)}, bf16[1,128,1024]{2,1,0:T(8,128)(2,1)}, u32[]{:S(2)}) copy-start(bf16[1,128,1024]{2,1,0:T(8,128)(2,1)} %copy-done.18) | copy-start | bytes 786436
  31.6 38.9 %collective-permute-start.7 = (bf16[8,128,512]{2,1,0:T(8,128)(2,1)}, bf16[8,128,512]{2,1,0:T(8,128)(2,1)S(1)}, u32[]{:S(2)}, u32[]{:S(2)}) collective-permute-start(bf16[8,128,512]{2,1,0:T(8,128)(2,1)} %collect_down.1), channel_id=1, source_target_pairs={{0,2},{1,3},{2,0},{3,1},{4,6},{5,7},{6,4},{7,5},{8,10},{9,11},{10,... | collective-permute-start | bytes 3145736 | tf_op jit(solution)/shard_map/ppermute | solution.py:397
  33.5 47.4 %collective-permute-start.6 = (bf16[1024,512]{1,0:T(8,128)(2,1)S(1)}, bf16[1024,512]{1,0:T(8,128)(2,1)}, u32[]{:S(2)}, u32[]{:S(2)}) collective-permute-start(bf16[1024,512]{1,0:T(8,128)(2,1)S(1)} %copy-done.5), channel_id=1, source_target_pairs={{0,2},{1,3},{2,0},{3,1},{4,6},{5,7},{6,4},{7,5},{8,10},{9,11},{10,... | collective-permute-start | bytes 3145736 | tf_op jit(solution)/shard_map/ppermute | solution.py:397
  34.8 5.1 %copy-start.9 = (bf16[2,128,512]{2,1,0:T(8,128)(2,1)}, bf16[2,128,512]{2,1,0:T(8,128)(2,1)S(1)}, u32[]{:S(2)}) copy-start(bf16[2,128,512]{2,1,0:T(8,128)(2,1)S(1)} %get-tuple-element.69.refs_8_) | copy-start | bytes 786436
  34.8 5.1 %copy-start.17 = (s32[64]{0:T(128)S(1)}, s32[64]{0:T(128)}, u32[]{:S(2)}) copy-start(s32[64]{0:T(128)} %ranks.5) | copy-start | bytes 772
  37.0 44.8 %collective-permute-start.2 = (bf16[4,128,1024]{2,1,0:T(8,128)(2,1)}, bf16[4,128,1024]{2,1,0:T(8,128)(2,1)}, u32[]{:S(2)}, u32[]{:S(2)}) collective-permute-start(bf16[4,128,1024]{2,1,0:T(8,128)(2,1)} %pad_maximum_fusion), channel_id=1, source_target_pairs={{0,1},{1,0},{2,3},{3,2},{4,5},{5,4},{6,7},{7,6},{8,9},{9,8},{10,11... | collective-permute-start | bytes 3145736 | tf_op jit(solution)/shard_map/ppermute | solution.py:397
  40.6 4.9 %collective-permute-start.3 = (bf16[1,128,128]{2,1,0:T(8,128)(2,1)S(1)}, bf16[1,128,128]{2,1,0:T(8,128)(2,1)S(1)}, u32[]{:S(2)}, u32[]{:S(2)}) collective-permute-start(bf16[1,128,128]{2,1,0:T(8,128)(2,1)S(1)} %back_low.1), channel_id=1, source_target_pairs={{0,8},{1,9},{2,10},{3,11},{4,12},{5,13},{6,14},{7,15},{8,0},{9,1},... | collective-permute-start | bytes 98312 | tf_op jit(solution)/shard_map/ppermute | solution.py:397
  45.5 4.3 %collective-permute-start.4 = (bf16[2,128,128]{2,1,0:T(8,128)(2,1)S(1)}, bf16[2,128,128]{2,1,0:T(8,128)(2,1)S(1)}, u32[]{:S(2)}, u32[]{:S(2)}) collective-permute-start(bf16[2,128,128]{2,1,0:T(8,128)(2,1)S(1)} %pad_maximum_fusion.6), channel_id=1, source_target_pairs={{0,4},{1,5},{2,6},{3,7},{4,0},{5,1},{6,2},{7,3},{8,12},{9,13},{10,... | collective-permute-start | bytes 196616 | tf_op jit(solution)/shard_map/ppermute | solution.py:397
  49.9 1.4 collective-permute-start.5
  50.0 20.5 %collective-permute-start.9 = (bf16[2,128,512]{2,1,0:T(8,128)(2,1)S(1)}, bf16[2,128,512]{2,1,0:T(8,128)(2,1)S(1)}, u32[]{:S(2)}, u32[]{:S(2)}) collective-permute-start(bf16[2,128,512]{2,1,0:T(8,128)(2,1)S(1)} %get-tuple-element.48), channel_id=1, source_target_pairs={{0,8},{1,9},{2,10},{3,11},{4,12},{5,13},{6,14},{7,15},{8,0},{9,1},... | collective-permute-start | bytes 786440 | tf_op jit(solution)/shard_map/ppermute | solution.py:397
  51.3 19.1 %collective-permute-start.11 = (bf16[2,128,512]{2,1,0:T(8,128)(2,1)S(1)}, bf16[2,128,512]{2,1,0:T(8,128)(2,1)S(1)}, u32[]{:S(2)}, u32[]{:S(2)}) collective-permute-start(bf16[2,128,512]{2,1,0:T(8,128)(2,1)S(1)} %get-tuple-element.50), channel_id=1, source_target_pairs={{0,12},{1,13},{2,14},{3,15},{4,8},{5,9},{6,10},{7,11},{8,4},{9,5},... | collective-permute-start | bytes 786440 | tf_op jit(solution)/shard_map/ppermute | solution.py:397
  53.6 34.9 %copy-start.6 = (bf16[1024,512]{1,0:T(8,128)(2,1)S(1)}, bf16[1024,512]{1,0:T(8,128)(2,1)}, u32[]{:S(2)}) copy-start(bf16[1024,512]{1,0:T(8,128)(2,1)} %weight.1) | copy-start | bytes 3145732
  70.4 24.9 %collective-permute-start.10 = (bf16[2,128,512]{2,1,0:T(8,128)(2,1)}, bf16[2,128,512]{2,1,0:T(8,128)(2,1)S(1)}, u32[]{:S(2)}, u32[]{:S(2)}) collective-permute-start(bf16[2,128,512]{2,1,0:T(8,128)(2,1)} %get-tuple-element.64), channel_id=1, source_target_pairs={{0,4},{1,5},{2,6},{3,7},{4,0},{5,1},{6,2},{7,3},{8,12},{9,13},{10,... | collective-permute-start | bytes 786440 | tf_op jit(solution)/shard_map/ppermute | solution.py:397
  70.4 24.9 %collective-permute-start.12 = (bf16[2,128,512]{2,1,0:T(8,128)(2,1)}, bf16[2,128,512]{2,1,0:T(8,128)(2,1)S(1)}, u32[]{:S(2)}, u32[]{:S(2)}) collective-permute-start(bf16[2,128,512]{2,1,0:T(8,128)(2,1)} %get-tuple-element.65), channel_id=1, source_target_pairs={{0,1},{1,0},{2,3},{3,2},{4,5},{5,4},{6,7},{7,6},{8,9},{9,8},{10,11... | collective-permute-start | bytes 786440 | tf_op jit(solution)/shard_map/ppermute | solution.py:397
  70.5 24.9 %collective-permute-start.13 = (bf16[2,128,512]{2,1,0:T(8,128)(2,1)}, bf16[2,128,512]{2,1,0:T(8,128)(2,1)S(1)}, u32[]{:S(2)}, u32[]{:S(2)}) collective-permute-start(bf16[2,128,512]{2,1,0:T(8,128)(2,1)} %get-tuple-element.66), channel_id=1, source_target_pairs={{0,9},{1,8},{2,11},{3,10},{4,13},{5,12},{6,15},{7,14},{8,1},{9,0},... | collective-permute-start | bytes 786440 | tf_op jit(solution)/shard_map/ppermute | solution.py:397
  80.9 18.2 %collective-permute-start.14 = (bf16[2,128,512]{2,1,0:T(8,128)(2,1)}, bf16[2,128,512]{2,1,0:T(8,128)(2,1)S(1)}, u32[]{:S(2)}, u32[]{:S(2)}) collective-permute-start(bf16[2,128,512]{2,1,0:T(8,128)(2,1)} %get-tuple-element.67), channel_id=1, source_target_pairs={{0,5},{1,4},{2,7},{3,6},{4,1},{5,0},{6,3},{7,2},{8,13},{9,12},{10,... | collective-permute-start | bytes 786440 | tf_op jit(solution)/shard_map/ppermute | solution.py:397
  81.8 17.3 %collective-permute-start.15 = (bf16[2,128,512]{2,1,0:T(8,128)(2,1)}, bf16[2,128,512]{2,1,0:T(8,128)(2,1)S(1)}, u32[]{:S(2)}, u32[]{:S(2)}) collective-permute-start(bf16[2,128,512]{2,1,0:T(8,128)(2,1)} %get-tuple-element.68), channel_id=1, source_target_pairs={{0,13},{1,12},{2,15},{3,14},{4,9},{5,8},{6,11},{7,10},{8,5},{9,4},... | collective-permute-start | bytes 786440 | tf_op jit(solution)/shard_map/ppermute | solution.py:397
  87.1 1.3 copy-start.2
  88.4 10.7 %copy-start.10 = (bf16[2,128,512]{2,1,0:T(8,128)(2,1)S(1)}, bf16[2,128,512]{2,1,0:T(8,128)(2,1)}, u32[]{:S(2)}) copy-start(bf16[2,128,512]{2,1,0:T(8,128)(2,1)} %copy-done.9) | copy-start | bytes 786436
  103.6 43.7 %copy-start.3 = (bf16[8,128,1024]{2,1,0:T(8,128)(2,1)S(1)}, bf16[8,128,1024]{2,1,0:T(8,128)(2,1)}, u32[]{:S(2)}) copy-start(bf16[8,128,1024]{2,1,0:T(8,128)(2,1)} %copy-done.2) | copy-start | bytes 6291460
  103.6 64.8 %copy-start.12 = (bf16[2,128,512]{2,1,0:T(8,128)(2,1)S(1)}, bf16[2,128,512]{2,1,0:T(8,128)(2,1)}, u32[]{:S(2)}) copy-start(bf16[2,128,512]{2,1,0:T(8,128)(2,1)} %copy-done.11) | copy-start | bytes 786436
  103.6 1.6 collective-permute-start.16
  105.3 6.4 %collective-permute-start.17 = (f32[2,128,128]{2,1,0:T(8,128)S(1)}, f32[2,128,128]{2,1,0:T(8,128)S(1)}, u32[]{:S(2)}, u32[]{:S(2)}) collective-permute-start(f32[2,128,128]{2,1,0:T(8,128)S(1)} %slice.25), channel_id=1, source_target_pairs={{0,4},{1,5},{2,6},{3,7},{4,0},{5,1},{6,2},{7,3},{8,12},{9,13},{10,... | collective-permute-start | bytes 393224 | tf_op jit(solution)/shard_map/ppermute | solution.py:397
  111.7 5.4 %collective-permute-start.18 = (f32[1,128,128]{2,1,0:T(8,128)S(1)}, f32[1,128,128]{2,1,0:T(8,128)S(1)}, u32[]{:S(2)}, u32[]{:S(2)}) collective-permute-start(f32[1,128,128]{2,1,0:T(8,128)S(1)} %get-tuple-element.92), channel_id=1, source_target_pairs={{0,8},{1,9},{2,10},{3,11},{4,12},{5,13},{6,14},{7,15},{8,0},{9,1},... | collective-permute-start | bytes 196616 | tf_op jit(solution)/shard_map/ppermute | solution.py:397
  113.8 64.8 %collective-permute-start.26 = (bf16[8,128,512]{2,1,0:T(8,128)(2,1)}, bf16[8,128,512]{2,1,0:T(8,128)(2,1)}, u32[]{:S(2)}, u32[]{:S(2)}) collective-permute-start(bf16[8,128,512]{2,1,0:T(8,128)(2,1)} %get-tuple-element.89), channel_id=1, source_target_pairs={{0,2},{1,3},{2,0},{3,1},{4,6},{5,7},{6,4},{7,5},{8,10},{9,11},{10,... | collective-permute-start | bytes 3145736 | tf_op jit(solution)/shard_map/ppermute | solution.py:397
  117.7 4.9 %collective-permute-start.28 = (bf16[1,128,128]{2,1,0:T(8,128)(2,1)S(1)}, bf16[1,128,128]{2,1,0:T(8,128)(2,1)S(1)}, u32[]{:S(2)}, u32[]{:S(2)}) collective-permute-start(bf16[1,128,128]{2,1,0:T(8,128)(2,1)S(1)} %hidden_low.1), channel_id=1, source_target_pairs={{0,8},{1,9},{2,10},{3,11},{4,12},{5,13},{6,14},{7,15},{8,0},{9,1},... | collective-permute-start | bytes 98312 | tf_op jit(solution)/shard_map/ppermute | solution.py:397
  122.6 4.5 %collective-permute-start.29 = (bf16[2,128,128]{2,1,0:T(8,128)(2,1)S(1)}, bf16[2,128,128]{2,1,0:T(8,128)(2,1)S(1)}, u32[]{:S(2)}, u32[]{:S(2)}) collective-permute-start(bf16[2,128,128]{2,1,0:T(8,128)(2,1)S(1)} %pad_maximum_fusion.7), channel_id=1, source_target_pairs={{0,4},{1,5},{2,6},{3,7},{4,0},{5,1},{6,2},{7,3},{8,12},{9,13},{10,... | collective-permute-start | bytes 196616 | tf_op jit(solution)/shard_map/ppermute | solution.py:397
  124.2 17.8 %collective-permute-start.8 = (bf16[2,128,512]{2,1,0:T(8,128)(2,1)S(1)}, bf16[2,128,512]{2,1,0:T(8,128)(2,1)S(1)}, u32[]{:S(2)}, u32[]{:S(2)}) collective-permute-start(bf16[2,128,512]{2,1,0:T(8,128)(2,1)S(1)} %get-tuple-element.57), channel_id=1, source_target_pairs={{0,8},{1,9},{2,10},{3,11},{4,12},{5,13},{6,14},{7,15},{8,0},{9,1},... | collective-permute-start | bytes 786440 | tf_op jit(solution)/shard_map/ppermute | solution.py:397
  126.5 15.5 %collective-permute-start.20 = (bf16[2,128,512]{2,1,0:T(8,128)(2,1)S(1)}, bf16[2,128,512]{2,1,0:T(8,128)(2,1)S(1)}, u32[]{:S(2)}, u32[]{:S(2)}) collective-permute-start(bf16[2,128,512]{2,1,0:T(8,128)(2,1)S(1)} %get-tuple-element.59), channel_id=1, source_target_pairs={{0,12},{1,13},{2,14},{3,15},{4,8},{5,9},{6,10},{7,11},{8,4},{9,5},... | collective-permute-start | bytes 786440 | tf_op jit(solution)/shard_map/ppermute | solution.py:397
  127.1 19.7 %collective-permute-start.30 = (bf16[4,128,128]{2,1,0:T(8,128)(2,1)S(1)}, bf16[4,128,128]{2,1,0:T(8,128)(2,1)}, u32[]{:S(2)}, u32[]{:S(2)}) collective-permute-start(bf16[4,128,128]{2,1,0:T(8,128)(2,1)S(1)} %pad_maximum_fusion.5), channel_id=1, source_target_pairs={{0,1},{1,0},{2,3},{3,2},{4,5},{5,4},{6,7},{7,6},{8,9},{9,8},{10,11... | collective-permute-start | bytes 393224 | tf_op jit(solution)/shard_map/ppermute | solution.py:397
  127.2 21.1 %collective-permute-start.19 = (bf16[2,128,512]{2,1,0:T(8,128)(2,1)}, bf16[2,128,512]{2,1,0:T(8,128)(2,1)}, u32[]{:S(2)}, u32[]{:S(2)}) collective-permute-start(bf16[2,128,512]{2,1,0:T(8,128)(2,1)} %get-tuple-element.83), channel_id=1, source_target_pairs={{0,4},{1,5},{2,6},{3,7},{4,0},{5,1},{6,2},{7,3},{8,12},{9,13},{10,... | collective-permute-start | bytes 786440 | tf_op jit(solution)/shard_map/ppermute | solution.py:397
  142.0 9.4 %collective-permute-start.21 = (bf16[2,128,512]{2,1,0:T(8,128)(2,1)}, bf16[2,128,512]{2,1,0:T(8,128)(2,1)}, u32[]{:S(2)}, u32[]{:S(2)}) collective-permute-start(bf16[2,128,512]{2,1,0:T(8,128)(2,1)} %get-tuple-element.84), channel_id=1, source_target_pairs={{0,1},{1,0},{2,3},{3,2},{4,5},{5,4},{6,7},{7,6},{8,9},{9,8},{10,11... | collective-permute-start | bytes 786440 | tf_op jit(solution)/shard_map/ppermute | solution.py:397
  142.7 14.6 %collective-permute-start.22 = (bf16[2,128,512]{2,1,0:T(8,128)(2,1)}, bf16[2,128,512]{2,1,0:T(8,128)(2,1)}, u32[]{:S(2)}, u32[]{:S(2)}) collective-permute-start(bf16[2,128,512]{2,1,0:T(8,128)(2,1)} %get-tuple-element.85), channel_id=1, source_target_pairs={{0,9},{1,8},{2,11},{3,10},{4,13},{5,12},{6,15},{7,14},{8,1},{9,0},... | collective-permute-start | bytes 786440 | tf_op jit(solution)/shard_map/ppermute | solution.py:397
  146.8 11.7 %collective-permute-start.23 = (bf16[2,128,512]{2,1,0:T(8,128)(2,1)S(1)}, bf16[2,128,512]{2,1,0:T(8,128)(2,1)}, u32[]{:S(2)}, u32[]{:S(2)}) collective-permute-start(bf16[2,128,512]{2,1,0:T(8,128)(2,1)S(1)} %get-tuple-element.86), channel_id=1, source_target_pairs={{0,5},{1,4},{2,7},{3,6},{4,1},{5,0},{6,3},{7,2},{8,13},{9,12},{10,... | collective-permute-start | bytes 786440 | tf_op jit(solution)/shard_map/ppermute | solution.py:397
  148.3 20.1 %collective-permute-start.24 = (bf16[2,128,512]{2,1,0:T(8,128)(2,1)S(1)}, bf16[2,128,512]{2,1,0:T(8,128)(2,1)S(1)}, u32[]{:S(2)}, u32[]{:S(2)}) collective-permute-start(bf16[2,128,512]{2,1,0:T(8,128)(2,1)S(1)} %get-tuple-element.87), channel_id=1, source_target_pairs={{0,13},{1,12},{2,15},{3,14},{4,9},{5,8},{6,11},{7,10},{8,5},{9,4},... | collective-permute-start | bytes 786440 | tf_op jit(solution)/shard_map/ppermute | solution.py:397
  151.4 20.6 %collective-permute-start.27 = (bf16[8,128,128]{2,1,0:T(8,128)(2,1)S(1)}, bf16[8,128,128]{2,1,0:T(8,128)(2,1)S(1)}, u32[]{:S(2)}, u32[]{:S(2)}) collective-permute-start(bf16[8,128,128]{2,1,0:T(8,128)(2,1)S(1)} %constant_dynamic-slice_fusion), channel_id=1, source_target_pairs={{0,2},{1,3},{2,0},{3,1},{4,6},{5,7},{6,4},{7,5},{8,10},{9,11},{10,... | collective-permute-start | bytes 786440 | tf_op jit(solution)/shard_map/ppermute | solution.py:397
  157.2 14.8 %collective-permute-start.31 = (bf16[8,128,128]{2,1,0:T(8,128)(2,1)S(1)}, bf16[8,128,128]{2,1,0:T(8,128)(2,1)S(1)}, u32[]{:S(2)}, u32[]{:S(2)}) collective-permute-start(bf16[8,128,128]{2,1,0:T(8,128)(2,1)S(1)} %pad_maximum_fusion.3.hiddens), channel_id=1, source_target_pairs={{0,2},{1,3},{2,0},{3,1},{4,6},{5,7},{6,4},{7,5},{8,10},{9,11},{10,... | collective-permute-start | bytes 786440 | tf_op jit(solution)/shard_map/ppermute | solution.py:397
  158.5 20.1 %collective-permute-start.25 = (bf16[8,128,128]{2,1,0:T(8,128)(2,1)S(1)}, bf16[8,128,128]{2,1,0:T(8,128)(2,1)S(1)}, u32[]{:S(2)}, u32[]{:S(2)}) collective-permute-start(bf16[8,128,128]{2,1,0:T(8,128)(2,1)S(1)} %pad_maximum_fusion.2.backs), channel_id=1, source_target_pairs={{0,2},{1,3},{2,0},{3,1},{4,6},{5,7},{6,4},{7,5},{8,10},{9,11},{10,... | collective-permute-start | bytes 786440 | tf_op jit(solution)/shard_map/ppermute | solution.py:397
  172.0 6.6 %copy-start.8 = (bf16[8,128,512]{2,1,0:T(8,128)(2,1)S(1)}, bf16[8,128,512]{2,1,0:T(8,128)(2,1)}, u32[]{:S(2)}) copy-start(bf16[8,128,512]{2,1,0:T(8,128)(2,1)} %copy-done.7) | copy-start | bytes 3145732
  (5 other events, 4.0 us)

commit v4 on v3

--- a/solution.py
+++ b/solution.py
@@ -16,6 +16,22 @@
     for bit in range(bits):
         line |= ((slot >> bit) & 1) << (bits - 1 - bit)
     return ((line // pair_bit) * 2 * pair_bit) | (line % pair_bit)
+
+
+def line_index(place):
+    return (place // (2 * pair_bit)) * pair_bit + place % pair_bit
+
+
+def line_place(index, side):
+    return (index // pair_bit) * 2 * pair_bit + side * pair_bit + index % pair_bit
+
+
+def slot_index(place, slot, members):
+    return line_index(place) ^ line_index(line_offset(slot, members))
+
+
+def side_of(place):
+    return (place // pair_bit) % 2
 
 
 def params():
@@ -94,27 +110,29 @@
 
 
 def pack_kernel(place, *refs):
-    count = len(refs) // 3
-    for slot in range(count):
-        out = refs[2 * count + slot]
-        out[0] = refs[2 * slot][...]
-        out[1] = refs[2 * slot + 1][...]
+    out = refs[-1]
+    for index in range(out.shape[0]):
+        for half in range(2):
+            out[index, half] = refs[2 * index + half][...]
 
 
 def pack_tokens(place, tokens, members, width):
     rows = tokens.shape[0]
 
-    def spec(flip):
-        return pl.BlockSpec((rows, width), lambda i, place: (0, place[0] ^ flip))
-
-    specs = []
-    for slot in range(members):
-        offset = line_offset(slot, members)
-        specs += [spec(offset), spec(offset ^ pair_bit)]
-    shape = jax.ShapeDtypeStruct((2, rows, width), tokens.dtype)
-    return call(
-        pack_kernel, "pack_tokens", (place,), [tokens] * len(specs), specs, [shape] * members
-    )
+    def spec(index, half):
+        return pl.BlockSpec(
+            (rows, width),
+            lambda i, place: (0, line_place(index, side_of(place[0]) ^ half)),
+        )
+
+    return call(
+        pack_kernel,
+        "pack_tokens",
+        (place,),
+        [tokens] * (2 * members),
+        [spec(index, half) for index in range(members) for half in range(2)],
+        [jax.ShapeDtypeStruct((members, 2, rows, width), tokens.dtype)],
+    )[0]
 
 
 def rank_row(ranks, adapter, extent):
@@ -141,27 +159,48 @@
     )[0]
 
 
-def input_kernel(adapters, place, gradients, backs, weight, weight_pair, down_pair, *refs):
-    members, rows, depth = gradients.shape
-    downs, outs = refs[:members], refs[members:]
-    for first in range(0, members, 4):
-        some = min(4, members - first)
-        lines = gradients[first : first + some].reshape(some * rows, depth)
+def column_of(place, width, lanes):
+    return pl.multiple_of(place * width // lanes * lanes, lanes)
+
+
+def input_kernel(adapters, place, backs, weight, weight_pair, down_pair, *refs):
+    members, rows, _ = backs.shape
+    gradients, downs, outs = refs[:members], refs[members : 2 * members], refs[2 * members : -2]
+    columns = refs[-2:]
+    lanes = columns[0].shape[2]
+    value_width = gradients[0].shape[2] // (2 * members)
+    piece = rows // len(outs)
+    some = min(4, members)
+    for first in range(0, members, some):
+        slots = range(first, first + some)
+        lines = jnp.concatenate([gradients[slot][0] for slot in slots], axis=0)
         for half in range(2):
             frozen = jnp.dot(
                 lines, (weight, weight_pair)[half][...], preferred_element_type=jnp.float32
             )
-            for slot in range(first, first + some):
+            for slot in slots:
                 down = downs[slot][0] if half == 0 else down_pair[slot]
                 low = jnp.dot(backs[slot], down, preferred_element_type=jnp.float32)
                 at = (slot - first) * rows
-                outs[slot][half] = (frozen[at : at + rows] + low).astype(jnp.bfloat16)
-
-
-def input_slices(adapters, place, gradients, backs, weight, weight_pair, down_maps, down_pair):
-    members, rows, _ = gradients.shape
-    operands = (gradients, backs, weight, weight_pair, down_pair)
-    shape = jax.ShapeDtypeStruct((2, rows, weight.shape[1]), jnp.bfloat16)
+                result = (frozen[at : at + rows] + low).astype(jnp.bfloat16)
+                index = slot_index(place[0], slot, members)
+                for part, out in enumerate(outs):
+                    out[index, half] = result[part * piece : (part + 1) * piece]
+    for side in range(2):
+        column = column_of(place[0] ^ (side * pair_bit), value_width, lanes)
+        for slot in range(members):
+            columns[side][slot] = gradients[slot][0, :, pl.ds(column, lanes)]
+
+
+def input_slices(
+    adapters, place, gradients, backs, weight, weight_pair, down_maps, down_pair, pieces
+):
+    members, rows, _ = backs.shape
+    width = weight.shape[1]
+    lanes = max(128, gradients[0].shape[2] // (2 * members))
+    operands = (backs, weight, weight_pair, down_pair) + tuple(gradients)
+    shape = jax.ShapeDtypeStruct((members, 2, rows // pieces, width), jnp.bfloat16)
+    columns = jax.ShapeDtypeStruct((members, rows, lanes), jnp.bfloat16)
     return call(
         input_kernel,
         "input_slices",
@@ -169,38 +208,37 @@
         operands + (down_maps,) * members,
         [whole(operand.shape) for operand in operands]
         + [picked(down_maps, line_offset(slot, members)) for slot in range(members)],
-        [shape] * members,
-    )
-
-
-def hidden_kernel(adapters, place, down_pair, *refs):
+        [shape] * pieces + [columns] * 2,
+    )
+
+
+def hidden_kernel(adapters, place, down_pair, tokens, *refs):
     members = down_pair.shape[0]
-    downs, tokens = refs[:members], refs[members : 2 * members]
-    parts, own, pair = refs[2 * members :]
+    downs = refs[:members]
+    parts, own, pair = refs[members:]
     across = (((1,), (1,)), ((), ()))
-    for slot in range(members):
-        own[slot] = tokens[slot][0]
-        pair[slot] = tokens[slot][1]
+    for slot in reversed(range(members)):
+        index = slot_index(place[0], slot, members)
+        own[slot] = tokens[index, 0]
+        pair[slot] = tokens[index, 1]
         parts[slot] = lax.dot_general(
-            tokens[slot][0], downs[slot][0], across, preferred_element_type=jnp.float32
+            tokens[index, 0], downs[slot][0], across, preferred_element_type=jnp.float32
         ) + lax.dot_general(
-            tokens[slot][1], down_pair[slot], across, preferred_element_type=jnp.float32
+            tokens[index, 1], down_pair[slot], across, preferred_element_type=jnp.float32
         )
 
 
 def hidden_parts(adapters, place, down_maps, down_pair, tokens):
-    members = len(tokens)
-    _, rows, width = tokens[0].shape
+    members, _, rows, width = tokens.shape
     extent = down_maps.shape[1]
-    tokens_shape = jax.ShapeDtypeStruct((members, rows, width), tokens[0].dtype)
+    tokens_shape = jax.ShapeDtypeStruct((members, rows, width), tokens.dtype)
     return call(
         hidden_kernel,
         "hidden_parts",
         (adapters, place),
-        [down_pair] + [down_maps] * members + list(tokens),
-        [whole(down_pair.shape)]
-        + [picked(down_maps, line_offset(slot, members)) for slot in range(members)]
-        + [whole(tokens[0].shape)] * members,
+        [down_pair, tokens] + [down_maps] * members,
+        [whole(down_pair.shape), whole(tokens.shape)]
+        + [picked(down_maps, line_offset(slot, members)) for slot in range(members)],
         [
             jax.ShapeDtypeStruct((members, rows, extent), jnp.float32),
             tokens_shape,
@@ -225,28 +263,34 @@
     )[0]
 
 
-def join_kernel(place, *refs):
+def join_kernel(place, source, *refs):
     out = refs[-1]
-    members = len(refs) - 1
-    width = refs[0].shape[2]
-    for slot in range(members):
+    members, _, _, width = source.shape
+    for index in range(members):
         for half in range(2):
-            source = place[0] ^ line_offset(slot, members) ^ (half * pair_bit)
-            columns = pl.ds(pl.multiple_of(source * width, width), width)
-            out[:, columns] = refs[slot][half]
-
-
-def join_columns(place, pieces):
-    members = len(pieces)
-    _, rows, width = pieces[0].shape
-    return call(
+            column = line_place(index, side_of(place[0]) ^ half) * width
+            out[:, pl.ds(pl.multiple_of(column, width), width)] = source[index, half]
+
+
+def join_columns(place, source, part, parts, before=None):
+    members, _, rows, width = source.shape
+    operands, specs, aliases = [source], [whole(source.shape)], {}
+    if before is not None:
+        operands, specs = operands + [before], specs + [pl.BlockSpec(memory_space=pl.ANY)]
+        aliases = {2: 0}
+    return pl.pallas_call(
         join_kernel,
-        "join_columns",
-        (place,),
-        pieces,
-        [whole(pieces[0].shape)] * members,
-        [jax.ShapeDtypeStruct((rows, 2 * members * width), pieces[0].dtype)],
-    )[0]
+        out_shape=jax.ShapeDtypeStruct((parts * rows, 2 * members * width), source.dtype),
+        grid_spec=pltpu.PrefetchScalarGridSpec(
+            num_scalar_prefetch=1,
+            grid=(1,),
+            in_specs=specs,
+            out_specs=pl.BlockSpec((rows, 2 * members * width), lambda i, place: (part, 0)),
+        ),
+        input_output_aliases=aliases,
+        compiler_params=params(),
+        name="join_columns",
+    )(place, *operands)
 
 
 def list_members(adapters, place, members, head, following):
@@ -359,24 +403,17 @@
 
 
 def up_gradients(adapters, place, ranks, gradients, gradients_pair, hiddens, hiddens_pair, width):
-    members, rows, lanes = gradients_pair.shape
+    members, _, lanes = gradients.shape
     extent = hiddens.shape[2]
     num_adapters = ranks.shape[0]
     chunk = 32 if num_adapters % 32 == 0 else 1
+    operands = (gradients, gradients_pair, hiddens, hiddens_pair)
     return call(
         up_gradient_kernel,
         "up_gradients",
         (adapters, place, ranks),
-        (gradients, gradients_pair, hiddens, hiddens_pair),
-        [
-            pl.BlockSpec(
-                (members, rows, lanes),
-                lambda i, adapters, place, ranks: (0, 0, place[0] * width // lanes),
-            ),
-            whole(gradients_pair.shape),
-            whole(hiddens.shape),
-            whole(hiddens.shape),
-        ],
+        operands,
+        [whole(operand.shape) for operand in operands],
         [jax.ShapeDtypeStruct((num_adapters, width, extent), jnp.bfloat16)],
         scratch=[
             pltpu.SMEM((2, num_adapters), jnp.int32),
@@ -392,6 +429,14 @@
     return lax.all_to_all(pieces, "dp", split_axis=0, concat_axis=0, tiled=True)
 
 
+def exchange_line(pieces):
+    members = pieces.shape[0]
+    groups = [[line_place(index, side) for index in range(members)] for side in range(2)]
+    return lax.all_to_all(
+        pieces, "dp", split_axis=0, concat_axis=0, axis_index_groups=groups, tiled=True
+    )
+
+
 def swap(array, flip):
     devices = lax.axis_size("dp")
     return lax.ppermute(array, "dp", [(i, i ^ flip) for i in range(devices)])
@@ -401,13 +446,18 @@
     return lax.optimization_barrier((first, second))
 
 
-def gather_step(held, members):
-    return jnp.concatenate([held, swap(held, line_offset(held.shape[0], members))], axis=0)
-
-
 def gather_line(held, members):
     while held.shape[0] < members:
-        held = gather_step(held, members)
+        arrived = swap(held, line_offset(held.shape[0], members))
+        held = jnp.concatenate([held, arrived], axis=0)
+    return held
+
+
+def gather_apart(own, members):
+    held = [own]
+    while len(held) < members:
+        offset = line_offset(len(held), members)
+        held = held + [swap(block, offset) for block in held]
     return held
 
 
@@ -425,68 +475,47 @@
     members = devices // 2
     num_adapters, extent, width = down_maps.shape
     rows, depth = output_gradient.shape
-    value_width = depth // devices
     place = lax.axis_index("dp").astype(jnp.int32).reshape(1)
     adapters = adapter_per_block
     offsets = [line_offset(slot, members) for slot in range(members)]
-    far = [slot for slot in range(members) if slot % 2]
-    near = [slot for slot in range(1, members) if slot % 2 == 0]
-
-    gradients = gather_step(output_gradient.reshape(1, rows, depth), members)
+
+    gradients = gather_apart(output_gradient.reshape(1, rows, depth), members)
     own_up = exchange(gather_up(adapters, place, up_maps)).reshape(depth, extent)
+    arrived = exchange_line(pack_tokens(place, tokens, members, width))
+    weight_pair = swap(value_weight, pair_bit)
     down_pair = swap(
         collect(adapters, place, down_maps, [o ^ pair_bit for o in offsets], "collect_down"),
         pair_bit,
     )
-    weight_pair = swap(value_weight, pair_bit)
-
-    packs = list(pack_tokens(place, tokens, members, width))
-    arrived = [packs[0]] + [None] * (members - 1)
-    early = far[: len(far) // 2]
-    for slot in early:
-        arrived[slot] = swap(packs[slot], offsets[slot])
-    gradients = gather_step(gradients, members)
-    gradients, packs = tie(gradients, packs)
-    for slot in near + far[len(far) // 2 :]:
-        arrived[slot] = swap(packs[slot], offsets[slot])
-    gradients = gather_line(gradients, members)
 
     backs = gather_line(back_rows(adapters, place, ranks, output_gradient, own_up), members)
-    slices = list(
-        input_slices(
-            adapters, place, gradients, backs, value_weight, weight_pair, down_maps, down_pair
-        )
-    )
-    results = [slices[0]] + [None] * (members - 1)
-    for slot in early:
-        results[slot] = swap(slices[slot], offsets[slot])
-
-    slices, arrived = tie(slices, arrived)
+    first, second, columns, columns_pair = input_slices(
+        adapters, place, gradients, backs, value_weight, weight_pair, down_maps, down_pair, 2
+    )
+    first_result = exchange_line(first)
+
+    second, arrived = tie(second, arrived)
     parts, tokens_own, tokens_pair = hidden_parts(
         adapters, place, down_maps, down_pair, arrived
     )
     kept, received = reduce_line(parts, members)
-    received, slices = tie(received, slices)
-    for slot in near + far[len(far) // 2 :]:
-        results[slot] = swap(slices[slot], offsets[slot])
-    input_grad = join_columns(place, results)
-
+    received, second = tie(received, second)
+    second_result = exchange_line(second)
+
+    columns_other = swap(columns_pair, pair_bit)
+    backs_pair = swap(backs, pair_bit)
     tokens_other = swap(tokens_pair, pair_bit)
-    backs_pair = swap(backs, pair_bit)
     down_gradient = down_gradients(
         adapters, place, backs, backs_pair, tokens_own, tokens_other, num_adapters
-    )
-
-    lanes = max(128, value_width)
-    column = (place[0] ^ pair_bit) * value_width // lanes * lanes
-    gradients_pair = swap(
-        lax.dynamic_slice(gradients, (0, 0, column), (members, rows, lanes)), pair_bit
     )
     hiddens = gather_line(hidden_rows(adapters, place, ranks, kept, received), members)
     hiddens_pair = swap(hiddens, pair_bit)
     up_gradient = up_gradients(
-        adapters, place, ranks, gradients, gradients_pair, hiddens, hiddens_pair, value_width
-    )
+        adapters, place, ranks, columns, columns_other, hiddens, hiddens_pair, depth // devices
+    )
+    half_joined = join_columns(place, first_result, 0, 2)
+    down_gradient, second_result = tie(down_gradient, second_result)
+    input_grad = join_columns(place, second_result, 1, 2, half_joined)
     return (input_grad, down_gradient, up_gradient)
 
 

time: 189 us -> 211 us (1.12)
  waiting for transfers between devices: 85.9 us -> 130 us
  starting transfers between devices: 51.6 us -> 39.3 us
  other arithmetic: 5.14 us -> 0.15 us
  Pallas kernels: 35.5 us -> 31.9 us
    ppermute x32 -> x22, waiting for transfers between devices: 83 us -> 121 us  [swap(): return lax.ppermute(array, 'dp', [(i, i ^ flip) for i in range(devices)])]
    ppermute x32 -> x22, starting transfers between devices: 46 us -> 20.3 us  [swap(): return lax.ppermute(array, 'dp', [(i, i ^ flip) for i in range(devices)])]
    all_to_all x0 -> x3, starting transfers between devices: none -> 11.6 us  [exchange_line(): lax.all_to_all(pieces, 'dp', split_axis=0, concat_axis=0, axis_index_grou...]
    pallas_call x10 -> x9, Pallas kernels: 35.5 us -> 28.5 us  [call(): pl.pallas_call(kernel, out_shape=out_shapes, grid_spec=pltpu.PrefetchScal...]
    all_to_all x1, waiting for transfers between devices: 2.89 us -> 8.54 us  [exchange(): return lax.all_to_all(pieces, 'dp', split_axis=0, concat_axis=0, tiled=True)]
    concatenate x8 -> x6, other arithmetic: 5.09 us -> 0.1 us  [gather_line(): held = jnp.concatenate([held, arrived], axis=0)]
    pallas_call x0 -> x2, Pallas kernels: none -> 3.34 us  [join_columns(): pl.pallas_call(join_kernel, out_shape=jax.ShapeDtypeStruct((parts * rows,...]
    unnamed x41 -> x40, local copies, waits for them, and re-layouts: 7.86 us -> 8.53 us
  transfers between devices with their start and end apart: 33 -> 26, of which waited for: 15 -> 14; matrix products, arithmetic and copies ran while one was open for 3% -> 0% of each run, Pallas kernels for 12% -> 14%
where the time goes in v4:
time: 211 us; the launch traced here: 210 us
  waiting for transfers between devices  130 us (62%)
  starting transfers between devices  39.3 us (19%)
  Pallas kernels  31.9 us (15%)
  local copies, waits for them, and re-layouts  8.57 us (4%)
    ppermute x22, waiting for transfers between devices, swap(): return lax.ppermute(array, 'dp', [(i, i ^ flip) for i in range(devices)])  121 us
    pallas_call x9, Pallas kernels, call(): pl.pallas_call(kernel, out_shape=out_shapes, grid_spec=pltpu.PrefetchScal...  28.5 us
    ppermute x22, starting transfers between devices, swap(): return lax.ppermute(array, 'dp', [(i, i ^ flip) for i in range(devices)])  20.3 us
    all_to_all x3, starting transfers between devices, exchange_line(): lax.all_to_all(pieces, 'dp', split_axis=0, concat_axis=0, axis_index_grou...  11.6 us
    all_to_all x1, waiting for transfers between devices, exchange(): return lax.all_to_all(pieces, 'dp', split_axis=0, concat_axis=0, tiled=True)  8.54 us
    unnamed x40, local copies, waits for them, and re-layouts  8.53 us
    all_to_all x1, starting transfers between devices, exchange(): return lax.all_to_all(pieces, 'dp', split_axis=0, concat_axis=0, tiled=True)  7.39 us
  transfers between devices with their start and end apart: 26, of which 14 were waited for; matrix products, arithmetic and copies ran while one was open for 0% of the time, Pallas kernels for 14%

profile of v4, /device:TPU:0, one launch (start us, length us, event | category | flops | bytes accessed | tf_op | source)
XLA Modules:
  0.0 210.5 jit_solution(7208256205498400952)
XLA Ops:
  0.6 1.2 copy-done.1
  1.9 0.7 copy-done.12
  2.5 1.3 gather_up.1
  3.8 7.4 %all-to-all-start = ((bf16[16,64,128]{2,1,0:T(8,128)(2,1)}), bf16[16,64,128]{2,1,0:T(8,128)(2,1)S(1)}, u32[]{:S(2)}, u32[]{:S(2)}) async-start(bf16[16,64,128]{2,1,0:T(8,128)(2,1)} %gather_up.1), calls=%async_computation | async-start | bytes 524288 | tf_op jit(solution)/shard_map/all_to_all | solution.py:429
  11.4 1.3 copy-done.2
  12.7 8.5 %all-to-all-done = bf16[16,64,128]{2,1,0:T(8,128)(2,1)S(1)} async-done(((bf16[16,64,128]{2,1,0:T(8,128)(2,1)}), bf16[16,64,128]{2,1,0:T(8,128)(2,1)S(1)}, u32[]{:S(2)}, u32[]{:S(2)}) %all-to-all-start) | async-done | bytes 262176 | tf_op jit(solution)/shard_map/all_to_all | solution.py:429
  21.2 3.6 %all-to-all-start.1 = ((bf16[8,2,128,512]{3,2,1,0:T(8,128)(2,1)}), bf16[8,2,128,512]{3,2,1,0:T(8,128)(2,1)S(1)}, u32[]{:S(2)}, u32[]{:S(2)}) async-start(bf16[8,2,128,512]{3,2,1,0:T(8,128)(2,1)} %copy-done.2), calls=%async_computation.1 | async-start | bytes 4194304 | tf_op jit(solution)/shard_map/all_to_all | solution.py:435
  24.9 1.9 collect_down.1
  26.9 2.0 collective-permute-start.5
  28.9 2.8 %collective-permute-start.6 = (bf16[1,128,1024]{2,1,0:T(8,128)(2,1)S(1)}, bf16[1,128,1024]{2,1,0:T(8,128)(2,1)S(1)}, u32[]{:S(2)}, u32[]{:S(2)}) collective-permute-start(bf16[1,128,1024]{2,1,0:T(8,128)(2,1)S(1)} %bitcast.3), channel_id=1, source_target_pairs={{0,8},{1,9},{2,10},{3,11},{4,12},{5,13},{6,14},{7,15},{8,0},{9,1},... | collective-permute-start | bytes 786440 | tf_op jit(solution)/shard_map/ppermute | solution.py:442
  31.7 0.8 back_low.1
  32.7 1.9 collective-permute-start.7
  34.6 51.9 %collective-permute-done = bf16[1,128,128]{2,1,0:T(8,128)(2,1)S(1)} collective-permute-done((bf16[1,128,128]{2,1,0:T(8,128)(2,1)S(1)}, bf16[1,128,128]{2,1,0:T(8,128)(2,1)S(1)}, u32[]{:S(2)}, u32[]{:S(2)}) %collective-permute-start) | collective-permute-done | bytes 32800 | tf_op jit(solution)/shard_map/ppermute | solution.py:442
  86.6 4.2 %collective-permute-done.1 = bf16[2,128,128]{2,1,0:T(8,128)(2,1)S(1)} collective-permute-done((bf16[2,128,128]{2,1,0:T(8,128)(2,1)S(1)}, bf16[2,128,128]{2,1,0:T(8,128)(2,1)S(1)}, u32[]{:S(2)}, u32[]{:S(2)}) %collective-permute-start.1) | collective-permute-done | bytes 65568 | tf_op jit(solution)/shard_map/ppermute | solution.py:442
  90.9 0.5 collective-permute-start.10
  91.4 6.1 %collective-permute-done.8.refs_3_ = bf16[1,128,1024]{2,1,0:T(8,128)(2,1)S(1)} collective-permute-done((bf16[1,128,1024]{2,1,0:T(8,128)(2,1)S(1)}, bf16[1,128,1024]{2,1,0:T(8,128)(2,1)S(1)}, u32[]{:S(2)}, u32[]{:S(2)}) %collective-permute-start.8) | collective-permute-done | bytes 262176 | tf_op jit(solution)/shard_map/ppermute | solution.py:442
  97.5 0.5 collective-permute-start.12
  98.1 1.0 collective-permute-done.11.refs_6_
  99.0 0.4 collective-permute-done.12.refs_7_
  99.4 1.0 copy-done.3
  100.4 1.0 copy-done.19
  101.4 6.4 %input_slices.1 = (bf16[8,2,64,512]{3,2,1,0:T(8,128)(2,1)S(1)}, bf16[8,2,64,512]{3,2,1,0:T(8,128)(2,1)}, bf16[8,128,128]{2,1,0:T(8,128)(2,1)S(1)}, bf16[8,128,128]{2,1,0:T(8,128)(2,1)S(1)}) custom-call(s32[16]{0:T(128)S(1)} %copy-done.13, s32[1]{0:T(128)} %bitcast.place, bf16[8,128,128]{2,1,0:T(8,128)(2,1)S(1)} %pad_maximum_fusion.backs, ...), custom_call_target="tpu_custom_call" | custom-call | tf_op jit(solution)/shard_map/input_slices/pallas_call | solution.py:54
  107.7 1.0 copy-done.7
  108.7 0.7 copy-done.10
  109.4 0.7 copy-done.17
  110.1 4.4 %all-to-all-start.3 = ((bf16[8,2,64,512]{3,2,1,0:T(8,128)(2,1)}), bf16[8,2,64,512]{3,2,1,0:T(8,128)(2,1)}, u32[]{:S(2)}, u32[]{:S(2)}) async-start(bf16[8,2,64,512]{3,2,1,0:T(8,128)(2,1)} %copy-done.7), calls=%async_computation.3 | async-start | bytes 2097152 | tf_op jit(solution)/shard_map/all_to_all | solution.py:435
  114.5 2.7 %hidden_parts.1 = (f32[8,128,128]{2,1,0:T(8,128)S(1)}, bf16[8,128,512]{2,1,0:T(8,128)(2,1)S(1)}, bf16[8,128,512]{2,1,0:T(8,128)(2,1)S(1)}) custom-call(s32[16]{0:T(128)S(1)} %copy-done.13, s32[1]{0:T(128)} %bitcast.place, bf16[8,128,512]{2,1,0:T(8,128)(2,1)S(1)} %copy-done.4, bf16[8,2,128,512]{3,2,1,0:T(8,128)(2,1)S(1)} %all-to-all-done.1.tokens, ...), custom_call_target="tpu_custom_call" | custom-call | tf_op jit(solution)/shard_map/hidden_parts/pallas_call | solution.py:54
  117.2 1.0 copy-done.8
  118.2 0.4 collective-permute-start.14
  118.6 1.2 collective-permute-done.14
  119.9 1.9 collective-permute-start.15
  121.8 13.4 %collective-permute-done.15 = f32[2,128,128]{2,1,0:T(8,128)S(1)} collective-permute-done((f32[2,128,128]{2,1,0:T(8,128)S(1)}, f32[2,128,128]{2,1,0:T(8,128)S(1)}, u32[]{:S(2)}, u32[]{:S(2)}) %collective-permute-start.15) | collective-permute-done | bytes 131104 | tf_op jit(solution)/shard_map/ppermute | solution.py:442
  135.3 4.6 %collective-permute-start.16 = (f32[1,128,128]{2,1,0:T(8,128)S(1)}, f32[1,128,128]{2,1,0:T(8,128)S(1)}, u32[]{:S(2)}, u32[]{:S(2)}) collective-permute-start(f32[1,128,128]{2,1,0:T(8,128)S(1)} %get-tuple-element.30), channel_id=1, source_target_pairs={{0,8},{1,9},{2,10},{3,11},{4,12},{5,13},{6,14},{7,15},{8,0},{9,1},... | collective-permute-start | bytes 196616 | tf_op jit(solution)/shard_map/ppermute | solution.py:442
  139.9 4.0 %collective-permute-done.16.received = f32[1,128,128]{2,1,0:T(8,128)S(1)} collective-permute-done((f32[1,128,128]{2,1,0:T(8,128)S(1)}, f32[1,128,128]{2,1,0:T(8,128)S(1)}, u32[]{:S(2)}, u32[]{:S(2)}) %collective-permute-start.16) | collective-permute-done | bytes 65568 | tf_op jit(solution)/shard_map/ppermute | solution.py:442
  143.8 3.6 %all-to-all-start.2 = ((bf16[8,2,64,512]{3,2,1,0:T(8,128)(2,1)}), bf16[8,2,64,512]{3,2,1,0:T(8,128)(2,1)S(1)}, u32[]{:S(2)}, u32[]{:S(2)}) async-start(bf16[8,2,64,512]{3,2,1,0:T(8,128)(2,1)} %get-tuple-element.22), calls=%async_computation.2 | async-start | bytes 2097152 | tf_op jit(solution)/shard_map/all_to_all | solution.py:435
  147.5 0.6 hidden_low.1
  148.1 2.8 %collective-permute-start.18 = (bf16[1,128,128]{2,1,0:T(8,128)(2,1)S(1)}, bf16[1,128,128]{2,1,0:T(8,128)(2,1)S(1)}, u32[]{:S(2)}, u32[]{:S(2)}) collective-permute-start(bf16[1,128,128]{2,1,0:T(8,128)(2,1)S(1)} %hidden_low.1), channel_id=1, source_target_pairs={{0,8},{1,9},{2,10},{3,11},{4,12},{5,13},{6,14},{7,15},{8,0},{9,1},... | collective-permute-start | bytes 98312 | tf_op jit(solution)/shard_map/ppermute | solution.py:442
  150.9 24.4 %collective-permute-done.18 = bf16[1,128,128]{2,1,0:T(8,128)(2,1)S(1)} collective-permute-done((bf16[1,128,128]{2,1,0:T(8,128)(2,1)S(1)}, bf16[1,128,128]{2,1,0:T(8,128)(2,1)S(1)}, u32[]{:S(2)}, u32[]{:S(2)}) %collective-permute-start.18) | collective-permute-done | bytes 32800 | tf_op jit(solution)/shard_map/ppermute | solution.py:442
  175.4 4.3 %collective-permute-done.19 = bf16[2,128,128]{2,1,0:T(8,128)(2,1)S(1)} collective-permute-done((bf16[2,128,128]{2,1,0:T(8,128)(2,1)S(1)}, bf16[2,128,128]{2,1,0:T(8,128)(2,1)S(1)}, u32[]{:S(2)}, u32[]{:S(2)}) %collective-permute-start.19) | collective-permute-done | bytes 65568 | tf_op jit(solution)/shard_map/ppermute | solution.py:442
  179.8 1.2 collective-permute-done.20
  181.1 0.8 collective-permute-start.21
  182.0 1.3 collective-permute-start.3
  183.2 2.3 %join_columns.2.refs_0_ = bf16[128,8192]{1,0:T(8,128)(2,1)} custom-call(s32[1]{0:T(128)} %bitcast.place, bf16[8,2,64,512]{3,2,1,0:T(8,128)(2,1)} %all-to-all-done.3.source), custom_call_target="tpu_custom_call" | custom-call | tf_op jit(solution)/shard_map/join_columns/pallas_call | solution.py:281
  185.5 3.4 %collective-permute-done.17.gradients_pair = bf16[8,128,128]{2,1,0:T(8,128)(2,1)S(1)} collective-permute-done((bf16[8,128,128]{2,1,0:T(8,128)(2,1)S(1)}, bf16[8,128,128]{2,1,0:T(8,128)(2,1)S(1)}, u32[]{:S(2)}, u32[]{:S(2)}) %collective-permute-start.17) | collective-permute-done | bytes 262176 | tf_op jit(solution)/shard_map/ppermute | solution.py:442
  188.9 5.6 %collective-permute-done.21.hiddens_pair = bf16[8,128,128]{2,1,0:T(8,128)(2,1)S(1)} collective-permute-done((bf16[8,128,128]{2,1,0:T(8,128)(2,1)S(1)}, bf16[8,128,128]{2,1,0:T(8,128)(2,1)S(1)}, u32[]{:S(2)}, u32[]{:S(2)}) %collective-permute-start.21) | collective-permute-done | bytes 262176 | tf_op jit(solution)/shard_map/ppermute | solution.py:442
  194.6 6.5 %up_gradients.1 = bf16[64,64,128]{2,1,0:T(8,128)(2,1)} custom-call(s32[16]{0:T(128)S(1)} %copy-done.13, s32[1]{0:T(128)} %bitcast.place, s32[64]{0:T(128)S(1)} %copy-done.14, bf16[8,128,128]{2,1,0:T(8,128)(2,1)S(1)} %copy-done.11, bf16[8,128,128]{2,1,0:T(8,128)(2,1)S(1)} %collective-permute-done.17.gradients_pair, ...), custom_call_target="tpu_custom_call" | custom-call | tf_op jit(solution)/shard_map/up_gradients/pallas_call | solution.py:54
  201.1 8.4 %down_gradients.1 = bf16[64,128,512]{2,1,0:T(8,128)(2,1)} custom-call(s32[16]{0:T(128)S(1)} %copy-done.13, s32[1]{0:T(128)} %bitcast.place, bf16[8,128,128]{2,1,0:T(8,128)(2,1)S(1)} %pad_maximum_fusion.backs, bf16[8,128,128]{2,1,0:T(8,128)(2,1)S(1)} %collective-permute-done.3.backs_pair, bf16[8,128,512]{2,1,0:T(8,128)(2,1)S(1)} %copy-done.9, ...), custom_call_target="tpu_custom_call" | custom-call | tf_op jit(solution)/shard_map/down_gradients/pallas_call | solution.py:54
  209.4 1.1 join_columns.3
  (66 shorter events, 1.2 us)
Async XLA Ops:
  0.6 1.2 copy-start.1
  1.9 0.7 copy-start.12
  2.5 8.7 %copy-start = (bf16[128,8192]{1,0:T(8,128)(2,1)S(1)}, bf16[128,8192]{1,0:T(8,128)(2,1)}, u32[]{:S(2)}) copy-start(bf16[128,8192]{1,0:T(8,128)(2,1)} %refs_15_.5) | copy-start | bytes 6291460
  3.8 17.4 %all-to-all-start = ((bf16[16,64,128]{2,1,0:T(8,128)(2,1)}), bf16[16,64,128]{2,1,0:T(8,128)(2,1)S(1)}, u32[]{:S(2)}, u32[]{:S(2)}) async-start(bf16[16,64,128]{2,1,0:T(8,128)(2,1)} %gather_up.1), calls=%async_computation | async-start | bytes 524288 | tf_op jit(solution)/shard_map/all_to_all | solution.py:429
  11.4 1.3 copy-start.2
  12.7 12.2 %copy-start.13 = (s32[16]{0:T(128)S(1)}, s32[16]{0:T(128)}, u32[]{:S(2)}) copy-start(s32[16]{0:T(128)} %adapters.15) | copy-start | bytes 196
  21.2 88.9 %all-to-all-start.1 = ((bf16[8,2,128,512]{3,2,1,0:T(8,128)(2,1)}), bf16[8,2,128,512]{3,2,1,0:T(8,128)(2,1)S(1)}, u32[]{:S(2)}, u32[]{:S(2)}) async-start(bf16[8,2,128,512]{3,2,1,0:T(8,128)(2,1)} %copy-done.2), calls=%async_computation.1 | async-start | bytes 4194304 | tf_op jit(solution)/shard_map/all_to_all | solution.py:435
  24.9 2.0 copy-start.5
  24.9 4.0 %copy-start.6 = (bf16[128,1024]{1,0:T(8,128)(2,1)S(1)}, bf16[128,1024]{1,0:T(8,128)(2,1)}, u32[]{:S(2)}) copy-start(bf16[128,1024]{1,0:T(8,128)(2,1)} %gradient.1) | copy-start | bytes 786436
  24.9 6.8 %copy-start.14 = (s32[64]{0:T(128)S(1)}, s32[64]{0:T(128)}, u32[]{:S(2)}) copy-start(s32[64]{0:T(128)} %ranks.5) | copy-start | bytes 772
  26.8 72.6 %collective-permute-start.4 = (bf16[8,128,512]{2,1,0:T(8,128)(2,1)S(1)}, bf16[8,128,512]{2,1,0:T(8,128)(2,1)S(1)}, u32[]{:S(2)}, u32[]{:S(2)}) collective-permute-start(bf16[8,128,512]{2,1,0:T(8,128)(2,1)S(1)} %collect_down.1), channel_id=1, source_target_pairs={{0,2},{1,3},{2,0},{3,1},{4,6},{5,7},{6,4},{7,5},{8,10},{9,11},{10,... | collective-permute-start | bytes 3145736 | tf_op jit(solution)/shard_map/ppermute | solution.py:442
  26.9 72.5 %collective-permute-start.5 = (bf16[1024,512]{1,0:T(8,128)(2,1)S(1)}, bf16[1024,512]{1,0:T(8,128)(2,1)S(1)}, u32[]{:S(2)}, u32[]{:S(2)}) collective-permute-start(bf16[1024,512]{1,0:T(8,128)(2,1)S(1)} %copy-done.5), channel_id=1, source_target_pairs={{0,2},{1,3},{2,0},{3,1},{4,6},{5,7},{6,4},{7,5},{8,10},{9,11},{10,... | collective-permute-start | bytes 3145736 | tf_op jit(solution)/shard_map/ppermute | solution.py:442
  28.9 57.6 %collective-permute-start.6 = (bf16[1,128,1024]{2,1,0:T(8,128)(2,1)S(1)}, bf16[1,128,1024]{2,1,0:T(8,128)(2,1)S(1)}, u32[]{:S(2)}, u32[]{:S(2)}) collective-permute-start(bf16[1,128,1024]{2,1,0:T(8,128)(2,1)S(1)} %bitcast.3), channel_id=1, source_target_pairs={{0,8},{1,9},{2,10},{3,11},{4,12},{5,13},{6,14},{7,15},{8,0},{9,1},... | collective-permute-start | bytes 786440 | tf_op jit(solution)/shard_map/ppermute | solution.py:442
  32.5 54.0 %collective-permute-start = (bf16[1,128,128]{2,1,0:T(8,128)(2,1)S(1)}, bf16[1,128,128]{2,1,0:T(8,128)(2,1)S(1)}, u32[]{:S(2)}, u32[]{:S(2)}) collective-permute-start(bf16[1,128,128]{2,1,0:T(8,128)(2,1)S(1)} %back_low.1), channel_id=1, source_target_pairs={{0,8},{1,9},{2,10},{3,11},{4,12},{5,13},{6,14},{7,15},{8,0},{9,1},... | collective-permute-start | bytes 98312 | tf_op jit(solution)/shard_map/ppermute | solution.py:442
  32.7 58.2 %collective-permute-start.7 = (bf16[1,128,1024]{2,1,0:T(8,128)(2,1)S(1)}, bf16[1,128,1024]{2,1,0:T(8,128)(2,1)S(1)}, u32[]{:S(2)}, u32[]{:S(2)}) collective-permute-start(bf16[1,128,1024]{2,1,0:T(8,128)(2,1)S(1)} %bitcast.4), channel_id=1, source_target_pairs={{0,4},{1,5},{2,6},{3,7},{4,0},{5,1},{6,2},{7,3},{8,12},{9,13},{10,... | collective-permute-start | bytes 786440 | tf_op jit(solution)/shard_map/ppermute | solution.py:442
  86.5 4.3 %collective-permute-start.1 = (bf16[2,128,128]{2,1,0:T(8,128)(2,1)S(1)}, bf16[2,128,128]{2,1,0:T(8,128)(2,1)S(1)}, u32[]{:S(2)}, u32[]{:S(2)}) collective-permute-start(bf16[2,128,128]{2,1,0:T(8,128)(2,1)S(1)} %pad_maximum_fusion.4), channel_id=1, source_target_pairs={{0,4},{1,5},{2,6},{3,7},{4,0},{5,1},{6,2},{7,3},{8,12},{9,13},{10,... | collective-permute-start | bytes 196616 | tf_op jit(solution)/shard_map/ppermute | solution.py:442
  86.6 4.4 %collective-permute-start.9 = (bf16[1,128,1024]{2,1,0:T(8,128)(2,1)S(1)}, bf16[1,128,1024]{2,1,0:T(8,128)(2,1)S(1)}, u32[]{:S(2)}, u32[]{:S(2)}) collective-permute-start(bf16[1,128,1024]{2,1,0:T(8,128)(2,1)S(1)} %bitcast.5), channel_id=1, source_target_pairs={{0,1},{1,0},{2,3},{3,2},{4,5},{5,4},{6,7},{7,6},{8,9},{9,8},{10,11... | collective-permute-start | bytes 786440 | tf_op jit(solution)/shard_map/ppermute | solution.py:442
  90.8 6.7 %collective-permute-start.8 = (bf16[1,128,1024]{2,1,0:T(8,128)(2,1)S(1)}, bf16[1,128,1024]{2,1,0:T(8,128)(2,1)S(1)}, u32[]{:S(2)}, u32[]{:S(2)}) collective-permute-start(bf16[1,128,1024]{2,1,0:T(8,128)(2,1)S(1)} %collective-permute-done.6.refs_1_), channel_id=1, source_target_pairs={{0,4},{1,5},{2,6},{3,7},{4,0},{5,1},{6,2},{7,3},{8,12},{9,13},{10,... | collective-permute-start | bytes 786440 | tf_op jit(solution)/shard_map/ppermute | solution.py:442
  90.8 6.7 %collective-permute-start.2 = (bf16[4,128,128]{2,1,0:T(8,128)(2,1)S(1)}, bf16[4,128,128]{2,1,0:T(8,128)(2,1)S(1)}, u32[]{:S(2)}, u32[]{:S(2)}) collective-permute-start(bf16[4,128,128]{2,1,0:T(8,128)(2,1)S(1)} %pad_maximum_fusion.2), channel_id=1, source_target_pairs={{0,1},{1,0},{2,3},{3,2},{4,5},{5,4},{6,7},{7,6},{8,9},{9,8},{10,11... | collective-permute-start | bytes 393224 | tf_op jit(solution)/shard_map/ppermute | solution.py:442
  90.9 7.1 %collective-permute-start.10 = (bf16[1,128,1024]{2,1,0:T(8,128)(2,1)S(1)}, bf16[1,128,1024]{2,1,0:T(8,128)(2,1)S(1)}, u32[]{:S(2)}, u32[]{:S(2)}) collective-permute-start(bf16[1,128,1024]{2,1,0:T(8,128)(2,1)S(1)} %collective-permute-done.6.refs_1_), channel_id=1, source_target_pairs={{0,1},{1,0},{2,3},{3,2},{4,5},{5,4},{6,7},{7,6},{8,9},{9,8},{10,11... | collective-permute-start | bytes 786440 | tf_op jit(solution)/shard_map/ppermute | solution.py:442
  97.5 1.5 collective-permute-start.11
  97.5 1.9 collective-permute-start.12
  99.4 1.0 copy-start.3
  100.4 1.0 copy-start.19
  107.7 1.0 copy-start.7
  108.7 0.7 copy-start.10
  109.4 0.7 copy-start.17
  110.1 4.4 %copy-start.4 = (bf16[8,128,512]{2,1,0:T(8,128)(2,1)S(1)}, bf16[8,128,512]{2,1,0:T(8,128)(2,1)}, u32[]{:S(2)}) copy-start(bf16[8,128,512]{2,1,0:T(8,128)(2,1)} %copy-done.3) | copy-start | bytes 3145732
  110.1 33.7 %all-to-all-start.3 = ((bf16[8,2,64,512]{3,2,1,0:T(8,128)(2,1)}), bf16[8,2,64,512]{3,2,1,0:T(8,128)(2,1)}, u32[]{:S(2)}, u32[]{:S(2)}) async-start(bf16[8,2,64,512]{3,2,1,0:T(8,128)(2,1)} %copy-done.7), calls=%async_computation.3 | async-start | bytes 2097152 | tf_op jit(solution)/shard_map/all_to_all | solution.py:435
  117.2 1.0 copy-start.8
  118.2 17.1 %copy-start.15 = (bf16[8,128,512]{2,1,0:T(8,128)(2,1)}, bf16[8,128,512]{2,1,0:T(8,128)(2,1)S(1)}, u32[]{:S(2)}) copy-start(bf16[8,128,512]{2,1,0:T(8,128)(2,1)S(1)} %get-tuple-element.19) | copy-start | bytes 3145732
  118.2 61.5 %copy-start.18 = (bf16[8,128,128]{2,1,0:T(8,128)(2,1)S(1)}, bf16[8,128,128]{2,1,0:T(8,128)(2,1)}, u32[]{:S(2)}) copy-start(bf16[8,128,128]{2,1,0:T(8,128)(2,1)} %copy-done.17) | copy-start | bytes 786436
  118.2 1.6 collective-permute-start.14
  119.9 15.4 %collective-permute-start.15 = (f32[2,128,128]{2,1,0:T(8,128)S(1)}, f32[2,128,128]{2,1,0:T(8,128)S(1)}, u32[]{:S(2)}, u32[]{:S(2)}) collective-permute-start(f32[2,128,128]{2,1,0:T(8,128)S(1)} %slice.25), channel_id=1, source_target_pairs={{0,4},{1,5},{2,6},{3,7},{4,0},{5,1},{6,2},{7,3},{8,12},{9,13},{10,... | collective-permute-start | bytes 393224 | tf_op jit(solution)/shard_map/ppermute | solution.py:442
  135.3 8.5 %collective-permute-start.16 = (f32[1,128,128]{2,1,0:T(8,128)S(1)}, f32[1,128,128]{2,1,0:T(8,128)S(1)}, u32[]{:S(2)}, u32[]{:S(2)}) collective-permute-start(f32[1,128,128]{2,1,0:T(8,128)S(1)} %get-tuple-element.30), channel_id=1, source_target_pairs={{0,8},{1,9},{2,10},{3,11},{4,12},{5,13},{6,14},{7,15},{8,0},{9,1},... | collective-permute-start | bytes 196616 | tf_op jit(solution)/shard_map/ppermute | solution.py:442
  139.9 7.5 %copy-start.16 = (bf16[8,128,512]{2,1,0:T(8,128)(2,1)S(1)}, bf16[8,128,512]{2,1,0:T(8,128)(2,1)}, u32[]{:S(2)}) copy-start(bf16[8,128,512]{2,1,0:T(8,128)(2,1)} %copy-done.15) | copy-start | bytes 3145732
  143.8 65.6 %all-to-all-start.2 = ((bf16[8,2,64,512]{3,2,1,0:T(8,128)(2,1)}), bf16[8,2,64,512]{3,2,1,0:T(8,128)(2,1)S(1)}, u32[]{:S(2)}, u32[]{:S(2)}) async-start(bf16[8,2,64,512]{3,2,1,0:T(8,128)(2,1)} %get-tuple-element.22), calls=%async_computation.2 | async-start | bytes 2097152 | tf_op jit(solution)/shard_map/all_to_all | solution.py:435
  147.4 53.7 %collective-permute-start.13 = (bf16[8,128,512]{2,1,0:T(8,128)(2,1)S(1)}, bf16[8,128,512]{2,1,0:T(8,128)(2,1)S(1)}, u32[]{:S(2)}, u32[]{:S(2)}) collective-permute-start(bf16[8,128,512]{2,1,0:T(8,128)(2,1)S(1)} %copy-done.16), channel_id=1, source_target_pairs={{0,2},{1,3},{2,0},{3,1},{4,6},{5,7},{6,4},{7,5},{8,10},{9,11},{10,... | collective-permute-start | bytes 3145736 | tf_op jit(solution)/shard_map/ppermute | solution.py:442
  147.5 47.1 %copy-start.11 = (bf16[8,128,128]{2,1,0:T(8,128)(2,1)S(1)}, bf16[8,128,128]{2,1,0:T(8,128)(2,1)}, u32[]{:S(2)}) copy-start(bf16[8,128,128]{2,1,0:T(8,128)(2,1)} %copy-done.10) | copy-start | bytes 786436
  148.1 27.3 %collective-permute-start.18 = (bf16[1,128,128]{2,1,0:T(8,128)(2,1)S(1)}, bf16[1,128,128]{2,1,0:T(8,128)(2,1)S(1)}, u32[]{:S(2)}, u32[]{:S(2)}) collective-permute-start(bf16[1,128,128]{2,1,0:T(8,128)(2,1)S(1)} %hidden_low.1), channel_id=1, source_target_pairs={{0,8},{1,9},{2,10},{3,11},{4,12},{5,13},{6,14},{7,15},{8,0},{9,1},... | collective-permute-start | bytes 98312 | tf_op jit(solution)/shard_map/ppermute | solution.py:442
  175.3 4.3 %collective-permute-start.19 = (bf16[2,128,128]{2,1,0:T(8,128)(2,1)S(1)}, bf16[2,128,128]{2,1,0:T(8,128)(2,1)S(1)}, u32[]{:S(2)}, u32[]{:S(2)}) collective-permute-start(bf16[2,128,128]{2,1,0:T(8,128)(2,1)S(1)} %pad_maximum_fusion.5), channel_id=1, source_target_pairs={{0,4},{1,5},{2,6},{3,7},{4,0},{5,1},{6,2},{7,3},{8,12},{9,13},{10,... | collective-permute-start | bytes 196616 | tf_op jit(solution)/shard_map/ppermute | solution.py:442
  179.7 1.4 collective-permute-start.20
  179.8 9.2 %collective-permute-start.17 = (bf16[8,128,128]{2,1,0:T(8,128)(2,1)S(1)}, bf16[8,128,128]{2,1,0:T(8,128)(2,1)S(1)}, u32[]{:S(2)}, u32[]{:S(2)}) collective-permute-start(bf16[8,128,128]{2,1,0:T(8,128)(2,1)S(1)} %copy-done.18), channel_id=1, source_target_pairs={{0,2},{1,3},{2,0},{3,1},{4,6},{5,7},{6,4},{7,5},{8,10},{9,11},{10,... | collective-permute-start | bytes 786440 | tf_op jit(solution)/shard_map/ppermute | solution.py:442
  181.1 19.9 %copy-start.9 = (bf16[8,128,512]{2,1,0:T(8,128)(2,1)S(1)}, bf16[8,128,512]{2,1,0:T(8,128)(2,1)}, u32[]{:S(2)}) copy-start(bf16[8,128,512]{2,1,0:T(8,128)(2,1)} %copy-done.8) | copy-start | bytes 3145732
  181.1 13.4 %collective-permute-start.21 = (bf16[8,128,128]{2,1,0:T(8,128)(2,1)S(1)}, bf16[8,128,128]{2,1,0:T(8,128)(2,1)S(1)}, u32[]{:S(2)}, u32[]{:S(2)}) collective-permute-start(bf16[8,128,128]{2,1,0:T(8,128)(2,1)S(1)} %pad_maximum_fusion.1.hiddens), channel_id=1, source_target_pairs={{0,2},{1,3},{2,0},{3,1},{4,6},{5,7},{6,4},{7,5},{8,10},{9,11},{10,... | collective-permute-start | bytes 786440 | tf_op jit(solution)/shard_map/ppermute | solution.py:442
  182.0 19.1 %collective-permute-start.3 = (bf16[8,128,128]{2,1,0:T(8,128)(2,1)S(1)}, bf16[8,128,128]{2,1,0:T(8,128)(2,1)S(1)}, u32[]{:S(2)}, u32[]{:S(2)}) collective-permute-start(bf16[8,128,128]{2,1,0:T(8,128)(2,1)S(1)} %pad_maximum_fusion.backs), channel_id=1, source_target_pairs={{0,2},{1,3},{2,0},{3,1},{4,6},{5,7},{6,4},{7,5},{8,10},{9,11},{10,... | collective-permute-start | bytes 786440 | tf_op jit(solution)/shard_map/ppermute | solution.py:442

commit v5 on v3

v5 whole, which is shorter than its diff:
```python
import functools

import jax
import jax.numpy as jnp
from jax import lax
from jax.experimental import pallas as pl
from jax.experimental.pallas import tpu as pltpu
from jax.sharding import PartitionSpec as P

adapter_alpha = 32.0
vmem_limit = 48 * 1024 * 1024
pair_bit = 2


def line_offset(slot, members):
    bits = members.bit_length() - 1
    line = 0
    for bit in range(bits):
        line |= ((slot >> bit) & 1) << (bits - 1 - bit)
    return ((line // pair_bit) * 2 * pair_bit) | (line % pair_bit)


def params():
    return pltpu.CompilerParams(vmem_limit_bytes=vmem_limit)


def whole(shape):
    return pl.BlockSpec(shape, lambda *_: (0,) * len(shape))


def picked(maps, flip):
    return pl.BlockSpec(
        (1,) + maps.shape[1:], lambda i, adapters, place, *_: (adapters[place[0] ^ flip], 0, 0)
    )


def call(kernel, name, prefetch, operands, in_specs, out_shapes, scratch=(), grid=(1,), out_specs=None):
    if out_specs is None:
        out_specs = [whole(shape.shape) for shape in out_shapes]
    return pl.pallas_call(
        kernel,
        out_shape=out_shapes,
        grid_spec=pltpu.PrefetchScalarGridSpec(
            num_scalar_prefetch=len(prefetch),
            grid=grid,
            in_specs=in_specs,
            out_specs=out_specs,
            scratch_shapes=list(scratch),
        ),
        compiler_params=params(),
        name=name,
    )(*prefetch, *operands)


def pair_kernel(adapters, place, weight, *refs):
    out = refs[-1]
    count, extent, _ = refs[0].shape[0] * (len(refs) - 1), *refs[0].shape[1:]
    for entry in range(count):
        out[entry * extent : (entry + 1) * extent] = refs[entry][0]
    out[count * extent :] = weight[...]


def for_pair(adapters, place, weight, down_maps, members):
    extent, width = down_maps.shape[1:]
    shape = jax.ShapeDtypeStruct((members * extent + weight.shape[0], width), weight.dtype)
    return call(
        pair_kernel,
        "for_pair",
        (adapters, place),
        [weight] + [down_maps] * members,
        [whole(weight.shape)]
        + [picked(down_maps, line_offset(slot, members) ^ pair_bit) for slot in range(members)],
        [shape],
    )[0]


def gather_up_kernel(adapters, up_maps, out, sems):
    copies = [
        pltpu.make_async_copy(up_maps.at[adapters[block]], out.at[block], sems.at[block])
        for block in range(out.shape[0])
    ]
    for copy in copies:
        copy.start()
    for copy in copies:
        copy.wait()


def gather_up(adapters, up_maps):
    shape = (adapters.shape[0],) + up_maps.shape[1:]
    return call(
        gather_up_kernel,
        "gather_up",
        (adapters,),
        [up_maps],
        [pl.BlockSpec(memory_space=pltpu.HBM)],
        [jax.ShapeDtypeStruct(shape, up_maps.dtype)],
        scratch=[pltpu.SemaphoreType.DMA((shape[0],))],
    )[0]


def pack_kernel(place, *refs):
    count = len(refs) // 3
    for slot in range(count):
        out = refs[2 * count + slot]
        out[0] = refs[2 * slot][...]
        out[1] = refs[2 * slot + 1][...]


def pack_tokens(place, tokens, members, width):
    rows = tokens.shape[0]

    def spec(flip):
        return pl.BlockSpec((rows, width), lambda i, place: (0, place[0] ^ flip))

    specs = []
    for slot in range(members):
        offset = line_offset(slot, members)
        specs += [spec(offset), spec(offset ^ pair_bit)]
    shape = jax.ShapeDtypeStruct((2, rows, width), tokens.dtype)
    return call(
        pack_kernel, "pack_tokens", (place,), [tokens] * len(specs), specs, [shape] * members
    )


def rank_row(ranks, adapter, extent):
    rank = jnp.full((1, extent), ranks[adapter], jnp.int32)
    alive = (lax.broadcasted_iota(jnp.int32, (1, extent), 1) < rank).astype(jnp.float32)
    return alive, adapter_alpha / rank.astype(jnp.float32)


def back_kernel(adapters, place, ranks, gradient, up, out):
    alive, factor = rank_row(ranks, adapters[place[0]], up.shape[1])
    back = jnp.dot(gradient[...], up[...], preferred_element_type=jnp.float32)
    out[0] = (factor * back * alive).astype(out.dtype)


def back_rows(adapters, place, ranks, gradient, up):
    shape = jax.ShapeDtypeStruct((1, gradient.shape[0], up.shape[1]), jnp.bfloat16)
    return call(
        back_kernel,
        "back_low",
        (adapters, place, ranks),
        (gradient, up),
        [whole(gradient.shape), whole(up.shape)],
        [shape],
    )[0]


def input_kernel(adapters, place, backs, pair, *refs):
    members, rows, _ = backs.shape
    gradients, downs = refs[:members], refs[members : 2 * members]
    weight = refs[2 * members]
    outs, columns = refs[2 * members + 1 : -2], refs[-2:]
    extent = downs[0].shape[1]
    lanes = columns[0].shape[2]
    value_width = gradients[0].shape[2] // (2 * members)
    some = min(4, members)
    for first in range(0, members, some):
        slots = range(first, first + some)
        lines = jnp.concatenate([gradients[slot][0] for slot in slots], axis=0)
        for half in range(2):
            right = weight[...] if half == 0 else pair[members * extent :]
            frozen = jnp.dot(lines, right, preferred_element_type=jnp.float32)
            for slot in slots:
                down = downs[slot][0] if half == 0 else pair[slot * extent : (slot + 1) * extent]
                low = jnp.dot(backs[slot], down, preferred_element_type=jnp.float32)
                at = (slot - first) * rows
                outs[slot][half] = (frozen[at : at + rows] + low).astype(jnp.bfloat16)
    for side in range(2):
        column = (place[0] ^ (side * pair_bit)) * value_width // lanes * lanes
        for slot in range(members):
            columns[side][slot] = gradients[slot][0, :, pl.ds(pl.multiple_of(column, lanes), lanes)]


def input_slices(adapters, place, gradients, backs, weight, pair, down_maps):
    members, rows, _ = backs.shape
    width = weight.shape[1]
    lanes = max(128, gradients[0].shape[2] // (2 * members))
    shape = jax.ShapeDtypeStruct((2, rows, width), jnp.bfloat16)
    columns = jax.ShapeDtypeStruct((members, rows, lanes), jnp.bfloat16)
    return call(
        input_kernel,
        "input_slices",
        (adapters, place),
        [backs, pair] + list(gradients) + [down_maps] * members + [weight],
        [whole(backs.shape), whole(pair.shape)]
        + [whole(gradients[0].shape)] * members
        + [picked(down_maps, line_offset(slot, members)) for slot in range(members)]
        + [whole(weight.shape)],
        [shape] * members + [columns] * 2,
    )


def hidden_kernel(adapters, place, pair, *refs):
    parts, own, other = refs[-3:]
    members = own.shape[0]
    downs, tokens = refs[:members], refs[members : 2 * members]
    extent = downs[0].shape[1]
    across = (((1,), (1,)), ((), ()))
    for slot in range(members):
        own[slot] = tokens[slot][0]
        other[slot] = tokens[slot][1]
        parts[slot] = lax.dot_general(
            tokens[slot][0], downs[slot][0], across, preferred_element_type=jnp.float32
        ) + lax.dot_general(
            tokens[slot][1],
            pair[slot * extent : (slot + 1) * extent],
            across,
            preferred_element_type=jnp.float32,
        )


def hidden_parts(adapters, place, down_maps, pair, tokens):
    members = len(tokens)
    _, rows, width = tokens[0].shape
    extent = down_maps.shape[1]
    tokens_shape = jax.ShapeDtypeStruct((members, rows, width), tokens[0].dtype)
    return call(
        hidden_kernel,
        "hidden_parts",
        (adapters, place),
        [pair] + [down_maps] * members + list(tokens),
        [whole(pair.shape)]
        + [picked(down_maps, line_offset(slot, members)) for slot in range(members)]
        + [whole(tokens[0].shape)] * members,
        [
            jax.ShapeDtypeStruct((members, rows, extent), jnp.float32),
            tokens_shape,
            tokens_shape,
        ],
    )


def hidden_low_kernel(adapters, place, ranks, kept, received, out):
    alive, _ = rank_row(ranks, adapters[place[0]], out.shape[2])
    out[0] = ((kept[0] + received[0]) * alive).astype(out.dtype)


def hidden_rows(adapters, place, ranks, kept, received):
    return call(
        hidden_low_kernel,
        "hidden_low",
        (adapters, place, ranks),
        (kept, received),
        [whole(kept.shape)] * 2,
        [jax.ShapeDtypeStruct(kept.shape, jnp.bfloat16)],
    )[0]


def join_kernel(place, *refs, offsets, aliased):
    pieces = refs[: len(offsets)]
    out, sems = refs[len(offsets) + aliased :]
    width = pieces[0].shape[2]
    copies = []
    for entry, offset in enumerate(offsets):
        for half in range(2):
            column = (place[0] ^ offset ^ (half * pair_bit)) * width
            copies.append(
                pltpu.make_async_copy(
                    pieces[entry].at[half],
                    out.at[:, pl.ds(pl.multiple_of(column, width), width)],
                    sems.at[2 * entry + half],
                )
            )
    for copy in copies:
        copy.start()
    for copy in copies:
        copy.wait()


def join_columns(place, pieces, offsets, columns, before=None):
    rows = pieces[0].shape[1]
    anywhere = pl.BlockSpec(memory_space=pl.ANY)
    rest = [] if before is None else [before]
    return pl.pallas_call(
        functools.partial(join_kernel, offsets=offsets, aliased=len(rest)),
        out_shape=jax.ShapeDtypeStruct((rows, columns), pieces[0].dtype),
        grid_spec=pltpu.PrefetchScalarGridSpec(
            num_scalar_prefetch=1,
            grid=(1,),
            in_specs=[anywhere] * (len(pieces) + len(rest)),
            out_specs=pl.BlockSpec(memory_space=pltpu.HBM),
            scratch_shapes=[pltpu.SemaphoreType.DMA((2 * len(pieces),))],
        ),
        input_output_aliases={1 + len(pieces): 0} if rest else {},
        compiler_params=params(),
        name="join_columns",
    )(place, *pieces, *rest)


def list_members(adapters, place, members, head, following):
    def clear(adapter, carry):
        head[adapter] = -1
        return carry

    lax.fori_loop(0, head.shape[0], clear, 0)
    for entry in reversed(range(2 * members)):
        side, slot = divmod(entry, members)
        adapter = adapters[place[0] ^ line_offset(slot, members) ^ (side * pair_bit)]
        following[entry] = head[adapter]
        head[adapter] = entry


def write_sums(head, following, products, ready, zero, out, sems, finish):
    num_adapters = out.shape[0]
    zero[...] = jnp.zeros_like(zero)

    def write(adapter, carry):
        first = head[adapter]

        @pl.when(first < 0)
        def _():
            pltpu.make_async_copy(zero, out.at[adapter], sems.at[adapter]).start()

        @pl.when(first >= 0)
        def _():
            def more(entry):
                products[first] += products[entry]
                return following[entry]

            lax.while_loop(lambda entry: entry >= 0, more, following[first])
            ready[first] = finish(adapter, products[first]).astype(out.dtype)
            pltpu.make_async_copy(ready.at[first], out.at[adapter], sems.at[adapter]).start()

        return carry

    lax.fori_loop(0, num_adapters, write, 0)

    def wait(adapter, carry):
        pltpu.make_async_copy(zero, out.at[adapter], sems.at[adapter]).wait()
        return carry

    lax.fori_loop(0, num_adapters, wait, 0)


def by_rows(left, right):
    return lax.dot_general(
        left, right, (((0,), (0,)), ((), ())), preferred_element_type=jnp.float32
    )


def sums_call(kernel, name, prefetch, operands, num_adapters, entries, product, scratch=()):
    return pl.pallas_call(
        kernel,
        out_shape=jax.ShapeDtypeStruct((num_adapters,) + product, jnp.bfloat16),
        grid_spec=pltpu.PrefetchScalarGridSpec(
            num_scalar_prefetch=len(prefetch),
            grid=(1,),
            in_specs=[whole(operand.shape) for operand in operands],
            out_specs=pl.BlockSpec(memory_space=pltpu.HBM),
            scratch_shapes=[
                pltpu.SMEM((num_adapters,), jnp.int32),
                pltpu.SMEM((entries,), jnp.int32),
                pltpu.VMEM((entries,) + product, jnp.float32),
                pltpu.VMEM((entries,) + product, jnp.bfloat16),
                pltpu.VMEM(product, jnp.bfloat16),
                pltpu.SemaphoreType.DMA((num_adapters,)),
                *scratch,
            ],
        ),
        compiler_params=params(),
        name=name,
    )(*prefetch, *operands)


def down_gradient_kernel(
    adapters, place, backs, backs_pair, own, other, out, head, following, products, ready, zero, sems
):
    members = own.shape[0]
    list_members(adapters, place, members, head, following)
    for slot in range(members):
        products[slot] = by_rows(backs[slot], own[slot])
        products[members + slot] = by_rows(backs_pair[slot], other[slot])
    write_sums(
        head, following, products, ready, zero, out, sems, lambda adapter, total: total
    )


def down_gradients(adapters, place, backs, backs_pair, own, other, num_adapters):
    members, _, width = own.shape
    return sums_call(
        down_gradient_kernel,
        "down_gradients",
        (adapters, place),
        (backs, backs_pair, own, other),
        num_adapters,
        2 * members,
        (backs.shape[2], width),
    )


def up_gradient_kernel(
    adapters,
    place,
    ranks,
    gradients,
    gradients_pair,
    hiddens,
    hiddens_pair,
    out,
    head,
    following,
    products,
    ready,
    zero,
    sems,
    lines,
):
    members, _, lanes = gradients.shape
    width, extent = out.shape[1:]
    list_members(adapters, place, members, head, following)
    inside = pl.multiple_of(lax.rem(place[0], lanes // width) * width, width)
    for slot in range(members):
        lines[slot] = by_rows(gradients[slot], hiddens[slot])
        lines[members + slot] = by_rows(gradients_pair[slot], hiddens_pair[slot])
    for entry in range(2 * members):
        products[entry] = lines[entry, pl.ds(inside, width), :]

    def finish(adapter, total):
        _, factor = rank_row(ranks, adapter, extent)
        return factor * total

    write_sums(head, following, products, ready, zero, out, sems, finish)


def up_gradients(adapters, place, ranks, gradients, gradients_pair, hiddens, hiddens_pair, width):
    members, _, lanes = gradients.shape
    extent = hiddens.shape[2]
    return sums_call(
        up_gradient_kernel,
        "up_gradients",
        (adapters, place, ranks),
        (gradients, gradients_pair, hiddens, hiddens_pair),
        ranks.shape[0],
        2 * members,
        (width, extent),
        [pltpu.VMEM((2 * members, lanes, extent), jnp.float32)],
    )


def exchange(pieces):
    return lax.all_to_all(pieces, "dp", split_axis=0, concat_axis=0, tiled=True)


def swap(array, flip):
    devices = lax.axis_size("dp")
    return lax.ppermute(array, "dp", [(i, i ^ flip) for i in range(devices)])


def tie(first, second):
    return lax.optimization_barrier((first, second))


def gather_step(held, members):
    arrived = swap(held, line_offset(held.shape[0], members))
    return jnp.concatenate([held, arrived], axis=0)


def reduce_step(parts, members):
    half = parts.shape[0] // 2
    return parts[:half], swap(parts[half:], line_offset(half, members))


def local(tokens, output_gradient, value_weight, down_maps, up_maps, adapter_per_block, ranks):
    devices = lax.axis_size("dp")
    members = devices // 2
    steps = members.bit_length() - 1
    num_adapters, extent, width = down_maps.shape
    rows, depth = output_gradient.shape
    place = lax.axis_index("dp").astype(jnp.int32).reshape(1)
    adapters = adapter_per_block
    offsets = [line_offset(slot, members) for slot in range(members)]

    far = [slot for slot in range(members) if slot % 2]
    near = [slot for slot in range(2, members, 2)]
    quarter = max(1, len(far) // 4)
    portions = [far[at : at + quarter] for at in range(0, len(far), quarter)]
    portions[2] = portions[2] + near[: len(near) // 2]
    portions[3] = portions[3] + near[len(near) // 2 :]

    def send(packs, portion):
        return {slot: swap(packs[slot], offsets[slot]) for slot in portion}

    own_gradient = output_gradient.reshape(1, rows, depth)
    gradients = [own_gradient] + [None] * (members - 1)
    for step in range(steps):
        gradients[1 << step] = swap(own_gradient, offsets[1 << step])
    own_up = exchange(gather_up(adapters, up_maps)).reshape(depth, extent)
    pair = swap(for_pair(adapters, place, value_weight, down_maps, members), pair_bit)
    packs = pack_tokens(place, tokens, members, width)
    arrived = {0: packs[0]}
    arrived.update(send(packs, portions[0]))

    first = [gradients[1 << step] for step in range(steps)]
    first, own_up, packs = lax.optimization_barrier((first, own_up, packs))
    for step in range(steps):
        gradients[1 << step] = first[step]

    backs = back_rows(adapters, place, ranks, output_gradient, own_up)
    for step in range(1, steps):
        for slot in range(1, 1 << step):
            gradients[slot + (1 << step)] = swap(gradients[slot], offsets[1 << step])
        backs = gather_step(backs, members)
        arrived.update(send(packs, portions[step]))
        done = [arrived[slot] for slot in portions[step - 1]]
        backs, gradients, packs, done = lax.optimization_barrier(
            (backs, gradients, packs, done)
        )
        arrived.update(zip(portions[step - 1], done))
        if step == 2:
            break
    for step in range(3, steps):
        for slot in range(1, 1 << step):
            gradients[slot + (1 << step)] = swap(gradients[slot], offsets[1 << step])
        backs = gather_step(backs, members)
    backs = gather_step(backs, members)
    arrived.update(send(packs, portions[3]))

    *slices, columns, columns_pair = input_slices(
        adapters, place, gradients, backs, value_weight, pair, down_maps
    )
    results = {0: slices[0]}
    results.update(send(slices, portions[0]))
    results.update(send(slices, portions[1]))

    columns_other = swap(columns_pair, pair_bit)
    backs_pair = swap(backs, pair_bit)
    arrived = [arrived[slot] for slot in range(members)]
    slices, arrived = lax.optimization_barrier((slices, arrived))
    parts, tokens_own, tokens_pair = hidden_parts(adapters, place, down_maps, pair, arrived)
    tokens_other = swap(tokens_pair, pair_bit)
    while parts.shape[0] > 2:
        kept, received = reduce_step(parts, members)
        parts = kept + received
    done = [results[slot] for slot in portions[0]]
    parts, done, columns_other, backs_pair, slices = lax.optimization_barrier(
        (parts, done, columns_other, backs_pair, slices)
    )
    results.update(zip(portions[0], done))
    results.update(send(slices, portions[2]))
    kept, received = reduce_step(parts, members)
    done = [results[slot] for slot in portions[1]]
    received, done, slices = lax.optimization_barrier((received, done, slices))
    results.update(zip(portions[1], done))
    results.update(send(slices, portions[3]))

    hiddens = hidden_rows(adapters, place, ranks, kept, received)
    hiddens = gather_step(gather_step(hiddens, members), members)
    down_gradient = down_gradients(
        adapters, place, backs, backs_pair, tokens_own, tokens_other, num_adapters
    )
    done = [results[slot] for slot in portions[2]]
    hiddens, done, down_gradient = lax.optimization_barrier((hiddens, done, down_gradient))
    results.update(zip(portions[2], done))
    while hiddens.shape[0] < members:
        hiddens = gather_step(hiddens, members)
    hiddens_pair = swap(hiddens, pair_bit)
    up_gradient = up_gradients(
        adapters, place, ranks, columns, columns_other, hiddens, hiddens_pair, depth // devices
    )

    def joined(slots, before=None):
        return join_columns(
            place,
            [results[slot] for slot in slots],
            [offsets[slot] for slot in slots],
            tokens.shape[1],
            before,
        )

    most = joined([0] + portions[0] + portions[1] + portions[2])
    up_gradient, most = lax.optimization_barrier((up_gradient, most))
    input_grad = joined(portions[3], most)
    return (input_grad, down_gradient, up_gradient)


def solution(mesh):
    in_specs = (
        P(("groups", "dp"), None),
        P(("groups", "dp"), None),
        P(None, "dp"),
        P(None, None, "dp"),
        P(None, "dp", None),
        P("groups"),
        P(),
    )
    out_specs = (P(("groups", "dp"), None), P("groups", None, "dp"), P("groups", "dp", None))
    return jax.shard_map(local, mesh=mesh, in_specs=in_specs, out_specs=out_specs, check_vma=False)
```

time: 189 us -> 195 us (1.032)
  waiting for transfers between devices: 85.9 us -> 114 us
  Pallas kernels: 35.5 us -> 27.5 us
  starting transfers between devices: 51.6 us -> 45.9 us
  other arithmetic: 5.14 us -> 0.09 us
  local copies, waits for them, and re-layouts: 9.27 us -> 6.24 us
    pallas_call x10 -> x7, Pallas kernels: 35.5 us -> 16.3 us  [call(): pl.pallas_call(kernel, out_shape=out_shapes, grid_spec=pltpu.PrefetchScal...]
    ppermute x32 -> x35, waiting for transfers between devices: 83 us -> 99.4 us  [swap(): return lax.ppermute(array, 'dp', [(i, i ^ flip) for i in range(devices)])]
    all_to_all x1, waiting for transfers between devices: 2.89 us -> 14.6 us  [exchange(): return lax.all_to_all(pieces, 'dp', split_axis=0, concat_axis=0, tiled=True)]
    pallas_call x0 -> x4, Pallas kernels: none -> 11.2 us  [the longest x2 9.11 us: sums_call(): pl.pallas_call(kernel, out_shape=jax.ShapeDtypeStruct((num_adapters,) + p...]
    ppermute x32 -> x35, starting transfers between devices: 46 us -> 40.9 us  [swap(): return lax.ppermute(array, 'dp', [(i, i ^ flip) for i in range(devices)])]
    concatenate x8 -> x4, other arithmetic: 5.09 us -> 0.04 us  [gather_step(): return jnp.concatenate([held, arrived], axis=0)]
    unnamed x41 -> x30, local copies, waits for them, and re-layouts: 7.86 us -> 6.16 us
  transfers between devices with their start and end apart: 33 -> 36, of which waited for: 15 -> 20; matrix products, arithmetic and copies ran while one was open for 3% -> 0% of each run, Pallas kernels for 12% -> 10%
where the time goes in v5:
time: 195 us
  waiting for transfers between devices  114 us (58%)
  starting transfers between devices  45.9 us (24%)
  Pallas kernels  27.5 us (14%)
  local copies, waits for them, and re-layouts  6.24 us (3%)
    ppermute x35, waiting for transfers between devices, swap(): return lax.ppermute(array, 'dp', [(i, i ^ flip) for i in range(devices)])  99.4 us
    ppermute x35, starting transfers between devices, swap(): return lax.ppermute(array, 'dp', [(i, i ^ flip) for i in range(devices)])  40.9 us
    pallas_call x7, Pallas kernels, call(): pl.pallas_call(kernel, out_shape=out_shapes, grid_spec=pltpu.PrefetchScal...  16.3 us
    all_to_all x1, waiting for transfers between devices, exchange(): return lax.all_to_all(pieces, 'dp', split_axis=0, concat_axis=0, tiled=True)  14.6 us
    pallas_call x2, Pallas kernels, sums_call(): pl.pallas_call(kernel, out_shape=jax.ShapeDtypeStruct((num_adapters,) + p...  9.11 us
    unnamed x30, local copies, waits for them, and re-layouts  6.16 us
    all_to_all x1, starting transfers between devices, exchange(): return lax.all_to_all(pieces, 'dp', split_axis=0, concat_axis=0, tiled=True)  4.99 us
  transfers between devices with their start and end apart: 36, of which 20 were waited for; matrix products, arithmetic and copies ran while one was open for 0% of the time, Pallas kernels for 10%

profile of v5, /device:TPU:0, one launch (start us, length us, event | category | flops | bytes accessed | tf_op | source)
XLA Modules:
  0.0 194.6 jit_solution(13160706874954144337)
XLA Ops:
  0.6 1.2 copy-done.1
  2.5 3.5 %for_pair.1 = bf16[2048,512]{1,0:T(8,128)(2,1)} custom-call(s32[16]{0:T(128)S(1)} %copy-done.5, s32[1]{0:T(128)} %bitcast.place, bf16[1024,512]{1,0:T(8,128)(2,1)S(1)} %copy-done.1, bf16[64,128,512]{2,1,0:T(8,128)(2,1)} %refs_7_.5, bf16[64,128,512]{2,1,0:T(8,128)(2,1)} %refs_7_.5, bf16[64,128,512]{2,1,0:T(8,128)(2,1)} %refs_7_.5, ...), custom_call_target="tpu_custom_call" | custom-call | tf_op jit(solution)/shard_map/for_pair/pallas_call | solution.py:40
  6.1 3.0 %collective-permute-start = (bf16[2048,512]{1,0:T(8,128)(2,1)}, bf16[2048,512]{1,0:T(8,128)(2,1)}, u32[]{:S(2)}, u32[]{:S(2)}) collective-permute-start(bf16[2048,512]{1,0:T(8,128)(2,1)} %for_pair.1), channel_id=1, source_target_pairs={{0,2},{1,3},{2,0},{3,1},{4,6},{5,7},{6,4},{7,5},{8,10},{9,11},{10,... | collective-permute-start | bytes 6291464 | tf_op jit(solution)/shard_map/ppermute | solution.py:447
  9.0 1.8 gather_up.1
  10.8 5.0 %all-to-all-start = ((bf16[16,64,128]{2,1,0:T(8,128)(2,1)}), bf16[16,64,128]{2,1,0:T(8,128)(2,1)S(1)}, u32[]{:S(2)}, u32[]{:S(2)}) async-start(bf16[16,64,128]{2,1,0:T(8,128)(2,1)} %gather_up.1), calls=%async_computation | async-start | bytes 524288 | tf_op jit(solution)/shard_map/all_to_all | solution.py:442
  16.3 1.7 collective-permute-start.2
  18.0 2.4 %collective-permute-start.1 = (bf16[1,128,1024]{2,1,0:T(8,128)(2,1)S(1)}, bf16[1,128,1024]{2,1,0:T(8,128)(2,1)}, u32[]{:S(2)}, u32[]{:S(2)}) collective-permute-start(bf16[1,128,1024]{2,1,0:T(8,128)(2,1)S(1)} %bitcast.5), channel_id=1, source_target_pairs={{0,8},{1,9},{2,10},{3,11},{4,12},{5,13},{6,14},{7,15},{8,0},{9,1},... | collective-permute-start | bytes 786440 | tf_op jit(solution)/shard_map/ppermute | solution.py:447
  20.4 0.9 pack_tokens.1
  26.0 8.0 %collective-permute-done.2.refs_2_ = bf16[1,128,1024]{2,1,0:T(8,128)(2,1)S(1)} collective-permute-done((bf16[1,128,1024]{2,1,0:T(8,128)(2,1)S(1)}, bf16[1,128,1024]{2,1,0:T(8,128)(2,1)S(1)}, u32[]{:S(2)}, u32[]{:S(2)}) %collective-permute-start.2) | collective-permute-done | bytes 262176 | tf_op jit(solution)/shard_map/ppermute | solution.py:447
  34.0 8.9 %collective-permute-done.1.refs_1_ = bf16[1,128,1024]{2,1,0:T(8,128)(2,1)} collective-permute-done((bf16[1,128,1024]{2,1,0:T(8,128)(2,1)S(1)}, bf16[1,128,1024]{2,1,0:T(8,128)(2,1)}, u32[]{:S(2)}, u32[]{:S(2)}) %collective-permute-start.1) | collective-permute-done | bytes 262176 | tf_op jit(solution)/shard_map/ppermute | solution.py:447
  42.9 14.6 %all-to-all-done = bf16[16,64,128]{2,1,0:T(8,128)(2,1)S(1)} async-done(((bf16[16,64,128]{2,1,0:T(8,128)(2,1)}), bf16[16,64,128]{2,1,0:T(8,128)(2,1)S(1)}, u32[]{:S(2)}, u32[]{:S(2)}) %all-to-all-start) | async-done | bytes 262176 | tf_op jit(solution)/shard_map/all_to_all | solution.py:442
  57.5 1.8 collective-permute-start.5
  60.1 2.7 %collective-permute-start.4 = (bf16[1,128,128]{2,1,0:T(8,128)(2,1)S(1)}, bf16[1,128,128]{2,1,0:T(8,128)(2,1)S(1)}, u32[]{:S(2)}, u32[]{:S(2)}) collective-permute-start(bf16[1,128,128]{2,1,0:T(8,128)(2,1)S(1)} %back_low.1), channel_id=1, source_target_pairs={{0,8},{1,9},{2,10},{3,11},{4,12},{5,13},{6,14},{7,15},{8,0},{9,1},... | collective-permute-start | bytes 98312 | tf_op jit(solution)/shard_map/ppermute | solution.py:447
  62.7 3.3 %collective-permute-done.4 = bf16[1,128,128]{2,1,0:T(8,128)(2,1)S(1)} collective-permute-done((bf16[1,128,128]{2,1,0:T(8,128)(2,1)S(1)}, bf16[1,128,128]{2,1,0:T(8,128)(2,1)S(1)}, u32[]{:S(2)}, u32[]{:S(2)}) %collective-permute-start.4) | collective-permute-done | bytes 32800 | tf_op jit(solution)/shard_map/ppermute | solution.py:447
  66.8 2.9 %collective-permute-start.7 = (bf16[2,128,128]{2,1,0:T(8,128)(2,1)S(1)}, bf16[2,128,128]{2,1,0:T(8,128)(2,1)S(1)}, u32[]{:S(2)}, u32[]{:S(2)}) collective-permute-start(bf16[2,128,128]{2,1,0:T(8,128)(2,1)S(1)} %pad_maximum_fusion.2), channel_id=1, source_target_pairs={{0,4},{1,5},{2,6},{3,7},{4,0},{5,1},{6,2},{7,3},{8,12},{9,13},{10,... | collective-permute-start | bytes 196616 | tf_op jit(solution)/shard_map/ppermute | solution.py:447
  69.7 1.3 collective-permute-start.11
  72.1 6.8 %collective-permute-done.11.refs_11_ = bf16[2,128,512]{2,1,0:T(8,128)(2,1)S(1)} collective-permute-done((bf16[2,128,512]{2,1,0:T(8,128)(2,1)}, bf16[2,128,512]{2,1,0:T(8,128)(2,1)S(1)}, u32[]{:S(2)}, u32[]{:S(2)}) %collective-permute-start.11) | collective-permute-done | bytes 262176 | tf_op jit(solution)/shard_map/ppermute | solution.py:447
  79.0 4.1 %collective-permute-start.13 = (bf16[2,128,512]{2,1,0:T(8,128)(2,1)}, bf16[2,128,512]{2,1,0:T(8,128)(2,1)S(1)}, u32[]{:S(2)}, u32[]{:S(2)}) collective-permute-start(bf16[2,128,512]{2,1,0:T(8,128)(2,1)} %copy-done.12), channel_id=1, source_target_pairs={{0,4},{1,5},{2,6},{3,7},{4,0},{5,1},{6,2},{7,3},{8,12},{9,13},{10,... | collective-permute-start | bytes 786440 | tf_op jit(solution)/shard_map/ppermute | solution.py:447
  83.2 1.2 collective-permute-start.15
  84.5 1.7 collective-permute-start.16
  86.3 1.1 collective-permute-start.17
  87.4 5.5 %input_slices.1 = (bf16[2,128,512]{2,1,0:T(8,128)(2,1)S(1)}, bf16[2,128,512]{2,1,0:T(8,128)(2,1)S(1)}, bf16[2,128,512]{2,1,0:T(8,128)(2,1)S(1)}, bf16[2,128,512]...) custom-call(s32[16]{0:T(128)S(1)} %copy-done.6, ...), custom_call_target="tpu_custom_call" | custom-call | tf_op jit(solution)/shard_map/input_slices/pallas_call | solution.py:40
  93.0 2.9 %collective-permute-done.13.refs_10_ = bf16[2,128,512]{2,1,0:T(8,128)(2,1)S(1)} collective-permute-done((bf16[2,128,512]{2,1,0:T(8,128)(2,1)}, bf16[2,128,512]{2,1,0:T(8,128)(2,1)S(1)}, u32[]{:S(2)}, u32[]{:S(2)}) %collective-permute-start.13) | collective-permute-done | bytes 262176 | tf_op jit(solution)/shard_map/ppermute | solution.py:447
  95.9 5.5 %collective-permute-done.16.refs_14_ = bf16[2,128,512]{2,1,0:T(8,128)(2,1)S(1)} collective-permute-done((bf16[2,128,512]{2,1,0:T(8,128)(2,1)}, bf16[2,128,512]{2,1,0:T(8,128)(2,1)S(1)}, u32[]{:S(2)}, u32[]{:S(2)}) %collective-permute-start.16) | collective-permute-done | bytes 262176 | tf_op jit(solution)/shard_map/ppermute | solution.py:447
  101.4 7.8 %collective-permute-done.17.refs_15_ = bf16[2,128,512]{2,1,0:T(8,128)(2,1)S(1)} collective-permute-done((bf16[2,128,512]{2,1,0:T(8,128)(2,1)}, bf16[2,128,512]{2,1,0:T(8,128)(2,1)S(1)}, u32[]{:S(2)}, u32[]{:S(2)}) %collective-permute-start.17) | collective-permute-done | bytes 262176 | tf_op jit(solution)/shard_map/ppermute | solution.py:447
  109.2 3.3 %hidden_parts.1 = (f32[8,128,128]{2,1,0:T(8,128)S(1)}, bf16[8,128,512]{2,1,0:T(8,128)(2,1)S(1)}, bf16[8,128,512]{2,1,0:T(8,128)(2,1)S(1)}) custom-call(s32[16]{0:T(128)S(1)} %copy-done.6, s32[1]{0:T(128)} %bitcast.place, bf16[2048,512]{1,0:T(8,128)(2,1)} %collective-permute-done.pair, bf16[64,128,512]{2,1,0:T(8,128)(2,1)} %refs_7_.5, ...), custom_call_target="tpu_custom_call" | custom-call | tf_op jit(solution)/shard_map/hidden_parts/pallas_call | solution.py:40
  112.9 1.2 collective-permute-start.32
  114.9 1.2 collective-permute-start.22
  116.0 0.9 collective-permute-start.21
  116.9 1.4 collective-permute-start.20
  118.3 1.6 collective-permute-done.19
  119.9 1.6 collective-permute-start.24
  121.5 22.9 %collective-permute-done.22.backs_pair = bf16[8,128,128]{2,1,0:T(8,128)(2,1)S(1)} collective-permute-done((bf16[8,128,128]{2,1,0:T(8,128)(2,1)S(1)}, bf16[8,128,128]{2,1,0:T(8,128)(2,1)S(1)}, u32[]{:S(2)}, u32[]{:S(2)}) %collective-permute-start.22) | collective-permute-done | bytes 262176 | tf_op jit(solution)/shard_map/ppermute | solution.py:447
  144.5 4.9 %collective-permute-done.21.gradients_pair = bf16[8,128,128]{2,1,0:T(8,128)(2,1)S(1)} collective-permute-done((bf16[8,128,128]{2,1,0:T(8,128)(2,1)S(1)}, bf16[8,128,128]{2,1,0:T(8,128)(2,1)S(1)}, u32[]{:S(2)}, u32[]{:S(2)}) %collective-permute-start.21) | collective-permute-done | bytes 262176 | tf_op jit(solution)/shard_map/ppermute | solution.py:447
  149.4 2.1 %collective-permute-start.23 = (f32[1,128,128]{2,1,0:T(8,128)S(1)}, f32[1,128,128]{2,1,0:T(8,128)S(1)}, u32[]{:S(2)}, u32[]{:S(2)}) collective-permute-start(f32[1,128,128]{2,1,0:T(8,128)S(1)} %get-tuple-element.182), channel_id=1, source_target_pairs={{0,8},{1,9},{2,10},{3,11},{4,12},{5,13},{6,14},{7,15},{8,0},{9,1},... | collective-permute-start | bytes 196616 | tf_op jit(solution)/shard_map/ppermute | solution.py:447
  151.5 3.9 %collective-permute-done.23.received = f32[1,128,128]{2,1,0:T(8,128)S(1)} collective-permute-done((f32[1,128,128]{2,1,0:T(8,128)S(1)}, f32[1,128,128]{2,1,0:T(8,128)S(1)}, u32[]{:S(2)}, u32[]{:S(2)}) %collective-permute-start.23) | collective-permute-done | bytes 65568 | tf_op jit(solution)/shard_map/ppermute | solution.py:447
  155.9 1.4 collective-permute-start.28
  157.7 3.2 %collective-permute-done.28 = bf16[1,128,128]{2,1,0:T(8,128)(2,1)S(1)} collective-permute-done((bf16[1,128,128]{2,1,0:T(8,128)(2,1)S(1)}, bf16[1,128,128]{2,1,0:T(8,128)(2,1)S(1)}, u32[]{:S(2)}, u32[]{:S(2)}) %collective-permute-start.28) | collective-permute-done | bytes 32800 | tf_op jit(solution)/shard_map/ppermute | solution.py:447
  161.1 8.9 %collective-permute-done.29 = bf16[2,128,128]{2,1,0:T(8,128)(2,1)S(1)} collective-permute-done((bf16[2,128,128]{2,1,0:T(8,128)(2,1)S(1)}, bf16[2,128,128]{2,1,0:T(8,128)(2,1)S(1)}, u32[]{:S(2)}, u32[]{:S(2)}) %collective-permute-start.29) | collective-permute-done | bytes 65568 | tf_op jit(solution)/shard_map/ppermute | solution.py:447
  170.0 5.5 %down_gradients.1 = bf16[64,128,512]{2,1,0:T(8,128)(2,1)} custom-call(s32[16]{0:T(128)S(1)} %copy-done.6, s32[1]{0:T(128)} %bitcast.place, bf16[8,128,128]{2,1,0:T(8,128)(2,1)S(1)} %constant_dynamic-update-slice_fusion.backs, bf16[8,128,128]{2,1,0:T(8,128)(2,1)S(1)} %collective-permute-done.22.backs_pair, bf16[8,128,512]{2,1,0:T(8,128)(2,1)S(1)} %get-tuple-element.171.own, ...), custom_call_target="tpu_custom_call" | custom-call | tf_op jit(solution)/shard_map/down_gradients/pallas_call | solution.py:343
  175.7 1.3 collective-permute-done.33
  177.0 1.2 collective-permute-start.34
  179.6 1.2 collective-permute-start.27
  180.8 1.1 join_columns.2.refs_3_
  181.9 3.5 %collective-permute-done.34.hiddens_pair = bf16[8,128,128]{2,1,0:T(8,128)(2,1)S(1)} collective-permute-done((bf16[8,128,128]{2,1,0:T(8,128)(2,1)S(1)}, bf16[8,128,128]{2,1,0:T(8,128)(2,1)S(1)}, u32[]{:S(2)}, u32[]{:S(2)}) %collective-permute-start.34) | collective-permute-done | bytes 262176 | tf_op jit(solution)/shard_map/ppermute | solution.py:447
  185.4 3.6 %up_gradients.1 = bf16[64,64,128]{2,1,0:T(8,128)(2,1)} custom-call(s32[16]{0:T(128)S(1)} %copy-done.6, s32[1]{0:T(128)} %bitcast.place, s32[64]{0:T(128)S(1)} %copy-done.7, bf16[8,128,128]{2,1,0:T(8,128)(2,1)S(1)} %get-tuple-element.167.gradients, bf16[8,128,128]{2,1,0:T(8,128)(2,1)S(1)} %collective-permute-done.21.gradients_pair, ...), custom_call_target="tpu_custom_call" | custom-call | tf_op jit(solution)/shard_map/up_gradients/pallas_call | solution.py:343
  189.0 4.6 %collective-permute-done.27.refs_2_ = bf16[2,128,512]{2,1,0:T(8,128)(2,1)S(1)} collective-permute-done((bf16[2,128,512]{2,1,0:T(8,128)(2,1)S(1)}, bf16[2,128,512]{2,1,0:T(8,128)(2,1)S(1)}, u32[]{:S(2)}, u32[]{:S(2)}) %collective-permute-start.27) | collective-permute-done | bytes 262176 | tf_op jit(solution)/shard_map/ppermute | solution.py:447
  193.6 0.9 join_columns.3
  (76 shorter events, 12.8 us)
Async XLA Ops:
  0.6 1.2 copy-start.1
  2.5 6.5 %copy-start.4 = (bf16[64,64,128]{2,1,0:T(8,128)(2,1)S(1)}, bf16[64,64,128]{2,1,0:T(8,128)(2,1)}, u32[]{:S(2)}) copy-start(bf16[64,64,128]{2,1,0:T(8,128)(2,1)} %up_maps.1) | copy-start | bytes 3145732
  2.5 13.3 %copy-start.3 = (bf16[128,1024]{1,0:T(8,128)(2,1)S(1)}, bf16[128,1024]{1,0:T(8,128)(2,1)}, u32[]{:S(2)}) copy-start(bf16[128,1024]{1,0:T(8,128)(2,1)} %gradient.1) | copy-start | bytes 786436
  2.5 17.8 %copy-start = (bf16[128,8192]{1,0:T(8,128)(2,1)S(1)}, bf16[128,8192]{1,0:T(8,128)(2,1)}, u32[]{:S(2)}) copy-start(bf16[128,8192]{1,0:T(8,128)(2,1)} %refs_15_.2) | copy-start | bytes 6291460
  6.1 80.2 %collective-permute-start = (bf16[2048,512]{1,0:T(8,128)(2,1)}, bf16[2048,512]{1,0:T(8,128)(2,1)}, u32[]{:S(2)}, u32[]{:S(2)}) collective-permute-start(bf16[2048,512]{1,0:T(8,128)(2,1)} %for_pair.1), channel_id=1, source_target_pairs={{0,2},{1,3},{2,0},{3,1},{4,6},{5,7},{6,4},{7,5},{8,10},{9,11},{10,... | collective-permute-start | bytes 6291464 | tf_op jit(solution)/shard_map/ppermute | solution.py:447
  10.8 46.7 %all-to-all-start = ((bf16[16,64,128]{2,1,0:T(8,128)(2,1)}), bf16[16,64,128]{2,1,0:T(8,128)(2,1)S(1)}, u32[]{:S(2)}, u32[]{:S(2)}) async-start(bf16[16,64,128]{2,1,0:T(8,128)(2,1)} %gather_up.1), calls=%async_computation | async-start | bytes 524288 | tf_op jit(solution)/shard_map/all_to_all | solution.py:442
  15.8 43.5 %copy-start.6 = (s32[16]{0:T(128)S(1)}, s32[16]{0:T(128)}, u32[]{:S(2)}) copy-start(s32[16]{0:T(128)} %adapters.15) | copy-start | bytes 196
  15.8 43.5 %copy-start.7 = (s32[64]{0:T(128)S(1)}, s32[64]{0:T(128)}, u32[]{:S(2)}) copy-start(s32[64]{0:T(128)} %ranks.5) | copy-start | bytes 772
  15.8 10.2 %collective-permute-start.3 = (bf16[1,128,1024]{2,1,0:T(8,128)(2,1)S(1)}, bf16[1,128,1024]{2,1,0:T(8,128)(2,1)S(1)}, u32[]{:S(2)}, u32[]{:S(2)}) collective-permute-start(bf16[1,128,1024]{2,1,0:T(8,128)(2,1)S(1)} %bitcast.3), channel_id=1, source_target_pairs={{0,1},{1,0},{2,3},{3,2},{4,5},{5,4},{6,7},{7,6},{8,9},{9,8},{10,11... | collective-permute-start | bytes 786440 | tf_op jit(solution)/shard_map/ppermute | solution.py:447
  16.3 17.7 %collective-permute-start.2 = (bf16[1,128,1024]{2,1,0:T(8,128)(2,1)S(1)}, bf16[1,128,1024]{2,1,0:T(8,128)(2,1)S(1)}, u32[]{:S(2)}, u32[]{:S(2)}) collective-permute-start(bf16[1,128,1024]{2,1,0:T(8,128)(2,1)S(1)} %bitcast.4), channel_id=1, source_target_pairs={{0,4},{1,5},{2,6},{3,7},{4,0},{5,1},{6,2},{7,3},{8,12},{9,13},{10,... | collective-permute-start | bytes 786440 | tf_op jit(solution)/shard_map/ppermute | solution.py:447
  18.0 24.9 %collective-permute-start.1 = (bf16[1,128,1024]{2,1,0:T(8,128)(2,1)S(1)}, bf16[1,128,1024]{2,1,0:T(8,128)(2,1)}, u32[]{:S(2)}, u32[]{:S(2)}) collective-permute-start(bf16[1,128,1024]{2,1,0:T(8,128)(2,1)S(1)} %bitcast.5), channel_id=1, source_target_pairs={{0,8},{1,9},{2,10},{3,11},{4,12},{5,13},{6,14},{7,15},{8,0},{9,1},... | collective-permute-start | bytes 786440 | tf_op jit(solution)/shard_map/ppermute | solution.py:447
  21.2 0.7 copy-start.8
  21.9 0.7 copy-start.9
  22.6 0.7 copy-start.10
  24.0 0.7 copy-start.12
  24.8 0.7 copy-start.13
  25.5 62.0 %copy-start.2 = (bf16[1024,512]{1,0:T(8,128)(2,1)S(1)}, bf16[1024,512]{1,0:T(8,128)(2,1)}, u32[]{:S(2)}) copy-start(bf16[1024,512]{1,0:T(8,128)(2,1)} %refs_16_.1) | copy-start | bytes 3145732
  25.5 40.6 %collective-permute-start.6 = (bf16[2,128,512]{2,1,0:T(8,128)(2,1)}, bf16[2,128,512]{2,1,0:T(8,128)(2,1)S(1)}, u32[]{:S(2)}, u32[]{:S(2)}) collective-permute-start(bf16[2,128,512]{2,1,0:T(8,128)(2,1)} %get-tuple-element.93), channel_id=1, source_target_pairs={{0,8},{1,9},{2,10},{3,11},{4,12},{5,13},{6,14},{7,15},{8,0},{9,1},... | collective-permute-start | bytes 786440 | tf_op jit(solution)/shard_map/ppermute | solution.py:447
  57.5 9.3 %collective-permute-start.5 = (bf16[1,128,1024]{2,1,0:T(8,128)(2,1)}, bf16[1,128,1024]{2,1,0:T(8,128)(2,1)S(1)}, u32[]{:S(2)}, u32[]{:S(2)}) collective-permute-start(bf16[1,128,1024]{2,1,0:T(8,128)(2,1)} %collective-permute-done.1.refs_1_), channel_id=1, source_target_pairs={{0,4},{1,5},{2,6},{3,7},{4,0},{5,1},{6,2},{7,3},{8,12},{9,13},{10,... | collective-permute-start | bytes 786440 | tf_op jit(solution)/shard_map/ppermute | solution.py:447
  60.1 6.0 %collective-permute-start.4 = (bf16[1,128,128]{2,1,0:T(8,128)(2,1)S(1)}, bf16[1,128,128]{2,1,0:T(8,128)(2,1)S(1)}, u32[]{:S(2)}, u32[]{:S(2)}) collective-permute-start(bf16[1,128,128]{2,1,0:T(8,128)(2,1)S(1)} %back_low.1), channel_id=1, source_target_pairs={{0,8},{1,9},{2,10},{3,11},{4,12},{5,13},{6,14},{7,15},{8,0},{9,1},... | collective-permute-start | bytes 98312 | tf_op jit(solution)/shard_map/ppermute | solution.py:447
  66.8 5.3 %collective-permute-start.7 = (bf16[2,128,128]{2,1,0:T(8,128)(2,1)S(1)}, bf16[2,128,128]{2,1,0:T(8,128)(2,1)S(1)}, u32[]{:S(2)}, u32[]{:S(2)}) collective-permute-start(bf16[2,128,128]{2,1,0:T(8,128)(2,1)S(1)} %pad_maximum_fusion.2), channel_id=1, source_target_pairs={{0,4},{1,5},{2,6},{3,7},{4,0},{5,1},{6,2},{7,3},{8,12},{9,13},{10,... | collective-permute-start | bytes 196616 | tf_op jit(solution)/shard_map/ppermute | solution.py:447
  69.7 9.3 %collective-permute-start.11 = (bf16[2,128,512]{2,1,0:T(8,128)(2,1)}, bf16[2,128,512]{2,1,0:T(8,128)(2,1)S(1)}, u32[]{:S(2)}, u32[]{:S(2)}) collective-permute-start(bf16[2,128,512]{2,1,0:T(8,128)(2,1)} %copy-done.13), channel_id=1, source_target_pairs={{0,12},{1,13},{2,14},{3,15},{4,8},{5,9},{6,10},{7,11},{8,4},{9,5},... | collective-permute-start | bytes 786440 | tf_op jit(solution)/shard_map/ppermute | solution.py:447
  71.0 7.9 %collective-permute-start.8 = (bf16[1,128,1024]{2,1,0:T(8,128)(2,1)}, bf16[1,128,1024]{2,1,0:T(8,128)(2,1)S(1)}, u32[]{:S(2)}, u32[]{:S(2)}) collective-permute-start(bf16[1,128,1024]{2,1,0:T(8,128)(2,1)} %collective-permute-done.1.refs_1_), channel_id=1, source_target_pairs={{0,1},{1,0},{2,3},{3,2},{4,5},{5,4},{6,7},{7,6},{8,9},{9,8},{10,11... | collective-permute-start | bytes 786440 | tf_op jit(solution)/shard_map/ppermute | solution.py:447
  71.0 7.9 %collective-permute-start.9 = (bf16[1,128,1024]{2,1,0:T(8,128)(2,1)S(1)}, bf16[1,128,1024]{2,1,0:T(8,128)(2,1)S(1)}, u32[]{:S(2)}, u32[]{:S(2)}) collective-permute-start(bf16[1,128,1024]{2,1,0:T(8,128)(2,1)S(1)} %collective-permute-done.2.refs_2_), channel_id=1, source_target_pairs={{0,1},{1,0},{2,3},{3,2},{4,5},{5,4},{6,7},{7,6},{8,9},{9,8},{10,11... | collective-permute-start | bytes 786440 | tf_op jit(solution)/shard_map/ppermute | solution.py:447
  72.1 6.9 %collective-permute-start.10 = (bf16[1,128,1024]{2,1,0:T(8,128)(2,1)S(1)}, bf16[1,128,1024]{2,1,0:T(8,128)(2,1)S(1)}, u32[]{:S(2)}, u32[]{:S(2)}) collective-permute-start(bf16[1,128,1024]{2,1,0:T(8,128)(2,1)S(1)} %collective-permute-done.5.refs_3_), channel_id=1, source_target_pairs={{0,1},{1,0},{2,3},{3,2},{4,5},{5,4},{6,7},{7,6},{8,9},{9,8},{10,11... | collective-permute-start | bytes 786440 | tf_op jit(solution)/shard_map/ppermute | solution.py:447
  78.9 5.6 %collective-permute-start.12 = (bf16[4,128,128]{2,1,0:T(8,128)(2,1)S(1)}, bf16[4,128,128]{2,1,0:T(8,128)(2,1)S(1)}, u32[]{:S(2)}, u32[]{:S(2)}) collective-permute-start(bf16[4,128,128]{2,1,0:T(8,128)(2,1)S(1)} %pad_maximum_fusion), channel_id=1, source_target_pairs={{0,1},{1,0},{2,3},{3,2},{4,5},{5,4},{6,7},{7,6},{8,9},{9,8},{10,11... | collective-permute-start | bytes 393224 | tf_op jit(solution)/shard_map/ppermute | solution.py:447
  79.0 16.9 %collective-permute-start.13 = (bf16[2,128,512]{2,1,0:T(8,128)(2,1)}, bf16[2,128,512]{2,1,0:T(8,128)(2,1)S(1)}, u32[]{:S(2)}, u32[]{:S(2)}) collective-permute-start(bf16[2,128,512]{2,1,0:T(8,128)(2,1)} %copy-done.12), channel_id=1, source_target_pairs={{0,4},{1,5},{2,6},{3,7},{4,0},{5,1},{6,2},{7,3},{8,12},{9,13},{10,... | collective-permute-start | bytes 786440 | tf_op jit(solution)/shard_map/ppermute | solution.py:447
  83.2 12.7 %collective-permute-start.15 = (bf16[2,128,512]{2,1,0:T(8,128)(2,1)}, bf16[2,128,512]{2,1,0:T(8,128)(2,1)S(1)}, u32[]{:S(2)}, u32[]{:S(2)}) collective-permute-start(bf16[2,128,512]{2,1,0:T(8,128)(2,1)} %copy-done.11), channel_id=1, source_target_pairs={{0,9},{1,8},{2,11},{3,10},{4,13},{5,12},{6,15},{7,14},{8,1},{9,0},... | collective-permute-start | bytes 786440 | tf_op jit(solution)/shard_map/ppermute | solution.py:447
  84.4 11.5 %collective-permute-start.14 = (bf16[2,128,512]{2,1,0:T(8,128)(2,1)}, bf16[2,128,512]{2,1,0:T(8,128)(2,1)S(1)}, u32[]{:S(2)}, u32[]{:S(2)}) collective-permute-start(bf16[2,128,512]{2,1,0:T(8,128)(2,1)} %copy-done.10), channel_id=1, source_target_pairs={{0,1},{1,0},{2,3},{3,2},{4,5},{5,4},{6,7},{7,6},{8,9},{9,8},{10,11... | collective-permute-start | bytes 786440 | tf_op jit(solution)/shard_map/ppermute | solution.py:447
  84.5 16.8 %collective-permute-start.16 = (bf16[2,128,512]{2,1,0:T(8,128)(2,1)}, bf16[2,128,512]{2,1,0:T(8,128)(2,1)S(1)}, u32[]{:S(2)}, u32[]{:S(2)}) collective-permute-start(bf16[2,128,512]{2,1,0:T(8,128)(2,1)} %copy-done.9), channel_id=1, source_target_pairs={{0,5},{1,4},{2,7},{3,6},{4,1},{5,0},{6,3},{7,2},{8,13},{9,12},{10,... | collective-permute-start | bytes 786440 | tf_op jit(solution)/shard_map/ppermute | solution.py:447
  86.3 22.9 %collective-permute-start.17 = (bf16[2,128,512]{2,1,0:T(8,128)(2,1)}, bf16[2,128,512]{2,1,0:T(8,128)(2,1)S(1)}, u32[]{:S(2)}, u32[]{:S(2)}) collective-permute-start(bf16[2,128,512]{2,1,0:T(8,128)(2,1)} %copy-done.8), channel_id=1, source_target_pairs={{0,13},{1,12},{2,15},{3,14},{4,9},{5,8},{6,11},{7,10},{8,5},{9,4},... | collective-permute-start | bytes 786440 | tf_op jit(solution)/shard_map/ppermute | solution.py:447
  112.5 1.6 collective-permute-start.18
  112.9 57.1 %collective-permute-start.32 = (bf16[8,128,512]{2,1,0:T(8,128)(2,1)S(1)}, bf16[8,128,512]{2,1,0:T(8,128)(2,1)S(1)}, u32[]{:S(2)}, u32[]{:S(2)}) collective-permute-start(bf16[8,128,512]{2,1,0:T(8,128)(2,1)S(1)} %get-tuple-element.172), channel_id=1, source_target_pairs={{0,2},{1,3},{2,0},{3,1},{4,6},{5,7},{6,4},{7,5},{8,10},{9,11},{10,... | collective-permute-start | bytes 3145736 | tf_op jit(solution)/shard_map/ppermute | solution.py:447
  114.2 5.8 %collective-permute-start.19 = (f32[2,128,128]{2,1,0:T(8,128)S(1)}, f32[2,128,128]{2,1,0:T(8,128)S(1)}, u32[]{:S(2)}, u32[]{:S(2)}) collective-permute-start(f32[2,128,128]{2,1,0:T(8,128)S(1)} %slice.25), channel_id=1, source_target_pairs={{0,4},{1,5},{2,6},{3,7},{4,0},{5,1},{6,2},{7,3},{8,12},{9,13},{10,... | collective-permute-start | bytes 393224 | tf_op jit(solution)/shard_map/ppermute | solution.py:447
  114.9 29.6 %collective-permute-start.22 = (bf16[8,128,128]{2,1,0:T(8,128)(2,1)S(1)}, bf16[8,128,128]{2,1,0:T(8,128)(2,1)S(1)}, u32[]{:S(2)}, u32[]{:S(2)}) collective-permute-start(bf16[8,128,128]{2,1,0:T(8,128)(2,1)S(1)} %constant_dynamic-update-slice_fusion.backs), channel_id=1, source_target_pairs={{0,2},{1,3},{2,0},{3,1},{4,6},{5,7},{6,4},{7,5},{8,10},{9,11},{10,... | collective-permute-start | bytes 786440 | tf_op jit(solution)/shard_map/ppermute | solution.py:447
  116.0 33.4 %collective-permute-start.21 = (bf16[8,128,128]{2,1,0:T(8,128)(2,1)S(1)}, bf16[8,128,128]{2,1,0:T(8,128)(2,1)S(1)}, u32[]{:S(2)}, u32[]{:S(2)}) collective-permute-start(bf16[8,128,128]{2,1,0:T(8,128)(2,1)S(1)} %get-tuple-element.152), channel_id=1, source_target_pairs={{0,2},{1,3},{2,0},{3,1},{4,6},{5,7},{6,4},{7,5},{8,10},{9,11},{10,... | collective-permute-start | bytes 786440 | tf_op jit(solution)/shard_map/ppermute | solution.py:447
  116.9 32.5 %collective-permute-start.20 = (bf16[2,128,512]{2,1,0:T(8,128)(2,1)S(1)}, bf16[2,128,512]{2,1,0:T(8,128)(2,1)S(1)}, u32[]{:S(2)}, u32[]{:S(2)}) collective-permute-start(bf16[2,128,512]{2,1,0:T(8,128)(2,1)S(1)} %get-tuple-element.131), channel_id=1, source_target_pairs={{0,8},{1,9},{2,10},{3,11},{4,12},{5,13},{6,14},{7,15},{8,0},{9,1},... | collective-permute-start | bytes 786440 | tf_op jit(solution)/shard_map/ppermute | solution.py:447
  119.9 31.5 %collective-permute-start.24 = (bf16[2,128,512]{2,1,0:T(8,128)(2,1)S(1)}, bf16[2,128,512]{2,1,0:T(8,128)(2,1)S(1)}, u32[]{:S(2)}, u32[]{:S(2)}) collective-permute-start(bf16[2,128,512]{2,1,0:T(8,128)(2,1)S(1)} %get-tuple-element.133), channel_id=1, source_target_pairs={{0,12},{1,13},{2,14},{3,15},{4,8},{5,9},{6,10},{7,11},{8,4},{9,5},... | collective-permute-start | bytes 786440 | tf_op jit(solution)/shard_map/ppermute | solution.py:447
  149.4 5.9 %collective-permute-start.23 = (f32[1,128,128]{2,1,0:T(8,128)S(1)}, f32[1,128,128]{2,1,0:T(8,128)S(1)}, u32[]{:S(2)}, u32[]{:S(2)}) collective-permute-start(f32[1,128,128]{2,1,0:T(8,128)S(1)} %get-tuple-element.182), channel_id=1, source_target_pairs={{0,8},{1,9},{2,10},{3,11},{4,12},{5,13},{6,14},{7,15},{8,0},{9,1},... | collective-permute-start | bytes 196616 | tf_op jit(solution)/shard_map/ppermute | solution.py:447
  155.9 5.0 %collective-permute-start.28 = (bf16[1,128,128]{2,1,0:T(8,128)(2,1)S(1)}, bf16[1,128,128]{2,1,0:T(8,128)(2,1)S(1)}, u32[]{:S(2)}, u32[]{:S(2)}) collective-permute-start(bf16[1,128,128]{2,1,0:T(8,128)(2,1)S(1)} %hidden_low.1), channel_id=1, source_target_pairs={{0,8},{1,9},{2,10},{3,11},{4,12},{5,13},{6,14},{7,15},{8,0},{9,1},... | collective-permute-start | bytes 98312 | tf_op jit(solution)/shard_map/ppermute | solution.py:447
  157.2 18.3 %collective-permute-start.31 = (bf16[2,128,512]{2,1,0:T(8,128)(2,1)S(1)}, bf16[2,128,512]{2,1,0:T(8,128)(2,1)S(1)}, u32[]{:S(2)}, u32[]{:S(2)}) collective-permute-start(bf16[2,128,512]{2,1,0:T(8,128)(2,1)S(1)} %get-tuple-element.159), channel_id=1, source_target_pairs={{0,4},{1,5},{2,6},{3,7},{4,0},{5,1},{6,2},{7,3},{8,12},{9,13},{10,... | collective-permute-start | bytes 786440 | tf_op jit(solution)/shard_map/ppermute | solution.py:447
  157.7 17.8 %collective-permute-start.30 = (bf16[2,128,512]{2,1,0:T(8,128)(2,1)S(1)}, bf16[2,128,512]{2,1,0:T(8,128)(2,1)S(1)}, u32[]{:S(2)}, u32[]{:S(2)}) collective-permute-start(bf16[2,128,512]{2,1,0:T(8,128)(2,1)S(1)} %get-tuple-element.161), channel_id=1, source_target_pairs={{0,9},{1,8},{2,11},{3,10},{4,13},{5,12},{6,15},{7,14},{8,1},{9,0},... | collective-permute-start | bytes 786440 | tf_op jit(solution)/shard_map/ppermute | solution.py:447
  160.9 9.1 %collective-permute-start.29 = (bf16[2,128,128]{2,1,0:T(8,128)(2,1)S(1)}, bf16[2,128,128]{2,1,0:T(8,128)(2,1)S(1)}, u32[]{:S(2)}, u32[]{:S(2)}) collective-permute-start(bf16[2,128,128]{2,1,0:T(8,128)(2,1)S(1)} %pad_maximum_fusion.3), channel_id=1, source_target_pairs={{0,4},{1,5},{2,6},{3,7},{4,0},{5,1},{6,2},{7,3},{8,12},{9,13},{10,... | collective-permute-start | bytes 196616 | tf_op jit(solution)/shard_map/ppermute | solution.py:447
  175.6 1.4 collective-permute-start.33
  177.0 8.4 %collective-permute-start.34 = (bf16[8,128,128]{2,1,0:T(8,128)(2,1)S(1)}, bf16[8,128,128]{2,1,0:T(8,128)(2,1)S(1)}, u32[]{:S(2)}, u32[]{:S(2)}) collective-permute-start(bf16[8,128,128]{2,1,0:T(8,128)(2,1)S(1)} %constant_dynamic-update-slice_fusion.2.hiddens), channel_id=1, source_target_pairs={{0,2},{1,3},{2,0},{3,1},{4,6},{5,7},{6,4},{7,5},{8,10},{9,11},{10,... | collective-permute-start | bytes 786440 | tf_op jit(solution)/shard_map/ppermute | solution.py:447
  178.2 10.8 %collective-permute-start.25 = (bf16[2,128,512]{2,1,0:T(8,128)(2,1)S(1)}, bf16[2,128,512]{2,1,0:T(8,128)(2,1)S(1)}, u32[]{:S(2)}, u32[]{:S(2)}) collective-permute-start(bf16[2,128,512]{2,1,0:T(8,128)(2,1)S(1)} %get-tuple-element.164), channel_id=1, source_target_pairs={{0,13},{1,12},{2,15},{3,14},{4,9},{5,8},{6,11},{7,10},{8,5},{9,4},... | collective-permute-start | bytes 786440 | tf_op jit(solution)/shard_map/ppermute | solution.py:447
  179.0 10.1 %collective-permute-start.26 = (bf16[2,128,512]{2,1,0:T(8,128)(2,1)S(1)}, bf16[2,128,512]{2,1,0:T(8,128)(2,1)S(1)}, u32[]{:S(2)}, u32[]{:S(2)}) collective-permute-start(bf16[2,128,512]{2,1,0:T(8,128)(2,1)S(1)} %get-tuple-element.165), channel_id=1, source_target_pairs={{0,1},{1,0},{2,3},{3,2},{4,5},{5,4},{6,7},{7,6},{8,9},{9,8},{10,11... | collective-permute-start | bytes 786440 | tf_op jit(solution)/shard_map/ppermute | solution.py:447
  179.6 14.0 %collective-permute-start.27 = (bf16[2,128,512]{2,1,0:T(8,128)(2,1)S(1)}, bf16[2,128,512]{2,1,0:T(8,128)(2,1)S(1)}, u32[]{:S(2)}, u32[]{:S(2)}) collective-permute-start(bf16[2,128,512]{2,1,0:T(8,128)(2,1)S(1)} %get-tuple-element.166), channel_id=1, source_target_pairs={{0,5},{1,4},{2,7},{3,6},{4,1},{5,0},{6,3},{7,2},{8,13},{9,12},{10,... | collective-permute-start | bytes 786440 | tf_op jit(solution)/shard_map/ppermute | solution.py:447
  (2 other events, 1.3 us)

commit v6 on v5

--- a/solution.py
+++ b/solution.py
@@ -10,14 +10,25 @@
 adapter_alpha = 32.0
 vmem_limit = 48 * 1024 * 1024
 pair_bit = 2
+line_bit = 4
 
 
 def line_offset(slot, members):
     bits = members.bit_length() - 1
-    line = 0
+    order = 0
     for bit in range(bits):
-        line |= ((slot >> bit) & 1) << (bits - 1 - bit)
-    return ((line // pair_bit) * 2 * pair_bit) | (line % pair_bit)
+        order |= ((slot >> bit) & 1) << (bits - 1 - bit)
+    return ((order // 2) * line_bit) | (order % 2)
+
+
+def entry_of(place, slot, members):
+    offset = line_offset(slot, members)
+    return (offset % 2) * (members // 2) + ((place ^ offset) // line_bit)
+
+
+def place_of(entry, place, side, members):
+    core, line = divmod(entry, members // 2)
+    return line * line_bit + ((place % line_bit) ^ core ^ (side * pair_bit))
 
 
 def params():
@@ -52,73 +63,103 @@
     )(*prefetch, *operands)
 
 
-def pair_kernel(adapters, place, weight, *refs):
-    out = refs[-1]
-    count, extent, _ = refs[0].shape[0] * (len(refs) - 1), *refs[0].shape[1:]
-    for entry in range(count):
-        out[entry * extent : (entry + 1) * extent] = refs[entry][0]
-    out[count * extent :] = weight[...]
-
-
-def for_pair(adapters, place, weight, down_maps, members):
-    extent, width = down_maps.shape[1:]
-    shape = jax.ShapeDtypeStruct((members * extent + weight.shape[0], width), weight.dtype)
-    return call(
-        pair_kernel,
-        "for_pair",
-        (adapters, place),
-        [weight] + [down_maps] * members,
-        [whole(weight.shape)]
-        + [picked(down_maps, line_offset(slot, members) ^ pair_bit) for slot in range(members)],
-        [shape],
-    )[0]
-
-
-def gather_up_kernel(adapters, up_maps, out, sems):
-    copies = [
-        pltpu.make_async_copy(up_maps.at[adapters[block]], out.at[block], sems.at[block])
-        for block in range(out.shape[0])
-    ]
+def run(copies):
     for copy in copies:
         copy.start()
     for copy in copies:
         copy.wait()
 
 
+def copy_call(kernel, name, prefetch, operands, out_shapes, copies):
+    hbm = pl.BlockSpec(memory_space=pltpu.HBM)
+    return pl.pallas_call(
+        kernel,
+        out_shape=out_shapes,
+        grid_spec=pltpu.PrefetchScalarGridSpec(
+            num_scalar_prefetch=len(prefetch),
+            grid=(1,),
+            in_specs=[hbm] * len(operands),
+            out_specs=[hbm] * len(out_shapes),
+            scratch_shapes=[pltpu.SemaphoreType.DMA((copies,))],
+        ),
+        compiler_params=params(),
+        name=name,
+    )(*prefetch, *operands)
+
+
+weight_cuts = 8
+
+
+def pair_kernel(adapters, place, weight, down_maps, out, sems):
+    extent = down_maps.shape[1]
+    depth = weight.shape[0]
+    members = (out.shape[0] - depth) // extent
+    copies = []
+    for slot in range(members):
+        block = place[0] ^ line_offset(slot, members) ^ pair_bit
+        copies.append((down_maps.at[adapters[block]], slot * extent, extent))
+    cut = depth // weight_cuts
+    for at in range(0, depth, cut):
+        copies.append((weight.at[pl.ds(at, cut)], members * extent + at, cut))
+    run(
+        [
+            pltpu.make_async_copy(source, out.at[pl.ds(at, rows)], sems.at[number])
+            for number, (source, at, rows) in enumerate(copies)
+        ]
+    )
+
+
+def for_pair(adapters, place, weight, down_maps, members):
+    extent, width = down_maps.shape[1:]
+    shape = jax.ShapeDtypeStruct((members * extent + weight.shape[0], width), weight.dtype)
+    return copy_call(
+        pair_kernel,
+        "for_pair",
+        (adapters, place),
+        (weight, down_maps),
+        [shape],
+        members + weight_cuts,
+    )[0]
+
+
+def gather_up_kernel(adapters, up_maps, out, sems):
+    run(
+        [
+            pltpu.make_async_copy(up_maps.at[adapters[block]], out.at[block], sems.at[block])
+            for block in range(out.shape[0])
+        ]
+    )
+
+
 def gather_up(adapters, up_maps):
-    shape = (adapters.shape[0],) + up_maps.shape[1:]
-    return call(
-        gather_up_kernel,
-        "gather_up",
-        (adapters,),
-        [up_maps],
-        [pl.BlockSpec(memory_space=pltpu.HBM)],
-        [jax.ShapeDtypeStruct(shape, up_maps.dtype)],
-        scratch=[pltpu.SemaphoreType.DMA((shape[0],))],
+    shape = jax.ShapeDtypeStruct((adapters.shape[0],) + up_maps.shape[1:], up_maps.dtype)
+    return copy_call(
+        gather_up_kernel, "gather_up", (adapters,), (up_maps,), [shape], adapters.shape[0]
     )[0]
 
 
-def pack_kernel(place, *refs):
-    count = len(refs) // 3
-    for slot in range(count):
-        out = refs[2 * count + slot]
-        out[0] = refs[2 * slot][...]
-        out[1] = refs[2 * slot + 1][...]
+def pack_kernel(place, tokens, *refs):
+    outs, sems = refs[:-1], refs[-1]
+    members = len(outs)
+    width = outs[0].shape[2]
+    copies = []
+    for slot in range(members):
+        for half in range(2):
+            column = (place[0] ^ line_offset(slot, members) ^ (half * pair_bit)) * width
+            copies.append(
+                pltpu.make_async_copy(
+                    tokens.at[:, pl.ds(pl.multiple_of(column, width), width)],
+                    outs[slot].at[half],
+                    sems.at[2 * slot + half],
+                )
+            )
+    run(copies)
 
 
 def pack_tokens(place, tokens, members, width):
-    rows = tokens.shape[0]
-
-    def spec(flip):
-        return pl.BlockSpec((rows, width), lambda i, place: (0, place[0] ^ flip))
-
-    specs = []
-    for slot in range(members):
-        offset = line_offset(slot, members)
-        specs += [spec(offset), spec(offset ^ pair_bit)]
-    shape = jax.ShapeDtypeStruct((2, rows, width), tokens.dtype)
-    return call(
-        pack_kernel, "pack_tokens", (place,), [tokens] * len(specs), specs, [shape] * members
+    shape = jax.ShapeDtypeStruct((2, tokens.shape[0], width), tokens.dtype)
+    return copy_call(
+        pack_kernel, "pack_tokens", (place,), (tokens,), [shape] * members, 2 * members
     )
 
 
@@ -131,11 +172,13 @@
 def back_kernel(adapters, place, ranks, gradient, up, out):
     alive, factor = rank_row(ranks, adapters[place[0]], up.shape[1])
     back = jnp.dot(gradient[...], up[...], preferred_element_type=jnp.float32)
-    out[0] = (factor * back * alive).astype(out.dtype)
-
-
-def back_rows(adapters, place, ranks, gradient, up):
-    shape = jax.ShapeDtypeStruct((1, gradient.shape[0], up.shape[1]), jnp.bfloat16)
+    low = (factor * back * alive).astype(out.dtype)
+    for line in range(out.shape[0]):
+        out[line] = low
+
+
+def back_rows(adapters, place, ranks, gradient, up, lines):
+    shape = jax.ShapeDtypeStruct((lines, gradient.shape[0], up.shape[1]), jnp.bfloat16)
     return call(
         back_kernel,
         "back_low",
@@ -163,13 +206,15 @@
             frozen = jnp.dot(lines, right, preferred_element_type=jnp.float32)
             for slot in slots:
                 down = downs[slot][0] if half == 0 else pair[slot * extent : (slot + 1) * extent]
-                low = jnp.dot(backs[slot], down, preferred_element_type=jnp.float32)
+                entry = entry_of(place[0], slot, members)
+                low = jnp.dot(backs[entry], down, preferred_element_type=jnp.float32)
                 at = (slot - first) * rows
                 outs[slot][half] = (frozen[at : at + rows] + low).astype(jnp.bfloat16)
     for side in range(2):
         column = (place[0] ^ (side * pair_bit)) * value_width // lanes * lanes
         for slot in range(members):
-            columns[side][slot] = gradients[slot][0, :, pl.ds(pl.multiple_of(column, lanes), lanes)]
+            entry = entry_of(place[0], slot, members)
+            columns[side][entry] = gradients[slot][0, :, pl.ds(pl.multiple_of(column, lanes), lanes)]
 
 
 def input_slices(adapters, place, gradients, backs, weight, pair, down_maps):
@@ -198,9 +243,10 @@
     extent = downs[0].shape[1]
     across = (((1,), (1,)), ((), ()))
     for slot in range(members):
-        own[slot] = tokens[slot][0]
-        other[slot] = tokens[slot][1]
-        parts[slot] = lax.dot_general(
+        entry = entry_of(place[0], slot, members)
+        own[entry] = tokens[slot][0]
+        other[entry] = tokens[slot][1]
+        parts[entry] = lax.dot_general(
             tokens[slot][0], downs[slot][0], across, preferred_element_type=jnp.float32
         ) + lax.dot_general(
             tokens[slot][1],
@@ -231,19 +277,24 @@
     )
 
 
-def hidden_low_kernel(adapters, place, ranks, kept, received, out):
+def hidden_low_kernel(adapters, place, ranks, parts, out):
     alive, _ = rank_row(ranks, adapters[place[0]], out.shape[2])
-    out[0] = ((kept[0] + received[0]) * alive).astype(out.dtype)
-
-
-def hidden_rows(adapters, place, ranks, kept, received):
+    total = parts[0]
+    for line in range(1, parts.shape[0]):
+        total += parts[line]
+    low = (total * alive).astype(out.dtype)
+    for line in range(out.shape[0]):
+        out[line] = low
+
+
+def hidden_rows(adapters, place, ranks, parts):
     return call(
         hidden_low_kernel,
         "hidden_low",
         (adapters, place, ranks),
-        (kept, received),
-        [whole(kept.shape)] * 2,
-        [jax.ShapeDtypeStruct(kept.shape, jnp.bfloat16)],
+        (parts,),
+        [whole(parts.shape)],
+        [jax.ShapeDtypeStruct(parts.shape, jnp.bfloat16)],
     )[0]
 
 
@@ -262,10 +313,7 @@
                     sems.at[2 * entry + half],
                 )
             )
-    for copy in copies:
-        copy.start()
-    for copy in copies:
-        copy.wait()
+    run(copies)
 
 
 def join_columns(place, pieces, offsets, columns, before=None):
@@ -295,8 +343,8 @@
 
     lax.fori_loop(0, head.shape[0], clear, 0)
     for entry in reversed(range(2 * members)):
-        side, slot = divmod(entry, members)
-        adapter = adapters[place[0] ^ line_offset(slot, members) ^ (side * pair_bit)]
+        side, own = divmod(entry, members)
+        adapter = adapters[place_of(own, place[0], side, members)]
         following[entry] = head[adapter]
         head[adapter] = entry
 
@@ -442,6 +490,14 @@
     return lax.all_to_all(pieces, "dp", split_axis=0, concat_axis=0, tiled=True)
 
 
+def exchange_line(pieces):
+    lines = pieces.shape[0]
+    groups = [[line * line_bit + first for line in range(lines)] for first in range(line_bit)]
+    return lax.all_to_all(
+        pieces, "dp", split_axis=0, concat_axis=0, axis_index_groups=groups, tiled=True
+    )
+
+
 def swap(array, flip):
     devices = lax.axis_size("dp")
     return lax.ppermute(array, "dp", [(i, i ^ flip) for i in range(devices)])
@@ -451,25 +507,21 @@
     return lax.optimization_barrier((first, second))
 
 
-def gather_step(held, members):
-    arrived = swap(held, line_offset(held.shape[0], members))
-    return jnp.concatenate([held, arrived], axis=0)
-
-
-def reduce_step(parts, members):
-    half = parts.shape[0] // 2
-    return parts[:half], swap(parts[half:], line_offset(half, members))
+def both_cores(held):
+    return jnp.concatenate([held, swap(held, 1)], axis=0)
 
 
 def local(tokens, output_gradient, value_weight, down_maps, up_maps, adapter_per_block, ranks):
     devices = lax.axis_size("dp")
     members = devices // 2
+    lines = members // 2
     steps = members.bit_length() - 1
     num_adapters, extent, width = down_maps.shape
     rows, depth = output_gradient.shape
     place = lax.axis_index("dp").astype(jnp.int32).reshape(1)
     adapters = adapter_per_block
     offsets = [line_offset(slot, members) for slot in range(members)]
+    barrier = lax.optimization_barrier
 
     far = [slot for slot in range(members) if slot % 2]
     near = [slot for slot in range(2, members, 2)]
@@ -481,39 +533,36 @@
     def send(packs, portion):
         return {slot: swap(packs[slot], offsets[slot]) for slot in portion}
 
+    def taken(pieces, portion):
+        return [pieces[slot] for slot in portion]
+
     own_gradient = output_gradient.reshape(1, rows, depth)
     gradients = [own_gradient] + [None] * (members - 1)
     for step in range(steps):
         gradients[1 << step] = swap(own_gradient, offsets[1 << step])
     own_up = exchange(gather_up(adapters, up_maps)).reshape(depth, extent)
-    pair = swap(for_pair(adapters, place, value_weight, down_maps, members), pair_bit)
+    pair = for_pair(adapters, place, value_weight, down_maps, members)
+    gradients[2], pair = barrier((gradients[2], pair))
+    pair = swap(pair, pair_bit)
     packs = pack_tokens(place, tokens, members, width)
+    gradients[1], packs = barrier((gradients[1], packs))
     arrived = {0: packs[0]}
     arrived.update(send(packs, portions[0]))
-
-    first = [gradients[1 << step] for step in range(steps)]
-    first, own_up, packs = lax.optimization_barrier((first, own_up, packs))
-    for step in range(steps):
-        gradients[1 << step] = first[step]
-
-    backs = back_rows(adapters, place, ranks, output_gradient, own_up)
     for step in range(1, steps):
         for slot in range(1, 1 << step):
             gradients[slot + (1 << step)] = swap(gradients[slot], offsets[1 << step])
-        backs = gather_step(backs, members)
-        arrived.update(send(packs, portions[step]))
-        done = [arrived[slot] for slot in portions[step - 1]]
-        backs, gradients, packs, done = lax.optimization_barrier(
-            (backs, gradients, packs, done)
-        )
-        arrived.update(zip(portions[step - 1], done))
-        if step == 2:
-            break
-    for step in range(3, steps):
-        for slot in range(1, 1 << step):
-            gradients[slot + (1 << step)] = swap(gradients[slot], offsets[1 << step])
-        backs = gather_step(backs, members)
-    backs = gather_step(backs, members)
+    gradients[: members // 2], own_up, packs = barrier(
+        (gradients[: members // 2], own_up, packs)
+    )
+
+    backs = exchange_line(back_rows(adapters, place, ranks, output_gradient, own_up, lines))
+    arrived.update(send(packs, portions[1]))
+    backs, gradients, packs, done = barrier(
+        (backs, gradients, packs, taken(arrived, portions[0] + portions[1]))
+    )
+    arrived.update(zip(portions[0] + portions[1], done))
+    backs = both_cores(backs)
+    arrived.update(send(packs, portions[2]))
     arrived.update(send(packs, portions[3]))
 
     *slices, columns, columns_pair = input_slices(
@@ -522,54 +571,44 @@
     results = {0: slices[0]}
     results.update(send(slices, portions[0]))
     results.update(send(slices, portions[1]))
-
     columns_other = swap(columns_pair, pair_bit)
     backs_pair = swap(backs, pair_bit)
-    arrived = [arrived[slot] for slot in range(members)]
-    slices, arrived = lax.optimization_barrier((slices, arrived))
+    slices, arrived = barrier((slices, taken(arrived, range(members))))
     parts, tokens_own, tokens_pair = hidden_parts(adapters, place, down_maps, pair, arrived)
+    parts = parts[:lines] + swap(parts[lines:], 1)
+    parts, tokens_pair, columns_other, backs_pair = barrier(
+        (parts, tokens_pair, columns_other, backs_pair)
+    )
     tokens_other = swap(tokens_pair, pair_bit)
-    while parts.shape[0] > 2:
-        kept, received = reduce_step(parts, members)
-        parts = kept + received
-    done = [results[slot] for slot in portions[0]]
-    parts, done, columns_other, backs_pair, slices = lax.optimization_barrier(
-        (parts, done, columns_other, backs_pair, slices)
-    )
+    parts = exchange_line(parts)
+    parts, done, slices = barrier((parts, taken(results, portions[0]), slices))
     results.update(zip(portions[0], done))
     results.update(send(slices, portions[2]))
-    kept, received = reduce_step(parts, members)
-    done = [results[slot] for slot in portions[1]]
-    received, done, slices = lax.optimization_barrier((received, done, slices))
+
+    hiddens = exchange_line(hidden_rows(adapters, place, ranks, parts))
+    hiddens, done, slices = barrier((hiddens, taken(results, portions[1]), slices))
     results.update(zip(portions[1], done))
     results.update(send(slices, portions[3]))
-
-    hiddens = hidden_rows(adapters, place, ranks, kept, received)
-    hiddens = gather_step(gather_step(hiddens, members), members)
+    hiddens = both_cores(hiddens)
+    hiddens_pair = swap(hiddens, pair_bit)
     down_gradient = down_gradients(
         adapters, place, backs, backs_pair, tokens_own, tokens_other, num_adapters
     )
-    done = [results[slot] for slot in portions[2]]
-    hiddens, done, down_gradient = lax.optimization_barrier((hiddens, done, down_gradient))
+    hiddens_pair, done, down_gradient = barrier(
+        (hiddens_pair, taken(results, portions[2]), down_gradient)
+    )
     results.update(zip(portions[2], done))
-    while hiddens.shape[0] < members:
-        hiddens = gather_step(hiddens, members)
-    hiddens_pair = swap(hiddens, pair_bit)
     up_gradient = up_gradients(
         adapters, place, ranks, columns, columns_other, hiddens, hiddens_pair, depth // devices
     )
 
     def joined(slots, before=None):
         return join_columns(
-            place,
-            [results[slot] for slot in slots],
-            [offsets[slot] for slot in slots],
-            tokens.shape[1],
-            before,
+            place, taken(results, slots), taken(offsets, slots), tokens.shape[1], before
         )
 
     most = joined([0] + portions[0] + portions[1] + portions[2])
-    up_gradient, most = lax.optimization_barrier((up_gradient, most))
+    up_gradient, most = barrier((up_gradient, most))
     input_grad = joined(portions[3], most)
     return (input_grad, down_gradient, up_gradient)
 

time: 195 us -> 230 us (1.18)
  Pallas kernels: 27.5 us -> 67.9 us
  waiting for transfers between devices: 114 us -> 101 us
  local copies, waits for them, and re-layouts: 6.24 us -> 10.5 us
    pallas_call x0 -> x3, Pallas kernels: none -> 35.6 us  [copy_call(): pl.pallas_call(kernel, out_shape=out_shapes, grid_spec=pltpu.PrefetchScal...]
    ppermute x35 -> x29, waiting for transfers between devices: 99.4 us -> 64.3 us  [swap(): return lax.ppermute(array, 'dp', [(i, i ^ flip) for i in range(devices)])]
    all_to_all x0 -> x3, waiting for transfers between devices: none -> 13.9 us  [exchange_line(): lax.all_to_all(pieces, 'dp', split_axis=0, concat_axis=0, axis_index_grou...]
    all_to_all x0 -> x3, starting transfers between devices: none -> 10.1 us  [exchange_line(): lax.all_to_all(pieces, 'dp', split_axis=0, concat_axis=0, axis_index_grou...]
    all_to_all x1, waiting for transfers between devices: 14.6 us -> 22.7 us  [exchange(): return lax.all_to_all(pieces, 'dp', split_axis=0, concat_axis=0, tiled=True)]
    pallas_call x2, Pallas kernels: 2.05 us -> 10.1 us  [join_columns(): pl.pallas_call(functools.partial(join_kernel, offsets=offsets, aliased=le...]
    ppermute x35 -> x29, starting transfers between devices: 40.9 us -> 33.1 us  [swap(): return lax.ppermute(array, 'dp', [(i, i ^ flip) for i in range(devices)])]
    unnamed x30 -> x58, local copies, waits for them, and re-layouts: 6.16 us -> 10.4 us
  transfers between devices with their start and end apart: 36 -> 33, of which waited for: 20 -> 13; matrix products, arithmetic and copies ran while one was open for 0% -> 0% of each run, Pallas kernels for 10% -> 28%
where the time goes in v6:
time: 230 us; the launch traced here: 228 us
  waiting for transfers between devices  101 us (44%)
  Pallas kernels  67.9 us (30%)
  starting transfers between devices  47.5 us (21%)
  local copies, waits for them, and re-layouts  10.5 us (5%)
    ppermute x29, waiting for transfers between devices, swap(): return lax.ppermute(array, 'dp', [(i, i ^ flip) for i in range(devices)])  64.3 us
    pallas_call x3, Pallas kernels, copy_call(): pl.pallas_call(kernel, out_shape=out_shapes, grid_spec=pltpu.PrefetchScal...  35.6 us
    ppermute x29, starting transfers between devices, swap(): return lax.ppermute(array, 'dp', [(i, i ^ flip) for i in range(devices)])  33.1 us
    all_to_all x1, waiting for transfers between devices, exchange(): return lax.all_to_all(pieces, 'dp', split_axis=0, concat_axis=0, tiled=True)  22.7 us
    all_to_all x3, waiting for transfers between devices, exchange_line(): lax.all_to_all(pieces, 'dp', split_axis=0, concat_axis=0, axis_index_grou...  13.9 us
    pallas_call x4, Pallas kernels, call(): pl.pallas_call(kernel, out_shape=out_shapes, grid_spec=pltpu.PrefetchScal...  13.2 us
    unnamed x58, local copies, waits for them, and re-layouts  10.4 us
    pallas_call x2, Pallas kernels, join_columns(): pl.pallas_call(functools.partial(join_kernel, offsets=offsets, aliased=le...  10.1 us
  transfers between devices with their start and end apart: 33, of which 13 were waited for; matrix products, arithmetic and copies ran while one was open for 0% of the time, Pallas kernels for 28%

profile of v6, /device:TPU:0, one launch (start us, length us, event | category | flops | bytes accessed | tf_op | source)
XLA Modules:
  0.0 228.3 jit_solution(16255508626864189831)
XLA Ops:
  0.6 3.1 %collective-permute-start = (bf16[1,128,1024]{2,1,0:T(8,128)(2,1)}, bf16[1,128,1024]{2,1,0:T(8,128)(2,1)}, u32[]{:S(2)}, u32[]{:S(2)}) collective-permute-start(bf16[1,128,1024]{2,1,0:T(8,128)(2,1)} %bitcast.3), channel_id=1, source_target_pairs={{0,4},{1,5},{2,6},{3,7},{4,0},{5,1},{6,2},{7,3},{8,12},{9,13},{10,... | collective-permute-start | bytes 786440 | tf_op jit(solution)/shard_map/ppermute | solution.py:503
  3.7 1.2 copy-done
  5.6 33.6 %for_pair.1 = bf16[2048,512]{1,0:T(8,128)(2,1)} custom-call(s32[16]{0:T(128)S(1)} %copy-done.12, s32[1]{0:T(128)} %bitcast.place, bf16[1024,512]{1,0:T(8,128)(2,1)S(1)} %copy-done, bf16[64,128,512]{2,1,0:T(8,128)(2,1)} %refs_7_.1), custom_call_target="tpu_custom_call" | custom-call | tf_op jit(solution)/shard_map/for_pair/pallas_call | solution.py:75
  39.2 1.6 collective-permute-start.1
  40.8 2.6 %collective-permute-start.2 = (bf16[1,128,1024]{2,1,0:T(8,128)(2,1)S(1)}, bf16[1,128,1024]{2,1,0:T(8,128)(2,1)}, u32[]{:S(2)}, u32[]{:S(2)}) collective-permute-start(bf16[1,128,1024]{2,1,0:T(8,128)(2,1)S(1)} %bitcast.4), channel_id=1, source_target_pairs={{0,8},{1,9},{2,10},{3,11},{4,12},{5,13},{6,14},{7,15},{8,0},{9,1},... | collective-permute-start | bytes 786440 | tf_op jit(solution)/shard_map/ppermute | solution.py:503
  43.4 1.1 gather_up.1
  45.2 4.3 %all-to-all-start = ((bf16[16,64,128]{2,1,0:T(8,128)(2,1)}), bf16[16,64,128]{2,1,0:T(8,128)(2,1)}, u32[]{:S(2)}, u32[]{:S(2)}) async-start(bf16[16,64,128]{2,1,0:T(8,128)(2,1)} %copy-done.4), calls=%async_computation | async-start | bytes 524288 | tf_op jit(solution)/shard_map/all_to_all | solution.py:490
  49.5 0.9 pack_tokens.1
  55.4 1.2 collective-permute-done.2.refs_1_
  56.6 1.8 collective-permute-start.3
  59.0 6.2 %collective-permute-done.3.refs_3_ = bf16[1,128,1024]{2,1,0:T(8,128)(2,1)S(1)} collective-permute-done((bf16[1,128,1024]{2,1,0:T(8,128)(2,1)}, bf16[1,128,1024]{2,1,0:T(8,128)(2,1)S(1)}, u32[]{:S(2)}, u32[]{:S(2)}) %collective-permute-start.3) | collective-permute-done | bytes 262176 | tf_op jit(solution)/shard_map/ppermute | solution.py:503
  65.2 1.5 collective-permute-start.8
  66.6 22.7 %all-to-all-done = bf16[16,64,128]{2,1,0:T(8,128)(2,1)} async-done(((bf16[16,64,128]{2,1,0:T(8,128)(2,1)}), bf16[16,64,128]{2,1,0:T(8,128)(2,1)}, u32[]{:S(2)}, u32[]{:S(2)}) %all-to-all-start) | async-done | bytes 262176 | tf_op jit(solution)/shard_map/all_to_all | solution.py:490
  89.3 2.5 %collective-permute-start.9 = (bf16[2,128,512]{2,1,0:T(8,128)(2,1)}, bf16[2,128,512]{2,1,0:T(8,128)(2,1)S(1)}, u32[]{:S(2)}, u32[]{:S(2)}) collective-permute-start(bf16[2,128,512]{2,1,0:T(8,128)(2,1)} %copy-done.27), channel_id=1, source_target_pairs={{0,12},{1,13},{2,14},{3,15},{4,8},{5,9},{6,10},{7,11},{8,4},{9,5},... | collective-permute-start | bytes 786440 | tf_op jit(solution)/shard_map/ppermute | solution.py:503
  91.8 2.4 %back_low.1 = bf16[4,128,128]{2,1,0:T(8,128)(2,1)} custom-call(s32[16]{0:T(128)S(1)} %copy-done.13, s32[1]{0:T(128)} %bitcast.place, s32[64]{0:T(128)S(1)} %copy-done.14, bf16[128,1024]{1,0:T(8,128)(2,1)S(1)} %copy-done.3, bf16[1024,128]{1,0:T(8,128)(2,1)} %bitcast.2.up), custom_call_target="tpu_custom_call" | custom-call | tf_op jit(solution)/shard_map/back_low/pallas_call | solution.py:51
  94.2 3.3 %all-to-all-start.1 = ((bf16[4,128,128]{2,1,0:T(8,128)(2,1)}), bf16[4,128,128]{2,1,0:T(8,128)(2,1)S(1)}, u32[]{:S(2)}, u32[]{:S(2)}) async-start(bf16[4,128,128]{2,1,0:T(8,128)(2,1)} %back_low.1), calls=%async_computation.1 | async-start | bytes 262144 | tf_op jit(solution)/shard_map/all_to_all | solution.py:496
  97.5 9.6 %all-to-all-done.1 = bf16[4,128,128]{2,1,0:T(8,128)(2,1)S(1)} async-done(((bf16[4,128,128]{2,1,0:T(8,128)(2,1)}), bf16[4,128,128]{2,1,0:T(8,128)(2,1)S(1)}, u32[]{:S(2)}, u32[]{:S(2)}) %all-to-all-start.1) | async-done | bytes 131104 | tf_op jit(solution)/shard_map/all_to_all | solution.py:496
  107.7 2.9 %collective-permute-start.13 = (bf16[2,128,512]{2,1,0:T(8,128)(2,1)}, bf16[2,128,512]{2,1,0:T(8,128)(2,1)S(1)}, u32[]{:S(2)}, u32[]{:S(2)}) collective-permute-start(bf16[2,128,512]{2,1,0:T(8,128)(2,1)} %copy-done.22), channel_id=1, source_target_pairs={{0,9},{1,8},{2,11},{3,10},{4,13},{5,12},{6,15},{7,14},{8,1},{9,0},... | collective-permute-start | bytes 786440 | tf_op jit(solution)/shard_map/ppermute | solution.py:503
  110.6 1.2 collective-permute-start.15
  111.8 5.5 %input_slices.1 = (bf16[2,128,512]{2,1,0:T(8,128)(2,1)S(1)}, bf16[2,128,512]{2,1,0:T(8,128)(2,1)S(1)}, bf16[2,128,512]{2,1,0:T(8,128)(2,1)S(1)}, bf16[2,128,512]...) custom-call(s32[16]{0:T(128)S(1)} %copy-done.13, ...), custom_call_target="tpu_custom_call" | custom-call | tf_op jit(solution)/shard_map/input_slices/pallas_call | solution.py:51
  118.7 0.7 copy-done.25
  120.2 1.4 collective-permute-done.11.refs_10_
  121.6 1.3 collective-permute-done.13.refs_13_
  122.8 4.0 %collective-permute-done.14.refs_14_ = bf16[2,128,512]{2,1,0:T(8,128)(2,1)S(1)} collective-permute-done((bf16[2,128,512]{2,1,0:T(8,128)(2,1)}, bf16[2,128,512]{2,1,0:T(8,128)(2,1)S(1)}, u32[]{:S(2)}, u32[]{:S(2)}) %collective-permute-start.14) | collective-permute-done | bytes 262176 | tf_op jit(solution)/shard_map/ppermute | solution.py:503
  126.8 6.7 %collective-permute-done.15.refs_15_ = bf16[2,128,512]{2,1,0:T(8,128)(2,1)S(1)} collective-permute-done((bf16[2,128,512]{2,1,0:T(8,128)(2,1)}, bf16[2,128,512]{2,1,0:T(8,128)(2,1)S(1)}, u32[]{:S(2)}, u32[]{:S(2)}) %collective-permute-start.15) | collective-permute-done | bytes 262176 | tf_op jit(solution)/shard_map/ppermute | solution.py:503
  133.6 4.1 %hidden_parts.1 = (f32[8,128,128]{2,1,0:T(8,128)S(1)}, bf16[8,128,512]{2,1,0:T(8,128)(2,1)S(1)}, bf16[8,128,512]{2,1,0:T(8,128)(2,1)}) custom-call(s32[16]{0:T(128)S(1)} %copy-done.13, s32[1]{0:T(128)} %bitcast.place, bf16[2048,512]{1,0:T(8,128)(2,1)} %collective-permute-done.1.pair, bf16[64,128,512]{2,1,0:T(8,128)(2,1)} %refs_7_.1, ...), custom_call_target="tpu_custom_call" | custom-call | tf_op jit(solution)/shard_map/hidden_parts/pallas_call | solution.py:51
  138.0 1.3 collective-permute-start.18
  140.0 0.7 slice_add_fusion
  140.8 6.4 %collective-permute-done.18.backs_pair = bf16[8,128,128]{2,1,0:T(8,128)(2,1)S(1)} collective-permute-done((bf16[8,128,128]{2,1,0:T(8,128)(2,1)S(1)}, bf16[8,128,128]{2,1,0:T(8,128)(2,1)S(1)}, u32[]{:S(2)}, u32[]{:S(2)}) %collective-permute-start.18) | collective-permute-done | bytes 262176 | tf_op jit(solution)/shard_map/ppermute | solution.py:503
  147.1 5.0 %collective-permute-done.17.gradients_pair = bf16[8,128,128]{2,1,0:T(8,128)(2,1)S(1)} collective-permute-done((bf16[8,128,128]{2,1,0:T(8,128)(2,1)S(1)}, bf16[8,128,128]{2,1,0:T(8,128)(2,1)S(1)}, u32[]{:S(2)}, u32[]{:S(2)}) %collective-permute-start.17) | collective-permute-done | bytes 262176 | tf_op jit(solution)/shard_map/ppermute | solution.py:503
  152.1 1.3 collective-permute-start.28
  153.5 3.4 %all-to-all-start.2 = ((f32[4,128,128]{2,1,0:T(8,128)}), f32[4,128,128]{2,1,0:T(8,128)S(1)}, u32[]{:S(2)}, u32[]{:S(2)}) async-start(f32[4,128,128]{2,1,0:T(8,128)} %slice_add_fusion), calls=%async_computation.2 | async-start | bytes 524288 | tf_op jit(solution)/shard_map/all_to_all | solution.py:496
  156.9 2.9 %collective-permute-start.19 = (bf16[2,128,512]{2,1,0:T(8,128)(2,1)}, bf16[2,128,512]{2,1,0:T(8,128)(2,1)S(1)}, u32[]{:S(2)}, u32[]{:S(2)}) collective-permute-start(bf16[2,128,512]{2,1,0:T(8,128)(2,1)} %copy-done.26), channel_id=1, source_target_pairs={{0,8},{1,9},{2,10},{3,11},{4,12},{5,13},{6,14},{7,15},{8,0},{9,1},... | collective-permute-start | bytes 786440 | tf_op jit(solution)/shard_map/ppermute | solution.py:503
  159.8 1.5 collective-permute-start.20
  161.2 22.1 %collective-permute-done.19.refs_1_ = bf16[2,128,512]{2,1,0:T(8,128)(2,1)S(1)} collective-permute-done((bf16[2,128,512]{2,1,0:T(8,128)(2,1)}, bf16[2,128,512]{2,1,0:T(8,128)(2,1)S(1)}, u32[]{:S(2)}, u32[]{:S(2)}) %collective-permute-start.19) | collective-permute-done | bytes 262176 | tf_op jit(solution)/shard_map/ppermute | solution.py:503
  183.4 1.2 hidden_low.1
  184.6 3.3 %all-to-all-start.3 = ((bf16[4,128,128]{2,1,0:T(8,128)(2,1)}), bf16[4,128,128]{2,1,0:T(8,128)(2,1)S(1)}, u32[]{:S(2)}, u32[]{:S(2)}) async-start(bf16[4,128,128]{2,1,0:T(8,128)(2,1)} %hidden_low.1), calls=%async_computation.3 | async-start | bytes 262144 | tf_op jit(solution)/shard_map/all_to_all | solution.py:496
  187.9 2.0 collective-permute-start.27
  189.9 4.3 %all-to-all-done.3 = bf16[4,128,128]{2,1,0:T(8,128)(2,1)S(1)} async-done(((bf16[4,128,128]{2,1,0:T(8,128)(2,1)}), bf16[4,128,128]{2,1,0:T(8,128)(2,1)S(1)}, u32[]{:S(2)}, u32[]{:S(2)}) %all-to-all-start.3) | async-done | bytes 131104 | tf_op jit(solution)/shard_map/all_to_all | solution.py:496
  194.2 1.4 collective-permute-start.26
  195.6 0.7 collective-permute-start.25
  196.4 2.0 collective-permute-start.21
  198.4 0.8 collective-permute-start.22
  199.2 5.5 %down_gradients.1 = bf16[64,128,512]{2,1,0:T(8,128)(2,1)} custom-call(s32[16]{0:T(128)S(1)} %copy-done.13, s32[1]{0:T(128)} %bitcast.place, bf16[8,128,128]{2,1,0:T(8,128)(2,1)S(1)} %constant_dynamic-update-slice_fusion.backs, bf16[8,128,128]{2,1,0:T(8,128)(2,1)S(1)} %collective-permute-done.18.backs_pair, bf16[8,128,512]{2,1,0:T(8,128)(2,1)S(1)} %get-tuple-element.181.own, ...), custom_call_target="tpu_custom_call" | custom-call | tf_op jit(solution)/shard_map/down_gradients/pallas_call | solution.py:391
  204.7 9.9 %collective-permute-done.26.refs_3_ = bf16[2,128,512]{2,1,0:T(8,128)(2,1)S(1)} collective-permute-done((bf16[2,128,512]{2,1,0:T(8,128)(2,1)}, bf16[2,128,512]{2,1,0:T(8,128)(2,1)S(1)}, u32[]{:S(2)}, u32[]{:S(2)}) %collective-permute-start.26) | collective-permute-done | bytes 262176 | tf_op jit(solution)/shard_map/ppermute | solution.py:503
  214.6 3.6 %up_gradients.1 = bf16[64,64,128]{2,1,0:T(8,128)(2,1)} custom-call(s32[16]{0:T(128)S(1)} %copy-done.13, s32[1]{0:T(128)} %bitcast.place, s32[64]{0:T(128)S(1)} %copy-done.14, bf16[8,128,128]{2,1,0:T(8,128)(2,1)S(1)} %copy-done.11, bf16[8,128,128]{2,1,0:T(8,128)(2,1)S(1)} %collective-permute-done.17.gradients_pair, ...), custom_call_target="tpu_custom_call" | custom-call | tf_op jit(solution)/shard_map/up_gradients/pallas_call | solution.py:391
  218.2 9.2 %join_columns.2.refs_3_ = bf16[128,8192]{1,0:T(8,128)(2,1)} custom-call(s32[1]{0:T(128)} %bitcast.place, bf16[2,128,512]{2,1,0:T(8,128)(2,1)S(1)} %copy-done.9, bf16[2,128,512]{2,1,0:T(8,128)(2,1)S(1)} %collective-permute-done.19.refs_1_, bf16[2,128,512]{2,1,0:T(8,128)(2,1)} %collective-permute-done.20.refs_2_, ...), custom_call_target="tpu_custom_call" | custom-call | tf_op jit(solution)/shard_map/join_columns/pallas_call | solution.py:323
  227.4 0.9 join_columns.3
  (91 shorter events, 10.6 us)
Async XLA Ops:
  0.6 38.6 %collective-permute-start = (bf16[1,128,1024]{2,1,0:T(8,128)(2,1)}, bf16[1,128,1024]{2,1,0:T(8,128)(2,1)}, u32[]{:S(2)}, u32[]{:S(2)}) collective-permute-start(bf16[1,128,1024]{2,1,0:T(8,128)(2,1)} %bitcast.3), channel_id=1, source_target_pairs={{0,4},{1,5},{2,6},{3,7},{4,0},{5,1},{6,2},{7,3},{8,12},{9,13},{10,... | collective-permute-start | bytes 786440 | tf_op jit(solution)/shard_map/ppermute | solution.py:503
  3.7 1.2 copy-start
  5.6 35.2 %copy-start.3 = (bf16[128,1024]{1,0:T(8,128)(2,1)S(1)}, bf16[128,1024]{1,0:T(8,128)(2,1)}, u32[]{:S(2)}) copy-start(bf16[128,1024]{1,0:T(8,128)(2,1)} %gradient.1) | copy-start | bytes 786436
  5.6 37.8 %copy-start.5 = (bf16[64,64,128]{2,1,0:T(8,128)(2,1)S(1)}, bf16[64,64,128]{2,1,0:T(8,128)(2,1)}, u32[]{:S(2)}) copy-start(bf16[64,64,128]{2,1,0:T(8,128)(2,1)} %up_maps.1) | copy-start | bytes 3145732
  5.6 43.9 %copy-start.2 = (bf16[128,8192]{1,0:T(8,128)(2,1)S(1)}, bf16[128,8192]{1,0:T(8,128)(2,1)}, u32[]{:S(2)}) copy-start(bf16[128,8192]{1,0:T(8,128)(2,1)} %tokens.1) | copy-start | bytes 6291460
  39.2 52.6 %copy-start.13 = (s32[16]{0:T(128)S(1)}, s32[16]{0:T(128)}, u32[]{:S(2)}) copy-start(s32[16]{0:T(128)} %adapters.15) | copy-start | bytes 196
  39.2 52.6 %copy-start.14 = (s32[64]{0:T(128)S(1)}, s32[64]{0:T(128)}, u32[]{:S(2)}) copy-start(s32[64]{0:T(128)} %ranks.5) | copy-start | bytes 772
  39.2 71.4 %collective-permute-start.1 = (bf16[2048,512]{1,0:T(8,128)(2,1)}, bf16[2048,512]{1,0:T(8,128)(2,1)}, u32[]{:S(2)}, u32[]{:S(2)}) collective-permute-start(bf16[2048,512]{1,0:T(8,128)(2,1)} %for_pair.1), channel_id=1, source_target_pairs={{0,2},{1,3},{2,0},{3,1},{4,6},{5,7},{6,4},{7,5},{8,10},{9,11},{10,... | collective-permute-start | bytes 6291464 | tf_op jit(solution)/shard_map/ppermute | solution.py:503
  40.8 15.8 %collective-permute-start.2 = (bf16[1,128,1024]{2,1,0:T(8,128)(2,1)S(1)}, bf16[1,128,1024]{2,1,0:T(8,128)(2,1)}, u32[]{:S(2)}, u32[]{:S(2)}) collective-permute-start(bf16[1,128,1024]{2,1,0:T(8,128)(2,1)S(1)} %bitcast.4), channel_id=1, source_target_pairs={{0,8},{1,9},{2,10},{3,11},{4,12},{5,13},{6,14},{7,15},{8,0},{9,1},... | collective-permute-start | bytes 786440 | tf_op jit(solution)/shard_map/ppermute | solution.py:503
  45.2 66.6 %copy-start.1 = (bf16[1024,512]{1,0:T(8,128)(2,1)S(1)}, bf16[1024,512]{1,0:T(8,128)(2,1)}, u32[]{:S(2)}) copy-start(bf16[1024,512]{1,0:T(8,128)(2,1)} %refs_16_.1) | copy-start | bytes 3145732
  45.2 44.1 %all-to-all-start = ((bf16[16,64,128]{2,1,0:T(8,128)(2,1)}), bf16[16,64,128]{2,1,0:T(8,128)(2,1)}, u32[]{:S(2)}, u32[]{:S(2)}) async-start(bf16[16,64,128]{2,1,0:T(8,128)(2,1)} %copy-done.4), calls=%async_computation | async-start | bytes 524288 | tf_op jit(solution)/shard_map/all_to_all | solution.py:490
  56.6 8.6 %collective-permute-start.3 = (bf16[1,128,1024]{2,1,0:T(8,128)(2,1)}, bf16[1,128,1024]{2,1,0:T(8,128)(2,1)S(1)}, u32[]{:S(2)}, u32[]{:S(2)}) collective-permute-start(bf16[1,128,1024]{2,1,0:T(8,128)(2,1)} %collective-permute-done.2.refs_1_), channel_id=1, source_target_pairs={{0,4},{1,5},{2,6},{3,7},{4,0},{5,1},{6,2},{7,3},{8,12},{9,13},{10,... | collective-permute-start | bytes 786440 | tf_op jit(solution)/shard_map/ppermute | solution.py:503
  58.4 30.9 %collective-permute-start.4 = (bf16[1,128,1024]{2,1,0:T(8,128)(2,1)S(1)}, bf16[1,128,1024]{2,1,0:T(8,128)(2,1)S(1)}, u32[]{:S(2)}, u32[]{:S(2)}) collective-permute-start(bf16[1,128,1024]{2,1,0:T(8,128)(2,1)S(1)} %bitcast.5), channel_id=1, source_target_pairs={{0,1},{1,0},{2,3},{3,2},{4,5},{5,4},{6,7},{7,6},{8,9},{9,8},{10,11... | collective-permute-start | bytes 786440 | tf_op jit(solution)/shard_map/ppermute | solution.py:503
  58.4 33.4 %collective-permute-start.6 = (bf16[1,128,1024]{2,1,0:T(8,128)(2,1)}, bf16[1,128,1024]{2,1,0:T(8,128)(2,1)S(1)}, u32[]{:S(2)}, u32[]{:S(2)}) collective-permute-start(bf16[1,128,1024]{2,1,0:T(8,128)(2,1)} %collective-permute-done.refs_2_), channel_id=1, source_target_pairs={{0,1},{1,0},{2,3},{3,2},{4,5},{5,4},{6,7},{7,6},{8,9},{9,8},{10,11... | collective-permute-start | bytes 786440 | tf_op jit(solution)/shard_map/ppermute | solution.py:503
  59.0 38.6 %collective-permute-start.5 = (bf16[1,128,1024]{2,1,0:T(8,128)(2,1)}, bf16[1,128,1024]{2,1,0:T(8,128)(2,1)S(1)}, u32[]{:S(2)}, u32[]{:S(2)}) collective-permute-start(bf16[1,128,1024]{2,1,0:T(8,128)(2,1)} %collective-permute-done.2.refs_1_), channel_id=1, source_target_pairs={{0,1},{1,0},{2,3},{3,2},{4,5},{5,4},{6,7},{7,6},{8,9},{9,8},{10,11... | collective-permute-start | bytes 786440 | tf_op jit(solution)/shard_map/ppermute | solution.py:503
  65.2 32.3 %collective-permute-start.8 = (bf16[2,128,512]{2,1,0:T(8,128)(2,1)}, bf16[2,128,512]{2,1,0:T(8,128)(2,1)S(1)}, u32[]{:S(2)}, u32[]{:S(2)}) collective-permute-start(bf16[2,128,512]{2,1,0:T(8,128)(2,1)} %get-tuple-element.109), channel_id=1, source_target_pairs={{0,8},{1,9},{2,10},{3,11},{4,12},{5,13},{6,14},{7,15},{8,0},{9,1},... | collective-permute-start | bytes 786440 | tf_op jit(solution)/shard_map/ppermute | solution.py:503
  89.3 17.8 %collective-permute-start.9 = (bf16[2,128,512]{2,1,0:T(8,128)(2,1)}, bf16[2,128,512]{2,1,0:T(8,128)(2,1)S(1)}, u32[]{:S(2)}, u32[]{:S(2)}) collective-permute-start(bf16[2,128,512]{2,1,0:T(8,128)(2,1)} %copy-done.27), channel_id=1, source_target_pairs={{0,12},{1,13},{2,14},{3,15},{4,8},{5,9},{6,10},{7,11},{8,4},{9,5},... | collective-permute-start | bytes 786440 | tf_op jit(solution)/shard_map/ppermute | solution.py:503
  91.8 15.3 %collective-permute-start.7 = (bf16[1,128,1024]{2,1,0:T(8,128)(2,1)S(1)}, bf16[1,128,1024]{2,1,0:T(8,128)(2,1)S(1)}, u32[]{:S(2)}, u32[]{:S(2)}) collective-permute-start(bf16[1,128,1024]{2,1,0:T(8,128)(2,1)S(1)} %collective-permute-done.3.refs_3_), channel_id=1, source_target_pairs={{0,1},{1,0},{2,3},{3,2},{4,5},{5,4},{6,7},{7,6},{8,9},{9,8},{10,11... | collective-permute-start | bytes 786440 | tf_op jit(solution)/shard_map/ppermute | solution.py:503
  94.2 12.9 %all-to-all-start.1 = ((bf16[4,128,128]{2,1,0:T(8,128)(2,1)}), bf16[4,128,128]{2,1,0:T(8,128)(2,1)S(1)}, u32[]{:S(2)}, u32[]{:S(2)}) async-start(bf16[4,128,128]{2,1,0:T(8,128)(2,1)} %back_low.1), calls=%async_computation.1 | async-start | bytes 262144 | tf_op jit(solution)/shard_map/all_to_all | solution.py:496
  107.1 3.4 %collective-permute-start.10 = (bf16[4,128,128]{2,1,0:T(8,128)(2,1)S(1)}, bf16[4,128,128]{2,1,0:T(8,128)(2,1)S(1)}, u32[]{:S(2)}, u32[]{:S(2)}) collective-permute-start(bf16[4,128,128]{2,1,0:T(8,128)(2,1)S(1)} %all-to-all-done.1), channel_id=1, source_target_pairs={{0,1},{1,0},{2,3},{3,2},{4,5},{5,4},{6,7},{7,6},{8,9},{9,8},{10,11... | collective-permute-start | bytes 393224 | tf_op jit(solution)/shard_map/ppermute | solution.py:503
  107.1 14.4 %collective-permute-start.11 = (bf16[2,128,512]{2,1,0:T(8,128)(2,1)}, bf16[2,128,512]{2,1,0:T(8,128)(2,1)S(1)}, u32[]{:S(2)}, u32[]{:S(2)}) collective-permute-start(bf16[2,128,512]{2,1,0:T(8,128)(2,1)} %copy-done.24), channel_id=1, source_target_pairs={{0,4},{1,5},{2,6},{3,7},{4,0},{5,1},{6,2},{7,3},{8,12},{9,13},{10,... | collective-permute-start | bytes 786440 | tf_op jit(solution)/shard_map/ppermute | solution.py:503
  107.4 14.1 %collective-permute-start.12 = (bf16[2,128,512]{2,1,0:T(8,128)(2,1)}, bf16[2,128,512]{2,1,0:T(8,128)(2,1)S(1)}, u32[]{:S(2)}, u32[]{:S(2)}) collective-permute-start(bf16[2,128,512]{2,1,0:T(8,128)(2,1)} %copy-done.23), channel_id=1, source_target_pairs={{0,1},{1,0},{2,3},{3,2},{4,5},{5,4},{6,7},{7,6},{8,9},{9,8},{10,11... | collective-permute-start | bytes 786440 | tf_op jit(solution)/shard_map/ppermute | solution.py:503
  107.7 15.2 %collective-permute-start.13 = (bf16[2,128,512]{2,1,0:T(8,128)(2,1)}, bf16[2,128,512]{2,1,0:T(8,128)(2,1)S(1)}, u32[]{:S(2)}, u32[]{:S(2)}) collective-permute-start(bf16[2,128,512]{2,1,0:T(8,128)(2,1)} %copy-done.22), channel_id=1, source_target_pairs={{0,9},{1,8},{2,11},{3,10},{4,13},{5,12},{6,15},{7,14},{8,1},{9,0},... | collective-permute-start | bytes 786440 | tf_op jit(solution)/shard_map/ppermute | solution.py:503
  110.5 16.3 %collective-permute-start.14 = (bf16[2,128,512]{2,1,0:T(8,128)(2,1)}, bf16[2,128,512]{2,1,0:T(8,128)(2,1)S(1)}, u32[]{:S(2)}, u32[]{:S(2)}) collective-permute-start(bf16[2,128,512]{2,1,0:T(8,128)(2,1)} %copy-done.21), channel_id=1, source_target_pairs={{0,5},{1,4},{2,7},{3,6},{4,1},{5,0},{6,3},{7,2},{8,13},{9,12},{10,... | collective-permute-start | bytes 786440 | tf_op jit(solution)/shard_map/ppermute | solution.py:503
  110.6 23.0 %collective-permute-start.15 = (bf16[2,128,512]{2,1,0:T(8,128)(2,1)}, bf16[2,128,512]{2,1,0:T(8,128)(2,1)S(1)}, u32[]{:S(2)}, u32[]{:S(2)}) collective-permute-start(bf16[2,128,512]{2,1,0:T(8,128)(2,1)} %copy-done.20), channel_id=1, source_target_pairs={{0,13},{1,12},{2,15},{3,14},{4,9},{5,8},{6,11},{7,10},{8,5},{9,4},... | collective-permute-start | bytes 786440 | tf_op jit(solution)/shard_map/ppermute | solution.py:503
  111.8 21.8 %copy-start.7 = (bf16[2,128,512]{2,1,0:T(8,128)(2,1)S(1)}, bf16[2,128,512]{2,1,0:T(8,128)(2,1)}, u32[]{:S(2)}) copy-start(bf16[2,128,512]{2,1,0:T(8,128)(2,1)} %copy-done.6) | copy-start | bytes 786436
  120.2 13.4 %copy-start.16 = (bf16[2,128,512]{2,1,0:T(8,128)(2,1)}, bf16[2,128,512]{2,1,0:T(8,128)(2,1)S(1)}, u32[]{:S(2)}) copy-start(bf16[2,128,512]{2,1,0:T(8,128)(2,1)S(1)} %get-tuple-element.175) | copy-start | bytes 786436
  120.2 17.5 %copy-start.10 = (bf16[8,128,128]{2,1,0:T(8,128)(2,1)}, bf16[8,128,128]{2,1,0:T(8,128)(2,1)S(1)}, u32[]{:S(2)}) copy-start(bf16[8,128,128]{2,1,0:T(8,128)(2,1)S(1)} %get-tuple-element.177.gradients) | copy-start | bytes 786436
  120.2 17.5 %copy-start.15 = (bf16[2,128,512]{2,1,0:T(8,128)(2,1)}, bf16[2,128,512]{2,1,0:T(8,128)(2,1)S(1)}, u32[]{:S(2)}) copy-start(bf16[2,128,512]{2,1,0:T(8,128)(2,1)S(1)} %get-tuple-element.176) | copy-start | bytes 786436
  120.2 17.5 %copy-start.17 = (bf16[2,128,512]{2,1,0:T(8,128)(2,1)}, bf16[2,128,512]{2,1,0:T(8,128)(2,1)S(1)}, u32[]{:S(2)}) copy-start(bf16[2,128,512]{2,1,0:T(8,128)(2,1)S(1)} %get-tuple-element.174) | copy-start | bytes 786436
  120.2 17.5 %copy-start.18 = (bf16[2,128,512]{2,1,0:T(8,128)(2,1)}, bf16[2,128,512]{2,1,0:T(8,128)(2,1)S(1)}, u32[]{:S(2)}) copy-start(bf16[2,128,512]{2,1,0:T(8,128)(2,1)S(1)} %get-tuple-element.171) | copy-start | bytes 786436
  137.7 2.3 %collective-permute-start.16 = (f32[4,128,128]{2,1,0:T(8,128)S(1)}, f32[4,128,128]{2,1,0:T(8,128)S(1)}, u32[]{:S(2)}, u32[]{:S(2)}) collective-permute-start(f32[4,128,128]{2,1,0:T(8,128)S(1)} %slice.7), channel_id=1, source_target_pairs={{0,1},{1,0},{2,3},{3,2},{4,5},{5,4},{6,7},{7,6},{8,9},{9,8},{10,11... | collective-permute-start | bytes 786440 | tf_op jit(solution)/shard_map/ppermute | solution.py:503
  138.0 9.1 %collective-permute-start.18 = (bf16[8,128,128]{2,1,0:T(8,128)(2,1)S(1)}, bf16[8,128,128]{2,1,0:T(8,128)(2,1)S(1)}, u32[]{:S(2)}, u32[]{:S(2)}) collective-permute-start(bf16[8,128,128]{2,1,0:T(8,128)(2,1)S(1)} %constant_dynamic-update-slice_fusion.backs), channel_id=1, source_target_pairs={{0,2},{1,3},{2,0},{3,1},{4,6},{5,7},{6,4},{7,5},{8,10},{9,11},{10,... | collective-permute-start | bytes 786440 | tf_op jit(solution)/shard_map/ppermute | solution.py:503
  139.4 12.8 %collective-permute-start.17 = (bf16[8,128,128]{2,1,0:T(8,128)(2,1)S(1)}, bf16[8,128,128]{2,1,0:T(8,128)(2,1)S(1)}, u32[]{:S(2)}, u32[]{:S(2)}) collective-permute-start(bf16[8,128,128]{2,1,0:T(8,128)(2,1)S(1)} %get-tuple-element.161), channel_id=1, source_target_pairs={{0,2},{1,3},{2,0},{3,1},{4,6},{5,7},{6,4},{7,5},{8,10},{9,11},{10,... | collective-permute-start | bytes 786440 | tf_op jit(solution)/shard_map/ppermute | solution.py:503
  152.1 47.1 %collective-permute-start.28 = (bf16[8,128,512]{2,1,0:T(8,128)(2,1)}, bf16[8,128,512]{2,1,0:T(8,128)(2,1)S(1)}, u32[]{:S(2)}, u32[]{:S(2)}) collective-permute-start(bf16[8,128,512]{2,1,0:T(8,128)(2,1)} %get-tuple-element.182), channel_id=1, source_target_pairs={{0,2},{1,3},{2,0},{3,1},{4,6},{5,7},{6,4},{7,5},{8,10},{9,11},{10,... | collective-permute-start | bytes 3145736 | tf_op jit(solution)/shard_map/ppermute | solution.py:503
  153.5 29.9 %all-to-all-start.2 = ((f32[4,128,128]{2,1,0:T(8,128)}), f32[4,128,128]{2,1,0:T(8,128)S(1)}, u32[]{:S(2)}, u32[]{:S(2)}) async-start(f32[4,128,128]{2,1,0:T(8,128)} %slice_add_fusion), calls=%async_computation.2 | async-start | bytes 524288 | tf_op jit(solution)/shard_map/all_to_all | solution.py:496
  156.9 26.5 %collective-permute-start.19 = (bf16[2,128,512]{2,1,0:T(8,128)(2,1)}, bf16[2,128,512]{2,1,0:T(8,128)(2,1)S(1)}, u32[]{:S(2)}, u32[]{:S(2)}) collective-permute-start(bf16[2,128,512]{2,1,0:T(8,128)(2,1)} %copy-done.26), channel_id=1, source_target_pairs={{0,8},{1,9},{2,10},{3,11},{4,12},{5,13},{6,14},{7,15},{8,0},{9,1},... | collective-permute-start | bytes 786440 | tf_op jit(solution)/shard_map/ppermute | solution.py:503
  159.8 30.1 %collective-permute-start.20 = (bf16[2,128,512]{2,1,0:T(8,128)(2,1)}, bf16[2,128,512]{2,1,0:T(8,128)(2,1)}, u32[]{:S(2)}, u32[]{:S(2)}) collective-permute-start(bf16[2,128,512]{2,1,0:T(8,128)(2,1)} %copy-done.25), channel_id=1, source_target_pairs={{0,12},{1,13},{2,14},{3,15},{4,8},{5,9},{6,10},{7,11},{8,4},{9,5},... | collective-permute-start | bytes 786440 | tf_op jit(solution)/shard_map/ppermute | solution.py:503
  184.6 9.6 %all-to-all-start.3 = ((bf16[4,128,128]{2,1,0:T(8,128)(2,1)}), bf16[4,128,128]{2,1,0:T(8,128)(2,1)S(1)}, u32[]{:S(2)}, u32[]{:S(2)}) async-start(bf16[4,128,128]{2,1,0:T(8,128)(2,1)} %hidden_low.1), calls=%async_computation.3 | async-start | bytes 262144 | tf_op jit(solution)/shard_map/all_to_all | solution.py:496
  187.9 10.5 %collective-permute-start.27 = (bf16[2,128,512]{2,1,0:T(8,128)(2,1)}, bf16[2,128,512]{2,1,0:T(8,128)(2,1)S(1)}, u32[]{:S(2)}, u32[]{:S(2)}) collective-permute-start(bf16[2,128,512]{2,1,0:T(8,128)(2,1)} %copy-done.19), channel_id=1, source_target_pairs={{0,4},{1,5},{2,6},{3,7},{4,0},{5,1},{6,2},{7,3},{8,12},{9,13},{10,... | collective-permute-start | bytes 786440 | tf_op jit(solution)/shard_map/ppermute | solution.py:503
  194.2 1.4 collective-permute-start.24
  194.2 20.4 %collective-permute-start.26 = (bf16[2,128,512]{2,1,0:T(8,128)(2,1)}, bf16[2,128,512]{2,1,0:T(8,128)(2,1)S(1)}, u32[]{:S(2)}, u32[]{:S(2)}) collective-permute-start(bf16[2,128,512]{2,1,0:T(8,128)(2,1)} %copy-done.18), channel_id=1, source_target_pairs={{0,9},{1,8},{2,11},{3,10},{4,13},{5,12},{6,15},{7,14},{8,1},{9,0},... | collective-permute-start | bytes 786440 | tf_op jit(solution)/shard_map/ppermute | solution.py:503
  195.6 19.0 %collective-permute-start.25 = (bf16[8,128,128]{2,1,0:T(8,128)(2,1)S(1)}, bf16[8,128,128]{2,1,0:T(8,128)(2,1)S(1)}, u32[]{:S(2)}, u32[]{:S(2)}) collective-permute-start(bf16[8,128,128]{2,1,0:T(8,128)(2,1)S(1)} %constant_dynamic-update-slice_fusion.2.hiddens), channel_id=1, source_target_pairs={{0,2},{1,3},{2,0},{3,1},{4,6},{5,7},{6,4},{7,5},{8,10},{9,11},{10,... | collective-permute-start | bytes 786440 | tf_op jit(solution)/shard_map/ppermute | solution.py:503
  196.4 31.0 %collective-permute-start.21 = (bf16[2,128,512]{2,1,0:T(8,128)(2,1)}, bf16[2,128,512]{2,1,0:T(8,128)(2,1)S(1)}, u32[]{:S(2)}, u32[]{:S(2)}) collective-permute-start(bf16[2,128,512]{2,1,0:T(8,128)(2,1)} %copy-done.17), channel_id=1, source_target_pairs={{0,13},{1,12},{2,15},{3,14},{4,9},{5,8},{6,11},{7,10},{8,5},{9,4},... | collective-permute-start | bytes 786440 | tf_op jit(solution)/shard_map/ppermute | solution.py:503
  198.4 29.0 %collective-permute-start.22 = (bf16[2,128,512]{2,1,0:T(8,128)(2,1)}, bf16[2,128,512]{2,1,0:T(8,128)(2,1)S(1)}, u32[]{:S(2)}, u32[]{:S(2)}) collective-permute-start(bf16[2,128,512]{2,1,0:T(8,128)(2,1)} %copy-done.16), channel_id=1, source_target_pairs={{0,1},{1,0},{2,3},{3,2},{4,5},{5,4},{6,7},{7,6},{8,9},{9,8},{10,11... | collective-permute-start | bytes 786440 | tf_op jit(solution)/shard_map/ppermute | solution.py:503
  199.2 28.2 %collective-permute-start.23 = (bf16[2,128,512]{2,1,0:T(8,128)(2,1)}, bf16[2,128,512]{2,1,0:T(8,128)(2,1)S(1)}, u32[]{:S(2)}, u32[]{:S(2)}) collective-permute-start(bf16[2,128,512]{2,1,0:T(8,128)(2,1)} %copy-done.15), channel_id=1, source_target_pairs={{0,5},{1,4},{2,7},{3,6},{4,1},{5,0},{6,3},{7,2},{8,13},{9,12},{10,... | collective-permute-start | bytes 786440 | tf_op jit(solution)/shard_map/ppermute | solution.py:503
  199.2 15.4 %copy-start.11 = (bf16[8,128,128]{2,1,0:T(8,128)(2,1)S(1)}, bf16[8,128,128]{2,1,0:T(8,128)(2,1)}, u32[]{:S(2)}) copy-start(bf16[8,128,128]{2,1,0:T(8,128)(2,1)} %copy-done.10) | copy-start | bytes 786436
  204.7 13.5 %copy-start.9 = (bf16[2,128,512]{2,1,0:T(8,128)(2,1)S(1)}, bf16[2,128,512]{2,1,0:T(8,128)(2,1)}, u32[]{:S(2)}) copy-start(bf16[2,128,512]{2,1,0:T(8,128)(2,1)} %copy-done.8) | copy-start | bytes 786436
  (13 other events, 9.1 us)

commit v7 on v6

--- a/solution.py
+++ b/solution.py
@@ -71,15 +71,14 @@
 
 
 def copy_call(kernel, name, prefetch, operands, out_shapes, copies):
-    hbm = pl.BlockSpec(memory_space=pltpu.HBM)
     return pl.pallas_call(
         kernel,
         out_shape=out_shapes,
         grid_spec=pltpu.PrefetchScalarGridSpec(
             num_scalar_prefetch=len(prefetch),
             grid=(1,),
-            in_specs=[hbm] * len(operands),
-            out_specs=[hbm] * len(out_shapes),
+            in_specs=[pl.BlockSpec(memory_space=pl.ANY)] * len(operands),
+            out_specs=[whole(shape.shape) for shape in out_shapes],
             scratch_shapes=[pltpu.SemaphoreType.DMA((copies,))],
         ),
         compiler_params=params(),
@@ -87,7 +86,7 @@
     )(*prefetch, *operands)
 
 
-weight_cuts = 8
+weight_cuts = 4
 
 
 def pair_kernel(adapters, place, weight, down_maps, out, sems):
@@ -122,20 +121,24 @@
     )[0]
 
 
-def gather_up_kernel(adapters, up_maps, out, sems):
-    run(
-        [
-            pltpu.make_async_copy(up_maps.at[adapters[block]], out.at[block], sems.at[block])
-            for block in range(out.shape[0])
-        ]
-    )
-
-
-def gather_up(adapters, up_maps):
-    shape = jax.ShapeDtypeStruct((adapters.shape[0],) + up_maps.shape[1:], up_maps.dtype)
+def gather_up_kernel(adapters, place, up_maps, own, pair, sems):
+    members = own.shape[0]
+    copies = []
+    for index in range(members):
+        block = (index // 2) * line_bit + place[0] % line_bit // pair_bit * pair_bit + index % 2
+        for side, out in enumerate((own, pair)):
+            source = up_maps.at[adapters[block ^ (side * pair_bit)]]
+            copies.append(
+                pltpu.make_async_copy(source, out.at[index], sems.at[2 * index + side])
+            )
+    run(copies)
+
+
+def gather_up(adapters, place, up_maps, members):
+    shape = jax.ShapeDtypeStruct((members,) + up_maps.shape[1:], up_maps.dtype)
     return copy_call(
-        gather_up_kernel, "gather_up", (adapters,), (up_maps,), [shape], adapters.shape[0]
-    )[0]
+        gather_up_kernel, "gather_up", (adapters, place), (up_maps,), [shape] * 2, 2 * members
+    )
 
 
 def pack_kernel(place, tokens, *refs):
@@ -169,23 +172,32 @@
     return alive, adapter_alpha / rank.astype(jnp.float32)
 
 
-def back_kernel(adapters, place, ranks, gradient, up, out):
-    alive, factor = rank_row(ranks, adapters[place[0]], up.shape[1])
+def back_kernel(adapters, place, ranks, gradient, ups, out, up):
+    members, _, value_width, extent = ups.shape
+    side = place[0] % line_bit // pair_bit
+    for index in range(members):
+        for half in range(2):
+            owner = (index // 2) * line_bit + (side ^ half) * pair_bit + index % 2
+            rows = pl.ds(pl.multiple_of(owner * value_width, value_width), value_width)
+            up[rows, :] = ups[index, half]
+    alive, factor = rank_row(ranks, adapters[place[0]], extent)
     back = jnp.dot(gradient[...], up[...], preferred_element_type=jnp.float32)
     low = (factor * back * alive).astype(out.dtype)
     for line in range(out.shape[0]):
         out[line] = low
 
 
-def back_rows(adapters, place, ranks, gradient, up, lines):
-    shape = jax.ShapeDtypeStruct((lines, gradient.shape[0], up.shape[1]), jnp.bfloat16)
+def back_rows(adapters, place, ranks, gradient, ups):
+    members, _, _, extent = ups.shape
+    rows, depth = gradient.shape
     return call(
         back_kernel,
         "back_low",
         (adapters, place, ranks),
-        (gradient, up),
-        [whole(gradient.shape), whole(up.shape)],
-        [shape],
+        (gradient, ups),
+        [whole(gradient.shape), whole(ups.shape)],
+        [jax.ShapeDtypeStruct((members // 2, rows, extent), jnp.bfloat16)],
+        scratch=[pltpu.VMEM((depth, extent), jnp.bfloat16)],
     )[0]
 
 
@@ -318,7 +330,6 @@
 
 def join_columns(place, pieces, offsets, columns, before=None):
     rows = pieces[0].shape[1]
-    anywhere = pl.BlockSpec(memory_space=pl.ANY)
     rest = [] if before is None else [before]
     return pl.pallas_call(
         functools.partial(join_kernel, offsets=offsets, aliased=len(rest)),
@@ -326,7 +337,8 @@
         grid_spec=pltpu.PrefetchScalarGridSpec(
             num_scalar_prefetch=1,
             grid=(1,),
-            in_specs=[anywhere] * (len(pieces) + len(rest)),
+            in_specs=[whole(piece.shape) for piece in pieces]
+            + [pl.BlockSpec(memory_space=pl.ANY)] * len(rest),
             out_specs=pl.BlockSpec(memory_space=pltpu.HBM),
             scratch_shapes=[pltpu.SemaphoreType.DMA((2 * len(pieces),))],
         ),
@@ -486,16 +498,26 @@
     )
 
 
-def exchange(pieces):
-    return lax.all_to_all(pieces, "dp", split_axis=0, concat_axis=0, tiled=True)
-
-
-def exchange_line(pieces):
-    lines = pieces.shape[0]
-    groups = [[line * line_bit + first for line in range(lines)] for first in range(line_bit)]
+def exchange(pieces, groups):
     return lax.all_to_all(
         pieces, "dp", split_axis=0, concat_axis=0, axis_index_groups=groups, tiled=True
     )
+
+
+def exchange_line(pieces):
+    groups = [
+        [line * line_bit + first for line in range(pieces.shape[0])] for first in range(line_bit)
+    ]
+    return exchange(pieces, groups)
+
+
+def exchange_side(pieces):
+    members = pieces.shape[0]
+    groups = [
+        [(index // 2) * line_bit + side * pair_bit + index % 2 for index in range(members)]
+        for side in range(2)
+    ]
+    return exchange(pieces, groups)
 
 
 def swap(array, flip):
@@ -540,10 +562,12 @@
     gradients = [own_gradient] + [None] * (members - 1)
     for step in range(steps):
         gradients[1 << step] = swap(own_gradient, offsets[1 << step])
-    own_up = exchange(gather_up(adapters, up_maps)).reshape(depth, extent)
+    ups, ups_pair = gather_up(adapters, place, up_maps, members)
+    ups_other = swap(ups_pair, pair_bit)
     pair = for_pair(adapters, place, value_weight, down_maps, members)
-    gradients[2], pair = barrier((gradients[2], pair))
+    ups_other, pair = barrier((ups_other, pair))
     pair = swap(pair, pair_bit)
+    ups = exchange_side(jnp.stack([ups, ups_other], axis=1))
     packs = pack_tokens(place, tokens, members, width)
     gradients[1], packs = barrier((gradients[1], packs))
     arrived = {0: packs[0]}
@@ -551,55 +575,44 @@
     for step in range(1, steps):
         for slot in range(1, 1 << step):
             gradients[slot + (1 << step)] = swap(gradients[slot], offsets[1 << step])
-    gradients[: members // 2], own_up, packs = barrier(
-        (gradients[: members // 2], own_up, packs)
-    )
-
-    backs = exchange_line(back_rows(adapters, place, ranks, output_gradient, own_up, lines))
-    arrived.update(send(packs, portions[1]))
+    gradients[: members // 2], ups, packs = barrier((gradients[: members // 2], ups, packs))
+
+    backs = exchange_line(back_rows(adapters, place, ranks, output_gradient, ups))
     backs, gradients, packs, done = barrier(
-        (backs, gradients, packs, taken(arrived, portions[0] + portions[1]))
-    )
-    arrived.update(zip(portions[0] + portions[1], done))
+        (backs, gradients, packs, taken(arrived, portions[0]))
+    )
+    arrived.update(zip(portions[0], done))
+    for portion in portions[1:]:
+        arrived.update(send(packs, portion))
     backs = both_cores(backs)
-    arrived.update(send(packs, portions[2]))
-    arrived.update(send(packs, portions[3]))
-
     *slices, columns, columns_pair = input_slices(
         adapters, place, gradients, backs, value_weight, pair, down_maps
     )
     results = {0: slices[0]}
     results.update(send(slices, portions[0]))
-    results.update(send(slices, portions[1]))
     columns_other = swap(columns_pair, pair_bit)
     backs_pair = swap(backs, pair_bit)
     slices, arrived = barrier((slices, taken(arrived, range(members))))
     parts, tokens_own, tokens_pair = hidden_parts(adapters, place, down_maps, pair, arrived)
     parts = parts[:lines] + swap(parts[lines:], 1)
-    parts, tokens_pair, columns_other, backs_pair = barrier(
-        (parts, tokens_pair, columns_other, backs_pair)
-    )
-    tokens_other = swap(tokens_pair, pair_bit)
-    parts = exchange_line(parts)
-    parts, done, slices = barrier((parts, taken(results, portions[0]), slices))
+    parts, done = barrier((parts, taken(results, portions[0])))
     results.update(zip(portions[0], done))
-    results.update(send(slices, portions[2]))
-
-    hiddens = exchange_line(hidden_rows(adapters, place, ranks, parts))
-    hiddens, done, slices = barrier((hiddens, taken(results, portions[1]), slices))
-    results.update(zip(portions[1], done))
-    results.update(send(slices, portions[3]))
+    hiddens = exchange_line(
+        hidden_rows(adapters, place, ranks, exchange_line(parts))
+    )
+    hiddens, slices, columns_other, backs_pair, tokens_pair = barrier(
+        (hiddens, slices, columns_other, backs_pair, tokens_pair)
+    )
+    for portion in portions[1:]:
+        results.update(send(slices, portion))
     hiddens = both_cores(hiddens)
     hiddens_pair = swap(hiddens, pair_bit)
+    tokens_other = swap(tokens_pair, pair_bit)
+    up_gradient = up_gradients(
+        adapters, place, ranks, columns, columns_other, hiddens, hiddens_pair, depth // devices
+    )
     down_gradient = down_gradients(
         adapters, place, backs, backs_pair, tokens_own, tokens_other, num_adapters
-    )
-    hiddens_pair, done, down_gradient = barrier(
-        (hiddens_pair, taken(results, portions[2]), down_gradient)
-    )
-    results.update(zip(portions[2], done))
-    up_gradient = up_gradients(
-        adapters, place, ranks, columns, columns_other, hiddens, hiddens_pair, depth // devices
     )
 
     def joined(slots, before=None):
@@ -608,7 +621,7 @@
         )
 
     most = joined([0] + portions[0] + portions[1] + portions[2])
-    up_gradient, most = barrier((up_gradient, most))
+    up_gradient, down_gradient, most = barrier((up_gradient, down_gradient, most))
     input_grad = joined(portions[3], most)
     return (input_grad, down_gradient, up_gradient)
 

time: 230 us -> 177 us (0.77)
  Pallas kernels: 67.9 us -> 29.2 us
  waiting for transfers between devices: 101 us -> 82.8 us
  starting transfers between devices: 47.5 us -> 50 us
    pallas_call x3, Pallas kernels: 35.6 us -> 5.69 us  [copy_call(): pl.pallas_call(kernel, out_shape=out_shapes, grid_spec=pltpu.PrefetchScal...]
    all_to_all x4, waiting for transfers between devices: 36.6 us -> 17.3 us  [exchange(): lax.all_to_all(pieces, 'dp', split_axis=0, concat_axis=0, axis_index_grou...]
    pallas_call x2, Pallas kernels: 10.1 us -> 2.06 us  [join_columns(): pl.pallas_call(functools.partial(join_kernel, offsets=offsets, aliased=le...]
    ppermute x29 -> x30, starting transfers between devices: 33.1 us -> 34.9 us  [swap(): return lax.ppermute(array, 'dp', [(i, i ^ flip) for i in range(devices)])]
    ppermute x29 -> x30, waiting for transfers between devices: 64.3 us -> 65.5 us  [swap(): return lax.ppermute(array, 'dp', [(i, i ^ flip) for i in range(devices)])]
    unnamed x58 -> x68, local copies, waits for them, and re-layouts: 10.4 us -> 11.2 us
  transfers between devices with their start and end apart: 33 -> 34, of which waited for: 13 -> 13; matrix products, arithmetic and copies ran while one was open for 0% -> 1% of each run, Pallas kernels for 28% -> 14%
where the time goes in v7:
time: 177 us; the launch traced here: 176 us
  waiting for transfers between devices  82.8 us (47%)
  starting transfers between devices  50 us (28%)
  Pallas kernels  29.2 us (16%)
  local copies, waits for them, and re-layouts  11.3 us (6%)
    ppermute x30, waiting for transfers between devices, swap(): return lax.ppermute(array, 'dp', [(i, i ^ flip) for i in range(devices)])  65.5 us
    ppermute x30, starting transfers between devices, swap(): return lax.ppermute(array, 'dp', [(i, i ^ flip) for i in range(devices)])  34.9 us
    all_to_all x4, waiting for transfers between devices, exchange(): lax.all_to_all(pieces, 'dp', split_axis=0, concat_axis=0, axis_index_grou...  17.3 us
    all_to_all x4, starting transfers between devices, exchange(): lax.all_to_all(pieces, 'dp', split_axis=0, concat_axis=0, axis_index_grou...  15.1 us
    pallas_call x4, Pallas kernels, call(): pl.pallas_call(kernel, out_shape=out_shapes, grid_spec=pltpu.PrefetchScal...  12.4 us
    unnamed x68, local copies, waits for them, and re-layouts  11.2 us
    pallas_call x2, Pallas kernels, sums_call(): pl.pallas_call(kernel, out_shape=jax.ShapeDtypeStruct((num_adapters,) + p...  9.09 us
    pallas_call x3, Pallas kernels, copy_call(): pl.pallas_call(kernel, out_shape=out_shapes, grid_spec=pltpu.PrefetchScal...  5.69 us
  transfers between devices with their start and end apart: 34, of which 13 were waited for; matrix products, arithmetic and copies ran while one was open for 1% of the time, Pallas kernels for 14%

profile of v7, /device:TPU:0, one launch (start us, length us, event | category | flops | bytes accessed | tf_op | source)
XLA Modules:
  0.0 175.8 jit_solution(11813301122662774188)
XLA Ops:
  0.6 1.2 copy-done.4
  2.5 1.1 gather_up.1
  3.6 3.0 %collective-permute-start = (bf16[8,64,128]{2,1,0:T(8,128)(2,1)S(1)}, bf16[8,64,128]{2,1,0:T(8,128)(2,1)S(1)}, u32[]{:S(2)}, u32[]{:S(2)}) collective-permute-start(bf16[8,64,128]{2,1,0:T(8,128)(2,1)S(1)} %get-tuple-element.93), channel_id=1, source_target_pairs={{0,2},{1,3},{2,0},{3,1},{4,6},{5,7},{6,4},{7,5},{8,10},{9,11},{10,... | collective-permute-start | bytes 393224 | tf_op jit(solution)/shard_map/ppermute | solution.py:525
  6.6 1.2 copy-done
  7.9 3.4 %for_pair.1 = bf16[2048,512]{1,0:T(8,128)(2,1)} custom-call(s32[16]{0:T(128)S(1)} %copy-done.13, s32[1]{0:T(128)} %bitcast.place, bf16[1024,512]{1,0:T(8,128)(2,1)S(1)} %copy-done, bf16[64,128,512]{2,1,0:T(8,128)(2,1)} %refs_7_.1), custom_call_target="tpu_custom_call" | custom-call | tf_op jit(solution)/shard_map/for_pair/pallas_call | solution.py:74
  11.9 2.6 %collective-permute-start.2 = (bf16[1,128,1024]{2,1,0:T(8,128)(2,1)S(1)}, bf16[1,128,1024]{2,1,0:T(8,128)(2,1)}, u32[]{:S(2)}, u32[]{:S(2)}) collective-permute-start(bf16[1,128,1024]{2,1,0:T(8,128)(2,1)S(1)} %bitcast.4), channel_id=1, source_target_pairs={{0,8},{1,9},{2,10},{3,11},{4,12},{5,13},{6,14},{7,15},{8,0},{9,1},... | collective-permute-start | bytes 786440 | tf_op jit(solution)/shard_map/ppermute | solution.py:525
  14.5 0.7 pad_maximum_fusion
  15.2 4.2 %all-to-all-start = ((bf16[8,2,64,128]{3,2,1,0:T(8,128)(2,1)}), bf16[8,2,64,128]{3,2,1,0:T(8,128)(2,1)}, u32[]{:S(2)}, u32[]{:S(2)}) async-start(bf16[8,2,64,128]{3,2,1,0:T(8,128)(2,1)} %pad_maximum_fusion), calls=%async_computation | async-start | bytes 524288 | tf_op jit(solution)/shard_map/all_to_all | solution.py:502
  19.4 1.9 %collective-permute-start.3 = (bf16[1,128,1024]{2,1,0:T(8,128)(2,1)S(1)}, bf16[1,128,1024]{2,1,0:T(8,128)(2,1)}, u32[]{:S(2)}, u32[]{:S(2)}) collective-permute-start(bf16[1,128,1024]{2,1,0:T(8,128)(2,1)S(1)} %bitcast.5), channel_id=1, source_target_pairs={{0,4},{1,5},{2,6},{3,7},{4,0},{5,1},{6,2},{7,3},{8,12},{9,13},{10,... | collective-permute-start | bytes 786440 | tf_op jit(solution)/shard_map/ppermute | solution.py:525
  21.3 1.2 pack_tokens.1
  25.3 0.7 copy-done.29
  27.5 2.6 %collective-permute-done.2.refs_1_ = bf16[1,128,1024]{2,1,0:T(8,128)(2,1)} collective-permute-done((bf16[1,128,1024]{2,1,0:T(8,128)(2,1)S(1)}, bf16[1,128,1024]{2,1,0:T(8,128)(2,1)}, u32[]{:S(2)}, u32[]{:S(2)}) %collective-permute-start.2) | collective-permute-done | bytes 262176 | tf_op jit(solution)/shard_map/ppermute | solution.py:525
  30.1 5.7 %collective-permute-done.3.refs_2_ = bf16[1,128,1024]{2,1,0:T(8,128)(2,1)} collective-permute-done((bf16[1,128,1024]{2,1,0:T(8,128)(2,1)S(1)}, bf16[1,128,1024]{2,1,0:T(8,128)(2,1)}, u32[]{:S(2)}, u32[]{:S(2)}) %collective-permute-start.3) | collective-permute-done | bytes 262176 | tf_op jit(solution)/shard_map/ppermute | solution.py:525
  35.8 1.9 %collective-permute-start.9 = (bf16[2,128,512]{2,1,0:T(8,128)(2,1)}, bf16[2,128,512]{2,1,0:T(8,128)(2,1)S(1)}, u32[]{:S(2)}, u32[]{:S(2)}) collective-permute-start(bf16[2,128,512]{2,1,0:T(8,128)(2,1)} %get-tuple-element.107), channel_id=1, source_target_pairs={{0,8},{1,9},{2,10},{3,11},{4,12},{5,13},{6,14},{7,15},{8,0},{9,1},... | collective-permute-start | bytes 786440 | tf_op jit(solution)/shard_map/ppermute | solution.py:525
  38.5 3.7 %collective-permute-done.4.refs_3_ = bf16[1,128,1024]{2,1,0:T(8,128)(2,1)S(1)} collective-permute-done((bf16[1,128,1024]{2,1,0:T(8,128)(2,1)}, bf16[1,128,1024]{2,1,0:T(8,128)(2,1)S(1)}, u32[]{:S(2)}, u32[]{:S(2)}) %collective-permute-start.4) | collective-permute-done | bytes 262176 | tf_op jit(solution)/shard_map/ppermute | solution.py:525
  42.3 2.4 %back_low.1 = bf16[4,128,128]{2,1,0:T(8,128)(2,1)} custom-call(s32[16]{0:T(128)S(1)} %copy-done.14, s32[1]{0:T(128)} %bitcast.place, s32[64]{0:T(128)S(1)} %copy-done.15, bf16[128,1024]{1,0:T(8,128)(2,1)S(1)} %copy-done.3, bf16[8,2,64,128]{3,2,1,0:T(8,128)(2,1)} %all-to-all-done.ups), custom_call_target="tpu_custom_call" | custom-call | tf_op jit(solution)/shard_map/back_low/pallas_call | solution.py:51
  44.7 4.0 %all-to-all-start.1 = ((bf16[4,128,128]{2,1,0:T(8,128)(2,1)}), bf16[4,128,128]{2,1,0:T(8,128)(2,1)S(1)}, u32[]{:S(2)}, u32[]{:S(2)}) async-start(bf16[4,128,128]{2,1,0:T(8,128)(2,1)} %back_low.1), calls=%async_computation.1 | async-start | bytes 262144 | tf_op jit(solution)/shard_map/all_to_all | solution.py:502
  48.8 2.0 %collective-permute-done.9.refs_9_ = bf16[2,128,512]{2,1,0:T(8,128)(2,1)S(1)} collective-permute-done((bf16[2,128,512]{2,1,0:T(8,128)(2,1)}, bf16[2,128,512]{2,1,0:T(8,128)(2,1)S(1)}, u32[]{:S(2)}, u32[]{:S(2)}) %collective-permute-start.9) | collective-permute-done | bytes 262176 | tf_op jit(solution)/shard_map/ppermute | solution.py:525
  50.8 4.4 %all-to-all-done.1 = bf16[4,128,128]{2,1,0:T(8,128)(2,1)S(1)} async-done(((bf16[4,128,128]{2,1,0:T(8,128)(2,1)}), bf16[4,128,128]{2,1,0:T(8,128)(2,1)S(1)}, u32[]{:S(2)}, u32[]{:S(2)}) %all-to-all-start.1) | async-done | bytes 131104 | tf_op jit(solution)/shard_map/all_to_all | solution.py:502
  55.2 1.1 collective-permute-start.11
  56.2 1.1 collective-permute-start.12
  57.6 1.2 collective-permute-start.14
  58.8 4.5 %collective-permute-done.11.refs_10_ = bf16[2,128,512]{2,1,0:T(8,128)(2,1)S(1)} collective-permute-done((bf16[2,128,512]{2,1,0:T(8,128)(2,1)}, bf16[2,128,512]{2,1,0:T(8,128)(2,1)S(1)}, u32[]{:S(2)}, u32[]{:S(2)}) %collective-permute-start.11) | collective-permute-done | bytes 262176 | tf_op jit(solution)/shard_map/ppermute | solution.py:525
  63.3 3.2 %collective-permute-start.16 = (bf16[2,128,512]{2,1,0:T(8,128)(2,1)}, bf16[2,128,512]{2,1,0:T(8,128)(2,1)S(1)}, u32[]{:S(2)}, u32[]{:S(2)}) collective-permute-start(bf16[2,128,512]{2,1,0:T(8,128)(2,1)} %copy-done.25), channel_id=1, source_target_pairs={{0,13},{1,12},{2,15},{3,14},{4,9},{5,8},{6,11},{7,10},{8,5},{9,4},... | collective-permute-start | bytes 786440 | tf_op jit(solution)/shard_map/ppermute | solution.py:525
  66.6 0.9 copy-done.8
  67.5 5.4 %input_slices.1 = (bf16[2,128,512]{2,1,0:T(8,128)(2,1)S(1)}, bf16[2,128,512]{2,1,0:T(8,128)(2,1)S(1)}, bf16[2,128,512]{2,1,0:T(8,128)(2,1)S(1)}, bf16[2,128,512]...) custom-call(s32[16]{0:T(128)S(1)} %copy-done.14, ...), custom_call_target="tpu_custom_call" | custom-call | tf_op jit(solution)/shard_map/input_slices/pallas_call | solution.py:51
  74.5 13.2 %collective-permute-done.14.refs_13_ = bf16[2,128,512]{2,1,0:T(8,128)(2,1)S(1)} collective-permute-done((bf16[2,128,512]{2,1,0:T(8,128)(2,1)}, bf16[2,128,512]{2,1,0:T(8,128)(2,1)S(1)}, u32[]{:S(2)}, u32[]{:S(2)}) %collective-permute-start.14) | collective-permute-done | bytes 262176 | tf_op jit(solution)/shard_map/ppermute | solution.py:525
  87.7 3.3 %hidden_parts.1 = (f32[8,128,128]{2,1,0:T(8,128)S(1)}, bf16[8,128,512]{2,1,0:T(8,128)(2,1)S(1)}, bf16[8,128,512]{2,1,0:T(8,128)(2,1)S(1)}) custom-call(s32[16]{0:T(128)S(1)} %copy-done.14, s32[1]{0:T(128)} %bitcast.place, bf16[2048,512]{1,0:T(8,128)(2,1)} %collective-permute-done.1.pair, bf16[64,128,512]{2,1,0:T(8,128)(2,1)} %refs_7_.1, ...), custom_call_target="tpu_custom_call" | custom-call | tf_op jit(solution)/shard_map/hidden_parts/pallas_call | solution.py:51
  91.8 6.1 %collective-permute-start.18 = (bf16[2,128,512]{2,1,0:T(8,128)(2,1)S(1)}, bf16[2,128,512]{2,1,0:T(8,128)(2,1)S(1)}, u32[]{:S(2)}, u32[]{:S(2)}) collective-permute-start(bf16[2,128,512]{2,1,0:T(8,128)(2,1)S(1)} %get-tuple-element.135), channel_id=1, source_target_pairs={{0,8},{1,9},{2,10},{3,11},{4,12},{5,13},{6,14},{7,15},{8,0},{9,1},... | collective-permute-start | bytes 786440 | tf_op jit(solution)/shard_map/ppermute | solution.py:525
  97.9 0.7 slice_add_fusion
  98.6 11.6 %collective-permute-done.18.refs_1_ = bf16[2,128,512]{2,1,0:T(8,128)(2,1)S(1)} collective-permute-done((bf16[2,128,512]{2,1,0:T(8,128)(2,1)S(1)}, bf16[2,128,512]{2,1,0:T(8,128)(2,1)S(1)}, u32[]{:S(2)}, u32[]{:S(2)}) %collective-permute-start.18) | collective-permute-done | bytes 262176 | tf_op jit(solution)/shard_map/ppermute | solution.py:525
  110.3 3.4 %all-to-all-start.2 = ((f32[4,128,128]{2,1,0:T(8,128)}), f32[4,128,128]{2,1,0:T(8,128)S(1)}, u32[]{:S(2)}, u32[]{:S(2)}) async-start(f32[4,128,128]{2,1,0:T(8,128)} %slice_add_fusion), calls=%async_computation.2 | async-start | bytes 524288 | tf_op jit(solution)/shard_map/all_to_all | solution.py:502
  113.7 1.6 collective-permute-start.20
  115.8 7.0 %all-to-all-done.2.parts = f32[4,128,128]{2,1,0:T(8,128)S(1)} async-done(((f32[4,128,128]{2,1,0:T(8,128)}), f32[4,128,128]{2,1,0:T(8,128)S(1)}, u32[]{:S(2)}, u32[]{:S(2)}) %all-to-all-start.2) | async-done | bytes 262176 | tf_op jit(solution)/shard_map/all_to_all | solution.py:502
  122.8 1.2 hidden_low.1
  124.0 3.5 %all-to-all-start.3 = ((bf16[4,128,128]{2,1,0:T(8,128)(2,1)}), bf16[4,128,128]{2,1,0:T(8,128)(2,1)S(1)}, u32[]{:S(2)}, u32[]{:S(2)}) async-start(bf16[4,128,128]{2,1,0:T(8,128)(2,1)} %hidden_low.1), calls=%async_computation.3 | async-start | bytes 262144 | tf_op jit(solution)/shard_map/all_to_all | solution.py:502
  127.5 5.9 %all-to-all-done.3 = bf16[4,128,128]{2,1,0:T(8,128)(2,1)S(1)} async-done(((bf16[4,128,128]{2,1,0:T(8,128)(2,1)}), bf16[4,128,128]{2,1,0:T(8,128)(2,1)S(1)}, u32[]{:S(2)}, u32[]{:S(2)}) %all-to-all-start.3) | async-done | bytes 131104 | tf_op jit(solution)/shard_map/all_to_all | solution.py:502
  133.4 1.5 collective-permute-start.26
  134.9 1.4 collective-permute-start.27
  136.4 2.7 %collective-permute-start.24 = (bf16[4,128,128]{2,1,0:T(8,128)(2,1)S(1)}, bf16[4,128,128]{2,1,0:T(8,128)(2,1)S(1)}, u32[]{:S(2)}, u32[]{:S(2)}) collective-permute-start(bf16[4,128,128]{2,1,0:T(8,128)(2,1)S(1)} %all-to-all-done.3), channel_id=1, source_target_pairs={{0,1},{1,0},{2,3},{3,2},{4,5},{5,4},{6,7},{7,6},{8,9},{9,8},{10,11... | collective-permute-start | bytes 393224 | tf_op jit(solution)/shard_map/ppermute | solution.py:525
  139.2 1.0 collective-permute-done.24
  140.7 5.4 %collective-permute-done.27.refs_2_ = bf16[2,128,512]{2,1,0:T(8,128)(2,1)S(1)} collective-permute-done((bf16[2,128,512]{2,1,0:T(8,128)(2,1)}, bf16[2,128,512]{2,1,0:T(8,128)(2,1)S(1)}, u32[]{:S(2)}, u32[]{:S(2)}) %collective-permute-start.27) | collective-permute-done | bytes 262176 | tf_op jit(solution)/shard_map/ppermute | solution.py:525
  146.1 15.7 %collective-permute-done.28.refs_3_ = bf16[2,128,512]{2,1,0:T(8,128)(2,1)S(1)} collective-permute-done((bf16[2,128,512]{2,1,0:T(8,128)(2,1)}, bf16[2,128,512]{2,1,0:T(8,128)(2,1)S(1)}, u32[]{:S(2)}, u32[]{:S(2)}) %collective-permute-start.28) | collective-permute-done | bytes 262176 | tf_op jit(solution)/shard_map/ppermute | solution.py:525
  161.8 2.8 %collective-permute-start.22 = (bf16[2,128,512]{2,1,0:T(8,128)(2,1)S(1)}, bf16[2,128,512]{2,1,0:T(8,128)(2,1)S(1)}, u32[]{:S(2)}, u32[]{:S(2)}) collective-permute-start(bf16[2,128,512]{2,1,0:T(8,128)(2,1)S(1)} %copy-done.20), channel_id=1, source_target_pairs={{0,1},{1,0},{2,3},{3,2},{4,5},{5,4},{6,7},{7,6},{8,9},{9,8},{10,11... | collective-permute-start | bytes 786440 | tf_op jit(solution)/shard_map/ppermute | solution.py:525
  164.6 1.1 join_columns.2.refs_3_
  165.7 3.6 %up_gradients.1 = bf16[64,64,128]{2,1,0:T(8,128)(2,1)} custom-call(s32[16]{0:T(128)S(1)} %copy-done.14, s32[1]{0:T(128)} %bitcast.place, s32[64]{0:T(128)S(1)} %copy-done.15, bf16[8,128,128]{2,1,0:T(8,128)(2,1)S(1)} %copy-done.10, bf16[8,128,128]{2,1,0:T(8,128)(2,1)S(1)} %collective-permute-done.19.gradients_pair, ...), custom_call_target="tpu_custom_call" | custom-call | tf_op jit(solution)/shard_map/up_gradients/pallas_call | solution.py:403
  169.4 5.5 %down_gradients.1 = bf16[64,128,512]{2,1,0:T(8,128)(2,1)} custom-call(s32[16]{0:T(128)S(1)} %copy-done.14, s32[1]{0:T(128)} %bitcast.place, bf16[8,128,128]{2,1,0:T(8,128)(2,1)S(1)} %constant_dynamic-update-slice_fusion.backs, bf16[8,128,128]{2,1,0:T(8,128)(2,1)S(1)} %collective-permute-done.20.backs_pair, bf16[8,128,512]{2,1,0:T(8,128)(2,1)S(1)} %get-tuple-element.174.own, ...), custom_call_target="tpu_custom_call" | custom-call | tf_op jit(solution)/shard_map/down_gradients/pallas_call | solution.py:403
  174.9 0.9 join_columns.3
  (104 shorter events, 10.0 us)
Async XLA Ops:
  3.6 7.7 %collective-permute-start = (bf16[8,64,128]{2,1,0:T(8,128)(2,1)S(1)}, bf16[8,64,128]{2,1,0:T(8,128)(2,1)S(1)}, u32[]{:S(2)}, u32[]{:S(2)}) collective-permute-start(bf16[8,64,128]{2,1,0:T(8,128)(2,1)S(1)} %get-tuple-element.93), channel_id=1, source_target_pairs={{0,2},{1,3},{2,0},{3,1},{4,6},{5,7},{6,4},{7,5},{8,10},{9,11},{10,... | collective-permute-start | bytes 393224 | tf_op jit(solution)/shard_map/ppermute | solution.py:525
  11.3 31.0 %copy-start.14 = (s32[16]{0:T(128)S(1)}, s32[16]{0:T(128)}, u32[]{:S(2)}) copy-start(s32[16]{0:T(128)} %adapters.15) | copy-start | bytes 196
  11.3 31.0 %copy-start.15 = (s32[64]{0:T(128)S(1)}, s32[64]{0:T(128)}, u32[]{:S(2)}) copy-start(s32[64]{0:T(128)} %ranks.5) | copy-start | bytes 772
  11.3 52.0 %collective-permute-start.1 = (bf16[2048,512]{1,0:T(8,128)(2,1)}, bf16[2048,512]{1,0:T(8,128)(2,1)}, u32[]{:S(2)}, u32[]{:S(2)}) collective-permute-start(bf16[2048,512]{1,0:T(8,128)(2,1)} %for_pair.1), channel_id=1, source_target_pairs={{0,2},{1,3},{2,0},{3,1},{4,6},{5,7},{6,4},{7,5},{8,10},{9,11},{10,... | collective-permute-start | bytes 6291464 | tf_op jit(solution)/shard_map/ppermute | solution.py:525
  11.9 18.2 %collective-permute-start.2 = (bf16[1,128,1024]{2,1,0:T(8,128)(2,1)S(1)}, bf16[1,128,1024]{2,1,0:T(8,128)(2,1)}, u32[]{:S(2)}, u32[]{:S(2)}) collective-permute-start(bf16[1,128,1024]{2,1,0:T(8,128)(2,1)S(1)} %bitcast.4), channel_id=1, source_target_pairs={{0,8},{1,9},{2,10},{3,11},{4,12},{5,13},{6,14},{7,15},{8,0},{9,1},... | collective-permute-start | bytes 786440 | tf_op jit(solution)/shard_map/ppermute | solution.py:525
  15.2 51.4 %copy-start.1 = (bf16[1024,512]{1,0:T(8,128)(2,1)S(1)}, bf16[1024,512]{1,0:T(8,128)(2,1)}, u32[]{:S(2)}) copy-start(bf16[1024,512]{1,0:T(8,128)(2,1)} %refs_16_.1) | copy-start | bytes 3145732
  15.2 27.1 %all-to-all-start = ((bf16[8,2,64,128]{3,2,1,0:T(8,128)(2,1)}), bf16[8,2,64,128]{3,2,1,0:T(8,128)(2,1)}, u32[]{:S(2)}, u32[]{:S(2)}) async-start(bf16[8,2,64,128]{3,2,1,0:T(8,128)(2,1)} %pad_maximum_fusion), calls=%async_computation | async-start | bytes 524288 | tf_op jit(solution)/shard_map/all_to_all | solution.py:502
  19.4 16.4 %collective-permute-start.3 = (bf16[1,128,1024]{2,1,0:T(8,128)(2,1)S(1)}, bf16[1,128,1024]{2,1,0:T(8,128)(2,1)}, u32[]{:S(2)}, u32[]{:S(2)}) collective-permute-start(bf16[1,128,1024]{2,1,0:T(8,128)(2,1)S(1)} %bitcast.5), channel_id=1, source_target_pairs={{0,4},{1,5},{2,6},{3,7},{4,0},{5,1},{6,2},{7,3},{8,12},{9,13},{10,... | collective-permute-start | bytes 786440 | tf_op jit(solution)/shard_map/ppermute | solution.py:525
  21.3 16.4 %collective-permute-start.5 = (bf16[1,128,1024]{2,1,0:T(8,128)(2,1)S(1)}, bf16[1,128,1024]{2,1,0:T(8,128)(2,1)S(1)}, u32[]{:S(2)}, u32[]{:S(2)}) collective-permute-start(bf16[1,128,1024]{2,1,0:T(8,128)(2,1)S(1)} %bitcast.6), channel_id=1, source_target_pairs={{0,1},{1,0},{2,3},{3,2},{4,5},{5,4},{6,7},{7,6},{8,9},{9,8},{10,11... | collective-permute-start | bytes 786440 | tf_op jit(solution)/shard_map/ppermute | solution.py:525
  30.1 12.0 %collective-permute-start.4 = (bf16[1,128,1024]{2,1,0:T(8,128)(2,1)}, bf16[1,128,1024]{2,1,0:T(8,128)(2,1)S(1)}, u32[]{:S(2)}, u32[]{:S(2)}) collective-permute-start(bf16[1,128,1024]{2,1,0:T(8,128)(2,1)} %collective-permute-done.2.refs_1_), channel_id=1, source_target_pairs={{0,4},{1,5},{2,6},{3,7},{4,0},{5,1},{6,2},{7,3},{8,12},{9,13},{10,... | collective-permute-start | bytes 786440 | tf_op jit(solution)/shard_map/ppermute | solution.py:525
  30.1 18.6 %collective-permute-start.6 = (bf16[1,128,1024]{2,1,0:T(8,128)(2,1)}, bf16[1,128,1024]{2,1,0:T(8,128)(2,1)S(1)}, u32[]{:S(2)}, u32[]{:S(2)}) collective-permute-start(bf16[1,128,1024]{2,1,0:T(8,128)(2,1)} %collective-permute-done.2.refs_1_), channel_id=1, source_target_pairs={{0,1},{1,0},{2,3},{3,2},{4,5},{5,4},{6,7},{7,6},{8,9},{9,8},{10,11... | collective-permute-start | bytes 786440 | tf_op jit(solution)/shard_map/ppermute | solution.py:525
  35.8 15.0 %collective-permute-start.9 = (bf16[2,128,512]{2,1,0:T(8,128)(2,1)}, bf16[2,128,512]{2,1,0:T(8,128)(2,1)S(1)}, u32[]{:S(2)}, u32[]{:S(2)}) collective-permute-start(bf16[2,128,512]{2,1,0:T(8,128)(2,1)} %get-tuple-element.107), channel_id=1, source_target_pairs={{0,8},{1,9},{2,10},{3,11},{4,12},{5,13},{6,14},{7,15},{8,0},{9,1},... | collective-permute-start | bytes 786440 | tf_op jit(solution)/shard_map/ppermute | solution.py:525
  38.5 10.3 %collective-permute-start.7 = (bf16[1,128,1024]{2,1,0:T(8,128)(2,1)}, bf16[1,128,1024]{2,1,0:T(8,128)(2,1)S(1)}, u32[]{:S(2)}, u32[]{:S(2)}) collective-permute-start(bf16[1,128,1024]{2,1,0:T(8,128)(2,1)} %collective-permute-done.3.refs_2_), channel_id=1, source_target_pairs={{0,1},{1,0},{2,3},{3,2},{4,5},{5,4},{6,7},{7,6},{8,9},{9,8},{10,11... | collective-permute-start | bytes 786440 | tf_op jit(solution)/shard_map/ppermute | solution.py:525
  42.1 8.7 %collective-permute-start.8 = (bf16[1,128,1024]{2,1,0:T(8,128)(2,1)S(1)}, bf16[1,128,1024]{2,1,0:T(8,128)(2,1)S(1)}, u32[]{:S(2)}, u32[]{:S(2)}) collective-permute-start(bf16[1,128,1024]{2,1,0:T(8,128)(2,1)S(1)} %collective-permute-done.4.refs_3_), channel_id=1, source_target_pairs={{0,1},{1,0},{2,3},{3,2},{4,5},{5,4},{6,7},{7,6},{8,9},{9,8},{10,11... | collective-permute-start | bytes 786440 | tf_op jit(solution)/shard_map/ppermute | solution.py:525
  44.7 10.5 %all-to-all-start.1 = ((bf16[4,128,128]{2,1,0:T(8,128)(2,1)}), bf16[4,128,128]{2,1,0:T(8,128)(2,1)S(1)}, u32[]{:S(2)}, u32[]{:S(2)}) async-start(bf16[4,128,128]{2,1,0:T(8,128)(2,1)} %back_low.1), calls=%async_computation.1 | async-start | bytes 262144 | tf_op jit(solution)/shard_map/all_to_all | solution.py:502
  55.2 8.1 %collective-permute-start.11 = (bf16[2,128,512]{2,1,0:T(8,128)(2,1)}, bf16[2,128,512]{2,1,0:T(8,128)(2,1)S(1)}, u32[]{:S(2)}, u32[]{:S(2)}) collective-permute-start(bf16[2,128,512]{2,1,0:T(8,128)(2,1)} %copy-done.32), channel_id=1, source_target_pairs={{0,4},{1,5},{2,6},{3,7},{4,0},{5,1},{6,2},{7,3},{8,12},{9,13},{10,... | collective-permute-start | bytes 786440 | tf_op jit(solution)/shard_map/ppermute | solution.py:525
  56.2 1.3 collective-permute-start.10
  56.2 18.2 %collective-permute-start.12 = (bf16[2,128,512]{2,1,0:T(8,128)(2,1)}, bf16[2,128,512]{2,1,0:T(8,128)(2,1)S(1)}, u32[]{:S(2)}, u32[]{:S(2)}) collective-permute-start(bf16[2,128,512]{2,1,0:T(8,128)(2,1)} %copy-done.30), channel_id=1, source_target_pairs={{0,12},{1,13},{2,14},{3,15},{4,8},{5,9},{6,10},{7,11},{8,4},{9,5},... | collective-permute-start | bytes 786440 | tf_op jit(solution)/shard_map/ppermute | solution.py:525
  57.4 17.1 %collective-permute-start.13 = (bf16[2,128,512]{2,1,0:T(8,128)(2,1)}, bf16[2,128,512]{2,1,0:T(8,128)(2,1)S(1)}, u32[]{:S(2)}, u32[]{:S(2)}) collective-permute-start(bf16[2,128,512]{2,1,0:T(8,128)(2,1)} %copy-done.29), channel_id=1, source_target_pairs={{0,1},{1,0},{2,3},{3,2},{4,5},{5,4},{6,7},{7,6},{8,9},{9,8},{10,11... | collective-permute-start | bytes 786440 | tf_op jit(solution)/shard_map/ppermute | solution.py:525
  57.6 30.1 %collective-permute-start.14 = (bf16[2,128,512]{2,1,0:T(8,128)(2,1)}, bf16[2,128,512]{2,1,0:T(8,128)(2,1)S(1)}, u32[]{:S(2)}, u32[]{:S(2)}) collective-permute-start(bf16[2,128,512]{2,1,0:T(8,128)(2,1)} %copy-done.28), channel_id=1, source_target_pairs={{0,9},{1,8},{2,11},{3,10},{4,13},{5,12},{6,15},{7,14},{8,1},{9,0},... | collective-permute-start | bytes 786440 | tf_op jit(solution)/shard_map/ppermute | solution.py:525
  63.3 24.3 %collective-permute-start.15 = (bf16[2,128,512]{2,1,0:T(8,128)(2,1)}, bf16[2,128,512]{2,1,0:T(8,128)(2,1)S(1)}, u32[]{:S(2)}, u32[]{:S(2)}) collective-permute-start(bf16[2,128,512]{2,1,0:T(8,128)(2,1)} %copy-done.26), channel_id=1, source_target_pairs={{0,5},{1,4},{2,7},{3,6},{4,1},{5,0},{6,3},{7,2},{8,13},{9,12},{10,... | collective-permute-start | bytes 786440 | tf_op jit(solution)/shard_map/ppermute | solution.py:525
  63.3 24.3 %collective-permute-start.16 = (bf16[2,128,512]{2,1,0:T(8,128)(2,1)}, bf16[2,128,512]{2,1,0:T(8,128)(2,1)S(1)}, u32[]{:S(2)}, u32[]{:S(2)}) collective-permute-start(bf16[2,128,512]{2,1,0:T(8,128)(2,1)} %copy-done.25), channel_id=1, source_target_pairs={{0,13},{1,12},{2,15},{3,14},{4,9},{5,8},{6,11},{7,10},{8,5},{9,4},... | collective-permute-start | bytes 786440 | tf_op jit(solution)/shard_map/ppermute | solution.py:525
  67.5 20.1 %copy-start.6 = (bf16[2,128,512]{2,1,0:T(8,128)(2,1)S(1)}, bf16[2,128,512]{2,1,0:T(8,128)(2,1)}, u32[]{:S(2)}) copy-start(bf16[2,128,512]{2,1,0:T(8,128)(2,1)} %copy-done.5) | copy-start | bytes 786436
  74.4 16.6 %copy-start.19 = (bf16[2,128,512]{2,1,0:T(8,128)(2,1)}, bf16[2,128,512]{2,1,0:T(8,128)(2,1)S(1)}, u32[]{:S(2)}) copy-start(bf16[2,128,512]{2,1,0:T(8,128)(2,1)S(1)} %get-tuple-element.168) | copy-start | bytes 786436
  74.4 16.6 %copy-start.21 = (bf16[2,128,512]{2,1,0:T(8,128)(2,1)}, bf16[2,128,512]{2,1,0:T(8,128)(2,1)S(1)}, u32[]{:S(2)}) copy-start(bf16[2,128,512]{2,1,0:T(8,128)(2,1)S(1)} %get-tuple-element.167) | copy-start | bytes 786436
  74.4 16.6 %copy-start.23 = (bf16[2,128,512]{2,1,0:T(8,128)(2,1)}, bf16[2,128,512]{2,1,0:T(8,128)(2,1)S(1)}, u32[]{:S(2)}) copy-start(bf16[2,128,512]{2,1,0:T(8,128)(2,1)S(1)} %get-tuple-element.179) | copy-start | bytes 786436
  74.4 16.6 %copy-start.24 = (bf16[2,128,512]{2,1,0:T(8,128)(2,1)}, bf16[2,128,512]{2,1,0:T(8,128)(2,1)S(1)}, u32[]{:S(2)}) copy-start(bf16[2,128,512]{2,1,0:T(8,128)(2,1)S(1)} %get-tuple-element.178) | copy-start | bytes 786436
  74.4 16.6 %copy-start.27 = (bf16[2,128,512]{2,1,0:T(8,128)(2,1)}, bf16[2,128,512]{2,1,0:T(8,128)(2,1)S(1)}, u32[]{:S(2)}) copy-start(bf16[2,128,512]{2,1,0:T(8,128)(2,1)S(1)} %get-tuple-element.177) | copy-start | bytes 786436
  91.1 55.0 %copy-start.22 = (bf16[2,128,512]{2,1,0:T(8,128)(2,1)S(1)}, bf16[2,128,512]{2,1,0:T(8,128)(2,1)}, u32[]{:S(2)}) copy-start(bf16[2,128,512]{2,1,0:T(8,128)(2,1)} %copy-done.21) | copy-start | bytes 786436
  91.1 70.7 %copy-start.20 = (bf16[2,128,512]{2,1,0:T(8,128)(2,1)S(1)}, bf16[2,128,512]{2,1,0:T(8,128)(2,1)}, u32[]{:S(2)}) copy-start(bf16[2,128,512]{2,1,0:T(8,128)(2,1)} %copy-done.19) | copy-start | bytes 786436
  91.1 73.5 %copy-start.18 = (bf16[2,128,512]{2,1,0:T(8,128)(2,1)S(1)}, bf16[2,128,512]{2,1,0:T(8,128)(2,1)}, u32[]{:S(2)}) copy-start(bf16[2,128,512]{2,1,0:T(8,128)(2,1)} %copy-done.17) | copy-start | bytes 786436
  91.1 73.5 %copy-start.12 = (bf16[2,128,512]{2,1,0:T(8,128)(2,1)S(1)}, bf16[2,128,512]{2,1,0:T(8,128)(2,1)}, u32[]{:S(2)}) copy-start(bf16[2,128,512]{2,1,0:T(8,128)(2,1)} %copy-done.11) | copy-start | bytes 786436
  91.2 6.7 %collective-permute-start.17 = (f32[4,128,128]{2,1,0:T(8,128)S(1)}, f32[4,128,128]{2,1,0:T(8,128)S(1)}, u32[]{:S(2)}, u32[]{:S(2)}) collective-permute-start(f32[4,128,128]{2,1,0:T(8,128)S(1)} %slice.7), channel_id=1, source_target_pairs={{0,1},{1,0},{2,3},{3,2},{4,5},{5,4},{6,7},{7,6},{8,9},{9,8},{10,11... | collective-permute-start | bytes 786440 | tf_op jit(solution)/shard_map/ppermute | solution.py:525
  91.8 18.5 %collective-permute-start.18 = (bf16[2,128,512]{2,1,0:T(8,128)(2,1)S(1)}, bf16[2,128,512]{2,1,0:T(8,128)(2,1)S(1)}, u32[]{:S(2)}, u32[]{:S(2)}) collective-permute-start(bf16[2,128,512]{2,1,0:T(8,128)(2,1)S(1)} %get-tuple-element.135), channel_id=1, source_target_pairs={{0,8},{1,9},{2,10},{3,11},{4,12},{5,13},{6,14},{7,15},{8,0},{9,1},... | collective-permute-start | bytes 786440 | tf_op jit(solution)/shard_map/ppermute | solution.py:525
  110.3 12.5 %all-to-all-start.2 = ((f32[4,128,128]{2,1,0:T(8,128)}), f32[4,128,128]{2,1,0:T(8,128)S(1)}, u32[]{:S(2)}, u32[]{:S(2)}) async-start(f32[4,128,128]{2,1,0:T(8,128)} %slice_add_fusion), calls=%async_computation.2 | async-start | bytes 524288 | tf_op jit(solution)/shard_map/all_to_all | solution.py:502
  113.7 13.8 %collective-permute-start.20 = (bf16[8,128,128]{2,1,0:T(8,128)(2,1)S(1)}, bf16[8,128,128]{2,1,0:T(8,128)(2,1)S(1)}, u32[]{:S(2)}, u32[]{:S(2)}) collective-permute-start(bf16[8,128,128]{2,1,0:T(8,128)(2,1)S(1)} %constant_dynamic-update-slice_fusion.backs), channel_id=1, source_target_pairs={{0,2},{1,3},{2,0},{3,1},{4,6},{5,7},{6,4},{7,5},{8,10},{9,11},{10,... | collective-permute-start | bytes 786440 | tf_op jit(solution)/shard_map/ppermute | solution.py:525
  115.3 12.2 %collective-permute-start.19 = (bf16[8,128,128]{2,1,0:T(8,128)(2,1)}, bf16[8,128,128]{2,1,0:T(8,128)(2,1)S(1)}, u32[]{:S(2)}, u32[]{:S(2)}) collective-permute-start(bf16[8,128,128]{2,1,0:T(8,128)(2,1)} %copy-done.31), channel_id=1, source_target_pairs={{0,2},{1,3},{2,0},{3,1},{4,6},{5,7},{6,4},{7,5},{8,10},{9,11},{10,... | collective-permute-start | bytes 786440 | tf_op jit(solution)/shard_map/ppermute | solution.py:525
  124.0 41.7 %copy-start.10 = (bf16[8,128,128]{2,1,0:T(8,128)(2,1)S(1)}, bf16[8,128,128]{2,1,0:T(8,128)(2,1)}, u32[]{:S(2)}) copy-start(bf16[8,128,128]{2,1,0:T(8,128)(2,1)} %copy-done.9) | copy-start | bytes 786436
  124.0 9.3 %all-to-all-start.3 = ((bf16[4,128,128]{2,1,0:T(8,128)(2,1)}), bf16[4,128,128]{2,1,0:T(8,128)(2,1)S(1)}, u32[]{:S(2)}, u32[]{:S(2)}) async-start(bf16[4,128,128]{2,1,0:T(8,128)(2,1)} %hidden_low.1), calls=%async_computation.3 | async-start | bytes 262144 | tf_op jit(solution)/shard_map/all_to_all | solution.py:502
  133.4 36.0 %collective-permute-start.26 = (bf16[8,128,512]{2,1,0:T(8,128)(2,1)}, bf16[8,128,512]{2,1,0:T(8,128)(2,1)S(1)}, u32[]{:S(2)}, u32[]{:S(2)}) collective-permute-start(bf16[8,128,512]{2,1,0:T(8,128)(2,1)} %copy-done.16), channel_id=1, source_target_pairs={{0,2},{1,3},{2,0},{3,1},{4,6},{5,7},{6,4},{7,5},{8,10},{9,11},{10,... | collective-permute-start | bytes 3145736 | tf_op jit(solution)/shard_map/ppermute | solution.py:525
  134.9 11.2 %collective-permute-start.27 = (bf16[2,128,512]{2,1,0:T(8,128)(2,1)}, bf16[2,128,512]{2,1,0:T(8,128)(2,1)S(1)}, u32[]{:S(2)}, u32[]{:S(2)}) collective-permute-start(bf16[2,128,512]{2,1,0:T(8,128)(2,1)} %copy-done.27), channel_id=1, source_target_pairs={{0,12},{1,13},{2,14},{3,15},{4,8},{5,9},{6,10},{7,11},{8,4},{9,5},... | collective-permute-start | bytes 786440 | tf_op jit(solution)/shard_map/ppermute | solution.py:525
  136.3 25.4 %collective-permute-start.28 = (bf16[2,128,512]{2,1,0:T(8,128)(2,1)}, bf16[2,128,512]{2,1,0:T(8,128)(2,1)S(1)}, u32[]{:S(2)}, u32[]{:S(2)}) collective-permute-start(bf16[2,128,512]{2,1,0:T(8,128)(2,1)} %copy-done.24), channel_id=1, source_target_pairs={{0,9},{1,8},{2,11},{3,10},{4,13},{5,12},{6,15},{7,14},{8,1},{9,0},... | collective-permute-start | bytes 786440 | tf_op jit(solution)/shard_map/ppermute | solution.py:525
  136.3 28.2 %collective-permute-start.29 = (bf16[2,128,512]{2,1,0:T(8,128)(2,1)}, bf16[2,128,512]{2,1,0:T(8,128)(2,1)S(1)}, u32[]{:S(2)}, u32[]{:S(2)}) collective-permute-start(bf16[2,128,512]{2,1,0:T(8,128)(2,1)} %copy-done.23), channel_id=1, source_target_pairs={{0,4},{1,5},{2,6},{3,7},{4,0},{5,1},{6,2},{7,3},{8,12},{9,13},{10,... | collective-permute-start | bytes 786440 | tf_op jit(solution)/shard_map/ppermute | solution.py:525
  136.4 3.7 %collective-permute-start.24 = (bf16[4,128,128]{2,1,0:T(8,128)(2,1)S(1)}, bf16[4,128,128]{2,1,0:T(8,128)(2,1)S(1)}, u32[]{:S(2)}, u32[]{:S(2)}) collective-permute-start(bf16[4,128,128]{2,1,0:T(8,128)(2,1)S(1)} %all-to-all-done.3), channel_id=1, source_target_pairs={{0,1},{1,0},{2,3},{3,2},{4,5},{5,4},{6,7},{7,6},{8,9},{9,8},{10,11... | collective-permute-start | bytes 393224 | tf_op jit(solution)/shard_map/ppermute | solution.py:525
  140.1 25.6 %collective-permute-start.25 = (bf16[8,128,128]{2,1,0:T(8,128)(2,1)S(1)}, bf16[8,128,128]{2,1,0:T(8,128)(2,1)S(1)}, u32[]{:S(2)}, u32[]{:S(2)}) collective-permute-start(bf16[8,128,128]{2,1,0:T(8,128)(2,1)S(1)} %constant_dynamic-update-slice_fusion.2.hiddens), channel_id=1, source_target_pairs={{0,2},{1,3},{2,0},{3,1},{4,6},{5,7},{6,4},{7,5},{8,10},{9,11},{10,... | collective-permute-start | bytes 786440 | tf_op jit(solution)/shard_map/ppermute | solution.py:525
  146.1 28.8 %collective-permute-start.21 = (bf16[2,128,512]{2,1,0:T(8,128)(2,1)S(1)}, bf16[2,128,512]{2,1,0:T(8,128)(2,1)S(1)}, u32[]{:S(2)}, u32[]{:S(2)}) collective-permute-start(bf16[2,128,512]{2,1,0:T(8,128)(2,1)S(1)} %copy-done.22), channel_id=1, source_target_pairs={{0,13},{1,12},{2,15},{3,14},{4,9},{5,8},{6,11},{7,10},{8,5},{9,4},... | collective-permute-start | bytes 786440 | tf_op jit(solution)/shard_map/ppermute | solution.py:525
  161.8 13.1 %collective-permute-start.22 = (bf16[2,128,512]{2,1,0:T(8,128)(2,1)S(1)}, bf16[2,128,512]{2,1,0:T(8,128)(2,1)S(1)}, u32[]{:S(2)}, u32[]{:S(2)}) collective-permute-start(bf16[2,128,512]{2,1,0:T(8,128)(2,1)S(1)} %copy-done.20), channel_id=1, source_target_pairs={{0,1},{1,0},{2,3},{3,2},{4,5},{5,4},{6,7},{7,6},{8,9},{9,8},{10,11... | collective-permute-start | bytes 786440 | tf_op jit(solution)/shard_map/ppermute | solution.py:525
  164.6 10.3 %collective-permute-start.23 = (bf16[2,128,512]{2,1,0:T(8,128)(2,1)S(1)}, bf16[2,128,512]{2,1,0:T(8,128)(2,1)S(1)}, u32[]{:S(2)}, u32[]{:S(2)}) collective-permute-start(bf16[2,128,512]{2,1,0:T(8,128)(2,1)S(1)} %copy-done.18), channel_id=1, source_target_pairs={{0,5},{1,4},{2,7},{3,6},{4,1},{5,0},{6,3},{7,2},{8,13},{9,12},{10,... | collective-permute-start | bytes 786440 | tf_op jit(solution)/shard_map/ppermute | solution.py:525
  (19 other events, 69.4 us)

commit v8 on v7

--- a/solution.py
+++ b/solution.py
@@ -203,16 +203,19 @@
 
 def input_kernel(adapters, place, backs, pair, *refs):
     members, rows, _ = backs.shape
-    gradients, downs = refs[:members], refs[members : 2 * members]
-    weight = refs[2 * members]
-    outs, columns = refs[2 * members + 1 : -2], refs[-2:]
+    apart = members // 2
+    gradients = [ref.at[0] for ref in refs[:apart]]
+    gradients += [refs[apart].at[slot] for slot in range(members - apart)]
+    downs = refs[apart + 1 : apart + 1 + members]
+    weight = refs[apart + 1 + members]
+    outs, columns = refs[apart + 2 + members : -2], refs[-2:]
     extent = downs[0].shape[1]
     lanes = columns[0].shape[2]
-    value_width = gradients[0].shape[2] // (2 * members)
+    value_width = gradients[0].shape[1] // (2 * members)
     some = min(4, members)
     for first in range(0, members, some):
         slots = range(first, first + some)
-        lines = jnp.concatenate([gradients[slot][0] for slot in slots], axis=0)
+        lines = jnp.concatenate([gradients[slot][...] for slot in slots], axis=0)
         for half in range(2):
             right = weight[...] if half == 0 else pair[members * extent :]
             frozen = jnp.dot(lines, right, preferred_element_type=jnp.float32)
@@ -226,7 +229,7 @@
         column = (place[0] ^ (side * pair_bit)) * value_width // lanes * lanes
         for slot in range(members):
             entry = entry_of(place[0], slot, members)
-            columns[side][entry] = gradients[slot][0, :, pl.ds(pl.multiple_of(column, lanes), lanes)]
+            columns[side][entry] = gradients[slot][:, pl.ds(pl.multiple_of(column, lanes), lanes)]
 
 
 def input_slices(adapters, place, gradients, backs, weight, pair, down_maps):
@@ -241,7 +244,7 @@
         (adapters, place),
         [backs, pair] + list(gradients) + [down_maps] * members + [weight],
         [whole(backs.shape), whole(pair.shape)]
-        + [whole(gradients[0].shape)] * members
+        + [whole(gradient.shape) for gradient in gradients]
         + [picked(down_maps, line_offset(slot, members)) for slot in range(members)]
         + [whole(weight.shape)],
         [shape] * members + [columns] * 2,
@@ -249,7 +252,7 @@
 
 
 def hidden_kernel(adapters, place, pair, *refs):
-    parts, own, other = refs[-3:]
+    parts, own, *others = refs[-4:]
     members = own.shape[0]
     downs, tokens = refs[:members], refs[members : 2 * members]
     extent = downs[0].shape[1]
@@ -257,7 +260,8 @@
     for slot in range(members):
         entry = entry_of(place[0], slot, members)
         own[entry] = tokens[slot][0]
-        other[entry] = tokens[slot][1]
+        core = line_offset(slot, members) % 2
+        others[core][entry - core * (members // 2)] = tokens[slot][1]
         parts[entry] = lax.dot_general(
             tokens[slot][0], downs[slot][0], across, preferred_element_type=jnp.float32
         ) + lax.dot_general(
@@ -272,7 +276,7 @@
     members = len(tokens)
     _, rows, width = tokens[0].shape
     extent = down_maps.shape[1]
-    tokens_shape = jax.ShapeDtypeStruct((members, rows, width), tokens[0].dtype)
+    others = jax.ShapeDtypeStruct((members // 2, rows, width), tokens[0].dtype)
     return call(
         hidden_kernel,
         "hidden_parts",
@@ -283,8 +287,9 @@
         + [whole(tokens[0].shape)] * members,
         [
             jax.ShapeDtypeStruct((members, rows, extent), jnp.float32),
-            tokens_shape,
-            tokens_shape,
+            jax.ShapeDtypeStruct((members, rows, width), tokens[0].dtype),
+            others,
+            others,
         ],
     )
 
@@ -424,25 +429,40 @@
 
 
 def down_gradient_kernel(
-    adapters, place, backs, backs_pair, own, other, out, head, following, products, ready, zero, sems
+    adapters,
+    place,
+    backs,
+    backs_pair,
+    own,
+    other_first,
+    other_second,
+    out,
+    head,
+    following,
+    products,
+    ready,
+    zero,
+    sems,
 ):
     members = own.shape[0]
+    others = (other_first, other_second)
     list_members(adapters, place, members, head, following)
     for slot in range(members):
         products[slot] = by_rows(backs[slot], own[slot])
-        products[members + slot] = by_rows(backs_pair[slot], other[slot])
+        core, line = divmod(slot, members // 2)
+        products[members + slot] = by_rows(backs_pair[slot], others[core][line])
     write_sums(
         head, following, products, ready, zero, out, sems, lambda adapter, total: total
     )
 
 
-def down_gradients(adapters, place, backs, backs_pair, own, other, num_adapters):
+def down_gradients(adapters, place, backs, backs_pair, own, others, num_adapters):
     members, _, width = own.shape
     return sums_call(
         down_gradient_kernel,
         "down_gradients",
         (adapters, place),
-        (backs, backs_pair, own, other),
+        (backs, backs_pair, own, *others),
         num_adapters,
         2 * members,
         (backs.shape[2], width),
@@ -549,8 +569,8 @@
     near = [slot for slot in range(2, members, 2)]
     quarter = max(1, len(far) // 4)
     portions = [far[at : at + quarter] for at in range(0, len(far), quarter)]
-    portions[2] = portions[2] + near[: len(near) // 2]
-    portions[3] = portions[3] + near[len(near) // 2 :]
+    for number, slot in enumerate(near):
+        portions[number % 3] = portions[number % 3] + [slot]
 
     def send(packs, portion):
         return {slot: swap(packs[slot], offsets[slot]) for slot in portion}
@@ -559,60 +579,79 @@
         return [pieces[slot] for slot in portion]
 
     own_gradient = output_gradient.reshape(1, rows, depth)
-    gradients = [own_gradient] + [None] * (members - 1)
-    for step in range(steps):
+    gradients = [own_gradient] + [None] * (lines - 1)
+    for step in range(steps - 1):
         gradients[1 << step] = swap(own_gradient, offsets[1 << step])
     ups, ups_pair = gather_up(adapters, place, up_maps, members)
     ups_other = swap(ups_pair, pair_bit)
     pair = for_pair(adapters, place, value_weight, down_maps, members)
     ups_other, pair = barrier((ups_other, pair))
     pair = swap(pair, pair_bit)
+    packs = pack_tokens(place, tokens, members, width)
+    gradients[1], ups_other, packs = barrier((gradients[1], ups_other, packs))
+
     ups = exchange_side(jnp.stack([ups, ups_other], axis=1))
-    packs = pack_tokens(place, tokens, members, width)
-    gradients[1], packs = barrier((gradients[1], packs))
     arrived = {0: packs[0]}
-    arrived.update(send(packs, portions[0]))
-    for step in range(1, steps):
+    arrived.update(send(packs, portions[0][:1]))
+    for step in range(1, steps - 1):
         for slot in range(1, 1 << step):
             gradients[slot + (1 << step)] = swap(gradients[slot], offsets[1 << step])
-    gradients[: members // 2], ups, packs = barrier((gradients[: members // 2], ups, packs))
+    ups, packs, done = barrier((ups, packs, taken(arrived, portions[0][:1])))
+    arrived.update(zip(portions[0][:1], done))
 
     backs = exchange_line(back_rows(adapters, place, ranks, output_gradient, ups))
+    arrived.update(send(packs, portions[1][:1]))
     backs, gradients, packs, done = barrier(
-        (backs, gradients, packs, taken(arrived, portions[0]))
-    )
-    arrived.update(zip(portions[0], done))
-    for portion in portions[1:]:
+        (backs, gradients, packs, taken(arrived, portions[1][:1]))
+    )
+    arrived.update(zip(portions[1][:1], done))
+
+    backs = both_cores(backs)
+    gradients.append(swap(jnp.concatenate(gradients, axis=0), 1))
+    for portion in (portions[2], portions[3], portions[0][1:], portions[1][1:]):
         arrived.update(send(packs, portion))
-    backs = both_cores(backs)
     *slices, columns, columns_pair = input_slices(
         adapters, place, gradients, backs, value_weight, pair, down_maps
     )
+    slices, arrived = barrier((slices, taken(arrived, range(members))))
+
+    parts, tokens_own, *tokens_pair = hidden_parts(
+        adapters, place, down_maps, pair, arrived
+    )
     results = {0: slices[0]}
     results.update(send(slices, portions[0]))
+    parts = parts[:lines] + swap(parts[lines:], 1)
+    tokens_other = [swap(tokens_pair[0], pair_bit)]
+    parts, done, slices, tokens_other, tokens_pair = barrier(
+        (parts, taken(results, portions[0]), slices, tokens_other, tokens_pair)
+    )
+    results.update(zip(portions[0], done))
+
+    results.update(send(slices, portions[1]))
+    parts = exchange_line(parts)
+    tokens_other.append(swap(tokens_pair[1], pair_bit))
+    parts, done, slices, tokens_other, columns_pair = barrier(
+        (parts, taken(results, portions[1]), slices, tokens_other, columns_pair)
+    )
+    results.update(zip(portions[1], done))
+
+    results.update(send(slices, portions[2]))
+    hiddens = exchange_line(hidden_rows(adapters, place, ranks, parts))
     columns_other = swap(columns_pair, pair_bit)
     backs_pair = swap(backs, pair_bit)
-    slices, arrived = barrier((slices, taken(arrived, range(members))))
-    parts, tokens_own, tokens_pair = hidden_parts(adapters, place, down_maps, pair, arrived)
-    parts = parts[:lines] + swap(parts[lines:], 1)
-    parts, done = barrier((parts, taken(results, portions[0])))
-    results.update(zip(portions[0], done))
-    hiddens = exchange_line(
-        hidden_rows(adapters, place, ranks, exchange_line(parts))
-    )
-    hiddens, slices, columns_other, backs_pair, tokens_pair = barrier(
-        (hiddens, slices, columns_other, backs_pair, tokens_pair)
-    )
-    for portion in portions[1:]:
-        results.update(send(slices, portion))
+    hiddens, done, slices, columns_other, backs_pair = barrier(
+        (hiddens, taken(results, portions[2]), slices, columns_other, backs_pair)
+    )
+    results.update(zip(portions[2], done))
+
+    results.update(send(slices, portions[3]))
     hiddens = both_cores(hiddens)
     hiddens_pair = swap(hiddens, pair_bit)
-    tokens_other = swap(tokens_pair, pair_bit)
+    down_gradient = down_gradients(
+        adapters, place, backs, backs_pair, tokens_own, tokens_other, num_adapters
+    )
     up_gradient = up_gradients(
         adapters, place, ranks, columns, columns_other, hiddens, hiddens_pair, depth // devices
-    )
-    down_gradient = down_gradients(
-        adapters, place, backs, backs_pair, tokens_own, tokens_other, num_adapters
     )
 
     def joined(slots, before=None):

time: 177 us -> 172 us (0.972)
  waiting for transfers between devices: 82.8 us -> 71 us
  starting transfers between devices: 50 us -> 53.2 us
  local copies, waits for them, and re-layouts: 11.3 us -> 13.1 us
    ppermute x30 -> x28, waiting for transfers between devices: 65.5 us -> 55.2 us  [swap(): return lax.ppermute(array, 'dp', [(i, i ^ flip) for i in range(devices)])]
    pallas_call x3, Pallas kernels: 5.69 us -> 3.6 us  [copy_call(): pl.pallas_call(kernel, out_shape=out_shapes, grid_spec=pltpu.PrefetchScal...]
    unnamed x68 -> x74, local copies, waits for them, and re-layouts: 11.2 us -> 13.1 us
    ppermute x30 -> x28, starting transfers between devices: 34.9 us -> 36.7 us  [swap(): return lax.ppermute(array, 'dp', [(i, i ^ flip) for i in range(devices)])]
  transfers between devices with their start and end apart: 34 -> 32, of which waited for: 13 -> 13; matrix products, arithmetic and copies ran while one was open for 1% -> 2% of each run, Pallas kernels for 14% -> 15%
where the time goes in v8:
time: 172 us; the launch traced here: 171 us
  waiting for transfers between devices  71 us (41%)
  starting transfers between devices  53.2 us (31%)
  Pallas kernels  30.1 us (18%)
  local copies, waits for them, and re-layouts  13.1 us (8%)
  other arithmetic  2.8 us (2%)
    ppermute x28, waiting for transfers between devices, swap(): return lax.ppermute(array, 'dp', [(i, i ^ flip) for i in range(devices)])  55.2 us
    ppermute x28, starting transfers between devices, swap(): return lax.ppermute(array, 'dp', [(i, i ^ flip) for i in range(devices)])  36.7 us
    all_to_all x4, starting transfers between devices, exchange(): lax.all_to_all(pieces, 'dp', split_axis=0, concat_axis=0, axis_index_grou...  16.4 us
    all_to_all x4, waiting for transfers between devices, exchange(): lax.all_to_all(pieces, 'dp', split_axis=0, concat_axis=0, axis_index_grou...  15.8 us
    pallas_call x4, Pallas kernels, call(): pl.pallas_call(kernel, out_shape=out_shapes, grid_spec=pltpu.PrefetchScal...  13.2 us
    unnamed x74, local copies, waits for them, and re-layouts  13.1 us
    pallas_call x2, Pallas kernels, sums_call(): pl.pallas_call(kernel, out_shape=jax.ShapeDtypeStruct((num_adapters,) + p...  10.2 us
    pallas_call x3, Pallas kernels, copy_call(): pl.pallas_call(kernel, out_shape=out_shapes, grid_spec=pltpu.PrefetchScal...  3.6 us
  transfers between devices with their start and end apart: 32, of which 13 were waited for; matrix products, arithmetic and copies ran while one was open for 2% of the time, Pallas kernels for 15%

profile of v8, /device:TPU:0, one launch (start us, length us, event | category | flops | bytes accessed | tf_op | source)
XLA Modules:
  0.0 171.1 jit_solution(11931828642553584402)
XLA Ops:
  0.6 4.1 %collective-permute-start.2 = (bf16[1,128,1024]{2,1,0:T(8,128)(2,1)}, bf16[1,128,1024]{2,1,0:T(8,128)(2,1)}, u32[]{:S(2)}, u32[]{:S(2)}) collective-permute-start(bf16[1,128,1024]{2,1,0:T(8,128)(2,1)} %bitcast.4), channel_id=1, source_target_pairs={{0,8},{1,9},{2,10},{3,11},{4,12},{5,13},{6,14},{7,15},{8,0},{9,1},... | collective-permute-start | bytes 786440 | tf_op jit(solution)/shard_map/ppermute | solution.py:545
  4.7 1.2 copy-done.4
  6.6 1.1 gather_up.1
  7.7 1.6 collective-permute-start
  9.3 1.2 copy-done
  10.5 2.0 %for_pair.1 = bf16[2048,512]{1,0:T(8,128)(2,1)S(1)} custom-call(s32[16]{0:T(128)S(1)} %copy-done.15, s32[1]{0:T(128)} %bitcast.place, bf16[1024,512]{1,0:T(8,128)(2,1)S(1)} %copy-done, bf16[64,128,512]{2,1,0:T(8,128)(2,1)} %refs_7_.3), custom_call_target="tpu_custom_call" | custom-call | tf_op jit(solution)/shard_map/for_pair/pallas_call | solution.py:74
  12.7 1.5 collective-permute-start.1
  18.3 0.7 copy-done.30
  19.0 0.7 copy-done.34
  20.4 0.7 pad_maximum_fusion.1
  21.1 4.2 %all-to-all-start = ((bf16[8,2,64,128]{3,2,1,0:T(8,128)(2,1)}), bf16[8,2,64,128]{3,2,1,0:T(8,128)(2,1)}, u32[]{:S(2)}, u32[]{:S(2)}) async-start(bf16[8,2,64,128]{3,2,1,0:T(8,128)(2,1)} %pad_maximum_fusion.1), calls=%async_computation | async-start | bytes 524288 | tf_op jit(solution)/shard_map/all_to_all | solution.py:522
  25.3 2.8 %collective-permute-start.3 = (bf16[2,128,512]{2,1,0:T(8,128)(2,1)}, bf16[2,128,512]{2,1,0:T(8,128)(2,1)S(1)}, u32[]{:S(2)}, u32[]{:S(2)}) collective-permute-start(bf16[2,128,512]{2,1,0:T(8,128)(2,1)} %copy-done.35), channel_id=1, source_target_pairs={{0,8},{1,9},{2,10},{3,11},{4,12},{5,13},{6,14},{7,15},{8,0},{9,1},... | collective-permute-start | bytes 786440 | tf_op jit(solution)/shard_map/ppermute | solution.py:545
  28.1 1.5 collective-permute-start.4
  30.2 16.1 %collective-permute-done.3.refs_9_ = bf16[2,128,512]{2,1,0:T(8,128)(2,1)S(1)} collective-permute-done((bf16[2,128,512]{2,1,0:T(8,128)(2,1)}, bf16[2,128,512]{2,1,0:T(8,128)(2,1)S(1)}, u32[]{:S(2)}, u32[]{:S(2)}) %collective-permute-start.3) | collective-permute-done | bytes 262176 | tf_op jit(solution)/shard_map/ppermute | solution.py:545
  46.3 0.7 copy-done.7
  47.0 1.2 collective-permute-start.6
  48.3 2.4 %back_low.1 = bf16[4,128,128]{2,1,0:T(8,128)(2,1)} custom-call(s32[16]{0:T(128)S(1)} %copy-done.16, s32[1]{0:T(128)} %bitcast.place, s32[64]{0:T(128)S(1)} %copy-done.17, bf16[128,1024]{1,0:T(8,128)(2,1)S(1)} %copy-done.2, bf16[8,2,64,128]{3,2,1,0:T(8,128)(2,1)} %all-to-all-done.ups), custom_call_target="tpu_custom_call" | custom-call | tf_op jit(solution)/shard_map/back_low/pallas_call | solution.py:51
  50.7 3.9 %all-to-all-start.1 = ((bf16[4,128,128]{2,1,0:T(8,128)(2,1)}), bf16[4,128,128]{2,1,0:T(8,128)(2,1)S(1)}, u32[]{:S(2)}, u32[]{:S(2)}) async-start(bf16[4,128,128]{2,1,0:T(8,128)(2,1)} %back_low.1), calls=%async_computation.1 | async-start | bytes 262144 | tf_op jit(solution)/shard_map/all_to_all | solution.py:522
  54.5 7.3 %all-to-all-done.1 = bf16[4,128,128]{2,1,0:T(8,128)(2,1)S(1)} async-done(((bf16[4,128,128]{2,1,0:T(8,128)(2,1)}), bf16[4,128,128]{2,1,0:T(8,128)(2,1)S(1)}, u32[]{:S(2)}, u32[]{:S(2)}) %all-to-all-start.1) | async-done | bytes 131104 | tf_op jit(solution)/shard_map/all_to_all | solution.py:522
  61.9 1.3 pad_maximum_fusion
  63.9 1.0 collective-permute-start.11
  64.8 1.3 collective-permute-done.7
  66.3 1.9 %collective-permute-start.13 = (bf16[2,128,512]{2,1,0:T(8,128)(2,1)S(1)}, bf16[2,128,512]{2,1,0:T(8,128)(2,1)S(1)}, u32[]{:S(2)}, u32[]{:S(2)}) collective-permute-start(bf16[2,128,512]{2,1,0:T(8,128)(2,1)S(1)} %copy-done.25), channel_id=1, source_target_pairs={{0,13},{1,12},{2,15},{3,14},{4,9},{5,8},{6,11},{7,10},{8,5},{9,4},... | collective-permute-start | bytes 786440 | tf_op jit(solution)/shard_map/ppermute | solution.py:545
  68.2 0.9 collective-permute-start.9
  69.2 5.5 %input_slices.1 = (bf16[2,128,512]{2,1,0:T(8,128)(2,1)S(1)}, bf16[2,128,512]{2,1,0:T(8,128)(2,1)S(1)}, bf16[2,128,512]{2,1,0:T(8,128)(2,1)S(1)}, bf16[2,128,512]...) custom-call(s32[16]{0:T(128)S(1)} %copy-done.16, ...), custom_call_target="tpu_custom_call" | custom-call | tf_op jit(solution)/shard_map/input_slices/pallas_call | solution.py:51
  76.1 3.0 %collective-permute-done.11.refs_13_ = bf16[2,128,512]{2,1,0:T(8,128)(2,1)S(1)} collective-permute-done((bf16[2,128,512]{2,1,0:T(8,128)(2,1)S(1)}, bf16[2,128,512]{2,1,0:T(8,128)(2,1)S(1)}, u32[]{:S(2)}, u32[]{:S(2)}) %collective-permute-start.11) | collective-permute-done | bytes 262176 | tf_op jit(solution)/shard_map/ppermute | solution.py:545
  79.2 6.4 %collective-permute-done.12.refs_14_ = bf16[2,128,512]{2,1,0:T(8,128)(2,1)S(1)} collective-permute-done((bf16[2,128,512]{2,1,0:T(8,128)(2,1)S(1)}, bf16[2,128,512]{2,1,0:T(8,128)(2,1)S(1)}, u32[]{:S(2)}, u32[]{:S(2)}) %collective-permute-start.12) | collective-permute-done | bytes 262176 | tf_op jit(solution)/shard_map/ppermute | solution.py:545
  85.6 5.9 %collective-permute-done.9.refs_10_ = bf16[2,128,512]{2,1,0:T(8,128)(2,1)S(1)} collective-permute-done((bf16[2,128,512]{2,1,0:T(8,128)(2,1)S(1)}, bf16[2,128,512]{2,1,0:T(8,128)(2,1)S(1)}, u32[]{:S(2)}, u32[]{:S(2)}) %collective-permute-start.9) | collective-permute-done | bytes 262176 | tf_op jit(solution)/shard_map/ppermute | solution.py:545
  91.5 4.1 %hidden_parts.1 = (f32[8,128,128]{2,1,0:T(8,128)S(1)}, bf16[8,128,512]{2,1,0:T(8,128)(2,1)S(1)}, bf16[4,128,512]{2,1,0:T(8,128)(2,1)S(1)}, bf16[4,128,512]{2,1,0:T(8,128)(2,1)}) custom-call(s32[16]{0:T(128)S(1)} %copy-done.16, s32[1]{0:T(128)} %bitcast.place, bf16[2048,512]{1,0:T(8,128)(2,1)} %collective-permute-done.1.pair, bf16[64,128,512]{2,1,0:T(8,128)(2,1)} %refs_7_.3, ...), custom_call_target="tpu_custom_call" | custom-call | tf_op jit(solution)/shard_map/hidden_parts/pallas_call | solution.py:51
  96.6 2.5 %collective-permute-start.16 = (bf16[2,128,512]{2,1,0:T(8,128)(2,1)S(1)}, bf16[2,128,512]{2,1,0:T(8,128)(2,1)S(1)}, u32[]{:S(2)}, u32[]{:S(2)}) collective-permute-start(bf16[2,128,512]{2,1,0:T(8,128)(2,1)S(1)} %get-tuple-element.161), channel_id=1, source_target_pairs={{0,4},{1,5},{2,6},{3,7},{4,0},{5,1},{6,2},{7,3},{8,12},{9,13},{10,... | collective-permute-start | bytes 786440 | tf_op jit(solution)/shard_map/ppermute | solution.py:545
  99.1 0.7 slice_add_fusion
  99.8 11.3 %collective-permute-done.15.refs_1_ = bf16[2,128,512]{2,1,0:T(8,128)(2,1)S(1)} collective-permute-done((bf16[2,128,512]{2,1,0:T(8,128)(2,1)S(1)}, bf16[2,128,512]{2,1,0:T(8,128)(2,1)S(1)}, u32[]{:S(2)}, u32[]{:S(2)}) %collective-permute-start.15) | collective-permute-done | bytes 262176 | tf_op jit(solution)/shard_map/ppermute | solution.py:545
  112.0 1.5 collective-permute-start.20
  113.5 3.4 %all-to-all-start.2 = ((f32[4,128,128]{2,1,0:T(8,128)}), f32[4,128,128]{2,1,0:T(8,128)S(1)}, u32[]{:S(2)}, u32[]{:S(2)}) async-start(f32[4,128,128]{2,1,0:T(8,128)} %slice_add_fusion), calls=%async_computation.2 | async-start | bytes 524288 | tf_op jit(solution)/shard_map/all_to_all | solution.py:522
  117.0 3.8 %collective-permute-start.18 = (bf16[2,128,512]{2,1,0:T(8,128)(2,1)}, bf16[2,128,512]{2,1,0:T(8,128)(2,1)S(1)}, u32[]{:S(2)}, u32[]{:S(2)}) collective-permute-start(bf16[2,128,512]{2,1,0:T(8,128)(2,1)} %copy-done.33), channel_id=1, source_target_pairs={{0,12},{1,13},{2,14},{3,15},{4,8},{5,9},{6,10},{7,11},{8,4},{9,5},... | collective-permute-start | bytes 786440 | tf_op jit(solution)/shard_map/ppermute | solution.py:545
  121.2 9.7 %collective-permute-done.18.refs_3_ = bf16[2,128,512]{2,1,0:T(8,128)(2,1)S(1)} collective-permute-done((bf16[2,128,512]{2,1,0:T(8,128)(2,1)}, bf16[2,128,512]{2,1,0:T(8,128)(2,1)S(1)}, u32[]{:S(2)}, u32[]{:S(2)}) %collective-permute-start.18) | collective-permute-done | bytes 262176 | tf_op jit(solution)/shard_map/ppermute | solution.py:545
  131.0 0.7 copy-done.11
  132.5 5.5 %collective-permute-start.21 = (bf16[2,128,512]{2,1,0:T(8,128)(2,1)}, bf16[2,128,512]{2,1,0:T(8,128)(2,1)}, u32[]{:S(2)}, u32[]{:S(2)}) collective-permute-start(bf16[2,128,512]{2,1,0:T(8,128)(2,1)} %copy-done.21), channel_id=1, source_target_pairs={{0,9},{1,8},{2,11},{3,10},{4,13},{5,12},{6,15},{7,14},{8,1},{9,0},... | collective-permute-start | bytes 786440 | tf_op jit(solution)/shard_map/ppermute | solution.py:545
  138.5 1.2 hidden_low.1
  139.7 5.0 %all-to-all-start.3 = ((bf16[4,128,128]{2,1,0:T(8,128)(2,1)}), bf16[4,128,128]{2,1,0:T(8,128)(2,1)S(1)}, u32[]{:S(2)}, u32[]{:S(2)}) async-start(bf16[4,128,128]{2,1,0:T(8,128)(2,1)} %hidden_low.1), calls=%async_computation.3 | async-start | bytes 262144 | tf_op jit(solution)/shard_map/all_to_all | solution.py:522
  144.7 8.4 %all-to-all-done.3 = bf16[4,128,128]{2,1,0:T(8,128)(2,1)S(1)} async-done(((bf16[4,128,128]{2,1,0:T(8,128)(2,1)}), bf16[4,128,128]{2,1,0:T(8,128)(2,1)S(1)}, u32[]{:S(2)}, u32[]{:S(2)}) %all-to-all-start.3) | async-done | bytes 131104 | tf_op jit(solution)/shard_map/all_to_all | solution.py:522
  153.1 1.3 collective-permute-start.26
  154.4 1.0 collective-permute-done.26
  156.0 1.7 %collective-permute-start.25 = (bf16[2,128,512]{2,1,0:T(8,128)(2,1)}, bf16[2,128,512]{2,1,0:T(8,128)(2,1)S(1)}, u32[]{:S(2)}, u32[]{:S(2)}) collective-permute-start(bf16[2,128,512]{2,1,0:T(8,128)(2,1)} %copy-done.18), channel_id=1, source_target_pairs={{0,13},{1,12},{2,15},{3,14},{4,9},{5,8},{6,11},{7,10},{8,5},{9,4},... | collective-permute-start | bytes 786440 | tf_op jit(solution)/shard_map/ppermute | solution.py:545
  157.7 6.0 %down_gradients.1 = bf16[64,128,512]{2,1,0:T(8,128)(2,1)} custom-call(s32[16]{0:T(128)S(1)} %copy-done.16, s32[1]{0:T(128)} %bitcast.place, bf16[8,128,128]{2,1,0:T(8,128)(2,1)S(1)} %constant_dynamic-update-slice_fusion.backs, bf16[8,128,128]{2,1,0:T(8,128)(2,1)} %collective-permute-done.24.backs_pair, bf16[8,128,512]{2,1,0:T(8,128)(2,1)S(1)} %get-tuple-element.189.own, ...), custom_call_target="tpu_custom_call" | custom-call | tf_op jit(solution)/shard_map/down_gradients/pallas_call | solution.py:408
  163.8 2.4 %join_columns.2.refs_1_ = bf16[128,8192]{1,0:T(8,128)(2,1)} custom-call(s32[1]{0:T(128)} %bitcast.place, bf16[2,128,512]{2,1,0:T(8,128)(2,1)S(1)} %get-tuple-element.162.refs_0_, bf16[2,128,512]{2,1,0:T(8,128)(2,1)S(1)} %collective-permute-done.15.refs_1_, bf16[2,128,512]{2,1,0:T(8,128)(2,1)S(1)} %copy-done.10, bf16[2,128,512]{2,1,0:T(8,128)(2,1)S(1)} %copy-done.12, ...), custom_call_target="tpu_custom_call" | custom-call | tf_op jit(solution)/shard_map/join_columns/pallas_call | solution.py:339
  166.2 4.1 %up_gradients.1 = bf16[64,64,128]{2,1,0:T(8,128)(2,1)} custom-call(s32[16]{0:T(128)S(1)} %copy-done.16, s32[1]{0:T(128)} %bitcast.place, s32[64]{0:T(128)S(1)} %copy-done.17, bf16[8,128,128]{2,1,0:T(8,128)(2,1)S(1)} %get-tuple-element.185.gradients, bf16[8,128,128]{2,1,0:T(8,128)(2,1)} %collective-permute-done.23.gradients_pair, ...), custom_call_target="tpu_custom_call" | custom-call | tf_op jit(solution)/shard_map/up_gradients/pallas_call | solution.py:408
  170.4 0.7 join_columns.3
  (107 shorter events, 12.7 us)
Async XLA Ops:
  0.6 19.8 %collective-permute-start.2 = (bf16[1,128,1024]{2,1,0:T(8,128)(2,1)}, bf16[1,128,1024]{2,1,0:T(8,128)(2,1)}, u32[]{:S(2)}, u32[]{:S(2)}) collective-permute-start(bf16[1,128,1024]{2,1,0:T(8,128)(2,1)} %bitcast.4), channel_id=1, source_target_pairs={{0,8},{1,9},{2,10},{3,11},{4,12},{5,13},{6,14},{7,15},{8,0},{9,1},... | collective-permute-start | bytes 786440 | tf_op jit(solution)/shard_map/ppermute | solution.py:545
  7.7 5.0 %collective-permute-start = (bf16[8,64,128]{2,1,0:T(8,128)(2,1)S(1)}, bf16[8,64,128]{2,1,0:T(8,128)(2,1)S(1)}, u32[]{:S(2)}, u32[]{:S(2)}) collective-permute-start(bf16[8,64,128]{2,1,0:T(8,128)(2,1)S(1)} %get-tuple-element.102), channel_id=1, source_target_pairs={{0,2},{1,3},{2,0},{3,1},{4,6},{5,7},{6,4},{7,5},{8,10},{9,11},{10,... | collective-permute-start | bytes 393224 | tf_op jit(solution)/shard_map/ppermute | solution.py:545
  12.5 15.6 %copy-start.2 = (bf16[128,1024]{1,0:T(8,128)(2,1)S(1)}, bf16[128,1024]{1,0:T(8,128)(2,1)}, u32[]{:S(2)}) copy-start(bf16[128,1024]{1,0:T(8,128)(2,1)} %gradient.1) | copy-start | bytes 786436
  12.6 35.7 %copy-start.16 = (s32[16]{0:T(128)S(1)}, s32[16]{0:T(128)}, u32[]{:S(2)}) copy-start(s32[16]{0:T(128)} %adapters.15) | copy-start | bytes 196
  12.6 35.7 %copy-start.17 = (s32[64]{0:T(128)S(1)}, s32[64]{0:T(128)}, u32[]{:S(2)}) copy-start(s32[64]{0:T(128)} %ranks.5) | copy-start | bytes 772
  12.7 55.5 %collective-permute-start.1 = (bf16[2048,512]{1,0:T(8,128)(2,1)S(1)}, bf16[2048,512]{1,0:T(8,128)(2,1)}, u32[]{:S(2)}, u32[]{:S(2)}) collective-permute-start(bf16[2048,512]{1,0:T(8,128)(2,1)S(1)} %for_pair.1), channel_id=1, source_target_pairs={{0,2},{1,3},{2,0},{3,1},{4,6},{5,7},{6,4},{7,5},{8,10},{9,11},{10,... | collective-permute-start | bytes 6291464 | tf_op jit(solution)/shard_map/ppermute | solution.py:545
  21.1 48.0 %copy-start.1 = (bf16[1024,512]{1,0:T(8,128)(2,1)S(1)}, bf16[1024,512]{1,0:T(8,128)(2,1)}, u32[]{:S(2)}) copy-start(bf16[1024,512]{1,0:T(8,128)(2,1)} %refs_13_.1) | copy-start | bytes 3145732
  21.1 25.9 %all-to-all-start = ((bf16[8,2,64,128]{3,2,1,0:T(8,128)(2,1)}), bf16[8,2,64,128]{3,2,1,0:T(8,128)(2,1)}, u32[]{:S(2)}, u32[]{:S(2)}) async-start(bf16[8,2,64,128]{3,2,1,0:T(8,128)(2,1)} %pad_maximum_fusion.1), calls=%async_computation | async-start | bytes 524288 | tf_op jit(solution)/shard_map/all_to_all | solution.py:522
  25.3 21.0 %collective-permute-start.3 = (bf16[2,128,512]{2,1,0:T(8,128)(2,1)}, bf16[2,128,512]{2,1,0:T(8,128)(2,1)S(1)}, u32[]{:S(2)}, u32[]{:S(2)}) collective-permute-start(bf16[2,128,512]{2,1,0:T(8,128)(2,1)} %copy-done.35), channel_id=1, source_target_pairs={{0,8},{1,9},{2,10},{3,11},{4,12},{5,13},{6,14},{7,15},{8,0},{9,1},... | collective-permute-start | bytes 786440 | tf_op jit(solution)/shard_map/ppermute | solution.py:545
  28.1 26.4 %collective-permute-start.4 = (bf16[1,128,1024]{2,1,0:T(8,128)(2,1)S(1)}, bf16[1,128,1024]{2,1,0:T(8,128)(2,1)}, u32[]{:S(2)}, u32[]{:S(2)}) collective-permute-start(bf16[1,128,1024]{2,1,0:T(8,128)(2,1)S(1)} %bitcast.5), channel_id=1, source_target_pairs={{0,4},{1,5},{2,6},{3,7},{4,0},{5,1},{6,2},{7,3},{8,12},{9,13},{10,... | collective-permute-start | bytes 786440 | tf_op jit(solution)/shard_map/ppermute | solution.py:545
  29.6 24.9 %collective-permute-start.5 = (bf16[1,128,1024]{2,1,0:T(8,128)(2,1)}, bf16[1,128,1024]{2,1,0:T(8,128)(2,1)}, u32[]{:S(2)}, u32[]{:S(2)}) collective-permute-start(bf16[1,128,1024]{2,1,0:T(8,128)(2,1)} %collective-permute-done.2.refs_1_), channel_id=1, source_target_pairs={{0,4},{1,5},{2,6},{3,7},{4,0},{5,1},{6,2},{7,3},{8,12},{9,13},{10,... | collective-permute-start | bytes 786440 | tf_op jit(solution)/shard_map/ppermute | solution.py:545
  47.0 14.8 %collective-permute-start.6 = (bf16[2,128,512]{2,1,0:T(8,128)(2,1)}, bf16[2,128,512]{2,1,0:T(8,128)(2,1)}, u32[]{:S(2)}, u32[]{:S(2)}) collective-permute-start(bf16[2,128,512]{2,1,0:T(8,128)(2,1)} %copy-done.34), channel_id=1, source_target_pairs={{0,12},{1,13},{2,14},{3,15},{4,8},{5,9},{6,10},{7,11},{8,4},{9,5},... | collective-permute-start | bytes 786440 | tf_op jit(solution)/shard_map/ppermute | solution.py:545
  50.7 11.2 %all-to-all-start.1 = ((bf16[4,128,128]{2,1,0:T(8,128)(2,1)}), bf16[4,128,128]{2,1,0:T(8,128)(2,1)S(1)}, u32[]{:S(2)}, u32[]{:S(2)}) async-start(bf16[4,128,128]{2,1,0:T(8,128)(2,1)} %back_low.1), calls=%async_computation.1 | async-start | bytes 262144 | tf_op jit(solution)/shard_map/all_to_all | solution.py:522
  61.8 4.3 %copy-start.27 = (bf16[2,128,512]{2,1,0:T(8,128)(2,1)S(1)}, bf16[2,128,512]{2,1,0:T(8,128)(2,1)}, u32[]{:S(2)}) copy-start(bf16[2,128,512]{2,1,0:T(8,128)(2,1)} %copy-done.26) | copy-start | bytes 786436
  61.8 4.5 %copy-start.25 = (bf16[2,128,512]{2,1,0:T(8,128)(2,1)S(1)}, bf16[2,128,512]{2,1,0:T(8,128)(2,1)}, u32[]{:S(2)}) copy-start(bf16[2,128,512]{2,1,0:T(8,128)(2,1)} %copy-done.24) | copy-start | bytes 786436
  61.8 6.4 %copy-start.23 = (bf16[2,128,512]{2,1,0:T(8,128)(2,1)S(1)}, bf16[2,128,512]{2,1,0:T(8,128)(2,1)}, u32[]{:S(2)}) copy-start(bf16[2,128,512]{2,1,0:T(8,128)(2,1)} %copy-done.22) | copy-start | bytes 786436
  63.2 3.1 %collective-permute-start.8 = (bf16[4,128,1024]{2,1,0:T(8,128)(2,1)S(1)}, bf16[4,128,1024]{2,1,0:T(8,128)(2,1)S(1)}, u32[]{:S(2)}, u32[]{:S(2)}) collective-permute-start(bf16[4,128,1024]{2,1,0:T(8,128)(2,1)S(1)} %pad_maximum_fusion), channel_id=1, source_target_pairs={{0,1},{1,0},{2,3},{3,2},{4,5},{5,4},{6,7},{7,6},{8,9},{9,8},{10,11... | collective-permute-start | bytes 3145736 | tf_op jit(solution)/shard_map/ppermute | solution.py:545
  63.3 2.8 %collective-permute-start.7 = (bf16[4,128,128]{2,1,0:T(8,128)(2,1)S(1)}, bf16[4,128,128]{2,1,0:T(8,128)(2,1)S(1)}, u32[]{:S(2)}, u32[]{:S(2)}) collective-permute-start(bf16[4,128,128]{2,1,0:T(8,128)(2,1)S(1)} %all-to-all-done.1), channel_id=1, source_target_pairs={{0,1},{1,0},{2,3},{3,2},{4,5},{5,4},{6,7},{7,6},{8,9},{9,8},{10,11... | collective-permute-start | bytes 393224 | tf_op jit(solution)/shard_map/ppermute | solution.py:545
  63.8 12.3 %collective-permute-start.10 = (bf16[2,128,512]{2,1,0:T(8,128)(2,1)S(1)}, bf16[2,128,512]{2,1,0:T(8,128)(2,1)S(1)}, u32[]{:S(2)}, u32[]{:S(2)}) collective-permute-start(bf16[2,128,512]{2,1,0:T(8,128)(2,1)S(1)} %copy-done.31), channel_id=1, source_target_pairs={{0,1},{1,0},{2,3},{3,2},{4,5},{5,4},{6,7},{7,6},{8,9},{9,8},{10,11... | collective-permute-start | bytes 786440 | tf_op jit(solution)/shard_map/ppermute | solution.py:545
  63.9 15.3 %collective-permute-start.11 = (bf16[2,128,512]{2,1,0:T(8,128)(2,1)S(1)}, bf16[2,128,512]{2,1,0:T(8,128)(2,1)S(1)}, u32[]{:S(2)}, u32[]{:S(2)}) collective-permute-start(bf16[2,128,512]{2,1,0:T(8,128)(2,1)S(1)} %copy-done.29), channel_id=1, source_target_pairs={{0,9},{1,8},{2,11},{3,10},{4,13},{5,12},{6,15},{7,14},{8,1},{9,0},... | collective-permute-start | bytes 786440 | tf_op jit(solution)/shard_map/ppermute | solution.py:545
  66.1 19.4 %collective-permute-start.12 = (bf16[2,128,512]{2,1,0:T(8,128)(2,1)S(1)}, bf16[2,128,512]{2,1,0:T(8,128)(2,1)S(1)}, u32[]{:S(2)}, u32[]{:S(2)}) collective-permute-start(bf16[2,128,512]{2,1,0:T(8,128)(2,1)S(1)} %copy-done.27), channel_id=1, source_target_pairs={{0,5},{1,4},{2,7},{3,6},{4,1},{5,0},{6,3},{7,2},{8,13},{9,12},{10,... | collective-permute-start | bytes 786440 | tf_op jit(solution)/shard_map/ppermute | solution.py:545
  66.3 19.2 %collective-permute-start.13 = (bf16[2,128,512]{2,1,0:T(8,128)(2,1)S(1)}, bf16[2,128,512]{2,1,0:T(8,128)(2,1)S(1)}, u32[]{:S(2)}, u32[]{:S(2)}) collective-permute-start(bf16[2,128,512]{2,1,0:T(8,128)(2,1)S(1)} %copy-done.25), channel_id=1, source_target_pairs={{0,13},{1,12},{2,15},{3,14},{4,9},{5,8},{6,11},{7,10},{8,5},{9,4},... | collective-permute-start | bytes 786440 | tf_op jit(solution)/shard_map/ppermute | solution.py:545
  68.2 23.3 %collective-permute-start.9 = (bf16[2,128,512]{2,1,0:T(8,128)(2,1)S(1)}, bf16[2,128,512]{2,1,0:T(8,128)(2,1)S(1)}, u32[]{:S(2)}, u32[]{:S(2)}) collective-permute-start(bf16[2,128,512]{2,1,0:T(8,128)(2,1)S(1)} %copy-done.23), channel_id=1, source_target_pairs={{0,4},{1,5},{2,6},{3,7},{4,0},{5,1},{6,2},{7,3},{8,12},{9,13},{10,... | collective-permute-start | bytes 786440 | tf_op jit(solution)/shard_map/ppermute | solution.py:545
  69.2 22.3 %copy-start.6 = (bf16[2,128,512]{2,1,0:T(8,128)(2,1)S(1)}, bf16[2,128,512]{2,1,0:T(8,128)(2,1)}, u32[]{:S(2)}) copy-start(bf16[2,128,512]{2,1,0:T(8,128)(2,1)} %copy-done.5) | copy-start | bytes 786436
  69.2 22.3 %copy-start.8 = (bf16[2,128,512]{2,1,0:T(8,128)(2,1)S(1)}, bf16[2,128,512]{2,1,0:T(8,128)(2,1)}, u32[]{:S(2)}) copy-start(bf16[2,128,512]{2,1,0:T(8,128)(2,1)} %copy-done.7) | copy-start | bytes 786436
  76.1 15.4 %copy-start.18 = (bf16[2,128,512]{2,1,0:T(8,128)(2,1)}, bf16[2,128,512]{2,1,0:T(8,128)(2,1)S(1)}, u32[]{:S(2)}) copy-start(bf16[2,128,512]{2,1,0:T(8,128)(2,1)S(1)} %get-tuple-element.184) | copy-start | bytes 786436
  76.1 19.5 %copy-start.19 = (bf16[8,128,128]{2,1,0:T(8,128)(2,1)}, bf16[8,128,128]{2,1,0:T(8,128)(2,1)S(1)}, u32[]{:S(2)}) copy-start(bf16[8,128,128]{2,1,0:T(8,128)(2,1)S(1)} %get-tuple-element.183) | copy-start | bytes 786436
  76.1 19.5 %copy-start.20 = (bf16[2,128,512]{2,1,0:T(8,128)(2,1)}, bf16[2,128,512]{2,1,0:T(8,128)(2,1)S(1)}, u32[]{:S(2)}) copy-start(bf16[2,128,512]{2,1,0:T(8,128)(2,1)S(1)} %get-tuple-element.181) | copy-start | bytes 786436
  76.1 19.5 %copy-start.21 = (bf16[2,128,512]{2,1,0:T(8,128)(2,1)}, bf16[2,128,512]{2,1,0:T(8,128)(2,1)S(1)}, u32[]{:S(2)}) copy-start(bf16[2,128,512]{2,1,0:T(8,128)(2,1)S(1)} %get-tuple-element.180) | copy-start | bytes 786436
  95.6 16.4 %collective-permute-start.17 = (bf16[4,128,512]{2,1,0:T(8,128)(2,1)S(1)}, bf16[4,128,512]{2,1,0:T(8,128)(2,1)S(1)}, u32[]{:S(2)}, u32[]{:S(2)}) collective-permute-start(bf16[4,128,512]{2,1,0:T(8,128)(2,1)S(1)} %get-tuple-element.168), channel_id=1, source_target_pairs={{0,2},{1,3},{2,0},{3,1},{4,6},{5,7},{6,4},{7,5},{8,10},{9,11},{10,... | collective-permute-start | bytes 1572872 | tf_op jit(solution)/shard_map/ppermute | solution.py:545
  96.2 2.9 %collective-permute-start.14 = (f32[4,128,128]{2,1,0:T(8,128)S(1)}, f32[4,128,128]{2,1,0:T(8,128)S(1)}, u32[]{:S(2)}, u32[]{:S(2)}) collective-permute-start(f32[4,128,128]{2,1,0:T(8,128)S(1)} %slice.7), channel_id=1, source_target_pairs={{0,1},{1,0},{2,3},{3,2},{4,5},{5,4},{6,7},{7,6},{8,9},{9,8},{10,11... | collective-permute-start | bytes 786440 | tf_op jit(solution)/shard_map/ppermute | solution.py:545
  96.3 14.8 %collective-permute-start.15 = (bf16[2,128,512]{2,1,0:T(8,128)(2,1)S(1)}, bf16[2,128,512]{2,1,0:T(8,128)(2,1)S(1)}, u32[]{:S(2)}, u32[]{:S(2)}) collective-permute-start(bf16[2,128,512]{2,1,0:T(8,128)(2,1)S(1)} %get-tuple-element.160), channel_id=1, source_target_pairs={{0,8},{1,9},{2,10},{3,11},{4,12},{5,13},{6,14},{7,15},{8,0},{9,1},... | collective-permute-start | bytes 786440 | tf_op jit(solution)/shard_map/ppermute | solution.py:545
  96.6 14.7 %collective-permute-start.16 = (bf16[2,128,512]{2,1,0:T(8,128)(2,1)S(1)}, bf16[2,128,512]{2,1,0:T(8,128)(2,1)S(1)}, u32[]{:S(2)}, u32[]{:S(2)}) collective-permute-start(bf16[2,128,512]{2,1,0:T(8,128)(2,1)S(1)} %get-tuple-element.161), channel_id=1, source_target_pairs={{0,4},{1,5},{2,6},{3,7},{4,0},{5,1},{6,2},{7,3},{8,12},{9,13},{10,... | collective-permute-start | bytes 786440 | tf_op jit(solution)/shard_map/ppermute | solution.py:545
  112.0 20.5 %collective-permute-start.20 = (bf16[4,128,512]{2,1,0:T(8,128)(2,1)}, bf16[4,128,512]{2,1,0:T(8,128)(2,1)S(1)}, u32[]{:S(2)}, u32[]{:S(2)}) collective-permute-start(bf16[4,128,512]{2,1,0:T(8,128)(2,1)} %get-tuple-element.177), channel_id=1, source_target_pairs={{0,2},{1,3},{2,0},{3,1},{4,6},{5,7},{6,4},{7,5},{8,10},{9,11},{10,... | collective-permute-start | bytes 1572872 | tf_op jit(solution)/shard_map/ppermute | solution.py:545
  113.5 19.0 %all-to-all-start.2 = ((f32[4,128,128]{2,1,0:T(8,128)}), f32[4,128,128]{2,1,0:T(8,128)S(1)}, u32[]{:S(2)}, u32[]{:S(2)}) async-start(f32[4,128,128]{2,1,0:T(8,128)} %slice_add_fusion), calls=%async_computation.2 | async-start | bytes 524288 | tf_op jit(solution)/shard_map/all_to_all | solution.py:522
  117.0 14.0 %collective-permute-start.18 = (bf16[2,128,512]{2,1,0:T(8,128)(2,1)}, bf16[2,128,512]{2,1,0:T(8,128)(2,1)S(1)}, u32[]{:S(2)}, u32[]{:S(2)}) collective-permute-start(bf16[2,128,512]{2,1,0:T(8,128)(2,1)} %copy-done.33), channel_id=1, source_target_pairs={{0,12},{1,13},{2,14},{3,15},{4,8},{5,9},{6,10},{7,11},{8,4},{9,5},... | collective-permute-start | bytes 786440 | tf_op jit(solution)/shard_map/ppermute | solution.py:545
  120.7 11.0 %collective-permute-start.19 = (bf16[2,128,512]{2,1,0:T(8,128)(2,1)}, bf16[2,128,512]{2,1,0:T(8,128)(2,1)S(1)}, u32[]{:S(2)}, u32[]{:S(2)}) collective-permute-start(bf16[2,128,512]{2,1,0:T(8,128)(2,1)} %copy-done.32), channel_id=1, source_target_pairs={{0,1},{1,0},{2,3},{3,2},{4,5},{5,4},{6,7},{7,6},{8,9},{9,8},{10,11... | collective-permute-start | bytes 786440 | tf_op jit(solution)/shard_map/ppermute | solution.py:545
  120.8 23.9 %collective-permute-start.24 = (bf16[8,128,128]{2,1,0:T(8,128)(2,1)S(1)}, bf16[8,128,128]{2,1,0:T(8,128)(2,1)}, u32[]{:S(2)}, u32[]{:S(2)}) collective-permute-start(bf16[8,128,128]{2,1,0:T(8,128)(2,1)S(1)} %constant_dynamic-update-slice_fusion.backs), channel_id=1, source_target_pairs={{0,2},{1,3},{2,0},{3,1},{4,6},{5,7},{6,4},{7,5},{8,10},{9,11},{10,... | collective-permute-start | bytes 786440 | tf_op jit(solution)/shard_map/ppermute | solution.py:545
  132.5 20.6 %collective-permute-start.21 = (bf16[2,128,512]{2,1,0:T(8,128)(2,1)}, bf16[2,128,512]{2,1,0:T(8,128)(2,1)}, u32[]{:S(2)}, u32[]{:S(2)}) collective-permute-start(bf16[2,128,512]{2,1,0:T(8,128)(2,1)} %copy-done.21), channel_id=1, source_target_pairs={{0,9},{1,8},{2,11},{3,10},{4,13},{5,12},{6,15},{7,14},{8,1},{9,0},... | collective-permute-start | bytes 786440 | tf_op jit(solution)/shard_map/ppermute | solution.py:545
  138.0 15.1 %collective-permute-start.22 = (bf16[2,128,512]{2,1,0:T(8,128)(2,1)}, bf16[2,128,512]{2,1,0:T(8,128)(2,1)}, u32[]{:S(2)}, u32[]{:S(2)}) collective-permute-start(bf16[2,128,512]{2,1,0:T(8,128)(2,1)} %copy-done.20), channel_id=1, source_target_pairs={{0,5},{1,4},{2,7},{3,6},{4,1},{5,0},{6,3},{7,2},{8,13},{9,12},{10,... | collective-permute-start | bytes 786440 | tf_op jit(solution)/shard_map/ppermute | solution.py:545
  138.0 15.1 %collective-permute-start.23 = (bf16[8,128,128]{2,1,0:T(8,128)(2,1)}, bf16[8,128,128]{2,1,0:T(8,128)(2,1)}, u32[]{:S(2)}, u32[]{:S(2)}) collective-permute-start(bf16[8,128,128]{2,1,0:T(8,128)(2,1)} %copy-done.19), channel_id=1, source_target_pairs={{0,2},{1,3},{2,0},{3,1},{4,6},{5,7},{6,4},{7,5},{8,10},{9,11},{10,... | collective-permute-start | bytes 786440 | tf_op jit(solution)/shard_map/ppermute | solution.py:545
  139.7 13.4 %all-to-all-start.3 = ((bf16[4,128,128]{2,1,0:T(8,128)(2,1)}), bf16[4,128,128]{2,1,0:T(8,128)(2,1)S(1)}, u32[]{:S(2)}, u32[]{:S(2)}) async-start(bf16[4,128,128]{2,1,0:T(8,128)(2,1)} %hidden_low.1), calls=%async_computation.3 | async-start | bytes 262144 | tf_op jit(solution)/shard_map/all_to_all | solution.py:522
  153.1 2.3 %collective-permute-start.26 = (bf16[4,128,128]{2,1,0:T(8,128)(2,1)S(1)}, bf16[4,128,128]{2,1,0:T(8,128)(2,1)S(1)}, u32[]{:S(2)}, u32[]{:S(2)}) collective-permute-start(bf16[4,128,128]{2,1,0:T(8,128)(2,1)S(1)} %all-to-all-done.3), channel_id=1, source_target_pairs={{0,1},{1,0},{2,3},{3,2},{4,5},{5,4},{6,7},{7,6},{8,9},{9,8},{10,11... | collective-permute-start | bytes 393224 | tf_op jit(solution)/shard_map/ppermute | solution.py:545
  155.4 10.8 %collective-permute-start.27 = (bf16[8,128,128]{2,1,0:T(8,128)(2,1)S(1)}, bf16[8,128,128]{2,1,0:T(8,128)(2,1)S(1)}, u32[]{:S(2)}, u32[]{:S(2)}) collective-permute-start(bf16[8,128,128]{2,1,0:T(8,128)(2,1)S(1)} %constant_dynamic-update-slice_fusion.2.hiddens), channel_id=1, source_target_pairs={{0,2},{1,3},{2,0},{3,1},{4,6},{5,7},{6,4},{7,5},{8,10},{9,11},{10,... | collective-permute-start | bytes 786440 | tf_op jit(solution)/shard_map/ppermute | solution.py:545
  156.0 14.4 %collective-permute-start.25 = (bf16[2,128,512]{2,1,0:T(8,128)(2,1)}, bf16[2,128,512]{2,1,0:T(8,128)(2,1)S(1)}, u32[]{:S(2)}, u32[]{:S(2)}) collective-permute-start(bf16[2,128,512]{2,1,0:T(8,128)(2,1)} %copy-done.18), channel_id=1, source_target_pairs={{0,13},{1,12},{2,15},{3,14},{4,9},{5,8},{6,11},{7,10},{8,5},{9,4},... | collective-permute-start | bytes 786440 | tf_op jit(solution)/shard_map/ppermute | solution.py:545
  157.7 6.1 %copy-start.10 = (bf16[2,128,512]{2,1,0:T(8,128)(2,1)S(1)}, bf16[2,128,512]{2,1,0:T(8,128)(2,1)}, u32[]{:S(2)}) copy-start(bf16[2,128,512]{2,1,0:T(8,128)(2,1)} %copy-done.9) | copy-start | bytes 786436
  157.7 6.1 %copy-start.12 = (bf16[2,128,512]{2,1,0:T(8,128)(2,1)S(1)}, bf16[2,128,512]{2,1,0:T(8,128)(2,1)}, u32[]{:S(2)}) copy-start(bf16[2,128,512]{2,1,0:T(8,128)(2,1)} %copy-done.11) | copy-start | bytes 786436
  157.7 6.1 %copy-start.14 = (bf16[2,128,512]{2,1,0:T(8,128)(2,1)S(1)}, bf16[2,128,512]{2,1,0:T(8,128)(2,1)}, u32[]{:S(2)}) copy-start(bf16[2,128,512]{2,1,0:T(8,128)(2,1)} %copy-done.13) | copy-start | bytes 786436
  (20 other events, 20.7 us)

commit v9 on v8

--- a/solution.py
+++ b/solution.py
@@ -21,14 +21,14 @@
     return ((order // 2) * line_bit) | (order % 2)
 
 
-def entry_of(place, slot, members):
+def entry_of(slot, members):
     offset = line_offset(slot, members)
-    return (offset % 2) * (members // 2) + ((place ^ offset) // line_bit)
-
-
-def place_of(entry, place, side, members):
+    return (offset % 2) * (members // 2) + offset // line_bit
+
+
+def entry_offset(entry, members):
     core, line = divmod(entry, members // 2)
-    return line * line_bit + ((place % line_bit) ^ core ^ (side * pair_bit))
+    return line * line_bit ^ core
 
 
 def params():
@@ -141,28 +141,32 @@
     )
 
 
-def pack_kernel(place, tokens, *refs):
+def pack_kernel(place, tokens, *refs, flips):
     outs, sems = refs[:-1], refs[-1]
-    members = len(outs)
     width = outs[0].shape[2]
     copies = []
-    for slot in range(members):
+    for number, out in enumerate(outs):
         for half in range(2):
-            column = (place[0] ^ line_offset(slot, members) ^ (half * pair_bit)) * width
+            column = (place[0] ^ flips[number] ^ (half * pair_bit)) * width
             copies.append(
                 pltpu.make_async_copy(
                     tokens.at[:, pl.ds(pl.multiple_of(column, width), width)],
-                    outs[slot].at[half],
-                    sems.at[2 * slot + half],
+                    out.at[half],
+                    sems.at[2 * number + half],
                 )
             )
     run(copies)
 
 
-def pack_tokens(place, tokens, members, width):
+def pack_tokens(place, tokens, flips, width):
     shape = jax.ShapeDtypeStruct((2, tokens.shape[0], width), tokens.dtype)
     return copy_call(
-        pack_kernel, "pack_tokens", (place,), (tokens,), [shape] * members, 2 * members
+        functools.partial(pack_kernel, flips=flips),
+        "pack_tokens",
+        (place,),
+        (tokens,),
+        [shape] * len(flips),
+        2 * len(flips),
     )
 
 
@@ -182,13 +186,11 @@
             up[rows, :] = ups[index, half]
     alive, factor = rank_row(ranks, adapters[place[0]], extent)
     back = jnp.dot(gradient[...], up[...], preferred_element_type=jnp.float32)
-    low = (factor * back * alive).astype(out.dtype)
-    for line in range(out.shape[0]):
-        out[line] = low
+    out[0] = (factor * back * alive).astype(out.dtype)
 
 
 def back_rows(adapters, place, ranks, gradient, ups):
-    members, _, _, extent = ups.shape
+    _, _, _, extent = ups.shape
     rows, depth = gradient.shape
     return call(
         back_kernel,
@@ -196,7 +198,7 @@
         (adapters, place, ranks),
         (gradient, ups),
         [whole(gradient.shape), whole(ups.shape)],
-        [jax.ShapeDtypeStruct((members // 2, rows, extent), jnp.bfloat16)],
+        [jax.ShapeDtypeStruct((1, rows, extent), jnp.bfloat16)],
         scratch=[pltpu.VMEM((depth, extent), jnp.bfloat16)],
     )[0]
 
@@ -221,14 +223,14 @@
             frozen = jnp.dot(lines, right, preferred_element_type=jnp.float32)
             for slot in slots:
                 down = downs[slot][0] if half == 0 else pair[slot * extent : (slot + 1) * extent]
-                entry = entry_of(place[0], slot, members)
+                entry = entry_of(slot, members)
                 low = jnp.dot(backs[entry], down, preferred_element_type=jnp.float32)
                 at = (slot - first) * rows
                 outs[slot][half] = (frozen[at : at + rows] + low).astype(jnp.bfloat16)
     for side in range(2):
         column = (place[0] ^ (side * pair_bit)) * value_width // lanes * lanes
         for slot in range(members):
-            entry = entry_of(place[0], slot, members)
+            entry = entry_of(slot, members)
             columns[side][entry] = gradients[slot][:, pl.ds(pl.multiple_of(column, lanes), lanes)]
 
 
@@ -258,7 +260,7 @@
     extent = downs[0].shape[1]
     across = (((1,), (1,)), ((), ()))
     for slot in range(members):
-        entry = entry_of(place[0], slot, members)
+        entry = entry_of(slot, members)
         own[entry] = tokens[slot][0]
         core = line_offset(slot, members) % 2
         others[core][entry - core * (members // 2)] = tokens[slot][1]
@@ -294,14 +296,31 @@
     )
 
 
-def hidden_low_kernel(adapters, place, ranks, parts, out):
+def core_sum_kernel(parts, received, *outs):
+    for line, out in enumerate(outs):
+        out[0] = parts[line] + received[line]
+
+
+def core_sums(parts, received):
+    lines, rows, extent = received.shape
+    shape = jax.ShapeDtypeStruct((1, rows, extent), jnp.float32)
+    return call(
+        core_sum_kernel,
+        "core_sums",
+        (),
+        (parts, received),
+        [whole(received.shape)] * 2,
+        [shape] * lines,
+    )
+
+
+def hidden_low_kernel(adapters, place, ranks, *refs):
+    out = refs[-1]
     alive, _ = rank_row(ranks, adapters[place[0]], out.shape[2])
-    total = parts[0]
-    for line in range(1, parts.shape[0]):
-        total += parts[line]
-    low = (total * alive).astype(out.dtype)
-    for line in range(out.shape[0]):
-        out[line] = low
+    total = refs[0][0]
+    for part in refs[1:-1]:
+        total += part[0]
+    out[0] = (total * alive).astype(out.dtype)
 
 
 def hidden_rows(adapters, place, ranks, parts):
@@ -309,9 +328,9 @@
         hidden_low_kernel,
         "hidden_low",
         (adapters, place, ranks),
-        (parts,),
-        [whole(parts.shape)],
-        [jax.ShapeDtypeStruct(parts.shape, jnp.bfloat16)],
+        parts,
+        [whole(part.shape) for part in parts],
+        [jax.ShapeDtypeStruct(parts[0].shape, jnp.bfloat16)],
     )[0]
 
 
@@ -361,7 +380,7 @@
     lax.fori_loop(0, head.shape[0], clear, 0)
     for entry in reversed(range(2 * members)):
         side, own = divmod(entry, members)
-        adapter = adapters[place_of(own, place[0], side, members)]
+        adapter = adapters[place[0] ^ entry_offset(own, members) ^ (side * pair_bit)]
         following[entry] = head[adapter]
         head[adapter] = entry
 
@@ -524,13 +543,6 @@
     )
 
 
-def exchange_line(pieces):
-    groups = [
-        [line * line_bit + first for line in range(pieces.shape[0])] for first in range(line_bit)
-    ]
-    return exchange(pieces, groups)
-
-
 def exchange_side(pieces):
     members = pieces.shape[0]
     groups = [
@@ -547,6 +559,12 @@
 
 def tie(first, second):
     return lax.optimization_barrier((first, second))
+
+
+def along_line(pieces):
+    return [pieces[0]] + [
+        swap(piece, line * line_bit) for line, piece in enumerate(pieces) if line
+    ]
 
 
 def both_cores(held):
@@ -570,7 +588,7 @@
     quarter = max(1, len(far) // 4)
     portions = [far[at : at + quarter] for at in range(0, len(far), quarter)]
     for number, slot in enumerate(near):
-        portions[number % 3] = portions[number % 3] + [slot]
+        portions[1 + number % 2] = portions[1 + number % 2] + [slot]
 
     def send(packs, portion):
         return {slot: swap(packs[slot], offsets[slot]) for slot in portion}
@@ -587,28 +605,31 @@
     pair = for_pair(adapters, place, value_weight, down_maps, members)
     ups_other, pair = barrier((ups_other, pair))
     pair = swap(pair, pair_bit)
-    packs = pack_tokens(place, tokens, members, width)
+    packs = dict(zip(portions[0], pack_tokens(place, tokens, taken(offsets, portions[0]), width)))
     gradients[1], ups_other, packs = barrier((gradients[1], ups_other, packs))
 
     ups = exchange_side(jnp.stack([ups, ups_other], axis=1))
-    arrived = {0: packs[0]}
-    arrived.update(send(packs, portions[0][:1]))
+    arrived = send(packs, portions[0])
     for step in range(1, steps - 1):
         for slot in range(1, 1 << step):
             gradients[slot + (1 << step)] = swap(gradients[slot], offsets[1 << step])
-    ups, packs, done = barrier((ups, packs, taken(arrived, portions[0][:1])))
-    arrived.update(zip(portions[0][:1], done))
-
-    backs = exchange_line(back_rows(adapters, place, ranks, output_gradient, ups))
-    arrived.update(send(packs, portions[1][:1]))
+    ups, tokens, done = barrier((ups, tokens, taken(arrived, portions[0])))
+    arrived.update(zip(portions[0], done))
+
+    rest = [slot for slot in range(members) if slot not in portions[0]]
+    packs = dict(zip(rest, pack_tokens(place, tokens, taken(offsets, rest), width)))
+    arrived[0] = packs[0]
+    backs = back_rows(adapters, place, ranks, output_gradient, ups)
+    backs = along_line([backs] * lines)
+    arrived.update(send(packs, portions[1]))
     backs, gradients, packs, done = barrier(
-        (backs, gradients, packs, taken(arrived, portions[1][:1]))
-    )
-    arrived.update(zip(portions[1][:1], done))
-
-    backs = both_cores(backs)
+        (backs, gradients, packs, taken(arrived, portions[1]))
+    )
+    arrived.update(zip(portions[1], done))
+
+    backs = both_cores(jnp.concatenate(backs, axis=0))
     gradients.append(swap(jnp.concatenate(gradients, axis=0), 1))
-    for portion in (portions[2], portions[3], portions[0][1:], portions[1][1:]):
+    for portion in portions[2:]:
         arrived.update(send(packs, portion))
     *slices, columns, columns_pair = input_slices(
         adapters, place, gradients, backs, value_weight, pair, down_maps
@@ -620,7 +641,7 @@
     )
     results = {0: slices[0]}
     results.update(send(slices, portions[0]))
-    parts = parts[:lines] + swap(parts[lines:], 1)
+    parts = core_sums(parts, swap(parts[lines:], 1))
     tokens_other = [swap(tokens_pair[0], pair_bit)]
     parts, done, slices, tokens_other, tokens_pair = barrier(
         (parts, taken(results, portions[0]), slices, tokens_other, tokens_pair)
@@ -628,7 +649,7 @@
     results.update(zip(portions[0], done))
 
     results.update(send(slices, portions[1]))
-    parts = exchange_line(parts)
+    parts = along_line(parts)
     tokens_other.append(swap(tokens_pair[1], pair_bit))
     parts, done, slices, tokens_other, columns_pair = barrier(
         (parts, taken(results, portions[1]), slices, tokens_other, columns_pair)
@@ -636,7 +657,7 @@
     results.update(zip(portions[1], done))
 
     results.update(send(slices, portions[2]))
-    hiddens = exchange_line(hidden_rows(adapters, place, ranks, parts))
+    hiddens = along_line([hidden_rows(adapters, place, ranks, parts)] * lines)
     columns_other = swap(columns_pair, pair_bit)
     backs_pair = swap(backs, pair_bit)
     hiddens, done, slices, columns_other, backs_pair = barrier(
@@ -645,7 +666,7 @@
     results.update(zip(portions[2], done))
 
     results.update(send(slices, portions[3]))
-    hiddens = both_cores(hiddens)
+    hiddens = both_cores(jnp.concatenate(hiddens, axis=0))
     hiddens_pair = swap(hiddens, pair_bit)
     down_gradient = down_gradients(
         adapters, place, backs, backs_pair, tokens_own, tokens_other, num_adapters

time: 172 us -> 186 us (1.081)
  waiting for transfers between devices: 71 us -> 95.7 us
  local copies, waits for them, and re-layouts: 13.1 us -> 3.96 us
  starting transfers between devices: 53.2 us -> 56.7 us
  Pallas kernels: 30.1 us -> 26.8 us
  other arithmetic: 2.8 us -> 0.91 us
    ppermute x28 -> x37, waiting for transfers between devices: 55.2 us -> 95.7 us  [swap(): return lax.ppermute(array, 'dp', [(i, i ^ flip) for i in range(devices)])]
    all_to_all x4 -> x1, waiting for transfers between devices: 15.8 us -> 0.01 us  [exchange(): lax.all_to_all(pieces, 'dp', split_axis=0, concat_axis=0, axis_index_grou...]
    ppermute x28 -> x37, starting transfers between devices: 36.7 us -> 51.8 us  [swap(): return lax.ppermute(array, 'dp', [(i, i ^ flip) for i in range(devices)])]
    all_to_all x4 -> x1, starting transfers between devices: 16.4 us -> 4.81 us  [exchange(): lax.all_to_all(pieces, 'dp', split_axis=0, concat_axis=0, axis_index_grou...]
    unnamed x74 -> x28, local copies, waits for them, and re-layouts: 13.1 us -> 3.9 us
    pallas_call x4 -> x5, Pallas kernels: 13.2 us -> 10.2 us  [call(): pl.pallas_call(kernel, out_shape=out_shapes, grid_spec=pltpu.PrefetchScal...]
    pallas_call x3 -> x4, Pallas kernels: 3.6 us -> 5.53 us  [copy_call(): pl.pallas_call(kernel, out_shape=out_shapes, grid_spec=pltpu.PrefetchScal...]
  transfers between devices with their start and end apart: 32 -> 38, of which waited for: 13 -> 16; matrix products, arithmetic and copies ran while one was open for 2% -> 1% of each run, Pallas kernels for 15% -> 12%
where the time goes in v9:
time: 186 us; the launch traced here: 185 us
  waiting for transfers between devices  95.7 us (51%)
  starting transfers between devices  56.7 us (30%)
  Pallas kernels  26.8 us (14%)
  local copies, waits for them, and re-layouts  3.96 us (2%)
    ppermute x37, waiting for transfers between devices, swap(): return lax.ppermute(array, 'dp', [(i, i ^ flip) for i in range(devices)])  95.7 us
    ppermute x37, starting transfers between devices, swap(): return lax.ppermute(array, 'dp', [(i, i ^ flip) for i in range(devices)])  51.8 us
    pallas_call x5, Pallas kernels, call(): pl.pallas_call(kernel, out_shape=out_shapes, grid_spec=pltpu.PrefetchScal...  10.2 us
    pallas_call x2, Pallas kernels, sums_call(): pl.pallas_call(kernel, out_shape=jax.ShapeDtypeStruct((num_adapters,) + p...  9.09 us
    pallas_call x4, Pallas kernels, copy_call(): pl.pallas_call(kernel, out_shape=out_shapes, grid_spec=pltpu.PrefetchScal...  5.53 us
    all_to_all x1, starting transfers between devices, exchange(): lax.all_to_all(pieces, 'dp', split_axis=0, concat_axis=0, axis_index_grou...  4.81 us
    unnamed x28, local copies, waits for them, and re-layouts  3.9 us
  transfers between devices with their start and end apart: 38, of which 16 were waited for; matrix products, arithmetic and copies ran while one was open for 1% of the time, Pallas kernels for 12%

profile of v9, /device:TPU:0, one launch (start us, length us, event | category | flops | bytes accessed | tf_op | source)
XLA Modules:
  0.0 185.1 jit_solution(15365791776623044166)
XLA Ops:
  0.6 4.1 %collective-permute-start.2 = (bf16[1,128,1024]{2,1,0:T(8,128)(2,1)}, bf16[1,128,1024]{2,1,0:T(8,128)(2,1)S(1)}, u32[]{:S(2)}, u32[]{:S(2)}) collective-permute-start(bf16[1,128,1024]{2,1,0:T(8,128)(2,1)} %bitcast.4), channel_id=1, source_target_pairs={{0,8},{1,9},{2,10},{3,11},{4,12},{5,13},{6,14},{7,15},{8,0},{9,1},... | collective-permute-start | bytes 786440 | tf_op jit(solution)/shard_map/ppermute | solution.py:557
  4.7 1.2 copy-done.4
  6.6 1.1 gather_up.1
  7.7 1.6 collective-permute-start
  9.3 1.2 copy-done.1
  10.5 3.3 %for_pair.1 = bf16[2048,512]{1,0:T(8,128)(2,1)} custom-call(s32[16]{0:T(128)S(1)} %copy-done.7, s32[1]{0:T(128)} %bitcast.place, bf16[1024,512]{1,0:T(8,128)(2,1)S(1)} %copy-done.1, bf16[64,128,512]{2,1,0:T(8,128)(2,1)} %refs_7_.3), custom_call_target="tpu_custom_call" | custom-call | tf_op jit(solution)/shard_map/for_pair/pallas_call | solution.py:74
  14.4 0.8 pack_tokens.2
  15.2 1.6 collective-permute-done.2.refs_1_
  16.9 0.7 pad_maximum_fusion.1
  17.6 4.8 %all-to-all-start = ((bf16[8,2,64,128]{3,2,1,0:T(8,128)(2,1)}), bf16[8,2,64,128]{3,2,1,0:T(8,128)(2,1)S(1)}, u32[]{:S(2)}, u32[]{:S(2)}) async-start(bf16[8,2,64,128]{3,2,1,0:T(8,128)(2,1)} %pad_maximum_fusion.1), calls=%async_computation | async-start | bytes 524288 | tf_op jit(solution)/shard_map/all_to_all | solution.py:541
  22.4 2.9 %collective-permute-start.3 = (bf16[2,128,512]{2,1,0:T(8,128)(2,1)}, bf16[2,128,512]{2,1,0:T(8,128)(2,1)S(1)}, u32[]{:S(2)}, u32[]{:S(2)}) collective-permute-start(bf16[2,128,512]{2,1,0:T(8,128)(2,1)} %pack_tokens.2), channel_id=1, source_target_pairs={{0,8},{1,9},{2,10},{3,11},{4,12},{5,13},{6,14},{7,15},{8,0},{9,1},... | collective-permute-start | bytes 786440 | tf_op jit(solution)/shard_map/ppermute | solution.py:557
  25.3 1.5 collective-permute-start.7
  27.4 16.1 %collective-permute-done.3.refs_9_ = bf16[2,128,512]{2,1,0:T(8,128)(2,1)S(1)} collective-permute-done((bf16[2,128,512]{2,1,0:T(8,128)(2,1)}, bf16[2,128,512]{2,1,0:T(8,128)(2,1)S(1)}, u32[]{:S(2)}, u32[]{:S(2)}) %collective-permute-start.3) | collective-permute-done | bytes 262176 | tf_op jit(solution)/shard_map/ppermute | solution.py:557
  44.7 0.9 collective-permute-start.11
  45.7 1.7 collective-permute-start.9
  47.3 0.8 back_low.1
  48.2 14.0 %collective-permute-done.4 = bf16[1,128,128]{2,1,0:T(8,128)(2,1)S(1)} collective-permute-done((bf16[1,128,128]{2,1,0:T(8,128)(2,1)S(1)}, bf16[1,128,128]{2,1,0:T(8,128)(2,1)S(1)}, u32[]{:S(2)}, u32[]{:S(2)}) %collective-permute-start.4) | collective-permute-done | bytes 32800 | tf_op jit(solution)/shard_map/ppermute | solution.py:557
  62.3 4.4 %collective-permute-start.5 = (bf16[1,128,128]{2,1,0:T(8,128)(2,1)S(1)}, bf16[1,128,128]{2,1,0:T(8,128)(2,1)S(1)}, u32[]{:S(2)}, u32[]{:S(2)}) collective-permute-start(bf16[1,128,128]{2,1,0:T(8,128)(2,1)S(1)} %back_low.1), channel_id=1, source_target_pairs={{0,8},{1,9},{2,10},{3,11},{4,12},{5,13},{6,14},{7,15},{8,0},{9,1},... | collective-permute-start | bytes 98312 | tf_op jit(solution)/shard_map/ppermute | solution.py:557
  66.7 1.9 %collective-permute-done.5 = bf16[1,128,128]{2,1,0:T(8,128)(2,1)S(1)} collective-permute-done((bf16[1,128,128]{2,1,0:T(8,128)(2,1)S(1)}, bf16[1,128,128]{2,1,0:T(8,128)(2,1)S(1)}, u32[]{:S(2)}, u32[]{:S(2)}) %collective-permute-start.5) | collective-permute-done | bytes 32800 | tf_op jit(solution)/shard_map/ppermute | solution.py:557
  68.6 2.9 %collective-permute-start.6 = (bf16[1,128,128]{2,1,0:T(8,128)(2,1)S(1)}, bf16[1,128,128]{2,1,0:T(8,128)(2,1)S(1)}, u32[]{:S(2)}, u32[]{:S(2)}) collective-permute-start(bf16[1,128,128]{2,1,0:T(8,128)(2,1)S(1)} %back_low.1), channel_id=1, source_target_pairs={{0,12},{1,13},{2,14},{3,15},{4,8},{5,9},{6,10},{7,11},{8,4},{9,5},... | collective-permute-start | bytes 98312 | tf_op jit(solution)/shard_map/ppermute | solution.py:557
  71.4 2.9 %collective-permute-done.6 = bf16[1,128,128]{2,1,0:T(8,128)(2,1)S(1)} collective-permute-done((bf16[1,128,128]{2,1,0:T(8,128)(2,1)S(1)}, bf16[1,128,128]{2,1,0:T(8,128)(2,1)S(1)}, u32[]{:S(2)}, u32[]{:S(2)}) %collective-permute-start.6) | collective-permute-done | bytes 32800 | tf_op jit(solution)/shard_map/ppermute | solution.py:557
  75.2 1.2 collective-permute-start.15
  76.4 1.0 collective-permute-done.12
  77.3 2.6 %collective-permute-start.16 = (bf16[2,128,512]{2,1,0:T(8,128)(2,1)S(1)}, bf16[2,128,512]{2,1,0:T(8,128)(2,1)S(1)}, u32[]{:S(2)}, u32[]{:S(2)}) collective-permute-start(bf16[2,128,512]{2,1,0:T(8,128)(2,1)S(1)} %get-tuple-element.144), channel_id=1, source_target_pairs={{0,13},{1,12},{2,15},{3,14},{4,9},{5,8},{6,11},{7,10},{8,5},{9,4},... | collective-permute-start | bytes 786440 | tf_op jit(solution)/shard_map/ppermute | solution.py:557
  80.0 5.5 %input_slices.1 = (bf16[2,128,512]{2,1,0:T(8,128)(2,1)S(1)}, bf16[2,128,512]{2,1,0:T(8,128)(2,1)S(1)}, bf16[2,128,512]{2,1,0:T(8,128)(2,1)S(1)}, bf16[2,128,512]...) custom-call(s32[16]{0:T(128)S(1)} %copy-done.8, ...), custom_call_target="tpu_custom_call" | custom-call | tf_op jit(solution)/shard_map/input_slices/pallas_call | solution.py:51
  85.5 10.1 %collective-permute-done.15.refs_13_ = bf16[2,128,512]{2,1,0:T(8,128)(2,1)S(1)} collective-permute-done((bf16[2,128,512]{2,1,0:T(8,128)(2,1)S(1)}, bf16[2,128,512]{2,1,0:T(8,128)(2,1)S(1)}, u32[]{:S(2)}, u32[]{:S(2)}) %collective-permute-start.15) | collective-permute-done | bytes 262176 | tf_op jit(solution)/shard_map/ppermute | solution.py:557
  95.6 3.3 %hidden_parts.1 = (f32[8,128,128]{2,1,0:T(8,128)S(1)}, bf16[8,128,512]{2,1,0:T(8,128)(2,1)S(1)}, bf16[4,128,512]{2,1,0:T(8,128)(2,1)S(1)}, bf16[4,128,512]{2,1,0:T(8,128)(2,1)S(1)}) custom-call(s32[16]{0:T(128)S(1)} %copy-done.8, s32[1]{0:T(128)} %bitcast.place, bf16[2048,512]{1,0:T(8,128)(2,1)} %collective-permute-done.1.pair, ...), custom_call_target="tpu_custom_call" | custom-call | tf_op jit(solution)/shard_map/hidden_parts/pallas_call | solution.py:51
  98.9 1.6 collective-permute-start.19
  100.8 6.9 %collective-permute-start.18 = (bf16[2,128,512]{2,1,0:T(8,128)(2,1)S(1)}, bf16[2,128,512]{2,1,0:T(8,128)(2,1)S(1)}, u32[]{:S(2)}, u32[]{:S(2)}) collective-permute-start(bf16[2,128,512]{2,1,0:T(8,128)(2,1)S(1)} %get-tuple-element.158), channel_id=1, source_target_pairs={{0,8},{1,9},{2,10},{3,11},{4,12},{5,13},{6,14},{7,15},{8,0},{9,1},... | collective-permute-start | bytes 786440 | tf_op jit(solution)/shard_map/ppermute | solution.py:557
  107.7 12.5 %collective-permute-done.18.refs_1_ = bf16[2,128,512]{2,1,0:T(8,128)(2,1)S(1)} collective-permute-done((bf16[2,128,512]{2,1,0:T(8,128)(2,1)S(1)}, bf16[2,128,512]{2,1,0:T(8,128)(2,1)S(1)}, u32[]{:S(2)}, u32[]{:S(2)}) %collective-permute-start.18) | collective-permute-done | bytes 262176 | tf_op jit(solution)/shard_map/ppermute | solution.py:557
  120.7 1.6 collective-permute-start.23
  122.9 1.4 collective-permute-start.20
  124.3 18.1 %collective-permute-done.20.refs_1_ = f32[1,128,128]{2,1,0:T(8,128)S(1)} collective-permute-done((f32[1,128,128]{2,1,0:T(8,128)S(1)}, f32[1,128,128]{2,1,0:T(8,128)S(1)}, u32[]{:S(2)}, u32[]{:S(2)}) %collective-permute-start.20) | collective-permute-done | bytes 65568 | tf_op jit(solution)/shard_map/ppermute | solution.py:557
  142.4 1.1 collective-permute-start.21
  143.5 4.6 %collective-permute-done.21.refs_2_ = f32[1,128,128]{2,1,0:T(8,128)S(1)} collective-permute-done((f32[1,128,128]{2,1,0:T(8,128)S(1)}, f32[1,128,128]{2,1,0:T(8,128)S(1)}, u32[]{:S(2)}, u32[]{:S(2)}) %collective-permute-start.21) | collective-permute-done | bytes 65568 | tf_op jit(solution)/shard_map/ppermute | solution.py:557
  148.1 2.3 %collective-permute-start.22 = (f32[1,128,128]{2,1,0:T(8,128)S(1)}, f32[1,128,128]{2,1,0:T(8,128)S(1)}, u32[]{:S(2)}, u32[]{:S(2)}) collective-permute-start(f32[1,128,128]{2,1,0:T(8,128)S(1)} %get-tuple-element.171), channel_id=1, source_target_pairs={{0,12},{1,13},{2,14},{3,15},{4,8},{5,9},{6,10},{7,11},{8,4},{9,5},... | collective-permute-start | bytes 196616 | tf_op jit(solution)/shard_map/ppermute | solution.py:557
  150.4 3.8 %collective-permute-done.22.refs_3_ = f32[1,128,128]{2,1,0:T(8,128)S(1)} collective-permute-done((f32[1,128,128]{2,1,0:T(8,128)S(1)}, f32[1,128,128]{2,1,0:T(8,128)S(1)}, u32[]{:S(2)}, u32[]{:S(2)}) %collective-permute-start.22) | collective-permute-done | bytes 65568 | tf_op jit(solution)/shard_map/ppermute | solution.py:557
  154.1 1.5 collective-permute-start.33
  157.0 2.9 %collective-permute-start.27 = (bf16[1,128,128]{2,1,0:T(8,128)(2,1)S(1)}, bf16[1,128,128]{2,1,0:T(8,128)(2,1)S(1)}, u32[]{:S(2)}, u32[]{:S(2)}) collective-permute-start(bf16[1,128,128]{2,1,0:T(8,128)(2,1)S(1)} %hidden_low.1), channel_id=1, source_target_pairs={{0,4},{1,5},{2,6},{3,7},{4,0},{5,1},{6,2},{7,3},{8,12},{9,13},{10,... | collective-permute-start | bytes 98312 | tf_op jit(solution)/shard_map/ppermute | solution.py:557
  159.9 2.3 %collective-permute-done.33.backs_pair = bf16[8,128,128]{2,1,0:T(8,128)(2,1)S(1)} collective-permute-done((bf16[8,128,128]{2,1,0:T(8,128)(2,1)S(1)}, bf16[8,128,128]{2,1,0:T(8,128)(2,1)S(1)}, u32[]{:S(2)}, u32[]{:S(2)}) %collective-permute-start.33) | collective-permute-done | bytes 262176 | tf_op jit(solution)/shard_map/ppermute | solution.py:557
  162.3 2.1 %collective-permute-start.29 = (bf16[1,128,128]{2,1,0:T(8,128)(2,1)S(1)}, bf16[1,128,128]{2,1,0:T(8,128)(2,1)S(1)}, u32[]{:S(2)}, u32[]{:S(2)}) collective-permute-start(bf16[1,128,128]{2,1,0:T(8,128)(2,1)S(1)} %hidden_low.1), channel_id=1, source_target_pairs={{0,12},{1,13},{2,14},{3,15},{4,8},{5,9},{6,10},{7,11},{8,4},{9,5},... | collective-permute-start | bytes 98312 | tf_op jit(solution)/shard_map/ppermute | solution.py:557
  164.4 4.6 %collective-permute-done.28 = bf16[1,128,128]{2,1,0:T(8,128)(2,1)S(1)} collective-permute-done((bf16[1,128,128]{2,1,0:T(8,128)(2,1)S(1)}, bf16[1,128,128]{2,1,0:T(8,128)(2,1)S(1)}, u32[]{:S(2)}, u32[]{:S(2)}) %collective-permute-start.28) | collective-permute-done | bytes 32800 | tf_op jit(solution)/shard_map/ppermute | solution.py:557
  169.0 1.0 collective-permute-done.30.refs_5_
  170.3 1.1 collective-permute-done.35
  172.0 1.9 %collective-permute-start.34 = (bf16[2,128,512]{2,1,0:T(8,128)(2,1)S(1)}, bf16[2,128,512]{2,1,0:T(8,128)(2,1)S(1)}, u32[]{:S(2)}, u32[]{:S(2)}) collective-permute-start(bf16[2,128,512]{2,1,0:T(8,128)(2,1)S(1)} %get-tuple-element.189), channel_id=1, source_target_pairs={{0,13},{1,12},{2,15},{3,14},{4,9},{5,8},{6,11},{7,10},{8,5},{9,4},... | collective-permute-start | bytes 786440 | tf_op jit(solution)/shard_map/ppermute | solution.py:557
  173.9 5.5 %down_gradients.1 = bf16[64,128,512]{2,1,0:T(8,128)(2,1)} custom-call(s32[16]{0:T(128)S(1)} %copy-done.8, s32[1]{0:T(128)} %bitcast.place, bf16[8,128,128]{2,1,0:T(8,128)(2,1)S(1)} %constant_dynamic-update-slice_fusion.backs, bf16[8,128,128]{2,1,0:T(8,128)(2,1)S(1)} %collective-permute-done.33.backs_pair, bf16[8,128,512]{2,1,0:T(8,128)(2,1)S(1)} %get-tuple-element.197.own, ...), custom_call_target="tpu_custom_call" | custom-call | tf_op jit(solution)/shard_map/down_gradients/pallas_call | solution.py:427
  179.4 1.3 join_columns.2.refs_1_
  180.7 3.6 %up_gradients.1 = bf16[64,64,128]{2,1,0:T(8,128)(2,1)} custom-call(s32[16]{0:T(128)S(1)} %copy-done.8, s32[1]{0:T(128)} %bitcast.place, s32[64]{0:T(128)S(1)} %copy-done.9, bf16[8,128,128]{2,1,0:T(8,128)(2,1)S(1)} %get-tuple-element.190.gradients, bf16[8,128,128]{2,1,0:T(8,128)(2,1)S(1)} %collective-permute-done.32.gradients_pair, ...), custom_call_target="tpu_custom_call" | custom-call | tf_op jit(solution)/shard_map/up_gradients/pallas_call | solution.py:427
  (76 shorter events, 8.6 us)
Async XLA Ops:
  0.6 16.2 %collective-permute-start.2 = (bf16[1,128,1024]{2,1,0:T(8,128)(2,1)}, bf16[1,128,1024]{2,1,0:T(8,128)(2,1)S(1)}, u32[]{:S(2)}, u32[]{:S(2)}) collective-permute-start(bf16[1,128,1024]{2,1,0:T(8,128)(2,1)} %bitcast.4), channel_id=1, source_target_pairs={{0,8},{1,9},{2,10},{3,11},{4,12},{5,13},{6,14},{7,15},{8,0},{9,1},... | collective-permute-start | bytes 786440 | tf_op jit(solution)/shard_map/ppermute | solution.py:557
  4.7 1.2 copy-start.4
  6.0 0.7 copy-start.7
  7.7 6.7 %copy-start = (bf16[128,8192]{1,0:T(8,128)(2,1)S(1)}, bf16[128,8192]{1,0:T(8,128)(2,1)}, u32[]{:S(2)}) copy-start(bf16[128,8192]{1,0:T(8,128)(2,1)} %tokens.2) | copy-start | bytes 6291460
  7.7 6.1 %collective-permute-start = (bf16[8,64,128]{2,1,0:T(8,128)(2,1)S(1)}, bf16[8,64,128]{2,1,0:T(8,128)(2,1)S(1)}, u32[]{:S(2)}, u32[]{:S(2)}) collective-permute-start(bf16[8,64,128]{2,1,0:T(8,128)(2,1)S(1)} %get-tuple-element.106), channel_id=1, source_target_pairs={{0,2},{1,3},{2,0},{3,1},{4,6},{5,7},{6,4},{7,5},{8,10},{9,11},{10,... | collective-permute-start | bytes 393224 | tf_op jit(solution)/shard_map/ppermute | solution.py:557
  9.3 1.2 copy-start.1
  13.8 11.5 %copy-start.3 = (bf16[128,1024]{1,0:T(8,128)(2,1)S(1)}, bf16[128,1024]{1,0:T(8,128)(2,1)}, u32[]{:S(2)}) copy-start(bf16[128,1024]{1,0:T(8,128)(2,1)} %gradient.1) | copy-start | bytes 786436
  13.8 66.2 %collective-permute-start.1 = (bf16[2048,512]{1,0:T(8,128)(2,1)}, bf16[2048,512]{1,0:T(8,128)(2,1)}, u32[]{:S(2)}, u32[]{:S(2)}) collective-permute-start(bf16[2048,512]{1,0:T(8,128)(2,1)} %for_pair.1), channel_id=1, source_target_pairs={{0,2},{1,3},{2,0},{3,1},{4,6},{5,7},{6,4},{7,5},{8,10},{9,11},{10,... | collective-permute-start | bytes 6291464 | tf_op jit(solution)/shard_map/ppermute | solution.py:557
  15.2 32.1 %copy-start.8 = (s32[16]{0:T(128)S(1)}, s32[16]{0:T(128)}, u32[]{:S(2)}) copy-start(s32[16]{0:T(128)} %adapters.15) | copy-start | bytes 196
  15.2 32.1 %copy-start.9 = (s32[64]{0:T(128)S(1)}, s32[64]{0:T(128)}, u32[]{:S(2)}) copy-start(s32[64]{0:T(128)} %ranks.5) | copy-start | bytes 772
  17.6 26.6 %all-to-all-start = ((bf16[8,2,64,128]{3,2,1,0:T(8,128)(2,1)}), bf16[8,2,64,128]{3,2,1,0:T(8,128)(2,1)S(1)}, u32[]{:S(2)}, u32[]{:S(2)}) async-start(bf16[8,2,64,128]{3,2,1,0:T(8,128)(2,1)} %pad_maximum_fusion.1), calls=%async_computation | async-start | bytes 524288 | tf_op jit(solution)/shard_map/all_to_all | solution.py:541
  22.4 21.1 %collective-permute-start.3 = (bf16[2,128,512]{2,1,0:T(8,128)(2,1)}, bf16[2,128,512]{2,1,0:T(8,128)(2,1)S(1)}, u32[]{:S(2)}, u32[]{:S(2)}) collective-permute-start(bf16[2,128,512]{2,1,0:T(8,128)(2,1)} %pack_tokens.2), channel_id=1, source_target_pairs={{0,8},{1,9},{2,10},{3,11},{4,12},{5,13},{6,14},{7,15},{8,0},{9,1},... | collective-permute-start | bytes 786440 | tf_op jit(solution)/shard_map/ppermute | solution.py:557
  25.3 20.3 %collective-permute-start.7 = (bf16[1,128,1024]{2,1,0:T(8,128)(2,1)S(1)}, bf16[1,128,1024]{2,1,0:T(8,128)(2,1)S(1)}, u32[]{:S(2)}, u32[]{:S(2)}) collective-permute-start(bf16[1,128,1024]{2,1,0:T(8,128)(2,1)S(1)} %bitcast.5), channel_id=1, source_target_pairs={{0,4},{1,5},{2,6},{3,7},{4,0},{5,1},{6,2},{7,3},{8,12},{9,13},{10,... | collective-permute-start | bytes 786440 | tf_op jit(solution)/shard_map/ppermute | solution.py:557
  26.8 21.3 %collective-permute-start.8 = (bf16[1,128,1024]{2,1,0:T(8,128)(2,1)S(1)}, bf16[1,128,1024]{2,1,0:T(8,128)(2,1)S(1)}, u32[]{:S(2)}, u32[]{:S(2)}) collective-permute-start(bf16[1,128,1024]{2,1,0:T(8,128)(2,1)S(1)} %collective-permute-done.2.refs_1_), channel_id=1, source_target_pairs={{0,4},{1,5},{2,6},{3,7},{4,0},{5,1},{6,2},{7,3},{8,12},{9,13},{10,... | collective-permute-start | bytes 786440 | tf_op jit(solution)/shard_map/ppermute | solution.py:557
  43.5 0.7 copy-start.5
  44.6 35.4 %copy-start.2 = (bf16[1024,512]{1,0:T(8,128)(2,1)S(1)}, bf16[1024,512]{1,0:T(8,128)(2,1)}, u32[]{:S(2)}) copy-start(bf16[1024,512]{1,0:T(8,128)(2,1)} %refs_13_.1) | copy-start | bytes 3145732
  44.7 29.6 %collective-permute-start.10 = (bf16[2,128,512]{2,1,0:T(8,128)(2,1)S(1)}, bf16[2,128,512]{2,1,0:T(8,128)(2,1)S(1)}, u32[]{:S(2)}, u32[]{:S(2)}) collective-permute-start(bf16[2,128,512]{2,1,0:T(8,128)(2,1)S(1)} %get-tuple-element.116), channel_id=1, source_target_pairs={{0,4},{1,5},{2,6},{3,7},{4,0},{5,1},{6,2},{7,3},{8,12},{9,13},{10,... | collective-permute-start | bytes 786440 | tf_op jit(solution)/shard_map/ppermute | solution.py:557
  44.7 29.5 %collective-permute-start.11 = (bf16[2,128,512]{2,1,0:T(8,128)(2,1)S(1)}, bf16[2,128,512]{2,1,0:T(8,128)(2,1)S(1)}, u32[]{:S(2)}, u32[]{:S(2)}) collective-permute-start(bf16[2,128,512]{2,1,0:T(8,128)(2,1)S(1)} %get-tuple-element.120), channel_id=1, source_target_pairs={{0,5},{1,4},{2,7},{3,6},{4,1},{5,0},{6,3},{7,2},{8,13},{9,12},{10,... | collective-permute-start | bytes 786440 | tf_op jit(solution)/shard_map/ppermute | solution.py:557
  45.7 28.6 %collective-permute-start.9 = (bf16[2,128,512]{2,1,0:T(8,128)(2,1)S(1)}, bf16[2,128,512]{2,1,0:T(8,128)(2,1)S(1)}, u32[]{:S(2)}, u32[]{:S(2)}) collective-permute-start(bf16[2,128,512]{2,1,0:T(8,128)(2,1)S(1)} %get-tuple-element.117), channel_id=1, source_target_pairs={{0,12},{1,13},{2,14},{3,15},{4,8},{5,9},{6,10},{7,11},{8,4},{9,5},... | collective-permute-start | bytes 786440 | tf_op jit(solution)/shard_map/ppermute | solution.py:557
  48.1 14.1 %collective-permute-start.4 = (bf16[1,128,128]{2,1,0:T(8,128)(2,1)S(1)}, bf16[1,128,128]{2,1,0:T(8,128)(2,1)S(1)}, u32[]{:S(2)}, u32[]{:S(2)}) collective-permute-start(bf16[1,128,128]{2,1,0:T(8,128)(2,1)S(1)} %back_low.1), channel_id=1, source_target_pairs={{0,4},{1,5},{2,6},{3,7},{4,0},{5,1},{6,2},{7,3},{8,12},{9,13},{10,... | collective-permute-start | bytes 98312 | tf_op jit(solution)/shard_map/ppermute | solution.py:557
  62.3 6.3 %collective-permute-start.5 = (bf16[1,128,128]{2,1,0:T(8,128)(2,1)S(1)}, bf16[1,128,128]{2,1,0:T(8,128)(2,1)S(1)}, u32[]{:S(2)}, u32[]{:S(2)}) collective-permute-start(bf16[1,128,128]{2,1,0:T(8,128)(2,1)S(1)} %back_low.1), channel_id=1, source_target_pairs={{0,8},{1,9},{2,10},{3,11},{4,12},{5,13},{6,14},{7,15},{8,0},{9,1},... | collective-permute-start | bytes 98312 | tf_op jit(solution)/shard_map/ppermute | solution.py:557
  68.6 5.7 %collective-permute-start.6 = (bf16[1,128,128]{2,1,0:T(8,128)(2,1)S(1)}, bf16[1,128,128]{2,1,0:T(8,128)(2,1)S(1)}, u32[]{:S(2)}, u32[]{:S(2)}) collective-permute-start(bf16[1,128,128]{2,1,0:T(8,128)(2,1)S(1)} %back_low.1), channel_id=1, source_target_pairs={{0,12},{1,13},{2,14},{3,15},{4,8},{5,9},{6,10},{7,11},{8,4},{9,5},... | collective-permute-start | bytes 98312 | tf_op jit(solution)/shard_map/ppermute | solution.py:557
  74.4 5.6 %collective-permute-start.13 = (bf16[4,128,1024]{2,1,0:T(8,128)(2,1)S(1)}, bf16[4,128,1024]{2,1,0:T(8,128)(2,1)S(1)}, u32[]{:S(2)}, u32[]{:S(2)}) collective-permute-start(bf16[4,128,1024]{2,1,0:T(8,128)(2,1)S(1)} %pad_maximum_fusion), channel_id=1, source_target_pairs={{0,1},{1,0},{2,3},{3,2},{4,5},{5,4},{6,7},{7,6},{8,9},{9,8},{10,11... | collective-permute-start | bytes 3145736 | tf_op jit(solution)/shard_map/ppermute | solution.py:557
  74.5 2.8 %collective-permute-start.12 = (bf16[4,128,128]{2,1,0:T(8,128)(2,1)S(1)}, bf16[4,128,128]{2,1,0:T(8,128)(2,1)S(1)}, u32[]{:S(2)}, u32[]{:S(2)}) collective-permute-start(bf16[4,128,128]{2,1,0:T(8,128)(2,1)S(1)} %pad_maximum_fusion.2), channel_id=1, source_target_pairs={{0,1},{1,0},{2,3},{3,2},{4,5},{5,4},{6,7},{7,6},{8,9},{9,8},{10,11... | collective-permute-start | bytes 393224 | tf_op jit(solution)/shard_map/ppermute | solution.py:557
  75.1 10.4 %collective-permute-start.14 = (bf16[2,128,512]{2,1,0:T(8,128)(2,1)S(1)}, bf16[2,128,512]{2,1,0:T(8,128)(2,1)S(1)}, u32[]{:S(2)}, u32[]{:S(2)}) collective-permute-start(bf16[2,128,512]{2,1,0:T(8,128)(2,1)S(1)} %get-tuple-element.141), channel_id=1, source_target_pairs={{0,1},{1,0},{2,3},{3,2},{4,5},{5,4},{6,7},{7,6},{8,9},{9,8},{10,11... | collective-permute-start | bytes 786440 | tf_op jit(solution)/shard_map/ppermute | solution.py:557
  75.2 20.4 %collective-permute-start.15 = (bf16[2,128,512]{2,1,0:T(8,128)(2,1)S(1)}, bf16[2,128,512]{2,1,0:T(8,128)(2,1)S(1)}, u32[]{:S(2)}, u32[]{:S(2)}) collective-permute-start(bf16[2,128,512]{2,1,0:T(8,128)(2,1)S(1)} %get-tuple-element.142), channel_id=1, source_target_pairs={{0,9},{1,8},{2,11},{3,10},{4,13},{5,12},{6,15},{7,14},{8,1},{9,0},... | collective-permute-start | bytes 786440 | tf_op jit(solution)/shard_map/ppermute | solution.py:557
  77.3 18.3 %collective-permute-start.16 = (bf16[2,128,512]{2,1,0:T(8,128)(2,1)S(1)}, bf16[2,128,512]{2,1,0:T(8,128)(2,1)S(1)}, u32[]{:S(2)}, u32[]{:S(2)}) collective-permute-start(bf16[2,128,512]{2,1,0:T(8,128)(2,1)S(1)} %get-tuple-element.144), channel_id=1, source_target_pairs={{0,13},{1,12},{2,15},{3,14},{4,9},{5,8},{6,11},{7,10},{8,5},{9,4},... | collective-permute-start | bytes 786440 | tf_op jit(solution)/shard_map/ppermute | solution.py:557
  80.0 15.6 %copy-start.6 = (bf16[2,128,512]{2,1,0:T(8,128)(2,1)S(1)}, bf16[2,128,512]{2,1,0:T(8,128)(2,1)}, u32[]{:S(2)}) copy-start(bf16[2,128,512]{2,1,0:T(8,128)(2,1)} %copy-done.5) | copy-start | bytes 786436
  98.9 21.2 %collective-permute-start.19 = (bf16[4,128,512]{2,1,0:T(8,128)(2,1)S(1)}, bf16[4,128,512]{2,1,0:T(8,128)(2,1)S(1)}, u32[]{:S(2)}, u32[]{:S(2)}) collective-permute-start(bf16[4,128,512]{2,1,0:T(8,128)(2,1)S(1)} %get-tuple-element.166), channel_id=1, source_target_pairs={{0,2},{1,3},{2,0},{3,1},{4,6},{5,7},{6,4},{7,5},{8,10},{9,11},{10,... | collective-permute-start | bytes 1572872 | tf_op jit(solution)/shard_map/ppermute | solution.py:557
  100.5 7.1 %collective-permute-start.17 = (f32[4,128,128]{2,1,0:T(8,128)S(1)}, f32[4,128,128]{2,1,0:T(8,128)S(1)}, u32[]{:S(2)}, u32[]{:S(2)}) collective-permute-start(f32[4,128,128]{2,1,0:T(8,128)S(1)} %slice.3), channel_id=1, source_target_pairs={{0,1},{1,0},{2,3},{3,2},{4,5},{5,4},{6,7},{7,6},{8,9},{9,8},{10,11... | collective-permute-start | bytes 786440 | tf_op jit(solution)/shard_map/ppermute | solution.py:557
  100.8 19.4 %collective-permute-start.18 = (bf16[2,128,512]{2,1,0:T(8,128)(2,1)S(1)}, bf16[2,128,512]{2,1,0:T(8,128)(2,1)S(1)}, u32[]{:S(2)}, u32[]{:S(2)}) collective-permute-start(bf16[2,128,512]{2,1,0:T(8,128)(2,1)S(1)} %get-tuple-element.158), channel_id=1, source_target_pairs={{0,8},{1,9},{2,10},{3,11},{4,12},{5,13},{6,14},{7,15},{8,0},{9,1},... | collective-permute-start | bytes 786440 | tf_op jit(solution)/shard_map/ppermute | solution.py:557
  120.2 35.5 %collective-permute-start.26 = (bf16[4,128,512]{2,1,0:T(8,128)(2,1)S(1)}, bf16[4,128,512]{2,1,0:T(8,128)(2,1)S(1)}, u32[]{:S(2)}, u32[]{:S(2)}) collective-permute-start(bf16[4,128,512]{2,1,0:T(8,128)(2,1)S(1)} %get-tuple-element.179), channel_id=1, source_target_pairs={{0,2},{1,3},{2,0},{3,1},{4,6},{5,7},{6,4},{7,5},{8,10},{9,11},{10,... | collective-permute-start | bytes 1572872 | tf_op jit(solution)/shard_map/ppermute | solution.py:557
  120.7 35.0 %collective-permute-start.23 = (bf16[2,128,512]{2,1,0:T(8,128)(2,1)S(1)}, bf16[2,128,512]{2,1,0:T(8,128)(2,1)S(1)}, u32[]{:S(2)}, u32[]{:S(2)}) collective-permute-start(bf16[2,128,512]{2,1,0:T(8,128)(2,1)S(1)} %get-tuple-element.172), channel_id=1, source_target_pairs={{0,12},{1,13},{2,14},{3,15},{4,8},{5,9},{6,10},{7,11},{8,4},{9,5},... | collective-permute-start | bytes 786440 | tf_op jit(solution)/shard_map/ppermute | solution.py:557
  122.3 33.4 %collective-permute-start.24 = (bf16[2,128,512]{2,1,0:T(8,128)(2,1)S(1)}, bf16[2,128,512]{2,1,0:T(8,128)(2,1)S(1)}, u32[]{:S(2)}, u32[]{:S(2)}) collective-permute-start(bf16[2,128,512]{2,1,0:T(8,128)(2,1)S(1)} %get-tuple-element.173), channel_id=1, source_target_pairs={{0,4},{1,5},{2,6},{3,7},{4,0},{5,1},{6,2},{7,3},{8,12},{9,13},{10,... | collective-permute-start | bytes 786440 | tf_op jit(solution)/shard_map/ppermute | solution.py:557
  122.3 33.4 %collective-permute-start.25 = (bf16[2,128,512]{2,1,0:T(8,128)(2,1)S(1)}, bf16[2,128,512]{2,1,0:T(8,128)(2,1)S(1)}, u32[]{:S(2)}, u32[]{:S(2)}) collective-permute-start(bf16[2,128,512]{2,1,0:T(8,128)(2,1)S(1)} %get-tuple-element.174), channel_id=1, source_target_pairs={{0,5},{1,4},{2,7},{3,6},{4,1},{5,0},{6,3},{7,2},{8,13},{9,12},{10,... | collective-permute-start | bytes 786440 | tf_op jit(solution)/shard_map/ppermute | solution.py:557
  122.9 19.5 %collective-permute-start.20 = (f32[1,128,128]{2,1,0:T(8,128)S(1)}, f32[1,128,128]{2,1,0:T(8,128)S(1)}, u32[]{:S(2)}, u32[]{:S(2)}) collective-permute-start(f32[1,128,128]{2,1,0:T(8,128)S(1)} %get-tuple-element.169), channel_id=1, source_target_pairs={{0,4},{1,5},{2,6},{3,7},{4,0},{5,1},{6,2},{7,3},{8,12},{9,13},{10,... | collective-permute-start | bytes 196616 | tf_op jit(solution)/shard_map/ppermute | solution.py:557
  142.4 5.7 %collective-permute-start.21 = (f32[1,128,128]{2,1,0:T(8,128)S(1)}, f32[1,128,128]{2,1,0:T(8,128)S(1)}, u32[]{:S(2)}, u32[]{:S(2)}) collective-permute-start(f32[1,128,128]{2,1,0:T(8,128)S(1)} %get-tuple-element.170), channel_id=1, source_target_pairs={{0,8},{1,9},{2,10},{3,11},{4,12},{5,13},{6,14},{7,15},{8,0},{9,1},... | collective-permute-start | bytes 196616 | tf_op jit(solution)/shard_map/ppermute | solution.py:557
  148.1 6.1 %collective-permute-start.22 = (f32[1,128,128]{2,1,0:T(8,128)S(1)}, f32[1,128,128]{2,1,0:T(8,128)S(1)}, u32[]{:S(2)}, u32[]{:S(2)}) collective-permute-start(f32[1,128,128]{2,1,0:T(8,128)S(1)} %get-tuple-element.171), channel_id=1, source_target_pairs={{0,12},{1,13},{2,14},{3,15},{4,8},{5,9},{6,10},{7,11},{8,4},{9,5},... | collective-permute-start | bytes 196616 | tf_op jit(solution)/shard_map/ppermute | solution.py:557
  154.1 8.0 %collective-permute-start.33 = (bf16[8,128,128]{2,1,0:T(8,128)(2,1)S(1)}, bf16[8,128,128]{2,1,0:T(8,128)(2,1)S(1)}, u32[]{:S(2)}, u32[]{:S(2)}) collective-permute-start(bf16[8,128,128]{2,1,0:T(8,128)(2,1)S(1)} %constant_dynamic-update-slice_fusion.backs), channel_id=1, source_target_pairs={{0,2},{1,3},{2,0},{3,1},{4,6},{5,7},{6,4},{7,5},{8,10},{9,11},{10,... | collective-permute-start | bytes 786440 | tf_op jit(solution)/shard_map/ppermute | solution.py:557
  155.7 14.3 %collective-permute-start.30 = (bf16[2,128,512]{2,1,0:T(8,128)(2,1)S(1)}, bf16[2,128,512]{2,1,0:T(8,128)(2,1)S(1)}, u32[]{:S(2)}, u32[]{:S(2)}) collective-permute-start(bf16[2,128,512]{2,1,0:T(8,128)(2,1)S(1)} %get-tuple-element.185), channel_id=1, source_target_pairs={{0,9},{1,8},{2,11},{3,10},{4,13},{5,12},{6,15},{7,14},{8,1},{9,0},... | collective-permute-start | bytes 786440 | tf_op jit(solution)/shard_map/ppermute | solution.py:557
  155.8 14.2 %collective-permute-start.31 = (bf16[2,128,512]{2,1,0:T(8,128)(2,1)S(1)}, bf16[2,128,512]{2,1,0:T(8,128)(2,1)S(1)}, u32[]{:S(2)}, u32[]{:S(2)}) collective-permute-start(bf16[2,128,512]{2,1,0:T(8,128)(2,1)S(1)} %get-tuple-element.186), channel_id=1, source_target_pairs={{0,1},{1,0},{2,3},{3,2},{4,5},{5,4},{6,7},{7,6},{8,9},{9,8},{10,11... | collective-permute-start | bytes 786440 | tf_op jit(solution)/shard_map/ppermute | solution.py:557
  155.8 14.2 %collective-permute-start.32 = (bf16[8,128,128]{2,1,0:T(8,128)(2,1)S(1)}, bf16[8,128,128]{2,1,0:T(8,128)(2,1)S(1)}, u32[]{:S(2)}, u32[]{:S(2)}) collective-permute-start(bf16[8,128,128]{2,1,0:T(8,128)(2,1)S(1)} %get-tuple-element.188), channel_id=1, source_target_pairs={{0,2},{1,3},{2,0},{3,1},{4,6},{5,7},{6,4},{7,5},{8,10},{9,11},{10,... | collective-permute-start | bytes 786440 | tf_op jit(solution)/shard_map/ppermute | solution.py:557
  157.0 5.4 %collective-permute-start.27 = (bf16[1,128,128]{2,1,0:T(8,128)(2,1)S(1)}, bf16[1,128,128]{2,1,0:T(8,128)(2,1)S(1)}, u32[]{:S(2)}, u32[]{:S(2)}) collective-permute-start(bf16[1,128,128]{2,1,0:T(8,128)(2,1)S(1)} %hidden_low.1), channel_id=1, source_target_pairs={{0,4},{1,5},{2,6},{3,7},{4,0},{5,1},{6,2},{7,3},{8,12},{9,13},{10,... | collective-permute-start | bytes 98312 | tf_op jit(solution)/shard_map/ppermute | solution.py:557
  162.1 6.9 %collective-permute-start.28 = (bf16[1,128,128]{2,1,0:T(8,128)(2,1)S(1)}, bf16[1,128,128]{2,1,0:T(8,128)(2,1)S(1)}, u32[]{:S(2)}, u32[]{:S(2)}) collective-permute-start(bf16[1,128,128]{2,1,0:T(8,128)(2,1)S(1)} %hidden_low.1), channel_id=1, source_target_pairs={{0,8},{1,9},{2,10},{3,11},{4,12},{5,13},{6,14},{7,15},{8,0},{9,1},... | collective-permute-start | bytes 98312 | tf_op jit(solution)/shard_map/ppermute | solution.py:557
  162.3 6.7 %collective-permute-start.29 = (bf16[1,128,128]{2,1,0:T(8,128)(2,1)S(1)}, bf16[1,128,128]{2,1,0:T(8,128)(2,1)S(1)}, u32[]{:S(2)}, u32[]{:S(2)}) collective-permute-start(bf16[1,128,128]{2,1,0:T(8,128)(2,1)S(1)} %hidden_low.1), channel_id=1, source_target_pairs={{0,12},{1,13},{2,14},{3,15},{4,8},{5,9},{6,10},{7,11},{8,4},{9,5},... | collective-permute-start | bytes 98312 | tf_op jit(solution)/shard_map/ppermute | solution.py:557
  170.0 1.4 collective-permute-start.35
  171.5 9.2 %collective-permute-start.36 = (bf16[8,128,128]{2,1,0:T(8,128)(2,1)S(1)}, bf16[8,128,128]{2,1,0:T(8,128)(2,1)S(1)}, u32[]{:S(2)}, u32[]{:S(2)}) collective-permute-start(bf16[8,128,128]{2,1,0:T(8,128)(2,1)S(1)} %constant_dynamic-update-slice_fusion.5.hiddens), channel_id=1, source_target_pairs={{0,2},{1,3},{2,0},{3,1},{4,6},{5,7},{6,4},{7,5},{8,10},{9,11},{10,... | collective-permute-start | bytes 786440 | tf_op jit(solution)/shard_map/ppermute | solution.py:557
  172.0 12.3 %collective-permute-start.34 = (bf16[2,128,512]{2,1,0:T(8,128)(2,1)S(1)}, bf16[2,128,512]{2,1,0:T(8,128)(2,1)S(1)}, u32[]{:S(2)}, u32[]{:S(2)}) collective-permute-start(bf16[2,128,512]{2,1,0:T(8,128)(2,1)S(1)} %get-tuple-element.189), channel_id=1, source_target_pairs={{0,13},{1,12},{2,15},{3,14},{4,9},{5,8},{6,11},{7,10},{8,5},{9,4},... | collective-permute-start | bytes 786440 | tf_op jit(solution)/shard_map/ppermute | solution.py:557

commit v10 on v7

--- a/solution.py
+++ b/solution.py
@@ -141,28 +141,32 @@
     )
 
 
-def pack_kernel(place, tokens, *refs):
+def pack_kernel(place, tokens, *refs, flips):
     outs, sems = refs[:-1], refs[-1]
-    members = len(outs)
     width = outs[0].shape[2]
     copies = []
-    for slot in range(members):
+    for number, out in enumerate(outs):
         for half in range(2):
-            column = (place[0] ^ line_offset(slot, members) ^ (half * pair_bit)) * width
+            column = (place[0] ^ flips[number] ^ (half * pair_bit)) * width
             copies.append(
                 pltpu.make_async_copy(
                     tokens.at[:, pl.ds(pl.multiple_of(column, width), width)],
-                    outs[slot].at[half],
-                    sems.at[2 * slot + half],
+                    out.at[half],
+                    sems.at[2 * number + half],
                 )
             )
     run(copies)
 
 
-def pack_tokens(place, tokens, members, width):
+def pack_tokens(place, tokens, flips, width):
     shape = jax.ShapeDtypeStruct((2, tokens.shape[0], width), tokens.dtype)
     return copy_call(
-        pack_kernel, "pack_tokens", (place,), (tokens,), [shape] * members, 2 * members
+        functools.partial(pack_kernel, flips=flips),
+        "pack_tokens",
+        (place,),
+        (tokens,),
+        [shape] * len(flips),
+        2 * len(flips),
     )
 
 
@@ -203,16 +207,19 @@
 
 def input_kernel(adapters, place, backs, pair, *refs):
     members, rows, _ = backs.shape
-    gradients, downs = refs[:members], refs[members : 2 * members]
-    weight = refs[2 * members]
-    outs, columns = refs[2 * members + 1 : -2], refs[-2:]
+    apart = members // 2
+    gradients = [ref.at[0] for ref in refs[:apart]]
+    gradients += [refs[apart].at[slot] for slot in range(members - apart)]
+    downs = refs[apart + 1 : apart + 1 + members]
+    weight = refs[apart + 1 + members]
+    outs, columns = refs[apart + 2 + members : -2], refs[-2:]
     extent = downs[0].shape[1]
     lanes = columns[0].shape[2]
-    value_width = gradients[0].shape[2] // (2 * members)
+    value_width = gradients[0].shape[1] // (2 * members)
     some = min(4, members)
     for first in range(0, members, some):
         slots = range(first, first + some)
-        lines = jnp.concatenate([gradients[slot][0] for slot in slots], axis=0)
+        lines = jnp.concatenate([gradients[slot][...] for slot in slots], axis=0)
         for half in range(2):
             right = weight[...] if half == 0 else pair[members * extent :]
             frozen = jnp.dot(lines, right, preferred_element_type=jnp.float32)
@@ -226,7 +233,7 @@
         column = (place[0] ^ (side * pair_bit)) * value_width // lanes * lanes
         for slot in range(members):
             entry = entry_of(place[0], slot, members)
-            columns[side][entry] = gradients[slot][0, :, pl.ds(pl.multiple_of(column, lanes), lanes)]
+            columns[side][entry] = gradients[slot][:, pl.ds(pl.multiple_of(column, lanes), lanes)]
 
 
 def input_slices(adapters, place, gradients, backs, weight, pair, down_maps):
@@ -241,7 +248,7 @@
         (adapters, place),
         [backs, pair] + list(gradients) + [down_maps] * members + [weight],
         [whole(backs.shape), whole(pair.shape)]
-        + [whole(gradients[0].shape)] * members
+        + [whole(gradient.shape) for gradient in gradients]
         + [picked(down_maps, line_offset(slot, members)) for slot in range(members)]
         + [whole(weight.shape)],
         [shape] * members + [columns] * 2,
@@ -546,11 +553,9 @@
     barrier = lax.optimization_barrier
 
     far = [slot for slot in range(members) if slot % 2]
+    quarter = max(1, len(far) // 4)
+    far = [far[at : at + quarter] for at in range(0, len(far), quarter)]
     near = [slot for slot in range(2, members, 2)]
-    quarter = max(1, len(far) // 4)
-    portions = [far[at : at + quarter] for at in range(0, len(far), quarter)]
-    portions[2] = portions[2] + near[: len(near) // 2]
-    portions[3] = portions[3] + near[len(near) // 2 :]
 
     def send(packs, portion):
         return {slot: swap(packs[slot], offsets[slot]) for slot in portion}
@@ -559,60 +564,74 @@
         return [pieces[slot] for slot in portion]
 
     own_gradient = output_gradient.reshape(1, rows, depth)
-    gradients = [own_gradient] + [None] * (members - 1)
-    for step in range(steps):
+    gradients = [own_gradient] + [None] * (lines - 1)
+    for step in range(steps - 1):
         gradients[1 << step] = swap(own_gradient, offsets[1 << step])
     ups, ups_pair = gather_up(adapters, place, up_maps, members)
     ups_other = swap(ups_pair, pair_bit)
     pair = for_pair(adapters, place, value_weight, down_maps, members)
     ups_other, pair = barrier((ups_other, pair))
     pair = swap(pair, pair_bit)
+    packs = dict(zip(far[0], pack_tokens(place, tokens, taken(offsets, far[0]), width)))
+    firsts = [gradients[1 << step] for step in range(steps - 1)]
+    firsts, ups_other, packs = barrier((firsts, ups_other, packs))
+    for step in range(steps - 1):
+        gradients[1 << step] = firsts[step]
+
     ups = exchange_side(jnp.stack([ups, ups_other], axis=1))
-    packs = pack_tokens(place, tokens, members, width)
-    gradients[1], packs = barrier((gradients[1], packs))
-    arrived = {0: packs[0]}
-    arrived.update(send(packs, portions[0]))
-    for step in range(1, steps):
+    arrived = send(packs, far[0])
+    for step in range(1, steps - 1):
         for slot in range(1, 1 << step):
             gradients[slot + (1 << step)] = swap(gradients[slot], offsets[1 << step])
-    gradients[: members // 2], ups, packs = barrier((gradients[: members // 2], ups, packs))
-
+    ups, tokens, done = barrier((ups, tokens, taken(arrived, far[0])))
+    arrived.update(zip(far[0], done))
+
+    rest = [slot for slot in range(members) if slot not in far[0]]
+    packs = dict(zip(rest, pack_tokens(place, tokens, taken(offsets, rest), width)))
+    arrived[0] = packs[0]
     backs = exchange_line(back_rows(adapters, place, ranks, output_gradient, ups))
-    backs, gradients, packs, done = barrier(
-        (backs, gradients, packs, taken(arrived, portions[0]))
-    )
-    arrived.update(zip(portions[0], done))
-    for portion in portions[1:]:
-        arrived.update(send(packs, portion))
+    window = far[1] + near[:1]
+    arrived.update(send(packs, window))
+    backs, gradients, packs, done = barrier((backs, gradients, packs, taken(arrived, window)))
+    arrived.update(zip(window, done))
+
     backs = both_cores(backs)
+    gradients.append(swap(jnp.concatenate(gradients, axis=0), 1))
+    arrived.update(send(packs, near[1:] + far[2] + far[3]))
     *slices, columns, columns_pair = input_slices(
         adapters, place, gradients, backs, value_weight, pair, down_maps
     )
+    slices, arrived = barrier((slices, taken(arrived, range(members))))
+
+    parts, tokens_own, tokens_pair = hidden_parts(adapters, place, down_maps, pair, arrived)
     results = {0: slices[0]}
-    results.update(send(slices, portions[0]))
+    window = near[:1] + far[0] + far[1]
+    results.update(send(slices, window))
+    tokens_other = swap(tokens_pair, pair_bit)
+    parts = exchange_line(parts[:lines] + swap(parts[lines:], 1))
+    parts, done, slices, tokens_other, columns_pair = barrier(
+        (parts, taken(results, window), slices, tokens_other, columns_pair)
+    )
+    results.update(zip(window, done))
+
+    window = near[1:2] + far[2]
+    results.update(send(slices, window))
+    hiddens = exchange_line(hidden_rows(adapters, place, ranks, parts))
     columns_other = swap(columns_pair, pair_bit)
     backs_pair = swap(backs, pair_bit)
-    slices, arrived = barrier((slices, taken(arrived, range(members))))
-    parts, tokens_own, tokens_pair = hidden_parts(adapters, place, down_maps, pair, arrived)
-    parts = parts[:lines] + swap(parts[lines:], 1)
-    parts, done = barrier((parts, taken(results, portions[0])))
-    results.update(zip(portions[0], done))
-    hiddens = exchange_line(
-        hidden_rows(adapters, place, ranks, exchange_line(parts))
-    )
-    hiddens, slices, columns_other, backs_pair, tokens_pair = barrier(
-        (hiddens, slices, columns_other, backs_pair, tokens_pair)
-    )
-    for portion in portions[1:]:
-        results.update(send(slices, portion))
+    hiddens, done, slices, columns_other, backs_pair = barrier(
+        (hiddens, taken(results, window), slices, columns_other, backs_pair)
+    )
+    results.update(zip(window, done))
+
+    results.update(send(slices, near[2:] + far[3]))
     hiddens = both_cores(hiddens)
     hiddens_pair = swap(hiddens, pair_bit)
-    tokens_other = swap(tokens_pair, pair_bit)
+    down_gradient = down_gradients(
+        adapters, place, backs, backs_pair, tokens_own, tokens_other, num_adapters
+    )
     up_gradient = up_gradients(
         adapters, place, ranks, columns, columns_other, hiddens, hiddens_pair, depth // devices
-    )
-    down_gradient = down_gradients(
-        adapters, place, backs, backs_pair, tokens_own, tokens_other, num_adapters
     )
 
     def joined(slots, before=None):
@@ -620,9 +639,9 @@
             place, taken(results, slots), taken(offsets, slots), tokens.shape[1], before
         )
 
-    most = joined([0] + portions[0] + portions[1] + portions[2])
+    most = joined([slot for slot in range(members) if slot not in far[3]])
     up_gradient, down_gradient, most = barrier((up_gradient, down_gradient, most))
-    input_grad = joined(portions[3], most)
+    input_grad = joined(far[3], most)
     return (input_grad, down_gradient, up_gradient)
 
 

time: 177 us -> 171 us (0.966)
  waiting for transfers between devices: 82.8 us -> 71.9 us
  starting transfers between devices: 50 us -> 53.1 us
  local copies, waits for them, and re-layouts: 11.3 us -> 8.41 us
  Pallas kernels: 29.2 us -> 31.3 us
    ppermute x30 -> x27, waiting for transfers between devices: 65.5 us -> 52.7 us  [swap(): return lax.ppermute(array, 'dp', [(i, i ^ flip) for i in range(devices)])]
    all_to_all x4, starting transfers between devices: 15.1 us -> 19.9 us  [exchange(): lax.all_to_all(pieces, 'dp', split_axis=0, concat_axis=0, axis_index_grou...]
    unnamed x68 -> x54, local copies, waits for them, and re-layouts: 11.2 us -> 8.35 us
    all_to_all x4, waiting for transfers between devices: 17.3 us -> 19.2 us  [exchange(): lax.all_to_all(pieces, 'dp', split_axis=0, concat_axis=0, axis_index_grou...]
    ppermute x30 -> x27, starting transfers between devices: 34.9 us -> 33.2 us  [swap(): return lax.ppermute(array, 'dp', [(i, i ^ flip) for i in range(devices)])]
    pallas_call x3 -> x4, Pallas kernels: 5.69 us -> 4.83 us  [copy_call(): pl.pallas_call(kernel, out_shape=out_shapes, grid_spec=pltpu.PrefetchScal...]
  transfers between devices with their start and end apart: 34 -> 31, of which waited for: 13 -> 13; matrix products, arithmetic and copies ran while one was open for 1% -> 1% of each run, Pallas kernels for 14% -> 16%
where the time goes in v10:
time: 171 us; the launch traced here: 168 us
  waiting for transfers between devices  71.9 us (42%)
  starting transfers between devices  53.1 us (31%)
  Pallas kernels  31.3 us (18%)
  local copies, waits for them, and re-layouts  8.41 us (5%)
  other arithmetic  2.71 us (2%)
    ppermute x27, waiting for transfers between devices, swap(): return lax.ppermute(array, 'dp', [(i, i ^ flip) for i in range(devices)])  52.7 us
    ppermute x27, starting transfers between devices, swap(): return lax.ppermute(array, 'dp', [(i, i ^ flip) for i in range(devices)])  33.2 us
    all_to_all x4, starting transfers between devices, exchange(): lax.all_to_all(pieces, 'dp', split_axis=0, concat_axis=0, axis_index_grou...  19.9 us
    all_to_all x4, waiting for transfers between devices, exchange(): lax.all_to_all(pieces, 'dp', split_axis=0, concat_axis=0, axis_index_grou...  19.2 us
    pallas_call x4, Pallas kernels, call(): pl.pallas_call(kernel, out_shape=out_shapes, grid_spec=pltpu.PrefetchScal...  13.2 us
    pallas_call x2, Pallas kernels, sums_call(): pl.pallas_call(kernel, out_shape=jax.ShapeDtypeStruct((num_adapters,) + p...  10.2 us
    unnamed x54, local copies, waits for them, and re-layouts  8.35 us
    pallas_call x4, Pallas kernels, copy_call(): pl.pallas_call(kernel, out_shape=out_shapes, grid_spec=pltpu.PrefetchScal...  4.83 us
  transfers between devices with their start and end apart: 31, of which 13 were waited for; matrix products, arithmetic and copies ran while one was open for 1% of the time, Pallas kernels for 16%

profile of v10, /device:TPU:0, one launch (start us, length us, event | category | flops | bytes accessed | tf_op | source)
XLA Modules:
  0.0 168.4 jit_solution(16964579687239100809)
XLA Ops:
  0.6 4.1 %collective-permute-start.2 = (bf16[1,128,1024]{2,1,0:T(8,128)(2,1)}, bf16[1,128,1024]{2,1,0:T(8,128)(2,1)}, u32[]{:S(2)}, u32[]{:S(2)}) collective-permute-start(bf16[1,128,1024]{2,1,0:T(8,128)(2,1)} %bitcast.4), channel_id=1, source_target_pairs={{0,8},{1,9},{2,10},{3,11},{4,12},{5,13},{6,14},{7,15},{8,0},{9,1},... | collective-permute-start | bytes 786440 | tf_op jit(solution)/shard_map/ppermute | solution.py:532
  4.7 1.6 collective-permute-start.3
  6.3 1.2 copy-done.5
  8.2 1.1 gather_up.1
  9.3 1.6 collective-permute-start
  10.9 1.6 copy-done
  12.6 2.1 %for_pair.1 = bf16[2048,512]{1,0:T(8,128)(2,1)S(1)} custom-call(s32[16]{0:T(128)S(1)} %copy-done.16, s32[1]{0:T(128)} %bitcast.place, bf16[1024,512]{1,0:T(8,128)(2,1)S(1)} %copy-done.2, bf16[64,128,512]{2,1,0:T(8,128)(2,1)} %refs_7_.3), custom_call_target="tpu_custom_call" | custom-call | tf_op jit(solution)/shard_map/for_pair/pallas_call | solution.py:74
  14.7 1.3 copy-done.4
  16.0 1.1 collective-permute-done.2.refs_1_
  17.3 0.7 pad_maximum_fusion.1
  18.0 4.5 %all-to-all-start = ((bf16[8,2,64,128]{3,2,1,0:T(8,128)(2,1)}), bf16[8,2,64,128]{3,2,1,0:T(8,128)(2,1)}, u32[]{:S(2)}, u32[]{:S(2)}) async-start(bf16[8,2,64,128]{3,2,1,0:T(8,128)(2,1)} %pad_maximum_fusion.1), calls=%async_computation | async-start | bytes 524288 | tf_op jit(solution)/shard_map/all_to_all | solution.py:509
  22.5 1.5 collective-permute-start.1
  24.0 2.9 %collective-permute-start.4 = (bf16[2,128,512]{2,1,0:T(8,128)(2,1)}, bf16[2,128,512]{2,1,0:T(8,128)(2,1)S(1)}, u32[]{:S(2)}, u32[]{:S(2)}) collective-permute-start(bf16[2,128,512]{2,1,0:T(8,128)(2,1)} %copy-done.14), channel_id=1, source_target_pairs={{0,8},{1,9},{2,10},{3,11},{4,12},{5,13},{6,14},{7,15},{8,0},{9,1},... | collective-permute-start | bytes 786440 | tf_op jit(solution)/shard_map/ppermute | solution.py:532
  27.0 1.5 collective-permute-start.5
  28.4 15.1 %collective-permute-done.4.refs_9_ = bf16[2,128,512]{2,1,0:T(8,128)(2,1)S(1)} collective-permute-done((bf16[2,128,512]{2,1,0:T(8,128)(2,1)}, bf16[2,128,512]{2,1,0:T(8,128)(2,1)S(1)}, u32[]{:S(2)}, u32[]{:S(2)}) %collective-permute-start.4) | collective-permute-done | bytes 262176 | tf_op jit(solution)/shard_map/ppermute | solution.py:532
  44.2 1.6 pack_tokens.3
  46.5 1.3 collective-permute-start.6
  47.8 2.4 %back_low.1 = bf16[4,128,128]{2,1,0:T(8,128)(2,1)} custom-call(s32[16]{0:T(128)S(1)} %copy-done.16, s32[1]{0:T(128)} %bitcast.place, s32[64]{0:T(128)S(1)} %copy-done.17, bf16[128,1024]{1,0:T(8,128)(2,1)S(1)} %copy-done.3, bf16[8,2,64,128]{3,2,1,0:T(8,128)(2,1)} %all-to-all-done.ups), custom_call_target="tpu_custom_call" | custom-call | tf_op jit(solution)/shard_map/back_low/pallas_call | solution.py:51
  50.2 4.4 %all-to-all-start.1 = ((bf16[4,128,128]{2,1,0:T(8,128)(2,1)}), bf16[4,128,128]{2,1,0:T(8,128)(2,1)S(1)}, u32[]{:S(2)}, u32[]{:S(2)}) async-start(bf16[4,128,128]{2,1,0:T(8,128)(2,1)} %back_low.1), calls=%async_computation.1 | async-start | bytes 262144 | tf_op jit(solution)/shard_map/all_to_all | solution.py:509
  54.6 9.1 %all-to-all-done.1 = bf16[4,128,128]{2,1,0:T(8,128)(2,1)S(1)} async-done(((bf16[4,128,128]{2,1,0:T(8,128)(2,1)}), bf16[4,128,128]{2,1,0:T(8,128)(2,1)S(1)}, u32[]{:S(2)}, u32[]{:S(2)}) %all-to-all-start.1) | async-done | bytes 131104 | tf_op jit(solution)/shard_map/all_to_all | solution.py:509
  63.7 1.2 pad_maximum_fusion
  65.6 1.3 collective-permute-start.11
  66.9 1.1 collective-permute-done.8
  68.0 0.7 collective-permute-start.12
  68.8 1.7 %collective-permute-start.13 = (bf16[2,128,512]{2,1,0:T(8,128)(2,1)}, bf16[2,128,512]{2,1,0:T(8,128)(2,1)S(1)}, u32[]{:S(2)}, u32[]{:S(2)}) collective-permute-start(bf16[2,128,512]{2,1,0:T(8,128)(2,1)} %get-tuple-element.117), channel_id=1, source_target_pairs={{0,13},{1,12},{2,15},{3,14},{4,9},{5,8},{6,11},{7,10},{8,5},{9,4},... | collective-permute-start | bytes 786440 | tf_op jit(solution)/shard_map/ppermute | solution.py:532
  70.9 5.5 %input_slices.1 = (bf16[2,128,512]{2,1,0:T(8,128)(2,1)S(1)}, bf16[2,128,512]{2,1,0:T(8,128)(2,1)S(1)}, bf16[2,128,512]{2,1,0:T(8,128)(2,1)S(1)}, bf16[2,128,512]...) custom-call(s32[16]{0:T(128)S(1)} %copy-done.16, ...), custom_call_target="tpu_custom_call" | custom-call | tf_op jit(solution)/shard_map/input_slices/pallas_call | solution.py:51
  77.1 3.4 %collective-permute-done.11.refs_13_ = bf16[2,128,512]{2,1,0:T(8,128)(2,1)S(1)} collective-permute-done((bf16[2,128,512]{2,1,0:T(8,128)(2,1)}, bf16[2,128,512]{2,1,0:T(8,128)(2,1)S(1)}, u32[]{:S(2)}, u32[]{:S(2)}) %collective-permute-start.11) | collective-permute-done | bytes 262176 | tf_op jit(solution)/shard_map/ppermute | solution.py:532
  80.5 6.7 %collective-permute-done.12.refs_14_ = bf16[2,128,512]{2,1,0:T(8,128)(2,1)S(1)} collective-permute-done((bf16[2,128,512]{2,1,0:T(8,128)(2,1)}, bf16[2,128,512]{2,1,0:T(8,128)(2,1)S(1)}, u32[]{:S(2)}, u32[]{:S(2)}) %collective-permute-start.12) | collective-permute-done | bytes 262176 | tf_op jit(solution)/shard_map/ppermute | solution.py:532
  87.3 4.1 %hidden_parts.1 = (f32[8,128,128]{2,1,0:T(8,128)S(1)}, bf16[8,128,512]{2,1,0:T(8,128)(2,1)S(1)}, bf16[8,128,512]{2,1,0:T(8,128)(2,1)}) custom-call(s32[16]{0:T(128)S(1)} %copy-done.16, s32[1]{0:T(128)} %bitcast.place, bf16[2048,512]{1,0:T(8,128)(2,1)} %collective-permute-done.1.pair, bf16[64,128,512]{2,1,0:T(8,128)(2,1)} %refs_7_.3, ...), custom_call_target="tpu_custom_call" | custom-call | tf_op jit(solution)/shard_map/hidden_parts/pallas_call | solution.py:51
  91.4 1.6 collective-permute-start.18
  93.1 1.5 collective-permute-done.14
  94.6 0.7 slice_add_fusion
  95.4 7.3 %all-to-all-start.2 = ((f32[4,128,128]{2,1,0:T(8,128)}), f32[4,128,128]{2,1,0:T(8,128)S(1)}, u32[]{:S(2)}, u32[]{:S(2)}) async-start(f32[4,128,128]{2,1,0:T(8,128)} %slice_add_fusion), calls=%async_computation.2 | async-start | bytes 524288 | tf_op jit(solution)/shard_map/all_to_all | solution.py:509
  102.7 2.0 %collective-permute-start.15 = (bf16[2,128,512]{2,1,0:T(8,128)(2,1)}, bf16[2,128,512]{2,1,0:T(8,128)(2,1)S(1)}, u32[]{:S(2)}, u32[]{:S(2)}) collective-permute-start(bf16[2,128,512]{2,1,0:T(8,128)(2,1)} %copy-done.25), channel_id=1, source_target_pairs={{0,4},{1,5},{2,6},{3,7},{4,0},{5,1},{6,2},{7,3},{8,12},{9,13},{10,... | collective-permute-start | bytes 786440 | tf_op jit(solution)/shard_map/ppermute | solution.py:532
  104.7 2.4 %collective-permute-start.16 = (bf16[2,128,512]{2,1,0:T(8,128)(2,1)}, bf16[2,128,512]{2,1,0:T(8,128)(2,1)S(1)}, u32[]{:S(2)}, u32[]{:S(2)}) collective-permute-start(bf16[2,128,512]{2,1,0:T(8,128)(2,1)} %copy-done.24), channel_id=1, source_target_pairs={{0,8},{1,9},{2,10},{3,11},{4,12},{5,13},{6,14},{7,15},{8,0},{9,1},... | collective-permute-start | bytes 786440 | tf_op jit(solution)/shard_map/ppermute | solution.py:532
  107.6 12.5 %collective-permute-done.15.refs_2_ = bf16[2,128,512]{2,1,0:T(8,128)(2,1)S(1)} collective-permute-done((bf16[2,128,512]{2,1,0:T(8,128)(2,1)}, bf16[2,128,512]{2,1,0:T(8,128)(2,1)S(1)}, u32[]{:S(2)}, u32[]{:S(2)}) %collective-permute-start.15) | collective-permute-done | bytes 262176 | tf_op jit(solution)/shard_map/ppermute | solution.py:532
  120.1 9.7 %collective-permute-done.16.refs_1_ = bf16[2,128,512]{2,1,0:T(8,128)(2,1)S(1)} collective-permute-done((bf16[2,128,512]{2,1,0:T(8,128)(2,1)}, bf16[2,128,512]{2,1,0:T(8,128)(2,1)S(1)}, u32[]{:S(2)}, u32[]{:S(2)}) %collective-permute-start.16) | collective-permute-done | bytes 262176 | tf_op jit(solution)/shard_map/ppermute | solution.py:532
  129.8 0.7 copy-done.10
  131.2 4.5 %collective-permute-start.20 = (bf16[2,128,512]{2,1,0:T(8,128)(2,1)}, bf16[2,128,512]{2,1,0:T(8,128)(2,1)}, u32[]{:S(2)}, u32[]{:S(2)}) collective-permute-start(bf16[2,128,512]{2,1,0:T(8,128)(2,1)} %copy-done.21), channel_id=1, source_target_pairs={{0,9},{1,8},{2,11},{3,10},{4,13},{5,12},{6,15},{7,14},{8,1},{9,0},... | collective-permute-start | bytes 786440 | tf_op jit(solution)/shard_map/ppermute | solution.py:532
  136.2 1.2 hidden_low.1
  137.4 3.7 %all-to-all-start.3 = ((bf16[4,128,128]{2,1,0:T(8,128)(2,1)}), bf16[4,128,128]{2,1,0:T(8,128)(2,1)S(1)}, u32[]{:S(2)}, u32[]{:S(2)}) async-start(bf16[4,128,128]{2,1,0:T(8,128)(2,1)} %hidden_low.1), calls=%async_computation.3 | async-start | bytes 262144 | tf_op jit(solution)/shard_map/all_to_all | solution.py:509
  141.1 10.1 %all-to-all-done.3 = bf16[4,128,128]{2,1,0:T(8,128)(2,1)S(1)} async-done(((bf16[4,128,128]{2,1,0:T(8,128)(2,1)}), bf16[4,128,128]{2,1,0:T(8,128)(2,1)S(1)}, u32[]{:S(2)}, u32[]{:S(2)}) %all-to-all-start.3) | async-done | bytes 131104 | tf_op jit(solution)/shard_map/all_to_all | solution.py:509
  151.5 1.1 collective-permute-done.24
  153.2 1.9 %collective-permute-start.23 = (bf16[2,128,512]{2,1,0:T(8,128)(2,1)}, bf16[2,128,512]{2,1,0:T(8,128)(2,1)S(1)}, u32[]{:S(2)}, u32[]{:S(2)}) collective-permute-start(bf16[2,128,512]{2,1,0:T(8,128)(2,1)} %copy-done.18), channel_id=1, source_target_pairs={{0,13},{1,12},{2,15},{3,14},{4,9},{5,8},{6,11},{7,10},{8,5},{9,4},... | collective-permute-start | bytes 786440 | tf_op jit(solution)/shard_map/ppermute | solution.py:532
  155.1 6.0 %down_gradients.1 = bf16[64,128,512]{2,1,0:T(8,128)(2,1)} custom-call(s32[16]{0:T(128)S(1)} %copy-done.16, s32[1]{0:T(128)} %bitcast.place, bf16[8,128,128]{2,1,0:T(8,128)(2,1)S(1)} %constant_dynamic-update-slice_fusion.backs, bf16[8,128,128]{2,1,0:T(8,128)(2,1)} %collective-permute-done.22.backs_pair, bf16[8,128,512]{2,1,0:T(8,128)(2,1)S(1)} %get-tuple-element.148.own, ...), custom_call_target="tpu_custom_call" | custom-call | tf_op jit(solution)/shard_map/down_gradients/pallas_call | solution.py:410
  161.2 2.4 %join_columns.2.refs_1_ = bf16[128,8192]{1,0:T(8,128)(2,1)} custom-call(s32[1]{0:T(128)} %bitcast.place, bf16[2,128,512]{2,1,0:T(8,128)(2,1)S(1)} %get-tuple-element.130.refs_0_, bf16[2,128,512]{2,1,0:T(8,128)(2,1)S(1)} %copy-done.11, bf16[2,128,512]{2,1,0:T(8,128)(2,1)S(1)} %collective-permute-done.15.refs_2_, bf16[2,128,512]{2,1,0:T(8,128)(2,1)S(1)} %copy-done.13, ...), custom_call_target="tpu_custom_call" | custom-call | tf_op jit(solution)/shard_map/join_columns/pallas_call | solution.py:341
  163.6 4.1 %up_gradients.1 = bf16[64,64,128]{2,1,0:T(8,128)(2,1)} custom-call(s32[16]{0:T(128)S(1)} %copy-done.16, s32[1]{0:T(128)} %bitcast.place, s32[64]{0:T(128)S(1)} %copy-done.17, bf16[8,128,128]{2,1,0:T(8,128)(2,1)S(1)} %get-tuple-element.144.gradients, bf16[8,128,128]{2,1,0:T(8,128)(2,1)} %collective-permute-done.21.gradients_pair, ...), custom_call_target="tpu_custom_call" | custom-call | tf_op jit(solution)/shard_map/up_gradients/pallas_call | solution.py:410
  167.7 0.7 join_columns.3
  (86 shorter events, 6.8 us)
Async XLA Ops:
  0.6 11.9 %copy-start.2 = (bf16[1024,512]{1,0:T(8,128)(2,1)S(1)}, bf16[1024,512]{1,0:T(8,128)(2,1)}, u32[]{:S(2)}) copy-start(bf16[1024,512]{1,0:T(8,128)(2,1)} %refs_13_.1) | copy-start | bytes 3145732
  0.6 16.5 %collective-permute-start.2 = (bf16[1,128,1024]{2,1,0:T(8,128)(2,1)}, bf16[1,128,1024]{2,1,0:T(8,128)(2,1)}, u32[]{:S(2)}, u32[]{:S(2)}) collective-permute-start(bf16[1,128,1024]{2,1,0:T(8,128)(2,1)} %bitcast.4), channel_id=1, source_target_pairs={{0,8},{1,9},{2,10},{3,11},{4,12},{5,13},{6,14},{7,15},{8,0},{9,1},... | collective-permute-start | bytes 786440 | tf_op jit(solution)/shard_map/ppermute | solution.py:532
  4.7 12.5 %collective-permute-start.3 = (bf16[1,128,1024]{2,1,0:T(8,128)(2,1)}, bf16[1,128,1024]{2,1,0:T(8,128)(2,1)}, u32[]{:S(2)}, u32[]{:S(2)}) collective-permute-start(bf16[1,128,1024]{2,1,0:T(8,128)(2,1)} %bitcast.5), channel_id=1, source_target_pairs={{0,4},{1,5},{2,6},{3,7},{4,0},{5,1},{6,2},{7,3},{8,12},{9,13},{10,... | collective-permute-start | bytes 786440 | tf_op jit(solution)/shard_map/ppermute | solution.py:532
  8.2 4.3 %copy-start.16 = (s32[16]{0:T(128)S(1)}, s32[16]{0:T(128)}, u32[]{:S(2)}) copy-start(s32[16]{0:T(128)} %adapters.15) | copy-start | bytes 196
  9.3 6.7 %collective-permute-start = (bf16[8,64,128]{2,1,0:T(8,128)(2,1)S(1)}, bf16[8,64,128]{2,1,0:T(8,128)(2,1)S(1)}, u32[]{:S(2)}, u32[]{:S(2)}) collective-permute-start(bf16[8,64,128]{2,1,0:T(8,128)(2,1)S(1)} %get-tuple-element.81), channel_id=1, source_target_pairs={{0,2},{1,3},{2,0},{3,1},{4,6},{5,7},{6,4},{7,5},{8,10},{9,11},{10,... | collective-permute-start | bytes 393224 | tf_op jit(solution)/shard_map/ppermute | solution.py:532
  12.6 2.1 %copy-start.14 = (bf16[2,128,512]{2,1,0:T(8,128)(2,1)}, bf16[2,128,512]{2,1,0:T(8,128)(2,1)S(1)}, u32[]{:S(2)}) copy-start(bf16[2,128,512]{2,1,0:T(8,128)(2,1)S(1)} %pack_tokens.2) | copy-start | bytes 786436
  12.6 31.6 %copy-start.1 = (bf16[128,8192]{1,0:T(8,128)(2,1)S(1)}, bf16[128,8192]{1,0:T(8,128)(2,1)}, u32[]{:S(2)}) copy-start(bf16[128,8192]{1,0:T(8,128)(2,1)} %tokens.2) | copy-start | bytes 6291460
  16.0 31.7 %copy-start.3 = (bf16[128,1024]{1,0:T(8,128)(2,1)S(1)}, bf16[128,1024]{1,0:T(8,128)(2,1)}, u32[]{:S(2)}) copy-start(bf16[128,1024]{1,0:T(8,128)(2,1)} %gradient.1) | copy-start | bytes 786436
  16.0 31.7 %copy-start.17 = (s32[64]{0:T(128)S(1)}, s32[64]{0:T(128)}, u32[]{:S(2)}) copy-start(s32[64]{0:T(128)} %ranks.5) | copy-start | bytes 772
  18.0 26.2 %all-to-all-start = ((bf16[8,2,64,128]{3,2,1,0:T(8,128)(2,1)}), bf16[8,2,64,128]{3,2,1,0:T(8,128)(2,1)}, u32[]{:S(2)}, u32[]{:S(2)}) async-start(bf16[8,2,64,128]{3,2,1,0:T(8,128)(2,1)} %pad_maximum_fusion.1), calls=%async_computation | async-start | bytes 524288 | tf_op jit(solution)/shard_map/all_to_all | solution.py:509
  22.5 48.4 %collective-permute-start.1 = (bf16[2048,512]{1,0:T(8,128)(2,1)}, bf16[2048,512]{1,0:T(8,128)(2,1)}, u32[]{:S(2)}, u32[]{:S(2)}) collective-permute-start(bf16[2048,512]{1,0:T(8,128)(2,1)} %copy-done.4), channel_id=1, source_target_pairs={{0,2},{1,3},{2,0},{3,1},{4,6},{5,7},{6,4},{7,5},{8,10},{9,11},{10,... | collective-permute-start | bytes 6291464 | tf_op jit(solution)/shard_map/ppermute | solution.py:532
  24.0 19.5 %collective-permute-start.4 = (bf16[2,128,512]{2,1,0:T(8,128)(2,1)}, bf16[2,128,512]{2,1,0:T(8,128)(2,1)S(1)}, u32[]{:S(2)}, u32[]{:S(2)}) collective-permute-start(bf16[2,128,512]{2,1,0:T(8,128)(2,1)} %copy-done.14), channel_id=1, source_target_pairs={{0,8},{1,9},{2,10},{3,11},{4,12},{5,13},{6,14},{7,15},{8,0},{9,1},... | collective-permute-start | bytes 786440 | tf_op jit(solution)/shard_map/ppermute | solution.py:532
  27.0 27.6 %collective-permute-start.5 = (bf16[1,128,1024]{2,1,0:T(8,128)(2,1)}, bf16[1,128,1024]{2,1,0:T(8,128)(2,1)}, u32[]{:S(2)}, u32[]{:S(2)}) collective-permute-start(bf16[1,128,1024]{2,1,0:T(8,128)(2,1)} %collective-permute-done.2.refs_1_), channel_id=1, source_target_pairs={{0,4},{1,5},{2,6},{3,7},{4,0},{5,1},{6,2},{7,3},{8,12},{9,13},{10,... | collective-permute-start | bytes 786440 | tf_op jit(solution)/shard_map/ppermute | solution.py:532
  46.5 17.2 %collective-permute-start.6 = (bf16[2,128,512]{2,1,0:T(8,128)(2,1)}, bf16[2,128,512]{2,1,0:T(8,128)(2,1)S(1)}, u32[]{:S(2)}, u32[]{:S(2)}) collective-permute-start(bf16[2,128,512]{2,1,0:T(8,128)(2,1)} %get-tuple-element.93), channel_id=1, source_target_pairs={{0,12},{1,13},{2,14},{3,15},{4,8},{5,9},{6,10},{7,11},{8,4},{9,5},... | collective-permute-start | bytes 786440 | tf_op jit(solution)/shard_map/ppermute | solution.py:532
  47.8 15.9 %collective-permute-start.7 = (bf16[2,128,512]{2,1,0:T(8,128)(2,1)}, bf16[2,128,512]{2,1,0:T(8,128)(2,1)S(1)}, u32[]{:S(2)}, u32[]{:S(2)}) collective-permute-start(bf16[2,128,512]{2,1,0:T(8,128)(2,1)} %get-tuple-element.92), channel_id=1, source_target_pairs={{0,4},{1,5},{2,6},{3,7},{4,0},{5,1},{6,2},{7,3},{8,12},{9,13},{10,... | collective-permute-start | bytes 786440 | tf_op jit(solution)/shard_map/ppermute | solution.py:532
  50.2 13.5 %all-to-all-start.1 = ((bf16[4,128,128]{2,1,0:T(8,128)(2,1)}), bf16[4,128,128]{2,1,0:T(8,128)(2,1)S(1)}, u32[]{:S(2)}, u32[]{:S(2)}) async-start(bf16[4,128,128]{2,1,0:T(8,128)(2,1)} %back_low.1), calls=%async_computation.1 | async-start | bytes 262144 | tf_op jit(solution)/shard_map/all_to_all | solution.py:509
  64.9 3.8 %collective-permute-start.9 = (bf16[4,128,1024]{2,1,0:T(8,128)(2,1)S(1)}, bf16[4,128,1024]{2,1,0:T(8,128)(2,1)S(1)}, u32[]{:S(2)}, u32[]{:S(2)}) collective-permute-start(bf16[4,128,1024]{2,1,0:T(8,128)(2,1)S(1)} %pad_maximum_fusion), channel_id=1, source_target_pairs={{0,1},{1,0},{2,3},{3,2},{4,5},{5,4},{6,7},{7,6},{8,9},{9,8},{10,11... | collective-permute-start | bytes 3145736 | tf_op jit(solution)/shard_map/ppermute | solution.py:532
  65.0 3.0 %collective-permute-start.8 = (bf16[4,128,128]{2,1,0:T(8,128)(2,1)S(1)}, bf16[4,128,128]{2,1,0:T(8,128)(2,1)S(1)}, u32[]{:S(2)}, u32[]{:S(2)}) collective-permute-start(bf16[4,128,128]{2,1,0:T(8,128)(2,1)S(1)} %all-to-all-done.1), channel_id=1, source_target_pairs={{0,1},{1,0},{2,3},{3,2},{4,5},{5,4},{6,7},{7,6},{8,9},{9,8},{10,11... | collective-permute-start | bytes 393224 | tf_op jit(solution)/shard_map/ppermute | solution.py:532
  65.5 11.6 %collective-permute-start.10 = (bf16[2,128,512]{2,1,0:T(8,128)(2,1)}, bf16[2,128,512]{2,1,0:T(8,128)(2,1)S(1)}, u32[]{:S(2)}, u32[]{:S(2)}) collective-permute-start(bf16[2,128,512]{2,1,0:T(8,128)(2,1)} %get-tuple-element.114), channel_id=1, source_target_pairs={{0,1},{1,0},{2,3},{3,2},{4,5},{5,4},{6,7},{7,6},{8,9},{9,8},{10,11... | collective-permute-start | bytes 786440 | tf_op jit(solution)/shard_map/ppermute | solution.py:532
  65.6 14.9 %collective-permute-start.11 = (bf16[2,128,512]{2,1,0:T(8,128)(2,1)}, bf16[2,128,512]{2,1,0:T(8,128)(2,1)S(1)}, u32[]{:S(2)}, u32[]{:S(2)}) collective-permute-start(bf16[2,128,512]{2,1,0:T(8,128)(2,1)} %get-tuple-element.115), channel_id=1, source_target_pairs={{0,9},{1,8},{2,11},{3,10},{4,13},{5,12},{6,15},{7,14},{8,1},{9,0},... | collective-permute-start | bytes 786440 | tf_op jit(solution)/shard_map/ppermute | solution.py:532
  68.0 19.2 %collective-permute-start.12 = (bf16[2,128,512]{2,1,0:T(8,128)(2,1)}, bf16[2,128,512]{2,1,0:T(8,128)(2,1)S(1)}, u32[]{:S(2)}, u32[]{:S(2)}) collective-permute-start(bf16[2,128,512]{2,1,0:T(8,128)(2,1)} %get-tuple-element.116), channel_id=1, source_target_pairs={{0,5},{1,4},{2,7},{3,6},{4,1},{5,0},{6,3},{7,2},{8,13},{9,12},{10,... | collective-permute-start | bytes 786440 | tf_op jit(solution)/shard_map/ppermute | solution.py:532
  68.8 18.4 %collective-permute-start.13 = (bf16[2,128,512]{2,1,0:T(8,128)(2,1)}, bf16[2,128,512]{2,1,0:T(8,128)(2,1)S(1)}, u32[]{:S(2)}, u32[]{:S(2)}) collective-permute-start(bf16[2,128,512]{2,1,0:T(8,128)(2,1)} %get-tuple-element.117), channel_id=1, source_target_pairs={{0,13},{1,12},{2,15},{3,14},{4,9},{5,8},{6,11},{7,10},{8,5},{9,4},... | collective-permute-start | bytes 786440 | tf_op jit(solution)/shard_map/ppermute | solution.py:532
  70.5 16.7 %copy-start.7 = (bf16[2,128,512]{2,1,0:T(8,128)(2,1)S(1)}, bf16[2,128,512]{2,1,0:T(8,128)(2,1)}, u32[]{:S(2)}) copy-start(bf16[2,128,512]{2,1,0:T(8,128)(2,1)} %copy-done.6) | copy-start | bytes 786436
  70.6 16.7 %copy-start.9 = (bf16[2,128,512]{2,1,0:T(8,128)(2,1)S(1)}, bf16[2,128,512]{2,1,0:T(8,128)(2,1)}, u32[]{:S(2)}) copy-start(bf16[2,128,512]{2,1,0:T(8,128)(2,1)} %copy-done.8) | copy-start | bytes 786436
  77.1 10.2 %copy-start.18 = (bf16[2,128,512]{2,1,0:T(8,128)(2,1)}, bf16[2,128,512]{2,1,0:T(8,128)(2,1)S(1)}, u32[]{:S(2)}) copy-start(bf16[2,128,512]{2,1,0:T(8,128)(2,1)S(1)} %get-tuple-element.143) | copy-start | bytes 786436
  77.1 10.2 %copy-start.19 = (bf16[2,128,512]{2,1,0:T(8,128)(2,1)}, bf16[2,128,512]{2,1,0:T(8,128)(2,1)S(1)}, u32[]{:S(2)}) copy-start(bf16[2,128,512]{2,1,0:T(8,128)(2,1)S(1)} %get-tuple-element.155) | copy-start | bytes 786436
  77.1 14.3 %copy-start.20 = (bf16[8,128,128]{2,1,0:T(8,128)(2,1)}, bf16[8,128,128]{2,1,0:T(8,128)(2,1)S(1)}, u32[]{:S(2)}) copy-start(bf16[8,128,128]{2,1,0:T(8,128)(2,1)S(1)} %get-tuple-element.142) | copy-start | bytes 786436
  77.1 14.3 %copy-start.21 = (bf16[2,128,512]{2,1,0:T(8,128)(2,1)}, bf16[2,128,512]{2,1,0:T(8,128)(2,1)S(1)}, u32[]{:S(2)}) copy-start(bf16[2,128,512]{2,1,0:T(8,128)(2,1)S(1)} %get-tuple-element.139) | copy-start | bytes 786436
  77.1 14.3 %copy-start.22 = (bf16[2,128,512]{2,1,0:T(8,128)(2,1)}, bf16[2,128,512]{2,1,0:T(8,128)(2,1)S(1)}, u32[]{:S(2)}) copy-start(bf16[2,128,512]{2,1,0:T(8,128)(2,1)S(1)} %get-tuple-element.138) | copy-start | bytes 786436
  77.1 14.3 %copy-start.23 = (bf16[2,128,512]{2,1,0:T(8,128)(2,1)}, bf16[2,128,512]{2,1,0:T(8,128)(2,1)S(1)}, u32[]{:S(2)}) copy-start(bf16[2,128,512]{2,1,0:T(8,128)(2,1)S(1)} %get-tuple-element.129) | copy-start | bytes 786436
  77.1 14.3 %copy-start.25 = (bf16[2,128,512]{2,1,0:T(8,128)(2,1)}, bf16[2,128,512]{2,1,0:T(8,128)(2,1)S(1)}, u32[]{:S(2)}) copy-start(bf16[2,128,512]{2,1,0:T(8,128)(2,1)S(1)} %get-tuple-element.127) | copy-start | bytes 786436
  91.4 39.7 %collective-permute-start.18 = (bf16[8,128,512]{2,1,0:T(8,128)(2,1)}, bf16[8,128,512]{2,1,0:T(8,128)(2,1)S(1)}, u32[]{:S(2)}, u32[]{:S(2)}) collective-permute-start(bf16[8,128,512]{2,1,0:T(8,128)(2,1)} %get-tuple-element.135), channel_id=1, source_target_pairs={{0,2},{1,3},{2,0},{3,1},{4,6},{5,7},{6,4},{7,5},{8,10},{9,11},{10,... | collective-permute-start | bytes 3145736 | tf_op jit(solution)/shard_map/ppermute | solution.py:532
  93.0 1.6 collective-permute-start.14
  95.4 35.8 %all-to-all-start.2 = ((f32[4,128,128]{2,1,0:T(8,128)}), f32[4,128,128]{2,1,0:T(8,128)S(1)}, u32[]{:S(2)}, u32[]{:S(2)}) async-start(f32[4,128,128]{2,1,0:T(8,128)} %slice_add_fusion), calls=%async_computation.2 | async-start | bytes 524288 | tf_op jit(solution)/shard_map/all_to_all | solution.py:509
  102.7 17.4 %collective-permute-start.15 = (bf16[2,128,512]{2,1,0:T(8,128)(2,1)}, bf16[2,128,512]{2,1,0:T(8,128)(2,1)S(1)}, u32[]{:S(2)}, u32[]{:S(2)}) collective-permute-start(bf16[2,128,512]{2,1,0:T(8,128)(2,1)} %copy-done.25), channel_id=1, source_target_pairs={{0,4},{1,5},{2,6},{3,7},{4,0},{5,1},{6,2},{7,3},{8,12},{9,13},{10,... | collective-permute-start | bytes 786440 | tf_op jit(solution)/shard_map/ppermute | solution.py:532
  104.7 25.1 %collective-permute-start.16 = (bf16[2,128,512]{2,1,0:T(8,128)(2,1)}, bf16[2,128,512]{2,1,0:T(8,128)(2,1)S(1)}, u32[]{:S(2)}, u32[]{:S(2)}) collective-permute-start(bf16[2,128,512]{2,1,0:T(8,128)(2,1)} %copy-done.24), channel_id=1, source_target_pairs={{0,8},{1,9},{2,10},{3,11},{4,12},{5,13},{6,14},{7,15},{8,0},{9,1},... | collective-permute-start | bytes 786440 | tf_op jit(solution)/shard_map/ppermute | solution.py:532
  107.1 23.4 %collective-permute-start.17 = (bf16[2,128,512]{2,1,0:T(8,128)(2,1)}, bf16[2,128,512]{2,1,0:T(8,128)(2,1)S(1)}, u32[]{:S(2)}, u32[]{:S(2)}) collective-permute-start(bf16[2,128,512]{2,1,0:T(8,128)(2,1)} %copy-done.23), channel_id=1, source_target_pairs={{0,12},{1,13},{2,14},{3,15},{4,8},{5,9},{6,10},{7,11},{8,4},{9,5},... | collective-permute-start | bytes 786440 | tf_op jit(solution)/shard_map/ppermute | solution.py:532
  107.1 34.0 %collective-permute-start.22 = (bf16[8,128,128]{2,1,0:T(8,128)(2,1)S(1)}, bf16[8,128,128]{2,1,0:T(8,128)(2,1)}, u32[]{:S(2)}, u32[]{:S(2)}) collective-permute-start(bf16[8,128,128]{2,1,0:T(8,128)(2,1)S(1)} %constant_dynamic-update-slice_fusion.backs), channel_id=1, source_target_pairs={{0,2},{1,3},{2,0},{3,1},{4,6},{5,7},{6,4},{7,5},{8,10},{9,11},{10,... | collective-permute-start | bytes 786440 | tf_op jit(solution)/shard_map/ppermute | solution.py:532
  131.2 20.0 %collective-permute-start.19 = (bf16[2,128,512]{2,1,0:T(8,128)(2,1)}, bf16[2,128,512]{2,1,0:T(8,128)(2,1)}, u32[]{:S(2)}, u32[]{:S(2)}) collective-permute-start(bf16[2,128,512]{2,1,0:T(8,128)(2,1)} %copy-done.22), channel_id=1, source_target_pairs={{0,1},{1,0},{2,3},{3,2},{4,5},{5,4},{6,7},{7,6},{8,9},{9,8},{10,11... | collective-permute-start | bytes 786440 | tf_op jit(solution)/shard_map/ppermute | solution.py:532
  131.2 20.0 %collective-permute-start.20 = (bf16[2,128,512]{2,1,0:T(8,128)(2,1)}, bf16[2,128,512]{2,1,0:T(8,128)(2,1)}, u32[]{:S(2)}, u32[]{:S(2)}) collective-permute-start(bf16[2,128,512]{2,1,0:T(8,128)(2,1)} %copy-done.21), channel_id=1, source_target_pairs={{0,9},{1,8},{2,11},{3,10},{4,13},{5,12},{6,15},{7,14},{8,1},{9,0},... | collective-permute-start | bytes 786440 | tf_op jit(solution)/shard_map/ppermute | solution.py:532
  135.7 15.5 %collective-permute-start.21 = (bf16[8,128,128]{2,1,0:T(8,128)(2,1)}, bf16[8,128,128]{2,1,0:T(8,128)(2,1)}, u32[]{:S(2)}, u32[]{:S(2)}) collective-permute-start(bf16[8,128,128]{2,1,0:T(8,128)(2,1)} %copy-done.20), channel_id=1, source_target_pairs={{0,2},{1,3},{2,0},{3,1},{4,6},{5,7},{6,4},{7,5},{8,10},{9,11},{10,... | collective-permute-start | bytes 786440 | tf_op jit(solution)/shard_map/ppermute | solution.py:532
  137.4 13.8 %all-to-all-start.3 = ((bf16[4,128,128]{2,1,0:T(8,128)(2,1)}), bf16[4,128,128]{2,1,0:T(8,128)(2,1)S(1)}, u32[]{:S(2)}, u32[]{:S(2)}) async-start(bf16[4,128,128]{2,1,0:T(8,128)(2,1)} %hidden_low.1), calls=%async_computation.3 | async-start | bytes 262144 | tf_op jit(solution)/shard_map/all_to_all | solution.py:509
  151.2 1.4 collective-permute-start.24
  151.3 9.8 %collective-permute-start.26 = (bf16[2,128,512]{2,1,0:T(8,128)(2,1)}, bf16[2,128,512]{2,1,0:T(8,128)(2,1)S(1)}, u32[]{:S(2)}, u32[]{:S(2)}) collective-permute-start(bf16[2,128,512]{2,1,0:T(8,128)(2,1)} %copy-done.19), channel_id=1, source_target_pairs={{0,5},{1,4},{2,7},{3,6},{4,1},{5,0},{6,3},{7,2},{8,13},{9,12},{10,... | collective-permute-start | bytes 786440 | tf_op jit(solution)/shard_map/ppermute | solution.py:532
  152.7 10.9 %collective-permute-start.25 = (bf16[8,128,128]{2,1,0:T(8,128)(2,1)S(1)}, bf16[8,128,128]{2,1,0:T(8,128)(2,1)S(1)}, u32[]{:S(2)}, u32[]{:S(2)}) collective-permute-start(bf16[8,128,128]{2,1,0:T(8,128)(2,1)S(1)} %constant_dynamic-update-slice_fusion.2.hiddens), channel_id=1, source_target_pairs={{0,2},{1,3},{2,0},{3,1},{4,6},{5,7},{6,4},{7,5},{8,10},{9,11},{10,... | collective-permute-start | bytes 786440 | tf_op jit(solution)/shard_map/ppermute | solution.py:532
  153.2 14.5 %collective-permute-start.23 = (bf16[2,128,512]{2,1,0:T(8,128)(2,1)}, bf16[2,128,512]{2,1,0:T(8,128)(2,1)S(1)}, u32[]{:S(2)}, u32[]{:S(2)}) collective-permute-start(bf16[2,128,512]{2,1,0:T(8,128)(2,1)} %copy-done.18), channel_id=1, source_target_pairs={{0,13},{1,12},{2,15},{3,14},{4,9},{5,8},{6,11},{7,10},{8,5},{9,4},... | collective-permute-start | bytes 786440 | tf_op jit(solution)/shard_map/ppermute | solution.py:532
  155.1 6.1 %copy-start.11 = (bf16[2,128,512]{2,1,0:T(8,128)(2,1)S(1)}, bf16[2,128,512]{2,1,0:T(8,128)(2,1)}, u32[]{:S(2)}) copy-start(bf16[2,128,512]{2,1,0:T(8,128)(2,1)} %copy-done.10) | copy-start | bytes 786436
  155.1 6.1 %copy-start.13 = (bf16[2,128,512]{2,1,0:T(8,128)(2,1)S(1)}, bf16[2,128,512]{2,1,0:T(8,128)(2,1)}, u32[]{:S(2)}) copy-start(bf16[2,128,512]{2,1,0:T(8,128)(2,1)} %copy-done.12) | copy-start | bytes 786436
  (9 other events, 8.3 us)

commit v11 on v10

--- a/solution.py
+++ b/solution.py
@@ -572,40 +572,49 @@
     pair = for_pair(adapters, place, value_weight, down_maps, members)
     ups_other, pair = barrier((ups_other, pair))
     pair = swap(pair, pair_bit)
-    packs = dict(zip(far[0], pack_tokens(place, tokens, taken(offsets, far[0]), width)))
+    early = near[:1] + far[0] + far[1]
+    packs = dict(zip(early, pack_tokens(place, tokens, taken(offsets, early), width)))
+    ups = exchange_side(jnp.stack([ups, ups_other], axis=1))
     firsts = [gradients[1 << step] for step in range(steps - 1)]
-    firsts, ups_other, packs = barrier((firsts, ups_other, packs))
+    firsts, packs = barrier((firsts, packs))
     for step in range(steps - 1):
         gradients[1 << step] = firsts[step]
-
-    ups = exchange_side(jnp.stack([ups, ups_other], axis=1))
-    arrived = send(packs, far[0])
+    window = near[:1] + far[0]
+    arrived = send(packs, window)
+    ups, gradients, packs, tokens, done = barrier(
+        (ups, [gradients[0]] + firsts, packs, tokens, taken(arrived, window))
+    )
+    arrived.update(zip(window, done))
+    gradients = {0: gradients[0], **{1 << step: gradients[1 + step] for step in range(steps - 1)}}
+
+    backs = exchange_line(back_rows(adapters, place, ranks, output_gradient, ups))
+    arrived.update(send(packs, far[1]))
     for step in range(1, steps - 1):
         for slot in range(1, 1 << step):
             gradients[slot + (1 << step)] = swap(gradients[slot], offsets[1 << step])
-    ups, tokens, done = barrier((ups, tokens, taken(arrived, far[0])))
-    arrived.update(zip(far[0], done))
-
-    rest = [slot for slot in range(members) if slot not in far[0]]
-    packs = dict(zip(rest, pack_tokens(place, tokens, taken(offsets, rest), width)))
+    gradients = taken(gradients, range(lines))
+    rest = [slot for slot in range(members) if slot not in early]
+    packs.update(zip(rest, pack_tokens(place, tokens, taken(offsets, rest), width)))
     arrived[0] = packs[0]
-    backs = exchange_line(back_rows(adapters, place, ranks, output_gradient, ups))
-    window = far[1] + near[:1]
-    arrived.update(send(packs, window))
-    backs, gradients, packs, done = barrier((backs, gradients, packs, taken(arrived, window)))
-    arrived.update(zip(window, done))
+    backs, gradients, packs, done = barrier((backs, gradients, packs, taken(arrived, far[1])))
+    arrived.update(zip(far[1], done))
 
     backs = both_cores(backs)
+    backs_pair = swap(backs, pair_bit)
     gradients.append(swap(jnp.concatenate(gradients, axis=0), 1))
     arrived.update(send(packs, near[1:] + far[2] + far[3]))
     *slices, columns, columns_pair = input_slices(
         adapters, place, gradients, backs, value_weight, pair, down_maps
     )
-    slices, arrived = barrier((slices, taken(arrived, range(members))))
+    slices, arrived, backs_pair = barrier((slices, taken(arrived, range(members)), backs_pair))
 
     parts, tokens_own, tokens_pair = hidden_parts(adapters, place, down_maps, pair, arrived)
     results = {0: slices[0]}
-    window = near[:1] + far[0] + far[1]
+    results.update(send(slices, far[0]))
+    parts, done, slices = barrier((parts, taken(results, far[0]), slices))
+    results.update(zip(far[0], done))
+
+    window = near[:1] + far[1]
     results.update(send(slices, window))
     tokens_other = swap(tokens_pair, pair_bit)
     parts = exchange_line(parts[:lines] + swap(parts[lines:], 1))
@@ -618,18 +627,17 @@
     results.update(send(slices, window))
     hiddens = exchange_line(hidden_rows(adapters, place, ranks, parts))
     columns_other = swap(columns_pair, pair_bit)
-    backs_pair = swap(backs, pair_bit)
-    hiddens, done, slices, columns_other, backs_pair = barrier(
-        (hiddens, taken(results, window), slices, columns_other, backs_pair)
+    down_gradient = down_gradients(
+        adapters, place, backs, backs_pair, tokens_own, tokens_other, num_adapters
+    )
+    hiddens, done, slices, columns_other, down_gradient = barrier(
+        (hiddens, taken(results, window), slices, columns_other, down_gradient)
     )
     results.update(zip(window, done))
 
     results.update(send(slices, near[2:] + far[3]))
     hiddens = both_cores(hiddens)
     hiddens_pair = swap(hiddens, pair_bit)
-    down_gradient = down_gradients(
-        adapters, place, backs, backs_pair, tokens_own, tokens_other, num_adapters
-    )
     up_gradient = up_gradients(
         adapters, place, ranks, columns, columns_other, hiddens, hiddens_pair, depth // devices
     )
@@ -640,7 +648,7 @@
         )
 
     most = joined([slot for slot in range(members) if slot not in far[3]])
-    up_gradient, down_gradient, most = barrier((up_gradient, down_gradient, most))
+    up_gradient, most = barrier((up_gradient, most))
     input_grad = joined(far[3], most)
     return (input_grad, down_gradient, up_gradient)
 

time: 171 us -> 173 us (1.012)
  local copies, waits for them, and re-layouts: 8.41 us -> 14.8 us
    all_to_all x4, waiting for transfers between devices: 19.2 us -> 11.7 us  [exchange(): lax.all_to_all(pieces, 'dp', split_axis=0, concat_axis=0, axis_index_grou...]
    ppermute x27, waiting for transfers between devices: 52.7 us -> 59.6 us  [swap(): return lax.ppermute(array, 'dp', [(i, i ^ flip) for i in range(devices)])]
    unnamed x54 -> x82, local copies, waits for them, and re-layouts: 8.35 us -> 14.7 us
    all_to_all x4, starting transfers between devices: 19.9 us -> 13.8 us  [exchange(): lax.all_to_all(pieces, 'dp', split_axis=0, concat_axis=0, axis_index_grou...]
    ppermute x27, starting transfers between devices: 33.2 us -> 37.6 us  [swap(): return lax.ppermute(array, 'dp', [(i, i ^ flip) for i in range(devices)])]
  transfers between devices with their start and end apart: 31 -> 31, of which waited for: 13 -> 13; matrix products, arithmetic and copies ran while one was open for 1% -> 2% of each run, Pallas kernels for 16% -> 17%
where the time goes in v11:
time: 173 us; the launch traced here: 172 us
  waiting for transfers between devices  71.3 us (41%)
  starting transfers between devices  51.4 us (30%)
  Pallas kernels  30.7 us (18%)
  local copies, waits for them, and re-layouts  14.8 us (9%)
  other arithmetic  2.78 us (2%)
    ppermute x27, waiting for transfers between devices, swap(): return lax.ppermute(array, 'dp', [(i, i ^ flip) for i in range(devices)])  59.6 us
    ppermute x27, starting transfers between devices, swap(): return lax.ppermute(array, 'dp', [(i, i ^ flip) for i in range(devices)])  37.6 us
    unnamed x82, local copies, waits for them, and re-layouts  14.7 us
    all_to_all x4, starting transfers between devices, exchange(): lax.all_to_all(pieces, 'dp', split_axis=0, concat_axis=0, axis_index_grou...  13.8 us
    pallas_call x4, Pallas kernels, call(): pl.pallas_call(kernel, out_shape=out_shapes, grid_spec=pltpu.PrefetchScal...  12.3 us
    all_to_all x4, waiting for transfers between devices, exchange(): lax.all_to_all(pieces, 'dp', split_axis=0, concat_axis=0, axis_index_grou...  11.7 us
    pallas_call x2, Pallas kernels, sums_call(): pl.pallas_call(kernel, out_shape=jax.ShapeDtypeStruct((num_adapters,) + p...  9.64 us
    pallas_call x4, Pallas kernels, copy_call(): pl.pallas_call(kernel, out_shape=out_shapes, grid_spec=pltpu.PrefetchScal...  5.7 us
  transfers between devices with their start and end apart: 31, of which 13 were waited for; matrix products, arithmetic and copies ran while one was open for 2% of the time, Pallas kernels for 17%

profile of v11, /device:TPU:0, one launch (start us, length us, event | category | flops | bytes accessed | tf_op | source)
XLA Modules:
  0.0 172.0 jit_solution(7336724704474246163)
XLA Ops:
  0.6 1.2 copy-done.6
  2.5 1.1 gather_up.1
  3.6 3.0 %collective-permute-start = (bf16[8,64,128]{2,1,0:T(8,128)(2,1)S(1)}, bf16[8,64,128]{2,1,0:T(8,128)(2,1)S(1)}, u32[]{:S(2)}, u32[]{:S(2)}) collective-permute-start(bf16[8,64,128]{2,1,0:T(8,128)(2,1)S(1)} %get-tuple-element.94), channel_id=1, source_target_pairs={{0,2},{1,3},{2,0},{3,1},{4,6},{5,7},{6,4},{7,5},{8,10},{9,11},{10,... | collective-permute-start | bytes 393224 | tf_op jit(solution)/shard_map/ppermute | solution.py:532
  6.6 1.2 copy-done.1
  8.5 3.4 %for_pair.1 = bf16[2048,512]{1,0:T(8,128)(2,1)} custom-call(s32[16]{0:T(128)S(1)} %copy-done.22, s32[1]{0:T(128)} %bitcast.place, bf16[1024,512]{1,0:T(8,128)(2,1)S(1)} %copy-done.1, bf16[64,128,512]{2,1,0:T(8,128)(2,1)} %refs_7_.3), custom_call_target="tpu_custom_call" | custom-call | tf_op jit(solution)/shard_map/for_pair/pallas_call | solution.py:74
  12.1 3.1 %collective-permute-start.2 = (bf16[1,128,1024]{2,1,0:T(8,128)(2,1)S(1)}, bf16[1,128,1024]{2,1,0:T(8,128)(2,1)}, u32[]{:S(2)}, u32[]{:S(2)}) collective-permute-start(bf16[1,128,1024]{2,1,0:T(8,128)(2,1)S(1)} %bitcast.4), channel_id=1, source_target_pairs={{0,8},{1,9},{2,10},{3,11},{4,12},{5,13},{6,14},{7,15},{8,0},{9,1},... | collective-permute-start | bytes 786440 | tf_op jit(solution)/shard_map/ppermute | solution.py:532
  15.1 1.6 collective-permute-start.3
  17.4 3.4 %all-to-all-start = ((bf16[8,2,64,128]{3,2,1,0:T(8,128)(2,1)}), bf16[8,2,64,128]{3,2,1,0:T(8,128)(2,1)S(1)}, u32[]{:S(2)}, u32[]{:S(2)}) async-start(bf16[8,2,64,128]{3,2,1,0:T(8,128)(2,1)} %pad_maximum_fusion.1), calls=%async_computation | async-start | bytes 524288 | tf_op jit(solution)/shard_map/all_to_all | solution.py:509
  20.9 0.9 pack_tokens.2
  21.8 6.8 %collective-permute-done.2.refs_1_ = bf16[1,128,1024]{2,1,0:T(8,128)(2,1)} collective-permute-done((bf16[1,128,1024]{2,1,0:T(8,128)(2,1)S(1)}, bf16[1,128,1024]{2,1,0:T(8,128)(2,1)}, u32[]{:S(2)}, u32[]{:S(2)}) %collective-permute-start.2) | collective-permute-done | bytes 262176 | tf_op jit(solution)/shard_map/ppermute | solution.py:532
  28.6 1.4 collective-permute-start.4
  30.0 1.9 %collective-permute-start.5 = (bf16[2,128,512]{2,1,0:T(8,128)(2,1)S(1)}, bf16[2,128,512]{2,1,0:T(8,128)(2,1)S(1)}, u32[]{:S(2)}, u32[]{:S(2)}) collective-permute-start(bf16[2,128,512]{2,1,0:T(8,128)(2,1)S(1)} %get-tuple-element.103), channel_id=1, source_target_pairs={{0,8},{1,9},{2,10},{3,11},{4,12},{5,13},{6,14},{7,15},{8,0},{9,1},... | collective-permute-start | bytes 786440 | tf_op jit(solution)/shard_map/ppermute | solution.py:532
  32.0 10.1 %collective-permute-done.4.refs_10_ = bf16[2,128,512]{2,1,0:T(8,128)(2,1)S(1)} collective-permute-done((bf16[2,128,512]{2,1,0:T(8,128)(2,1)S(1)}, bf16[2,128,512]{2,1,0:T(8,128)(2,1)S(1)}, u32[]{:S(2)}, u32[]{:S(2)}) %collective-permute-start.4) | collective-permute-done | bytes 262176 | tf_op jit(solution)/shard_map/ppermute | solution.py:532
  42.8 0.8 collective-permute-done.5.refs_9_
  44.8 2.8 %collective-permute-start.7 = (bf16[2,128,512]{2,1,0:T(8,128)(2,1)}, bf16[2,128,512]{2,1,0:T(8,128)(2,1)}, u32[]{:S(2)}, u32[]{:S(2)}) collective-permute-start(bf16[2,128,512]{2,1,0:T(8,128)(2,1)} %get-tuple-element.112), channel_id=1, source_target_pairs={{0,12},{1,13},{2,14},{3,15},{4,8},{5,9},{6,10},{7,11},{8,4},{9,5},... | collective-permute-start | bytes 786440 | tf_op jit(solution)/shard_map/ppermute | solution.py:532
  47.7 1.5 back_low.1
  49.1 3.3 %all-to-all-start.1 = ((bf16[4,128,128]{2,1,0:T(8,128)(2,1)}), bf16[4,128,128]{2,1,0:T(8,128)(2,1)S(1)}, u32[]{:S(2)}, u32[]{:S(2)}) async-start(bf16[4,128,128]{2,1,0:T(8,128)(2,1)} %back_low.1), calls=%async_computation.1 | async-start | bytes 262144 | tf_op jit(solution)/shard_map/all_to_all | solution.py:509
  56.3 6.5 %all-to-all-done.1 = bf16[4,128,128]{2,1,0:T(8,128)(2,1)S(1)} async-done(((bf16[4,128,128]{2,1,0:T(8,128)(2,1)}), bf16[4,128,128]{2,1,0:T(8,128)(2,1)S(1)}, u32[]{:S(2)}, u32[]{:S(2)}) %all-to-all-start.1) | async-done | bytes 131104 | tf_op jit(solution)/shard_map/all_to_all | solution.py:509
  62.8 1.3 pad_maximum_fusion
  64.9 1.4 collective-permute-start.11
  66.3 0.8 collective-permute-done.8
  67.1 0.8 collective-permute-start.12
  68.0 1.9 %collective-permute-start.13 = (bf16[2,128,512]{2,1,0:T(8,128)(2,1)S(1)}, bf16[2,128,512]{2,1,0:T(8,128)(2,1)S(1)}, u32[]{:S(2)}, u32[]{:S(2)}) collective-permute-start(bf16[2,128,512]{2,1,0:T(8,128)(2,1)S(1)} %copy-done.31), channel_id=1, source_target_pairs={{0,13},{1,12},{2,15},{3,14},{4,9},{5,8},{6,11},{7,10},{8,5},{9,4},... | collective-permute-start | bytes 786440 | tf_op jit(solution)/shard_map/ppermute | solution.py:532
  69.8 1.5 collective-permute-start.14
  71.3 5.4 %input_slices.1 = (bf16[2,128,512]{2,1,0:T(8,128)(2,1)S(1)}, bf16[2,128,512]{2,1,0:T(8,128)(2,1)S(1)}, bf16[2,128,512]{2,1,0:T(8,128)(2,1)S(1)}, bf16[2,128,512]...) custom-call(s32[16]{0:T(128)S(1)} %copy-done.23, ...), custom_call_target="tpu_custom_call" | custom-call | tf_op jit(solution)/shard_map/input_slices/pallas_call | solution.py:51
  81.1 5.4 %collective-permute-done.12.refs_14_ = bf16[2,128,512]{2,1,0:T(8,128)(2,1)S(1)} collective-permute-done((bf16[2,128,512]{2,1,0:T(8,128)(2,1)S(1)}, bf16[2,128,512]{2,1,0:T(8,128)(2,1)S(1)}, u32[]{:S(2)}, u32[]{:S(2)}) %collective-permute-start.12) | collective-permute-done | bytes 262176 | tf_op jit(solution)/shard_map/ppermute | solution.py:532
  86.5 6.1 %collective-permute-start.15 = (bf16[2,128,512]{2,1,0:T(8,128)(2,1)S(1)}, bf16[2,128,512]{2,1,0:T(8,128)(2,1)S(1)}, u32[]{:S(2)}, u32[]{:S(2)}) collective-permute-start(bf16[2,128,512]{2,1,0:T(8,128)(2,1)S(1)} %get-tuple-element.146), channel_id=1, source_target_pairs={{0,8},{1,9},{2,10},{3,11},{4,12},{5,13},{6,14},{7,15},{8,0},{9,1},... | collective-permute-start | bytes 786440 | tf_op jit(solution)/shard_map/ppermute | solution.py:532
  92.6 4.2 %hidden_parts.1 = (f32[8,128,128]{2,1,0:T(8,128)S(1)}, bf16[8,128,512]{2,1,0:T(8,128)(2,1)S(1)}, bf16[8,128,512]{2,1,0:T(8,128)(2,1)}) custom-call(s32[16]{0:T(128)S(1)} %copy-done.23, s32[1]{0:T(128)} %bitcast.place, bf16[2048,512]{1,0:T(8,128)(2,1)} %collective-permute-done.1.pair, bf16[64,128,512]{2,1,0:T(8,128)(2,1)} %refs_7_.3, ...), custom_call_target="tpu_custom_call" | custom-call | tf_op jit(solution)/shard_map/hidden_parts/pallas_call | solution.py:51
  96.8 1.6 collective-permute-start.19
  98.4 6.4 %collective-permute-done.15.refs_1_ = bf16[2,128,512]{2,1,0:T(8,128)(2,1)S(1)} collective-permute-done((bf16[2,128,512]{2,1,0:T(8,128)(2,1)S(1)}, bf16[2,128,512]{2,1,0:T(8,128)(2,1)S(1)}, u32[]{:S(2)}, u32[]{:S(2)}) %collective-permute-start.15) | collective-permute-done | bytes 262176 | tf_op jit(solution)/shard_map/ppermute | solution.py:532
  104.9 1.5 collective-permute-done.16
  107.1 3.4 %all-to-all-start.2 = ((f32[4,128,128]{2,1,0:T(8,128)}), f32[4,128,128]{2,1,0:T(8,128)S(1)}, u32[]{:S(2)}, u32[]{:S(2)}) async-start(f32[4,128,128]{2,1,0:T(8,128)} %slice_add_fusion), calls=%async_computation.2 | async-start | bytes 524288 | tf_op jit(solution)/shard_map/all_to_all | solution.py:509
  110.5 2.0 %collective-permute-start.17 = (bf16[2,128,512]{2,1,0:T(8,128)(2,1)}, bf16[2,128,512]{2,1,0:T(8,128)(2,1)S(1)}, u32[]{:S(2)}, u32[]{:S(2)}) collective-permute-start(bf16[2,128,512]{2,1,0:T(8,128)(2,1)} %copy-done.35), channel_id=1, source_target_pairs={{0,4},{1,5},{2,6},{3,7},{4,0},{5,1},{6,2},{7,3},{8,12},{9,13},{10,... | collective-permute-start | bytes 786440 | tf_op jit(solution)/shard_map/ppermute | solution.py:532
  112.5 2.4 %collective-permute-start.18 = (bf16[2,128,512]{2,1,0:T(8,128)(2,1)}, bf16[2,128,512]{2,1,0:T(8,128)(2,1)S(1)}, u32[]{:S(2)}, u32[]{:S(2)}) collective-permute-start(bf16[2,128,512]{2,1,0:T(8,128)(2,1)} %copy-done.32), channel_id=1, source_target_pairs={{0,12},{1,13},{2,14},{3,15},{4,8},{5,9},{6,10},{7,11},{8,4},{9,5},... | collective-permute-start | bytes 786440 | tf_op jit(solution)/shard_map/ppermute | solution.py:532
  114.9 8.4 %collective-permute-done.17.refs_2_ = bf16[2,128,512]{2,1,0:T(8,128)(2,1)S(1)} collective-permute-done((bf16[2,128,512]{2,1,0:T(8,128)(2,1)}, bf16[2,128,512]{2,1,0:T(8,128)(2,1)S(1)}, u32[]{:S(2)}, u32[]{:S(2)}) %collective-permute-start.17) | collective-permute-done | bytes 262176 | tf_op jit(solution)/shard_map/ppermute | solution.py:532
  123.3 7.5 %collective-permute-done.18.refs_3_ = bf16[2,128,512]{2,1,0:T(8,128)(2,1)S(1)} collective-permute-done((bf16[2,128,512]{2,1,0:T(8,128)(2,1)}, bf16[2,128,512]{2,1,0:T(8,128)(2,1)S(1)}, u32[]{:S(2)}, u32[]{:S(2)}) %collective-permute-start.18) | collective-permute-done | bytes 262176 | tf_op jit(solution)/shard_map/ppermute | solution.py:532
  131.5 1.1 collective-permute-start.21
  132.6 1.5 collective-permute-start.22
  134.1 1.2 hidden_low.1
  135.3 3.6 %all-to-all-start.3 = ((bf16[4,128,128]{2,1,0:T(8,128)(2,1)}), bf16[4,128,128]{2,1,0:T(8,128)(2,1)S(1)}, u32[]{:S(2)}, u32[]{:S(2)}) async-start(bf16[4,128,128]{2,1,0:T(8,128)(2,1)} %hidden_low.1), calls=%async_computation.3 | async-start | bytes 262144 | tf_op jit(solution)/shard_map/all_to_all | solution.py:509
  139.0 5.5 %down_gradients.1 = bf16[64,128,512]{2,1,0:T(8,128)(2,1)} custom-call(s32[16]{0:T(128)S(1)} %copy-done.23, s32[1]{0:T(128)} %bitcast.place, bf16[8,128,128]{2,1,0:T(8,128)(2,1)S(1)} %constant_dynamic-update-slice_fusion.backs, bf16[8,128,128]{2,1,0:T(8,128)(2,1)S(1)} %copy-done.18, bf16[8,128,512]{2,1,0:T(8,128)(2,1)S(1)} %get-tuple-element.170.own, ...), custom_call_target="tpu_custom_call" | custom-call | tf_op jit(solution)/shard_map/down_gradients/pallas_call | solution.py:410
  144.5 5.3 %all-to-all-done.3 = bf16[4,128,128]{2,1,0:T(8,128)(2,1)S(1)} async-done(((bf16[4,128,128]{2,1,0:T(8,128)(2,1)}), bf16[4,128,128]{2,1,0:T(8,128)(2,1)S(1)}, u32[]{:S(2)}, u32[]{:S(2)}) %all-to-all-start.3) | async-done | bytes 131104 | tf_op jit(solution)/shard_map/all_to_all | solution.py:509
  150.2 1.0 collective-permute-done.24
  151.2 1.6 collective-permute-start.25
  153.0 10.8 %collective-permute-done.26.refs_6_ = bf16[2,128,512]{2,1,0:T(8,128)(2,1)S(1)} collective-permute-done((bf16[2,128,512]{2,1,0:T(8,128)(2,1)}, bf16[2,128,512]{2,1,0:T(8,128)(2,1)S(1)}, u32[]{:S(2)}, u32[]{:S(2)}) %collective-permute-start.26) | collective-permute-done | bytes 262176 | tf_op jit(solution)/shard_map/ppermute | solution.py:532
  163.8 0.9 copy-done.20
  164.7 2.4 %join_columns.2.refs_1_ = bf16[128,8192]{1,0:T(8,128)(2,1)} custom-call(s32[1]{0:T(128)} %bitcast.place, bf16[2,128,512]{2,1,0:T(8,128)(2,1)S(1)} %copy-done.16, bf16[2,128,512]{2,1,0:T(8,128)(2,1)S(1)} %collective-permute-done.15.refs_1_, bf16[2,128,512]{2,1,0:T(8,128)(2,1)S(1)} %collective-permute-done.17.refs_2_, bf16[2,128,512]{2,1,0:T(8,128)(2,1)S(1)} %copy-done.20, ...), custom_call_target="tpu_custom_call" | custom-call | tf_op jit(solution)/shard_map/join_columns/pallas_call | solution.py:341
  167.1 4.2 %up_gradients.1 = bf16[64,64,128]{2,1,0:T(8,128)(2,1)} custom-call(s32[16]{0:T(128)S(1)} %copy-done.23, s32[1]{0:T(128)} %bitcast.place, s32[64]{0:T(128)S(1)} %copy-done.24, bf16[8,128,128]{2,1,0:T(8,128)(2,1)S(1)} %copy-done.14, bf16[8,128,128]{2,1,0:T(8,128)(2,1)} %collective-permute-done.22.gradients_pair, ...), custom_call_target="tpu_custom_call" | custom-call | tf_op jit(solution)/shard_map/up_gradients/pallas_call | solution.py:410
  (114 shorter events, 15.9 us)
Async XLA Ops:
  3.6 8.4 %collective-permute-start = (bf16[8,64,128]{2,1,0:T(8,128)(2,1)S(1)}, bf16[8,64,128]{2,1,0:T(8,128)(2,1)S(1)}, u32[]{:S(2)}, u32[]{:S(2)}) collective-permute-start(bf16[8,64,128]{2,1,0:T(8,128)(2,1)S(1)} %get-tuple-element.94), channel_id=1, source_target_pairs={{0,2},{1,3},{2,0},{3,1},{4,6},{5,7},{6,4},{7,5},{8,10},{9,11},{10,... | collective-permute-start | bytes 393224 | tf_op jit(solution)/shard_map/ppermute | solution.py:532
  8.5 12.3 %copy-start = (bf16[128,8192]{1,0:T(8,128)(2,1)S(1)}, bf16[128,8192]{1,0:T(8,128)(2,1)}, u32[]{:S(2)}) copy-start(bf16[128,8192]{1,0:T(8,128)(2,1)} %tokens.2) | copy-start | bytes 6291460
  11.9 35.7 %copy-start.23 = (s32[16]{0:T(128)S(1)}, s32[16]{0:T(128)}, u32[]{:S(2)}) copy-start(s32[16]{0:T(128)} %adapters.15) | copy-start | bytes 196
  12.0 35.7 %copy-start.24 = (s32[64]{0:T(128)S(1)}, s32[64]{0:T(128)}, u32[]{:S(2)}) copy-start(s32[64]{0:T(128)} %ranks.5) | copy-start | bytes 772
  12.0 57.8 %collective-permute-start.1 = (bf16[2048,512]{1,0:T(8,128)(2,1)}, bf16[2048,512]{1,0:T(8,128)(2,1)}, u32[]{:S(2)}, u32[]{:S(2)}) collective-permute-start(bf16[2048,512]{1,0:T(8,128)(2,1)} %for_pair.1), channel_id=1, source_target_pairs={{0,2},{1,3},{2,0},{3,1},{4,6},{5,7},{6,4},{7,5},{8,10},{9,11},{10,... | collective-permute-start | bytes 6291464 | tf_op jit(solution)/shard_map/ppermute | solution.py:532
  12.1 16.5 %collective-permute-start.2 = (bf16[1,128,1024]{2,1,0:T(8,128)(2,1)S(1)}, bf16[1,128,1024]{2,1,0:T(8,128)(2,1)}, u32[]{:S(2)}, u32[]{:S(2)}) collective-permute-start(bf16[1,128,1024]{2,1,0:T(8,128)(2,1)S(1)} %bitcast.4), channel_id=1, source_target_pairs={{0,8},{1,9},{2,10},{3,11},{4,12},{5,13},{6,14},{7,15},{8,0},{9,1},... | collective-permute-start | bytes 786440 | tf_op jit(solution)/shard_map/ppermute | solution.py:532
  15.1 13.5 %collective-permute-start.3 = (bf16[1,128,1024]{2,1,0:T(8,128)(2,1)S(1)}, bf16[1,128,1024]{2,1,0:T(8,128)(2,1)S(1)}, u32[]{:S(2)}, u32[]{:S(2)}) collective-permute-start(bf16[1,128,1024]{2,1,0:T(8,128)(2,1)S(1)} %bitcast.5), channel_id=1, source_target_pairs={{0,4},{1,5},{2,6},{3,7},{4,0},{5,1},{6,2},{7,3},{8,12},{9,13},{10,... | collective-permute-start | bytes 786440 | tf_op jit(solution)/shard_map/ppermute | solution.py:532
  17.4 26.8 %all-to-all-start = ((bf16[8,2,64,128]{3,2,1,0:T(8,128)(2,1)}), bf16[8,2,64,128]{3,2,1,0:T(8,128)(2,1)S(1)}, u32[]{:S(2)}, u32[]{:S(2)}) async-start(bf16[8,2,64,128]{3,2,1,0:T(8,128)(2,1)} %pad_maximum_fusion.1), calls=%async_computation | async-start | bytes 524288 | tf_op jit(solution)/shard_map/all_to_all | solution.py:509
  28.6 20.5 %copy-start.4 = (bf16[1,128,1024]{2,1,0:T(8,128)(2,1)}, bf16[1,128,1024]{2,1,0:T(8,128)(2,1)S(1)}, u32[]{:S(2)}) copy-start(bf16[1,128,1024]{2,1,0:T(8,128)(2,1)S(1)} %collective-permute-done.3.refs_2_) | copy-start | bytes 786436
  28.6 13.5 %collective-permute-start.4 = (bf16[2,128,512]{2,1,0:T(8,128)(2,1)S(1)}, bf16[2,128,512]{2,1,0:T(8,128)(2,1)S(1)}, u32[]{:S(2)}, u32[]{:S(2)}) collective-permute-start(bf16[2,128,512]{2,1,0:T(8,128)(2,1)S(1)} %get-tuple-element.104), channel_id=1, source_target_pairs={{0,4},{1,5},{2,6},{3,7},{4,0},{5,1},{6,2},{7,3},{8,12},{9,13},{10,... | collective-permute-start | bytes 786440 | tf_op jit(solution)/shard_map/ppermute | solution.py:532
  30.0 13.5 %collective-permute-start.5 = (bf16[2,128,512]{2,1,0:T(8,128)(2,1)S(1)}, bf16[2,128,512]{2,1,0:T(8,128)(2,1)S(1)}, u32[]{:S(2)}, u32[]{:S(2)}) collective-permute-start(bf16[2,128,512]{2,1,0:T(8,128)(2,1)S(1)} %get-tuple-element.103), channel_id=1, source_target_pairs={{0,8},{1,9},{2,10},{3,11},{4,12},{5,13},{6,14},{7,15},{8,0},{9,1},... | collective-permute-start | bytes 786440 | tf_op jit(solution)/shard_map/ppermute | solution.py:532
  44.2 18.6 %collective-permute-start.6 = (bf16[1,128,1024]{2,1,0:T(8,128)(2,1)}, bf16[1,128,1024]{2,1,0:T(8,128)(2,1)}, u32[]{:S(2)}, u32[]{:S(2)}) collective-permute-start(bf16[1,128,1024]{2,1,0:T(8,128)(2,1)} %collective-permute-done.2.refs_1_), channel_id=1, source_target_pairs={{0,4},{1,5},{2,6},{3,7},{4,0},{5,1},{6,2},{7,3},{8,12},{9,13},{10,... | collective-permute-start | bytes 786440 | tf_op jit(solution)/shard_map/ppermute | solution.py:532
  44.8 18.0 %collective-permute-start.7 = (bf16[2,128,512]{2,1,0:T(8,128)(2,1)}, bf16[2,128,512]{2,1,0:T(8,128)(2,1)}, u32[]{:S(2)}, u32[]{:S(2)}) collective-permute-start(bf16[2,128,512]{2,1,0:T(8,128)(2,1)} %get-tuple-element.112), channel_id=1, source_target_pairs={{0,12},{1,13},{2,14},{3,15},{4,8},{5,9},{6,10},{7,11},{8,4},{9,5},... | collective-permute-start | bytes 786440 | tf_op jit(solution)/shard_map/ppermute | solution.py:532
  49.1 13.7 %all-to-all-start.1 = ((bf16[4,128,128]{2,1,0:T(8,128)(2,1)}), bf16[4,128,128]{2,1,0:T(8,128)(2,1)S(1)}, u32[]{:S(2)}, u32[]{:S(2)}) async-start(bf16[4,128,128]{2,1,0:T(8,128)(2,1)} %back_low.1), calls=%async_computation.1 | async-start | bytes 262144 | tf_op jit(solution)/shard_map/all_to_all | solution.py:509
  52.4 18.9 %copy-start.2 = (bf16[1024,512]{1,0:T(8,128)(2,1)S(1)}, bf16[1024,512]{1,0:T(8,128)(2,1)}, u32[]{:S(2)}) copy-start(bf16[1024,512]{1,0:T(8,128)(2,1)} %refs_13_.1) | copy-start | bytes 3145732
  62.8 5.1 %copy-start.31 = (bf16[2,128,512]{2,1,0:T(8,128)(2,1)S(1)}, bf16[2,128,512]{2,1,0:T(8,128)(2,1)}, u32[]{:S(2)}) copy-start(bf16[2,128,512]{2,1,0:T(8,128)(2,1)} %copy-done.30) | copy-start | bytes 786436
  62.8 8.5 %copy-start.5 = (bf16[1,128,1024]{2,1,0:T(8,128)(2,1)S(1)}, bf16[1,128,1024]{2,1,0:T(8,128)(2,1)}, u32[]{:S(2)}) copy-start(bf16[1,128,1024]{2,1,0:T(8,128)(2,1)} %copy-done.4) | copy-start | bytes 786436
  64.2 3.7 %collective-permute-start.9 = (bf16[4,128,1024]{2,1,0:T(8,128)(2,1)S(1)}, bf16[4,128,1024]{2,1,0:T(8,128)(2,1)S(1)}, u32[]{:S(2)}, u32[]{:S(2)}) collective-permute-start(bf16[4,128,1024]{2,1,0:T(8,128)(2,1)S(1)} %pad_maximum_fusion), channel_id=1, source_target_pairs={{0,1},{1,0},{2,3},{3,2},{4,5},{5,4},{6,7},{7,6},{8,9},{9,8},{10,11... | collective-permute-start | bytes 3145736 | tf_op jit(solution)/shard_map/ppermute | solution.py:532
  64.3 2.8 %collective-permute-start.8 = (bf16[4,128,128]{2,1,0:T(8,128)(2,1)S(1)}, bf16[4,128,128]{2,1,0:T(8,128)(2,1)S(1)}, u32[]{:S(2)}, u32[]{:S(2)}) collective-permute-start(bf16[4,128,128]{2,1,0:T(8,128)(2,1)S(1)} %all-to-all-done.1), channel_id=1, source_target_pairs={{0,1},{1,0},{2,3},{3,2},{4,5},{5,4},{6,7},{7,6},{8,9},{9,8},{10,11... | collective-permute-start | bytes 393224 | tf_op jit(solution)/shard_map/ppermute | solution.py:532
  64.8 16.3 %collective-permute-start.10 = (bf16[2,128,512]{2,1,0:T(8,128)(2,1)S(1)}, bf16[2,128,512]{2,1,0:T(8,128)(2,1)S(1)}, u32[]{:S(2)}, u32[]{:S(2)}) collective-permute-start(bf16[2,128,512]{2,1,0:T(8,128)(2,1)S(1)} %copy-done.39), channel_id=1, source_target_pairs={{0,1},{1,0},{2,3},{3,2},{4,5},{5,4},{6,7},{7,6},{8,9},{9,8},{10,11... | collective-permute-start | bytes 786440 | tf_op jit(solution)/shard_map/ppermute | solution.py:532
  64.9 16.2 %collective-permute-start.11 = (bf16[2,128,512]{2,1,0:T(8,128)(2,1)S(1)}, bf16[2,128,512]{2,1,0:T(8,128)(2,1)S(1)}, u32[]{:S(2)}, u32[]{:S(2)}) collective-permute-start(bf16[2,128,512]{2,1,0:T(8,128)(2,1)S(1)} %copy-done.37), channel_id=1, source_target_pairs={{0,9},{1,8},{2,11},{3,10},{4,13},{5,12},{6,15},{7,14},{8,1},{9,0},... | collective-permute-start | bytes 786440 | tf_op jit(solution)/shard_map/ppermute | solution.py:532
  67.1 19.4 %collective-permute-start.12 = (bf16[2,128,512]{2,1,0:T(8,128)(2,1)S(1)}, bf16[2,128,512]{2,1,0:T(8,128)(2,1)S(1)}, u32[]{:S(2)}, u32[]{:S(2)}) collective-permute-start(bf16[2,128,512]{2,1,0:T(8,128)(2,1)S(1)} %copy-done.34), channel_id=1, source_target_pairs={{0,5},{1,4},{2,7},{3,6},{4,1},{5,0},{6,3},{7,2},{8,13},{9,12},{10,... | collective-permute-start | bytes 786440 | tf_op jit(solution)/shard_map/ppermute | solution.py:532
  67.9 24.7 %copy-start.8 = (bf16[2,128,512]{2,1,0:T(8,128)(2,1)S(1)}, bf16[2,128,512]{2,1,0:T(8,128)(2,1)}, u32[]{:S(2)}) copy-start(bf16[2,128,512]{2,1,0:T(8,128)(2,1)} %copy-done.7) | copy-start | bytes 786436
  67.9 24.7 %copy-start.10 = (bf16[2,128,512]{2,1,0:T(8,128)(2,1)S(1)}, bf16[2,128,512]{2,1,0:T(8,128)(2,1)}, u32[]{:S(2)}) copy-start(bf16[2,128,512]{2,1,0:T(8,128)(2,1)} %copy-done.9) | copy-start | bytes 786436
  67.9 24.7 %copy-start.12 = (bf16[2,128,512]{2,1,0:T(8,128)(2,1)S(1)}, bf16[2,128,512]{2,1,0:T(8,128)(2,1)}, u32[]{:S(2)}) copy-start(bf16[2,128,512]{2,1,0:T(8,128)(2,1)} %copy-done.11) | copy-start | bytes 786436
  68.0 18.5 %collective-permute-start.13 = (bf16[2,128,512]{2,1,0:T(8,128)(2,1)S(1)}, bf16[2,128,512]{2,1,0:T(8,128)(2,1)S(1)}, u32[]{:S(2)}, u32[]{:S(2)}) collective-permute-start(bf16[2,128,512]{2,1,0:T(8,128)(2,1)S(1)} %copy-done.31), channel_id=1, source_target_pairs={{0,13},{1,12},{2,15},{3,14},{4,9},{5,8},{6,11},{7,10},{8,5},{9,4},... | collective-permute-start | bytes 786440 | tf_op jit(solution)/shard_map/ppermute | solution.py:532
  69.8 16.7 %collective-permute-start.14 = (bf16[8,128,128]{2,1,0:T(8,128)(2,1)S(1)}, bf16[8,128,128]{2,1,0:T(8,128)(2,1)S(1)}, u32[]{:S(2)}, u32[]{:S(2)}) collective-permute-start(bf16[8,128,128]{2,1,0:T(8,128)(2,1)S(1)} %constant_dynamic-update-slice_fusion.backs), channel_id=1, source_target_pairs={{0,2},{1,3},{2,0},{3,1},{4,6},{5,7},{6,4},{7,5},{8,10},{9,11},{10,... | collective-permute-start | bytes 786440 | tf_op jit(solution)/shard_map/ppermute | solution.py:532
  81.1 15.7 %copy-start.25 = (bf16[2,128,512]{2,1,0:T(8,128)(2,1)}, bf16[2,128,512]{2,1,0:T(8,128)(2,1)S(1)}, u32[]{:S(2)}) copy-start(bf16[2,128,512]{2,1,0:T(8,128)(2,1)S(1)} %get-tuple-element.172) | copy-start | bytes 786436
  81.1 15.7 %copy-start.26 = (bf16[2,128,512]{2,1,0:T(8,128)(2,1)}, bf16[2,128,512]{2,1,0:T(8,128)(2,1)S(1)}, u32[]{:S(2)}) copy-start(bf16[2,128,512]{2,1,0:T(8,128)(2,1)S(1)} %get-tuple-element.181) | copy-start | bytes 786436
  81.1 15.7 %copy-start.27 = (bf16[8,128,128]{2,1,0:T(8,128)(2,1)}, bf16[8,128,128]{2,1,0:T(8,128)(2,1)S(1)}, u32[]{:S(2)}) copy-start(bf16[8,128,128]{2,1,0:T(8,128)(2,1)S(1)} %get-tuple-element.168) | copy-start | bytes 786436
  86.5 10.3 %copy-start.17 = (bf16[8,128,128]{2,1,0:T(8,128)(2,1)}, bf16[8,128,128]{2,1,0:T(8,128)(2,1)S(1)}, u32[]{:S(2)}) copy-start(bf16[8,128,128]{2,1,0:T(8,128)(2,1)S(1)} %collective-permute-done.14.backs_pair) | copy-start | bytes 786436
  86.5 18.3 %collective-permute-start.15 = (bf16[2,128,512]{2,1,0:T(8,128)(2,1)S(1)}, bf16[2,128,512]{2,1,0:T(8,128)(2,1)S(1)}, u32[]{:S(2)}, u32[]{:S(2)}) collective-permute-start(bf16[2,128,512]{2,1,0:T(8,128)(2,1)S(1)} %get-tuple-element.146), channel_id=1, source_target_pairs={{0,8},{1,9},{2,10},{3,11},{4,12},{5,13},{6,14},{7,15},{8,0},{9,1},... | collective-permute-start | bytes 786440 | tf_op jit(solution)/shard_map/ppermute | solution.py:532
  96.8 42.1 %copy-start.18 = (bf16[8,128,128]{2,1,0:T(8,128)(2,1)S(1)}, bf16[8,128,128]{2,1,0:T(8,128)(2,1)}, u32[]{:S(2)}) copy-start(bf16[8,128,128]{2,1,0:T(8,128)(2,1)} %copy-done.17) | copy-start | bytes 786436
  96.8 34.7 %collective-permute-start.19 = (bf16[8,128,512]{2,1,0:T(8,128)(2,1)}, bf16[8,128,512]{2,1,0:T(8,128)(2,1)S(1)}, u32[]{:S(2)}, u32[]{:S(2)}) collective-permute-start(bf16[8,128,512]{2,1,0:T(8,128)(2,1)} %get-tuple-element.161), channel_id=1, source_target_pairs={{0,2},{1,3},{2,0},{3,1},{4,6},{5,7},{6,4},{7,5},{8,10},{9,11},{10,... | collective-permute-start | bytes 3145736 | tf_op jit(solution)/shard_map/ppermute | solution.py:532
  104.8 1.6 collective-permute-start.16
  107.1 24.4 %all-to-all-start.2 = ((f32[4,128,128]{2,1,0:T(8,128)}), f32[4,128,128]{2,1,0:T(8,128)S(1)}, u32[]{:S(2)}, u32[]{:S(2)}) async-start(f32[4,128,128]{2,1,0:T(8,128)} %slice_add_fusion), calls=%async_computation.2 | async-start | bytes 524288 | tf_op jit(solution)/shard_map/all_to_all | solution.py:509
  110.5 12.7 %collective-permute-start.17 = (bf16[2,128,512]{2,1,0:T(8,128)(2,1)}, bf16[2,128,512]{2,1,0:T(8,128)(2,1)S(1)}, u32[]{:S(2)}, u32[]{:S(2)}) collective-permute-start(bf16[2,128,512]{2,1,0:T(8,128)(2,1)} %copy-done.35), channel_id=1, source_target_pairs={{0,4},{1,5},{2,6},{3,7},{4,0},{5,1},{6,2},{7,3},{8,12},{9,13},{10,... | collective-permute-start | bytes 786440 | tf_op jit(solution)/shard_map/ppermute | solution.py:532
  112.5 18.3 %collective-permute-start.18 = (bf16[2,128,512]{2,1,0:T(8,128)(2,1)}, bf16[2,128,512]{2,1,0:T(8,128)(2,1)S(1)}, u32[]{:S(2)}, u32[]{:S(2)}) collective-permute-start(bf16[2,128,512]{2,1,0:T(8,128)(2,1)} %copy-done.32), channel_id=1, source_target_pairs={{0,12},{1,13},{2,14},{3,15},{4,8},{5,9},{6,10},{7,11},{8,4},{9,5},... | collective-permute-start | bytes 786440 | tf_op jit(solution)/shard_map/ppermute | solution.py:532
  131.5 18.2 %collective-permute-start.20 = (bf16[2,128,512]{2,1,0:T(8,128)(2,1)}, bf16[2,128,512]{2,1,0:T(8,128)(2,1)}, u32[]{:S(2)}, u32[]{:S(2)}) collective-permute-start(bf16[2,128,512]{2,1,0:T(8,128)(2,1)} %copy-done.29), channel_id=1, source_target_pairs={{0,1},{1,0},{2,3},{3,2},{4,5},{5,4},{6,7},{7,6},{8,9},{9,8},{10,11... | collective-permute-start | bytes 786440 | tf_op jit(solution)/shard_map/ppermute | solution.py:532
  131.5 18.2 %collective-permute-start.21 = (bf16[2,128,512]{2,1,0:T(8,128)(2,1)}, bf16[2,128,512]{2,1,0:T(8,128)(2,1)}, u32[]{:S(2)}, u32[]{:S(2)}) collective-permute-start(bf16[2,128,512]{2,1,0:T(8,128)(2,1)} %copy-done.28), channel_id=1, source_target_pairs={{0,9},{1,8},{2,11},{3,10},{4,13},{5,12},{6,15},{7,14},{8,1},{9,0},... | collective-permute-start | bytes 786440 | tf_op jit(solution)/shard_map/ppermute | solution.py:532
  132.6 17.2 %collective-permute-start.22 = (bf16[8,128,128]{2,1,0:T(8,128)(2,1)}, bf16[8,128,128]{2,1,0:T(8,128)(2,1)}, u32[]{:S(2)}, u32[]{:S(2)}) collective-permute-start(bf16[8,128,128]{2,1,0:T(8,128)(2,1)} %copy-done.27), channel_id=1, source_target_pairs={{0,2},{1,3},{2,0},{3,1},{4,6},{5,7},{6,4},{7,5},{8,10},{9,11},{10,... | collective-permute-start | bytes 786440 | tf_op jit(solution)/shard_map/ppermute | solution.py:532
  135.3 14.4 %all-to-all-start.3 = ((bf16[4,128,128]{2,1,0:T(8,128)(2,1)}), bf16[4,128,128]{2,1,0:T(8,128)(2,1)S(1)}, u32[]{:S(2)}, u32[]{:S(2)}) async-start(bf16[4,128,128]{2,1,0:T(8,128)(2,1)} %hidden_low.1), calls=%async_computation.3 | async-start | bytes 262144 | tf_op jit(solution)/shard_map/all_to_all | solution.py:509
  139.0 24.8 %copy-start.16 = (bf16[2,128,512]{2,1,0:T(8,128)(2,1)S(1)}, bf16[2,128,512]{2,1,0:T(8,128)(2,1)}, u32[]{:S(2)}) copy-start(bf16[2,128,512]{2,1,0:T(8,128)(2,1)} %copy-done.15) | copy-start | bytes 786436
  149.8 1.4 collective-permute-start.24
  149.8 13.9 %collective-permute-start.26 = (bf16[2,128,512]{2,1,0:T(8,128)(2,1)}, bf16[2,128,512]{2,1,0:T(8,128)(2,1)S(1)}, u32[]{:S(2)}, u32[]{:S(2)}) collective-permute-start(bf16[2,128,512]{2,1,0:T(8,128)(2,1)} %copy-done.26), channel_id=1, source_target_pairs={{0,5},{1,4},{2,7},{3,6},{4,1},{5,0},{6,3},{7,2},{8,13},{9,12},{10,... | collective-permute-start | bytes 786440 | tf_op jit(solution)/shard_map/ppermute | solution.py:532
  150.2 16.9 %copy-start.14 = (bf16[8,128,128]{2,1,0:T(8,128)(2,1)S(1)}, bf16[8,128,128]{2,1,0:T(8,128)(2,1)}, u32[]{:S(2)}) copy-start(bf16[8,128,128]{2,1,0:T(8,128)(2,1)} %copy-done.13) | copy-start | bytes 786436
  151.2 15.9 %collective-permute-start.25 = (bf16[8,128,128]{2,1,0:T(8,128)(2,1)S(1)}, bf16[8,128,128]{2,1,0:T(8,128)(2,1)S(1)}, u32[]{:S(2)}, u32[]{:S(2)}) collective-permute-start(bf16[8,128,128]{2,1,0:T(8,128)(2,1)S(1)} %constant_dynamic-update-slice_fusion.2.hiddens), channel_id=1, source_target_pairs={{0,2},{1,3},{2,0},{3,1},{4,6},{5,7},{6,4},{7,5},{8,10},{9,11},{10,... | collective-permute-start | bytes 786440 | tf_op jit(solution)/shard_map/ppermute | solution.py:532
  152.8 18.5 %collective-permute-start.23 = (bf16[2,128,512]{2,1,0:T(8,128)(2,1)}, bf16[2,128,512]{2,1,0:T(8,128)(2,1)S(1)}, u32[]{:S(2)}, u32[]{:S(2)}) collective-permute-start(bf16[2,128,512]{2,1,0:T(8,128)(2,1)} %copy-done.25), channel_id=1, source_target_pairs={{0,13},{1,12},{2,15},{3,14},{4,9},{5,8},{6,11},{7,10},{8,5},{9,4},... | collective-permute-start | bytes 786440 | tf_op jit(solution)/shard_map/ppermute | solution.py:532
  (23 other events, 26.5 us)

commit v12 on v11

--- a/solution.py
+++ b/solution.py
@@ -574,58 +574,48 @@
     pair = swap(pair, pair_bit)
     early = near[:1] + far[0] + far[1]
     packs = dict(zip(early, pack_tokens(place, tokens, taken(offsets, early), width)))
+    firsts = [gradients[1 << step] for step in range(steps - 1)]
+    firsts, ups_other, packs = barrier((firsts, ups_other, packs))
+
     ups = exchange_side(jnp.stack([ups, ups_other], axis=1))
-    firsts = [gradients[1 << step] for step in range(steps - 1)]
-    firsts, packs = barrier((firsts, packs))
+    arrived = send(packs, early)
+    ups, firsts, tokens, done = barrier((ups, firsts, tokens, taken(arrived, early)))
+    arrived.update(zip(early, done))
     for step in range(steps - 1):
         gradients[1 << step] = firsts[step]
-    window = near[:1] + far[0]
-    arrived = send(packs, window)
-    ups, gradients, packs, tokens, done = barrier(
-        (ups, [gradients[0]] + firsts, packs, tokens, taken(arrived, window))
-    )
-    arrived.update(zip(window, done))
-    gradients = {0: gradients[0], **{1 << step: gradients[1 + step] for step in range(steps - 1)}}
-
+
+    late = [slot for slot in range(members) if slot not in early]
+    packs = dict(zip(late, pack_tokens(place, tokens, taken(offsets, late), width)))
+    arrived.update(send(packs, late[1:]))
+    arrived[0] = packs[0]
     backs = exchange_line(back_rows(adapters, place, ranks, output_gradient, ups))
-    arrived.update(send(packs, far[1]))
+    backs = both_cores(backs)
     for step in range(1, steps - 1):
         for slot in range(1, 1 << step):
             gradients[slot + (1 << step)] = swap(gradients[slot], offsets[1 << step])
-    gradients = taken(gradients, range(lines))
-    rest = [slot for slot in range(members) if slot not in early]
-    packs.update(zip(rest, pack_tokens(place, tokens, taken(offsets, rest), width)))
-    arrived[0] = packs[0]
-    backs, gradients, packs, done = barrier((backs, gradients, packs, taken(arrived, far[1])))
-    arrived.update(zip(far[1], done))
-
-    backs = both_cores(backs)
-    backs_pair = swap(backs, pair_bit)
     gradients.append(swap(jnp.concatenate(gradients, axis=0), 1))
-    arrived.update(send(packs, near[1:] + far[2] + far[3]))
+    backs, gradients, pair, arrived = barrier(
+        (backs, gradients, pair, taken(arrived, range(members)))
+    )
+
+    parts, tokens_own, tokens_pair = hidden_parts(adapters, place, down_maps, pair, arrived)
+    parts, gradients = barrier((parts, gradients))
+    tokens_other = swap(tokens_pair, pair_bit)
     *slices, columns, columns_pair = input_slices(
         adapters, place, gradients, backs, value_weight, pair, down_maps
     )
-    slices, arrived, backs_pair = barrier((slices, taken(arrived, range(members)), backs_pair))
-
-    parts, tokens_own, tokens_pair = hidden_parts(adapters, place, down_maps, pair, arrived)
     results = {0: slices[0]}
     results.update(send(slices, far[0]))
-    parts, done, slices = barrier((parts, taken(results, far[0]), slices))
+    parts = exchange_line(parts[:lines] + swap(parts[lines:], 1))
+    parts, done, slices, columns_pair, backs = barrier(
+        (parts, taken(results, far[0]), slices, columns_pair, backs)
+    )
     results.update(zip(far[0], done))
 
-    window = near[:1] + far[1]
-    results.update(send(slices, window))
-    tokens_other = swap(tokens_pair, pair_bit)
-    parts = exchange_line(parts[:lines] + swap(parts[lines:], 1))
-    parts, done, slices, tokens_other, columns_pair = barrier(
-        (parts, taken(results, window), slices, tokens_other, columns_pair)
-    )
-    results.update(zip(window, done))
-
-    window = near[1:2] + far[2]
+    window = near[:1] + far[1] + far[2]
     results.update(send(slices, window))
     hiddens = exchange_line(hidden_rows(adapters, place, ranks, parts))
+    backs_pair = swap(backs, pair_bit)
     columns_other = swap(columns_pair, pair_bit)
     down_gradient = down_gradients(
         adapters, place, backs, backs_pair, tokens_own, tokens_other, num_adapters
@@ -635,7 +625,7 @@
     )
     results.update(zip(window, done))
 
-    results.update(send(slices, near[2:] + far[3]))
+    results.update(send(slices, near[1:] + far[3]))
     hiddens = both_cores(hiddens)
     hiddens_pair = swap(hiddens, pair_bit)
     up_gradient = up_gradients(

time: 173 us -> 192 us (1.11); the launches traced: 172 us -> 189 us
  local copies, waits for them, and re-layouts: 14.8 us -> 21.2 us
  waiting for transfers between devices: 71.3 us -> 77.4 us
  starting transfers between devices: 51.4 us -> 56.1 us
    ppermute x27, waiting for transfers between devices: 59.6 us -> 68.1 us  [swap(): return lax.ppermute(array, 'dp', [(i, i ^ flip) for i in range(devices)])]
    unnamed x82 -> x91, local copies, waits for them, and re-layouts: 14.7 us -> 21.2 us
    all_to_all x4, starting transfers between devices: 13.8 us -> 19.6 us  [exchange(): lax.all_to_all(pieces, 'dp', split_axis=0, concat_axis=0, axis_index_grou...]
    all_to_all x4, waiting for transfers between devices: 11.7 us -> 9.26 us  [exchange(): lax.all_to_all(pieces, 'dp', split_axis=0, concat_axis=0, axis_index_grou...]
  transfers between devices with their start and end apart: 31 -> 31, of which waited for: 13 -> 14; matrix products, arithmetic and copies ran while one was open for 2% -> 1% of each run, Pallas kernels for 17% -> 14%
where the time goes in v12:
time: 192 us; the launch traced here: 189 us
  waiting for transfers between devices  77.4 us (40%)
  starting transfers between devices  56.1 us (29%)
  Pallas kernels  30.6 us (16%)
  local copies, waits for them, and re-layouts  21.2 us (11%)
  other arithmetic  2.65 us (1%)
    ppermute x27, waiting for transfers between devices, swap(): return lax.ppermute(array, 'dp', [(i, i ^ flip) for i in range(devices)])  68.1 us
    ppermute x27, starting transfers between devices, swap(): return lax.ppermute(array, 'dp', [(i, i ^ flip) for i in range(devices)])  36.6 us
    unnamed x91, local copies, waits for them, and re-layouts  21.2 us
    all_to_all x4, starting transfers between devices, exchange(): lax.all_to_all(pieces, 'dp', split_axis=0, concat_axis=0, axis_index_grou...  19.6 us
    pallas_call x4, Pallas kernels, call(): pl.pallas_call(kernel, out_shape=out_shapes, grid_spec=pltpu.PrefetchScal...  13.1 us
    pallas_call x2, Pallas kernels, sums_call(): pl.pallas_call(kernel, out_shape=jax.ShapeDtypeStruct((num_adapters,) + p...  9.93 us
    all_to_all x4, waiting for transfers between devices, exchange(): lax.all_to_all(pieces, 'dp', split_axis=0, concat_axis=0, axis_index_grou...  9.26 us
    pallas_call x4, Pallas kernels, copy_call(): pl.pallas_call(kernel, out_shape=out_shapes, grid_spec=pltpu.PrefetchScal...  5.53 us
  transfers between devices with their start and end apart: 31, of which 14 were waited for; matrix products, arithmetic and copies ran while one was open for 1% of the time, Pallas kernels for 14%

profile of v12, /device:TPU:0, one launch (start us, length us, event | category | flops | bytes accessed | tf_op | source)
XLA Modules:
  0.0 188.9 jit_solution(3519936983138367948)
XLA Ops:
  0.6 4.1 %collective-permute-start = (bf16[1,128,1024]{2,1,0:T(8,128)(2,1)}, bf16[1,128,1024]{2,1,0:T(8,128)(2,1)S(1)}, u32[]{:S(2)}, u32[]{:S(2)}) collective-permute-start(bf16[1,128,1024]{2,1,0:T(8,128)(2,1)} %bitcast.4), channel_id=1, source_target_pairs={{0,8},{1,9},{2,10},{3,11},{4,12},{5,13},{6,14},{7,15},{8,0},{9,1},... | collective-permute-start | bytes 786440 | tf_op jit(solution)/shard_map/ppermute | solution.py:532
  4.7 1.6 collective-permute-start.1
  6.3 1.2 copy-done.10
  8.2 1.1 gather_up.1
  9.3 1.6 collective-permute-start.2
  10.9 1.2 copy-done.1
  12.1 3.3 %for_pair.1 = bf16[2048,512]{1,0:T(8,128)(2,1)} custom-call(s32[16]{0:T(128)S(1)} %copy-done.27, s32[1]{0:T(128)} %bitcast.place, bf16[1024,512]{1,0:T(8,128)(2,1)S(1)} %copy-done.1, bf16[64,128,512]{2,1,0:T(8,128)(2,1)} %refs_12_.1), custom_call_target="tpu_custom_call" | custom-call | tf_op jit(solution)/shard_map/for_pair/pallas_call | solution.py:74
  18.0 4.5 %all-to-all-start = ((bf16[8,2,64,128]{3,2,1,0:T(8,128)(2,1)}), bf16[8,2,64,128]{3,2,1,0:T(8,128)(2,1)S(1)}, u32[]{:S(2)}, u32[]{:S(2)}) async-start(bf16[8,2,64,128]{3,2,1,0:T(8,128)(2,1)} %pad_maximum_fusion.1), calls=%async_computation | async-start | bytes 524288 | tf_op jit(solution)/shard_map/all_to_all | solution.py:509
  22.5 2.0 %collective-permute-start.3 = (bf16[2,128,512]{2,1,0:T(8,128)(2,1)}, bf16[2,128,512]{2,1,0:T(8,128)(2,1)S(1)}, u32[]{:S(2)}, u32[]{:S(2)}) collective-permute-start(bf16[2,128,512]{2,1,0:T(8,128)(2,1)} %copy-done.44), channel_id=1, source_target_pairs={{0,4},{1,5},{2,6},{3,7},{4,0},{5,1},{6,2},{7,3},{8,12},{9,13},{10,... | collective-permute-start | bytes 786440 | tf_op jit(solution)/shard_map/ppermute | solution.py:532
  24.5 2.4 %collective-permute-start.4 = (bf16[2,128,512]{2,1,0:T(8,128)(2,1)}, bf16[2,128,512]{2,1,0:T(8,128)(2,1)S(1)}, u32[]{:S(2)}, u32[]{:S(2)}) collective-permute-start(bf16[2,128,512]{2,1,0:T(8,128)(2,1)} %copy-done.43), channel_id=1, source_target_pairs={{0,8},{1,9},{2,10},{3,11},{4,12},{5,13},{6,14},{7,15},{8,0},{9,1},... | collective-permute-start | bytes 786440 | tf_op jit(solution)/shard_map/ppermute | solution.py:532
  26.9 13.8 %collective-permute-done.3.refs_10_ = bf16[2,128,512]{2,1,0:T(8,128)(2,1)S(1)} collective-permute-done((bf16[2,128,512]{2,1,0:T(8,128)(2,1)}, bf16[2,128,512]{2,1,0:T(8,128)(2,1)S(1)}, u32[]{:S(2)}, u32[]{:S(2)}) %collective-permute-start.3) | collective-permute-done | bytes 262176 | tf_op jit(solution)/shard_map/ppermute | solution.py:532
  41.4 8.2 %collective-permute-done.4.refs_9_ = bf16[2,128,512]{2,1,0:T(8,128)(2,1)S(1)} collective-permute-done((bf16[2,128,512]{2,1,0:T(8,128)(2,1)}, bf16[2,128,512]{2,1,0:T(8,128)(2,1)S(1)}, u32[]{:S(2)}, u32[]{:S(2)}) %collective-permute-start.4) | collective-permute-done | bytes 262176 | tf_op jit(solution)/shard_map/ppermute | solution.py:532
  51.7 5.0 %collective-permute-start.7 = (bf16[1,128,1024]{2,1,0:T(8,128)(2,1)S(1)}, bf16[1,128,1024]{2,1,0:T(8,128)(2,1)S(1)}, u32[]{:S(2)}, u32[]{:S(2)}) collective-permute-start(bf16[1,128,1024]{2,1,0:T(8,128)(2,1)S(1)} %collective-permute-done.refs_1_), channel_id=1, source_target_pairs={{0,4},{1,5},{2,6},{3,7},{4,0},{5,1},{6,2},{7,3},{8,12},{9,13},{10,... | collective-permute-start | bytes 786440 | tf_op jit(solution)/shard_map/ppermute | solution.py:532
  56.7 6.2 %collective-permute-done.7.refs_3_ = bf16[1,128,1024]{2,1,0:T(8,128)(2,1)S(1)} collective-permute-done((bf16[1,128,1024]{2,1,0:T(8,128)(2,1)S(1)}, bf16[1,128,1024]{2,1,0:T(8,128)(2,1)S(1)}, u32[]{:S(2)}, u32[]{:S(2)}) %collective-permute-start.7) | collective-permute-done | bytes 262176 | tf_op jit(solution)/shard_map/ppermute | solution.py:532
  63.0 1.1 pad_maximum_fusion
  64.1 1.5 back_low.1
  65.6 3.3 %all-to-all-start.1 = ((bf16[4,128,128]{2,1,0:T(8,128)(2,1)}), bf16[4,128,128]{2,1,0:T(8,128)(2,1)S(1)}, u32[]{:S(2)}, u32[]{:S(2)}) async-start(bf16[4,128,128]{2,1,0:T(8,128)(2,1)} %back_low.1), calls=%async_computation.1 | async-start | bytes 262144 | tf_op jit(solution)/shard_map/all_to_all | solution.py:509
  68.9 1.0 pack_tokens.3
  73.2 2.1 %all-to-all-done.1 = bf16[4,128,128]{2,1,0:T(8,128)(2,1)S(1)} async-done(((bf16[4,128,128]{2,1,0:T(8,128)(2,1)}), bf16[4,128,128]{2,1,0:T(8,128)(2,1)S(1)}, u32[]{:S(2)}, u32[]{:S(2)}) %all-to-all-start.1) | async-done | bytes 131104 | tf_op jit(solution)/shard_map/all_to_all | solution.py:509
  75.4 1.0 collective-permute-start.11
  76.4 1.2 collective-permute-start.12
  77.6 2.0 %collective-permute-start.13 = (bf16[2,128,512]{2,1,0:T(8,128)(2,1)}, bf16[2,128,512]{2,1,0:T(8,128)(2,1)S(1)}, u32[]{:S(2)}, u32[]{:S(2)}) collective-permute-start(bf16[2,128,512]{2,1,0:T(8,128)(2,1)} %copy-done.40), channel_id=1, source_target_pairs={{0,13},{1,12},{2,15},{3,14},{4,9},{5,8},{6,11},{7,10},{8,5},{9,4},... | collective-permute-start | bytes 786440 | tf_op jit(solution)/shard_map/ppermute | solution.py:532
  79.6 10.4 %collective-permute-done.11.refs_13_ = bf16[2,128,512]{2,1,0:T(8,128)(2,1)S(1)} collective-permute-done((bf16[2,128,512]{2,1,0:T(8,128)(2,1)}, bf16[2,128,512]{2,1,0:T(8,128)(2,1)S(1)}, u32[]{:S(2)}, u32[]{:S(2)}) %collective-permute-start.11) | collective-permute-done | bytes 262176 | tf_op jit(solution)/shard_map/ppermute | solution.py:532
  90.1 6.5 %collective-permute-done.13.refs_15_ = bf16[2,128,512]{2,1,0:T(8,128)(2,1)S(1)} collective-permute-done((bf16[2,128,512]{2,1,0:T(8,128)(2,1)}, bf16[2,128,512]{2,1,0:T(8,128)(2,1)S(1)}, u32[]{:S(2)}, u32[]{:S(2)}) %collective-permute-start.13) | collective-permute-done | bytes 262176 | tf_op jit(solution)/shard_map/ppermute | solution.py:532
  96.5 0.9 copy-done.16
  97.5 0.9 copy-done.18
  98.4 0.9 copy-done.20
  100.3 4.1 %hidden_parts.1 = (f32[8,128,128]{2,1,0:T(8,128)S(1)}, bf16[8,128,512]{2,1,0:T(8,128)(2,1)S(1)}, bf16[8,128,512]{2,1,0:T(8,128)(2,1)}) custom-call(s32[16]{0:T(128)S(1)} %copy-done.28, s32[1]{0:T(128)} %bitcast.place, bf16[2048,512]{1,0:T(8,128)(2,1)} %collective-permute-done.9.pair, bf16[64,128,512]{2,1,0:T(8,128)(2,1)} %refs_12_.1, ...), custom_call_target="tpu_custom_call" | custom-call | tf_op jit(solution)/shard_map/hidden_parts/pallas_call | solution.py:51
  104.4 1.0 copy-done.13
  106.0 1.5 collective-permute-start.21
  108.2 7.3 %all-to-all-start.2 = ((f32[4,128,128]{2,1,0:T(8,128)}), f32[4,128,128]{2,1,0:T(8,128)}, u32[]{:S(2)}, u32[]{:S(2)}) async-start(f32[4,128,128]{2,1,0:T(8,128)} %slice_add_fusion), calls=%async_computation.2 | async-start | bytes 524288 | tf_op jit(solution)/shard_map/all_to_all | solution.py:509
  115.5 5.4 %input_slices.1 = (bf16[2,128,512]{2,1,0:T(8,128)(2,1)S(1)}, bf16[2,128,512]{2,1,0:T(8,128)(2,1)S(1)}, bf16[2,128,512]{2,1,0:T(8,128)(2,1)S(1)}, bf16[2,128,512]...) custom-call(s32[16]{0:T(128)S(1)} %copy-done.28, ...), custom_call_target="tpu_custom_call" | custom-call | tf_op jit(solution)/shard_map/input_slices/pallas_call | solution.py:51
  127.3 2.9 %collective-permute-start.15 = (bf16[2,128,512]{2,1,0:T(8,128)(2,1)S(1)}, bf16[2,128,512]{2,1,0:T(8,128)(2,1)S(1)}, u32[]{:S(2)}, u32[]{:S(2)}) collective-permute-start(bf16[2,128,512]{2,1,0:T(8,128)(2,1)S(1)} %get-tuple-element.130), channel_id=1, source_target_pairs={{0,8},{1,9},{2,10},{3,11},{4,12},{5,13},{6,14},{7,15},{8,0},{9,1},... | collective-permute-start | bytes 786440 | tf_op jit(solution)/shard_map/ppermute | solution.py:532
  130.2 12.0 %collective-permute-done.15.refs_1_ = bf16[2,128,512]{2,1,0:T(8,128)(2,1)S(1)} collective-permute-done((bf16[2,128,512]{2,1,0:T(8,128)(2,1)S(1)}, bf16[2,128,512]{2,1,0:T(8,128)(2,1)S(1)}, u32[]{:S(2)}, u32[]{:S(2)}) %collective-permute-start.15) | collective-permute-done | bytes 262176 | tf_op jit(solution)/shard_map/ppermute | solution.py:532
  142.2 1.4 collective-permute-start.20
  144.0 2.8 %collective-permute-start.17 = (bf16[2,128,512]{2,1,0:T(8,128)(2,1)}, bf16[2,128,512]{2,1,0:T(8,128)(2,1)S(1)}, u32[]{:S(2)}, u32[]{:S(2)}) collective-permute-start(bf16[2,128,512]{2,1,0:T(8,128)(2,1)} %copy-done.38), channel_id=1, source_target_pairs={{0,12},{1,13},{2,14},{3,15},{4,8},{5,9},{6,10},{7,11},{8,4},{9,5},... | collective-permute-start | bytes 786440 | tf_op jit(solution)/shard_map/ppermute | solution.py:532
  146.8 3.1 %collective-permute-done.20.backs_pair = bf16[8,128,128]{2,1,0:T(8,128)(2,1)S(1)} collective-permute-done((bf16[8,128,128]{2,1,0:T(8,128)(2,1)S(1)}, bf16[8,128,128]{2,1,0:T(8,128)(2,1)S(1)}, u32[]{:S(2)}, u32[]{:S(2)}) %collective-permute-start.20) | collective-permute-done | bytes 262176 | tf_op jit(solution)/shard_map/ppermute | solution.py:532
  149.8 1.5 collective-permute-start.19
  151.4 2.2 %hidden_low.1 = bf16[4,128,128]{2,1,0:T(8,128)(2,1)} custom-call(s32[16]{0:T(128)S(1)} %copy-done.28, s32[1]{0:T(128)} %bitcast.place, s32[64]{0:T(128)S(1)} %copy-done.29, f32[4,128,128]{2,1,0:T(8,128)} %all-to-all-done.2.parts), custom_call_target="tpu_custom_call" | custom-call | tf_op jit(solution)/shard_map/hidden_low/pallas_call | solution.py:51
  153.5 4.4 %all-to-all-start.3 = ((bf16[4,128,128]{2,1,0:T(8,128)(2,1)}), bf16[4,128,128]{2,1,0:T(8,128)(2,1)S(1)}, u32[]{:S(2)}, u32[]{:S(2)}) async-start(bf16[4,128,128]{2,1,0:T(8,128)(2,1)} %hidden_low.1), calls=%async_computation.3 | async-start | bytes 262144 | tf_op jit(solution)/shard_map/all_to_all | solution.py:509
  158.0 1.2 copy-done.14
  159.2 6.3 %down_gradients.1 = bf16[64,128,512]{2,1,0:T(8,128)(2,1)} custom-call(s32[16]{0:T(128)S(1)} %copy-done.28, s32[1]{0:T(128)} %bitcast.place, bf16[8,128,128]{2,1,0:T(8,128)(2,1)S(1)} %pad_maximum_fusion.2.backs, bf16[8,128,128]{2,1,0:T(8,128)(2,1)S(1)} %collective-permute-done.20.backs_pair, bf16[8,128,512]{2,1,0:T(8,128)(2,1)S(1)} %copy-done.14, ...), custom_call_target="tpu_custom_call" | custom-call | tf_op jit(solution)/shard_map/down_gradients/pallas_call | solution.py:410
  165.5 7.1 %all-to-all-done.3 = bf16[4,128,128]{2,1,0:T(8,128)(2,1)S(1)} async-done(((bf16[4,128,128]{2,1,0:T(8,128)(2,1)}), bf16[4,128,128]{2,1,0:T(8,128)(2,1)S(1)}, u32[]{:S(2)}, u32[]{:S(2)}) %all-to-all-start.3) | async-done | bytes 131104 | tf_op jit(solution)/shard_map/all_to_all | solution.py:509
  174.8 2.1 %collective-permute-start.22 = (bf16[2,128,512]{2,1,0:T(8,128)(2,1)S(1)}, bf16[2,128,512]{2,1,0:T(8,128)(2,1)S(1)}, u32[]{:S(2)}, u32[]{:S(2)}) collective-permute-start(bf16[2,128,512]{2,1,0:T(8,128)(2,1)S(1)} %copy-done.31), channel_id=1, source_target_pairs={{0,13},{1,12},{2,15},{3,14},{4,9},{5,8},{6,11},{7,10},{8,5},{9,4},... | collective-permute-start | bytes 786440 | tf_op jit(solution)/shard_map/ppermute | solution.py:532
  176.9 4.7 %collective-permute-done.26.refs_6_ = bf16[2,128,512]{2,1,0:T(8,128)(2,1)S(1)} collective-permute-done((bf16[2,128,512]{2,1,0:T(8,128)(2,1)S(1)}, bf16[2,128,512]{2,1,0:T(8,128)(2,1)S(1)}, u32[]{:S(2)}, u32[]{:S(2)}) %collective-permute-start.26) | collective-permute-done | bytes 262176 | tf_op jit(solution)/shard_map/ppermute | solution.py:532
  181.6 1.3 join_columns.2.refs_1_
  183.0 3.6 %up_gradients.1 = bf16[64,64,128]{2,1,0:T(8,128)(2,1)} custom-call(s32[16]{0:T(128)S(1)} %copy-done.28, s32[1]{0:T(128)} %bitcast.place, s32[64]{0:T(128)S(1)} %copy-done.29, bf16[8,128,128]{2,1,0:T(8,128)(2,1)S(1)} %copy-done.24, bf16[8,128,128]{2,1,0:T(8,128)(2,1)S(1)} %collective-permute-done.19.gradients_pair, ...), custom_call_target="tpu_custom_call" | custom-call | tf_op jit(solution)/shard_map/up_gradients/pallas_call | solution.py:410
  186.6 1.6 collective-permute-done.22.refs_0_
  (123 shorter events, 21.2 us)
Async XLA Ops:
  0.6 16.3 %collective-permute-start = (bf16[1,128,1024]{2,1,0:T(8,128)(2,1)}, bf16[1,128,1024]{2,1,0:T(8,128)(2,1)S(1)}, u32[]{:S(2)}, u32[]{:S(2)}) collective-permute-start(bf16[1,128,1024]{2,1,0:T(8,128)(2,1)} %bitcast.4), channel_id=1, source_target_pairs={{0,8},{1,9},{2,10},{3,11},{4,12},{5,13},{6,14},{7,15},{8,0},{9,1},... | collective-permute-start | bytes 786440 | tf_op jit(solution)/shard_map/ppermute | solution.py:532
  4.7 12.4 %collective-permute-start.1 = (bf16[1,128,1024]{2,1,0:T(8,128)(2,1)}, bf16[1,128,1024]{2,1,0:T(8,128)(2,1)S(1)}, u32[]{:S(2)}, u32[]{:S(2)}) collective-permute-start(bf16[1,128,1024]{2,1,0:T(8,128)(2,1)} %bitcast.5), channel_id=1, source_target_pairs={{0,4},{1,5},{2,6},{3,7},{4,0},{5,1},{6,2},{7,3},{8,12},{9,13},{10,... | collective-permute-start | bytes 786440 | tf_op jit(solution)/shard_map/ppermute | solution.py:532
  9.3 6.8 %copy-start = (bf16[128,8192]{1,0:T(8,128)(2,1)S(1)}, bf16[128,8192]{1,0:T(8,128)(2,1)}, u32[]{:S(2)}) copy-start(bf16[128,8192]{1,0:T(8,128)(2,1)} %tokens.2) | copy-start | bytes 6291460
  9.3 6.1 %collective-permute-start.2 = (bf16[8,64,128]{2,1,0:T(8,128)(2,1)S(1)}, bf16[8,64,128]{2,1,0:T(8,128)(2,1)S(1)}, u32[]{:S(2)}, u32[]{:S(2)}) collective-permute-start(bf16[8,64,128]{2,1,0:T(8,128)(2,1)S(1)} %get-tuple-element.84), channel_id=1, source_target_pairs={{0,2},{1,3},{2,0},{3,1},{4,6},{5,7},{6,4},{7,5},{8,10},{9,11},{10,... | collective-permute-start | bytes 393224 | tf_op jit(solution)/shard_map/ppermute | solution.py:532
  15.4 47.6 %copy-start.3 = (bf16[128,1024]{1,0:T(8,128)(2,1)S(1)}, bf16[128,1024]{1,0:T(8,128)(2,1)}, u32[]{:S(2)}) copy-start(bf16[128,1024]{1,0:T(8,128)(2,1)} %gradient.1) | copy-start | bytes 786436
  15.4 81.1 %collective-permute-start.9 = (bf16[2048,512]{1,0:T(8,128)(2,1)}, bf16[2048,512]{1,0:T(8,128)(2,1)}, u32[]{:S(2)}, u32[]{:S(2)}) collective-permute-start(bf16[2048,512]{1,0:T(8,128)(2,1)} %for_pair.1), channel_id=1, source_target_pairs={{0,2},{1,3},{2,0},{3,1},{4,6},{5,7},{6,4},{7,5},{8,10},{9,11},{10,... | collective-permute-start | bytes 6291464 | tf_op jit(solution)/shard_map/ppermute | solution.py:532
  16.3 1.7 copy-start.43
  16.3 47.8 %copy-start.28 = (s32[16]{0:T(128)S(1)}, s32[16]{0:T(128)}, u32[]{:S(2)}) copy-start(s32[16]{0:T(128)} %adapters.15) | copy-start | bytes 196
  16.3 47.8 %copy-start.29 = (s32[64]{0:T(128)S(1)}, s32[64]{0:T(128)}, u32[]{:S(2)}) copy-start(s32[64]{0:T(128)} %ranks.5) | copy-start | bytes 772
  17.0 46.0 %copy-start.4 = (bf16[1,128,1024]{2,1,0:T(8,128)(2,1)}, bf16[1,128,1024]{2,1,0:T(8,128)(2,1)S(1)}, u32[]{:S(2)}) copy-start(bf16[1,128,1024]{2,1,0:T(8,128)(2,1)S(1)} %collective-permute-done.refs_1_) | copy-start | bytes 786436
  17.2 45.8 %copy-start.6 = (bf16[1,128,1024]{2,1,0:T(8,128)(2,1)}, bf16[1,128,1024]{2,1,0:T(8,128)(2,1)S(1)}, u32[]{:S(2)}) copy-start(bf16[1,128,1024]{2,1,0:T(8,128)(2,1)S(1)} %collective-permute-done.1.refs_2_) | copy-start | bytes 786436
  18.0 33.1 %all-to-all-start = ((bf16[8,2,64,128]{3,2,1,0:T(8,128)(2,1)}), bf16[8,2,64,128]{3,2,1,0:T(8,128)(2,1)S(1)}, u32[]{:S(2)}, u32[]{:S(2)}) async-start(bf16[8,2,64,128]{3,2,1,0:T(8,128)(2,1)} %pad_maximum_fusion.1), calls=%async_computation | async-start | bytes 524288 | tf_op jit(solution)/shard_map/all_to_all | solution.py:509
  22.5 18.2 %collective-permute-start.3 = (bf16[2,128,512]{2,1,0:T(8,128)(2,1)}, bf16[2,128,512]{2,1,0:T(8,128)(2,1)S(1)}, u32[]{:S(2)}, u32[]{:S(2)}) collective-permute-start(bf16[2,128,512]{2,1,0:T(8,128)(2,1)} %copy-done.44), channel_id=1, source_target_pairs={{0,4},{1,5},{2,6},{3,7},{4,0},{5,1},{6,2},{7,3},{8,12},{9,13},{10,... | collective-permute-start | bytes 786440 | tf_op jit(solution)/shard_map/ppermute | solution.py:532
  24.5 25.1 %collective-permute-start.4 = (bf16[2,128,512]{2,1,0:T(8,128)(2,1)}, bf16[2,128,512]{2,1,0:T(8,128)(2,1)S(1)}, u32[]{:S(2)}, u32[]{:S(2)}) collective-permute-start(bf16[2,128,512]{2,1,0:T(8,128)(2,1)} %copy-done.43), channel_id=1, source_target_pairs={{0,8},{1,9},{2,10},{3,11},{4,12},{5,13},{6,14},{7,15},{8,0},{9,1},... | collective-permute-start | bytes 786440 | tf_op jit(solution)/shard_map/ppermute | solution.py:532
  26.9 23.4 %collective-permute-start.5 = (bf16[2,128,512]{2,1,0:T(8,128)(2,1)S(1)}, bf16[2,128,512]{2,1,0:T(8,128)(2,1)S(1)}, u32[]{:S(2)}, u32[]{:S(2)}) collective-permute-start(bf16[2,128,512]{2,1,0:T(8,128)(2,1)S(1)} %get-tuple-element.94), channel_id=1, source_target_pairs={{0,12},{1,13},{2,14},{3,15},{4,8},{5,9},{6,10},{7,11},{8,4},{9,5},... | collective-permute-start | bytes 786440 | tf_op jit(solution)/shard_map/ppermute | solution.py:532
  51.7 11.2 %collective-permute-start.7 = (bf16[1,128,1024]{2,1,0:T(8,128)(2,1)S(1)}, bf16[1,128,1024]{2,1,0:T(8,128)(2,1)S(1)}, u32[]{:S(2)}, u32[]{:S(2)}) collective-permute-start(bf16[1,128,1024]{2,1,0:T(8,128)(2,1)S(1)} %collective-permute-done.refs_1_), channel_id=1, source_target_pairs={{0,4},{1,5},{2,6},{3,7},{4,0},{5,1},{6,2},{7,3},{8,12},{9,13},{10,... | collective-permute-start | bytes 786440 | tf_op jit(solution)/shard_map/ppermute | solution.py:532
  56.7 7.4 %copy-start.12 = (bf16[8,2,64,128]{3,2,1,0:T(8,128)(2,1)S(1)}, bf16[8,2,64,128]{3,2,1,0:T(8,128)(2,1)}, u32[]{:S(2)}) copy-start(bf16[8,2,64,128]{3,2,1,0:T(8,128)(2,1)} %copy-done.11) | copy-start | bytes 786436
  64.1 32.4 %collective-permute-start.8 = (bf16[4,128,1024]{2,1,0:T(8,128)(2,1)}, bf16[4,128,1024]{2,1,0:T(8,128)(2,1)S(1)}, u32[]{:S(2)}, u32[]{:S(2)}) collective-permute-start(bf16[4,128,1024]{2,1,0:T(8,128)(2,1)} %pad_maximum_fusion), channel_id=1, source_target_pairs={{0,1},{1,0},{2,3},{3,2},{4,5},{5,4},{6,7},{7,6},{8,9},{9,8},{10,11... | collective-permute-start | bytes 3145736 | tf_op jit(solution)/shard_map/ppermute | solution.py:532
  65.6 9.8 %all-to-all-start.1 = ((bf16[4,128,128]{2,1,0:T(8,128)(2,1)}), bf16[4,128,128]{2,1,0:T(8,128)(2,1)S(1)}, u32[]{:S(2)}, u32[]{:S(2)}) async-start(bf16[4,128,128]{2,1,0:T(8,128)(2,1)} %back_low.1), calls=%async_computation.1 | async-start | bytes 262144 | tf_op jit(solution)/shard_map/all_to_all | solution.py:509
  72.7 3.7 %collective-permute-start.10 = (bf16[2,128,512]{2,1,0:T(8,128)(2,1)}, bf16[2,128,512]{2,1,0:T(8,128)(2,1)S(1)}, u32[]{:S(2)}, u32[]{:S(2)}) collective-permute-start(bf16[2,128,512]{2,1,0:T(8,128)(2,1)} %get-tuple-element.104), channel_id=1, source_target_pairs={{0,1},{1,0},{2,3},{3,2},{4,5},{5,4},{6,7},{7,6},{8,9},{9,8},{10,11... | collective-permute-start | bytes 786440 | tf_op jit(solution)/shard_map/ppermute | solution.py:532
  75.4 2.3 %collective-permute-start.6 = (bf16[4,128,128]{2,1,0:T(8,128)(2,1)S(1)}, bf16[4,128,128]{2,1,0:T(8,128)(2,1)S(1)}, u32[]{:S(2)}, u32[]{:S(2)}) collective-permute-start(bf16[4,128,128]{2,1,0:T(8,128)(2,1)S(1)} %all-to-all-done.1), channel_id=1, source_target_pairs={{0,1},{1,0},{2,3},{3,2},{4,5},{5,4},{6,7},{7,6},{8,9},{9,8},{10,11... | collective-permute-start | bytes 393224 | tf_op jit(solution)/shard_map/ppermute | solution.py:532
  75.4 14.7 %collective-permute-start.11 = (bf16[2,128,512]{2,1,0:T(8,128)(2,1)}, bf16[2,128,512]{2,1,0:T(8,128)(2,1)S(1)}, u32[]{:S(2)}, u32[]{:S(2)}) collective-permute-start(bf16[2,128,512]{2,1,0:T(8,128)(2,1)} %copy-done.42), channel_id=1, source_target_pairs={{0,9},{1,8},{2,11},{3,10},{4,13},{5,12},{6,15},{7,14},{8,1},{9,0},... | collective-permute-start | bytes 786440 | tf_op jit(solution)/shard_map/ppermute | solution.py:532
  76.4 13.7 %collective-permute-start.12 = (bf16[2,128,512]{2,1,0:T(8,128)(2,1)}, bf16[2,128,512]{2,1,0:T(8,128)(2,1)S(1)}, u32[]{:S(2)}, u32[]{:S(2)}) collective-permute-start(bf16[2,128,512]{2,1,0:T(8,128)(2,1)} %copy-done.41), channel_id=1, source_target_pairs={{0,5},{1,4},{2,7},{3,6},{4,1},{5,0},{6,3},{7,2},{8,13},{9,12},{10,... | collective-permute-start | bytes 786440 | tf_op jit(solution)/shard_map/ppermute | solution.py:532
  77.6 18.9 %collective-permute-start.13 = (bf16[2,128,512]{2,1,0:T(8,128)(2,1)}, bf16[2,128,512]{2,1,0:T(8,128)(2,1)S(1)}, u32[]{:S(2)}, u32[]{:S(2)}) collective-permute-start(bf16[2,128,512]{2,1,0:T(8,128)(2,1)} %copy-done.40), channel_id=1, source_target_pairs={{0,13},{1,12},{2,15},{3,14},{4,9},{5,8},{6,11},{7,10},{8,5},{9,4},... | collective-permute-start | bytes 786440 | tf_op jit(solution)/shard_map/ppermute | solution.py:532
  100.3 15.1 %copy-start.5 = (bf16[1,128,1024]{2,1,0:T(8,128)(2,1)S(1)}, bf16[1,128,1024]{2,1,0:T(8,128)(2,1)}, u32[]{:S(2)}) copy-start(bf16[1,128,1024]{2,1,0:T(8,128)(2,1)} %copy-done.4) | copy-start | bytes 786436
  100.3 15.1 %copy-start.7 = (bf16[1,128,1024]{2,1,0:T(8,128)(2,1)S(1)}, bf16[1,128,1024]{2,1,0:T(8,128)(2,1)}, u32[]{:S(2)}) copy-start(bf16[1,128,1024]{2,1,0:T(8,128)(2,1)} %copy-done.6) | copy-start | bytes 786436
  100.3 15.1 %copy-start.9 = (bf16[1,128,1024]{2,1,0:T(8,128)(2,1)S(1)}, bf16[1,128,1024]{2,1,0:T(8,128)(2,1)}, u32[]{:S(2)}) copy-start(bf16[1,128,1024]{2,1,0:T(8,128)(2,1)} %copy-done.8) | copy-start | bytes 786436
  105.4 10.1 %copy-start.2 = (bf16[1024,512]{1,0:T(8,128)(2,1)S(1)}, bf16[1024,512]{1,0:T(8,128)(2,1)}, u32[]{:S(2)}) copy-start(bf16[1024,512]{1,0:T(8,128)(2,1)} %refs_13_.1) | copy-start | bytes 3145732
  105.4 2.1 %collective-permute-start.14 = (f32[4,128,128]{2,1,0:T(8,128)S(1)}, f32[4,128,128]{2,1,0:T(8,128)S(1)}, u32[]{:S(2)}, u32[]{:S(2)}) collective-permute-start(f32[4,128,128]{2,1,0:T(8,128)S(1)} %slice.7), channel_id=1, source_target_pairs={{0,1},{1,0},{2,3},{3,2},{4,5},{5,4},{6,7},{7,6},{8,9},{9,8},{10,11... | collective-permute-start | bytes 786440 | tf_op jit(solution)/shard_map/ppermute | solution.py:532
  106.0 52.0 %collective-permute-start.21 = (bf16[8,128,512]{2,1,0:T(8,128)(2,1)}, bf16[8,128,512]{2,1,0:T(8,128)(2,1)}, u32[]{:S(2)}, u32[]{:S(2)}) collective-permute-start(bf16[8,128,512]{2,1,0:T(8,128)(2,1)} %get-tuple-element.149), channel_id=1, source_target_pairs={{0,2},{1,3},{2,0},{3,1},{4,6},{5,7},{6,4},{7,5},{8,10},{9,11},{10,... | collective-permute-start | bytes 3145736 | tf_op jit(solution)/shard_map/ppermute | solution.py:532
  108.2 34.0 %all-to-all-start.2 = ((f32[4,128,128]{2,1,0:T(8,128)}), f32[4,128,128]{2,1,0:T(8,128)}, u32[]{:S(2)}, u32[]{:S(2)}) async-start(f32[4,128,128]{2,1,0:T(8,128)} %slice_add_fusion), calls=%async_computation.2 | async-start | bytes 524288 | tf_op jit(solution)/shard_map/all_to_all | solution.py:509
  127.3 15.0 %collective-permute-start.15 = (bf16[2,128,512]{2,1,0:T(8,128)(2,1)S(1)}, bf16[2,128,512]{2,1,0:T(8,128)(2,1)S(1)}, u32[]{:S(2)}, u32[]{:S(2)}) collective-permute-start(bf16[2,128,512]{2,1,0:T(8,128)(2,1)S(1)} %get-tuple-element.130), channel_id=1, source_target_pairs={{0,8},{1,9},{2,10},{3,11},{4,12},{5,13},{6,14},{7,15},{8,0},{9,1},... | collective-permute-start | bytes 786440 | tf_op jit(solution)/shard_map/ppermute | solution.py:532
  142.2 7.6 %collective-permute-start.20 = (bf16[8,128,128]{2,1,0:T(8,128)(2,1)S(1)}, bf16[8,128,128]{2,1,0:T(8,128)(2,1)S(1)}, u32[]{:S(2)}, u32[]{:S(2)}) collective-permute-start(bf16[8,128,128]{2,1,0:T(8,128)(2,1)S(1)} %pad_maximum_fusion.2.backs), channel_id=1, source_target_pairs={{0,2},{1,3},{2,0},{3,1},{4,6},{5,7},{6,4},{7,5},{8,10},{9,11},{10,... | collective-permute-start | bytes 786440 | tf_op jit(solution)/shard_map/ppermute | solution.py:532
  143.7 29.0 %collective-permute-start.16 = (bf16[2,128,512]{2,1,0:T(8,128)(2,1)}, bf16[2,128,512]{2,1,0:T(8,128)(2,1)S(1)}, u32[]{:S(2)}, u32[]{:S(2)}) collective-permute-start(bf16[2,128,512]{2,1,0:T(8,128)(2,1)} %copy-done.39), channel_id=1, source_target_pairs={{0,4},{1,5},{2,6},{3,7},{4,0},{5,1},{6,2},{7,3},{8,12},{9,13},{10,... | collective-permute-start | bytes 786440 | tf_op jit(solution)/shard_map/ppermute | solution.py:532
  144.0 28.7 %collective-permute-start.17 = (bf16[2,128,512]{2,1,0:T(8,128)(2,1)}, bf16[2,128,512]{2,1,0:T(8,128)(2,1)S(1)}, u32[]{:S(2)}, u32[]{:S(2)}) collective-permute-start(bf16[2,128,512]{2,1,0:T(8,128)(2,1)} %copy-done.38), channel_id=1, source_target_pairs={{0,12},{1,13},{2,14},{3,15},{4,8},{5,9},{6,10},{7,11},{8,4},{9,5},... | collective-permute-start | bytes 786440 | tf_op jit(solution)/shard_map/ppermute | solution.py:532
  146.8 25.9 %collective-permute-start.18 = (bf16[2,128,512]{2,1,0:T(8,128)(2,1)}, bf16[2,128,512]{2,1,0:T(8,128)(2,1)S(1)}, u32[]{:S(2)}, u32[]{:S(2)}) collective-permute-start(bf16[2,128,512]{2,1,0:T(8,128)(2,1)} %copy-done.37), channel_id=1, source_target_pairs={{0,9},{1,8},{2,11},{3,10},{4,13},{5,12},{6,15},{7,14},{8,1},{9,0},... | collective-permute-start | bytes 786440 | tf_op jit(solution)/shard_map/ppermute | solution.py:532
  149.8 22.8 %collective-permute-start.19 = (bf16[8,128,128]{2,1,0:T(8,128)(2,1)}, bf16[8,128,128]{2,1,0:T(8,128)(2,1)S(1)}, u32[]{:S(2)}, u32[]{:S(2)}) collective-permute-start(bf16[8,128,128]{2,1,0:T(8,128)(2,1)} %copy-done.36), channel_id=1, source_target_pairs={{0,2},{1,3},{2,0},{3,1},{4,6},{5,7},{6,4},{7,5},{8,10},{9,11},{10,... | collective-permute-start | bytes 786440 | tf_op jit(solution)/shard_map/ppermute | solution.py:532
  153.5 19.1 %all-to-all-start.3 = ((bf16[4,128,128]{2,1,0:T(8,128)(2,1)}), bf16[4,128,128]{2,1,0:T(8,128)(2,1)S(1)}, u32[]{:S(2)}, u32[]{:S(2)}) async-start(bf16[4,128,128]{2,1,0:T(8,128)(2,1)} %hidden_low.1), calls=%async_computation.3 | async-start | bytes 262144 | tf_op jit(solution)/shard_map/all_to_all | solution.py:509
  159.2 13.6 %copy-start.35 = (bf16[2,128,512]{2,1,0:T(8,128)(2,1)S(1)}, bf16[2,128,512]{2,1,0:T(8,128)(2,1)}, u32[]{:S(2)}) copy-start(bf16[2,128,512]{2,1,0:T(8,128)(2,1)} %copy-done.34) | copy-start | bytes 786436
  159.2 14.1 %copy-start.33 = (bf16[2,128,512]{2,1,0:T(8,128)(2,1)S(1)}, bf16[2,128,512]{2,1,0:T(8,128)(2,1)}, u32[]{:S(2)}) copy-start(bf16[2,128,512]{2,1,0:T(8,128)(2,1)} %copy-done.32) | copy-start | bytes 786436
  159.2 15.6 %copy-start.31 = (bf16[2,128,512]{2,1,0:T(8,128)(2,1)S(1)}, bf16[2,128,512]{2,1,0:T(8,128)(2,1)}, u32[]{:S(2)}) copy-start(bf16[2,128,512]{2,1,0:T(8,128)(2,1)} %copy-done.30) | copy-start | bytes 786436
  159.2 22.4 %copy-start.26 = (bf16[2,128,512]{2,1,0:T(8,128)(2,1)S(1)}, bf16[2,128,512]{2,1,0:T(8,128)(2,1)}, u32[]{:S(2)}) copy-start(bf16[2,128,512]{2,1,0:T(8,128)(2,1)} %copy-done.25) | copy-start | bytes 786436
  172.7 1.4 collective-permute-start.23
  172.8 4.2 %collective-permute-start.25 = (bf16[2,128,512]{2,1,0:T(8,128)(2,1)S(1)}, bf16[2,128,512]{2,1,0:T(8,128)(2,1)S(1)}, u32[]{:S(2)}, u32[]{:S(2)}) collective-permute-start(bf16[2,128,512]{2,1,0:T(8,128)(2,1)S(1)} %copy-done.35), channel_id=1, source_target_pairs={{0,1},{1,0},{2,3},{3,2},{4,5},{5,4},{6,7},{7,6},{8,9},{9,8},{10,11... | collective-permute-start | bytes 786440 | tf_op jit(solution)/shard_map/ppermute | solution.py:532
  173.3 8.3 %collective-permute-start.26 = (bf16[2,128,512]{2,1,0:T(8,128)(2,1)S(1)}, bf16[2,128,512]{2,1,0:T(8,128)(2,1)S(1)}, u32[]{:S(2)}, u32[]{:S(2)}) collective-permute-start(bf16[2,128,512]{2,1,0:T(8,128)(2,1)S(1)} %copy-done.33), channel_id=1, source_target_pairs={{0,5},{1,4},{2,7},{3,6},{4,1},{5,0},{6,3},{7,2},{8,13},{9,12},{10,... | collective-permute-start | bytes 786440 | tf_op jit(solution)/shard_map/ppermute | solution.py:532
  173.3 9.7 %copy-start.24 = (bf16[8,128,128]{2,1,0:T(8,128)(2,1)S(1)}, bf16[8,128,128]{2,1,0:T(8,128)(2,1)}, u32[]{:S(2)}) copy-start(bf16[8,128,128]{2,1,0:T(8,128)(2,1)} %copy-done.23) | copy-start | bytes 786436
  174.1 8.8 %collective-permute-start.24 = (bf16[8,128,128]{2,1,0:T(8,128)(2,1)S(1)}, bf16[8,128,128]{2,1,0:T(8,128)(2,1)S(1)}, u32[]{:S(2)}, u32[]{:S(2)}) collective-permute-start(bf16[8,128,128]{2,1,0:T(8,128)(2,1)S(1)} %constant_dynamic-update-slice_fusion.hiddens), channel_id=1, source_target_pairs={{0,2},{1,3},{2,0},{3,1},{4,6},{5,7},{6,4},{7,5},{8,10},{9,11},{10,... | collective-permute-start | bytes 786440 | tf_op jit(solution)/shard_map/ppermute | solution.py:532
  174.8 13.3 %collective-permute-start.22 = (bf16[2,128,512]{2,1,0:T(8,128)(2,1)S(1)}, bf16[2,128,512]{2,1,0:T(8,128)(2,1)S(1)}, u32[]{:S(2)}, u32[]{:S(2)}) collective-permute-start(bf16[2,128,512]{2,1,0:T(8,128)(2,1)S(1)} %copy-done.31), channel_id=1, source_target_pairs={{0,13},{1,12},{2,15},{3,14},{4,9},{5,8},{6,11},{7,10},{8,5},{9,4},... | collective-permute-start | bytes 786440 | tf_op jit(solution)/shard_map/ppermute | solution.py:532
  (28 other events, 23.1 us)

commit v13 on v6

v13 whole, which is shorter than its diff:
```python
import functools

import jax
import jax.numpy as jnp
from jax import lax
from jax.experimental import pallas as pl
from jax.experimental.pallas import tpu as pltpu
from jax.sharding import PartitionSpec as P

adapter_alpha = 32.0
vmem_limit = 48 * 1024 * 1024
pair_bit = 2
line_bit = 4


def line_offset(slot, members):
    bits = members.bit_length() - 1
    order = 0
    for bit in range(bits):
        order |= ((slot >> bit) & 1) << (bits - 1 - bit)
    return ((order // 2) * line_bit) | (order % 2)


def side_of(place):
    return place % line_bit // pair_bit


def side_index(place):
    return place // line_bit * pair_bit + place % pair_bit


def side_place(index, side):
    return index // pair_bit * line_bit + side * pair_bit + index % pair_bit


def params():
    return pltpu.CompilerParams(vmem_limit_bytes=vmem_limit)


def whole(shape):
    return pl.BlockSpec(shape, lambda *_: (0,) * len(shape))


def picked(maps, flip):
    return pl.BlockSpec(
        (1,) + maps.shape[1:], lambda i, adapters, place, *_: (adapters[place[0] ^ flip], 0, 0)
    )


def call(kernel, name, prefetch, operands, in_specs, out_shapes, scratch=(), grid=(1,), out_specs=None):
    if out_specs is None:
        out_specs = [whole(shape.shape) for shape in out_shapes]
    return pl.pallas_call(
        kernel,
        out_shape=out_shapes,
        grid_spec=pltpu.PrefetchScalarGridSpec(
            num_scalar_prefetch=len(prefetch),
            grid=grid,
            in_specs=in_specs,
            out_specs=out_specs,
            scratch_shapes=list(scratch),
        ),
        compiler_params=params(),
        name=name,
    )(*prefetch, *operands)


def run(copies):
    for copy in copies:
        copy.start()
    for copy in copies:
        copy.wait()


def copy_call(kernel, name, prefetch, operands, out_shapes, copies):
    return pl.pallas_call(
        kernel,
        out_shape=out_shapes,
        grid_spec=pltpu.PrefetchScalarGridSpec(
            num_scalar_prefetch=len(prefetch),
            grid=(1,),
            in_specs=[pl.BlockSpec(memory_space=pl.ANY)] * len(operands),
            out_specs=[whole(shape.shape) for shape in out_shapes],
            scratch_shapes=[pltpu.SemaphoreType.DMA((copies,))],
        ),
        compiler_params=params(),
        name=name,
    )(*prefetch, *operands)


weight_cuts = 4


def pair_kernel(adapters, place, weight, down_maps, out, sems):
    extent = down_maps.shape[1]
    depth = weight.shape[0]
    members = (out.shape[0] - depth) // extent
    copies = []
    for slot in range(members):
        block = place[0] ^ line_offset(slot, members) ^ pair_bit
        copies.append((down_maps.at[adapters[block]], slot * extent, extent))
    cut = depth // weight_cuts
    for at in range(0, depth, cut):
        copies.append((weight.at[pl.ds(at, cut)], members * extent + at, cut))
    run(
        [
            pltpu.make_async_copy(source, out.at[pl.ds(at, rows)], sems.at[number])
            for number, (source, at, rows) in enumerate(copies)
        ]
    )


def for_pair(adapters, place, weight, down_maps, members):
    extent, width = down_maps.shape[1:]
    shape = jax.ShapeDtypeStruct((members * extent + weight.shape[0], width), weight.dtype)
    return copy_call(
        pair_kernel,
        "for_pair",
        (adapters, place),
        (weight, down_maps),
        [shape],
        members + weight_cuts,
    )[0]


def gather_up_kernel(adapters, up_maps, out, sems):
    run(
        [
            pltpu.make_async_copy(up_maps.at[adapters[block]], out.at[block], sems.at[block])
            for block in range(out.shape[0])
        ]
    )


def gather_up(adapters, up_maps):
    shape = jax.ShapeDtypeStruct((adapters.shape[0],) + up_maps.shape[1:], up_maps.dtype)
    return copy_call(
        gather_up_kernel, "gather_up", (adapters,), (up_maps,), [shape], adapters.shape[0]
    )[0]


def pack_kernel(place, tokens, out, sems):
    members, _, _, width = out.shape
    copies = []
    for index in range(members):
        for half in range(2):
            column = side_place(index, side_of(place[0]) ^ half) * width
            copies.append(
                pltpu.make_async_copy(
                    tokens.at[:, pl.ds(pl.multiple_of(column, width), width)],
                    out.at[index, half],
                    sems.at[2 * index + half],
                )
            )
    run(copies)


def pack_tokens(place, tokens, members, width):
    shape = jax.ShapeDtypeStruct((members, 2, tokens.shape[0], width), tokens.dtype)
    return copy_call(pack_kernel, "pack_tokens", (place,), (tokens,), [shape], 2 * members)[0]


def rank_row(ranks, adapter, extent):
    rank = jnp.full((1, extent), ranks[adapter], jnp.int32)
    alive = (lax.broadcasted_iota(jnp.int32, (1, extent), 1) < rank).astype(jnp.float32)
    return alive, adapter_alpha / rank.astype(jnp.float32)


def back_kernel(adapters, place, ranks, gradient, up, out):
    alive, factor = rank_row(ranks, adapters[place[0]], up.shape[1])
    back = jnp.dot(gradient[...], up[...], preferred_element_type=jnp.float32)
    out[0] = (factor * back * alive).astype(out.dtype)


def back_rows(adapters, place, ranks, gradient, up):
    return call(
        back_kernel,
        "back_low",
        (adapters, place, ranks),
        (gradient, up),
        [whole(gradient.shape), whole(up.shape)],
        [jax.ShapeDtypeStruct((1, gradient.shape[0], up.shape[1]), jnp.bfloat16)],
    )[0]


def input_kernel(adapters, place, backs, pair, *refs):
    members, rows, _ = backs.shape
    apart = members // 2
    gradients = [ref.at[0] for ref in refs[:apart]]
    gradients += [refs[apart].at[slot] for slot in range(members - apart)]
    downs = refs[apart + 1 : apart + 1 + members]
    weight = refs[apart + 1 + members]
    out, *columns = refs[-3:]
    extent = downs[0].shape[1]
    lanes = columns[0].shape[2]
    value_width = gradients[0].shape[1] // (2 * members)
    some = min(4, members)
    for first in range(0, members, some):
        slots = range(first, first + some)
        lines = jnp.concatenate([gradients[slot][...] for slot in slots], axis=0)
        for half in range(2):
            right = weight[...] if half == 0 else pair[members * extent :]
            frozen = jnp.dot(lines, right, preferred_element_type=jnp.float32)
            for slot in slots:
                down = downs[slot][0] if half == 0 else pair[slot * extent : (slot + 1) * extent]
                index = side_index(place[0] ^ line_offset(slot, members))
                low = jnp.dot(backs[slot], down, preferred_element_type=jnp.float32)
                at = (slot - first) * rows
                out[index, half] = (frozen[at : at + rows] + low).astype(jnp.bfloat16)
    for side in range(2):
        column = (place[0] ^ (side * pair_bit)) * value_width // lanes * lanes
        for slot in range(members):
            columns[side][slot] = gradients[slot][:, pl.ds(pl.multiple_of(column, lanes), lanes)]


def input_slices(adapters, place, gradients, backs, weight, pair, down_maps):
    members, rows, _ = backs.shape
    width = weight.shape[1]
    lanes = max(128, gradients[0].shape[2] // (2 * members))
    shape = jax.ShapeDtypeStruct((members, 2, rows, width), jnp.bfloat16)
    columns = jax.ShapeDtypeStruct((members, rows, lanes), jnp.bfloat16)
    return call(
        input_kernel,
        "input_slices",
        (adapters, place),
        [backs, pair] + list(gradients) + [down_maps] * members + [weight],
        [whole(backs.shape), whole(pair.shape)]
        + [whole(gradient.shape) for gradient in gradients]
        + [picked(down_maps, line_offset(slot, members)) for slot in range(members)]
        + [whole(weight.shape)],
        [shape, columns, columns],
    )


def hidden_kernel(adapters, place, pair, tokens, *refs):
    parts, own, other = refs[-3:]
    members = own.shape[0]
    downs = refs[:members]
    extent = downs[0].shape[1]
    across = (((1,), (1,)), ((), ()))
    for slot in range(members):
        index = side_index(place[0] ^ line_offset(slot, members))
        own[slot] = tokens[index, 0]
        other[slot] = tokens[index, 1]
        parts[slot] = lax.dot_general(
            tokens[index, 0], downs[slot][0], across, preferred_element_type=jnp.float32
        ) + lax.dot_general(
            tokens[index, 1],
            pair[slot * extent : (slot + 1) * extent],
            across,
            preferred_element_type=jnp.float32,
        )


def hidden_parts(adapters, place, down_maps, pair, tokens):
    members, _, rows, width = tokens.shape
    extent = down_maps.shape[1]
    tokens_shape = jax.ShapeDtypeStruct((members, rows, width), tokens.dtype)
    return call(
        hidden_kernel,
        "hidden_parts",
        (adapters, place),
        [pair, tokens] + [down_maps] * members,
        [whole(pair.shape), whole(tokens.shape)]
        + [picked(down_maps, line_offset(slot, members)) for slot in range(members)],
        [
            jax.ShapeDtypeStruct((members, rows, extent), jnp.float32),
            tokens_shape,
            tokens_shape,
        ],
    )


def sum_kernel(total, received, *outs, flip):
    for slot in range(outs[0].shape[0]):
        value = total[slot] + received[slot ^ flip].astype(jnp.float32)
        for out in outs:
            out[slot] = value.astype(out.dtype)


def slot_sums(total, received, flip, types):
    shape = received.shape
    return call(
        functools.partial(sum_kernel, flip=flip),
        "slot_sums",
        (),
        (total, received),
        [whole(shape)] * 2,
        [jax.ShapeDtypeStruct(shape, kind) for kind in types],
    )


def hidden_low_kernel(adapters, place, ranks, total, received, out, *, flip, members):
    for slot in range(out.shape[0]):
        block = place[0] ^ line_offset(slot, members)
        alive, _ = rank_row(ranks, adapters[block], out.shape[2])
        value = total[slot] + received[slot ^ flip].astype(jnp.float32)
        out[slot] = (value * alive).astype(out.dtype)


def hidden_rows(adapters, place, ranks, total, received, flip, members):
    return call(
        functools.partial(hidden_low_kernel, flip=flip, members=members),
        "hidden_low",
        (adapters, place, ranks),
        (total, received),
        [whole(total.shape)] * 2,
        [jax.ShapeDtypeStruct(total.shape, jnp.bfloat16)],
    )[0]


def join_kernel(place, source, out, sems):
    members, _, _, width = source.shape
    copies = []
    for index in range(members):
        for half in range(2):
            column = side_place(index, side_of(place[0]) ^ half) * width
            copies.append(
                pltpu.make_async_copy(
                    source.at[index, half],
                    out.at[:, pl.ds(pl.multiple_of(column, width), width)],
                    sems.at[2 * index + half],
                )
            )
    run(copies)


def join_columns(place, source):
    members, _, rows, width = source.shape
    return pl.pallas_call(
        join_kernel,
        out_shape=jax.ShapeDtypeStruct((rows, 2 * members * width), source.dtype),
        grid_spec=pltpu.PrefetchScalarGridSpec(
            num_scalar_prefetch=1,
            grid=(1,),
            in_specs=[whole(source.shape)],
            out_specs=pl.BlockSpec(memory_space=pl.ANY),
            scratch_shapes=[pltpu.SemaphoreType.DMA((2 * members,))],
        ),
        compiler_params=params(),
        name="join_columns",
    )(place, source)


def list_members(adapters, place, members, head, following):
    def clear(adapter, carry):
        head[adapter] = -1
        return carry

    lax.fori_loop(0, head.shape[0], clear, 0)
    for entry in reversed(range(2 * members)):
        side, own = divmod(entry, members)
        adapter = adapters[place[0] ^ line_offset(own, members) ^ (side * pair_bit)]
        following[entry] = head[adapter]
        head[adapter] = entry


def write_sums(head, following, products, ready, zero, out, sems, finish):
    num_adapters = out.shape[0]
    zero[...] = jnp.zeros_like(zero)

    def write(adapter, carry):
        first = head[adapter]

        @pl.when(first < 0)
        def _():
            pltpu.make_async_copy(zero, out.at[adapter], sems.at[adapter]).start()

        @pl.when(first >= 0)
        def _():
            def more(entry):
                products[first] += products[entry]
                return following[entry]

            lax.while_loop(lambda entry: entry >= 0, more, following[first])
            ready[first] = finish(adapter, products[first]).astype(out.dtype)
            pltpu.make_async_copy(ready.at[first], out.at[adapter], sems.at[adapter]).start()

        return carry

    lax.fori_loop(0, num_adapters, write, 0)

    def wait(adapter, carry):
        pltpu.make_async_copy(zero, out.at[adapter], sems.at[adapter]).wait()
        return carry

    lax.fori_loop(0, num_adapters, wait, 0)


def by_rows(left, right):
    return lax.dot_general(
        left, right, (((0,), (0,)), ((), ())), preferred_element_type=jnp.float32
    )


def sums_call(kernel, name, prefetch, operands, num_adapters, entries, product, scratch=()):
    return pl.pallas_call(
        kernel,
        out_shape=jax.ShapeDtypeStruct((num_adapters,) + product, jnp.bfloat16),
        grid_spec=pltpu.PrefetchScalarGridSpec(
            num_scalar_prefetch=len(prefetch),
            grid=(1,),
            in_specs=[whole(operand.shape) for operand in operands],
            out_specs=pl.BlockSpec(memory_space=pltpu.HBM),
            scratch_shapes=[
                pltpu.SMEM((num_adapters,), jnp.int32),
                pltpu.SMEM((entries,), jnp.int32),
                pltpu.VMEM((entries,) + product, jnp.float32),
                pltpu.VMEM((entries,) + product, jnp.bfloat16),
                pltpu.VMEM(product, jnp.bfloat16),
                pltpu.SemaphoreType.DMA((num_adapters,)),
                *scratch,
            ],
        ),
        compiler_params=params(),
        name=name,
    )(*prefetch, *operands)


def down_gradient_kernel(
    adapters, place, backs, backs_pair, own, other, out, head, following, products, ready, zero, sems
):
    members = own.shape[0]
    list_members(adapters, place, members, head, following)
    for slot in range(members):
        products[slot] = by_rows(backs[slot], own[slot])
        products[members + slot] = by_rows(backs_pair[slot], other[slot])
    write_sums(
        head, following, products, ready, zero, out, sems, lambda adapter, total: total
    )


def down_gradients(adapters, place, backs, backs_pair, own, other, num_adapters):
    members, _, width = own.shape
    return sums_call(
        down_gradient_kernel,
        "down_gradients",
        (adapters, place),
        (backs, backs_pair, own, other),
        num_adapters,
        2 * members,
        (backs.shape[2], width),
    )


def up_gradient_kernel(
    adapters,
    place,
    ranks,
    gradients,
    gradients_pair,
    hiddens,
    hiddens_pair,
    out,
    head,
    following,
    products,
    ready,
    zero,
    sems,
    lines,
):
    members, _, lanes = gradients.shape
    width, extent = out.shape[1:]
    list_members(adapters, place, members, head, following)
    inside = pl.multiple_of(lax.rem(place[0], lanes // width) * width, width)
    for slot in range(members):
        lines[slot] = by_rows(gradients[slot], hiddens[slot])
        lines[members + slot] = by_rows(gradients_pair[slot], hiddens_pair[slot])
    for entry in range(2 * members):
        products[entry] = lines[entry, pl.ds(inside, width), :]

    def finish(adapter, total):
        _, factor = rank_row(ranks, adapter, extent)
        return factor * total

    write_sums(head, following, products, ready, zero, out, sems, finish)


def up_gradients(adapters, place, ranks, gradients, gradients_pair, hiddens, hiddens_pair, width):
    members, _, lanes = gradients.shape
    extent = hiddens.shape[2]
    return sums_call(
        up_gradient_kernel,
        "up_gradients",
        (adapters, place, ranks),
        (gradients, gradients_pair, hiddens, hiddens_pair),
        ranks.shape[0],
        2 * members,
        (width, extent),
        [pltpu.VMEM((2 * members, lanes, extent), jnp.float32)],
    )


def exchange(pieces):
    return lax.all_to_all(pieces, "dp", split_axis=0, concat_axis=0, tiled=True)


def exchange_side(pieces):
    members = pieces.shape[0]
    groups = [[side_place(index, side) for index in range(members)] for side in range(2)]
    return lax.all_to_all(
        pieces, "dp", split_axis=0, concat_axis=0, axis_index_groups=groups, tiled=True
    )


def swap(array, flip):
    devices = lax.axis_size("dp")
    return lax.ppermute(array, "dp", [(i, i ^ flip) for i in range(devices)])


def tie(first, second):
    return lax.optimization_barrier((first, second))


def gather_step(held, members):
    arrived = swap(held, line_offset(held.shape[0], members))
    return jnp.concatenate([held, arrived], axis=0)


def local(tokens, output_gradient, value_weight, down_maps, up_maps, adapter_per_block, ranks):
    devices = lax.axis_size("dp")
    members = devices // 2
    lines = members // 2
    steps = members.bit_length() - 1
    num_adapters, extent, width = down_maps.shape
    rows, depth = output_gradient.shape
    place = lax.axis_index("dp").astype(jnp.int32).reshape(1)
    adapters = adapter_per_block
    offsets = [line_offset(slot, members) for slot in range(members)]
    barrier = lax.optimization_barrier

    own_gradient = output_gradient.reshape(1, rows, depth)
    gradients = [own_gradient] + [None] * (lines - 1)
    for step in range(steps - 1):
        gradients[1 << step] = swap(own_gradient, offsets[1 << step])
    own_up = exchange(gather_up(adapters, up_maps)).reshape(depth, extent)
    packs = pack_tokens(place, tokens, members, width)
    pair = for_pair(adapters, place, value_weight, down_maps, members)
    firsts = [gradients[1 << step] for step in range(steps - 1)]
    firsts, own_up, packs, pair = barrier((firsts, own_up, packs, pair))
    for step in range(steps - 1):
        gradients[1 << step] = firsts[step]

    arrived = exchange_side(packs)
    pair = swap(pair, pair_bit)
    backs = back_rows(adapters, place, ranks, output_gradient, own_up)
    backs = gather_step(backs, members)
    for slot in range(1, 2):
        for step in range(1, min(2, steps - 1)):
            gradients[slot + (1 << step)] = swap(gradients[slot], offsets[1 << step])
    held = [gradients[slot] for slot in range(lines) if gradients[slot] is not None]
    arrived, backs, held, pair = barrier((arrived, backs, held, pair))
    known = [slot for slot in range(lines) if gradients[slot] is not None]
    for slot, block in zip(known, held):
        gradients[slot] = block

    parts, tokens_own, tokens_pair = hidden_parts(adapters, place, down_maps, pair, arrived)
    while backs.shape[0] < members:
        backs = gather_step(backs, members)
    for step in range(1, steps - 1):
        for slot in range(1, 1 << step):
            if gradients[slot + (1 << step)] is None:
                gradients[slot + (1 << step)] = swap(gradients[slot], offsets[1 << step])
    gradients.append(swap(jnp.concatenate(gradients, axis=0), 1))
    slices, columns, columns_pair = input_slices(
        adapters, place, gradients, backs, value_weight, pair, down_maps
    )
    received, flip = swap(parts[lines:], 1), 0
    total = parts
    for step in reversed(range(steps - 1)):
        flipped = 1 << step
        last = step == 0
        sums = slot_sums(
            total, received, flip, [jnp.float32] + [jnp.bfloat16] * last
        )
        total, flip = sums[0], flipped
        received = swap(sums[-1], offsets[flipped])
    received, slices, columns_pair, backs, tokens_pair = barrier(
        (received, slices, columns_pair, backs, tokens_pair)
    )

    result = exchange_side(slices)
    hiddens = hidden_rows(adapters, place, ranks, total, received, flip, members)
    hiddens = gather_step(hiddens, members)
    hiddens_pair = swap(hiddens, pair_bit)
    columns_other = swap(columns_pair, pair_bit)
    backs_pair = swap(backs, pair_bit)
    tokens_other = swap(tokens_pair, pair_bit)
    up_gradient = up_gradients(
        adapters, place, ranks, columns, columns_other, hiddens, hiddens_pair, depth // devices
    )
    down_gradient = down_gradients(
        adapters, place, backs, backs_pair, tokens_own, tokens_other, num_adapters
    )
    up_gradient, down_gradient, result = barrier((up_gradient, down_gradient, result))
    return (join_columns(place, result), down_gradient, up_gradient)


def solution(mesh):
    in_specs = (
        P(("groups", "dp"), None),
        P(("groups", "dp"), None),
        P(None, "dp"),
        P(None, None, "dp"),
        P(None, "dp", None),
        P("groups"),
        P(),
    )
    out_specs = (P(("groups", "dp"), None), P("groups", None, "dp"), P("groups", "dp", None))
    return jax.shard_map(local, mesh=mesh, in_specs=in_specs, out_specs=out_specs, check_vma=False)
```

time: 230 us -> 167 us (0.73)
  Pallas kernels: 67.9 us -> 26.3 us
  starting transfers between devices: 47.5 us -> 31.9 us
  waiting for transfers between devices: 101 us -> 97 us
    ppermute x29 -> x16, waiting for transfers between devices: 64.3 us -> 96.1 us  [swap(): return lax.ppermute(array, 'dp', [(i, i ^ flip) for i in range(devices)])]
    pallas_call x3, Pallas kernels: 35.6 us -> 5.5 us  [copy_call(): pl.pallas_call(kernel, out_shape=out_shapes, grid_spec=pltpu.PrefetchScal...]
    all_to_all x1, waiting for transfers between devices: 22.7 us -> 0.01 us  [exchange(): return lax.all_to_all(pieces, 'dp', split_axis=0, concat_axis=0, tiled=True)]
    ppermute x29 -> x16, starting transfers between devices: 33.1 us -> 16.4 us  [swap(): return lax.ppermute(array, 'dp', [(i, i ^ flip) for i in range(devices)])]
    all_to_all x3 -> x2, waiting for transfers between devices: 13.9 us -> 0.95 us  [exchange_side(): lax.all_to_all(pieces, 'dp', split_axis=0, concat_axis=0, axis_index_grou...]
    pallas_call x2 -> x1, Pallas kernels: 10.1 us -> 1.44 us  [join_columns(): pl.pallas_call(join_kernel, out_shape=jax.ShapeDtypeStruct((rows, 2 * mem...]
    all_to_all x1, starting transfers between devices: 4.33 us -> 7.4 us  [exchange(): return lax.all_to_all(pieces, 'dp', split_axis=0, concat_axis=0, tiled=True)]
    pallas_call x4 -> x6, Pallas kernels: 13.2 us -> 10.3 us  [call(): pl.pallas_call(kernel, out_shape=out_shapes, grid_spec=pltpu.PrefetchScal...]
  transfers between devices with their start and end apart: 33 -> 19, of which waited for: 13 -> 11; matrix products, arithmetic and copies ran while one was open for 0% -> 0% of each run, Pallas kernels for 28% -> 14%
where the time goes in v13:
time: 167 us
  waiting for transfers between devices  97 us (58%)
  starting transfers between devices  31.9 us (19%)
  Pallas kernels  26.3 us (16%)
  local copies, waits for them, and re-layouts  8.8 us (5%)
  other arithmetic  1.88 us (1%)
    ppermute x16, waiting for transfers between devices, swap(): return lax.ppermute(array, 'dp', [(i, i ^ flip) for i in range(devices)])  96.1 us
    ppermute x16, starting transfers between devices, swap(): return lax.ppermute(array, 'dp', [(i, i ^ flip) for i in range(devices)])  16.4 us
    pallas_call x6, Pallas kernels, call(): pl.pallas_call(kernel, out_shape=out_shapes, grid_spec=pltpu.PrefetchScal...  10.3 us
    pallas_call x2, Pallas kernels, sums_call(): pl.pallas_call(kernel, out_shape=jax.ShapeDtypeStruct((num_adapters,) + p...  9.08 us
    unnamed x32, local copies, waits for them, and re-layouts  8.76 us
    all_to_all x2, starting transfers between devices, exchange_side(): lax.all_to_all(pieces, 'dp', split_axis=0, concat_axis=0, axis_index_grou...  8.08 us
    all_to_all x1, starting transfers between devices, exchange(): return lax.all_to_all(pieces, 'dp', split_axis=0, concat_axis=0, tiled=True)  7.4 us
    pallas_call x3, Pallas kernels, copy_call(): pl.pallas_call(kernel, out_shape=out_shapes, grid_spec=pltpu.PrefetchScal...  5.5 us
  transfers between devices with their start and end apart: 19, of which 11 were waited for; matrix products, arithmetic and copies ran while one was open for 0% of the time, Pallas kernels for 14%

profile of v13, /device:TPU:0, one launch (start us, length us, event | category | flops | bytes accessed | tf_op | source)
XLA Modules:
  0.0 166.8 jit_solution(12975277620156222603)
XLA Ops:
  0.6 1.2 copy-done.6
  1.9 0.7 copy-done.11
  2.5 1.8 %gather_up.1 = bf16[16,64,128]{2,1,0:T(8,128)(2,1)} custom-call(s32[16]{0:T(128)S(1)} %copy-done.11, bf16[64,64,128]{2,1,0:T(8,128)(2,1)S(1)} %copy-done.6), custom_call_target="tpu_custom_call" | custom-call | tf_op jit(solution)/shard_map/gather_up/pallas_call | solution.py:76
  4.3 7.4 %all-to-all-start = ((bf16[16,64,128]{2,1,0:T(8,128)(2,1)}), bf16[16,64,128]{2,1,0:T(8,128)(2,1)S(1)}, u32[]{:S(2)}, u32[]{:S(2)}) async-start(bf16[16,64,128]{2,1,0:T(8,128)(2,1)} %gather_up.1), calls=%async_computation | async-start | bytes 524288 | tf_op jit(solution)/shard_map/all_to_all | solution.py:496
  11.7 2.8 %collective-permute-start = (bf16[1,128,1024]{2,1,0:T(8,128)(2,1)}, bf16[1,128,1024]{2,1,0:T(8,128)(2,1)}, u32[]{:S(2)}, u32[]{:S(2)}) collective-permute-start(bf16[1,128,1024]{2,1,0:T(8,128)(2,1)} %bitcast.3), channel_id=1, source_target_pairs={{0,8},{1,9},{2,10},{3,11},{4,12},{5,13},{6,14},{7,15},{8,0},{9,1},... | collective-permute-start | bytes 786440 | tf_op jit(solution)/shard_map/ppermute | solution.py:509
  14.5 1.5 collective-permute-start.1
  16.0 1.6 copy-done.3
  17.6 1.8 %pack_tokens.1 = bf16[8,2,128,512]{3,2,1,0:T(8,128)(2,1)} custom-call(s32[1]{0:T(128)} %bitcast.place, bf16[128,8192]{1,0:T(8,128)(2,1)S(1)} %copy-done.3), custom_call_target="tpu_custom_call" | custom-call | tf_op jit(solution)/shard_map/pack_tokens/pallas_call | solution.py:76
  19.4 1.9 %for_pair.1 = bf16[2048,512]{1,0:T(8,128)(2,1)S(1)} custom-call(s32[16]{0:T(128)S(1)} %copy-done.12, s32[1]{0:T(128)} %bitcast.place, bf16[1024,512]{1,0:T(8,128)(2,1)S(1)} %copy-done.1, bf16[64,128,512]{2,1,0:T(8,128)(2,1)} %refs_7_.3), custom_call_target="tpu_custom_call" | custom-call | tf_op jit(solution)/shard_map/for_pair/pallas_call | solution.py:76
  21.4 1.3 copy-done.5
  22.7 10.0 %collective-permute-done.refs_1_ = bf16[1,128,1024]{2,1,0:T(8,128)(2,1)} collective-permute-done((bf16[1,128,1024]{2,1,0:T(8,128)(2,1)}, bf16[1,128,1024]{2,1,0:T(8,128)(2,1)}, u32[]{:S(2)}, u32[]{:S(2)}) %collective-permute-start) | collective-permute-done | bytes 262176 | tf_op jit(solution)/shard_map/ppermute | solution.py:509
  32.7 0.7 copy-done.7
  33.4 4.5 %all-to-all-start.1 = ((bf16[8,2,128,512]{3,2,1,0:T(8,128)(2,1)}), bf16[8,2,128,512]{3,2,1,0:T(8,128)(2,1)}, u32[]{:S(2)}, u32[]{:S(2)}) async-start(bf16[8,2,128,512]{3,2,1,0:T(8,128)(2,1)} %pack_tokens.1), calls=%async_computation.1 | async-start | bytes 4194304 | tf_op jit(solution)/shard_map/all_to_all | solution.py:502
  37.9 1.5 collective-permute-start.4
  39.4 1.8 %collective-permute-start.3 = (bf16[1,128,1024]{2,1,0:T(8,128)(2,1)}, bf16[1,128,1024]{2,1,0:T(8,128)(2,1)}, u32[]{:S(2)}, u32[]{:S(2)}) collective-permute-start(bf16[1,128,1024]{2,1,0:T(8,128)(2,1)} %collective-permute-done.refs_1_), channel_id=1, source_target_pairs={{0,4},{1,5},{2,6},{3,7},{4,0},{5,1},{6,2},{7,3},{8,12},{9,13},{10,... | collective-permute-start | bytes 786440 | tf_op jit(solution)/shard_map/ppermute | solution.py:509
  41.2 0.9 copy-done.8
  42.2 0.8 back_low.1
  43.0 2.5 %collective-permute-start.2 = (bf16[1,128,128]{2,1,0:T(8,128)(2,1)S(1)}, bf16[1,128,128]{2,1,0:T(8,128)(2,1)S(1)}, u32[]{:S(2)}, u32[]{:S(2)}) collective-permute-start(bf16[1,128,128]{2,1,0:T(8,128)(2,1)S(1)} %back_low.1), channel_id=1, source_target_pairs={{0,8},{1,9},{2,10},{3,11},{4,12},{5,13},{6,14},{7,15},{8,0},{9,1},... | collective-permute-start | bytes 98312 | tf_op jit(solution)/shard_map/ppermute | solution.py:509
  45.4 42.8 %collective-permute-done.2 = bf16[1,128,128]{2,1,0:T(8,128)(2,1)S(1)} collective-permute-done((bf16[1,128,128]{2,1,0:T(8,128)(2,1)S(1)}, bf16[1,128,128]{2,1,0:T(8,128)(2,1)S(1)}, u32[]{:S(2)}, u32[]{:S(2)}) %collective-permute-start.2) | collective-permute-done | bytes 32800 | tf_op jit(solution)/shard_map/ppermute | solution.py:509
  88.3 1.8 %pad_maximum_fusion = bf16[4,128,1024]{2,1,0:T(8,128)(2,1)S(1)} fusion(bf16[1,128,1024]{2,1,0:T(8,128)(2,1)} %collective-permute-done.3.refs_3_, bf16[1,128,1024]{2,1,0:T(8,128)(2,1)} %collective-permute-done.1.refs_2_, bf16[1,128,1024]{2,1,0:T(8,128)(2,1)} %collective-permute-done.refs_1_, bf16[1,128,1024]{2,1,0:T(8,128)(2,1)S(1)} %bitcast.5), kind=kLoop, calls=%fused_computation | loop fusion | flops 1572864 | bytes 2097152 | tf_op jit(solution)/shard_map/concatenate | solution.py:565
  90.1 0.1 collective-permute-start.7
  90.2 3.3 %hidden_parts.1 = (f32[8,128,128]{2,1,0:T(8,128)S(1)}, bf16[8,128,512]{2,1,0:T(8,128)(2,1)S(1)}, bf16[8,128,512]{2,1,0:T(8,128)(2,1)S(1)}) custom-call(s32[16]{0:T(128)S(1)} %copy-done.12, s32[1]{0:T(128)} %bitcast.place, bf16[2048,512]{1,0:T(8,128)(2,1)S(1)} %collective-permute-done.4.pair, bf16[8,2,128,512]{3,2,1,0:T(8,128)(2,1)} %all-to-all-done.1.tokens, ...), custom_call_target="tpu_custom_call" | custom-call | tf_op jit(solution)/shard_map/hidden_parts/pallas_call | solution.py:53
  93.5 1.0 copy-done.9
  94.5 0.6 collective-permute-start.8
  95.0 1.2 collective-permute-done.8.received
  96.2 0.9 collective-permute-start.9
  97.2 2.2 %collective-permute-done.5 = bf16[2,128,128]{2,1,0:T(8,128)(2,1)S(1)} collective-permute-done((bf16[2,128,128]{2,1,0:T(8,128)(2,1)S(1)}, bf16[2,128,128]{2,1,0:T(8,128)(2,1)S(1)}, u32[]{:S(2)}, u32[]{:S(2)}) %collective-permute-start.5) | collective-permute-done | bytes 65568 | tf_op jit(solution)/shard_map/ppermute | solution.py:509
  99.4 0.1 collective-permute-start.6
  99.5 5.4 %collective-permute-done.9.received = f32[4,128,128]{2,1,0:T(8,128)S(1)} collective-permute-done((f32[4,128,128]{2,1,0:T(8,128)S(1)}, f32[4,128,128]{2,1,0:T(8,128)S(1)}, u32[]{:S(2)}, u32[]{:S(2)}) %collective-permute-start.9) | collective-permute-done | bytes 262176 | tf_op jit(solution)/shard_map/ppermute | solution.py:509
  105.0 0.3 collective-permute-start.10
  105.4 5.6 %input_slices.1 = (bf16[8,2,128,512]{3,2,1,0:T(8,128)(2,1)S(1)}, bf16[8,128,128]{2,1,0:T(8,128)(2,1)S(1)}, bf16[8,128,128]{2,1,0:T(8,128)(2,1)S(1)}) custom-call(s32[16]{0:T(128)S(1)} %copy-done.12, s32[1]{0:T(128)} %bitcast.place, bf16[8,128,128]{2,1,0:T(8,128)(2,1)S(1)} %constant_dynamic-update-slice_fusion.backs, bf16[2048,512]{1,0:T(8,128)(2,1)} %copy-done, ...), custom_call_target="tpu_custom_call" | custom-call | tf_op jit(solution)/shard_map/input_slices/pallas_call | solution.py:53
  111.0 1.3 copy-done.4
  112.3 0.4 collective-permute-done.10.received
  112.7 3.6 %all-to-all-start.2 = ((bf16[8,2,128,512]{3,2,1,0:T(8,128)(2,1)}), bf16[8,2,128,512]{3,2,1,0:T(8,128)(2,1)S(1)}, u32[]{:S(2)}, u32[]{:S(2)}) async-start(bf16[8,2,128,512]{3,2,1,0:T(8,128)(2,1)} %copy-done.4), calls=%async_computation.2 | async-start | bytes 4194304 | tf_op jit(solution)/shard_map/all_to_all | solution.py:502
  116.4 1.5 collective-permute-start.15
  117.9 0.6 hidden_low.1
  118.5 0.1 collective-permute-start.12
  118.6 0.6 collective-permute-start.11
  119.2 0.7 collective-permute-done.12
  119.9 0.8 collective-permute-start.13
  120.7 1.3 collective-permute-start.14
  122.0 26.2 %collective-permute-done.11.gradients_pair = bf16[8,128,128]{2,1,0:T(8,128)(2,1)S(1)} collective-permute-done((bf16[8,128,128]{2,1,0:T(8,128)(2,1)S(1)}, bf16[8,128,128]{2,1,0:T(8,128)(2,1)S(1)}, u32[]{:S(2)}, u32[]{:S(2)}) %collective-permute-start.11) | collective-permute-done | bytes 262176 | tf_op jit(solution)/shard_map/ppermute | solution.py:509
  148.2 5.6 %collective-permute-done.13.hiddens_pair = bf16[8,128,128]{2,1,0:T(8,128)(2,1)S(1)} collective-permute-done((bf16[8,128,128]{2,1,0:T(8,128)(2,1)S(1)}, bf16[8,128,128]{2,1,0:T(8,128)(2,1)S(1)}, u32[]{:S(2)}, u32[]{:S(2)}) %collective-permute-start.13) | collective-permute-done | bytes 262176 | tf_op jit(solution)/shard_map/ppermute | solution.py:509
  153.9 3.6 %up_gradients.1 = bf16[64,64,128]{2,1,0:T(8,128)(2,1)} custom-call(s32[16]{0:T(128)S(1)} %copy-done.12, s32[1]{0:T(128)} %bitcast.place, s32[64]{0:T(128)S(1)} %copy-done.13, bf16[8,128,128]{2,1,0:T(8,128)(2,1)S(1)} %get-tuple-element.42.gradients, bf16[8,128,128]{2,1,0:T(8,128)(2,1)S(1)} %collective-permute-done.11.gradients_pair, ...), custom_call_target="tpu_custom_call" | custom-call | tf_op jit(solution)/shard_map/up_gradients/pallas_call | solution.py:397
  157.5 1.4 collective-permute-done.14.backs_pair
  158.9 5.5 %down_gradients.1 = bf16[64,128,512]{2,1,0:T(8,128)(2,1)} custom-call(s32[16]{0:T(128)S(1)} %copy-done.12, s32[1]{0:T(128)} %bitcast.place, bf16[8,128,128]{2,1,0:T(8,128)(2,1)S(1)} %constant_dynamic-update-slice_fusion.backs, bf16[8,128,128]{2,1,0:T(8,128)(2,1)S(1)} %collective-permute-done.14.backs_pair, bf16[8,128,512]{2,1,0:T(8,128)(2,1)S(1)} %copy-done.10, ...), custom_call_target="tpu_custom_call" | custom-call | tf_op jit(solution)/shard_map/down_gradients/pallas_call | solution.py:397
  164.4 0.9 all-to-all-done.2.source
  165.3 1.4 join_columns.1
  (40 shorter events, 0.2 us)
Async XLA Ops:
  0.6 1.2 copy-start.6
  1.9 0.7 copy-start.11
  4.3 28.4 %all-to-all-start = ((bf16[16,64,128]{2,1,0:T(8,128)(2,1)}), bf16[16,64,128]{2,1,0:T(8,128)(2,1)S(1)}, u32[]{:S(2)}, u32[]{:S(2)}) async-start(bf16[16,64,128]{2,1,0:T(8,128)(2,1)} %gather_up.1), calls=%async_computation | async-start | bytes 524288 | tf_op jit(solution)/shard_map/all_to_all | solution.py:496
  11.7 21.0 %collective-permute-start = (bf16[1,128,1024]{2,1,0:T(8,128)(2,1)}, bf16[1,128,1024]{2,1,0:T(8,128)(2,1)}, u32[]{:S(2)}, u32[]{:S(2)}) collective-permute-start(bf16[1,128,1024]{2,1,0:T(8,128)(2,1)} %bitcast.3), channel_id=1, source_target_pairs={{0,8},{1,9},{2,10},{3,11},{4,12},{5,13},{6,14},{7,15},{8,0},{9,1},... | collective-permute-start | bytes 786440 | tf_op jit(solution)/shard_map/ppermute | solution.py:509
  14.5 18.2 %collective-permute-start.1 = (bf16[1,128,1024]{2,1,0:T(8,128)(2,1)}, bf16[1,128,1024]{2,1,0:T(8,128)(2,1)}, u32[]{:S(2)}, u32[]{:S(2)}) collective-permute-start(bf16[1,128,1024]{2,1,0:T(8,128)(2,1)} %bitcast.4), channel_id=1, source_target_pairs={{0,4},{1,5},{2,6},{3,7},{4,0},{5,1},{6,2},{7,3},{8,12},{9,13},{10,... | collective-permute-start | bytes 786440 | tf_op jit(solution)/shard_map/ppermute | solution.py:509
  16.0 1.6 copy-start.3
  17.6 1.8 %copy-start.1 = (bf16[1024,512]{1,0:T(8,128)(2,1)S(1)}, bf16[1024,512]{1,0:T(8,128)(2,1)}, u32[]{:S(2)}) copy-start(bf16[1024,512]{1,0:T(8,128)(2,1)} %refs_13_.1) | copy-start | bytes 3145732
  17.6 1.8 %copy-start.12 = (s32[16]{0:T(128)S(1)}, s32[16]{0:T(128)}, u32[]{:S(2)}) copy-start(s32[16]{0:T(128)} %adapters.15) | copy-start | bytes 196
  21.3 1.3 copy-start.5
  32.7 0.7 copy-start.7
  33.4 7.9 %copy-start.2 = (bf16[128,1024]{1,0:T(8,128)(2,1)S(1)}, bf16[128,1024]{1,0:T(8,128)(2,1)}, u32[]{:S(2)}) copy-start(bf16[128,1024]{1,0:T(8,128)(2,1)} %gradient.1) | copy-start | bytes 786436
  33.4 7.9 %copy-start.13 = (s32[64]{0:T(128)S(1)}, s32[64]{0:T(128)}, u32[]{:S(2)}) copy-start(s32[64]{0:T(128)} %ranks.5) | copy-start | bytes 772
  33.4 54.9 %all-to-all-start.1 = ((bf16[8,2,128,512]{3,2,1,0:T(8,128)(2,1)}), bf16[8,2,128,512]{3,2,1,0:T(8,128)(2,1)}, u32[]{:S(2)}, u32[]{:S(2)}) async-start(bf16[8,2,128,512]{3,2,1,0:T(8,128)(2,1)} %pack_tokens.1), calls=%async_computation.1 | async-start | bytes 4194304 | tf_op jit(solution)/shard_map/all_to_all | solution.py:502
  37.9 50.4 %collective-permute-start.4 = (bf16[2048,512]{1,0:T(8,128)(2,1)}, bf16[2048,512]{1,0:T(8,128)(2,1)S(1)}, u32[]{:S(2)}, u32[]{:S(2)}) collective-permute-start(bf16[2048,512]{1,0:T(8,128)(2,1)} %copy-done.5), channel_id=1, source_target_pairs={{0,2},{1,3},{2,0},{3,1},{4,6},{5,7},{6,4},{7,5},{8,10},{9,11},{10,... | collective-permute-start | bytes 6291464 | tf_op jit(solution)/shard_map/ppermute | solution.py:509
  39.4 48.8 %collective-permute-start.3 = (bf16[1,128,1024]{2,1,0:T(8,128)(2,1)}, bf16[1,128,1024]{2,1,0:T(8,128)(2,1)}, u32[]{:S(2)}, u32[]{:S(2)}) collective-permute-start(bf16[1,128,1024]{2,1,0:T(8,128)(2,1)} %collective-permute-done.refs_1_), channel_id=1, source_target_pairs={{0,4},{1,5},{2,6},{3,7},{4,0},{5,1},{6,2},{7,3},{8,12},{9,13},{10,... | collective-permute-start | bytes 786440 | tf_op jit(solution)/shard_map/ppermute | solution.py:509
  41.2 1.0 copy-start.8
  43.0 45.3 %collective-permute-start.2 = (bf16[1,128,128]{2,1,0:T(8,128)(2,1)S(1)}, bf16[1,128,128]{2,1,0:T(8,128)(2,1)S(1)}, u32[]{:S(2)}, u32[]{:S(2)}) collective-permute-start(bf16[1,128,128]{2,1,0:T(8,128)(2,1)S(1)} %back_low.1), channel_id=1, source_target_pairs={{0,8},{1,9},{2,10},{3,11},{4,12},{5,13},{6,14},{7,15},{8,0},{9,1},... | collective-permute-start | bytes 98312 | tf_op jit(solution)/shard_map/ppermute | solution.py:509
  88.3 5.2 %copy-start = (bf16[2048,512]{1,0:T(8,128)(2,1)}, bf16[2048,512]{1,0:T(8,128)(2,1)S(1)}, u32[]{:S(2)}) copy-start(bf16[2048,512]{1,0:T(8,128)(2,1)S(1)} %collective-permute-done.4.pair) | copy-start | bytes 6291460
  90.1 15.2 %collective-permute-start.7 = (bf16[4,128,1024]{2,1,0:T(8,128)(2,1)S(1)}, bf16[4,128,1024]{2,1,0:T(8,128)(2,1)S(1)}, u32[]{:S(2)}, u32[]{:S(2)}) collective-permute-start(bf16[4,128,1024]{2,1,0:T(8,128)(2,1)S(1)} %pad_maximum_fusion), channel_id=1, source_target_pairs={{0,1},{1,0},{2,3},{3,2},{4,5},{5,4},{6,7},{7,6},{8,9},{9,8},{10,11... | collective-permute-start | bytes 3145736 | tf_op jit(solution)/shard_map/ppermute | solution.py:509
  93.5 1.0 copy-start.9
  94.5 10.9 %copy-start.14 = (bf16[8,128,512]{2,1,0:T(8,128)(2,1)}, bf16[8,128,512]{2,1,0:T(8,128)(2,1)S(1)}, u32[]{:S(2)}) copy-start(bf16[8,128,512]{2,1,0:T(8,128)(2,1)S(1)} %get-tuple-element.54) | copy-start | bytes 3145732
  94.5 1.7 %collective-permute-start.8 = (f32[4,128,128]{2,1,0:T(8,128)S(1)}, f32[4,128,128]{2,1,0:T(8,128)S(1)}, u32[]{:S(2)}, u32[]{:S(2)}) collective-permute-start(f32[4,128,128]{2,1,0:T(8,128)S(1)} %slice.3), channel_id=1, source_target_pairs={{0,1},{1,0},{2,3},{3,2},{4,5},{5,4},{6,7},{7,6},{8,9},{9,8},{10,11... | collective-permute-start | bytes 786440 | tf_op jit(solution)/shard_map/ppermute | solution.py:509
  95.0 4.4 %collective-permute-start.5 = (bf16[2,128,128]{2,1,0:T(8,128)(2,1)S(1)}, bf16[2,128,128]{2,1,0:T(8,128)(2,1)S(1)}, u32[]{:S(2)}, u32[]{:S(2)}) collective-permute-start(bf16[2,128,128]{2,1,0:T(8,128)(2,1)S(1)} %pad_maximum_fusion.3), channel_id=1, source_target_pairs={{0,4},{1,5},{2,6},{3,7},{4,0},{5,1},{6,2},{7,3},{8,12},{9,13},{10,... | collective-permute-start | bytes 196616 | tf_op jit(solution)/shard_map/ppermute | solution.py:509
  96.2 8.7 %collective-permute-start.9 = (f32[4,128,128]{2,1,0:T(8,128)S(1)}, f32[4,128,128]{2,1,0:T(8,128)S(1)}, u32[]{:S(2)}, u32[]{:S(2)}) collective-permute-start(f32[4,128,128]{2,1,0:T(8,128)S(1)} %slot_sums.2.total), channel_id=1, source_target_pairs={{0,4},{1,5},{2,6},{3,7},{4,0},{5,1},{6,2},{7,3},{8,12},{9,13},{10,... | collective-permute-start | bytes 786440 | tf_op jit(solution)/shard_map/ppermute | solution.py:509
  99.4 5.9 %collective-permute-start.6 = (bf16[4,128,128]{2,1,0:T(8,128)(2,1)S(1)}, bf16[4,128,128]{2,1,0:T(8,128)(2,1)S(1)}, u32[]{:S(2)}, u32[]{:S(2)}) collective-permute-start(bf16[4,128,128]{2,1,0:T(8,128)(2,1)S(1)} %pad_maximum_fusion.2), channel_id=1, source_target_pairs={{0,1},{1,0},{2,3},{3,2},{4,5},{5,4},{6,7},{7,6},{8,9},{9,8},{10,11... | collective-permute-start | bytes 393224 | tf_op jit(solution)/shard_map/ppermute | solution.py:509
  105.0 7.8 %collective-permute-start.10 = (bf16[4,128,128]{2,1,0:T(8,128)(2,1)S(1)}, bf16[4,128,128]{2,1,0:T(8,128)(2,1)S(1)}, u32[]{:S(2)}, u32[]{:S(2)}) collective-permute-start(bf16[4,128,128]{2,1,0:T(8,128)(2,1)S(1)} %get-tuple-element.45), channel_id=1, source_target_pairs={{0,8},{1,9},{2,10},{3,11},{4,12},{5,13},{6,14},{7,15},{8,0},{9,1},... | collective-permute-start | bytes 393224 | tf_op jit(solution)/shard_map/ppermute | solution.py:509
  111.0 1.3 copy-start.4
  112.7 52.6 %all-to-all-start.2 = ((bf16[8,2,128,512]{3,2,1,0:T(8,128)(2,1)}), bf16[8,2,128,512]{3,2,1,0:T(8,128)(2,1)S(1)}, u32[]{:S(2)}, u32[]{:S(2)}) async-start(bf16[8,2,128,512]{3,2,1,0:T(8,128)(2,1)} %copy-done.4), calls=%async_computation.2 | async-start | bytes 4194304 | tf_op jit(solution)/shard_map/all_to_all | solution.py:502
  116.4 42.5 %copy-start.10 = (bf16[8,128,512]{2,1,0:T(8,128)(2,1)S(1)}, bf16[8,128,512]{2,1,0:T(8,128)(2,1)}, u32[]{:S(2)}) copy-start(bf16[8,128,512]{2,1,0:T(8,128)(2,1)} %copy-done.9) | copy-start | bytes 3145732
  116.4 42.5 %collective-permute-start.15 = (bf16[8,128,512]{2,1,0:T(8,128)(2,1)}, bf16[8,128,512]{2,1,0:T(8,128)(2,1)S(1)}, u32[]{:S(2)}, u32[]{:S(2)}) collective-permute-start(bf16[8,128,512]{2,1,0:T(8,128)(2,1)} %copy-done.14), channel_id=1, source_target_pairs={{0,2},{1,3},{2,0},{3,1},{4,6},{5,7},{6,4},{7,5},{8,10},{9,11},{10,... | collective-permute-start | bytes 3145736 | tf_op jit(solution)/shard_map/ppermute | solution.py:509
  118.5 1.4 collective-permute-start.12
  118.6 29.6 %collective-permute-start.11 = (bf16[8,128,128]{2,1,0:T(8,128)(2,1)S(1)}, bf16[8,128,128]{2,1,0:T(8,128)(2,1)S(1)}, u32[]{:S(2)}, u32[]{:S(2)}) collective-permute-start(bf16[8,128,128]{2,1,0:T(8,128)(2,1)S(1)} %get-tuple-element.49), channel_id=1, source_target_pairs={{0,2},{1,3},{2,0},{3,1},{4,6},{5,7},{6,4},{7,5},{8,10},{9,11},{10,... | collective-permute-start | bytes 786440 | tf_op jit(solution)/shard_map/ppermute | solution.py:509
  119.9 33.9 %collective-permute-start.13 = (bf16[8,128,128]{2,1,0:T(8,128)(2,1)S(1)}, bf16[8,128,128]{2,1,0:T(8,128)(2,1)S(1)}, u32[]{:S(2)}, u32[]{:S(2)}) collective-permute-start(bf16[8,128,128]{2,1,0:T(8,128)(2,1)S(1)} %pad_maximum_fusion.1.hiddens), channel_id=1, source_target_pairs={{0,2},{1,3},{2,0},{3,1},{4,6},{5,7},{6,4},{7,5},{8,10},{9,11},{10,... | collective-permute-start | bytes 786440 | tf_op jit(solution)/shard_map/ppermute | solution.py:509
  120.7 38.1 %collective-permute-start.14 = (bf16[8,128,128]{2,1,0:T(8,128)(2,1)S(1)}, bf16[8,128,128]{2,1,0:T(8,128)(2,1)S(1)}, u32[]{:S(2)}, u32[]{:S(2)}) collective-permute-start(bf16[8,128,128]{2,1,0:T(8,128)(2,1)S(1)} %constant_dynamic-update-slice_fusion.backs), channel_id=1, source_target_pairs={{0,2},{1,3},{2,0},{3,1},{4,6},{5,7},{6,4},{7,5},{8,10},{9,11},{10,... | collective-permute-start | bytes 786440 | tf_op jit(solution)/shard_map/ppermute | solution.py:509

commit v14 on v13

--- a/solution.py
+++ b/solution.py
@@ -25,12 +25,19 @@
     return place % line_bit // pair_bit
 
 
-def side_index(place):
-    return place // line_bit * pair_bit + place % pair_bit
-
-
-def side_place(index, side):
-    return index // pair_bit * line_bit + side * pair_bit + index % pair_bit
+def reversed_bits(number, count):
+    bits = count.bit_length() - 1
+    return sum(((number >> bit) & 1) << (bits - 1 - bit) for bit in range(bits))
+
+
+def side_index(place, members):
+    lines = members // 2
+    return place % pair_bit * lines + reversed_bits(place // line_bit, lines)
+
+
+def side_place(index, side, members):
+    core, line = divmod(index, members // 2)
+    return reversed_bits(line, members // 2) * line_bit + side * pair_bit + core
 
 
 def params():
@@ -144,7 +151,7 @@
     copies = []
     for index in range(members):
         for half in range(2):
-            column = side_place(index, side_of(place[0]) ^ half) * width
+            column = side_place(index, side_of(place[0]) ^ half, members) * width
             copies.append(
                 pltpu.make_async_copy(
                     tokens.at[:, pl.ds(pl.multiple_of(column, width), width)],
@@ -203,7 +210,7 @@
             frozen = jnp.dot(lines, right, preferred_element_type=jnp.float32)
             for slot in slots:
                 down = downs[slot][0] if half == 0 else pair[slot * extent : (slot + 1) * extent]
-                index = side_index(place[0] ^ line_offset(slot, members))
+                index = side_index(place[0] ^ line_offset(slot, members), members)
                 low = jnp.dot(backs[slot], down, preferred_element_type=jnp.float32)
                 at = (slot - first) * rows
                 out[index, half] = (frozen[at : at + rows] + low).astype(jnp.bfloat16)
@@ -233,15 +240,15 @@
 
 
 def hidden_kernel(adapters, place, pair, tokens, *refs):
-    parts, own, other = refs[-3:]
+    parts, own, *others = refs[-4:]
     members = own.shape[0]
     downs = refs[:members]
     extent = downs[0].shape[1]
     across = (((1,), (1,)), ((), ()))
     for slot in range(members):
-        index = side_index(place[0] ^ line_offset(slot, members))
+        index = side_index(place[0] ^ line_offset(slot, members), members)
         own[slot] = tokens[index, 0]
-        other[slot] = tokens[index, 1]
+        others[slot // (members // 2)][slot % (members // 2)] = tokens[index, 1]
         parts[slot] = lax.dot_general(
             tokens[index, 0], downs[slot][0], across, preferred_element_type=jnp.float32
         ) + lax.dot_general(
@@ -255,7 +262,7 @@
 def hidden_parts(adapters, place, down_maps, pair, tokens):
     members, _, rows, width = tokens.shape
     extent = down_maps.shape[1]
-    tokens_shape = jax.ShapeDtypeStruct((members, rows, width), tokens.dtype)
+    others = jax.ShapeDtypeStruct((members // 2, rows, width), tokens.dtype)
     return call(
         hidden_kernel,
         "hidden_parts",
@@ -265,8 +272,9 @@
         + [picked(down_maps, line_offset(slot, members)) for slot in range(members)],
         [
             jax.ShapeDtypeStruct((members, rows, extent), jnp.float32),
-            tokens_shape,
-            tokens_shape,
+            jax.ShapeDtypeStruct((members, rows, width), tokens.dtype),
+            others,
+            others,
         ],
     )
 
@@ -314,7 +322,7 @@
     copies = []
     for index in range(members):
         for half in range(2):
-            column = side_place(index, side_of(place[0]) ^ half) * width
+            column = side_place(index, side_of(place[0]) ^ half, members) * width
             copies.append(
                 pltpu.make_async_copy(
                     source.at[index, half],
@@ -418,25 +426,40 @@
 
 
 def down_gradient_kernel(
-    adapters, place, backs, backs_pair, own, other, out, head, following, products, ready, zero, sems
+    adapters,
+    place,
+    backs,
+    backs_pair,
+    own,
+    other_first,
+    other_second,
+    out,
+    head,
+    following,
+    products,
+    ready,
+    zero,
+    sems,
 ):
     members = own.shape[0]
+    others = (other_first, other_second)
     list_members(adapters, place, members, head, following)
     for slot in range(members):
         products[slot] = by_rows(backs[slot], own[slot])
-        products[members + slot] = by_rows(backs_pair[slot], other[slot])
+        core, line = divmod(slot, members // 2)
+        products[members + slot] = by_rows(backs_pair[slot], others[core][line])
     write_sums(
         head, following, products, ready, zero, out, sems, lambda adapter, total: total
     )
 
 
-def down_gradients(adapters, place, backs, backs_pair, own, other, num_adapters):
+def down_gradients(adapters, place, backs, backs_pair, own, others, num_adapters):
     members, _, width = own.shape
     return sums_call(
         down_gradient_kernel,
         "down_gradients",
         (adapters, place),
-        (backs, backs_pair, own, other),
+        (backs, backs_pair, own, *others),
         num_adapters,
         2 * members,
         (backs.shape[2], width),
@@ -498,7 +521,7 @@
 
 def exchange_side(pieces):
     members = pieces.shape[0]
-    groups = [[side_place(index, side) for index in range(members)] for side in range(2)]
+    groups = [[side_place(index, side, members) for index in range(members)] for side in range(2)]
     return lax.all_to_all(
         pieces, "dp", split_axis=0, concat_axis=0, axis_index_groups=groups, tiled=True
     )
@@ -537,47 +560,36 @@
     own_up = exchange(gather_up(adapters, up_maps)).reshape(depth, extent)
     packs = pack_tokens(place, tokens, members, width)
     pair = for_pair(adapters, place, value_weight, down_maps, members)
-    firsts = [gradients[1 << step] for step in range(steps - 1)]
-    firsts, own_up, packs, pair = barrier((firsts, own_up, packs, pair))
-    for step in range(steps - 1):
-        gradients[1 << step] = firsts[step]
+    for step in range(1, steps - 1):
+        for slot in range(1, 1 << step):
+            gradients[slot + (1 << step)] = swap(gradients[slot], offsets[1 << step])
+    gradients, own_up, packs, pair = barrier((gradients, own_up, packs, pair))
 
     arrived = exchange_side(packs)
     pair = swap(pair, pair_bit)
+    gradients.append(swap(jnp.concatenate(gradients, axis=0), 1))
     backs = back_rows(adapters, place, ranks, output_gradient, own_up)
     backs = gather_step(backs, members)
-    for slot in range(1, 2):
-        for step in range(1, min(2, steps - 1)):
-            gradients[slot + (1 << step)] = swap(gradients[slot], offsets[1 << step])
-    held = [gradients[slot] for slot in range(lines) if gradients[slot] is not None]
-    arrived, backs, held, pair = barrier((arrived, backs, held, pair))
-    known = [slot for slot in range(lines) if gradients[slot] is not None]
-    for slot, block in zip(known, held):
-        gradients[slot] = block
-
-    parts, tokens_own, tokens_pair = hidden_parts(adapters, place, down_maps, pair, arrived)
+    arrived, backs, gradients, pair = barrier((arrived, backs, gradients, pair))
+
+    parts, tokens_own, *tokens_pair = hidden_parts(
+        adapters, place, down_maps, pair, arrived
+    )
+    tokens_other = [swap(tokens_pair[0], pair_bit)]
     while backs.shape[0] < members:
         backs = gather_step(backs, members)
-    for step in range(1, steps - 1):
-        for slot in range(1, 1 << step):
-            if gradients[slot + (1 << step)] is None:
-                gradients[slot + (1 << step)] = swap(gradients[slot], offsets[1 << step])
-    gradients.append(swap(jnp.concatenate(gradients, axis=0), 1))
     slices, columns, columns_pair = input_slices(
         adapters, place, gradients, backs, value_weight, pair, down_maps
     )
-    received, flip = swap(parts[lines:], 1), 0
-    total = parts
+    total, flip = parts, 0
+    received = swap(parts[lines:], 1)
     for step in reversed(range(steps - 1)):
-        flipped = 1 << step
-        last = step == 0
-        sums = slot_sums(
-            total, received, flip, [jnp.float32] + [jnp.bfloat16] * last
-        )
-        total, flip = sums[0], flipped
-        received = swap(sums[-1], offsets[flipped])
-    received, slices, columns_pair, backs, tokens_pair = barrier(
-        (received, slices, columns_pair, backs, tokens_pair)
+        kinds = [jnp.float32] if step else [jnp.float32, jnp.bfloat16]
+        sums = slot_sums(total, received, flip, kinds)
+        total, flip = sums[0], 1 << step
+        received = swap(sums[-1], offsets[flip])
+    received, slices, columns_pair, backs, tokens_pair, tokens_other = barrier(
+        (received, slices, columns_pair, backs, tokens_pair, tokens_other)
     )
 
     result = exchange_side(slices)
@@ -586,7 +598,10 @@
     hiddens_pair = swap(hiddens, pair_bit)
     columns_other = swap(columns_pair, pair_bit)
     backs_pair = swap(backs, pair_bit)
-    tokens_other = swap(tokens_pair, pair_bit)
+    hiddens_pair, columns_other, backs_pair, tokens_pair = barrier(
+        (hiddens_pair, columns_other, backs_pair, tokens_pair)
+    )
+    tokens_other.append(swap(tokens_pair[1], pair_bit))
     up_gradient = up_gradients(
         adapters, place, ranks, columns, columns_other, hiddens, hiddens_pair, depth // devices
     )

time: 167 us -> 166 us (level)
  the two profiles are of different devices: /device:TPU:0 before, /device:TPU:10 now
where the time goes in v14:
time: 166 us
  waiting for transfers between devices  94.7 us (57%)
  starting transfers between devices  32.4 us (20%)
  Pallas kernels  26.2 us (16%)
  local copies, waits for them, and re-layouts  10.4 us (6%)
    ppermute x17, waiting for transfers between devices, swap(): return lax.ppermute(array, 'dp', [(i, i ^ flip) for i in range(devices)])  86.2 us
    ppermute x17, starting transfers between devices, swap(): return lax.ppermute(array, 'dp', [(i, i ^ flip) for i in range(devices)])  16.5 us
    all_to_all x2, starting transfers between devices, exchange_side(): lax.all_to_all(pieces, 'dp', split_axis=0, concat_axis=0, axis_index_grou...  11.6 us
    unnamed x50, local copies, waits for them, and re-layouts  10.4 us
    pallas_call x6, Pallas kernels, call(): pl.pallas_call(kernel, out_shape=out_shapes, grid_spec=pltpu.PrefetchScal...  10.1 us
    pallas_call x2, Pallas kernels, sums_call(): pl.pallas_call(kernel, out_shape=jax.ShapeDtypeStruct((num_adapters,) + p...  9.13 us
    all_to_all x2, waiting for transfers between devices, exchange_side(): lax.all_to_all(pieces, 'dp', split_axis=0, concat_axis=0, axis_index_grou...  8.51 us
    pallas_call x3, Pallas kernels, copy_call(): pl.pallas_call(kernel, out_shape=out_shapes, grid_spec=pltpu.PrefetchScal...  5.5 us
  transfers between devices with their start and end apart: 20, of which 11 were waited for; matrix products, arithmetic and copies ran while one was open for 1% of the time, Pallas kernels for 13%

profile of v14, /device:TPU:10, one launch (start us, length us, event | category | flops | bytes accessed | tf_op | source)
XLA Modules:
  0.0 166.0 jit_solution(4921342686185660249)
XLA Ops:
  0.6 2.7 %collective-permute-start = (bf16[1,128,1024]{2,1,0:T(8,128)(2,1)}, bf16[1,128,1024]{2,1,0:T(8,128)(2,1)S(1)}, u32[]{:S(2)}, u32[]{:S(2)}) collective-permute-start(bf16[1,128,1024]{2,1,0:T(8,128)(2,1)} %bitcast.3), channel_id=1, source_target_pairs={{0,8},{1,9},{2,10},{3,11},{4,12},{5,13},{6,14},{7,15},{8,0},{9,1},... | collective-permute-start | bytes 786440 | tf_op jit(solution)/shard_map/ppermute | solution.py:532
  3.3 1.2 copy-done.14
  4.5 0.7 copy-done.19
  5.2 1.8 %gather_up.1 = bf16[16,64,128]{2,1,0:T(8,128)(2,1)} custom-call(s32[16]{0:T(128)S(1)} %copy-done.19, bf16[64,64,128]{2,1,0:T(8,128)(2,1)S(1)} %copy-done.14), custom_call_target="tpu_custom_call" | custom-call | tf_op jit(solution)/shard_map/gather_up/pallas_call | solution.py:83
  6.9 4.3 %all-to-all-start = ((bf16[16,64,128]{2,1,0:T(8,128)(2,1)}), bf16[16,64,128]{2,1,0:T(8,128)(2,1)S(1)}, u32[]{:S(2)}, u32[]{:S(2)}) async-start(bf16[16,64,128]{2,1,0:T(8,128)(2,1)} %gather_up.1), calls=%async_computation | async-start | bytes 524288 | tf_op jit(solution)/shard_map/all_to_all | solution.py:519
  11.2 0.2 collective-permute-start.1
  11.4 6.2 %collective-permute-done.refs_1_ = bf16[1,128,1024]{2,1,0:T(8,128)(2,1)S(1)} collective-permute-done((bf16[1,128,1024]{2,1,0:T(8,128)(2,1)}, bf16[1,128,1024]{2,1,0:T(8,128)(2,1)S(1)}, u32[]{:S(2)}, u32[]{:S(2)}) %collective-permute-start) | collective-permute-done | bytes 262176 | tf_op jit(solution)/shard_map/ppermute | solution.py:532
  17.6 1.7 %copy-done.3 = bf16[128,8192]{1,0:T(8,128)(2,1)S(1)} copy-done((bf16[128,8192]{1,0:T(8,128)(2,1)S(1)}, bf16[128,8192]{1,0:T(8,128)(2,1)}, u32[]{:S(2)}) %copy-start.3) | copy-done | bytes 2097176
  19.3 1.8 %pack_tokens.1 = bf16[8,2,128,512]{3,2,1,0:T(8,128)(2,1)} custom-call(s32[1]{0:T(128)} %bitcast.place, bf16[128,8192]{1,0:T(8,128)(2,1)S(1)} %copy-done.3), custom_call_target="tpu_custom_call" | custom-call | tf_op jit(solution)/shard_map/pack_tokens/pallas_call | solution.py:83
  21.1 1.9 %for_pair.1 = bf16[2048,512]{1,0:T(8,128)(2,1)S(1)} custom-call(s32[16]{0:T(128)S(1)} %copy-done.20, s32[1]{0:T(128)} %bitcast.place, bf16[1024,512]{1,0:T(8,128)(2,1)S(1)} %copy-done.1, bf16[64,128,512]{2,1,0:T(8,128)(2,1)} %refs_7_.3), custom_call_target="tpu_custom_call" | custom-call | tf_op jit(solution)/shard_map/for_pair/pallas_call | solution.py:83
  23.1 1.3 copy-done.5
  24.4 4.5 %collective-permute-done.2.refs_3_ = bf16[1,128,1024]{2,1,0:T(8,128)(2,1)S(1)} collective-permute-done((bf16[1,128,1024]{2,1,0:T(8,128)(2,1)S(1)}, bf16[1,128,1024]{2,1,0:T(8,128)(2,1)S(1)}, u32[]{:S(2)}, u32[]{:S(2)}) %collective-permute-start.2) | collective-permute-done | bytes 262176 | tf_op jit(solution)/shard_map/ppermute | solution.py:532
  28.9 0.7 copy-done.12
  29.6 7.2 %all-to-all-start.1 = ((bf16[8,2,128,512]{3,2,1,0:T(8,128)(2,1)}), bf16[8,2,128,512]{3,2,1,0:T(8,128)(2,1)}, u32[]{:S(2)}, u32[]{:S(2)}) async-start(bf16[8,2,128,512]{3,2,1,0:T(8,128)(2,1)} %pack_tokens.1), calls=%async_computation.1 | async-start | bytes 4194304 | tf_op jit(solution)/shard_map/all_to_all | solution.py:525
  36.8 1.5 collective-permute-start.5
  38.4 1.2 pad_maximum_fusion
  39.6 0.1 collective-permute-start.4
  39.7 0.8 back_low.1
  40.5 2.4 %collective-permute-start.3 = (bf16[1,128,128]{2,1,0:T(8,128)(2,1)S(1)}, bf16[1,128,128]{2,1,0:T(8,128)(2,1)S(1)}, u32[]{:S(2)}, u32[]{:S(2)}) collective-permute-start(bf16[1,128,128]{2,1,0:T(8,128)(2,1)S(1)} %back_low.1), channel_id=1, source_target_pairs={{0,8},{1,9},{2,10},{3,11},{4,12},{5,13},{6,14},{7,15},{8,0},{9,1},... | collective-permute-start | bytes 98312 | tf_op jit(solution)/shard_map/ppermute | solution.py:532
  42.9 40.8 %collective-permute-done.3 = bf16[1,128,128]{2,1,0:T(8,128)(2,1)S(1)} collective-permute-done((bf16[1,128,128]{2,1,0:T(8,128)(2,1)S(1)}, bf16[1,128,128]{2,1,0:T(8,128)(2,1)S(1)}, u32[]{:S(2)}, u32[]{:S(2)}) %collective-permute-start.3) | collective-permute-done | bytes 32800 | tf_op jit(solution)/shard_map/ppermute | solution.py:532
  83.8 1.0 copy-done.6
  84.7 0.9 all-to-all-done.1.tokens
  85.6 3.3 %hidden_parts.1 = (f32[8,128,128]{2,1,0:T(8,128)S(1)}, bf16[8,128,512]{2,1,0:T(8,128)(2,1)S(1)}, bf16[4,128,512]{2,1,0:T(8,128)(2,1)S(1)}, bf16[4,128,512]{2,1,0:T(8,128)(2,1)S(1)}) custom-call(s32[16]{0:T(128)S(1)} %copy-done.20, s32[1]{0:T(128)} %bitcast.place, bf16[2048,512]{1,0:T(8,128)(2,1)S(1)} %collective-permute-done.5.pair, ...), custom_call_target="tpu_custom_call" | custom-call | tf_op jit(solution)/shard_map/hidden_parts/pallas_call | solution.py:60
  88.9 1.0 copy-done.17
  89.8 0.8 copy-done.22
  90.8 1.6 collective-permute-start.11
  92.3 2.9 %collective-permute-start.6 = (bf16[2,128,128]{2,1,0:T(8,128)(2,1)S(1)}, bf16[2,128,128]{2,1,0:T(8,128)(2,1)S(1)}, u32[]{:S(2)}, u32[]{:S(2)}) collective-permute-start(bf16[2,128,128]{2,1,0:T(8,128)(2,1)S(1)} %pad_maximum_fusion.3), channel_id=1, source_target_pairs={{0,4},{1,5},{2,6},{3,7},{4,0},{5,1},{6,2},{7,3},{8,12},{9,13},{10,... | collective-permute-start | bytes 196616 | tf_op jit(solution)/shard_map/ppermute | solution.py:532
  95.3 2.3 %collective-permute-done.6 = bf16[2,128,128]{2,1,0:T(8,128)(2,1)S(1)} collective-permute-done((bf16[2,128,128]{2,1,0:T(8,128)(2,1)S(1)}, bf16[2,128,128]{2,1,0:T(8,128)(2,1)S(1)}, u32[]{:S(2)}, u32[]{:S(2)}) %collective-permute-start.6) | collective-permute-done | bytes 65568 | tf_op jit(solution)/shard_map/ppermute | solution.py:532
  97.8 5.6 %collective-permute-done.9.received = f32[4,128,128]{2,1,0:T(8,128)S(1)} collective-permute-done((f32[4,128,128]{2,1,0:T(8,128)S(1)}, f32[4,128,128]{2,1,0:T(8,128)S(1)}, u32[]{:S(2)}, u32[]{:S(2)}) %collective-permute-start.9) | collective-permute-done | bytes 262176 | tf_op jit(solution)/shard_map/ppermute | solution.py:532
  103.5 1.4 collective-permute-start.10
  105.0 5.5 %input_slices.1 = (bf16[8,2,128,512]{3,2,1,0:T(8,128)(2,1)S(1)}, bf16[8,128,128]{2,1,0:T(8,128)(2,1)S(1)}, bf16[8,128,128]{2,1,0:T(8,128)(2,1)S(1)}) custom-call(s32[16]{0:T(128)S(1)} %copy-done.20, s32[1]{0:T(128)} %bitcast.place, bf16[8,128,128]{2,1,0:T(8,128)(2,1)S(1)} %constant_dynamic-update-slice_fusion.backs, bf16[2048,512]{1,0:T(8,128)(2,1)} %copy-done, ...), custom_call_target="tpu_custom_call" | custom-call | tf_op jit(solution)/shard_map/input_slices/pallas_call | solution.py:60
  110.5 1.3 copy-done.4
  111.8 0.7 copy-done.23
  112.5 4.4 %all-to-all-start.2 = ((bf16[8,2,128,512]{3,2,1,0:T(8,128)(2,1)}), bf16[8,2,128,512]{3,2,1,0:T(8,128)(2,1)S(1)}, u32[]{:S(2)}, u32[]{:S(2)}) async-start(bf16[8,2,128,512]{3,2,1,0:T(8,128)(2,1)} %copy-done.4), calls=%async_computation.2 | async-start | bytes 4194304 | tf_op jit(solution)/shard_map/all_to_all | solution.py:525
  116.9 0.6 hidden_low.1
  117.5 0.2 collective-permute-start.12
  117.7 0.6 collective-permute-start.14
  118.3 1.4 collective-permute-start.15
  119.8 0.7 collective-permute-start.13
  120.5 6.6 %collective-permute-done.14.gradients_pair = bf16[8,128,128]{2,1,0:T(8,128)(2,1)S(1)} collective-permute-done((bf16[8,128,128]{2,1,0:T(8,128)(2,1)}, bf16[8,128,128]{2,1,0:T(8,128)(2,1)S(1)}, u32[]{:S(2)}, u32[]{:S(2)}) %collective-permute-start.14) | collective-permute-done | bytes 262176 | tf_op jit(solution)/shard_map/ppermute | solution.py:532
  127.1 5.6 %collective-permute-done.15.backs_pair = bf16[8,128,128]{2,1,0:T(8,128)(2,1)S(1)} collective-permute-done((bf16[8,128,128]{2,1,0:T(8,128)(2,1)S(1)}, bf16[8,128,128]{2,1,0:T(8,128)(2,1)S(1)}, u32[]{:S(2)}, u32[]{:S(2)}) %collective-permute-start.15) | collective-permute-done | bytes 262176 | tf_op jit(solution)/shard_map/ppermute | solution.py:532
  132.7 5.1 %collective-permute-done.13.hiddens_pair = bf16[8,128,128]{2,1,0:T(8,128)(2,1)S(1)} collective-permute-done((bf16[8,128,128]{2,1,0:T(8,128)(2,1)S(1)}, bf16[8,128,128]{2,1,0:T(8,128)(2,1)S(1)}, u32[]{:S(2)}, u32[]{:S(2)}) %collective-permute-start.13) | collective-permute-done | bytes 262176 | tf_op jit(solution)/shard_map/ppermute | solution.py:532
  137.7 0.6 collective-permute-start.16
  138.3 3.6 %up_gradients.1 = bf16[64,64,128]{2,1,0:T(8,128)(2,1)} custom-call(s32[16]{0:T(128)S(1)} %copy-done.20, s32[1]{0:T(128)} %bitcast.place, s32[64]{0:T(128)S(1)} %copy-done.21, bf16[8,128,128]{2,1,0:T(8,128)(2,1)S(1)} %get-tuple-element.54.gradients, bf16[8,128,128]{2,1,0:T(8,128)(2,1)S(1)} %collective-permute-done.14.gradients_pair, ...), custom_call_target="tpu_custom_call" | custom-call | tf_op jit(solution)/shard_map/up_gradients/pallas_call | solution.py:405
  141.9 9.4 %collective-permute-done.16.other_second = bf16[4,128,512]{2,1,0:T(8,128)(2,1)S(1)} collective-permute-done((bf16[4,128,512]{2,1,0:T(8,128)(2,1)}, bf16[4,128,512]{2,1,0:T(8,128)(2,1)S(1)}, u32[]{:S(2)}, u32[]{:S(2)}) %collective-permute-start.16) | collective-permute-done | bytes 524320 | tf_op jit(solution)/shard_map/ppermute | solution.py:532
  151.3 5.5 %down_gradients.1 = bf16[64,128,512]{2,1,0:T(8,128)(2,1)} custom-call(s32[16]{0:T(128)S(1)} %copy-done.20, s32[1]{0:T(128)} %bitcast.place, bf16[8,128,128]{2,1,0:T(8,128)(2,1)S(1)} %constant_dynamic-update-slice_fusion.backs, bf16[8,128,128]{2,1,0:T(8,128)(2,1)S(1)} %collective-permute-done.15.backs_pair, bf16[8,128,512]{2,1,0:T(8,128)(2,1)S(1)} %copy-done.18, ...), custom_call_target="tpu_custom_call" | custom-call | tf_op jit(solution)/shard_map/down_gradients/pallas_call | solution.py:405
  156.9 7.6 %all-to-all-done.2.source = bf16[8,2,128,512]{3,2,1,0:T(8,128)(2,1)S(1)} async-done(((bf16[8,2,128,512]{3,2,1,0:T(8,128)(2,1)}), bf16[8,2,128,512]{3,2,1,0:T(8,128)(2,1)S(1)}, u32[]{:S(2)}, u32[]{:S(2)}) %all-to-all-start.2) | async-done | bytes 2097184 | tf_op jit(solution)/shard_map/all_to_all | solution.py:525
  164.5 1.4 join_columns.1
  (60 shorter events, 0.5 us)
Async XLA Ops:
  0.6 16.9 %collective-permute-start = (bf16[1,128,1024]{2,1,0:T(8,128)(2,1)}, bf16[1,128,1024]{2,1,0:T(8,128)(2,1)S(1)}, u32[]{:S(2)}, u32[]{:S(2)}) collective-permute-start(bf16[1,128,1024]{2,1,0:T(8,128)(2,1)} %bitcast.3), channel_id=1, source_target_pairs={{0,8},{1,9},{2,10},{3,11},{4,12},{5,13},{6,14},{7,15},{8,0},{9,1},... | collective-permute-start | bytes 786440 | tf_op jit(solution)/shard_map/ppermute | solution.py:532
  3.3 1.2 copy-start.14
  4.5 0.7 copy-start.19
  6.9 17.5 %all-to-all-start = ((bf16[16,64,128]{2,1,0:T(8,128)(2,1)}), bf16[16,64,128]{2,1,0:T(8,128)(2,1)S(1)}, u32[]{:S(2)}, u32[]{:S(2)}) async-start(bf16[16,64,128]{2,1,0:T(8,128)(2,1)} %gather_up.1), calls=%async_computation | async-start | bytes 524288 | tf_op jit(solution)/shard_map/all_to_all | solution.py:519
  11.2 13.2 %collective-permute-start.1 = (bf16[1,128,1024]{2,1,0:T(8,128)(2,1)}, bf16[1,128,1024]{2,1,0:T(8,128)(2,1)S(1)}, u32[]{:S(2)}, u32[]{:S(2)}) collective-permute-start(bf16[1,128,1024]{2,1,0:T(8,128)(2,1)} %bitcast.4), channel_id=1, source_target_pairs={{0,4},{1,5},{2,6},{3,7},{4,0},{5,1},{6,2},{7,3},{8,12},{9,13},{10,... | collective-permute-start | bytes 786440 | tf_op jit(solution)/shard_map/ppermute | solution.py:532
  17.6 5.5 %copy-start.8 = (bf16[1,128,1024]{2,1,0:T(8,128)(2,1)}, bf16[1,128,1024]{2,1,0:T(8,128)(2,1)S(1)}, u32[]{:S(2)}) copy-start(bf16[1,128,1024]{2,1,0:T(8,128)(2,1)S(1)} %collective-permute-done.refs_1_) | copy-start | bytes 786436
  17.6 11.3 %collective-permute-start.2 = (bf16[1,128,1024]{2,1,0:T(8,128)(2,1)S(1)}, bf16[1,128,1024]{2,1,0:T(8,128)(2,1)S(1)}, u32[]{:S(2)}, u32[]{:S(2)}) collective-permute-start(bf16[1,128,1024]{2,1,0:T(8,128)(2,1)S(1)} %collective-permute-done.refs_1_), channel_id=1, source_target_pairs={{0,4},{1,5},{2,6},{3,7},{4,0},{5,1},{6,2},{7,3},{8,12},{9,13},{10,... | collective-permute-start | bytes 786440 | tf_op jit(solution)/shard_map/ppermute | solution.py:532
  17.6 1.7 %copy-start.3 = (bf16[128,8192]{1,0:T(8,128)(2,1)S(1)}, bf16[128,8192]{1,0:T(8,128)(2,1)}, u32[]{:S(2)}) copy-start(bf16[128,8192]{1,0:T(8,128)(2,1)} %tokens.1) | copy-start | bytes 6291460
  19.3 1.8 %copy-start.1 = (bf16[1024,512]{1,0:T(8,128)(2,1)S(1)}, bf16[1024,512]{1,0:T(8,128)(2,1)}, u32[]{:S(2)}) copy-start(bf16[1024,512]{1,0:T(8,128)(2,1)} %refs_13_.1) | copy-start | bytes 3145732
  19.3 1.8 %copy-start.20 = (s32[16]{0:T(128)S(1)}, s32[16]{0:T(128)}, u32[]{:S(2)}) copy-start(s32[16]{0:T(128)} %adapters.15) | copy-start | bytes 196
  23.1 1.3 copy-start.5
  24.4 4.5 %copy-start.10 = (bf16[1,128,1024]{2,1,0:T(8,128)(2,1)}, bf16[1,128,1024]{2,1,0:T(8,128)(2,1)S(1)}, u32[]{:S(2)}) copy-start(bf16[1,128,1024]{2,1,0:T(8,128)(2,1)S(1)} %collective-permute-done.1.refs_2_) | copy-start | bytes 786436
  24.4 4.5 %copy-start.15 = (bf16[16,64,128]{2,1,0:T(8,128)(2,1)}, bf16[16,64,128]{2,1,0:T(8,128)(2,1)S(1)}, u32[]{:S(2)}) copy-start(bf16[16,64,128]{2,1,0:T(8,128)(2,1)S(1)} %all-to-all-done) | copy-start | bytes 786436
  28.9 0.7 copy-start.12
  28.9 9.5 %copy-start.2 = (bf16[128,1024]{1,0:T(8,128)(2,1)S(1)}, bf16[128,1024]{1,0:T(8,128)(2,1)}, u32[]{:S(2)}) copy-start(bf16[128,1024]{1,0:T(8,128)(2,1)} %gradient.1) | copy-start | bytes 786436
  29.6 56.0 %all-to-all-start.1 = ((bf16[8,2,128,512]{3,2,1,0:T(8,128)(2,1)}), bf16[8,2,128,512]{3,2,1,0:T(8,128)(2,1)}, u32[]{:S(2)}, u32[]{:S(2)}) async-start(bf16[8,2,128,512]{3,2,1,0:T(8,128)(2,1)} %pack_tokens.1), calls=%async_computation.1 | async-start | bytes 4194304 | tf_op jit(solution)/shard_map/all_to_all | solution.py:525
  36.8 2.9 %copy-start.16 = (bf16[16,64,128]{2,1,0:T(8,128)(2,1)S(1)}, bf16[16,64,128]{2,1,0:T(8,128)(2,1)}, u32[]{:S(2)}) copy-start(bf16[16,64,128]{2,1,0:T(8,128)(2,1)} %copy-done.15) | copy-start | bytes 786436
  36.8 2.9 %copy-start.21 = (s32[64]{0:T(128)S(1)}, s32[64]{0:T(128)}, u32[]{:S(2)}) copy-start(s32[64]{0:T(128)} %ranks.5) | copy-start | bytes 772
  36.8 47.9 %collective-permute-start.5 = (bf16[2048,512]{1,0:T(8,128)(2,1)}, bf16[2048,512]{1,0:T(8,128)(2,1)S(1)}, u32[]{:S(2)}, u32[]{:S(2)}) collective-permute-start(bf16[2048,512]{1,0:T(8,128)(2,1)} %copy-done.5), channel_id=1, source_target_pairs={{0,2},{1,3},{2,0},{3,1},{4,6},{5,7},{6,4},{7,5},{8,10},{9,11},{10,... | collective-permute-start | bytes 6291464 | tf_op jit(solution)/shard_map/ppermute | solution.py:532
  39.6 44.2 %collective-permute-start.4 = (bf16[4,128,1024]{2,1,0:T(8,128)(2,1)S(1)}, bf16[4,128,1024]{2,1,0:T(8,128)(2,1)S(1)}, u32[]{:S(2)}, u32[]{:S(2)}) collective-permute-start(bf16[4,128,1024]{2,1,0:T(8,128)(2,1)S(1)} %pad_maximum_fusion), channel_id=1, source_target_pairs={{0,1},{1,0},{2,3},{3,2},{4,5},{5,4},{6,7},{7,6},{8,9},{9,8},{10,11... | collective-permute-start | bytes 3145736 | tf_op jit(solution)/shard_map/ppermute | solution.py:532
  40.5 43.3 %collective-permute-start.3 = (bf16[1,128,128]{2,1,0:T(8,128)(2,1)S(1)}, bf16[1,128,128]{2,1,0:T(8,128)(2,1)S(1)}, u32[]{:S(2)}, u32[]{:S(2)}) collective-permute-start(bf16[1,128,128]{2,1,0:T(8,128)(2,1)S(1)} %back_low.1), channel_id=1, source_target_pairs={{0,8},{1,9},{2,10},{3,11},{4,12},{5,13},{6,14},{7,15},{8,0},{9,1},... | collective-permute-start | bytes 98312 | tf_op jit(solution)/shard_map/ppermute | solution.py:532
  83.8 1.0 copy-start.6
  84.7 4.1 %copy-start = (bf16[2048,512]{1,0:T(8,128)(2,1)}, bf16[2048,512]{1,0:T(8,128)(2,1)S(1)}, u32[]{:S(2)}) copy-start(bf16[2048,512]{1,0:T(8,128)(2,1)S(1)} %collective-permute-done.5.pair) | copy-start | bytes 6291460
  88.9 1.0 copy-start.17
  89.8 0.8 copy-start.22
  90.6 14.3 %copy-start.7 = (bf16[4,128,1024]{2,1,0:T(8,128)(2,1)S(1)}, bf16[4,128,1024]{2,1,0:T(8,128)(2,1)}, u32[]{:S(2)}) copy-start(bf16[4,128,1024]{2,1,0:T(8,128)(2,1)} %copy-done.6) | copy-start | bytes 3145732
  90.6 14.3 %copy-start.9 = (bf16[1,128,1024]{2,1,0:T(8,128)(2,1)S(1)}, bf16[1,128,1024]{2,1,0:T(8,128)(2,1)}, u32[]{:S(2)}) copy-start(bf16[1,128,1024]{2,1,0:T(8,128)(2,1)} %copy-done.8) | copy-start | bytes 786436
  90.7 14.3 %copy-start.11 = (bf16[1,128,1024]{2,1,0:T(8,128)(2,1)S(1)}, bf16[1,128,1024]{2,1,0:T(8,128)(2,1)}, u32[]{:S(2)}) copy-start(bf16[1,128,1024]{2,1,0:T(8,128)(2,1)} %copy-done.10) | copy-start | bytes 786436
  90.7 14.3 %copy-start.13 = (bf16[1,128,1024]{2,1,0:T(8,128)(2,1)S(1)}, bf16[1,128,1024]{2,1,0:T(8,128)(2,1)}, u32[]{:S(2)}) copy-start(bf16[1,128,1024]{2,1,0:T(8,128)(2,1)} %copy-done.12) | copy-start | bytes 786436
  90.7 4.5 %collective-permute-start.8 = (f32[4,128,128]{2,1,0:T(8,128)S(1)}, f32[4,128,128]{2,1,0:T(8,128)S(1)}, u32[]{:S(2)}, u32[]{:S(2)}) collective-permute-start(f32[4,128,128]{2,1,0:T(8,128)S(1)} %slice.3), channel_id=1, source_target_pairs={{0,1},{1,0},{2,3},{3,2},{4,5},{5,4},{6,7},{7,6},{8,9},{9,8},{10,11... | collective-permute-start | bytes 786440 | tf_op jit(solution)/shard_map/ppermute | solution.py:532
  90.8 21.7 %collective-permute-start.11 = (bf16[4,128,512]{2,1,0:T(8,128)(2,1)S(1)}, bf16[4,128,512]{2,1,0:T(8,128)(2,1)S(1)}, u32[]{:S(2)}, u32[]{:S(2)}) collective-permute-start(bf16[4,128,512]{2,1,0:T(8,128)(2,1)S(1)} %get-tuple-element.61), channel_id=1, source_target_pairs={{0,2},{1,3},{2,0},{3,1},{4,6},{5,7},{6,4},{7,5},{8,10},{9,11},{10,... | collective-permute-start | bytes 1572872 | tf_op jit(solution)/shard_map/ppermute | solution.py:532
  92.3 5.3 %collective-permute-start.6 = (bf16[2,128,128]{2,1,0:T(8,128)(2,1)S(1)}, bf16[2,128,128]{2,1,0:T(8,128)(2,1)S(1)}, u32[]{:S(2)}, u32[]{:S(2)}) collective-permute-start(bf16[2,128,128]{2,1,0:T(8,128)(2,1)S(1)} %pad_maximum_fusion.3), channel_id=1, source_target_pairs={{0,4},{1,5},{2,6},{3,7},{4,0},{5,1},{6,2},{7,3},{8,12},{9,13},{10,... | collective-permute-start | bytes 196616 | tf_op jit(solution)/shard_map/ppermute | solution.py:532
  95.3 8.2 %collective-permute-start.9 = (f32[4,128,128]{2,1,0:T(8,128)S(1)}, f32[4,128,128]{2,1,0:T(8,128)S(1)}, u32[]{:S(2)}, u32[]{:S(2)}) collective-permute-start(f32[4,128,128]{2,1,0:T(8,128)S(1)} %slot_sums.2.total), channel_id=1, source_target_pairs={{0,4},{1,5},{2,6},{3,7},{4,0},{5,1},{6,2},{7,3},{8,12},{9,13},{10,... | collective-permute-start | bytes 786440 | tf_op jit(solution)/shard_map/ppermute | solution.py:532
  97.7 7.2 %collective-permute-start.7 = (bf16[4,128,128]{2,1,0:T(8,128)(2,1)S(1)}, bf16[4,128,128]{2,1,0:T(8,128)(2,1)S(1)}, u32[]{:S(2)}, u32[]{:S(2)}) collective-permute-start(bf16[4,128,128]{2,1,0:T(8,128)(2,1)S(1)} %pad_maximum_fusion.2), channel_id=1, source_target_pairs={{0,1},{1,0},{2,3},{3,2},{4,5},{5,4},{6,7},{7,6},{8,9},{9,8},{10,11... | collective-permute-start | bytes 393224 | tf_op jit(solution)/shard_map/ppermute | solution.py:532
  103.5 9.0 %collective-permute-start.10 = (bf16[4,128,128]{2,1,0:T(8,128)(2,1)S(1)}, bf16[4,128,128]{2,1,0:T(8,128)(2,1)S(1)}, u32[]{:S(2)}, u32[]{:S(2)}) collective-permute-start(bf16[4,128,128]{2,1,0:T(8,128)(2,1)S(1)} %get-tuple-element.58), channel_id=1, source_target_pairs={{0,8},{1,9},{2,10},{3,11},{4,12},{5,13},{6,14},{7,15},{8,0},{9,1},... | collective-permute-start | bytes 393224 | tf_op jit(solution)/shard_map/ppermute | solution.py:532
  110.5 1.3 copy-start.4
  111.8 0.7 copy-start.23
  112.5 52.0 %all-to-all-start.2 = ((bf16[8,2,128,512]{3,2,1,0:T(8,128)(2,1)}), bf16[8,2,128,512]{3,2,1,0:T(8,128)(2,1)S(1)}, u32[]{:S(2)}, u32[]{:S(2)}) async-start(bf16[8,2,128,512]{3,2,1,0:T(8,128)(2,1)} %copy-done.4), calls=%async_computation.2 | async-start | bytes 4194304 | tf_op jit(solution)/shard_map/all_to_all | solution.py:525
  116.9 34.4 %copy-start.18 = (bf16[8,128,512]{2,1,0:T(8,128)(2,1)S(1)}, bf16[8,128,512]{2,1,0:T(8,128)(2,1)}, u32[]{:S(2)}) copy-start(bf16[8,128,512]{2,1,0:T(8,128)(2,1)} %copy-done.17) | copy-start | bytes 3145732
  117.5 2.3 %collective-permute-start.12 = (bf16[4,128,128]{2,1,0:T(8,128)(2,1)S(1)}, bf16[4,128,128]{2,1,0:T(8,128)(2,1)S(1)}, u32[]{:S(2)}, u32[]{:S(2)}) collective-permute-start(bf16[4,128,128]{2,1,0:T(8,128)(2,1)S(1)} %hidden_low.1), channel_id=1, source_target_pairs={{0,1},{1,0},{2,3},{3,2},{4,5},{5,4},{6,7},{7,6},{8,9},{9,8},{10,11... | collective-permute-start | bytes 393224 | tf_op jit(solution)/shard_map/ppermute | solution.py:532
  117.7 9.3 %collective-permute-start.14 = (bf16[8,128,128]{2,1,0:T(8,128)(2,1)}, bf16[8,128,128]{2,1,0:T(8,128)(2,1)S(1)}, u32[]{:S(2)}, u32[]{:S(2)}) collective-permute-start(bf16[8,128,128]{2,1,0:T(8,128)(2,1)} %copy-done.23), channel_id=1, source_target_pairs={{0,2},{1,3},{2,0},{3,1},{4,6},{5,7},{6,4},{7,5},{8,10},{9,11},{10,... | collective-permute-start | bytes 786440 | tf_op jit(solution)/shard_map/ppermute | solution.py:532
  118.3 14.3 %collective-permute-start.15 = (bf16[8,128,128]{2,1,0:T(8,128)(2,1)S(1)}, bf16[8,128,128]{2,1,0:T(8,128)(2,1)S(1)}, u32[]{:S(2)}, u32[]{:S(2)}) collective-permute-start(bf16[8,128,128]{2,1,0:T(8,128)(2,1)S(1)} %constant_dynamic-update-slice_fusion.backs), channel_id=1, source_target_pairs={{0,2},{1,3},{2,0},{3,1},{4,6},{5,7},{6,4},{7,5},{8,10},{9,11},{10,... | collective-permute-start | bytes 786440 | tf_op jit(solution)/shard_map/ppermute | solution.py:532
  119.8 17.9 %collective-permute-start.13 = (bf16[8,128,128]{2,1,0:T(8,128)(2,1)S(1)}, bf16[8,128,128]{2,1,0:T(8,128)(2,1)S(1)}, u32[]{:S(2)}, u32[]{:S(2)}) collective-permute-start(bf16[8,128,128]{2,1,0:T(8,128)(2,1)S(1)} %pad_maximum_fusion.1.hiddens), channel_id=1, source_target_pairs={{0,2},{1,3},{2,0},{3,1},{4,6},{5,7},{6,4},{7,5},{8,10},{9,11},{10,... | collective-permute-start | bytes 786440 | tf_op jit(solution)/shard_map/ppermute | solution.py:532
  137.7 13.6 %collective-permute-start.16 = (bf16[4,128,512]{2,1,0:T(8,128)(2,1)}, bf16[4,128,512]{2,1,0:T(8,128)(2,1)S(1)}, u32[]{:S(2)}, u32[]{:S(2)}) collective-permute-start(bf16[4,128,512]{2,1,0:T(8,128)(2,1)} %copy-done.22), channel_id=1, source_target_pairs={{0,2},{1,3},{2,0},{3,1},{4,6},{5,7},{6,4},{7,5},{8,10},{9,11},{10,... | collective-permute-start | bytes 1572872 | tf_op jit(solution)/shard_map/ppermute | solution.py:532

commit v15 on v14

--- a/solution.py
+++ b/solution.py
@@ -194,9 +194,10 @@
     members, rows, _ = backs.shape
     apart = members // 2
     gradients = [ref.at[0] for ref in refs[:apart]]
-    gradients += [refs[apart].at[slot] for slot in range(members - apart)]
-    downs = refs[apart + 1 : apart + 1 + members]
-    weight = refs[apart + 1 + members]
+    for ref in refs[apart : apart + 2]:
+        gradients += [ref.at[slot] for slot in range(ref.shape[0])]
+    downs = refs[apart + 2 : apart + 2 + members]
+    weight = refs[apart + 2 + members]
     out, *columns = refs[-3:]
     extent = downs[0].shape[1]
     lanes = columns[0].shape[2]
@@ -560,48 +561,49 @@
     own_up = exchange(gather_up(adapters, up_maps)).reshape(depth, extent)
     packs = pack_tokens(place, tokens, members, width)
     pair = for_pair(adapters, place, value_weight, down_maps, members)
+    across = [swap(jnp.concatenate(gradients[:2], axis=0), 1)]
+    firsts = [gradients[1 << step] for step in range(steps - 1)]
+    firsts, across, own_up, packs, pair = barrier((firsts, across, own_up, packs, pair))
+    for step in range(steps - 1):
+        gradients[1 << step] = firsts[step]
+
+    arrived = exchange_side(packs)
+    pair = swap(pair, pair_bit)
     for step in range(1, steps - 1):
         for slot in range(1, 1 << step):
             gradients[slot + (1 << step)] = swap(gradients[slot], offsets[1 << step])
-    gradients, own_up, packs, pair = barrier((gradients, own_up, packs, pair))
-
-    arrived = exchange_side(packs)
-    pair = swap(pair, pair_bit)
-    gradients.append(swap(jnp.concatenate(gradients, axis=0), 1))
+    across.append(swap(jnp.concatenate(gradients[2:], axis=0), 1))
     backs = back_rows(adapters, place, ranks, output_gradient, own_up)
-    backs = gather_step(backs, members)
-    arrived, backs, gradients, pair = barrier((arrived, backs, gradients, pair))
+    backs = [backs] + [swap(backs, offset) for offset in offsets[1:lines]]
+    arrived, backs, gradients, across, pair = barrier(
+        (arrived, backs, gradients, across, pair)
+    )
 
     parts, tokens_own, *tokens_pair = hidden_parts(
         adapters, place, down_maps, pair, arrived
     )
-    tokens_other = [swap(tokens_pair[0], pair_bit)]
-    while backs.shape[0] < members:
-        backs = gather_step(backs, members)
+    backs = gather_step(jnp.concatenate(backs, axis=0), members)
     slices, columns, columns_pair = input_slices(
-        adapters, place, gradients, backs, value_weight, pair, down_maps
-    )
-    total, flip = parts, 0
-    received = swap(parts[lines:], 1)
-    for step in reversed(range(steps - 1)):
+        adapters, place, gradients + across, backs, value_weight, pair, down_maps
+    )
+    total, received, flip = parts, swap(parts[lines:], 1), 0
+    for step in range(steps - 1):
         kinds = [jnp.float32] if step else [jnp.float32, jnp.bfloat16]
         sums = slot_sums(total, received, flip, kinds)
         total, flip = sums[0], 1 << step
         received = swap(sums[-1], offsets[flip])
-    received, slices, columns_pair, backs, tokens_pair, tokens_other = barrier(
-        (received, slices, columns_pair, backs, tokens_pair, tokens_other)
-    )
-
-    result = exchange_side(slices)
+        if step == 0:
+            received, slices, columns_pair, backs, tokens_pair = barrier(
+                (received, slices, columns_pair, backs, tokens_pair)
+            )
+            result = exchange_side(slices)
+
     hiddens = hidden_rows(adapters, place, ranks, total, received, flip, members)
     hiddens = gather_step(hiddens, members)
-    hiddens_pair = swap(hiddens, pair_bit)
     columns_other = swap(columns_pair, pair_bit)
     backs_pair = swap(backs, pair_bit)
-    hiddens_pair, columns_other, backs_pair, tokens_pair = barrier(
-        (hiddens_pair, columns_other, backs_pair, tokens_pair)
-    )
-    tokens_other.append(swap(tokens_pair[1], pair_bit))
+    tokens_other = [swap(half, pair_bit) for half in tokens_pair]
+    hiddens_pair = swap(hiddens, pair_bit)
     up_gradient = up_gradients(
         adapters, place, ranks, columns, columns_other, hiddens, hiddens_pair, depth // devices
     )

time: 166 us -> 188 us (1.13)
  the two profiles are of different devices: /device:TPU:10 before, /device:TPU:0 now
where the time goes in v15:
time: 188 us
  waiting for transfers between devices  112 us (60%)
  starting transfers between devices  36.4 us (19%)
  Pallas kernels  27.5 us (15%)
  local copies, waits for them, and re-layouts  7.89 us (4%)
  other arithmetic  2.92 us (2%)
    ppermute x19, waiting for transfers between devices, swap(): return lax.ppermute(array, 'dp', [(i, i ^ flip) for i in range(devices)])  112 us
    ppermute x19, starting transfers between devices, swap(): return lax.ppermute(array, 'dp', [(i, i ^ flip) for i in range(devices)])  22.2 us
    pallas_call x6, Pallas kernels, call(): pl.pallas_call(kernel, out_shape=out_shapes, grid_spec=pltpu.PrefetchScal...  11.5 us
    pallas_call x2, Pallas kernels, sums_call(): pl.pallas_call(kernel, out_shape=jax.ShapeDtypeStruct((num_adapters,) + p...  9.09 us
    all_to_all x2, starting transfers between devices, exchange_side(): lax.all_to_all(pieces, 'dp', split_axis=0, concat_axis=0, axis_index_grou...  8.11 us
    unnamed x42, local copies, waits for them, and re-layouts  7.85 us
    all_to_all x1, starting transfers between devices, exchange(): return lax.all_to_all(pieces, 'dp', split_axis=0, concat_axis=0, tiled=True)  6.05 us
    pallas_call x3, Pallas kernels, copy_call(): pl.pallas_call(kernel, out_shape=out_shapes, grid_spec=pltpu.PrefetchScal...  5.5 us
  transfers between devices with their start and end apart: 22, of which 13 were waited for; matrix products, arithmetic and copies ran while one was open for 1% of the time, Pallas kernels for 12%

profile of v15, /device:TPU:0, one launch (start us, length us, event | category | flops | bytes accessed | tf_op | source)
XLA Modules:
  0.0 187.9 jit_solution(18433348791118049478)
XLA Ops:
  0.6 4.1 %collective-permute-start = (bf16[1,128,1024]{2,1,0:T(8,128)(2,1)}, bf16[1,128,1024]{2,1,0:T(8,128)(2,1)}, u32[]{:S(2)}, u32[]{:S(2)}) collective-permute-start(bf16[1,128,1024]{2,1,0:T(8,128)(2,1)} %bitcast.3), channel_id=1, source_target_pairs={{0,8},{1,9},{2,10},{3,11},{4,12},{5,13},{6,14},{7,15},{8,0},{9,1},... | collective-permute-start | bytes 786440 | tf_op jit(solution)/shard_map/ppermute | solution.py:533
  4.8 12.2 %collective-permute-done.refs_1_ = bf16[1,128,1024]{2,1,0:T(8,128)(2,1)} collective-permute-done((bf16[1,128,1024]{2,1,0:T(8,128)(2,1)}, bf16[1,128,1024]{2,1,0:T(8,128)(2,1)}, u32[]{:S(2)}, u32[]{:S(2)}) %collective-permute-start) | collective-permute-done | bytes 262176 | tf_op jit(solution)/shard_map/ppermute | solution.py:533
  17.0 1.9 pad_maximum_fusion
  18.9 1.2 copy-done.8
  20.1 0.7 copy-done.13
  20.7 1.8 gather_up.1
  22.5 6.0 %all-to-all-start = ((bf16[16,64,128]{2,1,0:T(8,128)(2,1)}), bf16[16,64,128]{2,1,0:T(8,128)(2,1)}, u32[]{:S(2)}, u32[]{:S(2)}) async-start(bf16[16,64,128]{2,1,0:T(8,128)(2,1)} %gather_up.1), calls=%async_computation | async-start | bytes 524288 | tf_op jit(solution)/shard_map/all_to_all | solution.py:520
  28.6 1.9 %collective-permute-start.1 = (bf16[1,128,1024]{2,1,0:T(8,128)(2,1)S(1)}, bf16[1,128,1024]{2,1,0:T(8,128)(2,1)}, u32[]{:S(2)}, u32[]{:S(2)}) collective-permute-start(bf16[1,128,1024]{2,1,0:T(8,128)(2,1)S(1)} %bitcast.5), channel_id=1, source_target_pairs={{0,4},{1,5},{2,6},{3,7},{4,0},{5,1},{6,2},{7,3},{8,12},{9,13},{10,... | collective-permute-start | bytes 786440 | tf_op jit(solution)/shard_map/ppermute | solution.py:533
  30.5 1.8 pack_tokens.1
  32.4 1.9 %for_pair.1 = bf16[2048,512]{1,0:T(8,128)(2,1)S(1)} custom-call(s32[16]{0:T(128)S(1)} %copy-done.14, s32[1]{0:T(128)} %bitcast.place, bf16[1024,512]{1,0:T(8,128)(2,1)S(1)} %copy-done.1, bf16[64,128,512]{2,1,0:T(8,128)(2,1)} %refs_7_.3), custom_call_target="tpu_custom_call" | custom-call | tf_op jit(solution)/shard_map/for_pair/pallas_call | solution.py:83
  34.3 1.3 copy-done.5
  35.6 6.0 %collective-permute-done.1.refs_2_ = bf16[1,128,1024]{2,1,0:T(8,128)(2,1)} collective-permute-done((bf16[1,128,1024]{2,1,0:T(8,128)(2,1)S(1)}, bf16[1,128,1024]{2,1,0:T(8,128)(2,1)}, u32[]{:S(2)}, u32[]{:S(2)}) %collective-permute-start.1) | collective-permute-done | bytes 262176 | tf_op jit(solution)/shard_map/ppermute | solution.py:533
  41.6 4.5 %all-to-all-start.1 = ((bf16[8,2,128,512]{3,2,1,0:T(8,128)(2,1)}), bf16[8,2,128,512]{3,2,1,0:T(8,128)(2,1)}, u32[]{:S(2)}, u32[]{:S(2)}) async-start(bf16[8,2,128,512]{3,2,1,0:T(8,128)(2,1)} %pack_tokens.1), calls=%async_computation.1 | async-start | bytes 4194304 | tf_op jit(solution)/shard_map/all_to_all | solution.py:526
  46.1 1.5 collective-permute-start.8
  47.6 1.8 collective-permute-start.6
  49.5 39.1 %collective-permute-done.6.refs_3_ = bf16[1,128,1024]{2,1,0:T(8,128)(2,1)S(1)} collective-permute-done((bf16[1,128,1024]{2,1,0:T(8,128)(2,1)}, bf16[1,128,1024]{2,1,0:T(8,128)(2,1)S(1)}, u32[]{:S(2)}, u32[]{:S(2)}) %collective-permute-start.6) | collective-permute-done | bytes 262176 | tf_op jit(solution)/shard_map/ppermute | solution.py:533
  88.5 1.0 pad_maximum_fusion.1
  89.6 0.7 copy-done.6
  90.3 1.7 back_low.1
  92.0 2.5 %collective-permute-start.3 = (bf16[1,128,128]{2,1,0:T(8,128)(2,1)S(1)}, bf16[1,128,128]{2,1,0:T(8,128)(2,1)S(1)}, u32[]{:S(2)}, u32[]{:S(2)}) collective-permute-start(bf16[1,128,128]{2,1,0:T(8,128)(2,1)S(1)} %back_low.1), channel_id=1, source_target_pairs={{0,8},{1,9},{2,10},{3,11},{4,12},{5,13},{6,14},{7,15},{8,0},{9,1},... | collective-permute-start | bytes 98312 | tf_op jit(solution)/shard_map/ppermute | solution.py:533
  94.5 1.9 %collective-permute-start.5 = (bf16[1,128,128]{2,1,0:T(8,128)(2,1)S(1)}, bf16[1,128,128]{2,1,0:T(8,128)(2,1)S(1)}, u32[]{:S(2)}, u32[]{:S(2)}) collective-permute-start(bf16[1,128,128]{2,1,0:T(8,128)(2,1)S(1)} %back_low.1), channel_id=1, source_target_pairs={{0,12},{1,13},{2,14},{3,15},{4,8},{5,9},{6,10},{7,11},{8,4},{9,5},... | collective-permute-start | bytes 98312 | tf_op jit(solution)/shard_map/ppermute | solution.py:533
  96.4 0.9 collective-permute-done.3
  97.3 1.1 collective-permute-done.4
  98.4 1.8 collective-permute-done.5
  100.2 0.8 copy-done.11
  101.1 3.4 %hidden_parts.1 = (f32[8,128,128]{2,1,0:T(8,128)S(1)}, bf16[8,128,512]{2,1,0:T(8,128)(2,1)S(1)}, bf16[4,128,512]{2,1,0:T(8,128)(2,1)S(1)}, bf16[4,128,512]{2,1,0:T(8,128)(2,1)S(1)}) custom-call(s32[16]{0:T(128)S(1)} %copy-done.14, s32[1]{0:T(128)} %bitcast.place, bf16[2048,512]{1,0:T(8,128)(2,1)S(1)} %collective-permute-done.8.pair, ...), custom_call_target="tpu_custom_call" | custom-call | tf_op jit(solution)/shard_map/hidden_parts/pallas_call | solution.py:60
  104.5 1.0 copy-done.9
  105.6 0.6 collective-permute-start.9
  106.3 0.8 collective-permute-done.10.received
  107.3 5.7 %input_slices.1 = (bf16[8,2,128,512]{3,2,1,0:T(8,128)(2,1)S(1)}, bf16[8,128,128]{2,1,0:T(8,128)(2,1)S(1)}, bf16[8,128,128]{2,1,0:T(8,128)(2,1)S(1)}) custom-call(s32[16]{0:T(128)S(1)} %copy-done.14, s32[1]{0:T(128)} %bitcast.place, bf16[8,128,128]{2,1,0:T(8,128)(2,1)S(1)} %constant_dynamic-update-slice_fusion.backs, bf16[2048,512]{1,0:T(8,128)(2,1)} %copy-done, ...), custom_call_target="tpu_custom_call" | custom-call | tf_op jit(solution)/shard_map/input_slices/pallas_call | solution.py:60
  113.0 1.3 copy-done.4
  114.4 0.7 copy-done.18
  115.1 1.0 collective-permute-done.11.received
  116.1 3.6 %all-to-all-start.2 = ((bf16[8,2,128,512]{3,2,1,0:T(8,128)(2,1)}), bf16[8,2,128,512]{3,2,1,0:T(8,128)(2,1)S(1)}, u32[]{:S(2)}, u32[]{:S(2)}) async-start(bf16[8,2,128,512]{3,2,1,0:T(8,128)(2,1)} %copy-done.4), calls=%async_computation.2 | async-start | bytes 4194304 | tf_op jit(solution)/shard_map/all_to_all | solution.py:526
  119.8 2.0 %collective-permute-start.13 = (f32[4,128,128]{2,1,0:T(8,128)S(1)}, f32[4,128,128]{2,1,0:T(8,128)S(1)}, u32[]{:S(2)}, u32[]{:S(2)}) collective-permute-start(f32[4,128,128]{2,1,0:T(8,128)S(1)} %slot_sums.3.total), channel_id=1, source_target_pairs={{0,4},{1,5},{2,6},{3,7},{4,0},{5,1},{6,2},{7,3},{8,12},{9,13},{10,... | collective-permute-start | bytes 786440 | tf_op jit(solution)/shard_map/ppermute | solution.py:533
  121.8 1.5 collective-permute-start.17
  123.2 0.6 collective-permute-start.18
  123.8 38.4 %collective-permute-done.13.received = f32[4,128,128]{2,1,0:T(8,128)S(1)} collective-permute-done((f32[4,128,128]{2,1,0:T(8,128)S(1)}, f32[4,128,128]{2,1,0:T(8,128)S(1)}, u32[]{:S(2)}, u32[]{:S(2)}) %collective-permute-start.13) | collective-permute-done | bytes 262176 | tf_op jit(solution)/shard_map/ppermute | solution.py:533
  162.2 0.6 hidden_low.1
  162.9 1.5 collective-permute-start.16
  164.4 0.6 collective-permute-start.12
  165.0 1.5 collective-permute-start.15
  166.5 5.5 %collective-permute-done.16.backs_pair = bf16[8,128,128]{2,1,0:T(8,128)(2,1)S(1)} collective-permute-done((bf16[8,128,128]{2,1,0:T(8,128)(2,1)S(1)}, bf16[8,128,128]{2,1,0:T(8,128)(2,1)S(1)}, u32[]{:S(2)}, u32[]{:S(2)}) %collective-permute-start.16) | collective-permute-done | bytes 262176 | tf_op jit(solution)/shard_map/ppermute | solution.py:533
  172.0 5.5 %down_gradients.1 = bf16[64,128,512]{2,1,0:T(8,128)(2,1)} custom-call(s32[16]{0:T(128)S(1)} %copy-done.14, s32[1]{0:T(128)} %bitcast.place, bf16[8,128,128]{2,1,0:T(8,128)(2,1)S(1)} %constant_dynamic-update-slice_fusion.backs, bf16[8,128,128]{2,1,0:T(8,128)(2,1)S(1)} %collective-permute-done.16.backs_pair, bf16[8,128,512]{2,1,0:T(8,128)(2,1)S(1)} %copy-done.10, ...), custom_call_target="tpu_custom_call" | custom-call | tf_op jit(solution)/shard_map/down_gradients/pallas_call | solution.py:406
  177.5 0.1 collective-permute-done.12.gradients_pair
  177.7 5.2 %collective-permute-done.15.hiddens_pair = bf16[8,128,128]{2,1,0:T(8,128)(2,1)S(1)} collective-permute-done((bf16[8,128,128]{2,1,0:T(8,128)(2,1)S(1)}, bf16[8,128,128]{2,1,0:T(8,128)(2,1)S(1)}, u32[]{:S(2)}, u32[]{:S(2)}) %collective-permute-start.15) | collective-permute-done | bytes 262176 | tf_op jit(solution)/shard_map/ppermute | solution.py:533
  182.8 3.6 %up_gradients.1 = bf16[64,64,128]{2,1,0:T(8,128)(2,1)} custom-call(s32[16]{0:T(128)S(1)} %copy-done.14, s32[1]{0:T(128)} %bitcast.place, s32[64]{0:T(128)S(1)} %copy-done.15, bf16[8,128,128]{2,1,0:T(8,128)(2,1)S(1)} %get-tuple-element.56.gradients, bf16[8,128,128]{2,1,0:T(8,128)(2,1)S(1)} %collective-permute-done.12.gradients_pair, ...), custom_call_target="tpu_custom_call" | custom-call | tf_op jit(solution)/shard_map/up_gradients/pallas_call | solution.py:406
  186.4 1.5 join_columns.1
  (56 shorter events, 0.6 us)
Async XLA Ops:
  0.6 27.9 %copy-start.2 = (bf16[128,1024]{1,0:T(8,128)(2,1)S(1)}, bf16[128,1024]{1,0:T(8,128)(2,1)}, u32[]{:S(2)}) copy-start(bf16[128,1024]{1,0:T(8,128)(2,1)} %gradient.1) | copy-start | bytes 786436
  0.6 29.9 %copy-start.3 = (bf16[128,8192]{1,0:T(8,128)(2,1)S(1)}, bf16[128,8192]{1,0:T(8,128)(2,1)}, u32[]{:S(2)}) copy-start(bf16[128,8192]{1,0:T(8,128)(2,1)} %tokens.1) | copy-start | bytes 6291460
  0.6 16.3 %collective-permute-start = (bf16[1,128,1024]{2,1,0:T(8,128)(2,1)}, bf16[1,128,1024]{2,1,0:T(8,128)(2,1)}, u32[]{:S(2)}, u32[]{:S(2)}) collective-permute-start(bf16[1,128,1024]{2,1,0:T(8,128)(2,1)} %bitcast.3), channel_id=1, source_target_pairs={{0,8},{1,9},{2,10},{3,11},{4,12},{5,13},{6,14},{7,15},{8,0},{9,1},... | collective-permute-start | bytes 786440 | tf_op jit(solution)/shard_map/ppermute | solution.py:533
  18.9 22.7 %collective-permute-start.2 = (bf16[2,128,1024]{2,1,0:T(8,128)(2,1)}, bf16[2,128,1024]{2,1,0:T(8,128)(2,1)}, u32[]{:S(2)}, u32[]{:S(2)}) collective-permute-start(bf16[2,128,1024]{2,1,0:T(8,128)(2,1)} %pad_maximum_fusion), channel_id=1, source_target_pairs={{0,1},{1,0},{2,3},{3,2},{4,5},{5,4},{6,7},{7,6},{8,9},{9,8},{10,11... | collective-permute-start | bytes 1572872 | tf_op jit(solution)/shard_map/ppermute | solution.py:533
  18.9 1.2 copy-start.8
  20.1 0.7 copy-start.13
  22.5 19.1 %all-to-all-start = ((bf16[16,64,128]{2,1,0:T(8,128)(2,1)}), bf16[16,64,128]{2,1,0:T(8,128)(2,1)}, u32[]{:S(2)}, u32[]{:S(2)}) async-start(bf16[16,64,128]{2,1,0:T(8,128)(2,1)} %gather_up.1), calls=%async_computation | async-start | bytes 524288 | tf_op jit(solution)/shard_map/all_to_all | solution.py:520
  28.6 13.0 %collective-permute-start.1 = (bf16[1,128,1024]{2,1,0:T(8,128)(2,1)S(1)}, bf16[1,128,1024]{2,1,0:T(8,128)(2,1)}, u32[]{:S(2)}, u32[]{:S(2)}) collective-permute-start(bf16[1,128,1024]{2,1,0:T(8,128)(2,1)S(1)} %bitcast.5), channel_id=1, source_target_pairs={{0,4},{1,5},{2,6},{3,7},{4,0},{5,1},{6,2},{7,3},{8,12},{9,13},{10,... | collective-permute-start | bytes 786440 | tf_op jit(solution)/shard_map/ppermute | solution.py:533
  30.5 1.8 copy-start.1
  30.5 1.8 copy-start.14
  34.3 1.3 copy-start.5
  41.6 48.7 %copy-start.15 = (s32[64]{0:T(128)S(1)}, s32[64]{0:T(128)}, u32[]{:S(2)}) copy-start(s32[64]{0:T(128)} %ranks.5) | copy-start | bytes 772
  41.6 59.5 %all-to-all-start.1 = ((bf16[8,2,128,512]{3,2,1,0:T(8,128)(2,1)}), bf16[8,2,128,512]{3,2,1,0:T(8,128)(2,1)}, u32[]{:S(2)}, u32[]{:S(2)}) async-start(bf16[8,2,128,512]{3,2,1,0:T(8,128)(2,1)} %pack_tokens.1), calls=%async_computation.1 | async-start | bytes 4194304 | tf_op jit(solution)/shard_map/all_to_all | solution.py:526
  46.1 54.9 %collective-permute-start.8 = (bf16[2048,512]{1,0:T(8,128)(2,1)}, bf16[2048,512]{1,0:T(8,128)(2,1)S(1)}, u32[]{:S(2)}, u32[]{:S(2)}) collective-permute-start(bf16[2048,512]{1,0:T(8,128)(2,1)} %copy-done.5), channel_id=1, source_target_pairs={{0,2},{1,3},{2,0},{3,1},{4,6},{5,7},{6,4},{7,5},{8,10},{9,11},{10,... | collective-permute-start | bytes 6291464 | tf_op jit(solution)/shard_map/ppermute | solution.py:533
  47.6 40.9 %collective-permute-start.6 = (bf16[1,128,1024]{2,1,0:T(8,128)(2,1)}, bf16[1,128,1024]{2,1,0:T(8,128)(2,1)S(1)}, u32[]{:S(2)}, u32[]{:S(2)}) collective-permute-start(bf16[1,128,1024]{2,1,0:T(8,128)(2,1)} %collective-permute-done.refs_1_), channel_id=1, source_target_pairs={{0,4},{1,5},{2,6},{3,7},{4,0},{5,1},{6,2},{7,3},{8,12},{9,13},{10,... | collective-permute-start | bytes 786440 | tf_op jit(solution)/shard_map/ppermute | solution.py:533
  89.5 0.7 copy-start.6
  90.3 10.0 %collective-permute-start.7 = (bf16[2,128,1024]{2,1,0:T(8,128)(2,1)S(1)}, bf16[2,128,1024]{2,1,0:T(8,128)(2,1)S(1)}, u32[]{:S(2)}, u32[]{:S(2)}) collective-permute-start(bf16[2,128,1024]{2,1,0:T(8,128)(2,1)S(1)} %pad_maximum_fusion.1), channel_id=1, source_target_pairs={{0,1},{1,0},{2,3},{3,2},{4,5},{5,4},{6,7},{7,6},{8,9},{9,8},{10,11... | collective-permute-start | bytes 1572872 | tf_op jit(solution)/shard_map/ppermute | solution.py:533
  92.0 5.4 %collective-permute-start.3 = (bf16[1,128,128]{2,1,0:T(8,128)(2,1)S(1)}, bf16[1,128,128]{2,1,0:T(8,128)(2,1)S(1)}, u32[]{:S(2)}, u32[]{:S(2)}) collective-permute-start(bf16[1,128,128]{2,1,0:T(8,128)(2,1)S(1)} %back_low.1), channel_id=1, source_target_pairs={{0,8},{1,9},{2,10},{3,11},{4,12},{5,13},{6,14},{7,15},{8,0},{9,1},... | collective-permute-start | bytes 98312 | tf_op jit(solution)/shard_map/ppermute | solution.py:533
  94.5 3.9 %collective-permute-start.4 = (bf16[1,128,128]{2,1,0:T(8,128)(2,1)S(1)}, bf16[1,128,128]{2,1,0:T(8,128)(2,1)S(1)}, u32[]{:S(2)}, u32[]{:S(2)}) collective-permute-start(bf16[1,128,128]{2,1,0:T(8,128)(2,1)S(1)} %back_low.1), channel_id=1, source_target_pairs={{0,4},{1,5},{2,6},{3,7},{4,0},{5,1},{6,2},{7,3},{8,12},{9,13},{10,... | collective-permute-start | bytes 98312 | tf_op jit(solution)/shard_map/ppermute | solution.py:533
  94.5 5.7 %collective-permute-start.5 = (bf16[1,128,128]{2,1,0:T(8,128)(2,1)S(1)}, bf16[1,128,128]{2,1,0:T(8,128)(2,1)S(1)}, u32[]{:S(2)}, u32[]{:S(2)}) collective-permute-start(bf16[1,128,128]{2,1,0:T(8,128)(2,1)S(1)} %back_low.1), channel_id=1, source_target_pairs={{0,12},{1,13},{2,14},{3,15},{4,8},{5,9},{6,10},{7,11},{8,4},{9,5},... | collective-permute-start | bytes 98312 | tf_op jit(solution)/shard_map/ppermute | solution.py:533
  100.2 0.8 copy-start.11
  101.0 3.4 %copy-start = (bf16[2048,512]{1,0:T(8,128)(2,1)}, bf16[2048,512]{1,0:T(8,128)(2,1)S(1)}, u32[]{:S(2)}) copy-start(bf16[2048,512]{1,0:T(8,128)(2,1)S(1)} %collective-permute-done.8.pair) | copy-start | bytes 6291460
  104.5 1.0 copy-start.9
  105.5 0.8 copy-start.16
  105.5 1.8 copy-start.17
  105.5 1.8 copy-start.7
  105.5 1.9 copy-start.12
  105.5 1.6 collective-permute-start.10
  105.6 1.7 collective-permute-start.9
  107.1 9.0 %collective-permute-start.11 = (bf16[4,128,128]{2,1,0:T(8,128)(2,1)S(1)}, bf16[4,128,128]{2,1,0:T(8,128)(2,1)S(1)}, u32[]{:S(2)}, u32[]{:S(2)}) collective-permute-start(bf16[4,128,128]{2,1,0:T(8,128)(2,1)S(1)} %get-tuple-element.59), channel_id=1, source_target_pairs={{0,8},{1,9},{2,10},{3,11},{4,12},{5,13},{6,14},{7,15},{8,0},{9,1},... | collective-permute-start | bytes 393224 | tf_op jit(solution)/shard_map/ppermute | solution.py:533
  113.0 1.3 copy-start.4
  114.4 0.7 copy-start.18
  116.1 70.3 %all-to-all-start.2 = ((bf16[8,2,128,512]{3,2,1,0:T(8,128)(2,1)}), bf16[8,2,128,512]{3,2,1,0:T(8,128)(2,1)S(1)}, u32[]{:S(2)}, u32[]{:S(2)}) async-start(bf16[8,2,128,512]{3,2,1,0:T(8,128)(2,1)} %copy-done.4), calls=%async_computation.2 | async-start | bytes 4194304 | tf_op jit(solution)/shard_map/all_to_all | solution.py:526
  119.7 52.3 %copy-start.10 = (bf16[8,128,512]{2,1,0:T(8,128)(2,1)S(1)}, bf16[8,128,512]{2,1,0:T(8,128)(2,1)}, u32[]{:S(2)}) copy-start(bf16[8,128,512]{2,1,0:T(8,128)(2,1)} %copy-done.9) | copy-start | bytes 3145732
  119.8 42.4 %collective-permute-start.13 = (f32[4,128,128]{2,1,0:T(8,128)S(1)}, f32[4,128,128]{2,1,0:T(8,128)S(1)}, u32[]{:S(2)}, u32[]{:S(2)}) collective-permute-start(f32[4,128,128]{2,1,0:T(8,128)S(1)} %slot_sums.3.total), channel_id=1, source_target_pairs={{0,4},{1,5},{2,6},{3,7},{4,0},{5,1},{6,2},{7,3},{8,12},{9,13},{10,... | collective-permute-start | bytes 786440 | tf_op jit(solution)/shard_map/ppermute | solution.py:533
  121.8 50.3 %collective-permute-start.17 = (bf16[4,128,512]{2,1,0:T(8,128)(2,1)}, bf16[4,128,512]{2,1,0:T(8,128)(2,1)S(1)}, u32[]{:S(2)}, u32[]{:S(2)}) collective-permute-start(bf16[4,128,512]{2,1,0:T(8,128)(2,1)} %copy-done.17), channel_id=1, source_target_pairs={{0,2},{1,3},{2,0},{3,1},{4,6},{5,7},{6,4},{7,5},{8,10},{9,11},{10,... | collective-permute-start | bytes 1572872 | tf_op jit(solution)/shard_map/ppermute | solution.py:533
  123.2 48.8 %collective-permute-start.18 = (bf16[4,128,512]{2,1,0:T(8,128)(2,1)}, bf16[4,128,512]{2,1,0:T(8,128)(2,1)S(1)}, u32[]{:S(2)}, u32[]{:S(2)}) collective-permute-start(bf16[4,128,512]{2,1,0:T(8,128)(2,1)} %copy-done.16), channel_id=1, source_target_pairs={{0,2},{1,3},{2,0},{3,1},{4,6},{5,7},{6,4},{7,5},{8,10},{9,11},{10,... | collective-permute-start | bytes 1572872 | tf_op jit(solution)/shard_map/ppermute | solution.py:533
  162.8 2.2 %collective-permute-start.14 = (bf16[4,128,128]{2,1,0:T(8,128)(2,1)S(1)}, bf16[4,128,128]{2,1,0:T(8,128)(2,1)S(1)}, u32[]{:S(2)}, u32[]{:S(2)}) collective-permute-start(bf16[4,128,128]{2,1,0:T(8,128)(2,1)S(1)} %hidden_low.1), channel_id=1, source_target_pairs={{0,1},{1,0},{2,3},{3,2},{4,5},{5,4},{6,7},{7,6},{8,9},{9,8},{10,11... | collective-permute-start | bytes 393224 | tf_op jit(solution)/shard_map/ppermute | solution.py:533
  162.9 9.2 %collective-permute-start.16 = (bf16[8,128,128]{2,1,0:T(8,128)(2,1)S(1)}, bf16[8,128,128]{2,1,0:T(8,128)(2,1)S(1)}, u32[]{:S(2)}, u32[]{:S(2)}) collective-permute-start(bf16[8,128,128]{2,1,0:T(8,128)(2,1)S(1)} %constant_dynamic-update-slice_fusion.backs), channel_id=1, source_target_pairs={{0,2},{1,3},{2,0},{3,1},{4,6},{5,7},{6,4},{7,5},{8,10},{9,11},{10,... | collective-permute-start | bytes 786440 | tf_op jit(solution)/shard_map/ppermute | solution.py:533
  164.4 13.3 %collective-permute-start.12 = (bf16[8,128,128]{2,1,0:T(8,128)(2,1)}, bf16[8,128,128]{2,1,0:T(8,128)(2,1)S(1)}, u32[]{:S(2)}, u32[]{:S(2)}) collective-permute-start(bf16[8,128,128]{2,1,0:T(8,128)(2,1)} %copy-done.18), channel_id=1, source_target_pairs={{0,2},{1,3},{2,0},{3,1},{4,6},{5,7},{6,4},{7,5},{8,10},{9,11},{10,... | collective-permute-start | bytes 786440 | tf_op jit(solution)/shard_map/ppermute | solution.py:533
  165.0 17.8 %collective-permute-start.15 = (bf16[8,128,128]{2,1,0:T(8,128)(2,1)S(1)}, bf16[8,128,128]{2,1,0:T(8,128)(2,1)S(1)}, u32[]{:S(2)}, u32[]{:S(2)}) collective-permute-start(bf16[8,128,128]{2,1,0:T(8,128)(2,1)S(1)} %pad_maximum_fusion.2.hiddens), channel_id=1, source_target_pairs={{0,2},{1,3},{2,0},{3,1},{4,6},{5,7},{6,4},{7,5},{8,10},{9,11},{10,... | collective-permute-start | bytes 786440 | tf_op jit(solution)/shard_map/ppermute | solution.py:533

commit v16 on v15

--- a/solution.py
+++ b/solution.py
@@ -192,12 +192,9 @@
 
 def input_kernel(adapters, place, backs, pair, *refs):
     members, rows, _ = backs.shape
-    apart = members // 2
-    gradients = [ref.at[0] for ref in refs[:apart]]
-    for ref in refs[apart : apart + 2]:
-        gradients += [ref.at[slot] for slot in range(ref.shape[0])]
-    downs = refs[apart + 2 : apart + 2 + members]
-    weight = refs[apart + 2 + members]
+    gradients = [ref.at[0] for ref in refs[:members]]
+    downs = refs[members : 2 * members]
+    weight = refs[2 * members]
     out, *columns = refs[-3:]
     extent = downs[0].shape[1]
     lanes = columns[0].shape[2]
@@ -560,44 +557,51 @@
         gradients[1 << step] = swap(own_gradient, offsets[1 << step])
     own_up = exchange(gather_up(adapters, up_maps)).reshape(depth, extent)
     packs = pack_tokens(place, tokens, members, width)
-    pair = for_pair(adapters, place, value_weight, down_maps, members)
-    across = [swap(jnp.concatenate(gradients[:2], axis=0), 1)]
-    firsts = [gradients[1 << step] for step in range(steps - 1)]
-    firsts, across, own_up, packs, pair = barrier((firsts, across, own_up, packs, pair))
-    for step in range(steps - 1):
-        gradients[1 << step] = firsts[step]
+    firsts = [1 << step for step in range(steps - 1)]
+    across = {slot: swap(gradients[slot], 1) for slot in [0] + firsts}
+    held, crossed, own_up, packs, adapters = barrier(
+        ([gradients[slot] for slot in firsts], across, own_up, packs, adapters)
+    )
+    across = dict(crossed)
+    for slot, block in zip(firsts, held):
+        gradients[slot] = block
 
     arrived = exchange_side(packs)
-    pair = swap(pair, pair_bit)
+    pair = swap(for_pair(adapters, place, value_weight, down_maps, members), pair_bit)
     for step in range(1, steps - 1):
         for slot in range(1, 1 << step):
             gradients[slot + (1 << step)] = swap(gradients[slot], offsets[1 << step])
-    across.append(swap(jnp.concatenate(gradients[2:], axis=0), 1))
     backs = back_rows(adapters, place, ranks, output_gradient, own_up)
     backs = [backs] + [swap(backs, offset) for offset in offsets[1:lines]]
-    arrived, backs, gradients, across, pair = barrier(
-        (arrived, backs, gradients, across, pair)
-    )
+    arrived, backs, gradients, pair = barrier((arrived, backs, gradients, pair))
 
     parts, tokens_own, *tokens_pair = hidden_parts(
         adapters, place, down_maps, pair, arrived
     )
+    for slot in range(lines):
+        if slot not in across:
+            across[slot] = swap(gradients[slot], 1)
     backs = gather_step(jnp.concatenate(backs, axis=0), members)
     slices, columns, columns_pair = input_slices(
-        adapters, place, gradients + across, backs, value_weight, pair, down_maps
+        adapters,
+        place,
+        gradients + [across[slot] for slot in range(lines)],
+        backs,
+        value_weight,
+        pair,
+        down_maps,
     )
     total, received, flip = parts, swap(parts[lines:], 1), 0
-    for step in range(steps - 1):
+    for step in reversed(range(steps - 1)):
         kinds = [jnp.float32] if step else [jnp.float32, jnp.bfloat16]
         sums = slot_sums(total, received, flip, kinds)
         total, flip = sums[0], 1 << step
         received = swap(sums[-1], offsets[flip])
-        if step == 0:
-            received, slices, columns_pair, backs, tokens_pair = barrier(
-                (received, slices, columns_pair, backs, tokens_pair)
-            )
-            result = exchange_side(slices)
-
+    received, slices, columns_pair, backs, tokens_pair = barrier(
+        (received, slices, columns_pair, backs, tokens_pair)
+    )
+
+    result = exchange_side(slices)
     hiddens = hidden_rows(adapters, place, ranks, total, received, flip, members)
     hiddens = gather_step(hiddens, members)
     columns_other = swap(columns_pair, pair_bit)

time: 188 us -> 160 us (0.85)
  waiting for transfers between devices: 112 us -> 88.5 us
  starting transfers between devices: 36.4 us -> 32.7 us
  other arithmetic: 2.92 us -> 0.05 us
  local copies, waits for them, and re-layouts: 7.89 us -> 10.3 us
    ppermute x19 -> x21, waiting for transfers between devices: 112 us -> 86.7 us  [swap(): return lax.ppermute(array, 'dp', [(i, i ^ flip) for i in range(devices)])]
    concatenate x2 -> x0, other arithmetic: 2.87 us -> none  [the longest x1 1.87 us: local(): across = [swap(jnp.concatenate(gradients[:2], axis=0), 1)]]
    all_to_all x1, starting transfers between devices: 6.05 us -> 3.55 us  [exchange(): return lax.all_to_all(pieces, 'dp', split_axis=0, concat_axis=0, tiled=True)]
    unnamed x42 -> x64, local copies, waits for them, and re-layouts: 7.85 us -> 10.3 us
    ppermute x19 -> x21, starting transfers between devices: 22.2 us -> 20.9 us  [swap(): return lax.ppermute(array, 'dp', [(i, i ^ flip) for i in range(devices)])]
  transfers between devices with their start and end apart: 22 -> 24, of which waited for: 13 -> 11; matrix products, arithmetic and copies ran while one was open for 1% -> 0% of each run, Pallas kernels for 12% -> 13%
where the time goes in v16:
time: 160 us; the launch traced here: 159 us
  waiting for transfers between devices  88.5 us (55%)
  starting transfers between devices  32.7 us (20%)
  Pallas kernels  26.4 us (16%)
  local copies, waits for them, and re-layouts  10.3 us (6%)
    ppermute x21, waiting for transfers between devices, swap(): return lax.ppermute(array, 'dp', [(i, i ^ flip) for i in range(devices)])  86.7 us
    ppermute x21, starting transfers between devices, swap(): return lax.ppermute(array, 'dp', [(i, i ^ flip) for i in range(devices)])  20.9 us
    pallas_call x6, Pallas kernels, call(): pl.pallas_call(kernel, out_shape=out_shapes, grid_spec=pltpu.PrefetchScal...  10.4 us
    unnamed x64, local copies, waits for them, and re-layouts  10.3 us
    pallas_call x2, Pallas kernels, sums_call(): pl.pallas_call(kernel, out_shape=jax.ShapeDtypeStruct((num_adapters,) + p...  9.07 us
    all_to_all x2, starting transfers between devices, exchange_side(): lax.all_to_all(pieces, 'dp', split_axis=0, concat_axis=0, axis_index_grou...  8.23 us
    pallas_call x3, Pallas kernels, copy_call(): pl.pallas_call(kernel, out_shape=out_shapes, grid_spec=pltpu.PrefetchScal...  5.5 us
    all_to_all x1, starting transfers between devices, exchange(): return lax.all_to_all(pieces, 'dp', split_axis=0, concat_axis=0, tiled=True)  3.55 us
  transfers between devices with their start and end apart: 24, of which 11 were waited for; matrix products, arithmetic and copies ran while one was open for 0% of the time, Pallas kernels for 13%

profile of v16, /device:TPU:0, one launch (start us, length us, event | category | flops | bytes accessed | tf_op | source)
XLA Modules:
  0.0 159.0 jit_solution(12893643082641271697)
XLA Ops:
  0.6 4.1 %collective-permute-start = (bf16[1,128,1024]{2,1,0:T(8,128)(2,1)}, bf16[1,128,1024]{2,1,0:T(8,128)(2,1)S(1)}, u32[]{:S(2)}, u32[]{:S(2)}) collective-permute-start(bf16[1,128,1024]{2,1,0:T(8,128)(2,1)} %bitcast.3), channel_id=1, source_target_pairs={{0,8},{1,9},{2,10},{3,11},{4,12},{5,13},{6,14},{7,15},{8,0},{9,1},... | collective-permute-start | bytes 786440 | tf_op jit(solution)/shard_map/ppermute | solution.py:530
  4.7 1.6 collective-permute-start.1
  6.3 1.2 copy-done.5
  7.5 0.7 copy-done.23
  8.2 1.8 %gather_up.1 = bf16[16,64,128]{2,1,0:T(8,128)(2,1)} custom-call(s32[16]{0:T(128)S(1)} %copy-done.23, bf16[64,64,128]{2,1,0:T(8,128)(2,1)S(1)} %copy-done.5), custom_call_target="tpu_custom_call" | custom-call | tf_op jit(solution)/shard_map/gather_up/pallas_call | solution.py:83
  10.0 3.5 %all-to-all-start = ((bf16[16,64,128]{2,1,0:T(8,128)(2,1)}), bf16[16,64,128]{2,1,0:T(8,128)(2,1)S(1)}, u32[]{:S(2)}, u32[]{:S(2)}) async-start(bf16[16,64,128]{2,1,0:T(8,128)(2,1)} %gather_up.1), calls=%async_computation | async-start | bytes 524288 | tf_op jit(solution)/shard_map/all_to_all | solution.py:517
  13.8 3.2 %collective-permute-done.refs_1_ = bf16[1,128,1024]{2,1,0:T(8,128)(2,1)S(1)} collective-permute-done((bf16[1,128,1024]{2,1,0:T(8,128)(2,1)}, bf16[1,128,1024]{2,1,0:T(8,128)(2,1)S(1)}, u32[]{:S(2)}, u32[]{:S(2)}) %collective-permute-start) | collective-permute-done | bytes 262176 | tf_op jit(solution)/shard_map/ppermute | solution.py:530
  17.0 0.4 collective-permute-done.1.refs_2_
  17.5 1.6 %copy-done.2 = bf16[128,8192]{1,0:T(8,128)(2,1)S(1)} copy-done((bf16[128,8192]{1,0:T(8,128)(2,1)S(1)}, bf16[128,8192]{1,0:T(8,128)(2,1)}, u32[]{:S(2)}) %copy-start.2) | copy-done | bytes 2097176
  19.1 1.8 %pack_tokens.1 = bf16[8,2,128,512]{3,2,1,0:T(8,128)(2,1)} custom-call(s32[1]{0:T(128)} %bitcast.place, bf16[128,8192]{1,0:T(8,128)(2,1)S(1)} %copy-done.2), custom_call_target="tpu_custom_call" | custom-call | tf_op jit(solution)/shard_map/pack_tokens/pallas_call | solution.py:83
  21.0 0.7 copy-done.15
  21.7 1.8 %all-to-all-done = bf16[16,64,128]{2,1,0:T(8,128)(2,1)S(1)} async-done(((bf16[16,64,128]{2,1,0:T(8,128)(2,1)}), bf16[16,64,128]{2,1,0:T(8,128)(2,1)S(1)}, u32[]{:S(2)}, u32[]{:S(2)}) %all-to-all-start) | async-done | bytes 262176 | tf_op jit(solution)/shard_map/all_to_all | solution.py:517
  23.5 0.7 copy-done.6
  24.3 0.7 copy-done.17
  25.0 4.3 %all-to-all-start.1 = ((bf16[8,2,128,512]{3,2,1,0:T(8,128)(2,1)}), bf16[8,2,128,512]{3,2,1,0:T(8,128)(2,1)}, u32[]{:S(2)}, u32[]{:S(2)}) async-start(bf16[8,2,128,512]{3,2,1,0:T(8,128)(2,1)} %pack_tokens.1), calls=%async_computation.1 | async-start | bytes 4194304 | tf_op jit(solution)/shard_map/all_to_all | solution.py:523
  29.4 1.9 %for_pair.1 = bf16[2048,512]{1,0:T(8,128)(2,1)S(1)} custom-call(s32[16]{0:T(128)S(1)} %copy-done.24, s32[1]{0:T(128)} %bitcast.place, bf16[1024,512]{1,0:T(8,128)(2,1)S(1)} %copy-done.1, bf16[64,128,512]{2,1,0:T(8,128)(2,1)} %refs_7_.1), custom_call_target="tpu_custom_call" | custom-call | tf_op jit(solution)/shard_map/for_pair/pallas_call | solution.py:83
  31.4 0.9 collective-permute-start.9
  32.3 2.0 %collective-permute-start.8 = (bf16[1,128,1024]{2,1,0:T(8,128)(2,1)S(1)}, bf16[1,128,1024]{2,1,0:T(8,128)(2,1)S(1)}, u32[]{:S(2)}, u32[]{:S(2)}) collective-permute-start(bf16[1,128,1024]{2,1,0:T(8,128)(2,1)S(1)} %copy-done.11), channel_id=1, source_target_pairs={{0,4},{1,5},{2,6},{3,7},{4,0},{5,1},{6,2},{7,3},{8,12},{9,13},{10,... | collective-permute-start | bytes 786440 | tf_op jit(solution)/shard_map/ppermute | solution.py:530
  34.3 0.8 back_low.1
  35.0 2.4 %collective-permute-start.5 = (bf16[1,128,128]{2,1,0:T(8,128)(2,1)S(1)}, bf16[1,128,128]{2,1,0:T(8,128)(2,1)S(1)}, u32[]{:S(2)}, u32[]{:S(2)}) collective-permute-start(bf16[1,128,128]{2,1,0:T(8,128)(2,1)S(1)} %back_low.1), channel_id=1, source_target_pairs={{0,8},{1,9},{2,10},{3,11},{4,12},{5,13},{6,14},{7,15},{8,0},{9,1},... | collective-permute-start | bytes 98312 | tf_op jit(solution)/shard_map/ppermute | solution.py:530
  37.5 0.6 collective-permute-start.6
  38.0 1.5 collective-permute-start.7
  39.5 41.3 %collective-permute-done.5 = bf16[1,128,128]{2,1,0:T(8,128)(2,1)S(1)} collective-permute-done((bf16[1,128,128]{2,1,0:T(8,128)(2,1)S(1)}, bf16[1,128,128]{2,1,0:T(8,128)(2,1)S(1)}, u32[]{:S(2)}, u32[]{:S(2)}) %collective-permute-start.5) | collective-permute-done | bytes 32800 | tf_op jit(solution)/shard_map/ppermute | solution.py:530
  80.8 0.7 copy-done.21
  81.6 3.5 %hidden_parts.1 = (f32[8,128,128]{2,1,0:T(8,128)S(1)}, bf16[8,128,512]{2,1,0:T(8,128)(2,1)S(1)}, bf16[4,128,512]{2,1,0:T(8,128)(2,1)S(1)}, bf16[4,128,512]{2,1,0:T(8,128)(2,1)S(1)}) custom-call(s32[16]{0:T(128)S(1)} %copy-done.24, s32[1]{0:T(128)} %bitcast.place, bf16[2048,512]{1,0:T(8,128)(2,1)S(1)} %collective-permute-done.9.pair, ...), custom_call_target="tpu_custom_call" | custom-call | tf_op jit(solution)/shard_map/hidden_parts/pallas_call | solution.py:60
  85.1 1.0 copy-done.8
  86.1 0.8 copy-done.26
  87.0 1.5 collective-permute-done.12.received
  88.5 1.0 collective-permute-start.13
  89.5 0.5 collective-permute-start.11
  90.1 6.9 %collective-permute-done.13.received = f32[4,128,128]{2,1,0:T(8,128)S(1)} collective-permute-done((f32[4,128,128]{2,1,0:T(8,128)S(1)}, f32[4,128,128]{2,1,0:T(8,128)S(1)}, u32[]{:S(2)}, u32[]{:S(2)}) %collective-permute-start.13) | collective-permute-done | bytes 262176 | tf_op jit(solution)/shard_map/ppermute | solution.py:530
  97.0 0.7 collective-permute-start.14
  97.8 5.5 %input_slices.1 = (bf16[8,2,128,512]{3,2,1,0:T(8,128)(2,1)S(1)}, bf16[8,128,128]{2,1,0:T(8,128)(2,1)S(1)}, bf16[8,128,128]{2,1,0:T(8,128)(2,1)S(1)}) custom-call(s32[16]{0:T(128)S(1)} %copy-done.24, s32[1]{0:T(128)} %bitcast.place, bf16[8,128,128]{2,1,0:T(8,128)(2,1)S(1)} %constant_dynamic-update-slice_fusion.backs, bf16[2048,512]{1,0:T(8,128)(2,1)} %copy-done, ...), custom_call_target="tpu_custom_call" | custom-call | tf_op jit(solution)/shard_map/input_slices/pallas_call | solution.py:60
  103.3 1.3 copy-done.3
  104.7 0.7 copy-done.28
  105.5 3.9 %all-to-all-start.2 = ((bf16[8,2,128,512]{3,2,1,0:T(8,128)(2,1)}), bf16[8,2,128,512]{3,2,1,0:T(8,128)(2,1)S(1)}, u32[]{:S(2)}, u32[]{:S(2)}) async-start(bf16[8,2,128,512]{3,2,1,0:T(8,128)(2,1)} %copy-done.3), calls=%async_computation.2 | async-start | bytes 4194304 | tf_op jit(solution)/shard_map/all_to_all | solution.py:523
  109.4 1.0 collective-permute-start.19
  110.4 1.1 collective-permute-start.20
  111.5 0.6 hidden_low.1
  112.1 1.0 collective-permute-start.15
  113.5 1.0 collective-permute-start.17
  114.5 1.1 collective-permute-start.18
  115.6 25.6 %collective-permute-done.15.gradients_pair = bf16[8,128,128]{2,1,0:T(8,128)(2,1)S(1)} collective-permute-done((bf16[8,128,128]{2,1,0:T(8,128)(2,1)S(1)}, bf16[8,128,128]{2,1,0:T(8,128)(2,1)S(1)}, u32[]{:S(2)}, u32[]{:S(2)}) %collective-permute-start.15) | collective-permute-done | bytes 262176 | tf_op jit(solution)/shard_map/ppermute | solution.py:530
  141.2 5.6 %collective-permute-done.17.hiddens_pair = bf16[8,128,128]{2,1,0:T(8,128)(2,1)S(1)} collective-permute-done((bf16[8,128,128]{2,1,0:T(8,128)(2,1)S(1)}, bf16[8,128,128]{2,1,0:T(8,128)(2,1)S(1)}, u32[]{:S(2)}, u32[]{:S(2)}) %collective-permute-start.17) | collective-permute-done | bytes 262176 | tf_op jit(solution)/shard_map/ppermute | solution.py:530
  146.8 3.6 %up_gradients.1 = bf16[64,64,128]{2,1,0:T(8,128)(2,1)} custom-call(s32[16]{0:T(128)S(1)} %copy-done.24, s32[1]{0:T(128)} %bitcast.place, s32[64]{0:T(128)S(1)} %copy-done.25, bf16[8,128,128]{2,1,0:T(8,128)(2,1)S(1)} %get-tuple-element.56.gradients, bf16[8,128,128]{2,1,0:T(8,128)(2,1)S(1)} %collective-permute-done.15.gradients_pair, ...), custom_call_target="tpu_custom_call" | custom-call | tf_op jit(solution)/shard_map/up_gradients/pallas_call | solution.py:403
  150.4 1.6 collective-permute-done.18.backs_pair
  152.0 5.5 %down_gradients.1 = bf16[64,128,512]{2,1,0:T(8,128)(2,1)} custom-call(s32[16]{0:T(128)S(1)} %copy-done.24, s32[1]{0:T(128)} %bitcast.place, bf16[8,128,128]{2,1,0:T(8,128)(2,1)S(1)} %constant_dynamic-update-slice_fusion.backs, bf16[8,128,128]{2,1,0:T(8,128)(2,1)S(1)} %collective-permute-done.18.backs_pair, bf16[8,128,512]{2,1,0:T(8,128)(2,1)S(1)} %copy-done.9, ...), custom_call_target="tpu_custom_call" | custom-call | tf_op jit(solution)/shard_map/down_gradients/pallas_call | solution.py:403
  157.5 1.5 join_columns.1
  (80 shorter events, 1.4 us)
Async XLA Ops:
  0.6 16.3 %collective-permute-start = (bf16[1,128,1024]{2,1,0:T(8,128)(2,1)}, bf16[1,128,1024]{2,1,0:T(8,128)(2,1)S(1)}, u32[]{:S(2)}, u32[]{:S(2)}) collective-permute-start(bf16[1,128,1024]{2,1,0:T(8,128)(2,1)} %bitcast.3), channel_id=1, source_target_pairs={{0,8},{1,9},{2,10},{3,11},{4,12},{5,13},{6,14},{7,15},{8,0},{9,1},... | collective-permute-start | bytes 786440 | tf_op jit(solution)/shard_map/ppermute | solution.py:530
  4.7 12.7 %collective-permute-start.1 = (bf16[1,128,1024]{2,1,0:T(8,128)(2,1)}, bf16[1,128,1024]{2,1,0:T(8,128)(2,1)S(1)}, u32[]{:S(2)}, u32[]{:S(2)}) collective-permute-start(bf16[1,128,1024]{2,1,0:T(8,128)(2,1)} %bitcast.4), channel_id=1, source_target_pairs={{0,4},{1,5},{2,6},{3,7},{4,0},{5,1},{6,2},{7,3},{8,12},{9,13},{10,... | collective-permute-start | bytes 786440 | tf_op jit(solution)/shard_map/ppermute | solution.py:530
  6.3 1.2 copy-start.5
  10.0 13.6 %all-to-all-start = ((bf16[16,64,128]{2,1,0:T(8,128)(2,1)}), bf16[16,64,128]{2,1,0:T(8,128)(2,1)S(1)}, u32[]{:S(2)}, u32[]{:S(2)}) async-start(bf16[16,64,128]{2,1,0:T(8,128)(2,1)} %gather_up.1), calls=%async_computation | async-start | bytes 524288 | tf_op jit(solution)/shard_map/all_to_all | solution.py:517
  13.5 7.4 %collective-permute-start.2 = (bf16[1,128,1024]{2,1,0:T(8,128)(2,1)}, bf16[1,128,1024]{2,1,0:T(8,128)(2,1)S(1)}, u32[]{:S(2)}, u32[]{:S(2)}) collective-permute-start(bf16[1,128,1024]{2,1,0:T(8,128)(2,1)} %bitcast.5), channel_id=1, source_target_pairs={{0,1},{1,0},{2,3},{3,2},{4,5},{5,4},{6,7},{7,6},{8,9},{9,8},{10,11... | collective-permute-start | bytes 786440 | tf_op jit(solution)/shard_map/ppermute | solution.py:530
  17.0 4.0 %copy-start.10 = (bf16[1,128,1024]{2,1,0:T(8,128)(2,1)}, bf16[1,128,1024]{2,1,0:T(8,128)(2,1)S(1)}, u32[]{:S(2)}) copy-start(bf16[1,128,1024]{2,1,0:T(8,128)(2,1)S(1)} %collective-permute-done.refs_1_) | copy-start | bytes 786436
  17.0 7.2 %collective-permute-start.3 = (bf16[1,128,1024]{2,1,0:T(8,128)(2,1)S(1)}, bf16[1,128,1024]{2,1,0:T(8,128)(2,1)S(1)}, u32[]{:S(2)}, u32[]{:S(2)}) collective-permute-start(bf16[1,128,1024]{2,1,0:T(8,128)(2,1)S(1)} %collective-permute-done.refs_1_), channel_id=1, source_target_pairs={{0,1},{1,0},{2,3},{3,2},{4,5},{5,4},{6,7},{7,6},{8,9},{9,8},{10,11... | collective-permute-start | bytes 786440 | tf_op jit(solution)/shard_map/ppermute | solution.py:530
  17.4 3.5 %copy-start.13 = (bf16[1,128,1024]{2,1,0:T(8,128)(2,1)}, bf16[1,128,1024]{2,1,0:T(8,128)(2,1)S(1)}, u32[]{:S(2)}) copy-start(bf16[1,128,1024]{2,1,0:T(8,128)(2,1)S(1)} %collective-permute-done.1.refs_2_) | copy-start | bytes 786436
  17.4 6.8 %collective-permute-start.4 = (bf16[1,128,1024]{2,1,0:T(8,128)(2,1)S(1)}, bf16[1,128,1024]{2,1,0:T(8,128)(2,1)S(1)}, u32[]{:S(2)}, u32[]{:S(2)}) collective-permute-start(bf16[1,128,1024]{2,1,0:T(8,128)(2,1)S(1)} %collective-permute-done.1.refs_2_), channel_id=1, source_target_pairs={{0,1},{1,0},{2,3},{3,2},{4,5},{5,4},{6,7},{7,6},{8,9},{9,8},{10,11... | collective-permute-start | bytes 786440 | tf_op jit(solution)/shard_map/ppermute | solution.py:530
  17.5 1.6 %copy-start.2 = (bf16[128,8192]{1,0:T(8,128)(2,1)S(1)}, bf16[128,8192]{1,0:T(8,128)(2,1)}, u32[]{:S(2)}) copy-start(bf16[128,8192]{1,0:T(8,128)(2,1)} %tokens.1) | copy-start | bytes 6291460
  24.2 0.8 copy-start.19
  24.2 5.1 %copy-start.1 = (bf16[1024,512]{1,0:T(8,128)(2,1)S(1)}, bf16[1024,512]{1,0:T(8,128)(2,1)}, u32[]{:S(2)}) copy-start(bf16[1024,512]{1,0:T(8,128)(2,1)} %refs_16_.1) | copy-start | bytes 3145732
  24.3 5.1 %copy-start.24 = (s32[16]{0:T(128)S(1)}, s32[16]{0:T(128)}, u32[]{:S(2)}) copy-start(s32[16]{0:T(128)} %adapters.8) | copy-start | bytes 196
  25.0 56.5 %all-to-all-start.1 = ((bf16[8,2,128,512]{3,2,1,0:T(8,128)(2,1)}), bf16[8,2,128,512]{3,2,1,0:T(8,128)(2,1)}, u32[]{:S(2)}, u32[]{:S(2)}) async-start(bf16[8,2,128,512]{3,2,1,0:T(8,128)(2,1)} %pack_tokens.1), calls=%async_computation.1 | async-start | bytes 4194304 | tf_op jit(solution)/shard_map/all_to_all | solution.py:523
  29.4 2.9 %copy-start.11 = (bf16[1,128,1024]{2,1,0:T(8,128)(2,1)S(1)}, bf16[1,128,1024]{2,1,0:T(8,128)(2,1)}, u32[]{:S(2)}) copy-start(bf16[1,128,1024]{2,1,0:T(8,128)(2,1)} %copy-done.10) | copy-start | bytes 786436
  29.4 4.9 %copy-start.4 = (bf16[128,1024]{1,0:T(8,128)(2,1)S(1)}, bf16[128,1024]{1,0:T(8,128)(2,1)}, u32[]{:S(2)}) copy-start(bf16[128,1024]{1,0:T(8,128)(2,1)} %gradient.1) | copy-start | bytes 786436
  29.4 4.9 %copy-start.7 = (bf16[16,64,128]{2,1,0:T(8,128)(2,1)S(1)}, bf16[16,64,128]{2,1,0:T(8,128)(2,1)}, u32[]{:S(2)}) copy-start(bf16[16,64,128]{2,1,0:T(8,128)(2,1)} %copy-done.6) | copy-start | bytes 786436
  29.4 4.8 %copy-start.25 = (s32[64]{0:T(128)S(1)}, s32[64]{0:T(128)}, u32[]{:S(2)}) copy-start(s32[64]{0:T(128)} %ranks.5) | copy-start | bytes 772
  31.4 50.2 %collective-permute-start.9 = (bf16[2048,512]{1,0:T(8,128)(2,1)S(1)}, bf16[2048,512]{1,0:T(8,128)(2,1)S(1)}, u32[]{:S(2)}, u32[]{:S(2)}) collective-permute-start(bf16[2048,512]{1,0:T(8,128)(2,1)S(1)} %for_pair.1), channel_id=1, source_target_pairs={{0,2},{1,3},{2,0},{3,1},{4,6},{5,7},{6,4},{7,5},{8,10},{9,11},{10,... | collective-permute-start | bytes 6291464 | tf_op jit(solution)/shard_map/ppermute | solution.py:530
  32.3 48.6 %collective-permute-start.8 = (bf16[1,128,1024]{2,1,0:T(8,128)(2,1)S(1)}, bf16[1,128,1024]{2,1,0:T(8,128)(2,1)S(1)}, u32[]{:S(2)}, u32[]{:S(2)}) collective-permute-start(bf16[1,128,1024]{2,1,0:T(8,128)(2,1)S(1)} %copy-done.11), channel_id=1, source_target_pairs={{0,4},{1,5},{2,6},{3,7},{4,0},{5,1},{6,2},{7,3},{8,12},{9,13},{10,... | collective-permute-start | bytes 786440 | tf_op jit(solution)/shard_map/ppermute | solution.py:530
  35.0 45.8 %collective-permute-start.5 = (bf16[1,128,128]{2,1,0:T(8,128)(2,1)S(1)}, bf16[1,128,128]{2,1,0:T(8,128)(2,1)S(1)}, u32[]{:S(2)}, u32[]{:S(2)}) collective-permute-start(bf16[1,128,128]{2,1,0:T(8,128)(2,1)S(1)} %back_low.1), channel_id=1, source_target_pairs={{0,8},{1,9},{2,10},{3,11},{4,12},{5,13},{6,14},{7,15},{8,0},{9,1},... | collective-permute-start | bytes 98312 | tf_op jit(solution)/shard_map/ppermute | solution.py:530
  37.5 43.4 %collective-permute-start.6 = (bf16[1,128,128]{2,1,0:T(8,128)(2,1)S(1)}, bf16[1,128,128]{2,1,0:T(8,128)(2,1)S(1)}, u32[]{:S(2)}, u32[]{:S(2)}) collective-permute-start(bf16[1,128,128]{2,1,0:T(8,128)(2,1)S(1)} %back_low.1), channel_id=1, source_target_pairs={{0,4},{1,5},{2,6},{3,7},{4,0},{5,1},{6,2},{7,3},{8,12},{9,13},{10,... | collective-permute-start | bytes 98312 | tf_op jit(solution)/shard_map/ppermute | solution.py:530
  38.0 42.8 %collective-permute-start.7 = (bf16[1,128,128]{2,1,0:T(8,128)(2,1)S(1)}, bf16[1,128,128]{2,1,0:T(8,128)(2,1)S(1)}, u32[]{:S(2)}, u32[]{:S(2)}) collective-permute-start(bf16[1,128,128]{2,1,0:T(8,128)(2,1)S(1)} %back_low.1), channel_id=1, source_target_pairs={{0,12},{1,13},{2,14},{3,15},{4,8},{5,9},{6,10},{7,11},{8,4},{9,5},... | collective-permute-start | bytes 98312 | tf_op jit(solution)/shard_map/ppermute | solution.py:530
  81.5 3.5 %copy-start = (bf16[2048,512]{1,0:T(8,128)(2,1)}, bf16[2048,512]{1,0:T(8,128)(2,1)S(1)}, u32[]{:S(2)}) copy-start(bf16[2048,512]{1,0:T(8,128)(2,1)S(1)} %collective-permute-done.9.pair) | copy-start | bytes 6291460
  81.6 8.0 %copy-start.22 = (bf16[1,128,1024]{2,1,0:T(8,128)(2,1)S(1)}, bf16[1,128,1024]{2,1,0:T(8,128)(2,1)}, u32[]{:S(2)}) copy-start(bf16[1,128,1024]{2,1,0:T(8,128)(2,1)} %copy-done.21) | copy-start | bytes 786436
  85.1 1.0 copy-start.8
  86.0 0.8 copy-start.26
  86.9 10.9 %copy-start.27 = (bf16[4,128,512]{2,1,0:T(8,128)(2,1)}, bf16[4,128,512]{2,1,0:T(8,128)(2,1)S(1)}, u32[]{:S(2)}) copy-start(bf16[4,128,512]{2,1,0:T(8,128)(2,1)S(1)} %get-tuple-element.69) | copy-start | bytes 1572868
  86.9 10.9 %copy-start.12 = (bf16[1,128,1024]{2,1,0:T(8,128)(2,1)S(1)}, bf16[1,128,1024]{2,1,0:T(8,128)(2,1)}, u32[]{:S(2)}) copy-start(bf16[1,128,1024]{2,1,0:T(8,128)(2,1)} %copy-done.10) | copy-start | bytes 786436
  86.9 10.9 %copy-start.14 = (bf16[1,128,1024]{2,1,0:T(8,128)(2,1)S(1)}, bf16[1,128,1024]{2,1,0:T(8,128)(2,1)}, u32[]{:S(2)}) copy-start(bf16[1,128,1024]{2,1,0:T(8,128)(2,1)} %copy-done.13) | copy-start | bytes 786436
  86.9 10.9 %copy-start.16 = (bf16[1,128,1024]{2,1,0:T(8,128)(2,1)S(1)}, bf16[1,128,1024]{2,1,0:T(8,128)(2,1)}, u32[]{:S(2)}) copy-start(bf16[1,128,1024]{2,1,0:T(8,128)(2,1)} %copy-done.15) | copy-start | bytes 786436
  86.9 11.0 %copy-start.18 = (bf16[1,128,1024]{2,1,0:T(8,128)(2,1)S(1)}, bf16[1,128,1024]{2,1,0:T(8,128)(2,1)}, u32[]{:S(2)}) copy-start(bf16[1,128,1024]{2,1,0:T(8,128)(2,1)} %copy-done.17) | copy-start | bytes 786436
  86.9 11.0 %copy-start.20 = (bf16[1,128,1024]{2,1,0:T(8,128)(2,1)S(1)}, bf16[1,128,1024]{2,1,0:T(8,128)(2,1)}, u32[]{:S(2)}) copy-start(bf16[1,128,1024]{2,1,0:T(8,128)(2,1)} %copy-done.19) | copy-start | bytes 786436
  86.9 1.6 %collective-permute-start.12 = (f32[4,128,128]{2,1,0:T(8,128)S(1)}, f32[4,128,128]{2,1,0:T(8,128)S(1)}, u32[]{:S(2)}, u32[]{:S(2)}) collective-permute-start(f32[4,128,128]{2,1,0:T(8,128)S(1)} %slice.3), channel_id=1, source_target_pairs={{0,1},{1,0},{2,3},{3,2},{4,5},{5,4},{6,7},{7,6},{8,9},{9,8},{10,11... | collective-permute-start | bytes 786440 | tf_op jit(solution)/shard_map/ppermute | solution.py:530
  88.5 8.4 %collective-permute-start.13 = (f32[4,128,128]{2,1,0:T(8,128)S(1)}, f32[4,128,128]{2,1,0:T(8,128)S(1)}, u32[]{:S(2)}, u32[]{:S(2)}) collective-permute-start(f32[4,128,128]{2,1,0:T(8,128)S(1)} %slot_sums.2.total), channel_id=1, source_target_pairs={{0,4},{1,5},{2,6},{3,7},{4,0},{5,1},{6,2},{7,3},{8,12},{9,13},{10,... | collective-permute-start | bytes 786440 | tf_op jit(solution)/shard_map/ppermute | solution.py:530
  89.5 8.2 %collective-permute-start.10 = (bf16[4,128,128]{2,1,0:T(8,128)(2,1)S(1)}, bf16[4,128,128]{2,1,0:T(8,128)(2,1)S(1)}, u32[]{:S(2)}, u32[]{:S(2)}) collective-permute-start(bf16[4,128,128]{2,1,0:T(8,128)(2,1)S(1)} %pad_maximum_fusion.1), channel_id=1, source_target_pairs={{0,1},{1,0},{2,3},{3,2},{4,5},{5,4},{6,7},{7,6},{8,9},{9,8},{10,11... | collective-permute-start | bytes 393224 | tf_op jit(solution)/shard_map/ppermute | solution.py:530
  89.5 8.3 %collective-permute-start.11 = (bf16[1,128,1024]{2,1,0:T(8,128)(2,1)S(1)}, bf16[1,128,1024]{2,1,0:T(8,128)(2,1)S(1)}, u32[]{:S(2)}, u32[]{:S(2)}) collective-permute-start(bf16[1,128,1024]{2,1,0:T(8,128)(2,1)S(1)} %copy-done.22), channel_id=1, source_target_pairs={{0,1},{1,0},{2,3},{3,2},{4,5},{5,4},{6,7},{7,6},{8,9},{9,8},{10,11... | collective-permute-start | bytes 786440 | tf_op jit(solution)/shard_map/ppermute | solution.py:530
  97.0 8.5 %collective-permute-start.14 = (bf16[4,128,128]{2,1,0:T(8,128)(2,1)S(1)}, bf16[4,128,128]{2,1,0:T(8,128)(2,1)S(1)}, u32[]{:S(2)}, u32[]{:S(2)}) collective-permute-start(bf16[4,128,128]{2,1,0:T(8,128)(2,1)S(1)} %get-tuple-element.59), channel_id=1, source_target_pairs={{0,8},{1,9},{2,10},{3,11},{4,12},{5,13},{6,14},{7,15},{8,0},{9,1},... | collective-permute-start | bytes 393224 | tf_op jit(solution)/shard_map/ppermute | solution.py:530
  103.3 1.3 copy-start.3
  105.5 6.6 %copy-start.29 = (bf16[8,128,128]{2,1,0:T(8,128)(2,1)S(1)}, bf16[8,128,128]{2,1,0:T(8,128)(2,1)}, u32[]{:S(2)}) copy-start(bf16[8,128,128]{2,1,0:T(8,128)(2,1)} %copy-done.28) | copy-start | bytes 786436
  105.5 52.0 %all-to-all-start.2 = ((bf16[8,2,128,512]{3,2,1,0:T(8,128)(2,1)}), bf16[8,2,128,512]{3,2,1,0:T(8,128)(2,1)S(1)}, u32[]{:S(2)}, u32[]{:S(2)}) async-start(bf16[8,2,128,512]{3,2,1,0:T(8,128)(2,1)} %copy-done.3), calls=%async_computation.2 | async-start | bytes 4194304 | tf_op jit(solution)/shard_map/all_to_all | solution.py:523
  109.4 42.6 %copy-start.9 = (bf16[8,128,512]{2,1,0:T(8,128)(2,1)S(1)}, bf16[8,128,512]{2,1,0:T(8,128)(2,1)}, u32[]{:S(2)}) copy-start(bf16[8,128,512]{2,1,0:T(8,128)(2,1)} %copy-done.8) | copy-start | bytes 3145732
  109.4 42.6 %collective-permute-start.19 = (bf16[4,128,512]{2,1,0:T(8,128)(2,1)}, bf16[4,128,512]{2,1,0:T(8,128)(2,1)S(1)}, u32[]{:S(2)}, u32[]{:S(2)}) collective-permute-start(bf16[4,128,512]{2,1,0:T(8,128)(2,1)} %copy-done.27), channel_id=1, source_target_pairs={{0,2},{1,3},{2,0},{3,1},{4,6},{5,7},{6,4},{7,5},{8,10},{9,11},{10,... | collective-permute-start | bytes 1572872 | tf_op jit(solution)/shard_map/ppermute | solution.py:530
  110.4 41.7 %collective-permute-start.20 = (bf16[4,128,512]{2,1,0:T(8,128)(2,1)}, bf16[4,128,512]{2,1,0:T(8,128)(2,1)S(1)}, u32[]{:S(2)}, u32[]{:S(2)}) collective-permute-start(bf16[4,128,512]{2,1,0:T(8,128)(2,1)} %copy-done.26), channel_id=1, source_target_pairs={{0,2},{1,3},{2,0},{3,1},{4,6},{5,7},{6,4},{7,5},{8,10},{9,11},{10,... | collective-permute-start | bytes 1572872 | tf_op jit(solution)/shard_map/ppermute | solution.py:530
  112.0 1.4 collective-permute-start.16
  112.1 29.1 %collective-permute-start.15 = (bf16[8,128,128]{2,1,0:T(8,128)(2,1)S(1)}, bf16[8,128,128]{2,1,0:T(8,128)(2,1)S(1)}, u32[]{:S(2)}, u32[]{:S(2)}) collective-permute-start(bf16[8,128,128]{2,1,0:T(8,128)(2,1)S(1)} %copy-done.29), channel_id=1, source_target_pairs={{0,2},{1,3},{2,0},{3,1},{4,6},{5,7},{6,4},{7,5},{8,10},{9,11},{10,... | collective-permute-start | bytes 786440 | tf_op jit(solution)/shard_map/ppermute | solution.py:530
  113.5 33.4 %collective-permute-start.17 = (bf16[8,128,128]{2,1,0:T(8,128)(2,1)S(1)}, bf16[8,128,128]{2,1,0:T(8,128)(2,1)S(1)}, u32[]{:S(2)}, u32[]{:S(2)}) collective-permute-start(bf16[8,128,128]{2,1,0:T(8,128)(2,1)S(1)} %pad_maximum_fusion.hiddens), channel_id=1, source_target_pairs={{0,2},{1,3},{2,0},{3,1},{4,6},{5,7},{6,4},{7,5},{8,10},{9,11},{10,... | collective-permute-start | bytes 786440 | tf_op jit(solution)/shard_map/ppermute | solution.py:530
  114.5 37.5 %collective-permute-start.18 = (bf16[8,128,128]{2,1,0:T(8,128)(2,1)S(1)}, bf16[8,128,128]{2,1,0:T(8,128)(2,1)S(1)}, u32[]{:S(2)}, u32[]{:S(2)}) collective-permute-start(bf16[8,128,128]{2,1,0:T(8,128)(2,1)S(1)} %constant_dynamic-update-slice_fusion.backs), channel_id=1, source_target_pairs={{0,2},{1,3},{2,0},{3,1},{4,6},{5,7},{6,4},{7,5},{8,10},{9,11},{10,... | collective-permute-start | bytes 786440 | tf_op jit(solution)/shard_map/ppermute | solution.py:530
  (6 other events, 4.2 us)

commit v17 on v16

--- a/solution.py
+++ b/solution.py
@@ -192,17 +192,13 @@
 
 def input_kernel(adapters, place, backs, pair, *refs):
     members, rows, _ = backs.shape
-    gradients = [ref.at[0] for ref in refs[:members]]
-    downs = refs[members : 2 * members]
-    weight = refs[2 * members]
-    out, *columns = refs[-3:]
+    gradients, downs = refs[:members], refs[members : 2 * members]
+    weight, out = refs[2 * members :]
     extent = downs[0].shape[1]
-    lanes = columns[0].shape[2]
-    value_width = gradients[0].shape[1] // (2 * members)
     some = min(4, members)
     for first in range(0, members, some):
         slots = range(first, first + some)
-        lines = jnp.concatenate([gradients[slot][...] for slot in slots], axis=0)
+        lines = jnp.concatenate([gradients[slot][0] for slot in slots], axis=0)
         for half in range(2):
             right = weight[...] if half == 0 else pair[members * extent :]
             frozen = jnp.dot(lines, right, preferred_element_type=jnp.float32)
@@ -212,28 +208,51 @@
                 low = jnp.dot(backs[slot], down, preferred_element_type=jnp.float32)
                 at = (slot - first) * rows
                 out[index, half] = (frozen[at : at + rows] + low).astype(jnp.bfloat16)
-    for side in range(2):
-        column = (place[0] ^ (side * pair_bit)) * value_width // lanes * lanes
-        for slot in range(members):
-            columns[side][slot] = gradients[slot][:, pl.ds(pl.multiple_of(column, lanes), lanes)]
-
-
-def input_slices(adapters, place, gradients, backs, weight, pair, down_maps):
-    members, rows, _ = backs.shape
-    width = weight.shape[1]
-    lanes = max(128, gradients[0].shape[2] // (2 * members))
-    shape = jax.ShapeDtypeStruct((members, 2, rows, width), jnp.bfloat16)
-    columns = jax.ShapeDtypeStruct((members, rows, lanes), jnp.bfloat16)
+
+
+def input_slices(adapters, place, gradients, backs, weight, pair, down_maps, part, parts):
+    members, rows, extent = backs.shape
+    depth, width = weight.shape
+    rows //= parts
     return call(
         input_kernel,
         "input_slices",
         (adapters, place),
         [backs, pair] + list(gradients) + [down_maps] * members + [weight],
-        [whole(backs.shape), whole(pair.shape)]
-        + [whole(gradient.shape) for gradient in gradients]
+        [pl.BlockSpec((members, rows, extent), lambda *_: (0, part, 0)), whole(pair.shape)]
+        + [pl.BlockSpec((1, rows, depth), lambda *_: (0, part, 0))] * members
         + [picked(down_maps, line_offset(slot, members)) for slot in range(members)]
         + [whole(weight.shape)],
-        [shape, columns, columns],
+        [jax.ShapeDtypeStruct((members, 2, rows, width), jnp.bfloat16)],
+    )[0]
+
+
+def columns_kernel(place, *refs):
+    *gradients, own, pair = refs
+    for slot in range(own.shape[0]):
+        own[slot] = gradients[2 * slot][0]
+        pair[slot] = gradients[2 * slot + 1][0]
+
+
+def gradient_columns(place, gradients, value_width):
+    members = len(gradients)
+    rows = gradients[0].shape[1]
+    lanes = max(128, value_width)
+
+    def spec(side):
+        return pl.BlockSpec(
+            (1, rows, lanes),
+            lambda i, place: (0, 0, (place[0] ^ (side * pair_bit)) * value_width // lanes),
+        )
+
+    shape = jax.ShapeDtypeStruct((members, rows, lanes), gradients[0].dtype)
+    return call(
+        columns_kernel,
+        "gradient_columns",
+        (place,),
+        [gradient for gradient in gradients for _ in range(2)],
+        [spec(0), spec(1)] * members,
+        [shape, shape],
     )
 
 
@@ -315,37 +334,41 @@
     )[0]
 
 
-def join_kernel(place, source, out, sems):
-    members, _, _, width = source.shape
+def join_kernel(place, source, *refs, part):
+    out, sems = refs[-2:]
+    members, _, rows, width = source.shape
     copies = []
     for index in range(members):
         for half in range(2):
             column = side_place(index, side_of(place[0]) ^ half, members) * width
+            columns = pl.ds(pl.multiple_of(column, width), width)
             copies.append(
                 pltpu.make_async_copy(
                     source.at[index, half],
-                    out.at[:, pl.ds(pl.multiple_of(column, width), width)],
+                    out.at[pl.ds(part * rows, rows), columns],
                     sems.at[2 * index + half],
                 )
             )
     run(copies)
 
 
-def join_columns(place, source):
+def join_columns(place, source, part, parts, before=()):
     members, _, rows, width = source.shape
+    shape = jax.ShapeDtypeStruct((parts * rows, 2 * members * width), source.dtype)
     return pl.pallas_call(
-        join_kernel,
-        out_shape=jax.ShapeDtypeStruct((rows, 2 * members * width), source.dtype),
+        functools.partial(join_kernel, part=part),
+        out_shape=shape,
         grid_spec=pltpu.PrefetchScalarGridSpec(
             num_scalar_prefetch=1,
             grid=(1,),
-            in_specs=[whole(source.shape)],
+            in_specs=[whole(source.shape)] + [pl.BlockSpec(memory_space=pl.ANY)] * len(before),
             out_specs=pl.BlockSpec(memory_space=pl.ANY),
             scratch_shapes=[pltpu.SemaphoreType.DMA((2 * members,))],
         ),
+        input_output_aliases={2: 0} if before else {},
         compiler_params=params(),
         name="join_columns",
-    )(place, source)
+    )(place, source, *before)
 
 
 def list_members(adapters, place, members, head, following):
@@ -575,47 +598,55 @@
     backs = [backs] + [swap(backs, offset) for offset in offsets[1:lines]]
     arrived, backs, gradients, pair = barrier((arrived, backs, gradients, pair))
 
-    parts, tokens_own, *tokens_pair = hidden_parts(
-        adapters, place, down_maps, pair, arrived
-    )
     for slot in range(lines):
         if slot not in across:
             across[slot] = swap(gradients[slot], 1)
+    gradients = gradients + [across[slot] for slot in range(lines)]
     backs = gather_step(jnp.concatenate(backs, axis=0), members)
-    slices, columns, columns_pair = input_slices(
-        adapters,
-        place,
-        gradients + [across[slot] for slot in range(lines)],
-        backs,
-        value_weight,
-        pair,
-        down_maps,
-    )
+    slices = input_slices(
+        adapters, place, gradients, backs, value_weight, pair, down_maps, 0, 2
+    )
+    slices, arrived = barrier((slices, arrived))
+    first = exchange_side(slices)
+
+    parts, tokens_own, *tokens_pair = hidden_parts(
+        adapters, place, down_maps, pair, arrived
+    )
+    columns, columns_other = gradient_columns(place, gradients, depth // devices)
+    columns_other = swap(columns_other, pair_bit)
+    backs_pair = swap(backs, pair_bit)
+    tokens_other = [swap(tokens_pair[0], pair_bit)]
     total, received, flip = parts, swap(parts[lines:], 1), 0
     for step in reversed(range(steps - 1)):
         kinds = [jnp.float32] if step else [jnp.float32, jnp.bfloat16]
         sums = slot_sums(total, received, flip, kinds)
         total, flip = sums[0], 1 << step
         received = swap(sums[-1], offsets[flip])
-    received, slices, columns_pair, backs, tokens_pair = barrier(
-        (received, slices, columns_pair, backs, tokens_pair)
-    )
-
-    result = exchange_side(slices)
+        if step == 1:
+            received, backs, columns_other, backs_pair, tokens_other, tokens_pair = barrier(
+                (received, backs, columns_other, backs_pair, tokens_other, tokens_pair)
+            )
+            slices = input_slices(
+                adapters, place, gradients, backs, value_weight, pair, down_maps, 1, 2
+            )
+    second = exchange_side(slices)
+
     hiddens = hidden_rows(adapters, place, ranks, total, received, flip, members)
     hiddens = gather_step(hiddens, members)
-    columns_other = swap(columns_pair, pair_bit)
-    backs_pair = swap(backs, pair_bit)
-    tokens_other = [swap(half, pair_bit) for half in tokens_pair]
     hiddens_pair = swap(hiddens, pair_bit)
+    tokens_other.append(swap(tokens_pair[1], pair_bit))
     up_gradient = up_gradients(
         adapters, place, ranks, columns, columns_other, hiddens, hiddens_pair, depth // devices
     )
     down_gradient = down_gradients(
         adapters, place, backs, backs_pair, tokens_own, tokens_other, num_adapters
     )
-    up_gradient, down_gradient, result = barrier((up_gradient, down_gradient, result))
-    return (join_columns(place, result), down_gradient, up_gradient)
+    joined = join_columns(place, first, 0, 2)
+    up_gradient, down_gradient, joined, second = barrier(
+        (up_gradient, down_gradient, joined, second)
+    )
+    input_grad = join_columns(place, second, 1, 2, (joined,))
+    return (input_grad, down_gradient, up_gradient)
 
 
 def solution(mesh):

time: 160 us -> 192 us (1.20)
  waiting for transfers between devices: 88.5 us -> 98.1 us
  starting transfers between devices: 32.7 us -> 41.4 us
  local copies, waits for them, and re-layouts: 10.3 us -> 18.9 us
  Pallas kernels: 26.4 us -> 31.9 us
    ppermute x21, waiting for transfers between devices: 86.7 us -> 95.6 us  [swap(): return lax.ppermute(array, 'dp', [(i, i ^ flip) for i in range(devices)])]
    unnamed x64 -> x94, local copies, waits for them, and re-layouts: 10.3 us -> 18.9 us
    all_to_all x2 -> x3, starting transfers between devices: 8.23 us -> 13.9 us  [exchange_side(): lax.all_to_all(pieces, 'dp', split_axis=0, concat_axis=0, axis_index_grou...]
    pallas_call x6 -> x8, Pallas kernels: 10.4 us -> 13.9 us  [call(): pl.pallas_call(kernel, out_shape=out_shapes, grid_spec=pltpu.PrefetchScal...]
    ppermute x21, starting transfers between devices: 20.9 us -> 24 us  [swap(): return lax.ppermute(array, 'dp', [(i, i ^ flip) for i in range(devices)])]
    pallas_call x1 -> x2, Pallas kernels: 1.45 us -> 3.42 us  [join_columns(): pl.pallas_call(functools.partial(join_kernel, part=part), out_shape=shape...]
  transfers between devices with their start and end apart: 24 -> 25, of which waited for: 11 -> 11; matrix products, arithmetic and copies ran while one was open for 0% -> 0% of each run, Pallas kernels for 13% -> 14%
where the time goes in v17:
time: 192 us
  waiting for transfers between devices  98.1 us (51%)
  starting transfers between devices  41.4 us (22%)
  Pallas kernels  31.9 us (17%)
  local copies, waits for them, and re-layouts  18.9 us (10%)
    ppermute x21, waiting for transfers between devices, swap(): return lax.ppermute(array, 'dp', [(i, i ^ flip) for i in range(devices)])  95.6 us
    ppermute x21, starting transfers between devices, swap(): return lax.ppermute(array, 'dp', [(i, i ^ flip) for i in range(devices)])  24 us
    unnamed x94, local copies, waits for them, and re-layouts  18.9 us
    pallas_call x8, Pallas kernels, call(): pl.pallas_call(kernel, out_shape=out_shapes, grid_spec=pltpu.PrefetchScal...  13.9 us
    all_to_all x3, starting transfers between devices, exchange_side(): lax.all_to_all(pieces, 'dp', split_axis=0, concat_axis=0, axis_index_grou...  13.9 us
    pallas_call x2, Pallas kernels, sums_call(): pl.pallas_call(kernel, out_shape=jax.ShapeDtypeStruct((num_adapters,) + p...  9.08 us
    pallas_call x3, Pallas kernels, copy_call(): pl.pallas_call(kernel, out_shape=out_shapes, grid_spec=pltpu.PrefetchScal...  5.5 us
  transfers between devices with their start and end apart: 25, of which 11 were waited for; matrix products, arithmetic and copies ran while one was open for 0% of the time, Pallas kernels for 14%

profile of v17, /device:TPU:0, one launch (start us, length us, event | category | flops | bytes accessed | tf_op | source)
XLA Modules:
  0.0 191.5 jit_solution(13529310447822069690)
XLA Ops:
  0.6 4.1 %collective-permute-start = (bf16[1,128,1024]{2,1,0:T(8,128)(2,1)}, bf16[1,128,1024]{2,1,0:T(8,128)(2,1)S(1)}, u32[]{:S(2)}, u32[]{:S(2)}) collective-permute-start(bf16[1,128,1024]{2,1,0:T(8,128)(2,1)} %bitcast.3), channel_id=1, source_target_pairs={{0,8},{1,9},{2,10},{3,11},{4,12},{5,13},{6,14},{7,15},{8,0},{9,1},... | collective-permute-start | bytes 786440 | tf_op jit(solution)/shard_map/ppermute | solution.py:553
  4.7 1.6 collective-permute-start.1
  6.3 1.2 copy-done.30
  8.2 1.8 gather_up.1
  10.0 3.5 %all-to-all-start = ((bf16[16,64,128]{2,1,0:T(8,128)(2,1)}), bf16[16,64,128]{2,1,0:T(8,128)(2,1)S(1)}, u32[]{:S(2)}, u32[]{:S(2)}) async-start(bf16[16,64,128]{2,1,0:T(8,128)(2,1)} %gather_up.1), calls=%async_computation | async-start | bytes 524288 | tf_op jit(solution)/shard_map/all_to_all | solution.py:540
  13.8 3.2 %collective-permute-done.refs_2_.refs_3_.refs_1_ = bf16[1,128,1024]{2,1,0:T(8,128)(2,1)S(1)} collective-permute-done((bf16[1,128,1024]{2,1,0:T(8,128)(2,1)}, bf16[1,128,1024]{2,1,0:T(8,128)(2,1)S(1)}, u32[]{:S(2)}, u32[]{:S(2)}) %collective-permute-start) | collective-permute-done | bytes 262176 | tf_op jit(solution)/shard_map/ppermute | solution.py:553
  17.5 1.6 copy-done.29
  19.1 1.8 pack_tokens.1
  21.0 2.5 %all-to-all-done = bf16[16,64,128]{2,1,0:T(8,128)(2,1)S(1)} async-done(((bf16[16,64,128]{2,1,0:T(8,128)(2,1)}), bf16[16,64,128]{2,1,0:T(8,128)(2,1)S(1)}, u32[]{:S(2)}, u32[]{:S(2)}) %all-to-all-start) | async-done | bytes 262176 | tf_op jit(solution)/shard_map/all_to_all | solution.py:540
  25.1 4.4 %all-to-all-start.1 = ((bf16[8,2,128,512]{3,2,1,0:T(8,128)(2,1)}), bf16[8,2,128,512]{3,2,1,0:T(8,128)(2,1)}, u32[]{:S(2)}, u32[]{:S(2)}) async-start(bf16[8,2,128,512]{3,2,1,0:T(8,128)(2,1)} %pack_tokens.1), calls=%async_computation.1 | async-start | bytes 4194304 | tf_op jit(solution)/shard_map/all_to_all | solution.py:546
  29.5 1.9 %for_pair.1 = bf16[2048,512]{1,0:T(8,128)(2,1)S(1)} custom-call(s32[16]{0:T(128)S(1)} %copy-done.42, s32[1]{0:T(128)} %bitcast.place, bf16[1024,512]{1,0:T(8,128)(2,1)S(1)} %copy-done.2, bf16[64,128,512]{2,1,0:T(8,128)(2,1)} %refs_15_.3), custom_call_target="tpu_custom_call" | custom-call | tf_op jit(solution)/shard_map/for_pair/pallas_call | solution.py:83
  31.5 0.8 collective-permute-start.9
  32.3 2.0 %collective-permute-start.8 = (bf16[1,128,1024]{2,1,0:T(8,128)(2,1)S(1)}, bf16[1,128,1024]{2,1,0:T(8,128)(2,1)S(1)}, u32[]{:S(2)}, u32[]{:S(2)}) collective-permute-start(bf16[1,128,1024]{2,1,0:T(8,128)(2,1)S(1)} %copy-done.5), channel_id=1, source_target_pairs={{0,4},{1,5},{2,6},{3,7},{4,0},{5,1},{6,2},{7,3},{8,12},{9,13},{10,... | collective-permute-start | bytes 786440 | tf_op jit(solution)/shard_map/ppermute | solution.py:553
  35.1 2.4 %collective-permute-start.5 = (bf16[1,128,128]{2,1,0:T(8,128)(2,1)S(1)}, bf16[1,128,128]{2,1,0:T(8,128)(2,1)S(1)}, u32[]{:S(2)}, u32[]{:S(2)}) collective-permute-start(bf16[1,128,128]{2,1,0:T(8,128)(2,1)S(1)} %back_low.1), channel_id=1, source_target_pairs={{0,8},{1,9},{2,10},{3,11},{4,12},{5,13},{6,14},{7,15},{8,0},{9,1},... | collective-permute-start | bytes 98312 | tf_op jit(solution)/shard_map/ppermute | solution.py:553
  38.1 1.5 collective-permute-start.7
  39.5 41.4 %collective-permute-done.5 = bf16[1,128,128]{2,1,0:T(8,128)(2,1)S(1)} collective-permute-done((bf16[1,128,128]{2,1,0:T(8,128)(2,1)S(1)}, bf16[1,128,128]{2,1,0:T(8,128)(2,1)S(1)}, u32[]{:S(2)}, u32[]{:S(2)}) %collective-permute-start.5) | collective-permute-done | bytes 32800 | tf_op jit(solution)/shard_map/ppermute | solution.py:553
  82.3 0.8 collective-permute-done.11
  83.7 0.9 copy-done.6
  84.6 0.9 copy-done.9
  85.6 0.9 copy-done.12
  86.5 0.9 copy-done.15
  87.5 0.9 copy-done.18
  88.4 0.9 copy-done.21
  89.4 4.0 %input_slices.2 = bf16[8,2,64,512]{3,2,1,0:T(8,128)(2,1)S(1)} custom-call(s32[16]{0:T(128)S(1)} %copy-done.42, s32[1]{0:T(128)} %bitcast.place, bf16[8,128,128]{2,1,0:T(8,128)(2,1)S(1)} %constant_dynamic-update-slice_fusion.backs, bf16[2048,512]{1,0:T(8,128)(2,1)} %copy-done, bf16[1,128,1024]{2,1,0:T(8,128)(2,1)S(1)} %bitcast.6, ...), custom_call_target="tpu_custom_call" | custom-call | tf_op jit(solution)/shard_map/input_slices/pallas_call | solution.py:60
  94.1 1.0 copy-done.25
  95.8 4.4 %all-to-all-start.2 = ((bf16[8,2,64,512]{3,2,1,0:T(8,128)(2,1)}), bf16[8,2,64,512]{3,2,1,0:T(8,128)(2,1)}, u32[]{:S(2)}, u32[]{:S(2)}) async-start(bf16[8,2,64,512]{3,2,1,0:T(8,128)(2,1)} %copy-done.25), calls=%async_computation.2 | async-start | bytes 2097152 | tf_op jit(solution)/shard_map/all_to_all | solution.py:546
  100.3 3.3 %hidden_parts.1 = (f32[8,128,128]{2,1,0:T(8,128)S(1)}, bf16[8,128,512]{2,1,0:T(8,128)(2,1)S(1)}, bf16[4,128,512]{2,1,0:T(8,128)(2,1)S(1)}, bf16[4,128,512]{2,1,0:T(8,128)(2,1)S(1)}) custom-call(s32[16]{0:T(128)S(1)} %copy-done.42, s32[1]{0:T(128)} %bitcast.place, bf16[2048,512]{1,0:T(8,128)(2,1)S(1)} %copy-done.1, ...), custom_call_target="tpu_custom_call" | custom-call | tf_op jit(solution)/shard_map/hidden_parts/pallas_call | solution.py:60
  103.5 1.0 copy-done.33
  105.0 0.9 collective-permute-start.16
  105.9 1.1 collective-permute-start.15
  107.2 0.9 collective-permute-start.14
  108.2 1.7 collective-permute-start.13
  110.0 15.4 %collective-permute-done.15.backs_pair = bf16[8,128,128]{2,1,0:T(8,128)(2,1)S(1)} collective-permute-done((bf16[8,128,128]{2,1,0:T(8,128)(2,1)S(1)}, bf16[8,128,128]{2,1,0:T(8,128)(2,1)S(1)}, u32[]{:S(2)}, u32[]{:S(2)}) %collective-permute-start.15) | collective-permute-done | bytes 262176 | tf_op jit(solution)/shard_map/ppermute | solution.py:553
  126.1 4.1 %collective-permute-done.14.gradients_pair = bf16[8,128,128]{2,1,0:T(8,128)(2,1)S(1)} collective-permute-done((bf16[8,128,128]{2,1,0:T(8,128)(2,1)S(1)}, bf16[8,128,128]{2,1,0:T(8,128)(2,1)S(1)}, u32[]{:S(2)}, u32[]{:S(2)}) %collective-permute-start.14) | collective-permute-done | bytes 262176 | tf_op jit(solution)/shard_map/ppermute | solution.py:553
  131.6 5.1 %input_slices.3 = bf16[8,2,64,512]{3,2,1,0:T(8,128)(2,1)} custom-call(s32[16]{0:T(128)S(1)} %copy-done.42, s32[1]{0:T(128)} %bitcast.place, bf16[8,128,128]{2,1,0:T(8,128)(2,1)S(1)} %copy-done.27, bf16[2048,512]{1,0:T(8,128)(2,1)} %copy-done, bf16[1,128,1024]{2,1,0:T(8,128)(2,1)S(1)} %bitcast.9, bf16[1,128,1024]{2,1,0:T(8,128)(2,1)S(1)} %copy-done.7, ...), custom_call_target="tpu_custom_call" | custom-call | tf_op jit(solution)/shard_map/input_slices/pallas_call | solution.py:60
  136.7 5.1 %all-to-all-start.3 = ((bf16[8,2,64,512]{3,2,1,0:T(8,128)(2,1)}), bf16[8,2,64,512]{3,2,1,0:T(8,128)(2,1)S(1)}, u32[]{:S(2)}, u32[]{:S(2)}) async-start(bf16[8,2,64,512]{3,2,1,0:T(8,128)(2,1)} %input_slices.3), calls=%async_computation.3 | async-start | bytes 2097152 | tf_op jit(solution)/shard_map/all_to_all | solution.py:546
  141.8 0.9 copy-done.40
  142.8 3.0 %collective-permute-start.17 = (bf16[4,128,128]{2,1,0:T(8,128)(2,1)S(1)}, bf16[4,128,128]{2,1,0:T(8,128)(2,1)S(1)}, u32[]{:S(2)}, u32[]{:S(2)}) collective-permute-start(bf16[4,128,128]{2,1,0:T(8,128)(2,1)S(1)} %get-tuple-element.68), channel_id=1, source_target_pairs={{0,8},{1,9},{2,10},{3,11},{4,12},{5,13},{6,14},{7,15},{8,0},{9,1},... | collective-permute-start | bytes 393224 | tf_op jit(solution)/shard_map/ppermute | solution.py:553
  145.8 0.9 collective-permute-start.20
  146.7 27.4 %collective-permute-done.17.received = bf16[4,128,128]{2,1,0:T(8,128)(2,1)S(1)} collective-permute-done((bf16[4,128,128]{2,1,0:T(8,128)(2,1)S(1)}, bf16[4,128,128]{2,1,0:T(8,128)(2,1)S(1)}, u32[]{:S(2)}, u32[]{:S(2)}) %collective-permute-start.17) | collective-permute-done | bytes 131104 | tf_op jit(solution)/shard_map/ppermute | solution.py:553
  174.7 1.3 collective-permute-done.18
  176.1 0.9 collective-permute-start.19
  177.0 0.9 copy-done.38
  178.0 5.5 %down_gradients.1 = bf16[64,128,512]{2,1,0:T(8,128)(2,1)} custom-call(s32[16]{0:T(128)S(1)} %copy-done.42, s32[1]{0:T(128)} %bitcast.place, bf16[8,128,128]{2,1,0:T(8,128)(2,1)S(1)} %copy-done.28, bf16[8,128,128]{2,1,0:T(8,128)(2,1)S(1)} %copy-done.38, bf16[8,128,512]{2,1,0:T(8,128)(2,1)S(1)} %copy-done.34, ...), custom_call_target="tpu_custom_call" | custom-call | tf_op jit(solution)/shard_map/down_gradients/pallas_call | solution.py:426
  183.4 1.0 collective-permute-done.19.hiddens_pair
  184.5 3.6 %up_gradients.1 = bf16[64,64,128]{2,1,0:T(8,128)(2,1)} custom-call(s32[16]{0:T(128)S(1)} %copy-done.42, s32[1]{0:T(128)} %bitcast.place, s32[64]{0:T(128)S(1)} %copy-done.43, bf16[8,128,128]{2,1,0:T(8,128)(2,1)S(1)} %get-tuple-element.53.gradients, bf16[8,128,128]{2,1,0:T(8,128)(2,1)S(1)} %copy-done.36, bf16[8,128,128]{2,1,0:T(8,128)(2,1)S(1)} %pad_maximum_fusion.hiddens, ...), custom_call_target="tpu_custom_call" | custom-call | tf_op jit(solution)/shard_map/up_gradients/pallas_call | solution.py:426
  188.1 2.3 %join_columns.2.refs_0_ = bf16[128,8192]{1,0:T(8,128)(2,1)} custom-call(s32[1]{0:T(128)} %bitcast.place, bf16[8,2,64,512]{3,2,1,0:T(8,128)(2,1)} %all-to-all-done.2.source), custom_call_target="tpu_custom_call" | custom-call | tf_op jit(solution)/shard_map/join_columns/pallas_call | solution.py:358
  190.4 1.1 join_columns.3
  (115 shorter events, 11.3 us)
Async XLA Ops:
  0.6 16.3 %collective-permute-start = (bf16[1,128,1024]{2,1,0:T(8,128)(2,1)}, bf16[1,128,1024]{2,1,0:T(8,128)(2,1)S(1)}, u32[]{:S(2)}, u32[]{:S(2)}) collective-permute-start(bf16[1,128,1024]{2,1,0:T(8,128)(2,1)} %bitcast.3), channel_id=1, source_target_pairs={{0,8},{1,9},{2,10},{3,11},{4,12},{5,13},{6,14},{7,15},{8,0},{9,1},... | collective-permute-start | bytes 786440 | tf_op jit(solution)/shard_map/ppermute | solution.py:553
  4.7 12.7 %collective-permute-start.1 = (bf16[1,128,1024]{2,1,0:T(8,128)(2,1)}, bf16[1,128,1024]{2,1,0:T(8,128)(2,1)S(1)}, u32[]{:S(2)}, u32[]{:S(2)}) collective-permute-start(bf16[1,128,1024]{2,1,0:T(8,128)(2,1)} %bitcast.4), channel_id=1, source_target_pairs={{0,4},{1,5},{2,6},{3,7},{4,0},{5,1},{6,2},{7,3},{8,12},{9,13},{10,... | collective-permute-start | bytes 786440 | tf_op jit(solution)/shard_map/ppermute | solution.py:553
  10.0 13.6 %all-to-all-start = ((bf16[16,64,128]{2,1,0:T(8,128)(2,1)}), bf16[16,64,128]{2,1,0:T(8,128)(2,1)S(1)}, u32[]{:S(2)}, u32[]{:S(2)}) async-start(bf16[16,64,128]{2,1,0:T(8,128)(2,1)} %gather_up.1), calls=%async_computation | async-start | bytes 524288 | tf_op jit(solution)/shard_map/all_to_all | solution.py:540
  13.5 7.4 %collective-permute-start.2 = (bf16[1,128,1024]{2,1,0:T(8,128)(2,1)}, bf16[1,128,1024]{2,1,0:T(8,128)(2,1)S(1)}, u32[]{:S(2)}, u32[]{:S(2)}) collective-permute-start(bf16[1,128,1024]{2,1,0:T(8,128)(2,1)} %bitcast.5), channel_id=1, source_target_pairs={{0,1},{1,0},{2,3},{3,2},{4,5},{5,4},{6,7},{7,6},{8,9},{9,8},{10,11... | collective-permute-start | bytes 786440 | tf_op jit(solution)/shard_map/ppermute | solution.py:553
  17.0 4.0 %copy-start.4 = (bf16[1,128,1024]{2,1,0:T(8,128)(2,1)}, bf16[1,128,1024]{2,1,0:T(8,128)(2,1)S(1)}, u32[]{:S(2)}) copy-start(bf16[1,128,1024]{2,1,0:T(8,128)(2,1)S(1)} %collective-permute-done.refs_2_.refs_3_.refs_1_) | copy-start | bytes 786436
  17.0 7.2 %collective-permute-start.3 = (bf16[1,128,1024]{2,1,0:T(8,128)(2,1)S(1)}, bf16[1,128,1024]{2,1,0:T(8,128)(2,1)S(1)}, u32[]{:S(2)}, u32[]{:S(2)}) collective-permute-start(bf16[1,128,1024]{2,1,0:T(8,128)(2,1)S(1)} %collective-permute-done.refs_2_.refs_3_.refs_1_), channel_id=1, source_target_pairs={{0,1},{1,0},{2,3},{3,2},{4,5},{5,4},{6,7},{7,6},{8,9},{9,8},{10,11... | collective-permute-start | bytes 786440 | tf_op jit(solution)/shard_map/ppermute | solution.py:553
  17.4 3.5 %copy-start.8 = (bf16[1,128,1024]{2,1,0:T(8,128)(2,1)}, bf16[1,128,1024]{2,1,0:T(8,128)(2,1)S(1)}, u32[]{:S(2)}) copy-start(bf16[1,128,1024]{2,1,0:T(8,128)(2,1)S(1)} %collective-permute-done.1.refs_4_.refs_5_.refs_2_) | copy-start | bytes 786436
  17.4 6.8 %collective-permute-start.4 = (bf16[1,128,1024]{2,1,0:T(8,128)(2,1)S(1)}, bf16[1,128,1024]{2,1,0:T(8,128)(2,1)S(1)}, u32[]{:S(2)}, u32[]{:S(2)}) collective-permute-start(bf16[1,128,1024]{2,1,0:T(8,128)(2,1)S(1)} %collective-permute-done.1.refs_4_.refs_5_.refs_2_), channel_id=1, source_target_pairs={{0,1},{1,0},{2,3},{3,2},{4,5},{5,4},{6,7},{7,6},{8,9},{9,8},{10,11... | collective-permute-start | bytes 786440 | tf_op jit(solution)/shard_map/ppermute | solution.py:553
  21.0 3.3 %copy-start.11 = (bf16[1,128,1024]{2,1,0:T(8,128)(2,1)}, bf16[1,128,1024]{2,1,0:T(8,128)(2,1)S(1)}, u32[]{:S(2)}) copy-start(bf16[1,128,1024]{2,1,0:T(8,128)(2,1)S(1)} %collective-permute-done.2.refs_8_.refs_9_.refs_4_) | copy-start | bytes 786436
  24.2 5.2 %copy-start.2 = (bf16[1024,512]{1,0:T(8,128)(2,1)S(1)}, bf16[1024,512]{1,0:T(8,128)(2,1)}, u32[]{:S(2)}) copy-start(bf16[1024,512]{1,0:T(8,128)(2,1)} %refs_16_.3) | copy-start | bytes 3145732
  24.3 5.2 %copy-start.42 = (s32[16]{0:T(128)S(1)}, s32[16]{0:T(128)}, u32[]{:S(2)}) copy-start(s32[16]{0:T(128)} %adapters.9) | copy-start | bytes 196
  25.1 56.6 %all-to-all-start.1 = ((bf16[8,2,128,512]{3,2,1,0:T(8,128)(2,1)}), bf16[8,2,128,512]{3,2,1,0:T(8,128)(2,1)}, u32[]{:S(2)}, u32[]{:S(2)}) async-start(bf16[8,2,128,512]{3,2,1,0:T(8,128)(2,1)} %pack_tokens.1), calls=%async_computation.1 | async-start | bytes 4194304 | tf_op jit(solution)/shard_map/all_to_all | solution.py:546
  29.5 2.8 %copy-start.5 = (bf16[1,128,1024]{2,1,0:T(8,128)(2,1)S(1)}, bf16[1,128,1024]{2,1,0:T(8,128)(2,1)}, u32[]{:S(2)}) copy-start(bf16[1,128,1024]{2,1,0:T(8,128)(2,1)} %copy-done.4) | copy-start | bytes 786436
  29.5 4.8 %copy-start.3 = (bf16[128,1024]{1,0:T(8,128)(2,1)S(1)}, bf16[128,1024]{1,0:T(8,128)(2,1)}, u32[]{:S(2)}) copy-start(bf16[128,1024]{1,0:T(8,128)(2,1)} %gradient.1) | copy-start | bytes 786436
  29.5 4.8 %copy-start.32 = (bf16[16,64,128]{2,1,0:T(8,128)(2,1)S(1)}, bf16[16,64,128]{2,1,0:T(8,128)(2,1)}, u32[]{:S(2)}) copy-start(bf16[16,64,128]{2,1,0:T(8,128)(2,1)} %copy-done.31) | copy-start | bytes 786436
  29.5 4.8 %copy-start.43 = (s32[64]{0:T(128)S(1)}, s32[64]{0:T(128)}, u32[]{:S(2)}) copy-start(s32[64]{0:T(128)} %ranks.5) | copy-start | bytes 772
  31.5 50.2 %collective-permute-start.9 = (bf16[2048,512]{1,0:T(8,128)(2,1)S(1)}, bf16[2048,512]{1,0:T(8,128)(2,1)S(1)}, u32[]{:S(2)}, u32[]{:S(2)}) collective-permute-start(bf16[2048,512]{1,0:T(8,128)(2,1)S(1)} %for_pair.1), channel_id=1, source_target_pairs={{0,2},{1,3},{2,0},{3,1},{4,6},{5,7},{6,4},{7,5},{8,10},{9,11},{10,... | collective-permute-start | bytes 6291464 | tf_op jit(solution)/shard_map/ppermute | solution.py:553
  32.3 48.6 %collective-permute-start.8 = (bf16[1,128,1024]{2,1,0:T(8,128)(2,1)S(1)}, bf16[1,128,1024]{2,1,0:T(8,128)(2,1)S(1)}, u32[]{:S(2)}, u32[]{:S(2)}) collective-permute-start(bf16[1,128,1024]{2,1,0:T(8,128)(2,1)S(1)} %copy-done.5), channel_id=1, source_target_pairs={{0,4},{1,5},{2,6},{3,7},{4,0},{5,1},{6,2},{7,3},{8,12},{9,13},{10,... | collective-permute-start | bytes 786440 | tf_op jit(solution)/shard_map/ppermute | solution.py:553
  35.1 45.8 %collective-permute-start.5 = (bf16[1,128,128]{2,1,0:T(8,128)(2,1)S(1)}, bf16[1,128,128]{2,1,0:T(8,128)(2,1)S(1)}, u32[]{:S(2)}, u32[]{:S(2)}) collective-permute-start(bf16[1,128,128]{2,1,0:T(8,128)(2,1)S(1)} %back_low.1), channel_id=1, source_target_pairs={{0,8},{1,9},{2,10},{3,11},{4,12},{5,13},{6,14},{7,15},{8,0},{9,1},... | collective-permute-start | bytes 98312 | tf_op jit(solution)/shard_map/ppermute | solution.py:553
  37.5 43.4 %collective-permute-start.6 = (bf16[1,128,128]{2,1,0:T(8,128)(2,1)S(1)}, bf16[1,128,128]{2,1,0:T(8,128)(2,1)S(1)}, u32[]{:S(2)}, u32[]{:S(2)}) collective-permute-start(bf16[1,128,128]{2,1,0:T(8,128)(2,1)S(1)} %back_low.1), channel_id=1, source_target_pairs={{0,4},{1,5},{2,6},{3,7},{4,0},{5,1},{6,2},{7,3},{8,12},{9,13},{10,... | collective-permute-start | bytes 98312 | tf_op jit(solution)/shard_map/ppermute | solution.py:553
  38.1 42.8 %collective-permute-start.7 = (bf16[1,128,128]{2,1,0:T(8,128)(2,1)S(1)}, bf16[1,128,128]{2,1,0:T(8,128)(2,1)S(1)}, u32[]{:S(2)}, u32[]{:S(2)}) collective-permute-start(bf16[1,128,128]{2,1,0:T(8,128)(2,1)S(1)} %back_low.1), channel_id=1, source_target_pairs={{0,12},{1,13},{2,14},{3,15},{4,8},{5,9},{6,10},{7,11},{8,4},{9,5},... | collective-permute-start | bytes 98312 | tf_op jit(solution)/shard_map/ppermute | solution.py:553
  81.6 2.0 %copy-start = (bf16[2048,512]{1,0:T(8,128)(2,1)}, bf16[2048,512]{1,0:T(8,128)(2,1)S(1)}, u32[]{:S(2)}) copy-start(bf16[2048,512]{1,0:T(8,128)(2,1)S(1)} %collective-permute-done.9.pair) | copy-start | bytes 6291460
  81.7 1.4 collective-permute-start.11
  81.8 1.9 collective-permute-start.10
  95.8 4.4 %copy-start.1 = (bf16[2048,512]{1,0:T(8,128)(2,1)S(1)}, bf16[2048,512]{1,0:T(8,128)(2,1)}, u32[]{:S(2)}) copy-start(bf16[2048,512]{1,0:T(8,128)(2,1)} %copy-done) | copy-start | bytes 6291460
  95.8 40.9 %all-to-all-start.2 = ((bf16[8,2,64,512]{3,2,1,0:T(8,128)(2,1)}), bf16[8,2,64,512]{3,2,1,0:T(8,128)(2,1)}, u32[]{:S(2)}, u32[]{:S(2)}) async-start(bf16[8,2,64,512]{3,2,1,0:T(8,128)(2,1)} %copy-done.25), calls=%async_computation.2 | async-start | bytes 2097152 | tf_op jit(solution)/shard_map/all_to_all | solution.py:546
  100.2 5.7 %copy-start.27 = (bf16[8,128,128]{2,1,0:T(8,128)(2,1)S(1)}, bf16[8,128,128]{2,1,0:T(8,128)(2,1)}, u32[]{:S(2)}) copy-start(bf16[8,128,128]{2,1,0:T(8,128)(2,1)} %copy-done.26) | copy-start | bytes 786436
  100.2 6.8 %copy-start.7 = (bf16[1,128,1024]{2,1,0:T(8,128)(2,1)S(1)}, bf16[1,128,1024]{2,1,0:T(8,128)(2,1)}, u32[]{:S(2)}) copy-start(bf16[1,128,1024]{2,1,0:T(8,128)(2,1)} %copy-done.4) | copy-start | bytes 786436
  100.2 6.8 %copy-start.10 = (bf16[1,128,1024]{2,1,0:T(8,128)(2,1)S(1)}, bf16[1,128,1024]{2,1,0:T(8,128)(2,1)}, u32[]{:S(2)}) copy-start(bf16[1,128,1024]{2,1,0:T(8,128)(2,1)} %copy-done.8) | copy-start | bytes 786436
  100.2 6.8 %copy-start.13 = (bf16[1,128,1024]{2,1,0:T(8,128)(2,1)S(1)}, bf16[1,128,1024]{2,1,0:T(8,128)(2,1)}, u32[]{:S(2)}) copy-start(bf16[1,128,1024]{2,1,0:T(8,128)(2,1)} %copy-done.11) | copy-start | bytes 786436
  100.2 6.8 %copy-start.16 = (bf16[1,128,1024]{2,1,0:T(8,128)(2,1)S(1)}, bf16[1,128,1024]{2,1,0:T(8,128)(2,1)}, u32[]{:S(2)}) copy-start(bf16[1,128,1024]{2,1,0:T(8,128)(2,1)} %copy-done.14) | copy-start | bytes 786436
  100.2 6.8 %copy-start.19 = (bf16[1,128,1024]{2,1,0:T(8,128)(2,1)S(1)}, bf16[1,128,1024]{2,1,0:T(8,128)(2,1)}, u32[]{:S(2)}) copy-start(bf16[1,128,1024]{2,1,0:T(8,128)(2,1)} %copy-done.17) | copy-start | bytes 786436
  100.2 6.8 %copy-start.22 = (bf16[1,128,1024]{2,1,0:T(8,128)(2,1)S(1)}, bf16[1,128,1024]{2,1,0:T(8,128)(2,1)}, u32[]{:S(2)}) copy-start(bf16[1,128,1024]{2,1,0:T(8,128)(2,1)} %copy-done.20) | copy-start | bytes 786436
  100.3 6.8 %copy-start.24 = (bf16[1,128,1024]{2,1,0:T(8,128)(2,1)S(1)}, bf16[1,128,1024]{2,1,0:T(8,128)(2,1)}, u32[]{:S(2)}) copy-start(bf16[1,128,1024]{2,1,0:T(8,128)(2,1)} %copy-done.23) | copy-start | bytes 786436
  104.5 27.1 %copy-start.44 = (bf16[4,128,512]{2,1,0:T(8,128)(2,1)}, bf16[4,128,512]{2,1,0:T(8,128)(2,1)S(1)}, u32[]{:S(2)}) copy-start(bf16[4,128,512]{2,1,0:T(8,128)(2,1)S(1)} %get-tuple-element.73) | copy-start | bytes 1572868
  104.5 3.7 %collective-permute-start.12 = (f32[4,128,128]{2,1,0:T(8,128)S(1)}, f32[4,128,128]{2,1,0:T(8,128)S(1)}, u32[]{:S(2)}, u32[]{:S(2)}) collective-permute-start(f32[4,128,128]{2,1,0:T(8,128)S(1)} %slice.3), channel_id=1, source_target_pairs={{0,1},{1,0},{2,3},{3,2},{4,5},{5,4},{6,7},{7,6},{8,9},{9,8},{10,11... | collective-permute-start | bytes 786440 | tf_op jit(solution)/shard_map/ppermute | solution.py:553
  105.0 25.9 %collective-permute-start.16 = (bf16[4,128,512]{2,1,0:T(8,128)(2,1)S(1)}, bf16[4,128,512]{2,1,0:T(8,128)(2,1)S(1)}, u32[]{:S(2)}, u32[]{:S(2)}) collective-permute-start(bf16[4,128,512]{2,1,0:T(8,128)(2,1)S(1)} %get-tuple-element.63), channel_id=1, source_target_pairs={{0,2},{1,3},{2,0},{3,1},{4,6},{5,7},{6,4},{7,5},{8,10},{9,11},{10,... | collective-permute-start | bytes 1572872 | tf_op jit(solution)/shard_map/ppermute | solution.py:553
  105.9 19.5 %collective-permute-start.15 = (bf16[8,128,128]{2,1,0:T(8,128)(2,1)S(1)}, bf16[8,128,128]{2,1,0:T(8,128)(2,1)S(1)}, u32[]{:S(2)}, u32[]{:S(2)}) collective-permute-start(bf16[8,128,128]{2,1,0:T(8,128)(2,1)S(1)} %copy-done.27), channel_id=1, source_target_pairs={{0,2},{1,3},{2,0},{3,1},{4,6},{5,7},{6,4},{7,5},{8,10},{9,11},{10,... | collective-permute-start | bytes 786440 | tf_op jit(solution)/shard_map/ppermute | solution.py:553
  107.2 22.9 %collective-permute-start.14 = (bf16[8,128,128]{2,1,0:T(8,128)(2,1)S(1)}, bf16[8,128,128]{2,1,0:T(8,128)(2,1)S(1)}, u32[]{:S(2)}, u32[]{:S(2)}) collective-permute-start(bf16[8,128,128]{2,1,0:T(8,128)(2,1)S(1)} %get-tuple-element.62), channel_id=1, source_target_pairs={{0,2},{1,3},{2,0},{3,1},{4,6},{5,7},{6,4},{7,5},{8,10},{9,11},{10,... | collective-permute-start | bytes 786440 | tf_op jit(solution)/shard_map/ppermute | solution.py:553
  108.2 22.7 %collective-permute-start.13 = (f32[4,128,128]{2,1,0:T(8,128)S(1)}, f32[4,128,128]{2,1,0:T(8,128)S(1)}, u32[]{:S(2)}, u32[]{:S(2)}) collective-permute-start(f32[4,128,128]{2,1,0:T(8,128)S(1)} %slot_sums.2.total), channel_id=1, source_target_pairs={{0,4},{1,5},{2,6},{3,7},{4,0},{5,1},{6,2},{7,3},{8,12},{9,13},{10,... | collective-permute-start | bytes 786440 | tf_op jit(solution)/shard_map/ppermute | solution.py:553
  136.7 40.3 %copy-start.28 = (bf16[8,128,128]{2,1,0:T(8,128)(2,1)S(1)}, bf16[8,128,128]{2,1,0:T(8,128)(2,1)}, u32[]{:S(2)}) copy-start(bf16[8,128,128]{2,1,0:T(8,128)(2,1)} %copy-done.26) | copy-start | bytes 786436
  136.7 40.3 %copy-start.34 = (bf16[8,128,512]{2,1,0:T(8,128)(2,1)S(1)}, bf16[8,128,512]{2,1,0:T(8,128)(2,1)}, u32[]{:S(2)}) copy-start(bf16[8,128,512]{2,1,0:T(8,128)(2,1)} %copy-done.33) | copy-start | bytes 3145732
  136.7 53.7 %all-to-all-start.3 = ((bf16[8,2,64,512]{3,2,1,0:T(8,128)(2,1)}), bf16[8,2,64,512]{3,2,1,0:T(8,128)(2,1)S(1)}, u32[]{:S(2)}, u32[]{:S(2)}) async-start(bf16[8,2,64,512]{3,2,1,0:T(8,128)(2,1)} %input_slices.3), calls=%async_computation.3 | async-start | bytes 2097152 | tf_op jit(solution)/shard_map/all_to_all | solution.py:546
  142.8 31.2 %collective-permute-start.17 = (bf16[4,128,128]{2,1,0:T(8,128)(2,1)S(1)}, bf16[4,128,128]{2,1,0:T(8,128)(2,1)S(1)}, u32[]{:S(2)}, u32[]{:S(2)}) collective-permute-start(bf16[4,128,128]{2,1,0:T(8,128)(2,1)S(1)} %get-tuple-element.68), channel_id=1, source_target_pairs={{0,8},{1,9},{2,10},{3,11},{4,12},{5,13},{6,14},{7,15},{8,0},{9,1},... | collective-permute-start | bytes 393224 | tf_op jit(solution)/shard_map/ppermute | solution.py:553
  145.8 31.2 %collective-permute-start.20 = (bf16[4,128,512]{2,1,0:T(8,128)(2,1)}, bf16[4,128,512]{2,1,0:T(8,128)(2,1)S(1)}, u32[]{:S(2)}, u32[]{:S(2)}) collective-permute-start(bf16[4,128,512]{2,1,0:T(8,128)(2,1)} %copy-done.44), channel_id=1, source_target_pairs={{0,2},{1,3},{2,0},{3,1},{4,6},{5,7},{6,4},{7,5},{8,10},{9,11},{10,... | collective-permute-start | bytes 1572872 | tf_op jit(solution)/shard_map/ppermute | solution.py:553
  174.6 1.4 collective-permute-start.18
  176.1 8.4 %collective-permute-start.19 = (bf16[8,128,128]{2,1,0:T(8,128)(2,1)S(1)}, bf16[8,128,128]{2,1,0:T(8,128)(2,1)S(1)}, u32[]{:S(2)}, u32[]{:S(2)}) collective-permute-start(bf16[8,128,128]{2,1,0:T(8,128)(2,1)S(1)} %pad_maximum_fusion.hiddens), channel_id=1, source_target_pairs={{0,2},{1,3},{2,0},{3,1},{4,6},{5,7},{6,4},{7,5},{8,10},{9,11},{10,... | collective-permute-start | bytes 786440 | tf_op jit(solution)/shard_map/ppermute | solution.py:553
  178.0 6.5 %copy-start.36 = (bf16[8,128,128]{2,1,0:T(8,128)(2,1)S(1)}, bf16[8,128,128]{2,1,0:T(8,128)(2,1)}, u32[]{:S(2)}) copy-start(bf16[8,128,128]{2,1,0:T(8,128)(2,1)} %copy-done.35) | copy-start | bytes 786436
  (22 other events, 19.6 us)

commit v18 on v17

--- a/solution.py
+++ b/solution.py
@@ -8,7 +8,7 @@
 from jax.sharding import PartitionSpec as P
 
 adapter_alpha = 32.0
-vmem_limit = 48 * 1024 * 1024
+vmem_limit = 60 * 1024 * 1024
 pair_bit = 2
 line_bit = 4
 
@@ -257,15 +257,12 @@
 
 
 def hidden_kernel(adapters, place, pair, tokens, *refs):
-    parts, own, *others = refs[-4:]
-    members = own.shape[0]
-    downs = refs[:members]
+    *downs, parts = refs
+    members = parts.shape[0]
     extent = downs[0].shape[1]
     across = (((1,), (1,)), ((), ()))
     for slot in range(members):
         index = side_index(place[0] ^ line_offset(slot, members), members)
-        own[slot] = tokens[index, 0]
-        others[slot // (members // 2)][slot % (members // 2)] = tokens[index, 1]
         parts[slot] = lax.dot_general(
             tokens[index, 0], downs[slot][0], across, preferred_element_type=jnp.float32
         ) + lax.dot_general(
@@ -277,9 +274,8 @@
 
 
 def hidden_parts(adapters, place, down_maps, pair, tokens):
-    members, _, rows, width = tokens.shape
+    members, _, rows, _ = tokens.shape
     extent = down_maps.shape[1]
-    others = jax.ShapeDtypeStruct((members // 2, rows, width), tokens.dtype)
     return call(
         hidden_kernel,
         "hidden_parts",
@@ -287,12 +283,27 @@
         [pair, tokens] + [down_maps] * members,
         [whole(pair.shape), whole(tokens.shape)]
         + [picked(down_maps, line_offset(slot, members)) for slot in range(members)],
-        [
-            jax.ShapeDtypeStruct((members, rows, extent), jnp.float32),
-            jax.ShapeDtypeStruct((members, rows, width), tokens.dtype),
-            others,
-            others,
-        ],
+        [jax.ShapeDtypeStruct((members, rows, extent), jnp.float32)],
+    )[0]
+
+
+def pair_tokens_kernel(tokens, first, second):
+    half = first.shape[0]
+    for index in range(half):
+        first[index] = tokens[index, 0]
+        second[index] = tokens[half + index, 0]
+
+
+def pair_tokens(tokens):
+    members, _, rows, width = tokens.shape
+    shape = jax.ShapeDtypeStruct((members // 2, rows, width), tokens.dtype)
+    return call(
+        pair_tokens_kernel,
+        "pair_tokens",
+        (),
+        (tokens,),
+        [pl.BlockSpec((members, 1, rows, width), lambda *_: (0, 1, 0, 0))],
+        [shape, shape],
     )
 
 
@@ -334,41 +345,37 @@
     )[0]
 
 
-def join_kernel(place, source, *refs, part):
-    out, sems = refs[-2:]
-    members, _, rows, width = source.shape
+def join_kernel(place, source, out, sems):
+    members, _, _, width = source.shape
     copies = []
     for index in range(members):
         for half in range(2):
             column = side_place(index, side_of(place[0]) ^ half, members) * width
-            columns = pl.ds(pl.multiple_of(column, width), width)
             copies.append(
                 pltpu.make_async_copy(
                     source.at[index, half],
-                    out.at[pl.ds(part * rows, rows), columns],
+                    out.at[:, pl.ds(pl.multiple_of(column, width), width)],
                     sems.at[2 * index + half],
                 )
             )
     run(copies)
 
 
-def join_columns(place, source, part, parts, before=()):
+def join_columns(place, source):
     members, _, rows, width = source.shape
-    shape = jax.ShapeDtypeStruct((parts * rows, 2 * members * width), source.dtype)
     return pl.pallas_call(
-        functools.partial(join_kernel, part=part),
-        out_shape=shape,
+        join_kernel,
+        out_shape=jax.ShapeDtypeStruct((rows, 2 * members * width), source.dtype),
         grid_spec=pltpu.PrefetchScalarGridSpec(
             num_scalar_prefetch=1,
             grid=(1,),
-            in_specs=[whole(source.shape)] + [pl.BlockSpec(memory_space=pl.ANY)] * len(before),
+            in_specs=[whole(source.shape)],
             out_specs=pl.BlockSpec(memory_space=pl.ANY),
             scratch_shapes=[pltpu.SemaphoreType.DMA((2 * members,))],
         ),
-        input_output_aliases={2: 0} if before else {},
         compiler_params=params(),
         name="join_columns",
-    )(place, source, *before)
+    )(place, source)
 
 
 def list_members(adapters, place, members, head, following):
@@ -422,14 +429,14 @@
     )
 
 
-def sums_call(kernel, name, prefetch, operands, num_adapters, entries, product, scratch=()):
+def sums_call(kernel, name, prefetch, operands, num_adapters, entries, product, scratch=(), specs=None):
     return pl.pallas_call(
         kernel,
         out_shape=jax.ShapeDtypeStruct((num_adapters,) + product, jnp.bfloat16),
         grid_spec=pltpu.PrefetchScalarGridSpec(
             num_scalar_prefetch=len(prefetch),
             grid=(1,),
-            in_specs=[whole(operand.shape) for operand in operands],
+            in_specs=specs or [whole(operand.shape) for operand in operands],
             out_specs=pl.BlockSpec(memory_space=pltpu.HBM),
             scratch_shapes=[
                 pltpu.SMEM((num_adapters,), jnp.int32),
@@ -451,7 +458,7 @@
     place,
     backs,
     backs_pair,
-    own,
+    tokens,
     other_first,
     other_second,
     out,
@@ -462,28 +469,38 @@
     zero,
     sems,
 ):
-    members = own.shape[0]
-    others = (other_first, other_second)
+    members = tokens.shape[0]
+    half = members // 2
     list_members(adapters, place, members, head, following)
     for slot in range(members):
-        products[slot] = by_rows(backs[slot], own[slot])
-        core, line = divmod(slot, members // 2)
-        products[members + slot] = by_rows(backs_pair[slot], others[core][line])
+        index = side_index(place[0] ^ line_offset(slot, members), members)
+        products[slot] = by_rows(backs[slot], tokens[index, 0])
+        for number, other in enumerate((other_first, other_second)):
+
+            @pl.when(index // half == number)
+            def _(slot=slot, index=index, other=other):
+                products[members + slot] = by_rows(backs_pair[slot], other[lax.rem(index, half)])
+
     write_sums(
         head, following, products, ready, zero, out, sems, lambda adapter, total: total
     )
 
 
-def down_gradients(adapters, place, backs, backs_pair, own, others, num_adapters):
-    members, _, width = own.shape
+def down_gradients(adapters, place, backs, backs_pair, tokens, others, num_adapters):
+    members, _, rows, width = tokens.shape
+    extent = backs.shape[2]
+    operands = (backs, backs_pair, tokens, *others)
+    specs = [whole(operand.shape) for operand in operands]
+    specs[2] = pl.BlockSpec((members, 1, rows, width), lambda *_: (0, 0, 0, 0))
     return sums_call(
         down_gradient_kernel,
         "down_gradients",
         (adapters, place),
-        (backs, backs_pair, own, *others),
+        operands,
         num_adapters,
         2 * members,
-        (backs.shape[2], width),
+        (extent, width),
+        specs=specs,
     )
 
 
@@ -596,57 +613,43 @@
             gradients[slot + (1 << step)] = swap(gradients[slot], offsets[1 << step])
     backs = back_rows(adapters, place, ranks, output_gradient, own_up)
     backs = [backs] + [swap(backs, offset) for offset in offsets[1:lines]]
-    arrived, backs, gradients, pair = barrier((arrived, backs, gradients, pair))
-
+    arrived, backs[0], gradients, pair = barrier((arrived, backs[0], gradients, pair))
+
+    parts = hidden_parts(adapters, place, down_maps, pair, arrived)
     for slot in range(lines):
         if slot not in across:
             across[slot] = swap(gradients[slot], 1)
+    backs = gather_step(jnp.concatenate(backs, axis=0), members)
     gradients = gradients + [across[slot] for slot in range(lines)]
-    backs = gather_step(jnp.concatenate(backs, axis=0), members)
     slices = input_slices(
-        adapters, place, gradients, backs, value_weight, pair, down_maps, 0, 2
-    )
-    slices, arrived = barrier((slices, arrived))
-    first = exchange_side(slices)
-
-    parts, tokens_own, *tokens_pair = hidden_parts(
-        adapters, place, down_maps, pair, arrived
-    )
-    columns, columns_other = gradient_columns(place, gradients, depth // devices)
-    columns_other = swap(columns_other, pair_bit)
-    backs_pair = swap(backs, pair_bit)
-    tokens_other = [swap(tokens_pair[0], pair_bit)]
+        adapters, place, gradients, backs, value_weight, pair, down_maps, 0, 1
+    )
     total, received, flip = parts, swap(parts[lines:], 1), 0
     for step in reversed(range(steps - 1)):
         kinds = [jnp.float32] if step else [jnp.float32, jnp.bfloat16]
         sums = slot_sums(total, received, flip, kinds)
         total, flip = sums[0], 1 << step
         received = swap(sums[-1], offsets[flip])
-        if step == 1:
-            received, backs, columns_other, backs_pair, tokens_other, tokens_pair = barrier(
-                (received, backs, columns_other, backs_pair, tokens_other, tokens_pair)
-            )
-            slices = input_slices(
-                adapters, place, gradients, backs, value_weight, pair, down_maps, 1, 2
-            )
-    second = exchange_side(slices)
-
+    received, slices, backs, gradients, arrived = barrier(
+        (received, slices, backs, gradients, arrived)
+    )
+
+    result = exchange_side(slices)
     hiddens = hidden_rows(adapters, place, ranks, total, received, flip, members)
     hiddens = gather_step(hiddens, members)
+    columns, columns_other = gradient_columns(place, gradients, depth // devices)
+    columns_other = swap(columns_other, pair_bit)
+    backs_pair = swap(backs, pair_bit)
+    tokens_other = [swap(half, pair_bit) for half in pair_tokens(arrived)]
     hiddens_pair = swap(hiddens, pair_bit)
-    tokens_other.append(swap(tokens_pair[1], pair_bit))
     up_gradient = up_gradients(
         adapters, place, ranks, columns, columns_other, hiddens, hiddens_pair, depth // devices
     )
     down_gradient = down_gradients(
-        adapters, place, backs, backs_pair, tokens_own, tokens_other, num_adapters
-    )
-    joined = join_columns(place, first, 0, 2)
-    up_gradient, down_gradient, joined, second = barrier(
-        (up_gradient, down_gradient, joined, second)
-    )
-    input_grad = join_columns(place, second, 1, 2, (joined,))
-    return (input_grad, down_gradient, up_gradient)
+        adapters, place, backs, backs_pair, arrived, tokens_other, num_adapters
+    )
+    up_gradient, down_gradient, result = barrier((up_gradient, down_gradient, result))
+    return (join_columns(place, result), down_gradient, up_gradient)
 
 
 def solution(mesh):

time: 192 us -> 187 us (0.974)
  Pallas kernels: 31.9 us -> 51.2 us
  waiting for transfers between devices: 98.1 us -> 86.5 us
  local copies, waits for them, and re-layouts: 18.9 us -> 10.4 us
  starting transfers between devices: 41.4 us -> 36.7 us
    pallas_call x8, Pallas kernels: 13.9 us -> 25 us  [call(): pl.pallas_call(kernel, out_shape=out_shapes, grid_spec=pltpu.PrefetchScal...]
    ppermute x21, waiting for transfers between devices: 95.6 us -> 85.1 us  [swap(): return lax.ppermute(array, 'dp', [(i, i ^ flip) for i in range(devices)])]
    unnamed x94 -> x50, local copies, waits for them, and re-layouts: 18.9 us -> 9.41 us
    pallas_call x2, Pallas kernels: 9.08 us -> 13.9 us  [sums_call(): pl.pallas_call(kernel, out_shape=jax.ShapeDtypeStruct((num_adapters,) + p...]
    all_to_all x3 -> x2, starting transfers between devices: 13.9 us -> 9.39 us  [exchange_side(): lax.all_to_all(pieces, 'dp', split_axis=0, concat_axis=0, axis_index_grou...]
    pallas_call x3, Pallas kernels: 5.5 us -> 9.24 us  [copy_call(): pl.pallas_call(kernel, out_shape=out_shapes, grid_spec=pltpu.PrefetchScal...]
  transfers between devices with their start and end apart: 25 -> 24, of which waited for: 11 -> 11; matrix products, arithmetic and copies ran while one was open for 0% -> 0% of each run, Pallas kernels for 14% -> 23%
where the time goes in v18:
time: 187 us; the launch traced here: 186 us
  waiting for transfers between devices  86.5 us (46%)
  Pallas kernels  51.2 us (27%)
  starting transfers between devices  36.7 us (20%)
  local copies, waits for them, and re-layouts  10.4 us (6%)
    ppermute x21, waiting for transfers between devices, swap(): return lax.ppermute(array, 'dp', [(i, i ^ flip) for i in range(devices)])  85.1 us
    pallas_call x8, Pallas kernels, call(): pl.pallas_call(kernel, out_shape=out_shapes, grid_spec=pltpu.PrefetchScal...  25 us
    ppermute x21, starting transfers between devices, swap(): return lax.ppermute(array, 'dp', [(i, i ^ flip) for i in range(devices)])  23.8 us
    pallas_call x2, Pallas kernels, sums_call(): pl.pallas_call(kernel, out_shape=jax.ShapeDtypeStruct((num_adapters,) + p...  13.9 us
    unnamed x50, local copies, waits for them, and re-layouts  9.41 us
    all_to_all x2, starting transfers between devices, exchange_side(): lax.all_to_all(pieces, 'dp', split_axis=0, concat_axis=0, axis_index_grou...  9.39 us
    pallas_call x3, Pallas kernels, copy_call(): pl.pallas_call(kernel, out_shape=out_shapes, grid_spec=pltpu.PrefetchScal...  9.24 us
  transfers between devices with their start and end apart: 24, of which 11 were waited for; matrix products, arithmetic and copies ran while one was open for 0% of the time, Pallas kernels for 23%

profile of v18, /device:TPU:0, one launch (start us, length us, event | category | flops | bytes accessed | tf_op | source)
XLA Modules:
  0.0 185.7 jit_solution(13502256630186658010)
XLA Ops:
  0.6 3.1 %collective-permute-start.1 = (bf16[1,128,1024]{2,1,0:T(8,128)(2,1)}, bf16[1,128,1024]{2,1,0:T(8,128)(2,1)S(1)}, u32[]{:S(2)}, u32[]{:S(2)}) collective-permute-start(bf16[1,128,1024]{2,1,0:T(8,128)(2,1)} %bitcast.3), channel_id=1, source_target_pairs={{0,4},{1,5},{2,6},{3,7},{4,0},{5,1},{6,2},{7,3},{8,12},{9,13},{10,... | collective-permute-start | bytes 786440 | tf_op jit(solution)/shard_map/ppermute | solution.py:570
  3.7 2.6 %collective-permute-start = (bf16[1,128,1024]{2,1,0:T(8,128)(2,1)}, bf16[1,128,1024]{2,1,0:T(8,128)(2,1)S(1)}, u32[]{:S(2)}, u32[]{:S(2)}) collective-permute-start(bf16[1,128,1024]{2,1,0:T(8,128)(2,1)} %bitcast.4), channel_id=1, source_target_pairs={{0,8},{1,9},{2,10},{3,11},{4,12},{5,13},{6,14},{7,15},{8,0},{9,1},... | collective-permute-start | bytes 786440 | tf_op jit(solution)/shard_map/ppermute | solution.py:570
  6.3 2.4 %gather_up.1 = bf16[16,64,128]{2,1,0:T(8,128)(2,1)} custom-call(s32[16]{0:T(128)} %adapters.8, bf16[64,64,128]{2,1,0:T(8,128)(2,1)} %up_maps.1), custom_call_target="tpu_custom_call" | custom-call | tf_op jit(solution)/shard_map/gather_up/pallas_call | solution.py:83
  8.7 3.5 %all-to-all-start = ((bf16[16,64,128]{2,1,0:T(8,128)(2,1)}), bf16[16,64,128]{2,1,0:T(8,128)(2,1)S(1)}, u32[]{:S(2)}, u32[]{:S(2)}) async-start(bf16[16,64,128]{2,1,0:T(8,128)(2,1)} %gather_up.1), calls=%async_computation | async-start | bytes 524288 | tf_op jit(solution)/shard_map/all_to_all | solution.py:557
  12.6 3.5 %collective-permute-done.1.refs_2_.refs_4_.refs_5_ = bf16[1,128,1024]{2,1,0:T(8,128)(2,1)S(1)} collective-permute-done((bf16[1,128,1024]{2,1,0:T(8,128)(2,1)}, bf16[1,128,1024]{2,1,0:T(8,128)(2,1)S(1)}, u32[]{:S(2)}, u32[]{:S(2)}) %collective-permute-start.1) | collective-permute-done | bytes 262176 | tf_op jit(solution)/shard_map/ppermute | solution.py:570
  16.1 3.0 %collective-permute-done.refs_1_.refs_2_.refs_3_ = bf16[1,128,1024]{2,1,0:T(8,128)(2,1)S(1)} collective-permute-done((bf16[1,128,1024]{2,1,0:T(8,128)(2,1)}, bf16[1,128,1024]{2,1,0:T(8,128)(2,1)S(1)}, u32[]{:S(2)}, u32[]{:S(2)}) %collective-permute-start) | collective-permute-done | bytes 262176 | tf_op jit(solution)/shard_map/ppermute | solution.py:570
  19.1 3.2 %pack_tokens.1 = bf16[8,2,128,512]{3,2,1,0:T(8,128)(2,1)} custom-call(s32[1]{0:T(128)} %bitcast.place, bf16[128,8192]{1,0:T(8,128)(2,1)} %tokens.1), custom_call_target="tpu_custom_call" | custom-call | tf_op jit(solution)/shard_map/pack_tokens/pallas_call | solution.py:83
  22.3 1.4 all-to-all-done
  23.7 0.7 copy-done.12
  24.6 5.6 %all-to-all-start.1 = ((bf16[8,2,128,512]{3,2,1,0:T(8,128)(2,1)}), bf16[8,2,128,512]{3,2,1,0:T(8,128)(2,1)S(1)}, u32[]{:S(2)}, u32[]{:S(2)}) async-start(bf16[8,2,128,512]{3,2,1,0:T(8,128)(2,1)} %pack_tokens.1), calls=%async_computation.1 | async-start | bytes 4194304 | tf_op jit(solution)/shard_map/all_to_all | solution.py:563
  30.2 3.7 %for_pair.1 = bf16[2048,512]{1,0:T(8,128)(2,1)} custom-call(s32[16]{0:T(128)} %adapters.8, s32[1]{0:T(128)} %bitcast.place, bf16[1024,512]{1,0:T(8,128)(2,1)} %refs_16_.1, bf16[64,128,512]{2,1,0:T(8,128)(2,1)} %refs_15_.1), custom_call_target="tpu_custom_call" | custom-call | tf_op jit(solution)/shard_map/for_pair/pallas_call | solution.py:83
  33.9 1.6 collective-permute-start.6
  35.5 2.0 %collective-permute-start.5 = (bf16[1,128,1024]{2,1,0:T(8,128)(2,1)S(1)}, bf16[1,128,1024]{2,1,0:T(8,128)(2,1)S(1)}, u32[]{:S(2)}, u32[]{:S(2)}) collective-permute-start(bf16[1,128,1024]{2,1,0:T(8,128)(2,1)S(1)} %collective-permute-done.refs_1_.refs_2_.refs_3_), channel_id=1, source_target_pairs={{0,4},{1,5},{2,6},{3,7},{4,0},{5,1},{6,2},{7,3},{8,12},{9,13},{10,... | collective-permute-start | bytes 786440 | tf_op jit(solution)/shard_map/ppermute | solution.py:570
  37.5 2.5 %back_low.1 = bf16[1,128,128]{2,1,0:T(8,128)(2,1)} custom-call(s32[16]{0:T(128)} %adapters.8, s32[1]{0:T(128)} %bitcast.place, s32[64]{0:T(128)} %ranks.5, bf16[128,1024]{1,0:T(8,128)(2,1)} %gradient.1, bf16[1024,128]{1,0:T(8,128)(2,1)} %bitcast.9), custom_call_target="tpu_custom_call" | custom-call | tf_op jit(solution)/shard_map/back_low/pallas_call | solution.py:60
  40.0 32.7 %collective-permute-done.5.refs_3_.refs_6_.refs_7_ = bf16[1,128,1024]{2,1,0:T(8,128)(2,1)S(1)} collective-permute-done((bf16[1,128,1024]{2,1,0:T(8,128)(2,1)S(1)}, bf16[1,128,1024]{2,1,0:T(8,128)(2,1)S(1)}, u32[]{:S(2)}, u32[]{:S(2)}) %collective-permute-start.5) | collective-permute-done | bytes 262176 | tf_op jit(solution)/shard_map/ppermute | solution.py:570
  72.7 9.6 %collective-permute-done.6.pair = bf16[2048,512]{1,0:T(8,128)(2,1)} collective-permute-done((bf16[2048,512]{1,0:T(8,128)(2,1)}, bf16[2048,512]{1,0:T(8,128)(2,1)}, u32[]{:S(2)}, u32[]{:S(2)}) %collective-permute-start.6) | collective-permute-done | bytes 2097184 | tf_op jit(solution)/shard_map/ppermute | solution.py:570
  82.3 1.3 copy-done
  83.6 4.6 %hidden_parts.1.total = f32[8,128,128]{2,1,0:T(8,128)} custom-call(s32[16]{0:T(128)} %adapters.8, s32[1]{0:T(128)} %bitcast.place, bf16[2048,512]{1,0:T(8,128)(2,1)} %collective-permute-done.6.pair, bf16[8,2,128,512]{3,2,1,0:T(8,128)(2,1)} %copy-done, bf16[64,128,512]{2,1,0:T(8,128)(2,1)} %refs_15_.1, bf16[64,128,512]{2,1,0:T(8,128)(2,1)} %refs_15_.1, ...), custom_call_target="tpu_custom_call" | custom-call | tf_op jit(solution)/shard_map/hidden_parts/pallas_call | solution.py:60
  88.2 1.0 slice.4
  89.3 3.5 %collective-permute-start.12 = (bf16[1,128,128]{2,1,0:T(8,128)(2,1)S(1)}, bf16[1,128,128]{2,1,0:T(8,128)(2,1)S(1)}, u32[]{:S(2)}, u32[]{:S(2)}) collective-permute-start(bf16[1,128,128]{2,1,0:T(8,128)(2,1)S(1)} %copy-done.16), channel_id=1, source_target_pairs={{0,12},{1,13},{2,14},{3,15},{4,8},{5,9},{6,10},{7,11},{8,4},{9,5},... | collective-permute-start | bytes 98312 | tf_op jit(solution)/shard_map/ppermute | solution.py:570
  92.8 0.9 collective-permute-start.10
  93.8 1.6 collective-permute-done.12
  95.4 1.7 collective-permute-done.11
  97.7 0.7 copy-done.21
  98.4 1.8 slot_sums.2.total
  100.2 2.0 %collective-permute-start.8 = (f32[4,128,128]{2,1,0:T(8,128)}, f32[4,128,128]{2,1,0:T(8,128)S(1)}, u32[]{:S(2)}, u32[]{:S(2)}) collective-permute-start(f32[4,128,128]{2,1,0:T(8,128)} %slot_sums.2.total), channel_id=1, source_target_pairs={{0,4},{1,5},{2,6},{3,7},{4,0},{5,1},{6,2},{7,3},{8,12},{9,13},{10,... | collective-permute-start | bytes 786440 | tf_op jit(solution)/shard_map/ppermute | solution.py:570
  102.7 5.0 %collective-permute-done.8.received = f32[4,128,128]{2,1,0:T(8,128)S(1)} collective-permute-done((f32[4,128,128]{2,1,0:T(8,128)}, f32[4,128,128]{2,1,0:T(8,128)S(1)}, u32[]{:S(2)}, u32[]{:S(2)}) %collective-permute-start.8) | collective-permute-done | bytes 262176 | tf_op jit(solution)/shard_map/ppermute | solution.py:570
  107.7 0.7 copy-done.20
  108.4 1.8 slot_sums.3
  110.2 1.5 collective-permute-start.9
  111.7 0.7 copy-done.9
  112.4 0.7 copy-done.8
  113.1 7.8 %input_slices.1 = bf16[8,2,128,512]{3,2,1,0:T(8,128)(2,1)} custom-call(s32[16]{0:T(128)} %adapters.8, s32[1]{0:T(128)} %bitcast.place, bf16[8,128,128]{2,1,0:T(8,128)(2,1)} %copy-done.9, bf16[2048,512]{1,0:T(8,128)(2,1)} %collective-permute-done.6.pair, bf16[1,128,1024]{2,1,0:T(8,128)(2,1)} %bitcast.6, bf16[1,128,1024]{2,1,0:T(8,128)(2,1)} %copy-done.3, ...), custom_call_target="tpu_custom_call" | custom-call | tf_op jit(solution)/shard_map/input_slices/pallas_call | solution.py:60
  121.6 3.8 %all-to-all-start.2 = ((bf16[8,2,128,512]{3,2,1,0:T(8,128)(2,1)}), bf16[8,2,128,512]{3,2,1,0:T(8,128)(2,1)S(1)}, u32[]{:S(2)}, u32[]{:S(2)}) async-start(bf16[8,2,128,512]{3,2,1,0:T(8,128)(2,1)} %input_slices.1), calls=%async_computation.2 | async-start | bytes 4194304 | tf_op jit(solution)/shard_map/all_to_all | solution.py:563
  125.4 2.3 %pair_tokens.1 = (bf16[4,128,512]{2,1,0:T(8,128)(2,1)}, bf16[4,128,512]{2,1,0:T(8,128)(2,1)}) custom-call(bf16[8,2,128,512]{3,2,1,0:T(8,128)(2,1)} %copy-done), custom_call_target="tpu_custom_call" | custom-call | tf_op jit(solution)/shard_map/pair_tokens/pallas_call | solution.py:60
  127.6 1.5 collective-permute-start.19
  129.6 2.4 %hidden_low.1 = bf16[4,128,128]{2,1,0:T(8,128)(2,1)} custom-call(s32[16]{0:T(128)} %adapters.8, s32[1]{0:T(128)} %bitcast.place, s32[64]{0:T(128)} %ranks.5, f32[4,128,128]{2,1,0:T(8,128)} %get-tuple-element.65.total, bf16[4,128,128]{2,1,0:T(8,128)(2,1)} %copy-done.22), custom_call_target="tpu_custom_call" | custom-call | tf_op jit(solution)/shard_map/hidden_low/pallas_call | solution.py:60
  132.0 1.9 %gradient_columns.1 = (bf16[8,128,128]{2,1,0:T(8,128)(2,1)}, bf16[8,128,128]{2,1,0:T(8,128)(2,1)}) custom-call(s32[1]{0:T(128)} %bitcast.place, bf16[1,128,1024]{2,1,0:T(8,128)(2,1)} %bitcast.7, bf16[1,128,1024]{2,1,0:T(8,128)(2,1)} %bitcast.8, bf16[1,128,1024]{2,1,0:T(8,128)(2,1)} %copy-done.3, bf16[1,128,1024]{2,1,0:T(8,128)(2,1)} %copy-done.3, ...), custom_call_target="tpu_custom_call" | custom-call | tf_op jit(solution)/shard_map/gradient_columns/pallas_call | solution.py:60
  134.0 1.5 collective-permute-start.15
  136.1 1.5 collective-permute-start.18
  137.7 21.8 %collective-permute-done.15.gradients_pair = bf16[8,128,128]{2,1,0:T(8,128)(2,1)S(1)} collective-permute-done((bf16[8,128,128]{2,1,0:T(8,128)(2,1)}, bf16[8,128,128]{2,1,0:T(8,128)(2,1)S(1)}, u32[]{:S(2)}, u32[]{:S(2)}) %collective-permute-start.15) | collective-permute-done | bytes 262176 | tf_op jit(solution)/shard_map/ppermute | solution.py:570
  159.4 5.6 %collective-permute-done.17.hiddens_pair = bf16[8,128,128]{2,1,0:T(8,128)(2,1)S(1)} collective-permute-done((bf16[8,128,128]{2,1,0:T(8,128)(2,1)S(1)}, bf16[8,128,128]{2,1,0:T(8,128)(2,1)S(1)}, u32[]{:S(2)}, u32[]{:S(2)}) %collective-permute-start.17) | collective-permute-done | bytes 262176 | tf_op jit(solution)/shard_map/ppermute | solution.py:570
  165.0 0.7 copy-done.19
  165.7 4.5 %up_gradients.1 = bf16[64,64,128]{2,1,0:T(8,128)(2,1)} custom-call(s32[16]{0:T(128)} %adapters.8, s32[1]{0:T(128)} %bitcast.place, s32[64]{0:T(128)} %ranks.5, bf16[8,128,128]{2,1,0:T(8,128)(2,1)} %get-tuple-element.63.gradients, bf16[8,128,128]{2,1,0:T(8,128)(2,1)} %copy-done.18, bf16[8,128,128]{2,1,0:T(8,128)(2,1)} %copy-done.11, ...), custom_call_target="tpu_custom_call" | custom-call | tf_op jit(solution)/shard_map/up_gradients/pallas_call | solution.py:433
  171.2 0.8 copy-done.14
  172.0 9.4 %down_gradients.1 = bf16[64,128,512]{2,1,0:T(8,128)(2,1)} custom-call(s32[16]{0:T(128)} %adapters.8, s32[1]{0:T(128)} %bitcast.place, bf16[8,128,128]{2,1,0:T(8,128)(2,1)} %copy-done.9, bf16[8,128,128]{2,1,0:T(8,128)(2,1)} %copy-done.17, bf16[8,2,128,512]{3,2,1,0:T(8,128)(2,1)} %copy-done, bf16[4,128,512]{2,1,0:T(8,128)(2,1)} %copy-done.13, ...), custom_call_target="tpu_custom_call" | custom-call | tf_op jit(solution)/shard_map/down_gradients/pallas_call | solution.py:433
  181.4 1.3 copy-done.1
  182.7 3.0 %join_columns.1 = bf16[128,8192]{1,0:T(8,128)(2,1)} custom-call(s32[1]{0:T(128)} %bitcast.place, bf16[8,2,128,512]{3,2,1,0:T(8,128)(2,1)} %copy-done.1), custom_call_target="tpu_custom_call" | custom-call | tf_op jit(solution)/shard_map/join_columns/pallas_call | solution.py:366
  (68 shorter events, 4.4 us)
Async XLA Ops:
  0.6 15.4 %collective-permute-start.1 = (bf16[1,128,1024]{2,1,0:T(8,128)(2,1)}, bf16[1,128,1024]{2,1,0:T(8,128)(2,1)S(1)}, u32[]{:S(2)}, u32[]{:S(2)}) collective-permute-start(bf16[1,128,1024]{2,1,0:T(8,128)(2,1)} %bitcast.3), channel_id=1, source_target_pairs={{0,4},{1,5},{2,6},{3,7},{4,0},{5,1},{6,2},{7,3},{8,12},{9,13},{10,... | collective-permute-start | bytes 786440 | tf_op jit(solution)/shard_map/ppermute | solution.py:570
  3.7 15.4 %collective-permute-start = (bf16[1,128,1024]{2,1,0:T(8,128)(2,1)}, bf16[1,128,1024]{2,1,0:T(8,128)(2,1)S(1)}, u32[]{:S(2)}, u32[]{:S(2)}) collective-permute-start(bf16[1,128,1024]{2,1,0:T(8,128)(2,1)} %bitcast.4), channel_id=1, source_target_pairs={{0,8},{1,9},{2,10},{3,11},{4,12},{5,13},{6,14},{7,15},{8,0},{9,1},... | collective-permute-start | bytes 786440 | tf_op jit(solution)/shard_map/ppermute | solution.py:570
  8.7 15.0 %all-to-all-start = ((bf16[16,64,128]{2,1,0:T(8,128)(2,1)}), bf16[16,64,128]{2,1,0:T(8,128)(2,1)S(1)}, u32[]{:S(2)}, u32[]{:S(2)}) async-start(bf16[16,64,128]{2,1,0:T(8,128)(2,1)} %gather_up.1), calls=%async_computation | async-start | bytes 524288 | tf_op jit(solution)/shard_map/all_to_all | solution.py:557
  12.3 10.0 %collective-permute-start.2 = (bf16[1,128,1024]{2,1,0:T(8,128)(2,1)}, bf16[1,128,1024]{2,1,0:T(8,128)(2,1)S(1)}, u32[]{:S(2)}, u32[]{:S(2)}) collective-permute-start(bf16[1,128,1024]{2,1,0:T(8,128)(2,1)} %bitcast.5), channel_id=1, source_target_pairs={{0,1},{1,0},{2,3},{3,2},{4,5},{5,4},{6,7},{7,6},{8,9},{9,8},{10,11... | collective-permute-start | bytes 786440 | tf_op jit(solution)/shard_map/ppermute | solution.py:570
  16.1 6.2 %copy-start.2 = (bf16[1,128,1024]{2,1,0:T(8,128)(2,1)}, bf16[1,128,1024]{2,1,0:T(8,128)(2,1)S(1)}, u32[]{:S(2)}) copy-start(bf16[1,128,1024]{2,1,0:T(8,128)(2,1)S(1)} %collective-permute-done.1.refs_2_.refs_4_.refs_5_) | copy-start | bytes 786436
  16.1 7.6 %collective-permute-start.4 = (bf16[1,128,1024]{2,1,0:T(8,128)(2,1)S(1)}, bf16[1,128,1024]{2,1,0:T(8,128)(2,1)S(1)}, u32[]{:S(2)}, u32[]{:S(2)}) collective-permute-start(bf16[1,128,1024]{2,1,0:T(8,128)(2,1)S(1)} %collective-permute-done.1.refs_2_.refs_4_.refs_5_), channel_id=1, source_target_pairs={{0,1},{1,0},{2,3},{3,2},{4,5},{5,4},{6,7},{7,6},{8,9},{9,8},{10,11... | collective-permute-start | bytes 786440 | tf_op jit(solution)/shard_map/ppermute | solution.py:570
  19.1 16.4 %copy-start.3 = (bf16[1,128,1024]{2,1,0:T(8,128)(2,1)}, bf16[1,128,1024]{2,1,0:T(8,128)(2,1)S(1)}, u32[]{:S(2)}) copy-start(bf16[1,128,1024]{2,1,0:T(8,128)(2,1)S(1)} %collective-permute-done.refs_1_.refs_2_.refs_3_) | copy-start | bytes 786436
  19.1 4.6 %collective-permute-start.3 = (bf16[1,128,1024]{2,1,0:T(8,128)(2,1)S(1)}, bf16[1,128,1024]{2,1,0:T(8,128)(2,1)S(1)}, u32[]{:S(2)}, u32[]{:S(2)}) collective-permute-start(bf16[1,128,1024]{2,1,0:T(8,128)(2,1)S(1)} %collective-permute-done.refs_1_.refs_2_.refs_3_), channel_id=1, source_target_pairs={{0,1},{1,0},{2,3},{3,2},{4,5},{5,4},{6,7},{7,6},{8,9},{9,8},{10,11... | collective-permute-start | bytes 786440 | tf_op jit(solution)/shard_map/ppermute | solution.py:570
  22.3 2.1 %copy-start.4 = (bf16[1,128,1024]{2,1,0:T(8,128)(2,1)}, bf16[1,128,1024]{2,1,0:T(8,128)(2,1)S(1)}, u32[]{:S(2)}) copy-start(bf16[1,128,1024]{2,1,0:T(8,128)(2,1)S(1)} %collective-permute-done.2.refs_4_.refs_8_.refs_9_) | copy-start | bytes 786436
  23.7 0.7 copy-start.12
  23.7 0.8 copy-start.5
  23.7 0.9 copy-start.6
  24.6 57.7 %all-to-all-start.1 = ((bf16[8,2,128,512]{3,2,1,0:T(8,128)(2,1)}), bf16[8,2,128,512]{3,2,1,0:T(8,128)(2,1)S(1)}, u32[]{:S(2)}, u32[]{:S(2)}) async-start(bf16[8,2,128,512]{3,2,1,0:T(8,128)(2,1)} %pack_tokens.1), calls=%async_computation.1 | async-start | bytes 4194304 | tf_op jit(solution)/shard_map/all_to_all | solution.py:563
  33.9 48.4 %collective-permute-start.6 = (bf16[2048,512]{1,0:T(8,128)(2,1)}, bf16[2048,512]{1,0:T(8,128)(2,1)}, u32[]{:S(2)}, u32[]{:S(2)}) collective-permute-start(bf16[2048,512]{1,0:T(8,128)(2,1)} %for_pair.1), channel_id=1, source_target_pairs={{0,2},{1,3},{2,0},{3,1},{4,6},{5,7},{6,4},{7,5},{8,10},{9,11},{10,... | collective-permute-start | bytes 6291464 | tf_op jit(solution)/shard_map/ppermute | solution.py:570
  35.5 37.3 %collective-permute-start.5 = (bf16[1,128,1024]{2,1,0:T(8,128)(2,1)S(1)}, bf16[1,128,1024]{2,1,0:T(8,128)(2,1)S(1)}, u32[]{:S(2)}, u32[]{:S(2)}) collective-permute-start(bf16[1,128,1024]{2,1,0:T(8,128)(2,1)S(1)} %collective-permute-done.refs_1_.refs_2_.refs_3_), channel_id=1, source_target_pairs={{0,4},{1,5},{2,6},{3,7},{4,0},{5,1},{6,2},{7,3},{8,12},{9,13},{10,... | collective-permute-start | bytes 786440 | tf_op jit(solution)/shard_map/ppermute | solution.py:570
  40.0 49.3 %copy-start.16 = (bf16[1,128,128]{2,1,0:T(8,128)(2,1)S(1)}, bf16[1,128,128]{2,1,0:T(8,128)(2,1)}, u32[]{:S(2)}) copy-start(bf16[1,128,128]{2,1,0:T(8,128)(2,1)} %back_low.1) | copy-start | bytes 98308
  72.7 29.5 %copy-start.7 = (bf16[1,128,1024]{2,1,0:T(8,128)(2,1)}, bf16[1,128,1024]{2,1,0:T(8,128)(2,1)S(1)}, u32[]{:S(2)}) copy-start(bf16[1,128,1024]{2,1,0:T(8,128)(2,1)S(1)} %collective-permute-done.5.refs_3_.refs_6_.refs_7_) | copy-start | bytes 786436
  82.3 1.3 copy-start
  89.2 8.5 %collective-permute-start.7 = (f32[4,128,128]{2,1,0:T(8,128)S(1)}, f32[4,128,128]{2,1,0:T(8,128)S(1)}, u32[]{:S(2)}, u32[]{:S(2)}) collective-permute-start(f32[4,128,128]{2,1,0:T(8,128)S(1)} %slice.4), channel_id=1, source_target_pairs={{0,1},{1,0},{2,3},{3,2},{4,5},{5,4},{6,7},{7,6},{8,9},{9,8},{10,11... | collective-permute-start | bytes 786440 | tf_op jit(solution)/shard_map/ppermute | solution.py:570
  89.3 6.1 %collective-permute-start.12 = (bf16[1,128,128]{2,1,0:T(8,128)(2,1)S(1)}, bf16[1,128,128]{2,1,0:T(8,128)(2,1)S(1)}, u32[]{:S(2)}, u32[]{:S(2)}) collective-permute-start(bf16[1,128,128]{2,1,0:T(8,128)(2,1)S(1)} %copy-done.16), channel_id=1, source_target_pairs={{0,12},{1,13},{2,14},{3,15},{4,8},{5,9},{6,10},{7,11},{8,4},{9,5},... | collective-permute-start | bytes 98312 | tf_op jit(solution)/shard_map/ppermute | solution.py:570
  92.8 4.3 %collective-permute-start.11 = (bf16[1,128,128]{2,1,0:T(8,128)(2,1)S(1)}, bf16[1,128,128]{2,1,0:T(8,128)(2,1)S(1)}, u32[]{:S(2)}, u32[]{:S(2)}) collective-permute-start(bf16[1,128,128]{2,1,0:T(8,128)(2,1)S(1)} %copy-done.16), channel_id=1, source_target_pairs={{0,4},{1,5},{2,6},{3,7},{4,0},{5,1},{6,2},{7,3},{8,12},{9,13},{10,... | collective-permute-start | bytes 98312 | tf_op jit(solution)/shard_map/ppermute | solution.py:570
  92.8 4.8 %collective-permute-start.10 = (bf16[1,128,128]{2,1,0:T(8,128)(2,1)S(1)}, bf16[1,128,128]{2,1,0:T(8,128)(2,1)S(1)}, u32[]{:S(2)}, u32[]{:S(2)}) collective-permute-start(bf16[1,128,128]{2,1,0:T(8,128)(2,1)S(1)} %copy-done.16), channel_id=1, source_target_pairs={{0,8},{1,9},{2,10},{3,11},{4,12},{5,13},{6,14},{7,15},{8,0},{9,1},... | collective-permute-start | bytes 98312 | tf_op jit(solution)/shard_map/ppermute | solution.py:570
  97.7 0.7 copy-start.21
  100.2 7.5 %collective-permute-start.8 = (f32[4,128,128]{2,1,0:T(8,128)}, f32[4,128,128]{2,1,0:T(8,128)S(1)}, u32[]{:S(2)}, u32[]{:S(2)}) collective-permute-start(f32[4,128,128]{2,1,0:T(8,128)} %slot_sums.2.total), channel_id=1, source_target_pairs={{0,4},{1,5},{2,6},{3,7},{4,0},{5,1},{6,2},{7,3},{8,12},{9,13},{10,... | collective-permute-start | bytes 786440 | tf_op jit(solution)/shard_map/ppermute | solution.py:570
  102.2 9.5 %collective-permute-start.13 = (bf16[4,128,128]{2,1,0:T(8,128)(2,1)S(1)}, bf16[4,128,128]{2,1,0:T(8,128)(2,1)S(1)}, u32[]{:S(2)}, u32[]{:S(2)}) collective-permute-start(bf16[4,128,128]{2,1,0:T(8,128)(2,1)S(1)} %pad_maximum_fusion.1), channel_id=1, source_target_pairs={{0,1},{1,0},{2,3},{3,2},{4,5},{5,4},{6,7},{7,6},{8,9},{9,8},{10,11... | collective-permute-start | bytes 393224 | tf_op jit(solution)/shard_map/ppermute | solution.py:570
  102.2 9.5 %collective-permute-start.14 = (bf16[1,128,1024]{2,1,0:T(8,128)(2,1)S(1)}, bf16[1,128,1024]{2,1,0:T(8,128)(2,1)S(1)}, u32[]{:S(2)}, u32[]{:S(2)}) collective-permute-start(bf16[1,128,1024]{2,1,0:T(8,128)(2,1)S(1)} %collective-permute-done.5.refs_3_.refs_6_.refs_7_), channel_id=1, source_target_pairs={{0,1},{1,0},{2,3},{3,2},{4,5},{5,4},{6,7},{7,6},{8,9},{9,8},{10,11... | collective-permute-start | bytes 786440 | tf_op jit(solution)/shard_map/ppermute | solution.py:570
  107.7 0.7 copy-start.20
  110.2 10.7 %collective-permute-start.9 = (bf16[4,128,128]{2,1,0:T(8,128)(2,1)}, bf16[4,128,128]{2,1,0:T(8,128)(2,1)S(1)}, u32[]{:S(2)}, u32[]{:S(2)}) collective-permute-start(bf16[4,128,128]{2,1,0:T(8,128)(2,1)} %get-tuple-element.46), channel_id=1, source_target_pairs={{0,8},{1,9},{2,10},{3,11},{4,12},{5,13},{6,14},{7,15},{8,0},{9,1},... | collective-permute-start | bytes 393224 | tf_op jit(solution)/shard_map/ppermute | solution.py:570
  111.7 0.7 copy-start.9
  112.4 0.7 copy-start.8
  120.9 0.7 copy-start.22
  121.6 59.8 %all-to-all-start.2 = ((bf16[8,2,128,512]{3,2,1,0:T(8,128)(2,1)}), bf16[8,2,128,512]{3,2,1,0:T(8,128)(2,1)S(1)}, u32[]{:S(2)}, u32[]{:S(2)}) async-start(bf16[8,2,128,512]{3,2,1,0:T(8,128)(2,1)} %input_slices.1), calls=%async_computation.2 | async-start | bytes 4194304 | tf_op jit(solution)/shard_map/all_to_all | solution.py:563
  127.6 42.6 %collective-permute-start.19 = (bf16[4,128,512]{2,1,0:T(8,128)(2,1)}, bf16[4,128,512]{2,1,0:T(8,128)(2,1)S(1)}, u32[]{:S(2)}, u32[]{:S(2)}) collective-permute-start(bf16[4,128,512]{2,1,0:T(8,128)(2,1)} %get-tuple-element.69), channel_id=1, source_target_pairs={{0,2},{1,3},{2,0},{3,1},{4,6},{5,7},{6,4},{7,5},{8,10},{9,11},{10,... | collective-permute-start | bytes 1572872 | tf_op jit(solution)/shard_map/ppermute | solution.py:570
  129.2 41.1 %collective-permute-start.20 = (bf16[4,128,512]{2,1,0:T(8,128)(2,1)}, bf16[4,128,512]{2,1,0:T(8,128)(2,1)S(1)}, u32[]{:S(2)}, u32[]{:S(2)}) collective-permute-start(bf16[4,128,512]{2,1,0:T(8,128)(2,1)} %get-tuple-element.70), channel_id=1, source_target_pairs={{0,2},{1,3},{2,0},{3,1},{4,6},{5,7},{6,4},{7,5},{8,10},{9,11},{10,... | collective-permute-start | bytes 1572872 | tf_op jit(solution)/shard_map/ppermute | solution.py:570
  132.0 3.5 %copy-start.15 = (bf16[4,128,128]{2,1,0:T(8,128)(2,1)S(1)}, bf16[4,128,128]{2,1,0:T(8,128)(2,1)}, u32[]{:S(2)}) copy-start(bf16[4,128,128]{2,1,0:T(8,128)(2,1)} %hidden_low.1) | copy-start | bytes 393220
  132.0 4.1 %copy-start.10 = (bf16[8,128,128]{2,1,0:T(8,128)(2,1)S(1)}, bf16[8,128,128]{2,1,0:T(8,128)(2,1)}, u32[]{:S(2)}) copy-start(bf16[8,128,128]{2,1,0:T(8,128)(2,1)} %copy-done.9) | copy-start | bytes 786436
  132.0 3.5 %collective-permute-start.16 = (bf16[4,128,128]{2,1,0:T(8,128)(2,1)}, bf16[4,128,128]{2,1,0:T(8,128)(2,1)S(1)}, u32[]{:S(2)}, u32[]{:S(2)}) collective-permute-start(bf16[4,128,128]{2,1,0:T(8,128)(2,1)} %hidden_low.1), channel_id=1, source_target_pairs={{0,1},{1,0},{2,3},{3,2},{4,5},{5,4},{6,7},{7,6},{8,9},{9,8},{10,11... | collective-permute-start | bytes 393224 | tf_op jit(solution)/shard_map/ppermute | solution.py:570
  134.0 25.4 %collective-permute-start.15 = (bf16[8,128,128]{2,1,0:T(8,128)(2,1)}, bf16[8,128,128]{2,1,0:T(8,128)(2,1)S(1)}, u32[]{:S(2)}, u32[]{:S(2)}) collective-permute-start(bf16[8,128,128]{2,1,0:T(8,128)(2,1)} %get-tuple-element.64), channel_id=1, source_target_pairs={{0,2},{1,3},{2,0},{3,1},{4,6},{5,7},{6,4},{7,5},{8,10},{9,11},{10,... | collective-permute-start | bytes 786440 | tf_op jit(solution)/shard_map/ppermute | solution.py:570
  135.5 30.2 %copy-start.11 = (bf16[8,128,128]{2,1,0:T(8,128)(2,1)}, bf16[8,128,128]{2,1,0:T(8,128)(2,1)S(1)}, u32[]{:S(2)}) copy-start(bf16[8,128,128]{2,1,0:T(8,128)(2,1)S(1)} %pad_maximum_fusion.hiddens) | copy-start | bytes 786436
  135.5 29.5 %collective-permute-start.17 = (bf16[8,128,128]{2,1,0:T(8,128)(2,1)S(1)}, bf16[8,128,128]{2,1,0:T(8,128)(2,1)S(1)}, u32[]{:S(2)}, u32[]{:S(2)}) collective-permute-start(bf16[8,128,128]{2,1,0:T(8,128)(2,1)S(1)} %pad_maximum_fusion.hiddens), channel_id=1, source_target_pairs={{0,2},{1,3},{2,0},{3,1},{4,6},{5,7},{6,4},{7,5},{8,10},{9,11},{10,... | collective-permute-start | bytes 786440 | tf_op jit(solution)/shard_map/ppermute | solution.py:570
  136.1 34.2 %collective-permute-start.18 = (bf16[8,128,128]{2,1,0:T(8,128)(2,1)S(1)}, bf16[8,128,128]{2,1,0:T(8,128)(2,1)S(1)}, u32[]{:S(2)}, u32[]{:S(2)}) collective-permute-start(bf16[8,128,128]{2,1,0:T(8,128)(2,1)S(1)} %copy-done.10), channel_id=1, source_target_pairs={{0,2},{1,3},{2,0},{3,1},{4,6},{5,7},{6,4},{7,5},{8,10},{9,11},{10,... | collective-permute-start | bytes 786440 | tf_op jit(solution)/shard_map/ppermute | solution.py:570
  159.4 5.6 %copy-start.18 = (bf16[8,128,128]{2,1,0:T(8,128)(2,1)}, bf16[8,128,128]{2,1,0:T(8,128)(2,1)S(1)}, u32[]{:S(2)}) copy-start(bf16[8,128,128]{2,1,0:T(8,128)(2,1)S(1)} %collective-permute-done.15.gradients_pair) | copy-start | bytes 786436
  165.0 0.7 copy-start.19
  170.3 0.7 copy-start.17
  170.3 0.9 copy-start.13
  171.2 0.8 copy-start.14
  181.4 1.3 copy-start.1

commit v19 on v18

--- a/solution.py
+++ b/solution.py
@@ -8,7 +8,7 @@
 from jax.sharding import PartitionSpec as P
 
 adapter_alpha = 32.0
-vmem_limit = 60 * 1024 * 1024
+vmem_limit = 48 * 1024 * 1024
 pair_bit = 2
 line_bit = 4
 
@@ -599,21 +599,23 @@
     packs = pack_tokens(place, tokens, members, width)
     firsts = [1 << step for step in range(steps - 1)]
     across = {slot: swap(gradients[slot], 1) for slot in [0] + firsts}
-    held, crossed, own_up, packs, adapters = barrier(
-        ([gradients[slot] for slot in firsts], across, own_up, packs, adapters)
+    pair = for_pair(adapters, place, value_weight, down_maps, members)
+    gradients[2], pair = barrier((gradients[2], pair))
+    pair = swap(pair, pair_bit)
+    held, crossed, own_up, packs = barrier(
+        ([gradients[slot] for slot in firsts], across, own_up, packs)
     )
     across = dict(crossed)
     for slot, block in zip(firsts, held):
         gradients[slot] = block
 
     arrived = exchange_side(packs)
-    pair = swap(for_pair(adapters, place, value_weight, down_maps, members), pair_bit)
     for step in range(1, steps - 1):
         for slot in range(1, 1 << step):
             gradients[slot + (1 << step)] = swap(gradients[slot], offsets[1 << step])
     backs = back_rows(adapters, place, ranks, output_gradient, own_up)
     backs = [backs] + [swap(backs, offset) for offset in offsets[1:lines]]
-    arrived, backs[0], gradients, pair = barrier((arrived, backs[0], gradients, pair))
+    arrived, backs, gradients, pair = barrier((arrived, backs, gradients, pair))
 
     parts = hidden_parts(adapters, place, down_maps, pair, arrived)
     for slot in range(lines):

time: 187 us -> 168 us (0.90)
  Pallas kernels: 51.2 us -> 30.3 us
    pallas_call x8, Pallas kernels: 25 us -> 11.5 us  [call(): pl.pallas_call(kernel, out_shape=out_shapes, grid_spec=pltpu.PrefetchScal...]
    pallas_call x3, Pallas kernels: 9.24 us -> 4.18 us  [copy_call(): pl.pallas_call(kernel, out_shape=out_shapes, grid_spec=pltpu.PrefetchScal...]
    ppermute x21, starting transfers between devices: 23.8 us -> 20.7 us  [swap(): return lax.ppermute(array, 'dp', [(i, i ^ flip) for i in range(devices)])]
    all_to_all x2, starting transfers between devices: 9.39 us -> 12.1 us  [exchange_side(): lax.all_to_all(pieces, 'dp', split_axis=0, concat_axis=0, axis_index_grou...]
    unnamed x50 -> x54, local copies, waits for them, and re-layouts: 9.41 us -> 11.9 us
    pallas_call x2, Pallas kernels: 13.9 us -> 11.6 us  [sums_call(): pl.pallas_call(kernel, out_shape=jax.ShapeDtypeStruct((num_adapters,) + p...]
    ppermute x21, waiting for transfers between devices: 85.1 us -> 87.1 us  [swap(): return lax.ppermute(array, 'dp', [(i, i ^ flip) for i in range(devices)])]
  transfers between devices with their start and end apart: 24 -> 24, of which waited for: 11 -> 10; matrix products, arithmetic and copies ran while one was open for 0% -> 1% of each run, Pallas kernels for 23% -> 15%
where the time goes in v19:
time: 168 us
  waiting for transfers between devices  87.1 us (52%)
  starting transfers between devices  37.1 us (22%)
  Pallas kernels  30.3 us (18%)
  local copies, waits for them, and re-layouts  11.9 us (7%)
    ppermute x21, waiting for transfers between devices, swap(): return lax.ppermute(array, 'dp', [(i, i ^ flip) for i in range(devices)])  87.1 us
    ppermute x21, starting transfers between devices, swap(): return lax.ppermute(array, 'dp', [(i, i ^ flip) for i in range(devices)])  20.7 us
    all_to_all x2, starting transfers between devices, exchange_side(): lax.all_to_all(pieces, 'dp', split_axis=0, concat_axis=0, axis_index_grou...  12.1 us
    unnamed x54, local copies, waits for them, and re-layouts  11.9 us
    pallas_call x2, Pallas kernels, sums_call(): pl.pallas_call(kernel, out_shape=jax.ShapeDtypeStruct((num_adapters,) + p...  11.6 us
    pallas_call x8, Pallas kernels, call(): pl.pallas_call(kernel, out_shape=out_shapes, grid_spec=pltpu.PrefetchScal...  11.5 us
    all_to_all x1, starting transfers between devices, exchange(): return lax.all_to_all(pieces, 'dp', split_axis=0, concat_axis=0, tiled=True)  4.21 us
    pallas_call x3, Pallas kernels, copy_call(): pl.pallas_call(kernel, out_shape=out_shapes, grid_spec=pltpu.PrefetchScal...  4.18 us
  transfers between devices with their start and end apart: 24, of which 10 were waited for; matrix products, arithmetic and copies ran while one was open for 1% of the time, Pallas kernels for 15%

profile of v19, /device:TPU:0, one launch (start us, length us, event | category | flops | bytes accessed | tf_op | source)
XLA Modules:
  0.0 167.5 jit_solution(7296643450517215233)
XLA Ops:
  0.6 3.1 %collective-permute-start.1 = (bf16[1,128,1024]{2,1,0:T(8,128)(2,1)}, bf16[1,128,1024]{2,1,0:T(8,128)(2,1)S(1)}, u32[]{:S(2)}, u32[]{:S(2)}) collective-permute-start(bf16[1,128,1024]{2,1,0:T(8,128)(2,1)} %bitcast.3), channel_id=1, source_target_pairs={{0,4},{1,5},{2,6},{3,7},{4,0},{5,1},{6,2},{7,3},{8,12},{9,13},{10,... | collective-permute-start | bytes 786440 | tf_op jit(solution)/shard_map/ppermute | solution.py:570
  3.7 2.6 %collective-permute-start = (bf16[1,128,1024]{2,1,0:T(8,128)(2,1)}, bf16[1,128,1024]{2,1,0:T(8,128)(2,1)}, u32[]{:S(2)}, u32[]{:S(2)}) collective-permute-start(bf16[1,128,1024]{2,1,0:T(8,128)(2,1)} %bitcast.4), channel_id=1, source_target_pairs={{0,8},{1,9},{2,10},{3,11},{4,12},{5,13},{6,14},{7,15},{8,0},{9,1},... | collective-permute-start | bytes 786440 | tf_op jit(solution)/shard_map/ppermute | solution.py:570
  6.3 1.2 copy-done.18
  7.5 0.7 copy-done.21
  8.2 1.8 %gather_up.1 = bf16[16,64,128]{2,1,0:T(8,128)(2,1)} custom-call(s32[16]{0:T(128)S(1)} %copy-done.21, bf16[64,64,128]{2,1,0:T(8,128)(2,1)S(1)} %copy-done.18), custom_call_target="tpu_custom_call" | custom-call | tf_op jit(solution)/shard_map/gather_up/pallas_call | solution.py:83
  10.0 4.2 %all-to-all-start = ((bf16[16,64,128]{2,1,0:T(8,128)(2,1)}), bf16[16,64,128]{2,1,0:T(8,128)(2,1)}, u32[]{:S(2)}, u32[]{:S(2)}) async-start(bf16[16,64,128]{2,1,0:T(8,128)(2,1)} %gather_up.1), calls=%async_computation | async-start | bytes 524288 | tf_op jit(solution)/shard_map/all_to_all | solution.py:557
  14.4 1.3 collective-permute-done.1.refs_2_.refs_4_.refs_5_
  15.7 2.8 %collective-permute-done.refs_1_.refs_2_.refs_3_ = bf16[1,128,1024]{2,1,0:T(8,128)(2,1)} collective-permute-done((bf16[1,128,1024]{2,1,0:T(8,128)(2,1)}, bf16[1,128,1024]{2,1,0:T(8,128)(2,1)}, u32[]{:S(2)}, u32[]{:S(2)}) %collective-permute-start) | collective-permute-done | bytes 262176 | tf_op jit(solution)/shard_map/ppermute | solution.py:570
  18.5 1.6 copy-done.14
  20.1 0.5 pack_tokens.1
  20.7 1.3 copy-done.3
  22.0 1.9 %for_pair.1 = bf16[2048,512]{1,0:T(8,128)(2,1)S(1)} custom-call(s32[16]{0:T(128)S(1)} %copy-done.22, s32[1]{0:T(128)} %bitcast.place, bf16[1024,512]{1,0:T(8,128)(2,1)S(1)} %copy-done.4, bf16[64,128,512]{2,1,0:T(8,128)(2,1)} %refs_15_.1), custom_call_target="tpu_custom_call" | custom-call | tf_op jit(solution)/shard_map/for_pair/pallas_call | solution.py:83
  23.9 1.3 copy-done.15
  25.3 7.8 %all-to-all-start.1 = ((bf16[8,2,128,512]{3,2,1,0:T(8,128)(2,1)}), bf16[8,2,128,512]{3,2,1,0:T(8,128)(2,1)S(1)}, u32[]{:S(2)}, u32[]{:S(2)}) async-start(bf16[8,2,128,512]{3,2,1,0:T(8,128)(2,1)} %copy-done.3), calls=%async_computation.1 | async-start | bytes 4194304 | tf_op jit(solution)/shard_map/all_to_all | solution.py:563
  33.1 1.5 collective-permute-start.9
  34.6 2.0 %collective-permute-start.8 = (bf16[1,128,1024]{2,1,0:T(8,128)(2,1)}, bf16[1,128,1024]{2,1,0:T(8,128)(2,1)S(1)}, u32[]{:S(2)}, u32[]{:S(2)}) collective-permute-start(bf16[1,128,1024]{2,1,0:T(8,128)(2,1)} %collective-permute-done.refs_1_.refs_2_.refs_3_), channel_id=1, source_target_pairs={{0,4},{1,5},{2,6},{3,7},{4,0},{5,1},{6,2},{7,3},{8,12},{9,13},{10,... | collective-permute-start | bytes 786440 | tf_op jit(solution)/shard_map/ppermute | solution.py:570
  36.6 1.7 %back_low.1 = bf16[1,128,128]{2,1,0:T(8,128)(2,1)S(1)} custom-call(s32[16]{0:T(128)S(1)} %copy-done.22, s32[1]{0:T(128)} %bitcast.place, s32[64]{0:T(128)S(1)} %copy-done.23, bf16[128,1024]{1,0:T(8,128)(2,1)S(1)} %copy-done.5, bf16[1024,128]{1,0:T(8,128)(2,1)} %bitcast.2.up), custom_call_target="tpu_custom_call" | custom-call | tf_op jit(solution)/shard_map/back_low/pallas_call | solution.py:60
  38.4 2.4 %collective-permute-start.7 = (bf16[1,128,128]{2,1,0:T(8,128)(2,1)S(1)}, bf16[1,128,128]{2,1,0:T(8,128)(2,1)S(1)}, u32[]{:S(2)}, u32[]{:S(2)}) collective-permute-start(bf16[1,128,128]{2,1,0:T(8,128)(2,1)S(1)} %back_low.1), channel_id=1, source_target_pairs={{0,12},{1,13},{2,14},{3,15},{4,8},{5,9},{6,10},{7,11},{8,4},{9,5},... | collective-permute-start | bytes 98312 | tf_op jit(solution)/shard_map/ppermute | solution.py:570
  40.8 0.6 collective-permute-start.6
  41.4 1.5 collective-permute-start.5
  42.8 36.0 %collective-permute-done.7 = bf16[1,128,128]{2,1,0:T(8,128)(2,1)S(1)} collective-permute-done((bf16[1,128,128]{2,1,0:T(8,128)(2,1)S(1)}, bf16[1,128,128]{2,1,0:T(8,128)(2,1)S(1)}, u32[]{:S(2)}, u32[]{:S(2)}) %collective-permute-start.7) | collective-permute-done | bytes 32800 | tf_op jit(solution)/shard_map/ppermute | solution.py:570
  78.8 6.2 %collective-permute-done.5 = bf16[1,128,128]{2,1,0:T(8,128)(2,1)S(1)} collective-permute-done((bf16[1,128,128]{2,1,0:T(8,128)(2,1)S(1)}, bf16[1,128,128]{2,1,0:T(8,128)(2,1)S(1)}, u32[]{:S(2)}, u32[]{:S(2)}) %collective-permute-start.5) | collective-permute-done | bytes 32800 | tf_op jit(solution)/shard_map/ppermute | solution.py:570
  85.0 0.7 copy-done.9
  85.7 1.3 copy-done
  87.0 1.6 copy-done.1
  88.6 2.6 %hidden_parts.1.total = f32[8,128,128]{2,1,0:T(8,128)S(1)} custom-call(s32[16]{0:T(128)S(1)} %copy-done.22, s32[1]{0:T(128)} %bitcast.place, bf16[2048,512]{1,0:T(8,128)(2,1)S(1)} %copy-done.1, bf16[8,2,128,512]{3,2,1,0:T(8,128)(2,1)S(1)} %all-to-all-done.1.tokens, bf16[64,128,512]{2,1,0:T(8,128)(2,1)} %refs_15_.1, bf16[64,128,512]{2,1,0:T(8,128)(2,1)} %refs_15_.1, ...), custom_call_target="tpu_custom_call" | custom-call | tf_op jit(solution)/shard_map/hidden_parts/pallas_call | solution.py:60
  91.4 1.5 collective-permute-done.10.received
  92.9 0.3 collective-permute-start.11
  93.2 0.5 collective-permute-start.14
  93.7 7.6 %collective-permute-done.11.received = f32[4,128,128]{2,1,0:T(8,128)S(1)} collective-permute-done((f32[4,128,128]{2,1,0:T(8,128)S(1)}, f32[4,128,128]{2,1,0:T(8,128)S(1)}, u32[]{:S(2)}, u32[]{:S(2)}) %collective-permute-start.11) | collective-permute-done | bytes 262176 | tf_op jit(solution)/shard_map/ppermute | solution.py:570
  101.4 0.8 constant_dynamic-update-slice_fusion.1
  102.3 5.6 %input_slices.1 = bf16[8,2,128,512]{3,2,1,0:T(8,128)(2,1)S(1)} custom-call(s32[16]{0:T(128)S(1)} %copy-done.22, s32[1]{0:T(128)} %bitcast.place, bf16[8,128,128]{2,1,0:T(8,128)(2,1)S(1)} %constant_dynamic-update-slice_fusion.backs, bf16[2048,512]{1,0:T(8,128)(2,1)} %copy-done, bf16[1,128,1024]{2,1,0:T(8,128)(2,1)S(1)} %bitcast.6, ...), custom_call_target="tpu_custom_call" | custom-call | tf_op jit(solution)/shard_map/input_slices/pallas_call | solution.py:60
  107.9 1.3 copy-done.2
  109.2 0.4 collective-permute-done.12.received
  109.6 4.3 %all-to-all-start.2 = ((bf16[8,2,128,512]{3,2,1,0:T(8,128)(2,1)}), bf16[8,2,128,512]{3,2,1,0:T(8,128)(2,1)}, u32[]{:S(2)}, u32[]{:S(2)}) async-start(bf16[8,2,128,512]{3,2,1,0:T(8,128)(2,1)} %copy-done.2), calls=%async_computation.2 | async-start | bytes 4194304 | tf_op jit(solution)/shard_map/all_to_all | solution.py:563
  114.1 1.6 collective-permute-start.19
  115.7 0.5 collective-permute-start.20
  116.2 0.6 hidden_low.1
  116.9 0.9 gradient_columns.1
  117.8 1.6 collective-permute-start.15
  119.5 0.6 collective-permute-start.17
  120.0 1.5 collective-permute-start.18
  121.5 24.2 %collective-permute-done.15.gradients_pair = bf16[8,128,128]{2,1,0:T(8,128)(2,1)S(1)} collective-permute-done((bf16[8,128,128]{2,1,0:T(8,128)(2,1)S(1)}, bf16[8,128,128]{2,1,0:T(8,128)(2,1)S(1)}, u32[]{:S(2)}, u32[]{:S(2)}) %collective-permute-start.15) | collective-permute-done | bytes 262176 | tf_op jit(solution)/shard_map/ppermute | solution.py:570
  145.7 5.6 %collective-permute-done.17.hiddens_pair = bf16[8,128,128]{2,1,0:T(8,128)(2,1)S(1)} collective-permute-done((bf16[8,128,128]{2,1,0:T(8,128)(2,1)S(1)}, bf16[8,128,128]{2,1,0:T(8,128)(2,1)S(1)}, u32[]{:S(2)}, u32[]{:S(2)}) %collective-permute-start.17) | collective-permute-done | bytes 262176 | tf_op jit(solution)/shard_map/ppermute | solution.py:570
  151.4 3.6 %up_gradients.1 = bf16[64,64,128]{2,1,0:T(8,128)(2,1)} custom-call(s32[16]{0:T(128)S(1)} %copy-done.22, s32[1]{0:T(128)} %bitcast.place, s32[64]{0:T(128)S(1)} %copy-done.23, bf16[8,128,128]{2,1,0:T(8,128)(2,1)S(1)} %get-tuple-element.71.gradients, bf16[8,128,128]{2,1,0:T(8,128)(2,1)S(1)} %collective-permute-done.15.gradients_pair, ...), custom_call_target="tpu_custom_call" | custom-call | tf_op jit(solution)/shard_map/up_gradients/pallas_call | solution.py:433
  154.9 1.5 collective-permute-done.18.backs_pair
  156.4 8.1 %down_gradients.1 = bf16[64,128,512]{2,1,0:T(8,128)(2,1)} custom-call(s32[16]{0:T(128)S(1)} %copy-done.22, s32[1]{0:T(128)} %bitcast.place, bf16[8,128,128]{2,1,0:T(8,128)(2,1)S(1)} %copy-done.17, bf16[8,128,128]{2,1,0:T(8,128)(2,1)S(1)} %collective-permute-done.18.backs_pair, bf16[8,2,128,512]{3,2,1,0:T(8,128)(2,1)S(1)} %all-to-all-done.1.tokens, ...), custom_call_target="tpu_custom_call" | custom-call | tf_op jit(solution)/shard_map/down_gradients/pallas_call | solution.py:433
  164.5 3.0 %join_columns.1 = bf16[128,8192]{1,0:T(8,128)(2,1)} custom-call(s32[1]{0:T(128)} %bitcast.place, bf16[8,2,128,512]{3,2,1,0:T(8,128)(2,1)} %all-to-all-done.2.source), custom_call_target="tpu_custom_call" | custom-call | tf_op jit(solution)/shard_map/join_columns/pallas_call | solution.py:366
  (72 shorter events, 0.8 us)
Async XLA Ops:
  0.6 15.1 %collective-permute-start.1 = (bf16[1,128,1024]{2,1,0:T(8,128)(2,1)}, bf16[1,128,1024]{2,1,0:T(8,128)(2,1)S(1)}, u32[]{:S(2)}, u32[]{:S(2)}) collective-permute-start(bf16[1,128,1024]{2,1,0:T(8,128)(2,1)} %bitcast.3), channel_id=1, source_target_pairs={{0,4},{1,5},{2,6},{3,7},{4,0},{5,1},{6,2},{7,3},{8,12},{9,13},{10,... | collective-permute-start | bytes 786440 | tf_op jit(solution)/shard_map/ppermute | solution.py:570
  3.7 14.8 %collective-permute-start = (bf16[1,128,1024]{2,1,0:T(8,128)(2,1)}, bf16[1,128,1024]{2,1,0:T(8,128)(2,1)}, u32[]{:S(2)}, u32[]{:S(2)}) collective-permute-start(bf16[1,128,1024]{2,1,0:T(8,128)(2,1)} %bitcast.4), channel_id=1, source_target_pairs={{0,8},{1,9},{2,10},{3,11},{4,12},{5,13},{6,14},{7,15},{8,0},{9,1},... | collective-permute-start | bytes 786440 | tf_op jit(solution)/shard_map/ppermute | solution.py:570
  6.3 1.2 copy-start.18
  10.0 15.3 %all-to-all-start = ((bf16[16,64,128]{2,1,0:T(8,128)(2,1)}), bf16[16,64,128]{2,1,0:T(8,128)(2,1)}, u32[]{:S(2)}, u32[]{:S(2)}) async-start(bf16[16,64,128]{2,1,0:T(8,128)(2,1)} %gather_up.1), calls=%async_computation | async-start | bytes 524288 | tf_op jit(solution)/shard_map/all_to_all | solution.py:557
  14.2 11.1 %collective-permute-start.2 = (bf16[1,128,1024]{2,1,0:T(8,128)(2,1)}, bf16[1,128,1024]{2,1,0:T(8,128)(2,1)}, u32[]{:S(2)}, u32[]{:S(2)}) collective-permute-start(bf16[1,128,1024]{2,1,0:T(8,128)(2,1)} %bitcast.5), channel_id=1, source_target_pairs={{0,1},{1,0},{2,3},{3,2},{4,5},{5,4},{6,7},{7,6},{8,9},{9,8},{10,11... | collective-permute-start | bytes 786440 | tf_op jit(solution)/shard_map/ppermute | solution.py:570
  15.7 4.9 %copy-start.6 = (bf16[1,128,1024]{2,1,0:T(8,128)(2,1)}, bf16[1,128,1024]{2,1,0:T(8,128)(2,1)S(1)}, u32[]{:S(2)}) copy-start(bf16[1,128,1024]{2,1,0:T(8,128)(2,1)S(1)} %collective-permute-done.1.refs_2_.refs_4_.refs_5_) | copy-start | bytes 786436
  15.7 9.5 %collective-permute-start.4 = (bf16[1,128,1024]{2,1,0:T(8,128)(2,1)S(1)}, bf16[1,128,1024]{2,1,0:T(8,128)(2,1)}, u32[]{:S(2)}, u32[]{:S(2)}) collective-permute-start(bf16[1,128,1024]{2,1,0:T(8,128)(2,1)S(1)} %collective-permute-done.1.refs_2_.refs_4_.refs_5_), channel_id=1, source_target_pairs={{0,1},{1,0},{2,3},{3,2},{4,5},{5,4},{6,7},{7,6},{8,9},{9,8},{10,11... | collective-permute-start | bytes 786440 | tf_op jit(solution)/shard_map/ppermute | solution.py:570
  18.5 6.7 %collective-permute-start.3 = (bf16[1,128,1024]{2,1,0:T(8,128)(2,1)}, bf16[1,128,1024]{2,1,0:T(8,128)(2,1)}, u32[]{:S(2)}, u32[]{:S(2)}) collective-permute-start(bf16[1,128,1024]{2,1,0:T(8,128)(2,1)} %collective-permute-done.refs_1_.refs_2_.refs_3_), channel_id=1, source_target_pairs={{0,1},{1,0},{2,3},{3,2},{4,5},{5,4},{6,7},{7,6},{8,9},{9,8},{10,11... | collective-permute-start | bytes 786440 | tf_op jit(solution)/shard_map/ppermute | solution.py:570
  18.5 1.6 copy-start.14
  20.1 1.8 %copy-start.4 = (bf16[1024,512]{1,0:T(8,128)(2,1)S(1)}, bf16[1024,512]{1,0:T(8,128)(2,1)}, u32[]{:S(2)}) copy-start(bf16[1024,512]{1,0:T(8,128)(2,1)} %refs_16_.1) | copy-start | bytes 3145732
  20.1 1.8 %copy-start.22 = (s32[16]{0:T(128)S(1)}, s32[16]{0:T(128)}, u32[]{:S(2)}) copy-start(s32[16]{0:T(128)} %adapters.15) | copy-start | bytes 196
  20.6 1.3 copy-start.3
  23.9 1.3 copy-start.15
  25.3 11.4 %copy-start.5 = (bf16[128,1024]{1,0:T(8,128)(2,1)S(1)}, bf16[128,1024]{1,0:T(8,128)(2,1)}, u32[]{:S(2)}) copy-start(bf16[128,1024]{1,0:T(8,128)(2,1)} %gradient.1) | copy-start | bytes 786436
  25.3 11.4 %copy-start.23 = (s32[64]{0:T(128)S(1)}, s32[64]{0:T(128)}, u32[]{:S(2)}) copy-start(s32[64]{0:T(128)} %ranks.5) | copy-start | bytes 772
  25.3 61.8 %all-to-all-start.1 = ((bf16[8,2,128,512]{3,2,1,0:T(8,128)(2,1)}), bf16[8,2,128,512]{3,2,1,0:T(8,128)(2,1)S(1)}, u32[]{:S(2)}, u32[]{:S(2)}) async-start(bf16[8,2,128,512]{3,2,1,0:T(8,128)(2,1)} %copy-done.3), calls=%async_computation.1 | async-start | bytes 4194304 | tf_op jit(solution)/shard_map/all_to_all | solution.py:563
  33.1 52.6 %collective-permute-start.9 = (bf16[2048,512]{1,0:T(8,128)(2,1)}, bf16[2048,512]{1,0:T(8,128)(2,1)S(1)}, u32[]{:S(2)}, u32[]{:S(2)}) collective-permute-start(bf16[2048,512]{1,0:T(8,128)(2,1)} %copy-done.15), channel_id=1, source_target_pairs={{0,2},{1,3},{2,0},{3,1},{4,6},{5,7},{6,4},{7,5},{8,10},{9,11},{10,... | collective-permute-start | bytes 6291464 | tf_op jit(solution)/shard_map/ppermute | solution.py:570
  34.6 50.4 %collective-permute-start.8 = (bf16[1,128,1024]{2,1,0:T(8,128)(2,1)}, bf16[1,128,1024]{2,1,0:T(8,128)(2,1)S(1)}, u32[]{:S(2)}, u32[]{:S(2)}) collective-permute-start(bf16[1,128,1024]{2,1,0:T(8,128)(2,1)} %collective-permute-done.refs_1_.refs_2_.refs_3_), channel_id=1, source_target_pairs={{0,4},{1,5},{2,6},{3,7},{4,0},{5,1},{6,2},{7,3},{8,12},{9,13},{10,... | collective-permute-start | bytes 786440 | tf_op jit(solution)/shard_map/ppermute | solution.py:570
  38.4 40.4 %collective-permute-start.7 = (bf16[1,128,128]{2,1,0:T(8,128)(2,1)S(1)}, bf16[1,128,128]{2,1,0:T(8,128)(2,1)S(1)}, u32[]{:S(2)}, u32[]{:S(2)}) collective-permute-start(bf16[1,128,128]{2,1,0:T(8,128)(2,1)S(1)} %back_low.1), channel_id=1, source_target_pairs={{0,12},{1,13},{2,14},{3,15},{4,8},{5,9},{6,10},{7,11},{8,4},{9,5},... | collective-permute-start | bytes 98312 | tf_op jit(solution)/shard_map/ppermute | solution.py:570
  40.8 38.0 %collective-permute-start.6 = (bf16[1,128,128]{2,1,0:T(8,128)(2,1)S(1)}, bf16[1,128,128]{2,1,0:T(8,128)(2,1)S(1)}, u32[]{:S(2)}, u32[]{:S(2)}) collective-permute-start(bf16[1,128,128]{2,1,0:T(8,128)(2,1)S(1)} %back_low.1), channel_id=1, source_target_pairs={{0,4},{1,5},{2,6},{3,7},{4,0},{5,1},{6,2},{7,3},{8,12},{9,13},{10,... | collective-permute-start | bytes 98312 | tf_op jit(solution)/shard_map/ppermute | solution.py:570
  41.4 43.7 %collective-permute-start.5 = (bf16[1,128,128]{2,1,0:T(8,128)(2,1)S(1)}, bf16[1,128,128]{2,1,0:T(8,128)(2,1)S(1)}, u32[]{:S(2)}, u32[]{:S(2)}) collective-permute-start(bf16[1,128,128]{2,1,0:T(8,128)(2,1)S(1)} %back_low.1), channel_id=1, source_target_pairs={{0,8},{1,9},{2,10},{3,11},{4,12},{5,13},{6,14},{7,15},{8,0},{9,1},... | collective-permute-start | bytes 98312 | tf_op jit(solution)/shard_map/ppermute | solution.py:570
  78.8 12.5 %copy-start.24 = (bf16[1,128,128]{2,1,0:T(8,128)(2,1)}, bf16[1,128,128]{2,1,0:T(8,128)(2,1)S(1)}, u32[]{:S(2)}) copy-start(bf16[1,128,128]{2,1,0:T(8,128)(2,1)S(1)} %collective-permute-done.7) | copy-start | bytes 98308
  85.0 0.7 copy-start.9
  85.7 1.3 copy-start
  87.0 1.6 copy-start.1
  88.6 4.5 %copy-start.10 = (bf16[1,128,1024]{2,1,0:T(8,128)(2,1)S(1)}, bf16[1,128,1024]{2,1,0:T(8,128)(2,1)}, u32[]{:S(2)}) copy-start(bf16[1,128,1024]{2,1,0:T(8,128)(2,1)} %copy-done.9) | copy-start | bytes 786436
  91.2 11.1 %copy-start.7 = (bf16[1,128,1024]{2,1,0:T(8,128)(2,1)S(1)}, bf16[1,128,1024]{2,1,0:T(8,128)(2,1)}, u32[]{:S(2)}) copy-start(bf16[1,128,1024]{2,1,0:T(8,128)(2,1)} %copy-done.6) | copy-start | bytes 786436
  91.2 1.6 collective-permute-start.10
  92.9 8.4 %collective-permute-start.11 = (f32[4,128,128]{2,1,0:T(8,128)S(1)}, f32[4,128,128]{2,1,0:T(8,128)S(1)}, u32[]{:S(2)}, u32[]{:S(2)}) collective-permute-start(f32[4,128,128]{2,1,0:T(8,128)S(1)} %slot_sums.2.total), channel_id=1, source_target_pairs={{0,4},{1,5},{2,6},{3,7},{4,0},{5,1},{6,2},{7,3},{8,12},{9,13},{10,... | collective-permute-start | bytes 786440 | tf_op jit(solution)/shard_map/ppermute | solution.py:570
  93.2 9.0 %collective-permute-start.13 = (bf16[4,128,128]{2,1,0:T(8,128)(2,1)S(1)}, bf16[4,128,128]{2,1,0:T(8,128)(2,1)S(1)}, u32[]{:S(2)}, u32[]{:S(2)}) collective-permute-start(bf16[4,128,128]{2,1,0:T(8,128)(2,1)S(1)} %pad_maximum_fusion.1), channel_id=1, source_target_pairs={{0,1},{1,0},{2,3},{3,2},{4,5},{5,4},{6,7},{7,6},{8,9},{9,8},{10,11... | collective-permute-start | bytes 393224 | tf_op jit(solution)/shard_map/ppermute | solution.py:570
  93.2 9.1 %collective-permute-start.14 = (bf16[1,128,1024]{2,1,0:T(8,128)(2,1)S(1)}, bf16[1,128,1024]{2,1,0:T(8,128)(2,1)S(1)}, u32[]{:S(2)}, u32[]{:S(2)}) collective-permute-start(bf16[1,128,1024]{2,1,0:T(8,128)(2,1)S(1)} %copy-done.10), channel_id=1, source_target_pairs={{0,1},{1,0},{2,3},{3,2},{4,5},{5,4},{6,7},{7,6},{8,9},{9,8},{10,11... | collective-permute-start | bytes 786440 | tf_op jit(solution)/shard_map/ppermute | solution.py:570
  101.3 0.9 copy-start.19
  101.3 8.3 %collective-permute-start.12 = (bf16[4,128,128]{2,1,0:T(8,128)(2,1)S(1)}, bf16[4,128,128]{2,1,0:T(8,128)(2,1)S(1)}, u32[]{:S(2)}, u32[]{:S(2)}) collective-permute-start(bf16[4,128,128]{2,1,0:T(8,128)(2,1)S(1)} %get-tuple-element.51), channel_id=1, source_target_pairs={{0,8},{1,9},{2,10},{3,11},{4,12},{5,13},{6,14},{7,15},{8,0},{9,1},... | collective-permute-start | bytes 393224 | tf_op jit(solution)/shard_map/ppermute | solution.py:570
  102.2 5.6 %copy-start.16 = (bf16[8,128,128]{2,1,0:T(8,128)(2,1)}, bf16[8,128,128]{2,1,0:T(8,128)(2,1)S(1)}, u32[]{:S(2)}) copy-start(bf16[8,128,128]{2,1,0:T(8,128)(2,1)S(1)} %constant_dynamic-update-slice_fusion.backs) | copy-start | bytes 786436
  102.3 5.6 %copy-start.12 = (bf16[1,128,1024]{2,1,0:T(8,128)(2,1)}, bf16[1,128,1024]{2,1,0:T(8,128)(2,1)S(1)}, u32[]{:S(2)}) copy-start(bf16[1,128,1024]{2,1,0:T(8,128)(2,1)S(1)} %collective-permute-done.14.refs_7_.refs_14_.refs_15_) | copy-start | bytes 786436
  107.9 1.3 copy-start.2
  109.6 54.9 %all-to-all-start.2 = ((bf16[8,2,128,512]{3,2,1,0:T(8,128)(2,1)}), bf16[8,2,128,512]{3,2,1,0:T(8,128)(2,1)}, u32[]{:S(2)}, u32[]{:S(2)}) async-start(bf16[8,2,128,512]{3,2,1,0:T(8,128)(2,1)} %copy-done.2), calls=%async_computation.2 | async-start | bytes 4194304 | tf_op jit(solution)/shard_map/all_to_all | solution.py:563
  113.9 2.2 %copy-start.20 = (f32[4,128,128]{2,1,0:T(8,128)S(1)}, f32[4,128,128]{2,1,0:T(8,128)}, u32[]{:S(2)}) copy-start(f32[4,128,128]{2,1,0:T(8,128)} %copy-done.19) | copy-start | bytes 786436
  114.0 2.9 %copy-start.8 = (bf16[1,128,1024]{2,1,0:T(8,128)(2,1)S(1)}, bf16[1,128,1024]{2,1,0:T(8,128)(2,1)}, u32[]{:S(2)}) copy-start(bf16[1,128,1024]{2,1,0:T(8,128)(2,1)} %copy-done.6) | copy-start | bytes 786436
  114.0 2.9 %copy-start.11 = (bf16[1,128,1024]{2,1,0:T(8,128)(2,1)S(1)}, bf16[1,128,1024]{2,1,0:T(8,128)(2,1)}, u32[]{:S(2)}) copy-start(bf16[1,128,1024]{2,1,0:T(8,128)(2,1)} %copy-done.9) | copy-start | bytes 786436
  114.0 2.9 %copy-start.13 = (bf16[1,128,1024]{2,1,0:T(8,128)(2,1)S(1)}, bf16[1,128,1024]{2,1,0:T(8,128)(2,1)}, u32[]{:S(2)}) copy-start(bf16[1,128,1024]{2,1,0:T(8,128)(2,1)} %copy-done.12) | copy-start | bytes 786436
  114.1 42.4 %collective-permute-start.19 = (bf16[4,128,512]{2,1,0:T(8,128)(2,1)S(1)}, bf16[4,128,512]{2,1,0:T(8,128)(2,1)S(1)}, u32[]{:S(2)}, u32[]{:S(2)}) collective-permute-start(bf16[4,128,512]{2,1,0:T(8,128)(2,1)S(1)} %get-tuple-element.77), channel_id=1, source_target_pairs={{0,2},{1,3},{2,0},{3,1},{4,6},{5,7},{6,4},{7,5},{8,10},{9,11},{10,... | collective-permute-start | bytes 1572872 | tf_op jit(solution)/shard_map/ppermute | solution.py:570
  115.7 40.8 %collective-permute-start.20 = (bf16[4,128,512]{2,1,0:T(8,128)(2,1)S(1)}, bf16[4,128,512]{2,1,0:T(8,128)(2,1)S(1)}, u32[]{:S(2)}, u32[]{:S(2)}) collective-permute-start(bf16[4,128,512]{2,1,0:T(8,128)(2,1)S(1)} %get-tuple-element.78), channel_id=1, source_target_pairs={{0,2},{1,3},{2,0},{3,1},{4,6},{5,7},{6,4},{7,5},{8,10},{9,11},{10,... | collective-permute-start | bytes 1572872 | tf_op jit(solution)/shard_map/ppermute | solution.py:570
  116.8 3.3 %copy-start.17 = (bf16[8,128,128]{2,1,0:T(8,128)(2,1)S(1)}, bf16[8,128,128]{2,1,0:T(8,128)(2,1)}, u32[]{:S(2)}) copy-start(bf16[8,128,128]{2,1,0:T(8,128)(2,1)} %copy-done.16) | copy-start | bytes 786436
  116.8 2.6 %collective-permute-start.16 = (bf16[4,128,128]{2,1,0:T(8,128)(2,1)S(1)}, bf16[4,128,128]{2,1,0:T(8,128)(2,1)S(1)}, u32[]{:S(2)}, u32[]{:S(2)}) collective-permute-start(bf16[4,128,128]{2,1,0:T(8,128)(2,1)S(1)} %hidden_low.1), channel_id=1, source_target_pairs={{0,1},{1,0},{2,3},{3,2},{4,5},{5,4},{6,7},{7,6},{8,9},{9,8},{10,11... | collective-permute-start | bytes 393224 | tf_op jit(solution)/shard_map/ppermute | solution.py:570
  117.8 27.9 %collective-permute-start.15 = (bf16[8,128,128]{2,1,0:T(8,128)(2,1)S(1)}, bf16[8,128,128]{2,1,0:T(8,128)(2,1)S(1)}, u32[]{:S(2)}, u32[]{:S(2)}) collective-permute-start(bf16[8,128,128]{2,1,0:T(8,128)(2,1)S(1)} %get-tuple-element.72), channel_id=1, source_target_pairs={{0,2},{1,3},{2,0},{3,1},{4,6},{5,7},{6,4},{7,5},{8,10},{9,11},{10,... | collective-permute-start | bytes 786440 | tf_op jit(solution)/shard_map/ppermute | solution.py:570
  119.5 31.9 %collective-permute-start.17 = (bf16[8,128,128]{2,1,0:T(8,128)(2,1)S(1)}, bf16[8,128,128]{2,1,0:T(8,128)(2,1)S(1)}, u32[]{:S(2)}, u32[]{:S(2)}) collective-permute-start(bf16[8,128,128]{2,1,0:T(8,128)(2,1)S(1)} %pad_maximum_fusion.hiddens), channel_id=1, source_target_pairs={{0,2},{1,3},{2,0},{3,1},{4,6},{5,7},{6,4},{7,5},{8,10},{9,11},{10,... | collective-permute-start | bytes 786440 | tf_op jit(solution)/shard_map/ppermute | solution.py:570
  120.0 36.4 %collective-permute-start.18 = (bf16[8,128,128]{2,1,0:T(8,128)(2,1)S(1)}, bf16[8,128,128]{2,1,0:T(8,128)(2,1)S(1)}, u32[]{:S(2)}, u32[]{:S(2)}) collective-permute-start(bf16[8,128,128]{2,1,0:T(8,128)(2,1)S(1)} %copy-done.17), channel_id=1, source_target_pairs={{0,2},{1,3},{2,0},{3,1},{4,6},{5,7},{6,4},{7,5},{8,10},{9,11},{10,... | collective-permute-start | bytes 786440 | tf_op jit(solution)/shard_map/ppermute | solution.py:570
  (1 other events, 0.7 us)

commit v20 on v16

--- a/solution.py
+++ b/solution.py
@@ -578,6 +578,7 @@
     parts, tokens_own, *tokens_pair = hidden_parts(
         adapters, place, down_maps, pair, arrived
     )
+    tokens_other = [swap(tokens_pair[0], pair_bit)]
     for slot in range(lines):
         if slot not in across:
             across[slot] = swap(gradients[slot], 1)
@@ -593,12 +594,11 @@
     )
     total, received, flip = parts, swap(parts[lines:], 1), 0
     for step in reversed(range(steps - 1)):
-        kinds = [jnp.float32] if step else [jnp.float32, jnp.bfloat16]
-        sums = slot_sums(total, received, flip, kinds)
+        sums = slot_sums(total, received, flip, [jnp.float32, jnp.bfloat16])
         total, flip = sums[0], 1 << step
         received = swap(sums[-1], offsets[flip])
-    received, slices, columns_pair, backs, tokens_pair = barrier(
-        (received, slices, columns_pair, backs, tokens_pair)
+    received, slices, columns_pair, backs, tokens_pair, tokens_other = barrier(
+        (received, slices, columns_pair, backs, tokens_pair, tokens_other)
     )
 
     result = exchange_side(slices)
@@ -606,7 +606,7 @@
     hiddens = gather_step(hiddens, members)
     columns_other = swap(columns_pair, pair_bit)
     backs_pair = swap(backs, pair_bit)
-    tokens_other = [swap(half, pair_bit) for half in tokens_pair]
+    tokens_other.append(swap(tokens_pair[1], pair_bit))
     hiddens_pair = swap(hiddens, pair_bit)
     up_gradient = up_gradients(
         adapters, place, ranks, columns, columns_other, hiddens, hiddens_pair, depth // devices

time: 160 us -> 157 us (0.981)
  the two profiles are of different devices: /device:TPU:0 before, /device:TPU:10 now
where the time goes in v20:
time: 157 us; the launch traced here: 156 us
  waiting for transfers between devices  83.4 us (53%)
  starting transfers between devices  31.9 us (20%)
  Pallas kernels  26.4 us (17%)
  local copies, waits for them, and re-layouts  12.5 us (8%)
    ppermute x21, waiting for transfers between devices, swap(): return lax.ppermute(array, 'dp', [(i, i ^ flip) for i in range(devices)])  72.4 us
    ppermute x21, starting transfers between devices, swap(): return lax.ppermute(array, 'dp', [(i, i ^ flip) for i in range(devices)])  16.3 us
    unnamed x72, local copies, waits for them, and re-layouts  12.5 us
    all_to_all x2, waiting for transfers between devices, exchange_side(): lax.all_to_all(pieces, 'dp', split_axis=0, concat_axis=0, axis_index_grou...  11.1 us
    all_to_all x2, starting transfers between devices, exchange_side(): lax.all_to_all(pieces, 'dp', split_axis=0, concat_axis=0, axis_index_grou...  10.7 us
    pallas_call x6, Pallas kernels, call(): pl.pallas_call(kernel, out_shape=out_shapes, grid_spec=pltpu.PrefetchScal...  10.4 us
    pallas_call x2, Pallas kernels, sums_call(): pl.pallas_call(kernel, out_shape=jax.ShapeDtypeStruct((num_adapters,) + p...  9.08 us
    pallas_call x3, Pallas kernels, copy_call(): pl.pallas_call(kernel, out_shape=out_shapes, grid_spec=pltpu.PrefetchScal...  5.5 us
  transfers between devices with their start and end apart: 24, of which 10 were waited for; matrix products, arithmetic and copies ran while one was open for 2% of the time, Pallas kernels for 14%

profile of v20, /device:TPU:10, one launch (start us, length us, event | category | flops | bytes accessed | tf_op | source)
XLA Modules:
  0.0 156.1 jit_solution(4808404778721284502)
XLA Ops:
  0.6 2.7 %collective-permute-start = (bf16[1,128,1024]{2,1,0:T(8,128)(2,1)}, bf16[1,128,1024]{2,1,0:T(8,128)(2,1)S(1)}, u32[]{:S(2)}, u32[]{:S(2)}) collective-permute-start(bf16[1,128,1024]{2,1,0:T(8,128)(2,1)} %bitcast.3), channel_id=1, source_target_pairs={{0,8},{1,9},{2,10},{3,11},{4,12},{5,13},{6,14},{7,15},{8,0},{9,1},... | collective-permute-start | bytes 786440 | tf_op jit(solution)/shard_map/ppermute | solution.py:530
  3.7 1.2 copy-done.5
  5.0 0.7 copy-done.27
  5.6 1.8 %gather_up.1 = bf16[16,64,128]{2,1,0:T(8,128)(2,1)} custom-call(s32[16]{0:T(128)S(1)} %copy-done.27, bf16[64,64,128]{2,1,0:T(8,128)(2,1)S(1)} %copy-done.5), custom_call_target="tpu_custom_call" | custom-call | tf_op jit(solution)/shard_map/gather_up/pallas_call | solution.py:83
  7.4 4.9 %all-to-all-start = ((bf16[16,64,128]{2,1,0:T(8,128)(2,1)}), bf16[16,64,128]{2,1,0:T(8,128)(2,1)S(1)}, u32[]{:S(2)}, u32[]{:S(2)}) async-start(bf16[16,64,128]{2,1,0:T(8,128)(2,1)} %gather_up.1), calls=%async_computation | async-start | bytes 524288 | tf_op jit(solution)/shard_map/all_to_all | solution.py:517
  12.5 2.5 %collective-permute-done.refs_1_ = bf16[1,128,1024]{2,1,0:T(8,128)(2,1)S(1)} collective-permute-done((bf16[1,128,1024]{2,1,0:T(8,128)(2,1)}, bf16[1,128,1024]{2,1,0:T(8,128)(2,1)S(1)}, u32[]{:S(2)}, u32[]{:S(2)}) %collective-permute-start) | collective-permute-done | bytes 262176 | tf_op jit(solution)/shard_map/ppermute | solution.py:530
  14.9 1.8 %collective-permute-done.1.refs_2_ = bf16[1,128,1024]{2,1,0:T(8,128)(2,1)S(1)} collective-permute-done((bf16[1,128,1024]{2,1,0:T(8,128)(2,1)}, bf16[1,128,1024]{2,1,0:T(8,128)(2,1)S(1)}, u32[]{:S(2)}, u32[]{:S(2)}) %collective-permute-start.1) | collective-permute-done | bytes 262176 | tf_op jit(solution)/shard_map/ppermute | solution.py:530
  16.8 1.7 %copy-done.2 = bf16[128,8192]{1,0:T(8,128)(2,1)S(1)} copy-done((bf16[128,8192]{1,0:T(8,128)(2,1)S(1)}, bf16[128,8192]{1,0:T(8,128)(2,1)}, u32[]{:S(2)}) %copy-start.2) | copy-done | bytes 2097176
  18.5 1.8 %pack_tokens.1 = bf16[8,2,128,512]{3,2,1,0:T(8,128)(2,1)} custom-call(s32[1]{0:T(128)} %bitcast.place, bf16[128,8192]{1,0:T(8,128)(2,1)S(1)} %copy-done.2), custom_call_target="tpu_custom_call" | custom-call | tf_op jit(solution)/shard_map/pack_tokens/pallas_call | solution.py:83
  20.3 0.7 copy-done.15
  21.0 0.7 copy-done.6
  21.7 0.7 copy-done.17
  22.5 5.8 %all-to-all-start.1 = ((bf16[8,2,128,512]{3,2,1,0:T(8,128)(2,1)}), bf16[8,2,128,512]{3,2,1,0:T(8,128)(2,1)}, u32[]{:S(2)}, u32[]{:S(2)}) async-start(bf16[8,2,128,512]{3,2,1,0:T(8,128)(2,1)} %pack_tokens.1), calls=%async_computation.1 | async-start | bytes 4194304 | tf_op jit(solution)/shard_map/all_to_all | solution.py:523
  28.3 1.9 %for_pair.1 = bf16[2048,512]{1,0:T(8,128)(2,1)S(1)} custom-call(s32[16]{0:T(128)S(1)} %copy-done.28, s32[1]{0:T(128)} %bitcast.place, bf16[1024,512]{1,0:T(8,128)(2,1)S(1)} %copy-done.1, bf16[64,128,512]{2,1,0:T(8,128)(2,1)} %refs_7_.1), custom_call_target="tpu_custom_call" | custom-call | tf_op jit(solution)/shard_map/for_pair/pallas_call | solution.py:83
  30.3 1.0 collective-permute-start.9
  31.3 0.8 back_low.1
  32.0 3.0 %collective-permute-start.5 = (bf16[1,128,128]{2,1,0:T(8,128)(2,1)S(1)}, bf16[1,128,128]{2,1,0:T(8,128)(2,1)S(1)}, u32[]{:S(2)}, u32[]{:S(2)}) collective-permute-start(bf16[1,128,128]{2,1,0:T(8,128)(2,1)S(1)} %back_low.1), channel_id=1, source_target_pairs={{0,8},{1,9},{2,10},{3,11},{4,12},{5,13},{6,14},{7,15},{8,0},{9,1},... | collective-permute-start | bytes 98312 | tf_op jit(solution)/shard_map/ppermute | solution.py:530
  35.0 1.5 collective-permute-start.6
  36.5 39.4 %collective-permute-done.5 = bf16[1,128,128]{2,1,0:T(8,128)(2,1)S(1)} collective-permute-done((bf16[1,128,128]{2,1,0:T(8,128)(2,1)S(1)}, bf16[1,128,128]{2,1,0:T(8,128)(2,1)S(1)}, u32[]{:S(2)}, u32[]{:S(2)}) %collective-permute-start.5) | collective-permute-done | bytes 32800 | tf_op jit(solution)/shard_map/ppermute | solution.py:530
  75.9 2.9 %collective-permute-done.7 = bf16[1,128,128]{2,1,0:T(8,128)(2,1)} collective-permute-done((bf16[1,128,128]{2,1,0:T(8,128)(2,1)S(1)}, bf16[1,128,128]{2,1,0:T(8,128)(2,1)}, u32[]{:S(2)}, u32[]{:S(2)}) %collective-permute-start.7) | collective-permute-done | bytes 32800 | tf_op jit(solution)/shard_map/ppermute | solution.py:530
  78.8 0.7 copy-done.21
  79.6 3.5 %hidden_parts.1 = (f32[8,128,128]{2,1,0:T(8,128)S(1)}, bf16[8,128,512]{2,1,0:T(8,128)(2,1)S(1)}, bf16[4,128,512]{2,1,0:T(8,128)(2,1)S(1)}, bf16[4,128,512]{2,1,0:T(8,128)(2,1)S(1)}) custom-call(s32[16]{0:T(128)S(1)} %copy-done.28, s32[1]{0:T(128)} %bitcast.place, bf16[2048,512]{1,0:T(8,128)(2,1)S(1)} %collective-permute-done.9.pair, ...), custom_call_target="tpu_custom_call" | custom-call | tf_op jit(solution)/shard_map/hidden_parts/pallas_call | solution.py:60
  83.1 1.0 copy-done.8
  84.2 1.0 collective-permute-start.15
  85.2 0.8 pad_maximum_fusion.1
  86.2 1.1 collective-permute-start.13
  87.3 0.8 constant_dynamic-update-slice_fusion.3
  88.2 0.8 constant_dynamic-update-slice_fusion.2
  88.9 3.1 %collective-permute-done.13.received = bf16[4,128,128]{2,1,0:T(8,128)(2,1)S(1)} collective-permute-done((bf16[4,128,128]{2,1,0:T(8,128)(2,1)S(1)}, bf16[4,128,128]{2,1,0:T(8,128)(2,1)S(1)}, u32[]{:S(2)}, u32[]{:S(2)}) %collective-permute-start.13) | collective-permute-done | bytes 131104 | tf_op jit(solution)/shard_map/ppermute | solution.py:530
  92.1 0.9 collective-permute-start.14
  93.0 0.8 constant_dynamic-update-slice_fusion.1
  93.8 5.5 %input_slices.1 = (bf16[8,2,128,512]{3,2,1,0:T(8,128)(2,1)S(1)}, bf16[8,128,128]{2,1,0:T(8,128)(2,1)S(1)}, bf16[8,128,128]{2,1,0:T(8,128)(2,1)S(1)}) custom-call(s32[16]{0:T(128)S(1)} %copy-done.28, s32[1]{0:T(128)} %bitcast.place, bf16[8,128,128]{2,1,0:T(8,128)(2,1)S(1)} %constant_dynamic-update-slice_fusion.backs, bf16[2048,512]{1,0:T(8,128)(2,1)} %copy-done, ...), custom_call_target="tpu_custom_call" | custom-call | tf_op jit(solution)/shard_map/input_slices/pallas_call | solution.py:60
  99.3 1.3 copy-done.3
  100.7 0.7 copy-done.23
  101.4 0.7 copy-done.31
  102.1 5.0 %all-to-all-start.2 = ((bf16[8,2,128,512]{3,2,1,0:T(8,128)(2,1)}), bf16[8,2,128,512]{3,2,1,0:T(8,128)(2,1)S(1)}, u32[]{:S(2)}, u32[]{:S(2)}) async-start(bf16[8,2,128,512]{3,2,1,0:T(8,128)(2,1)} %copy-done.3), calls=%async_computation.2 | async-start | bytes 4194304 | tf_op jit(solution)/shard_map/all_to_all | solution.py:523
  107.0 1.1 collective-permute-start.20
  108.2 0.6 hidden_low.1
  108.8 1.0 collective-permute-start.16
  110.2 1.0 collective-permute-start.18
  111.2 1.1 collective-permute-start.19
  112.3 15.4 %collective-permute-done.16.gradients_pair = bf16[8,128,128]{2,1,0:T(8,128)(2,1)S(1)} collective-permute-done((bf16[8,128,128]{2,1,0:T(8,128)(2,1)}, bf16[8,128,128]{2,1,0:T(8,128)(2,1)S(1)}, u32[]{:S(2)}, u32[]{:S(2)}) %collective-permute-start.16) | collective-permute-done | bytes 262176 | tf_op jit(solution)/shard_map/ppermute | solution.py:530
  127.6 5.6 %collective-permute-done.18.hiddens_pair = bf16[8,128,128]{2,1,0:T(8,128)(2,1)S(1)} collective-permute-done((bf16[8,128,128]{2,1,0:T(8,128)(2,1)S(1)}, bf16[8,128,128]{2,1,0:T(8,128)(2,1)S(1)}, u32[]{:S(2)}, u32[]{:S(2)}) %collective-permute-start.18) | collective-permute-done | bytes 262176 | tf_op jit(solution)/shard_map/ppermute | solution.py:530
  133.2 3.6 %up_gradients.1 = bf16[64,64,128]{2,1,0:T(8,128)(2,1)} custom-call(s32[16]{0:T(128)S(1)} %copy-done.28, s32[1]{0:T(128)} %bitcast.place, s32[64]{0:T(128)S(1)} %copy-done.29, bf16[8,128,128]{2,1,0:T(8,128)(2,1)S(1)} %copy-done.24, bf16[8,128,128]{2,1,0:T(8,128)(2,1)S(1)} %collective-permute-done.16.gradients_pair, ...), custom_call_target="tpu_custom_call" | custom-call | tf_op jit(solution)/shard_map/up_gradients/pallas_call | solution.py:403
  136.9 1.2 collective-permute-done.19.backs_pair
  138.1 5.5 %down_gradients.1 = bf16[64,128,512]{2,1,0:T(8,128)(2,1)} custom-call(s32[16]{0:T(128)S(1)} %copy-done.28, s32[1]{0:T(128)} %bitcast.place, bf16[8,128,128]{2,1,0:T(8,128)(2,1)S(1)} %constant_dynamic-update-slice_fusion.backs, bf16[8,128,128]{2,1,0:T(8,128)(2,1)S(1)} %collective-permute-done.19.backs_pair, bf16[8,128,512]{2,1,0:T(8,128)(2,1)S(1)} %copy-done.9, ...), custom_call_target="tpu_custom_call" | custom-call | tf_op jit(solution)/shard_map/down_gradients/pallas_call | solution.py:403
  143.6 11.1 %all-to-all-done.2.source = bf16[8,2,128,512]{3,2,1,0:T(8,128)(2,1)S(1)} async-done(((bf16[8,2,128,512]{3,2,1,0:T(8,128)(2,1)}), bf16[8,2,128,512]{3,2,1,0:T(8,128)(2,1)S(1)}, u32[]{:S(2)}, u32[]{:S(2)}) %all-to-all-start.2) | async-done | bytes 2097184 | tf_op jit(solution)/shard_map/all_to_all | solution.py:523
  154.6 1.4 join_columns.1
  (88 shorter events, 1.8 us)
Async XLA Ops:
  0.6 14.3 %collective-permute-start = (bf16[1,128,1024]{2,1,0:T(8,128)(2,1)}, bf16[1,128,1024]{2,1,0:T(8,128)(2,1)S(1)}, u32[]{:S(2)}, u32[]{:S(2)}) collective-permute-start(bf16[1,128,1024]{2,1,0:T(8,128)(2,1)} %bitcast.3), channel_id=1, source_target_pairs={{0,8},{1,9},{2,10},{3,11},{4,12},{5,13},{6,14},{7,15},{8,0},{9,1},... | collective-permute-start | bytes 786440 | tf_op jit(solution)/shard_map/ppermute | solution.py:530
  3.3 13.5 %collective-permute-start.1 = (bf16[1,128,1024]{2,1,0:T(8,128)(2,1)}, bf16[1,128,1024]{2,1,0:T(8,128)(2,1)S(1)}, u32[]{:S(2)}, u32[]{:S(2)}) collective-permute-start(bf16[1,128,1024]{2,1,0:T(8,128)(2,1)} %bitcast.4), channel_id=1, source_target_pairs={{0,4},{1,5},{2,6},{3,7},{4,0},{5,1},{6,2},{7,3},{8,12},{9,13},{10,... | collective-permute-start | bytes 786440 | tf_op jit(solution)/shard_map/ppermute | solution.py:530
  7.4 13.6 %all-to-all-start = ((bf16[16,64,128]{2,1,0:T(8,128)(2,1)}), bf16[16,64,128]{2,1,0:T(8,128)(2,1)S(1)}, u32[]{:S(2)}, u32[]{:S(2)}) async-start(bf16[16,64,128]{2,1,0:T(8,128)(2,1)} %gather_up.1), calls=%async_computation | async-start | bytes 524288 | tf_op jit(solution)/shard_map/all_to_all | solution.py:517
  12.3 8.0 %collective-permute-start.2 = (bf16[1,128,1024]{2,1,0:T(8,128)(2,1)}, bf16[1,128,1024]{2,1,0:T(8,128)(2,1)S(1)}, u32[]{:S(2)}, u32[]{:S(2)}) collective-permute-start(bf16[1,128,1024]{2,1,0:T(8,128)(2,1)} %bitcast.5), channel_id=1, source_target_pairs={{0,1},{1,0},{2,3},{3,2},{4,5},{5,4},{6,7},{7,6},{8,9},{9,8},{10,11... | collective-permute-start | bytes 786440 | tf_op jit(solution)/shard_map/ppermute | solution.py:530
  14.9 5.3 %copy-start.10 = (bf16[1,128,1024]{2,1,0:T(8,128)(2,1)}, bf16[1,128,1024]{2,1,0:T(8,128)(2,1)S(1)}, u32[]{:S(2)}) copy-start(bf16[1,128,1024]{2,1,0:T(8,128)(2,1)S(1)} %collective-permute-done.refs_1_) | copy-start | bytes 786436
  14.9 6.8 %collective-permute-start.3 = (bf16[1,128,1024]{2,1,0:T(8,128)(2,1)S(1)}, bf16[1,128,1024]{2,1,0:T(8,128)(2,1)S(1)}, u32[]{:S(2)}, u32[]{:S(2)}) collective-permute-start(bf16[1,128,1024]{2,1,0:T(8,128)(2,1)S(1)} %collective-permute-done.refs_1_), channel_id=1, source_target_pairs={{0,1},{1,0},{2,3},{3,2},{4,5},{5,4},{6,7},{7,6},{8,9},{9,8},{10,11... | collective-permute-start | bytes 786440 | tf_op jit(solution)/shard_map/ppermute | solution.py:530
  16.8 3.5 %copy-start.13 = (bf16[1,128,1024]{2,1,0:T(8,128)(2,1)}, bf16[1,128,1024]{2,1,0:T(8,128)(2,1)S(1)}, u32[]{:S(2)}) copy-start(bf16[1,128,1024]{2,1,0:T(8,128)(2,1)S(1)} %collective-permute-done.1.refs_2_) | copy-start | bytes 786436
  16.8 4.9 %collective-permute-start.4 = (bf16[1,128,1024]{2,1,0:T(8,128)(2,1)S(1)}, bf16[1,128,1024]{2,1,0:T(8,128)(2,1)S(1)}, u32[]{:S(2)}, u32[]{:S(2)}) collective-permute-start(bf16[1,128,1024]{2,1,0:T(8,128)(2,1)S(1)} %collective-permute-done.1.refs_2_), channel_id=1, source_target_pairs={{0,1},{1,0},{2,3},{3,2},{4,5},{5,4},{6,7},{7,6},{8,9},{9,8},{10,11... | collective-permute-start | bytes 786440 | tf_op jit(solution)/shard_map/ppermute | solution.py:530
  16.8 1.7 %copy-start.2 = (bf16[128,8192]{1,0:T(8,128)(2,1)S(1)}, bf16[128,8192]{1,0:T(8,128)(2,1)}, u32[]{:S(2)}) copy-start(bf16[128,8192]{1,0:T(8,128)(2,1)} %tokens.1) | copy-start | bytes 6291460
  21.7 6.5 %copy-start.1 = (bf16[1024,512]{1,0:T(8,128)(2,1)S(1)}, bf16[1024,512]{1,0:T(8,128)(2,1)}, u32[]{:S(2)}) copy-start(bf16[1024,512]{1,0:T(8,128)(2,1)} %refs_16_.1) | copy-start | bytes 3145732
  21.7 6.5 %copy-start.28 = (s32[16]{0:T(128)S(1)}, s32[16]{0:T(128)}, u32[]{:S(2)}) copy-start(s32[16]{0:T(128)} %adapters.8) | copy-start | bytes 196
  22.5 57.0 %all-to-all-start.1 = ((bf16[8,2,128,512]{3,2,1,0:T(8,128)(2,1)}), bf16[8,2,128,512]{3,2,1,0:T(8,128)(2,1)}, u32[]{:S(2)}, u32[]{:S(2)}) async-start(bf16[8,2,128,512]{3,2,1,0:T(8,128)(2,1)} %pack_tokens.1), calls=%async_computation.1 | async-start | bytes 4194304 | tf_op jit(solution)/shard_map/all_to_all | solution.py:523
  28.3 3.0 %copy-start.11 = (bf16[1,128,1024]{2,1,0:T(8,128)(2,1)S(1)}, bf16[1,128,1024]{2,1,0:T(8,128)(2,1)}, u32[]{:S(2)}) copy-start(bf16[1,128,1024]{2,1,0:T(8,128)(2,1)} %copy-done.10) | copy-start | bytes 786436
  28.3 3.0 %copy-start.4 = (bf16[128,1024]{1,0:T(8,128)(2,1)S(1)}, bf16[128,1024]{1,0:T(8,128)(2,1)}, u32[]{:S(2)}) copy-start(bf16[128,1024]{1,0:T(8,128)(2,1)} %gradient.1) | copy-start | bytes 786436
  28.3 3.0 %copy-start.7 = (bf16[16,64,128]{2,1,0:T(8,128)(2,1)S(1)}, bf16[16,64,128]{2,1,0:T(8,128)(2,1)}, u32[]{:S(2)}) copy-start(bf16[16,64,128]{2,1,0:T(8,128)(2,1)} %copy-done.6) | copy-start | bytes 786436
  28.3 3.0 %copy-start.29 = (s32[64]{0:T(128)S(1)}, s32[64]{0:T(128)}, u32[]{:S(2)}) copy-start(s32[64]{0:T(128)} %ranks.5) | copy-start | bytes 772
  30.3 49.3 %collective-permute-start.9 = (bf16[2048,512]{1,0:T(8,128)(2,1)S(1)}, bf16[2048,512]{1,0:T(8,128)(2,1)S(1)}, u32[]{:S(2)}, u32[]{:S(2)}) collective-permute-start(bf16[2048,512]{1,0:T(8,128)(2,1)S(1)} %for_pair.1), channel_id=1, source_target_pairs={{0,2},{1,3},{2,0},{3,1},{4,6},{5,7},{6,4},{7,5},{8,10},{9,11},{10,... | collective-permute-start | bytes 6291464 | tf_op jit(solution)/shard_map/ppermute | solution.py:530
  31.2 47.6 %collective-permute-start.8 = (bf16[1,128,1024]{2,1,0:T(8,128)(2,1)S(1)}, bf16[1,128,1024]{2,1,0:T(8,128)(2,1)S(1)}, u32[]{:S(2)}, u32[]{:S(2)}) collective-permute-start(bf16[1,128,1024]{2,1,0:T(8,128)(2,1)S(1)} %copy-done.11), channel_id=1, source_target_pairs={{0,4},{1,5},{2,6},{3,7},{4,0},{5,1},{6,2},{7,3},{8,12},{9,13},{10,... | collective-permute-start | bytes 786440 | tf_op jit(solution)/shard_map/ppermute | solution.py:530
  32.0 43.9 %collective-permute-start.5 = (bf16[1,128,128]{2,1,0:T(8,128)(2,1)S(1)}, bf16[1,128,128]{2,1,0:T(8,128)(2,1)S(1)}, u32[]{:S(2)}, u32[]{:S(2)}) collective-permute-start(bf16[1,128,128]{2,1,0:T(8,128)(2,1)S(1)} %back_low.1), channel_id=1, source_target_pairs={{0,8},{1,9},{2,10},{3,11},{4,12},{5,13},{6,14},{7,15},{8,0},{9,1},... | collective-permute-start | bytes 98312 | tf_op jit(solution)/shard_map/ppermute | solution.py:530
  35.0 40.9 %collective-permute-start.6 = (bf16[1,128,128]{2,1,0:T(8,128)(2,1)S(1)}, bf16[1,128,128]{2,1,0:T(8,128)(2,1)S(1)}, u32[]{:S(2)}, u32[]{:S(2)}) collective-permute-start(bf16[1,128,128]{2,1,0:T(8,128)(2,1)S(1)} %back_low.1), channel_id=1, source_target_pairs={{0,4},{1,5},{2,6},{3,7},{4,0},{5,1},{6,2},{7,3},{8,12},{9,13},{10,... | collective-permute-start | bytes 98312 | tf_op jit(solution)/shard_map/ppermute | solution.py:530
  36.5 42.4 %collective-permute-start.7 = (bf16[1,128,128]{2,1,0:T(8,128)(2,1)S(1)}, bf16[1,128,128]{2,1,0:T(8,128)(2,1)}, u32[]{:S(2)}, u32[]{:S(2)}) collective-permute-start(bf16[1,128,128]{2,1,0:T(8,128)(2,1)S(1)} %back_low.1), channel_id=1, source_target_pairs={{0,12},{1,13},{2,14},{3,15},{4,8},{5,9},{6,10},{7,11},{8,4},{9,5},... | collective-permute-start | bytes 98312 | tf_op jit(solution)/shard_map/ppermute | solution.py:530
  75.9 9.2 %copy-start.33 = (bf16[1,128,128]{2,1,0:T(8,128)(2,1)}, bf16[1,128,128]{2,1,0:T(8,128)(2,1)S(1)}, u32[]{:S(2)}) copy-start(bf16[1,128,128]{2,1,0:T(8,128)(2,1)S(1)} %collective-permute-done.5) | copy-start | bytes 98308
  75.9 9.2 %copy-start.32 = (bf16[1,128,128]{2,1,0:T(8,128)(2,1)}, bf16[1,128,128]{2,1,0:T(8,128)(2,1)S(1)}, u32[]{:S(2)}) copy-start(bf16[1,128,128]{2,1,0:T(8,128)(2,1)S(1)} %collective-permute-done.6) | copy-start | bytes 98308
  79.6 3.5 %copy-start = (bf16[2048,512]{1,0:T(8,128)(2,1)}, bf16[2048,512]{1,0:T(8,128)(2,1)S(1)}, u32[]{:S(2)}) copy-start(bf16[2048,512]{1,0:T(8,128)(2,1)S(1)} %collective-permute-done.9.pair) | copy-start | bytes 6291460
  79.6 8.6 %copy-start.22 = (bf16[1,128,1024]{2,1,0:T(8,128)(2,1)S(1)}, bf16[1,128,1024]{2,1,0:T(8,128)(2,1)}, u32[]{:S(2)}) copy-start(bf16[1,128,1024]{2,1,0:T(8,128)(2,1)} %copy-done.21) | copy-start | bytes 786436
  84.1 2.1 %copy-start.30 = (bf16[4,128,512]{2,1,0:T(8,128)(2,1)}, bf16[4,128,512]{2,1,0:T(8,128)(2,1)S(1)}, u32[]{:S(2)}) copy-start(bf16[4,128,512]{2,1,0:T(8,128)(2,1)S(1)} %get-tuple-element.74) | copy-start | bytes 1572868
  84.1 9.7 %copy-start.12 = (bf16[1,128,1024]{2,1,0:T(8,128)(2,1)S(1)}, bf16[1,128,1024]{2,1,0:T(8,128)(2,1)}, u32[]{:S(2)}) copy-start(bf16[1,128,1024]{2,1,0:T(8,128)(2,1)} %copy-done.10) | copy-start | bytes 786436
  84.1 9.8 %copy-start.14 = (bf16[1,128,1024]{2,1,0:T(8,128)(2,1)S(1)}, bf16[1,128,1024]{2,1,0:T(8,128)(2,1)}, u32[]{:S(2)}) copy-start(bf16[1,128,1024]{2,1,0:T(8,128)(2,1)} %copy-done.13) | copy-start | bytes 786436
  84.1 9.8 %copy-start.16 = (bf16[1,128,1024]{2,1,0:T(8,128)(2,1)S(1)}, bf16[1,128,1024]{2,1,0:T(8,128)(2,1)}, u32[]{:S(2)}) copy-start(bf16[1,128,1024]{2,1,0:T(8,128)(2,1)} %copy-done.15) | copy-start | bytes 786436
  84.1 9.8 %copy-start.18 = (bf16[1,128,1024]{2,1,0:T(8,128)(2,1)S(1)}, bf16[1,128,1024]{2,1,0:T(8,128)(2,1)}, u32[]{:S(2)}) copy-start(bf16[1,128,1024]{2,1,0:T(8,128)(2,1)} %copy-done.17) | copy-start | bytes 786436
  84.1 9.8 %copy-start.20 = (bf16[1,128,1024]{2,1,0:T(8,128)(2,1)S(1)}, bf16[1,128,1024]{2,1,0:T(8,128)(2,1)}, u32[]{:S(2)}) copy-start(bf16[1,128,1024]{2,1,0:T(8,128)(2,1)} %copy-done.19) | copy-start | bytes 786436
  84.1 2.1 %collective-permute-start.12 = (f32[4,128,128]{2,1,0:T(8,128)S(1)}, f32[4,128,128]{2,1,0:T(8,128)S(1)}, u32[]{:S(2)}, u32[]{:S(2)}) collective-permute-start(f32[4,128,128]{2,1,0:T(8,128)S(1)} %slice.3), channel_id=1, source_target_pairs={{0,1},{1,0},{2,3},{3,2},{4,5},{5,4},{6,7},{7,6},{8,9},{9,8},{10,11... | collective-permute-start | bytes 786440 | tf_op jit(solution)/shard_map/ppermute | solution.py:530
  84.2 17.2 %collective-permute-start.15 = (bf16[4,128,512]{2,1,0:T(8,128)(2,1)S(1)}, bf16[4,128,512]{2,1,0:T(8,128)(2,1)S(1)}, u32[]{:S(2)}, u32[]{:S(2)}) collective-permute-start(bf16[4,128,512]{2,1,0:T(8,128)(2,1)S(1)} %get-tuple-element.66), channel_id=1, source_target_pairs={{0,2},{1,3},{2,0},{3,1},{4,6},{5,7},{6,4},{7,5},{8,10},{9,11},{10,... | collective-permute-start | bytes 1572872 | tf_op jit(solution)/shard_map/ppermute | solution.py:530
  85.9 7.8 %collective-permute-start.10 = (bf16[4,128,128]{2,1,0:T(8,128)(2,1)S(1)}, bf16[4,128,128]{2,1,0:T(8,128)(2,1)S(1)}, u32[]{:S(2)}, u32[]{:S(2)}) collective-permute-start(bf16[4,128,128]{2,1,0:T(8,128)(2,1)S(1)} %pad_maximum_fusion.1), channel_id=1, source_target_pairs={{0,1},{1,0},{2,3},{3,2},{4,5},{5,4},{6,7},{7,6},{8,9},{9,8},{10,11... | collective-permute-start | bytes 393224 | tf_op jit(solution)/shard_map/ppermute | solution.py:530
  86.2 5.8 %collective-permute-start.13 = (bf16[4,128,128]{2,1,0:T(8,128)(2,1)S(1)}, bf16[4,128,128]{2,1,0:T(8,128)(2,1)S(1)}, u32[]{:S(2)}, u32[]{:S(2)}) collective-permute-start(bf16[4,128,128]{2,1,0:T(8,128)(2,1)S(1)} %get-tuple-element.62), channel_id=1, source_target_pairs={{0,4},{1,5},{2,6},{3,7},{4,0},{5,1},{6,2},{7,3},{8,12},{9,13},{10,... | collective-permute-start | bytes 393224 | tf_op jit(solution)/shard_map/ppermute | solution.py:530
  88.1 5.7 %collective-permute-start.11 = (bf16[1,128,1024]{2,1,0:T(8,128)(2,1)S(1)}, bf16[1,128,1024]{2,1,0:T(8,128)(2,1)S(1)}, u32[]{:S(2)}, u32[]{:S(2)}) collective-permute-start(bf16[1,128,1024]{2,1,0:T(8,128)(2,1)S(1)} %copy-done.22), channel_id=1, source_target_pairs={{0,1},{1,0},{2,3},{3,2},{4,5},{5,4},{6,7},{7,6},{8,9},{9,8},{10,11... | collective-permute-start | bytes 786440 | tf_op jit(solution)/shard_map/ppermute | solution.py:530
  92.1 1.7 %copy-start.25 = (f32[4,128,128]{2,1,0:T(8,128)}, f32[4,128,128]{2,1,0:T(8,128)S(1)}, u32[]{:S(2)}) copy-start(f32[4,128,128]{2,1,0:T(8,128)S(1)} %get-tuple-element.69.total) | copy-start | bytes 786436
  92.1 9.3 %collective-permute-start.14 = (bf16[4,128,128]{2,1,0:T(8,128)(2,1)S(1)}, bf16[4,128,128]{2,1,0:T(8,128)(2,1)S(1)}, u32[]{:S(2)}, u32[]{:S(2)}) collective-permute-start(bf16[4,128,128]{2,1,0:T(8,128)(2,1)S(1)} %get-tuple-element.63), channel_id=1, source_target_pairs={{0,8},{1,9},{2,10},{3,11},{4,12},{5,13},{6,14},{7,15},{8,0},{9,1},... | collective-permute-start | bytes 393224 | tf_op jit(solution)/shard_map/ppermute | solution.py:530
  99.3 1.3 copy-start.3
  102.1 6.1 %copy-start.26 = (f32[4,128,128]{2,1,0:T(8,128)S(1)}, f32[4,128,128]{2,1,0:T(8,128)}, u32[]{:S(2)}) copy-start(f32[4,128,128]{2,1,0:T(8,128)} %copy-done.25) | copy-start | bytes 786436
  102.1 31.2 %copy-start.24 = (bf16[8,128,128]{2,1,0:T(8,128)(2,1)S(1)}, bf16[8,128,128]{2,1,0:T(8,128)(2,1)}, u32[]{:S(2)}) copy-start(bf16[8,128,128]{2,1,0:T(8,128)(2,1)} %copy-done.23) | copy-start | bytes 786436
  102.1 52.6 %all-to-all-start.2 = ((bf16[8,2,128,512]{3,2,1,0:T(8,128)(2,1)}), bf16[8,2,128,512]{3,2,1,0:T(8,128)(2,1)S(1)}, u32[]{:S(2)}, u32[]{:S(2)}) async-start(bf16[8,2,128,512]{3,2,1,0:T(8,128)(2,1)} %copy-done.3), calls=%async_computation.2 | async-start | bytes 4194304 | tf_op jit(solution)/shard_map/all_to_all | solution.py:523
  107.0 31.0 %copy-start.9 = (bf16[8,128,512]{2,1,0:T(8,128)(2,1)S(1)}, bf16[8,128,512]{2,1,0:T(8,128)(2,1)}, u32[]{:S(2)}) copy-start(bf16[8,128,512]{2,1,0:T(8,128)(2,1)} %copy-done.8) | copy-start | bytes 3145732
  107.0 31.0 %collective-permute-start.20 = (bf16[4,128,512]{2,1,0:T(8,128)(2,1)}, bf16[4,128,512]{2,1,0:T(8,128)(2,1)S(1)}, u32[]{:S(2)}, u32[]{:S(2)}) collective-permute-start(bf16[4,128,512]{2,1,0:T(8,128)(2,1)} %copy-done.30), channel_id=1, source_target_pairs={{0,2},{1,3},{2,0},{3,1},{4,6},{5,7},{6,4},{7,5},{8,10},{9,11},{10,... | collective-permute-start | bytes 1572872 | tf_op jit(solution)/shard_map/ppermute | solution.py:530
  108.7 1.4 collective-permute-start.17
  108.8 18.8 %collective-permute-start.16 = (bf16[8,128,128]{2,1,0:T(8,128)(2,1)}, bf16[8,128,128]{2,1,0:T(8,128)(2,1)S(1)}, u32[]{:S(2)}, u32[]{:S(2)}) collective-permute-start(bf16[8,128,128]{2,1,0:T(8,128)(2,1)} %copy-done.31), channel_id=1, source_target_pairs={{0,2},{1,3},{2,0},{3,1},{4,6},{5,7},{6,4},{7,5},{8,10},{9,11},{10,... | collective-permute-start | bytes 786440 | tf_op jit(solution)/shard_map/ppermute | solution.py:530
  110.2 23.1 %collective-permute-start.18 = (bf16[8,128,128]{2,1,0:T(8,128)(2,1)S(1)}, bf16[8,128,128]{2,1,0:T(8,128)(2,1)S(1)}, u32[]{:S(2)}, u32[]{:S(2)}) collective-permute-start(bf16[8,128,128]{2,1,0:T(8,128)(2,1)S(1)} %pad_maximum_fusion.hiddens), channel_id=1, source_target_pairs={{0,2},{1,3},{2,0},{3,1},{4,6},{5,7},{6,4},{7,5},{8,10},{9,11},{10,... | collective-permute-start | bytes 786440 | tf_op jit(solution)/shard_map/ppermute | solution.py:530
  111.2 26.9 %collective-permute-start.19 = (bf16[8,128,128]{2,1,0:T(8,128)(2,1)S(1)}, bf16[8,128,128]{2,1,0:T(8,128)(2,1)S(1)}, u32[]{:S(2)}, u32[]{:S(2)}) collective-permute-start(bf16[8,128,128]{2,1,0:T(8,128)(2,1)S(1)} %constant_dynamic-update-slice_fusion.backs), channel_id=1, source_target_pairs={{0,2},{1,3},{2,0},{3,1},{4,6},{5,7},{6,4},{7,5},{8,10},{9,11},{10,... | collective-permute-start | bytes 786440 | tf_op jit(solution)/shard_map/ppermute | solution.py:530
  (10 other events, 7.9 us)

commit v21 on v20

--- a/solution.py
+++ b/solution.py
@@ -25,19 +25,14 @@
     return place % line_bit // pair_bit
 
 
-def reversed_bits(number, count):
-    bits = count.bit_length() - 1
-    return sum(((number >> bit) & 1) << (bits - 1 - bit) for bit in range(bits))
-
-
 def side_index(place, members):
     lines = members // 2
-    return place % pair_bit * lines + reversed_bits(place // line_bit, lines)
+    return place % pair_bit * lines + place // line_bit
 
 
 def side_place(index, side, members):
     core, line = divmod(index, members // 2)
-    return reversed_bits(line, members // 2) * line_bit + side * pair_bit + core
+    return line * line_bit + side * pair_bit + core
 
 
 def params():

time: 157 us -> 159 us (1.013)
  the two profiles are of different devices: /device:TPU:10 before, /device:TPU:0 now
where the time goes in v21:
time: 159 us; the launch traced here: 158 us
  waiting for transfers between devices  84.5 us (53%)
  starting transfers between devices  32.9 us (21%)
  Pallas kernels  26.4 us (17%)
  local copies, waits for them, and re-layouts  12.5 us (8%)
    ppermute x21, waiting for transfers between devices, swap(): return lax.ppermute(array, 'dp', [(i, i ^ flip) for i in range(devices)])  70.9 us
    ppermute x21, starting transfers between devices, swap(): return lax.ppermute(array, 'dp', [(i, i ^ flip) for i in range(devices)])  21.1 us
    unnamed x72, local copies, waits for them, and re-layouts  12.5 us
    all_to_all x2, waiting for transfers between devices, exchange_side(): lax.all_to_all(pieces, 'dp', split_axis=0, concat_axis=0, axis_index_grou...  11.7 us
    pallas_call x6, Pallas kernels, call(): pl.pallas_call(kernel, out_shape=out_shapes, grid_spec=pltpu.PrefetchScal...  10.4 us
    pallas_call x2, Pallas kernels, sums_call(): pl.pallas_call(kernel, out_shape=jax.ShapeDtypeStruct((num_adapters,) + p...  9.06 us
    all_to_all x2, starting transfers between devices, exchange_side(): lax.all_to_all(pieces, 'dp', split_axis=0, concat_axis=0, axis_index_grou...  8.24 us
    pallas_call x3, Pallas kernels, copy_call(): pl.pallas_call(kernel, out_shape=out_shapes, grid_spec=pltpu.PrefetchScal...  5.5 us
  transfers between devices with their start and end apart: 24, of which 10 were waited for; matrix products, arithmetic and copies ran while one was open for 2% of the time, Pallas kernels for 14%

profile of v21, /device:TPU:0, one launch (start us, length us, event | category | flops | bytes accessed | tf_op | source)
XLA Modules:
  0.0 158.0 jit_solution(1571456827446205480)
XLA Ops:
  0.6 4.1 %collective-permute-start = (bf16[1,128,1024]{2,1,0:T(8,128)(2,1)}, bf16[1,128,1024]{2,1,0:T(8,128)(2,1)S(1)}, u32[]{:S(2)}, u32[]{:S(2)}) collective-permute-start(bf16[1,128,1024]{2,1,0:T(8,128)(2,1)} %bitcast.3), channel_id=1, source_target_pairs={{0,8},{1,9},{2,10},{3,11},{4,12},{5,13},{6,14},{7,15},{8,0},{9,1},... | collective-permute-start | bytes 786440 | tf_op jit(solution)/shard_map/ppermute | solution.py:525
  4.7 1.6 collective-permute-start.1
  6.3 1.2 copy-done.5
  7.5 0.7 copy-done.27
  8.2 1.8 %gather_up.1 = bf16[16,64,128]{2,1,0:T(8,128)(2,1)} custom-call(s32[16]{0:T(128)S(1)} %copy-done.27, bf16[64,64,128]{2,1,0:T(8,128)(2,1)S(1)} %copy-done.5), custom_call_target="tpu_custom_call" | custom-call | tf_op jit(solution)/shard_map/gather_up/pallas_call | solution.py:78
  10.0 3.5 %all-to-all-start = ((bf16[16,64,128]{2,1,0:T(8,128)(2,1)}), bf16[16,64,128]{2,1,0:T(8,128)(2,1)S(1)}, u32[]{:S(2)}, u32[]{:S(2)}) async-start(bf16[16,64,128]{2,1,0:T(8,128)(2,1)} %gather_up.1), calls=%async_computation | async-start | bytes 524288 | tf_op jit(solution)/shard_map/all_to_all | solution.py:512
  13.8 3.2 %collective-permute-done.refs_1_ = bf16[1,128,1024]{2,1,0:T(8,128)(2,1)S(1)} collective-permute-done((bf16[1,128,1024]{2,1,0:T(8,128)(2,1)}, bf16[1,128,1024]{2,1,0:T(8,128)(2,1)S(1)}, u32[]{:S(2)}, u32[]{:S(2)}) %collective-permute-start) | collective-permute-done | bytes 262176 | tf_op jit(solution)/shard_map/ppermute | solution.py:525
  17.5 1.6 %copy-done.2 = bf16[128,8192]{1,0:T(8,128)(2,1)S(1)} copy-done((bf16[128,8192]{1,0:T(8,128)(2,1)S(1)}, bf16[128,8192]{1,0:T(8,128)(2,1)}, u32[]{:S(2)}) %copy-start.2) | copy-done | bytes 2097176
  19.1 1.8 %pack_tokens.1 = bf16[8,2,128,512]{3,2,1,0:T(8,128)(2,1)} custom-call(s32[1]{0:T(128)} %bitcast.place, bf16[128,8192]{1,0:T(8,128)(2,1)S(1)} %copy-done.2), custom_call_target="tpu_custom_call" | custom-call | tf_op jit(solution)/shard_map/pack_tokens/pallas_call | solution.py:78
  21.0 0.7 copy-done.15
  21.7 1.9 %all-to-all-done = bf16[16,64,128]{2,1,0:T(8,128)(2,1)S(1)} async-done(((bf16[16,64,128]{2,1,0:T(8,128)(2,1)}), bf16[16,64,128]{2,1,0:T(8,128)(2,1)S(1)}, u32[]{:S(2)}, u32[]{:S(2)}) %all-to-all-start) | async-done | bytes 262176 | tf_op jit(solution)/shard_map/all_to_all | solution.py:512
  23.5 0.7 copy-done.6
  24.3 0.7 copy-done.17
  25.0 4.4 %all-to-all-start.1 = ((bf16[8,2,128,512]{3,2,1,0:T(8,128)(2,1)}), bf16[8,2,128,512]{3,2,1,0:T(8,128)(2,1)}, u32[]{:S(2)}, u32[]{:S(2)}) async-start(bf16[8,2,128,512]{3,2,1,0:T(8,128)(2,1)} %pack_tokens.1), calls=%async_computation.1 | async-start | bytes 4194304 | tf_op jit(solution)/shard_map/all_to_all | solution.py:518
  29.5 1.9 %for_pair.1 = bf16[2048,512]{1,0:T(8,128)(2,1)S(1)} custom-call(s32[16]{0:T(128)S(1)} %copy-done.28, s32[1]{0:T(128)} %bitcast.place, bf16[1024,512]{1,0:T(8,128)(2,1)S(1)} %copy-done.1, bf16[64,128,512]{2,1,0:T(8,128)(2,1)} %refs_7_.1), custom_call_target="tpu_custom_call" | custom-call | tf_op jit(solution)/shard_map/for_pair/pallas_call | solution.py:78
  31.4 0.8 collective-permute-start.9
  32.3 2.0 %collective-permute-start.8 = (bf16[1,128,1024]{2,1,0:T(8,128)(2,1)S(1)}, bf16[1,128,1024]{2,1,0:T(8,128)(2,1)S(1)}, u32[]{:S(2)}, u32[]{:S(2)}) collective-permute-start(bf16[1,128,1024]{2,1,0:T(8,128)(2,1)S(1)} %copy-done.11), channel_id=1, source_target_pairs={{0,4},{1,5},{2,6},{3,7},{4,0},{5,1},{6,2},{7,3},{8,12},{9,13},{10,... | collective-permute-start | bytes 786440 | tf_op jit(solution)/shard_map/ppermute | solution.py:525
  34.3 0.8 back_low.1
  35.0 2.4 %collective-permute-start.5 = (bf16[1,128,128]{2,1,0:T(8,128)(2,1)S(1)}, bf16[1,128,128]{2,1,0:T(8,128)(2,1)S(1)}, u32[]{:S(2)}, u32[]{:S(2)}) collective-permute-start(bf16[1,128,128]{2,1,0:T(8,128)(2,1)S(1)} %back_low.1), channel_id=1, source_target_pairs={{0,8},{1,9},{2,10},{3,11},{4,12},{5,13},{6,14},{7,15},{8,0},{9,1},... | collective-permute-start | bytes 98312 | tf_op jit(solution)/shard_map/ppermute | solution.py:525
  38.0 1.5 collective-permute-start.7
  39.5 41.3 %collective-permute-done.5 = bf16[1,128,128]{2,1,0:T(8,128)(2,1)S(1)} collective-permute-done((bf16[1,128,128]{2,1,0:T(8,128)(2,1)S(1)}, bf16[1,128,128]{2,1,0:T(8,128)(2,1)S(1)}, u32[]{:S(2)}, u32[]{:S(2)}) %collective-permute-start.5) | collective-permute-done | bytes 32800 | tf_op jit(solution)/shard_map/ppermute | solution.py:525
  80.8 0.7 copy-done.21
  81.6 3.5 %hidden_parts.1 = (f32[8,128,128]{2,1,0:T(8,128)S(1)}, bf16[8,128,512]{2,1,0:T(8,128)(2,1)S(1)}, bf16[4,128,512]{2,1,0:T(8,128)(2,1)S(1)}, bf16[4,128,512]{2,1,0:T(8,128)(2,1)S(1)}) custom-call(s32[16]{0:T(128)S(1)} %copy-done.28, s32[1]{0:T(128)} %bitcast.place, bf16[2048,512]{1,0:T(8,128)(2,1)S(1)} %collective-permute-done.9.pair, ...), custom_call_target="tpu_custom_call" | custom-call | tf_op jit(solution)/shard_map/hidden_parts/pallas_call | solution.py:55
  85.1 1.0 copy-done.8
  86.2 1.0 collective-permute-start.15
  87.2 0.8 pad_maximum_fusion.1
  88.2 1.0 collective-permute-start.13
  89.3 0.8 constant_dynamic-update-slice_fusion.3
  90.1 0.8 constant_dynamic-update-slice_fusion.2
  90.9 3.2 %collective-permute-done.13.received = bf16[4,128,128]{2,1,0:T(8,128)(2,1)S(1)} collective-permute-done((bf16[4,128,128]{2,1,0:T(8,128)(2,1)S(1)}, bf16[4,128,128]{2,1,0:T(8,128)(2,1)S(1)}, u32[]{:S(2)}, u32[]{:S(2)}) %collective-permute-start.13) | collective-permute-done | bytes 131104 | tf_op jit(solution)/shard_map/ppermute | solution.py:525
  94.1 0.9 collective-permute-start.14
  95.0 0.8 constant_dynamic-update-slice_fusion.1
  95.9 5.5 %input_slices.1 = (bf16[8,2,128,512]{3,2,1,0:T(8,128)(2,1)S(1)}, bf16[8,128,128]{2,1,0:T(8,128)(2,1)S(1)}, bf16[8,128,128]{2,1,0:T(8,128)(2,1)S(1)}) custom-call(s32[16]{0:T(128)S(1)} %copy-done.28, s32[1]{0:T(128)} %bitcast.place, bf16[8,128,128]{2,1,0:T(8,128)(2,1)S(1)} %constant_dynamic-update-slice_fusion.backs, bf16[2048,512]{1,0:T(8,128)(2,1)} %copy-done, ...), custom_call_target="tpu_custom_call" | custom-call | tf_op jit(solution)/shard_map/input_slices/pallas_call | solution.py:55
  101.4 1.3 copy-done.3
  102.7 0.7 copy-done.23
  103.4 0.7 copy-done.31
  104.1 3.9 %all-to-all-start.2 = ((bf16[8,2,128,512]{3,2,1,0:T(8,128)(2,1)}), bf16[8,2,128,512]{3,2,1,0:T(8,128)(2,1)S(1)}, u32[]{:S(2)}, u32[]{:S(2)}) async-start(bf16[8,2,128,512]{3,2,1,0:T(8,128)(2,1)} %copy-done.3), calls=%async_computation.2 | async-start | bytes 4194304 | tf_op jit(solution)/shard_map/all_to_all | solution.py:518
  108.0 1.2 collective-permute-start.20
  110.0 0.9 collective-permute-start.16
  111.2 1.0 collective-permute-start.18
  112.2 1.1 collective-permute-start.19
  113.3 15.3 %collective-permute-done.16.gradients_pair = bf16[8,128,128]{2,1,0:T(8,128)(2,1)S(1)} collective-permute-done((bf16[8,128,128]{2,1,0:T(8,128)(2,1)}, bf16[8,128,128]{2,1,0:T(8,128)(2,1)S(1)}, u32[]{:S(2)}, u32[]{:S(2)}) %collective-permute-start.16) | collective-permute-done | bytes 262176 | tf_op jit(solution)/shard_map/ppermute | solution.py:525
  128.6 5.6 %collective-permute-done.18.hiddens_pair = bf16[8,128,128]{2,1,0:T(8,128)(2,1)S(1)} collective-permute-done((bf16[8,128,128]{2,1,0:T(8,128)(2,1)S(1)}, bf16[8,128,128]{2,1,0:T(8,128)(2,1)S(1)}, u32[]{:S(2)}, u32[]{:S(2)}) %collective-permute-start.18) | collective-permute-done | bytes 262176 | tf_op jit(solution)/shard_map/ppermute | solution.py:525
  134.2 3.6 %up_gradients.1 = bf16[64,64,128]{2,1,0:T(8,128)(2,1)} custom-call(s32[16]{0:T(128)S(1)} %copy-done.28, s32[1]{0:T(128)} %bitcast.place, s32[64]{0:T(128)S(1)} %copy-done.29, bf16[8,128,128]{2,1,0:T(8,128)(2,1)S(1)} %copy-done.24, bf16[8,128,128]{2,1,0:T(8,128)(2,1)S(1)} %collective-permute-done.16.gradients_pair, ...), custom_call_target="tpu_custom_call" | custom-call | tf_op jit(solution)/shard_map/up_gradients/pallas_call | solution.py:398
  137.8 1.6 collective-permute-done.19.backs_pair
  139.4 5.5 %down_gradients.1 = bf16[64,128,512]{2,1,0:T(8,128)(2,1)} custom-call(s32[16]{0:T(128)S(1)} %copy-done.28, s32[1]{0:T(128)} %bitcast.place, bf16[8,128,128]{2,1,0:T(8,128)(2,1)S(1)} %constant_dynamic-update-slice_fusion.backs, bf16[8,128,128]{2,1,0:T(8,128)(2,1)S(1)} %collective-permute-done.19.backs_pair, bf16[8,128,512]{2,1,0:T(8,128)(2,1)S(1)} %copy-done.9, ...), custom_call_target="tpu_custom_call" | custom-call | tf_op jit(solution)/shard_map/down_gradients/pallas_call | solution.py:398
  144.9 11.7 %all-to-all-done.2.source = bf16[8,2,128,512]{3,2,1,0:T(8,128)(2,1)S(1)} async-done(((bf16[8,2,128,512]{3,2,1,0:T(8,128)(2,1)}), bf16[8,2,128,512]{3,2,1,0:T(8,128)(2,1)S(1)}, u32[]{:S(2)}, u32[]{:S(2)}) %all-to-all-start.2) | async-done | bytes 2097184 | tf_op jit(solution)/shard_map/all_to_all | solution.py:518
  156.6 1.4 join_columns.1
  (88 shorter events, 3.2 us)
Async XLA Ops:
  0.6 16.3 %collective-permute-start = (bf16[1,128,1024]{2,1,0:T(8,128)(2,1)}, bf16[1,128,1024]{2,1,0:T(8,128)(2,1)S(1)}, u32[]{:S(2)}, u32[]{:S(2)}) collective-permute-start(bf16[1,128,1024]{2,1,0:T(8,128)(2,1)} %bitcast.3), channel_id=1, source_target_pairs={{0,8},{1,9},{2,10},{3,11},{4,12},{5,13},{6,14},{7,15},{8,0},{9,1},... | collective-permute-start | bytes 786440 | tf_op jit(solution)/shard_map/ppermute | solution.py:525
  4.7 12.7 %collective-permute-start.1 = (bf16[1,128,1024]{2,1,0:T(8,128)(2,1)}, bf16[1,128,1024]{2,1,0:T(8,128)(2,1)S(1)}, u32[]{:S(2)}, u32[]{:S(2)}) collective-permute-start(bf16[1,128,1024]{2,1,0:T(8,128)(2,1)} %bitcast.4), channel_id=1, source_target_pairs={{0,4},{1,5},{2,6},{3,7},{4,0},{5,1},{6,2},{7,3},{8,12},{9,13},{10,... | collective-permute-start | bytes 786440 | tf_op jit(solution)/shard_map/ppermute | solution.py:525
  10.0 13.6 %all-to-all-start = ((bf16[16,64,128]{2,1,0:T(8,128)(2,1)}), bf16[16,64,128]{2,1,0:T(8,128)(2,1)S(1)}, u32[]{:S(2)}, u32[]{:S(2)}) async-start(bf16[16,64,128]{2,1,0:T(8,128)(2,1)} %gather_up.1), calls=%async_computation | async-start | bytes 524288 | tf_op jit(solution)/shard_map/all_to_all | solution.py:512
  13.5 7.4 %collective-permute-start.2 = (bf16[1,128,1024]{2,1,0:T(8,128)(2,1)}, bf16[1,128,1024]{2,1,0:T(8,128)(2,1)S(1)}, u32[]{:S(2)}, u32[]{:S(2)}) collective-permute-start(bf16[1,128,1024]{2,1,0:T(8,128)(2,1)} %bitcast.5), channel_id=1, source_target_pairs={{0,1},{1,0},{2,3},{3,2},{4,5},{5,4},{6,7},{7,6},{8,9},{9,8},{10,11... | collective-permute-start | bytes 786440 | tf_op jit(solution)/shard_map/ppermute | solution.py:525
  17.0 4.0 %copy-start.10 = (bf16[1,128,1024]{2,1,0:T(8,128)(2,1)}, bf16[1,128,1024]{2,1,0:T(8,128)(2,1)S(1)}, u32[]{:S(2)}) copy-start(bf16[1,128,1024]{2,1,0:T(8,128)(2,1)S(1)} %collective-permute-done.refs_1_) | copy-start | bytes 786436
  17.0 7.2 %collective-permute-start.3 = (bf16[1,128,1024]{2,1,0:T(8,128)(2,1)S(1)}, bf16[1,128,1024]{2,1,0:T(8,128)(2,1)S(1)}, u32[]{:S(2)}, u32[]{:S(2)}) collective-permute-start(bf16[1,128,1024]{2,1,0:T(8,128)(2,1)S(1)} %collective-permute-done.refs_1_), channel_id=1, source_target_pairs={{0,1},{1,0},{2,3},{3,2},{4,5},{5,4},{6,7},{7,6},{8,9},{9,8},{10,11... | collective-permute-start | bytes 786440 | tf_op jit(solution)/shard_map/ppermute | solution.py:525
  17.4 3.5 %copy-start.13 = (bf16[1,128,1024]{2,1,0:T(8,128)(2,1)}, bf16[1,128,1024]{2,1,0:T(8,128)(2,1)S(1)}, u32[]{:S(2)}) copy-start(bf16[1,128,1024]{2,1,0:T(8,128)(2,1)S(1)} %collective-permute-done.1.refs_2_) | copy-start | bytes 786436
  17.4 6.8 %collective-permute-start.4 = (bf16[1,128,1024]{2,1,0:T(8,128)(2,1)S(1)}, bf16[1,128,1024]{2,1,0:T(8,128)(2,1)S(1)}, u32[]{:S(2)}, u32[]{:S(2)}) collective-permute-start(bf16[1,128,1024]{2,1,0:T(8,128)(2,1)S(1)} %collective-permute-done.1.refs_2_), channel_id=1, source_target_pairs={{0,1},{1,0},{2,3},{3,2},{4,5},{5,4},{6,7},{7,6},{8,9},{9,8},{10,11... | collective-permute-start | bytes 786440 | tf_op jit(solution)/shard_map/ppermute | solution.py:525
  17.5 1.6 %copy-start.2 = (bf16[128,8192]{1,0:T(8,128)(2,1)S(1)}, bf16[128,8192]{1,0:T(8,128)(2,1)}, u32[]{:S(2)}) copy-start(bf16[128,8192]{1,0:T(8,128)(2,1)} %tokens.1) | copy-start | bytes 6291460
  24.2 5.2 %copy-start.1 = (bf16[1024,512]{1,0:T(8,128)(2,1)S(1)}, bf16[1024,512]{1,0:T(8,128)(2,1)}, u32[]{:S(2)}) copy-start(bf16[1024,512]{1,0:T(8,128)(2,1)} %refs_16_.1) | copy-start | bytes 3145732
  24.3 5.2 %copy-start.28 = (s32[16]{0:T(128)S(1)}, s32[16]{0:T(128)}, u32[]{:S(2)}) copy-start(s32[16]{0:T(128)} %adapters.8) | copy-start | bytes 196
  25.0 56.5 %all-to-all-start.1 = ((bf16[8,2,128,512]{3,2,1,0:T(8,128)(2,1)}), bf16[8,2,128,512]{3,2,1,0:T(8,128)(2,1)}, u32[]{:S(2)}, u32[]{:S(2)}) async-start(bf16[8,2,128,512]{3,2,1,0:T(8,128)(2,1)} %pack_tokens.1), calls=%async_computation.1 | async-start | bytes 4194304 | tf_op jit(solution)/shard_map/all_to_all | solution.py:518
  29.4 2.8 %copy-start.11 = (bf16[1,128,1024]{2,1,0:T(8,128)(2,1)S(1)}, bf16[1,128,1024]{2,1,0:T(8,128)(2,1)}, u32[]{:S(2)}) copy-start(bf16[1,128,1024]{2,1,0:T(8,128)(2,1)} %copy-done.10) | copy-start | bytes 786436
  29.4 4.8 %copy-start.4 = (bf16[128,1024]{1,0:T(8,128)(2,1)S(1)}, bf16[128,1024]{1,0:T(8,128)(2,1)}, u32[]{:S(2)}) copy-start(bf16[128,1024]{1,0:T(8,128)(2,1)} %gradient.1) | copy-start | bytes 786436
  29.4 4.8 %copy-start.7 = (bf16[16,64,128]{2,1,0:T(8,128)(2,1)S(1)}, bf16[16,64,128]{2,1,0:T(8,128)(2,1)}, u32[]{:S(2)}) copy-start(bf16[16,64,128]{2,1,0:T(8,128)(2,1)} %copy-done.6) | copy-start | bytes 786436
  29.4 4.8 %copy-start.29 = (s32[64]{0:T(128)S(1)}, s32[64]{0:T(128)}, u32[]{:S(2)}) copy-start(s32[64]{0:T(128)} %ranks.5) | copy-start | bytes 772
  31.4 50.1 %collective-permute-start.9 = (bf16[2048,512]{1,0:T(8,128)(2,1)S(1)}, bf16[2048,512]{1,0:T(8,128)(2,1)S(1)}, u32[]{:S(2)}, u32[]{:S(2)}) collective-permute-start(bf16[2048,512]{1,0:T(8,128)(2,1)S(1)} %for_pair.1), channel_id=1, source_target_pairs={{0,2},{1,3},{2,0},{3,1},{4,6},{5,7},{6,4},{7,5},{8,10},{9,11},{10,... | collective-permute-start | bytes 6291464 | tf_op jit(solution)/shard_map/ppermute | solution.py:525
  32.3 48.6 %collective-permute-start.8 = (bf16[1,128,1024]{2,1,0:T(8,128)(2,1)S(1)}, bf16[1,128,1024]{2,1,0:T(8,128)(2,1)S(1)}, u32[]{:S(2)}, u32[]{:S(2)}) collective-permute-start(bf16[1,128,1024]{2,1,0:T(8,128)(2,1)S(1)} %copy-done.11), channel_id=1, source_target_pairs={{0,4},{1,5},{2,6},{3,7},{4,0},{5,1},{6,2},{7,3},{8,12},{9,13},{10,... | collective-permute-start | bytes 786440 | tf_op jit(solution)/shard_map/ppermute | solution.py:525
  35.0 45.8 %collective-permute-start.5 = (bf16[1,128,128]{2,1,0:T(8,128)(2,1)S(1)}, bf16[1,128,128]{2,1,0:T(8,128)(2,1)S(1)}, u32[]{:S(2)}, u32[]{:S(2)}) collective-permute-start(bf16[1,128,128]{2,1,0:T(8,128)(2,1)S(1)} %back_low.1), channel_id=1, source_target_pairs={{0,8},{1,9},{2,10},{3,11},{4,12},{5,13},{6,14},{7,15},{8,0},{9,1},... | collective-permute-start | bytes 98312 | tf_op jit(solution)/shard_map/ppermute | solution.py:525
  37.5 43.3 %collective-permute-start.6 = (bf16[1,128,128]{2,1,0:T(8,128)(2,1)S(1)}, bf16[1,128,128]{2,1,0:T(8,128)(2,1)S(1)}, u32[]{:S(2)}, u32[]{:S(2)}) collective-permute-start(bf16[1,128,128]{2,1,0:T(8,128)(2,1)S(1)} %back_low.1), channel_id=1, source_target_pairs={{0,4},{1,5},{2,6},{3,7},{4,0},{5,1},{6,2},{7,3},{8,12},{9,13},{10,... | collective-permute-start | bytes 98312 | tf_op jit(solution)/shard_map/ppermute | solution.py:525
  38.0 42.8 %collective-permute-start.7 = (bf16[1,128,128]{2,1,0:T(8,128)(2,1)S(1)}, bf16[1,128,128]{2,1,0:T(8,128)(2,1)}, u32[]{:S(2)}, u32[]{:S(2)}) collective-permute-start(bf16[1,128,128]{2,1,0:T(8,128)(2,1)S(1)} %back_low.1), channel_id=1, source_target_pairs={{0,12},{1,13},{2,14},{3,15},{4,8},{5,9},{6,10},{7,11},{8,4},{9,5},... | collective-permute-start | bytes 98312 | tf_op jit(solution)/shard_map/ppermute | solution.py:525
  80.8 6.4 %copy-start.33 = (bf16[1,128,128]{2,1,0:T(8,128)(2,1)}, bf16[1,128,128]{2,1,0:T(8,128)(2,1)S(1)}, u32[]{:S(2)}) copy-start(bf16[1,128,128]{2,1,0:T(8,128)(2,1)S(1)} %collective-permute-done.5) | copy-start | bytes 98308
  80.8 6.4 %copy-start.32 = (bf16[1,128,128]{2,1,0:T(8,128)(2,1)}, bf16[1,128,128]{2,1,0:T(8,128)(2,1)S(1)}, u32[]{:S(2)}) copy-start(bf16[1,128,128]{2,1,0:T(8,128)(2,1)S(1)} %collective-permute-done.6) | copy-start | bytes 98308
  81.6 3.5 %copy-start = (bf16[2048,512]{1,0:T(8,128)(2,1)}, bf16[2048,512]{1,0:T(8,128)(2,1)S(1)}, u32[]{:S(2)}) copy-start(bf16[2048,512]{1,0:T(8,128)(2,1)S(1)} %collective-permute-done.9.pair) | copy-start | bytes 6291460
  81.6 8.5 %copy-start.22 = (bf16[1,128,1024]{2,1,0:T(8,128)(2,1)S(1)}, bf16[1,128,1024]{2,1,0:T(8,128)(2,1)}, u32[]{:S(2)}) copy-start(bf16[1,128,1024]{2,1,0:T(8,128)(2,1)} %copy-done.21) | copy-start | bytes 786436
  86.1 2.1 %copy-start.30 = (bf16[4,128,512]{2,1,0:T(8,128)(2,1)}, bf16[4,128,512]{2,1,0:T(8,128)(2,1)S(1)}, u32[]{:S(2)}) copy-start(bf16[4,128,512]{2,1,0:T(8,128)(2,1)S(1)} %get-tuple-element.74) | copy-start | bytes 1572868
  86.1 9.8 %copy-start.12 = (bf16[1,128,1024]{2,1,0:T(8,128)(2,1)S(1)}, bf16[1,128,1024]{2,1,0:T(8,128)(2,1)}, u32[]{:S(2)}) copy-start(bf16[1,128,1024]{2,1,0:T(8,128)(2,1)} %copy-done.10) | copy-start | bytes 786436
  86.1 9.8 %copy-start.14 = (bf16[1,128,1024]{2,1,0:T(8,128)(2,1)S(1)}, bf16[1,128,1024]{2,1,0:T(8,128)(2,1)}, u32[]{:S(2)}) copy-start(bf16[1,128,1024]{2,1,0:T(8,128)(2,1)} %copy-done.13) | copy-start | bytes 786436
  86.1 9.8 %copy-start.16 = (bf16[1,128,1024]{2,1,0:T(8,128)(2,1)S(1)}, bf16[1,128,1024]{2,1,0:T(8,128)(2,1)}, u32[]{:S(2)}) copy-start(bf16[1,128,1024]{2,1,0:T(8,128)(2,1)} %copy-done.15) | copy-start | bytes 786436
  86.1 9.8 %copy-start.18 = (bf16[1,128,1024]{2,1,0:T(8,128)(2,1)S(1)}, bf16[1,128,1024]{2,1,0:T(8,128)(2,1)}, u32[]{:S(2)}) copy-start(bf16[1,128,1024]{2,1,0:T(8,128)(2,1)} %copy-done.17) | copy-start | bytes 786436
  86.1 9.8 %copy-start.20 = (bf16[1,128,1024]{2,1,0:T(8,128)(2,1)S(1)}, bf16[1,128,1024]{2,1,0:T(8,128)(2,1)}, u32[]{:S(2)}) copy-start(bf16[1,128,1024]{2,1,0:T(8,128)(2,1)} %copy-done.19) | copy-start | bytes 786436
  86.1 2.1 %collective-permute-start.12 = (f32[4,128,128]{2,1,0:T(8,128)S(1)}, f32[4,128,128]{2,1,0:T(8,128)S(1)}, u32[]{:S(2)}, u32[]{:S(2)}) collective-permute-start(f32[4,128,128]{2,1,0:T(8,128)S(1)} %slice.3), channel_id=1, source_target_pairs={{0,1},{1,0},{2,3},{3,2},{4,5},{5,4},{6,7},{7,6},{8,9},{9,8},{10,11... | collective-permute-start | bytes 786440 | tf_op jit(solution)/shard_map/ppermute | solution.py:525
  86.2 17.2 %collective-permute-start.15 = (bf16[4,128,512]{2,1,0:T(8,128)(2,1)S(1)}, bf16[4,128,512]{2,1,0:T(8,128)(2,1)S(1)}, u32[]{:S(2)}, u32[]{:S(2)}) collective-permute-start(bf16[4,128,512]{2,1,0:T(8,128)(2,1)S(1)} %get-tuple-element.66), channel_id=1, source_target_pairs={{0,2},{1,3},{2,0},{3,1},{4,6},{5,7},{6,4},{7,5},{8,10},{9,11},{10,... | collective-permute-start | bytes 1572872 | tf_op jit(solution)/shard_map/ppermute | solution.py:525
  87.9 7.8 %collective-permute-start.10 = (bf16[4,128,128]{2,1,0:T(8,128)(2,1)S(1)}, bf16[4,128,128]{2,1,0:T(8,128)(2,1)S(1)}, u32[]{:S(2)}, u32[]{:S(2)}) collective-permute-start(bf16[4,128,128]{2,1,0:T(8,128)(2,1)S(1)} %pad_maximum_fusion.1), channel_id=1, source_target_pairs={{0,1},{1,0},{2,3},{3,2},{4,5},{5,4},{6,7},{7,6},{8,9},{9,8},{10,11... | collective-permute-start | bytes 393224 | tf_op jit(solution)/shard_map/ppermute | solution.py:525
  88.2 5.8 %collective-permute-start.13 = (bf16[4,128,128]{2,1,0:T(8,128)(2,1)S(1)}, bf16[4,128,128]{2,1,0:T(8,128)(2,1)S(1)}, u32[]{:S(2)}, u32[]{:S(2)}) collective-permute-start(bf16[4,128,128]{2,1,0:T(8,128)(2,1)S(1)} %get-tuple-element.62), channel_id=1, source_target_pairs={{0,4},{1,5},{2,6},{3,7},{4,0},{5,1},{6,2},{7,3},{8,12},{9,13},{10,... | collective-permute-start | bytes 393224 | tf_op jit(solution)/shard_map/ppermute | solution.py:525
  90.0 5.8 %collective-permute-start.11 = (bf16[1,128,1024]{2,1,0:T(8,128)(2,1)S(1)}, bf16[1,128,1024]{2,1,0:T(8,128)(2,1)S(1)}, u32[]{:S(2)}, u32[]{:S(2)}) collective-permute-start(bf16[1,128,1024]{2,1,0:T(8,128)(2,1)S(1)} %copy-done.22), channel_id=1, source_target_pairs={{0,1},{1,0},{2,3},{3,2},{4,5},{5,4},{6,7},{7,6},{8,9},{9,8},{10,11... | collective-permute-start | bytes 786440 | tf_op jit(solution)/shard_map/ppermute | solution.py:525
  94.1 1.7 %copy-start.25 = (f32[4,128,128]{2,1,0:T(8,128)}, f32[4,128,128]{2,1,0:T(8,128)S(1)}, u32[]{:S(2)}) copy-start(f32[4,128,128]{2,1,0:T(8,128)S(1)} %get-tuple-element.69.total) | copy-start | bytes 786436
  94.1 9.3 %collective-permute-start.14 = (bf16[4,128,128]{2,1,0:T(8,128)(2,1)S(1)}, bf16[4,128,128]{2,1,0:T(8,128)(2,1)S(1)}, u32[]{:S(2)}, u32[]{:S(2)}) collective-permute-start(bf16[4,128,128]{2,1,0:T(8,128)(2,1)S(1)} %get-tuple-element.63), channel_id=1, source_target_pairs={{0,8},{1,9},{2,10},{3,11},{4,12},{5,13},{6,14},{7,15},{8,0},{9,1},... | collective-permute-start | bytes 393224 | tf_op jit(solution)/shard_map/ppermute | solution.py:525
  101.4 1.3 copy-start.3
  104.1 5.1 %copy-start.26 = (f32[4,128,128]{2,1,0:T(8,128)S(1)}, f32[4,128,128]{2,1,0:T(8,128)}, u32[]{:S(2)}) copy-start(f32[4,128,128]{2,1,0:T(8,128)} %copy-done.25) | copy-start | bytes 786436
  104.1 30.1 %copy-start.24 = (bf16[8,128,128]{2,1,0:T(8,128)(2,1)S(1)}, bf16[8,128,128]{2,1,0:T(8,128)(2,1)}, u32[]{:S(2)}) copy-start(bf16[8,128,128]{2,1,0:T(8,128)(2,1)} %copy-done.23) | copy-start | bytes 786436
  104.1 52.5 %all-to-all-start.2 = ((bf16[8,2,128,512]{3,2,1,0:T(8,128)(2,1)}), bf16[8,2,128,512]{3,2,1,0:T(8,128)(2,1)S(1)}, u32[]{:S(2)}, u32[]{:S(2)}) async-start(bf16[8,2,128,512]{3,2,1,0:T(8,128)(2,1)} %copy-done.3), calls=%async_computation.2 | async-start | bytes 4194304 | tf_op jit(solution)/shard_map/all_to_all | solution.py:518
  108.0 31.4 %copy-start.9 = (bf16[8,128,512]{2,1,0:T(8,128)(2,1)S(1)}, bf16[8,128,512]{2,1,0:T(8,128)(2,1)}, u32[]{:S(2)}) copy-start(bf16[8,128,512]{2,1,0:T(8,128)(2,1)} %copy-done.8) | copy-start | bytes 3145732
  108.0 31.4 %collective-permute-start.20 = (bf16[4,128,512]{2,1,0:T(8,128)(2,1)}, bf16[4,128,512]{2,1,0:T(8,128)(2,1)S(1)}, u32[]{:S(2)}, u32[]{:S(2)}) collective-permute-start(bf16[4,128,512]{2,1,0:T(8,128)(2,1)} %copy-done.30), channel_id=1, source_target_pairs={{0,2},{1,3},{2,0},{3,1},{4,6},{5,7},{6,4},{7,5},{8,10},{9,11},{10,... | collective-permute-start | bytes 1572872 | tf_op jit(solution)/shard_map/ppermute | solution.py:525
  109.8 1.4 collective-permute-start.17
  110.0 18.6 %collective-permute-start.16 = (bf16[8,128,128]{2,1,0:T(8,128)(2,1)}, bf16[8,128,128]{2,1,0:T(8,128)(2,1)S(1)}, u32[]{:S(2)}, u32[]{:S(2)}) collective-permute-start(bf16[8,128,128]{2,1,0:T(8,128)(2,1)} %copy-done.31), channel_id=1, source_target_pairs={{0,2},{1,3},{2,0},{3,1},{4,6},{5,7},{6,4},{7,5},{8,10},{9,11},{10,... | collective-permute-start | bytes 786440 | tf_op jit(solution)/shard_map/ppermute | solution.py:525
  111.2 23.0 %collective-permute-start.18 = (bf16[8,128,128]{2,1,0:T(8,128)(2,1)S(1)}, bf16[8,128,128]{2,1,0:T(8,128)(2,1)S(1)}, u32[]{:S(2)}, u32[]{:S(2)}) collective-permute-start(bf16[8,128,128]{2,1,0:T(8,128)(2,1)S(1)} %pad_maximum_fusion.hiddens), channel_id=1, source_target_pairs={{0,2},{1,3},{2,0},{3,1},{4,6},{5,7},{6,4},{7,5},{8,10},{9,11},{10,... | collective-permute-start | bytes 786440 | tf_op jit(solution)/shard_map/ppermute | solution.py:525
  112.2 27.2 %collective-permute-start.19 = (bf16[8,128,128]{2,1,0:T(8,128)(2,1)S(1)}, bf16[8,128,128]{2,1,0:T(8,128)(2,1)S(1)}, u32[]{:S(2)}, u32[]{:S(2)}) collective-permute-start(bf16[8,128,128]{2,1,0:T(8,128)(2,1)S(1)} %constant_dynamic-update-slice_fusion.backs), channel_id=1, source_target_pairs={{0,2},{1,3},{2,0},{3,1},{4,6},{5,7},{6,4},{7,5},{8,10},{9,11},{10,... | collective-permute-start | bytes 786440 | tf_op jit(solution)/shard_map/ppermute | solution.py:525
  (10 other events, 7.9 us)

commit v22 on v21

--- a/solution.py
+++ b/solution.py
@@ -27,12 +27,16 @@
 
 def side_index(place, members):
     lines = members // 2
-    return place % pair_bit * lines + place // line_bit
+    line = place // line_bit
+    order = line
+    for shift in range(1, lines.bit_length() - 1):
+        order = order ^ (line >> shift)
+    return place % pair_bit * lines + order
 
 
 def side_place(index, side, members):
     core, line = divmod(index, members // 2)
-    return line * line_bit + side * pair_bit + core
+    return (line ^ (line >> 1)) * line_bit + side * pair_bit + core
 
 
 def params():

time: 159 us -> 159 us (level)
  no operation moved by 1% of the time
where the time goes in v22:
time: 159 us; the launch traced here: 158 us
  waiting for transfers between devices  84.4 us (53%)
  starting transfers between devices  32.8 us (21%)
  Pallas kernels  26.4 us (17%)
  local copies, waits for them, and re-layouts  12.5 us (8%)
    ppermute x21, waiting for transfers between devices, swap(): return lax.ppermute(array, 'dp', [(i, i ^ flip) for i in range(devices)])  70.9 us
    ppermute x21, starting transfers between devices, swap(): return lax.ppermute(array, 'dp', [(i, i ^ flip) for i in range(devices)])  21 us
    unnamed x72, local copies, waits for them, and re-layouts  12.5 us
    all_to_all x2, waiting for transfers between devices, exchange_side(): lax.all_to_all(pieces, 'dp', split_axis=0, concat_axis=0, axis_index_grou...  11.7 us
    pallas_call x6, Pallas kernels, call(): pl.pallas_call(kernel, out_shape=out_shapes, grid_spec=pltpu.PrefetchScal...  10.4 us
    pallas_call x2, Pallas kernels, sums_call(): pl.pallas_call(kernel, out_shape=jax.ShapeDtypeStruct((num_adapters,) + p...  9.08 us
    all_to_all x2, starting transfers between devices, exchange_side(): lax.all_to_all(pieces, 'dp', split_axis=0, concat_axis=0, axis_index_grou...  8.33 us
    pallas_call x3, Pallas kernels, copy_call(): pl.pallas_call(kernel, out_shape=out_shapes, grid_spec=pltpu.PrefetchScal...  5.5 us
  transfers between devices with their start and end apart: 24, of which 10 were waited for; matrix products, arithmetic and copies ran while one was open for 2% of the time, Pallas kernels for 14%

profile of v22, /device:TPU:0, one launch (start us, length us, event | category | flops | bytes accessed | tf_op | source)
XLA Modules:
  0.0 158.0 jit_solution(7774828772000452125)
XLA Ops:
  0.6 4.1 %collective-permute-start = (bf16[1,128,1024]{2,1,0:T(8,128)(2,1)}, bf16[1,128,1024]{2,1,0:T(8,128)(2,1)S(1)}, u32[]{:S(2)}, u32[]{:S(2)}) collective-permute-start(bf16[1,128,1024]{2,1,0:T(8,128)(2,1)} %bitcast.3), channel_id=1, source_target_pairs={{0,8},{1,9},{2,10},{3,11},{4,12},{5,13},{6,14},{7,15},{8,0},{9,1},... | collective-permute-start | bytes 786440 | tf_op jit(solution)/shard_map/ppermute | solution.py:529
  4.7 1.6 collective-permute-start.1
  6.3 1.2 copy-done.5
  7.5 0.7 copy-done.27
  8.2 1.8 %gather_up.1 = bf16[16,64,128]{2,1,0:T(8,128)(2,1)} custom-call(s32[16]{0:T(128)S(1)} %copy-done.27, bf16[64,64,128]{2,1,0:T(8,128)(2,1)S(1)} %copy-done.5), custom_call_target="tpu_custom_call" | custom-call | tf_op jit(solution)/shard_map/gather_up/pallas_call | solution.py:82
  10.0 3.5 %all-to-all-start = ((bf16[16,64,128]{2,1,0:T(8,128)(2,1)}), bf16[16,64,128]{2,1,0:T(8,128)(2,1)S(1)}, u32[]{:S(2)}, u32[]{:S(2)}) async-start(bf16[16,64,128]{2,1,0:T(8,128)(2,1)} %gather_up.1), calls=%async_computation | async-start | bytes 524288 | tf_op jit(solution)/shard_map/all_to_all | solution.py:516
  13.8 3.2 %collective-permute-done.refs_1_ = bf16[1,128,1024]{2,1,0:T(8,128)(2,1)S(1)} collective-permute-done((bf16[1,128,1024]{2,1,0:T(8,128)(2,1)}, bf16[1,128,1024]{2,1,0:T(8,128)(2,1)S(1)}, u32[]{:S(2)}, u32[]{:S(2)}) %collective-permute-start) | collective-permute-done | bytes 262176 | tf_op jit(solution)/shard_map/ppermute | solution.py:529
  17.5 1.6 %copy-done.2 = bf16[128,8192]{1,0:T(8,128)(2,1)S(1)} copy-done((bf16[128,8192]{1,0:T(8,128)(2,1)S(1)}, bf16[128,8192]{1,0:T(8,128)(2,1)}, u32[]{:S(2)}) %copy-start.2) | copy-done | bytes 2097176
  19.1 1.8 %pack_tokens.1 = bf16[8,2,128,512]{3,2,1,0:T(8,128)(2,1)} custom-call(s32[1]{0:T(128)} %bitcast.place, bf16[128,8192]{1,0:T(8,128)(2,1)S(1)} %copy-done.2), custom_call_target="tpu_custom_call" | custom-call | tf_op jit(solution)/shard_map/pack_tokens/pallas_call | solution.py:82
  21.0 0.7 copy-done.15
  21.7 1.9 %all-to-all-done = bf16[16,64,128]{2,1,0:T(8,128)(2,1)S(1)} async-done(((bf16[16,64,128]{2,1,0:T(8,128)(2,1)}), bf16[16,64,128]{2,1,0:T(8,128)(2,1)S(1)}, u32[]{:S(2)}, u32[]{:S(2)}) %all-to-all-start) | async-done | bytes 262176 | tf_op jit(solution)/shard_map/all_to_all | solution.py:516
  23.5 0.7 copy-done.6
  24.3 0.7 copy-done.17
  25.0 4.4 %all-to-all-start.1 = ((bf16[8,2,128,512]{3,2,1,0:T(8,128)(2,1)}), bf16[8,2,128,512]{3,2,1,0:T(8,128)(2,1)}, u32[]{:S(2)}, u32[]{:S(2)}) async-start(bf16[8,2,128,512]{3,2,1,0:T(8,128)(2,1)} %pack_tokens.1), calls=%async_computation.1 | async-start | bytes 4194304 | tf_op jit(solution)/shard_map/all_to_all | solution.py:522
  29.5 1.9 %for_pair.1 = bf16[2048,512]{1,0:T(8,128)(2,1)S(1)} custom-call(s32[16]{0:T(128)S(1)} %copy-done.28, s32[1]{0:T(128)} %bitcast.place, bf16[1024,512]{1,0:T(8,128)(2,1)S(1)} %copy-done.1, bf16[64,128,512]{2,1,0:T(8,128)(2,1)} %refs_7_.1), custom_call_target="tpu_custom_call" | custom-call | tf_op jit(solution)/shard_map/for_pair/pallas_call | solution.py:82
  31.4 0.8 collective-permute-start.9
  32.3 2.0 %collective-permute-start.8 = (bf16[1,128,1024]{2,1,0:T(8,128)(2,1)S(1)}, bf16[1,128,1024]{2,1,0:T(8,128)(2,1)S(1)}, u32[]{:S(2)}, u32[]{:S(2)}) collective-permute-start(bf16[1,128,1024]{2,1,0:T(8,128)(2,1)S(1)} %copy-done.11), channel_id=1, source_target_pairs={{0,4},{1,5},{2,6},{3,7},{4,0},{5,1},{6,2},{7,3},{8,12},{9,13},{10,... | collective-permute-start | bytes 786440 | tf_op jit(solution)/shard_map/ppermute | solution.py:529
  34.3 0.8 back_low.1
  35.0 2.4 %collective-permute-start.5 = (bf16[1,128,128]{2,1,0:T(8,128)(2,1)S(1)}, bf16[1,128,128]{2,1,0:T(8,128)(2,1)S(1)}, u32[]{:S(2)}, u32[]{:S(2)}) collective-permute-start(bf16[1,128,128]{2,1,0:T(8,128)(2,1)S(1)} %back_low.1), channel_id=1, source_target_pairs={{0,8},{1,9},{2,10},{3,11},{4,12},{5,13},{6,14},{7,15},{8,0},{9,1},... | collective-permute-start | bytes 98312 | tf_op jit(solution)/shard_map/ppermute | solution.py:529
  38.0 1.5 collective-permute-start.7
  39.5 41.3 %collective-permute-done.5 = bf16[1,128,128]{2,1,0:T(8,128)(2,1)S(1)} collective-permute-done((bf16[1,128,128]{2,1,0:T(8,128)(2,1)S(1)}, bf16[1,128,128]{2,1,0:T(8,128)(2,1)S(1)}, u32[]{:S(2)}, u32[]{:S(2)}) %collective-permute-start.5) | collective-permute-done | bytes 32800 | tf_op jit(solution)/shard_map/ppermute | solution.py:529
  80.8 0.7 copy-done.21
  81.6 3.5 %hidden_parts.1 = (f32[8,128,128]{2,1,0:T(8,128)S(1)}, bf16[8,128,512]{2,1,0:T(8,128)(2,1)S(1)}, bf16[4,128,512]{2,1,0:T(8,128)(2,1)S(1)}, bf16[4,128,512]{2,1,0:T(8,128)(2,1)S(1)}) custom-call(s32[16]{0:T(128)S(1)} %copy-done.28, s32[1]{0:T(128)} %bitcast.place, bf16[2048,512]{1,0:T(8,128)(2,1)S(1)} %collective-permute-done.9.pair, ...), custom_call_target="tpu_custom_call" | custom-call | tf_op jit(solution)/shard_map/hidden_parts/pallas_call | solution.py:59
  85.1 1.0 copy-done.8
  86.2 1.0 collective-permute-start.15
  87.2 0.8 pad_maximum_fusion.1
  88.2 1.0 collective-permute-start.13
  89.3 0.8 constant_dynamic-update-slice_fusion.3
  90.1 0.8 constant_dynamic-update-slice_fusion.2
  90.9 3.2 %collective-permute-done.13.received = bf16[4,128,128]{2,1,0:T(8,128)(2,1)S(1)} collective-permute-done((bf16[4,128,128]{2,1,0:T(8,128)(2,1)S(1)}, bf16[4,128,128]{2,1,0:T(8,128)(2,1)S(1)}, u32[]{:S(2)}, u32[]{:S(2)}) %collective-permute-start.13) | collective-permute-done | bytes 131104 | tf_op jit(solution)/shard_map/ppermute | solution.py:529
  94.1 0.8 collective-permute-start.14
  94.9 0.8 constant_dynamic-update-slice_fusion.1
  95.8 5.5 %input_slices.1 = (bf16[8,2,128,512]{3,2,1,0:T(8,128)(2,1)S(1)}, bf16[8,128,128]{2,1,0:T(8,128)(2,1)S(1)}, bf16[8,128,128]{2,1,0:T(8,128)(2,1)S(1)}) custom-call(s32[16]{0:T(128)S(1)} %copy-done.28, s32[1]{0:T(128)} %bitcast.place, bf16[8,128,128]{2,1,0:T(8,128)(2,1)S(1)} %constant_dynamic-update-slice_fusion.backs, bf16[2048,512]{1,0:T(8,128)(2,1)} %copy-done, ...), custom_call_target="tpu_custom_call" | custom-call | tf_op jit(solution)/shard_map/input_slices/pallas_call | solution.py:59
  101.3 1.3 copy-done.3
  102.6 0.7 copy-done.23
  103.3 0.7 copy-done.31
  104.0 4.0 %all-to-all-start.2 = ((bf16[8,2,128,512]{3,2,1,0:T(8,128)(2,1)}), bf16[8,2,128,512]{3,2,1,0:T(8,128)(2,1)S(1)}, u32[]{:S(2)}, u32[]{:S(2)}) async-start(bf16[8,2,128,512]{3,2,1,0:T(8,128)(2,1)} %copy-done.3), calls=%async_computation.2 | async-start | bytes 4194304 | tf_op jit(solution)/shard_map/all_to_all | solution.py:522
  108.0 1.2 collective-permute-start.20
  110.0 0.9 collective-permute-start.16
  111.2 1.0 collective-permute-start.18
  112.2 1.1 collective-permute-start.19
  113.3 15.3 %collective-permute-done.16.gradients_pair = bf16[8,128,128]{2,1,0:T(8,128)(2,1)S(1)} collective-permute-done((bf16[8,128,128]{2,1,0:T(8,128)(2,1)}, bf16[8,128,128]{2,1,0:T(8,128)(2,1)S(1)}, u32[]{:S(2)}, u32[]{:S(2)}) %collective-permute-start.16) | collective-permute-done | bytes 262176 | tf_op jit(solution)/shard_map/ppermute | solution.py:529
  128.6 5.6 %collective-permute-done.18.hiddens_pair = bf16[8,128,128]{2,1,0:T(8,128)(2,1)S(1)} collective-permute-done((bf16[8,128,128]{2,1,0:T(8,128)(2,1)S(1)}, bf16[8,128,128]{2,1,0:T(8,128)(2,1)S(1)}, u32[]{:S(2)}, u32[]{:S(2)}) %collective-permute-start.18) | collective-permute-done | bytes 262176 | tf_op jit(solution)/shard_map/ppermute | solution.py:529
  134.2 3.6 %up_gradients.1 = bf16[64,64,128]{2,1,0:T(8,128)(2,1)} custom-call(s32[16]{0:T(128)S(1)} %copy-done.28, s32[1]{0:T(128)} %bitcast.place, s32[64]{0:T(128)S(1)} %copy-done.29, bf16[8,128,128]{2,1,0:T(8,128)(2,1)S(1)} %copy-done.24, bf16[8,128,128]{2,1,0:T(8,128)(2,1)S(1)} %collective-permute-done.16.gradients_pair, ...), custom_call_target="tpu_custom_call" | custom-call | tf_op jit(solution)/shard_map/up_gradients/pallas_call | solution.py:402
  137.8 1.6 collective-permute-done.19.backs_pair
  139.4 5.5 %down_gradients.1 = bf16[64,128,512]{2,1,0:T(8,128)(2,1)} custom-call(s32[16]{0:T(128)S(1)} %copy-done.28, s32[1]{0:T(128)} %bitcast.place, bf16[8,128,128]{2,1,0:T(8,128)(2,1)S(1)} %constant_dynamic-update-slice_fusion.backs, bf16[8,128,128]{2,1,0:T(8,128)(2,1)S(1)} %collective-permute-done.19.backs_pair, bf16[8,128,512]{2,1,0:T(8,128)(2,1)S(1)} %copy-done.9, ...), custom_call_target="tpu_custom_call" | custom-call | tf_op jit(solution)/shard_map/down_gradients/pallas_call | solution.py:402
  144.9 11.7 %all-to-all-done.2.source = bf16[8,2,128,512]{3,2,1,0:T(8,128)(2,1)S(1)} async-done(((bf16[8,2,128,512]{3,2,1,0:T(8,128)(2,1)}), bf16[8,2,128,512]{3,2,1,0:T(8,128)(2,1)S(1)}, u32[]{:S(2)}, u32[]{:S(2)}) %all-to-all-start.2) | async-done | bytes 2097184 | tf_op jit(solution)/shard_map/all_to_all | solution.py:522
  156.6 1.4 join_columns.1
  (88 shorter events, 3.2 us)
Async XLA Ops:
  0.6 16.3 %collective-permute-start = (bf16[1,128,1024]{2,1,0:T(8,128)(2,1)}, bf16[1,128,1024]{2,1,0:T(8,128)(2,1)S(1)}, u32[]{:S(2)}, u32[]{:S(2)}) collective-permute-start(bf16[1,128,1024]{2,1,0:T(8,128)(2,1)} %bitcast.3), channel_id=1, source_target_pairs={{0,8},{1,9},{2,10},{3,11},{4,12},{5,13},{6,14},{7,15},{8,0},{9,1},... | collective-permute-start | bytes 786440 | tf_op jit(solution)/shard_map/ppermute | solution.py:529
  4.7 12.7 %collective-permute-start.1 = (bf16[1,128,1024]{2,1,0:T(8,128)(2,1)}, bf16[1,128,1024]{2,1,0:T(8,128)(2,1)S(1)}, u32[]{:S(2)}, u32[]{:S(2)}) collective-permute-start(bf16[1,128,1024]{2,1,0:T(8,128)(2,1)} %bitcast.4), channel_id=1, source_target_pairs={{0,4},{1,5},{2,6},{3,7},{4,0},{5,1},{6,2},{7,3},{8,12},{9,13},{10,... | collective-permute-start | bytes 786440 | tf_op jit(solution)/shard_map/ppermute | solution.py:529
  10.0 13.6 %all-to-all-start = ((bf16[16,64,128]{2,1,0:T(8,128)(2,1)}), bf16[16,64,128]{2,1,0:T(8,128)(2,1)S(1)}, u32[]{:S(2)}, u32[]{:S(2)}) async-start(bf16[16,64,128]{2,1,0:T(8,128)(2,1)} %gather_up.1), calls=%async_computation | async-start | bytes 524288 | tf_op jit(solution)/shard_map/all_to_all | solution.py:516
  13.5 7.4 %collective-permute-start.2 = (bf16[1,128,1024]{2,1,0:T(8,128)(2,1)}, bf16[1,128,1024]{2,1,0:T(8,128)(2,1)S(1)}, u32[]{:S(2)}, u32[]{:S(2)}) collective-permute-start(bf16[1,128,1024]{2,1,0:T(8,128)(2,1)} %bitcast.5), channel_id=1, source_target_pairs={{0,1},{1,0},{2,3},{3,2},{4,5},{5,4},{6,7},{7,6},{8,9},{9,8},{10,11... | collective-permute-start | bytes 786440 | tf_op jit(solution)/shard_map/ppermute | solution.py:529
  17.0 4.0 %copy-start.10 = (bf16[1,128,1024]{2,1,0:T(8,128)(2,1)}, bf16[1,128,1024]{2,1,0:T(8,128)(2,1)S(1)}, u32[]{:S(2)}) copy-start(bf16[1,128,1024]{2,1,0:T(8,128)(2,1)S(1)} %collective-permute-done.refs_1_) | copy-start | bytes 786436
  17.0 7.2 %collective-permute-start.3 = (bf16[1,128,1024]{2,1,0:T(8,128)(2,1)S(1)}, bf16[1,128,1024]{2,1,0:T(8,128)(2,1)S(1)}, u32[]{:S(2)}, u32[]{:S(2)}) collective-permute-start(bf16[1,128,1024]{2,1,0:T(8,128)(2,1)S(1)} %collective-permute-done.refs_1_), channel_id=1, source_target_pairs={{0,1},{1,0},{2,3},{3,2},{4,5},{5,4},{6,7},{7,6},{8,9},{9,8},{10,11... | collective-permute-start | bytes 786440 | tf_op jit(solution)/shard_map/ppermute | solution.py:529
  17.4 3.5 %copy-start.13 = (bf16[1,128,1024]{2,1,0:T(8,128)(2,1)}, bf16[1,128,1024]{2,1,0:T(8,128)(2,1)S(1)}, u32[]{:S(2)}) copy-start(bf16[1,128,1024]{2,1,0:T(8,128)(2,1)S(1)} %collective-permute-done.1.refs_2_) | copy-start | bytes 786436
  17.4 6.8 %collective-permute-start.4 = (bf16[1,128,1024]{2,1,0:T(8,128)(2,1)S(1)}, bf16[1,128,1024]{2,1,0:T(8,128)(2,1)S(1)}, u32[]{:S(2)}, u32[]{:S(2)}) collective-permute-start(bf16[1,128,1024]{2,1,0:T(8,128)(2,1)S(1)} %collective-permute-done.1.refs_2_), channel_id=1, source_target_pairs={{0,1},{1,0},{2,3},{3,2},{4,5},{5,4},{6,7},{7,6},{8,9},{9,8},{10,11... | collective-permute-start | bytes 786440 | tf_op jit(solution)/shard_map/ppermute | solution.py:529
  17.5 1.6 %copy-start.2 = (bf16[128,8192]{1,0:T(8,128)(2,1)S(1)}, bf16[128,8192]{1,0:T(8,128)(2,1)}, u32[]{:S(2)}) copy-start(bf16[128,8192]{1,0:T(8,128)(2,1)} %tokens.1) | copy-start | bytes 6291460
  24.2 5.2 %copy-start.1 = (bf16[1024,512]{1,0:T(8,128)(2,1)S(1)}, bf16[1024,512]{1,0:T(8,128)(2,1)}, u32[]{:S(2)}) copy-start(bf16[1024,512]{1,0:T(8,128)(2,1)} %refs_16_.1) | copy-start | bytes 3145732
  24.3 5.2 %copy-start.28 = (s32[16]{0:T(128)S(1)}, s32[16]{0:T(128)}, u32[]{:S(2)}) copy-start(s32[16]{0:T(128)} %adapters.8) | copy-start | bytes 196
  25.0 56.5 %all-to-all-start.1 = ((bf16[8,2,128,512]{3,2,1,0:T(8,128)(2,1)}), bf16[8,2,128,512]{3,2,1,0:T(8,128)(2,1)}, u32[]{:S(2)}, u32[]{:S(2)}) async-start(bf16[8,2,128,512]{3,2,1,0:T(8,128)(2,1)} %pack_tokens.1), calls=%async_computation.1 | async-start | bytes 4194304 | tf_op jit(solution)/shard_map/all_to_all | solution.py:522
  29.4 2.8 %copy-start.11 = (bf16[1,128,1024]{2,1,0:T(8,128)(2,1)S(1)}, bf16[1,128,1024]{2,1,0:T(8,128)(2,1)}, u32[]{:S(2)}) copy-start(bf16[1,128,1024]{2,1,0:T(8,128)(2,1)} %copy-done.10) | copy-start | bytes 786436
  29.4 4.8 %copy-start.4 = (bf16[128,1024]{1,0:T(8,128)(2,1)S(1)}, bf16[128,1024]{1,0:T(8,128)(2,1)}, u32[]{:S(2)}) copy-start(bf16[128,1024]{1,0:T(8,128)(2,1)} %gradient.1) | copy-start | bytes 786436
  29.4 4.8 %copy-start.7 = (bf16[16,64,128]{2,1,0:T(8,128)(2,1)S(1)}, bf16[16,64,128]{2,1,0:T(8,128)(2,1)}, u32[]{:S(2)}) copy-start(bf16[16,64,128]{2,1,0:T(8,128)(2,1)} %copy-done.6) | copy-start | bytes 786436
  29.4 4.8 %copy-start.29 = (s32[64]{0:T(128)S(1)}, s32[64]{0:T(128)}, u32[]{:S(2)}) copy-start(s32[64]{0:T(128)} %ranks.5) | copy-start | bytes 772
  31.4 50.2 %collective-permute-start.9 = (bf16[2048,512]{1,0:T(8,128)(2,1)S(1)}, bf16[2048,512]{1,0:T(8,128)(2,1)S(1)}, u32[]{:S(2)}, u32[]{:S(2)}) collective-permute-start(bf16[2048,512]{1,0:T(8,128)(2,1)S(1)} %for_pair.1), channel_id=1, source_target_pairs={{0,2},{1,3},{2,0},{3,1},{4,6},{5,7},{6,4},{7,5},{8,10},{9,11},{10,... | collective-permute-start | bytes 6291464 | tf_op jit(solution)/shard_map/ppermute | solution.py:529
  32.3 48.6 %collective-permute-start.8 = (bf16[1,128,1024]{2,1,0:T(8,128)(2,1)S(1)}, bf16[1,128,1024]{2,1,0:T(8,128)(2,1)S(1)}, u32[]{:S(2)}, u32[]{:S(2)}) collective-permute-start(bf16[1,128,1024]{2,1,0:T(8,128)(2,1)S(1)} %copy-done.11), channel_id=1, source_target_pairs={{0,4},{1,5},{2,6},{3,7},{4,0},{5,1},{6,2},{7,3},{8,12},{9,13},{10,... | collective-permute-start | bytes 786440 | tf_op jit(solution)/shard_map/ppermute | solution.py:529
  35.0 45.8 %collective-permute-start.5 = (bf16[1,128,128]{2,1,0:T(8,128)(2,1)S(1)}, bf16[1,128,128]{2,1,0:T(8,128)(2,1)S(1)}, u32[]{:S(2)}, u32[]{:S(2)}) collective-permute-start(bf16[1,128,128]{2,1,0:T(8,128)(2,1)S(1)} %back_low.1), channel_id=1, source_target_pairs={{0,8},{1,9},{2,10},{3,11},{4,12},{5,13},{6,14},{7,15},{8,0},{9,1},... | collective-permute-start | bytes 98312 | tf_op jit(solution)/shard_map/ppermute | solution.py:529
  37.5 43.3 %collective-permute-start.6 = (bf16[1,128,128]{2,1,0:T(8,128)(2,1)S(1)}, bf16[1,128,128]{2,1,0:T(8,128)(2,1)S(1)}, u32[]{:S(2)}, u32[]{:S(2)}) collective-permute-start(bf16[1,128,128]{2,1,0:T(8,128)(2,1)S(1)} %back_low.1), channel_id=1, source_target_pairs={{0,4},{1,5},{2,6},{3,7},{4,0},{5,1},{6,2},{7,3},{8,12},{9,13},{10,... | collective-permute-start | bytes 98312 | tf_op jit(solution)/shard_map/ppermute | solution.py:529
  38.0 42.8 %collective-permute-start.7 = (bf16[1,128,128]{2,1,0:T(8,128)(2,1)S(1)}, bf16[1,128,128]{2,1,0:T(8,128)(2,1)}, u32[]{:S(2)}, u32[]{:S(2)}) collective-permute-start(bf16[1,128,128]{2,1,0:T(8,128)(2,1)S(1)} %back_low.1), channel_id=1, source_target_pairs={{0,12},{1,13},{2,14},{3,15},{4,8},{5,9},{6,10},{7,11},{8,4},{9,5},... | collective-permute-start | bytes 98312 | tf_op jit(solution)/shard_map/ppermute | solution.py:529
  80.8 6.4 %copy-start.33 = (bf16[1,128,128]{2,1,0:T(8,128)(2,1)}, bf16[1,128,128]{2,1,0:T(8,128)(2,1)S(1)}, u32[]{:S(2)}) copy-start(bf16[1,128,128]{2,1,0:T(8,128)(2,1)S(1)} %collective-permute-done.5) | copy-start | bytes 98308
  80.8 6.4 %copy-start.32 = (bf16[1,128,128]{2,1,0:T(8,128)(2,1)}, bf16[1,128,128]{2,1,0:T(8,128)(2,1)S(1)}, u32[]{:S(2)}) copy-start(bf16[1,128,128]{2,1,0:T(8,128)(2,1)S(1)} %collective-permute-done.6) | copy-start | bytes 98308
  81.6 3.5 %copy-start = (bf16[2048,512]{1,0:T(8,128)(2,1)}, bf16[2048,512]{1,0:T(8,128)(2,1)S(1)}, u32[]{:S(2)}) copy-start(bf16[2048,512]{1,0:T(8,128)(2,1)S(1)} %collective-permute-done.9.pair) | copy-start | bytes 6291460
  81.6 8.5 %copy-start.22 = (bf16[1,128,1024]{2,1,0:T(8,128)(2,1)S(1)}, bf16[1,128,1024]{2,1,0:T(8,128)(2,1)}, u32[]{:S(2)}) copy-start(bf16[1,128,1024]{2,1,0:T(8,128)(2,1)} %copy-done.21) | copy-start | bytes 786436
  86.1 2.1 %copy-start.30 = (bf16[4,128,512]{2,1,0:T(8,128)(2,1)}, bf16[4,128,512]{2,1,0:T(8,128)(2,1)S(1)}, u32[]{:S(2)}) copy-start(bf16[4,128,512]{2,1,0:T(8,128)(2,1)S(1)} %get-tuple-element.74) | copy-start | bytes 1572868
  86.1 9.7 %copy-start.12 = (bf16[1,128,1024]{2,1,0:T(8,128)(2,1)S(1)}, bf16[1,128,1024]{2,1,0:T(8,128)(2,1)}, u32[]{:S(2)}) copy-start(bf16[1,128,1024]{2,1,0:T(8,128)(2,1)} %copy-done.10) | copy-start | bytes 786436
  86.1 9.7 %copy-start.14 = (bf16[1,128,1024]{2,1,0:T(8,128)(2,1)S(1)}, bf16[1,128,1024]{2,1,0:T(8,128)(2,1)}, u32[]{:S(2)}) copy-start(bf16[1,128,1024]{2,1,0:T(8,128)(2,1)} %copy-done.13) | copy-start | bytes 786436
  86.1 9.7 %copy-start.16 = (bf16[1,128,1024]{2,1,0:T(8,128)(2,1)S(1)}, bf16[1,128,1024]{2,1,0:T(8,128)(2,1)}, u32[]{:S(2)}) copy-start(bf16[1,128,1024]{2,1,0:T(8,128)(2,1)} %copy-done.15) | copy-start | bytes 786436
  86.1 9.7 %copy-start.18 = (bf16[1,128,1024]{2,1,0:T(8,128)(2,1)S(1)}, bf16[1,128,1024]{2,1,0:T(8,128)(2,1)}, u32[]{:S(2)}) copy-start(bf16[1,128,1024]{2,1,0:T(8,128)(2,1)} %copy-done.17) | copy-start | bytes 786436
  86.1 9.7 %copy-start.20 = (bf16[1,128,1024]{2,1,0:T(8,128)(2,1)S(1)}, bf16[1,128,1024]{2,1,0:T(8,128)(2,1)}, u32[]{:S(2)}) copy-start(bf16[1,128,1024]{2,1,0:T(8,128)(2,1)} %copy-done.19) | copy-start | bytes 786436
  86.1 2.1 %collective-permute-start.12 = (f32[4,128,128]{2,1,0:T(8,128)S(1)}, f32[4,128,128]{2,1,0:T(8,128)S(1)}, u32[]{:S(2)}, u32[]{:S(2)}) collective-permute-start(f32[4,128,128]{2,1,0:T(8,128)S(1)} %slice.3), channel_id=1, source_target_pairs={{0,1},{1,0},{2,3},{3,2},{4,5},{5,4},{6,7},{7,6},{8,9},{9,8},{10,11... | collective-permute-start | bytes 786440 | tf_op jit(solution)/shard_map/ppermute | solution.py:529
  86.2 17.1 %collective-permute-start.15 = (bf16[4,128,512]{2,1,0:T(8,128)(2,1)S(1)}, bf16[4,128,512]{2,1,0:T(8,128)(2,1)S(1)}, u32[]{:S(2)}, u32[]{:S(2)}) collective-permute-start(bf16[4,128,512]{2,1,0:T(8,128)(2,1)S(1)} %get-tuple-element.66), channel_id=1, source_target_pairs={{0,2},{1,3},{2,0},{3,1},{4,6},{5,7},{6,4},{7,5},{8,10},{9,11},{10,... | collective-permute-start | bytes 1572872 | tf_op jit(solution)/shard_map/ppermute | solution.py:529
  88.0 7.8 %collective-permute-start.10 = (bf16[4,128,128]{2,1,0:T(8,128)(2,1)S(1)}, bf16[4,128,128]{2,1,0:T(8,128)(2,1)S(1)}, u32[]{:S(2)}, u32[]{:S(2)}) collective-permute-start(bf16[4,128,128]{2,1,0:T(8,128)(2,1)S(1)} %pad_maximum_fusion.1), channel_id=1, source_target_pairs={{0,1},{1,0},{2,3},{3,2},{4,5},{5,4},{6,7},{7,6},{8,9},{9,8},{10,11... | collective-permute-start | bytes 393224 | tf_op jit(solution)/shard_map/ppermute | solution.py:529
  88.2 5.8 %collective-permute-start.13 = (bf16[4,128,128]{2,1,0:T(8,128)(2,1)S(1)}, bf16[4,128,128]{2,1,0:T(8,128)(2,1)S(1)}, u32[]{:S(2)}, u32[]{:S(2)}) collective-permute-start(bf16[4,128,128]{2,1,0:T(8,128)(2,1)S(1)} %get-tuple-element.62), channel_id=1, source_target_pairs={{0,4},{1,5},{2,6},{3,7},{4,0},{5,1},{6,2},{7,3},{8,12},{9,13},{10,... | collective-permute-start | bytes 393224 | tf_op jit(solution)/shard_map/ppermute | solution.py:529
  90.1 5.7 %collective-permute-start.11 = (bf16[1,128,1024]{2,1,0:T(8,128)(2,1)S(1)}, bf16[1,128,1024]{2,1,0:T(8,128)(2,1)S(1)}, u32[]{:S(2)}, u32[]{:S(2)}) collective-permute-start(bf16[1,128,1024]{2,1,0:T(8,128)(2,1)S(1)} %copy-done.22), channel_id=1, source_target_pairs={{0,1},{1,0},{2,3},{3,2},{4,5},{5,4},{6,7},{7,6},{8,9},{9,8},{10,11... | collective-permute-start | bytes 786440 | tf_op jit(solution)/shard_map/ppermute | solution.py:529
  94.1 1.6 %copy-start.25 = (f32[4,128,128]{2,1,0:T(8,128)}, f32[4,128,128]{2,1,0:T(8,128)S(1)}, u32[]{:S(2)}) copy-start(f32[4,128,128]{2,1,0:T(8,128)S(1)} %get-tuple-element.69.total) | copy-start | bytes 786436
  94.1 9.2 %collective-permute-start.14 = (bf16[4,128,128]{2,1,0:T(8,128)(2,1)S(1)}, bf16[4,128,128]{2,1,0:T(8,128)(2,1)S(1)}, u32[]{:S(2)}, u32[]{:S(2)}) collective-permute-start(bf16[4,128,128]{2,1,0:T(8,128)(2,1)S(1)} %get-tuple-element.63), channel_id=1, source_target_pairs={{0,8},{1,9},{2,10},{3,11},{4,12},{5,13},{6,14},{7,15},{8,0},{9,1},... | collective-permute-start | bytes 393224 | tf_op jit(solution)/shard_map/ppermute | solution.py:529
  101.3 1.3 copy-start.3
  104.0 5.2 %copy-start.26 = (f32[4,128,128]{2,1,0:T(8,128)S(1)}, f32[4,128,128]{2,1,0:T(8,128)}, u32[]{:S(2)}) copy-start(f32[4,128,128]{2,1,0:T(8,128)} %copy-done.25) | copy-start | bytes 786436
  104.0 30.2 %copy-start.24 = (bf16[8,128,128]{2,1,0:T(8,128)(2,1)S(1)}, bf16[8,128,128]{2,1,0:T(8,128)(2,1)}, u32[]{:S(2)}) copy-start(bf16[8,128,128]{2,1,0:T(8,128)(2,1)} %copy-done.23) | copy-start | bytes 786436
  104.0 52.6 %all-to-all-start.2 = ((bf16[8,2,128,512]{3,2,1,0:T(8,128)(2,1)}), bf16[8,2,128,512]{3,2,1,0:T(8,128)(2,1)S(1)}, u32[]{:S(2)}, u32[]{:S(2)}) async-start(bf16[8,2,128,512]{3,2,1,0:T(8,128)(2,1)} %copy-done.3), calls=%async_computation.2 | async-start | bytes 4194304 | tf_op jit(solution)/shard_map/all_to_all | solution.py:522
  108.0 31.4 %copy-start.9 = (bf16[8,128,512]{2,1,0:T(8,128)(2,1)S(1)}, bf16[8,128,512]{2,1,0:T(8,128)(2,1)}, u32[]{:S(2)}) copy-start(bf16[8,128,512]{2,1,0:T(8,128)(2,1)} %copy-done.8) | copy-start | bytes 3145732
  108.0 31.4 %collective-permute-start.20 = (bf16[4,128,512]{2,1,0:T(8,128)(2,1)}, bf16[4,128,512]{2,1,0:T(8,128)(2,1)S(1)}, u32[]{:S(2)}, u32[]{:S(2)}) collective-permute-start(bf16[4,128,512]{2,1,0:T(8,128)(2,1)} %copy-done.30), channel_id=1, source_target_pairs={{0,2},{1,3},{2,0},{3,1},{4,6},{5,7},{6,4},{7,5},{8,10},{9,11},{10,... | collective-permute-start | bytes 1572872 | tf_op jit(solution)/shard_map/ppermute | solution.py:529
  109.8 1.4 collective-permute-start.17
  110.0 18.6 %collective-permute-start.16 = (bf16[8,128,128]{2,1,0:T(8,128)(2,1)}, bf16[8,128,128]{2,1,0:T(8,128)(2,1)S(1)}, u32[]{:S(2)}, u32[]{:S(2)}) collective-permute-start(bf16[8,128,128]{2,1,0:T(8,128)(2,1)} %copy-done.31), channel_id=1, source_target_pairs={{0,2},{1,3},{2,0},{3,1},{4,6},{5,7},{6,4},{7,5},{8,10},{9,11},{10,... | collective-permute-start | bytes 786440 | tf_op jit(solution)/shard_map/ppermute | solution.py:529
  111.2 23.0 %collective-permute-start.18 = (bf16[8,128,128]{2,1,0:T(8,128)(2,1)S(1)}, bf16[8,128,128]{2,1,0:T(8,128)(2,1)S(1)}, u32[]{:S(2)}, u32[]{:S(2)}) collective-permute-start(bf16[8,128,128]{2,1,0:T(8,128)(2,1)S(1)} %pad_maximum_fusion.hiddens), channel_id=1, source_target_pairs={{0,2},{1,3},{2,0},{3,1},{4,6},{5,7},{6,4},{7,5},{8,10},{9,11},{10,... | collective-permute-start | bytes 786440 | tf_op jit(solution)/shard_map/ppermute | solution.py:529
  112.2 27.2 %collective-permute-start.19 = (bf16[8,128,128]{2,1,0:T(8,128)(2,1)S(1)}, bf16[8,128,128]{2,1,0:T(8,128)(2,1)S(1)}, u32[]{:S(2)}, u32[]{:S(2)}) collective-permute-start(bf16[8,128,128]{2,1,0:T(8,128)(2,1)S(1)} %constant_dynamic-update-slice_fusion.backs), channel_id=1, source_target_pairs={{0,2},{1,3},{2,0},{3,1},{4,6},{5,7},{6,4},{7,5},{8,10},{9,11},{10,... | collective-permute-start | bytes 786440 | tf_op jit(solution)/shard_map/ppermute | solution.py:529
  (10 other events, 7.9 us)
